TPU v7x, 32 devices: a whole 2x2x4 slice. The times are simulated.
32 devices in a mesh: tok: 4 (over z), row: 2 (over y), col: 4 (over x, core).
Axes of the slice: x: 2, y: 2, z: 4, core: 2. Of those that a mesh axis runs over, the one named last changes fastest.
Arguments:
- activations: bfloat16 [1408, 4096], P(('tok', 'row'), 'col'), may hold values from -512 to 512
- norm_gain: bfloat16 [4096], P('col'), may hold values from 1.5 to 10
- qkv_weight: bfloat16 [4096, 16, 384], P('row', 'col'), may hold values from -0.09375 to 0.09375
- doc_ids: int32 [1408], P(('tok', 'row')), may hold values from 0 to 3, never falling along the last dimension, each value on 1 to 1056 neighbouring positions
Outputs:
- attended: bfloat16 [1408, 2048], P(('tok', 'row'), 'col')
Inputs may be any that keep to these rules, and one draw needn't show every extreme that they name: `doc_ids`: never falls along the sequence; each of the 4 documents holds 1 to 1056 tokens and one holds exactly 1056.
All inputs are finite; a program needn't handle non-finite values.
Results may differ from a plain program's by a relative error of at most 0.007.
The roundings to bfloat16 on the way count: a program that leaves them out, or rounds other values in their place, can miss the bound.
Values may be sent and summed in bfloat16 or wider, within the bound.
No kernel may reach another device: no remote copies, remote signals or barrier semaphores. Data moves between devices by JAX's collectives and lax.ppermute only.
A program may use at most 128 MiB of HBM per device.

v0:
```python
import math

import jax
import jax.numpy as jnp
from jax import lax
from jax.experimental import pallas as pl
from jax.experimental.pallas import tpu as pltpu
from jax.sharding import PartitionSpec as P

EPS = 1e-05
MIB = 1 << 20


def rotary_tables(places, head_size):
    half = head_size // 2
    spacing = jnp.arange(half).astype(jnp.float32) * (2.0 / head_size)
    inverse = jnp.power(10000.0, -spacing)
    angles = places.astype(jnp.float32)[:, None] * inverse[None, :]
    cosine, sine = jnp.cos(angles), jnp.sin(angles)
    return (
        jnp.concatenate([cosine, cosine], axis=1),
        jnp.concatenate([-sine, sine], axis=1),
    )


def weight_copies(first_head, triple, weight_hbm, weight_buffer, semaphores):
    depth = weight_buffer.shape[0] // 2
    columns = weight_buffer.shape[1]
    first = pl.multiple_of(first_head * triple, 128)
    return [
        pltpu.make_async_copy(
            weight_hbm.at[pl.ds(half * depth, depth), pl.ds(first, columns)],
            weight_buffer.at[pl.ds(half * depth, depth), :],
            semaphores.at[half],
        )
        for half in range(2)
    ]


def project_heads(normed_ref, copies, weight_buffer, cos_ref, sin_ref, out_ref):
    heads, size = out_ref.shape[0], out_ref.shape[3]
    depth = weight_buffer.shape[0] // 2
    for copy in copies:
        copy.wait()
    for head in range(heads):
        columns = slice(head * 3 * size, (head + 1) * 3 * size)
        part = jnp.dot(
            normed_ref[0], weight_buffer[:depth, columns], preferred_element_type=jnp.float32
        ) + jnp.dot(
            normed_ref[1], weight_buffer[depth:, columns], preferred_element_type=jnp.float32
        )
        for kind in range(3):
            piece = part[:, kind * size : (kind + 1) * size]
            if kind < 2:
                piece = piece * cos_ref[...] + pltpu.roll(piece, size // 2, 1) * sin_ref[...]
            out_ref[head, kind] = piece


def normalise_project_kernel(
    place_ref, a_near, a_far, b_near, b_far, squares_ref, gain_ref, weight_hbm, cos_ref, sin_ref,
    out_ref, normed_ref, weight_buffer, semaphores,
):
    rows = a_near.shape[0]
    features = 2 * gain_ref.shape[0] * gain_ref.shape[2]
    core, near_row, head = place_ref[0], place_ref[1], place_ref[2]
    copies = weight_copies(head, 3 * cos_ref.shape[1], weight_hbm, weight_buffer, semaphores)
    for copy in copies:
        copy.start()
    for shards, half in (((a_near, a_far), core), ((b_near, b_far), 1 - core)):
        gain = gain_ref[half]
        for shard, row in zip(shards, (near_row, 1 - near_row)):
            at = pl.ds(pl.multiple_of(row * rows, 16), rows)
            factor = lax.rsqrt(squares_ref[at, :] / features + EPS)
            normed_ref[half, at, :] = (shard[...].astype(jnp.float32) * factor * gain).astype(
                jnp.bfloat16
            )
    project_heads(normed_ref, copies, weight_buffer, cos_ref, sin_ref, out_ref)


def project_kernel(
    place_ref, normed_ref, weight_hbm, cos_ref, sin_ref, out_ref, weight_buffer, semaphores
):
    copies = weight_copies(
        place_ref[0], 3 * cos_ref.shape[1], weight_hbm, weight_buffer, semaphores
    )
    for copy in copies:
        copy.start()
    project_heads(normed_ref, copies, weight_buffer, cos_ref, sin_ref, out_ref)


def attend_kernel(scale, query_ref, *refs):
    key_value_refs, (key_place_ref, place_ref, start_ref, out_ref) = refs[:-4], refs[-4:]
    key_places = key_place_ref[...]
    visible = (key_places <= place_ref[...]) & (key_places >= start_ref[...])
    keys = jnp.concatenate([ref[0] for ref in key_value_refs], axis=0)
    values = jnp.concatenate([ref[1] for ref in key_value_refs], axis=0)
    scores = (
        lax.dot_general(
            query_ref[...], keys, (((1,), (1,)), ((), ())), preferred_element_type=jnp.float32
        )
        * scale
    )
    masked = jnp.where(visible, scores, -1e30)
    top = jnp.max(masked, axis=1, keepdims=True)
    exponentials = jnp.where(visible, jnp.exp(masked - top), 0.0)
    total = jnp.sum(exponentials, axis=1, keepdims=True)
    summed = jnp.dot(
        exponentials.astype(jnp.bfloat16), values, preferred_element_type=jnp.float32
    )
    out_ref[...] = (summed / total).astype(jnp.bfloat16)


def attend_gathered(query, keys, values, places, starts, scale):
    heads, count, size = query.shape
    chunk = math.gcd(keys.shape[1], 1024)
    rounds = keys.shape[1] // chunk
    stacked = (
        keys.reshape(heads, rounds, chunk, size).transpose(1, 0, 2, 3),
        values.reshape(heads, rounds, chunk, size).transpose(1, 0, 2, 3),
        jnp.arange(rounds * chunk, dtype=jnp.int32).reshape(rounds, chunk),
    )

    def advance(state, blocks):
        running, totals, summed = state
        block_keys, block_values, key_places = blocks
        scores = (
            jnp.einsum("hqd,hkd->hqk", query, block_keys, preferred_element_type=jnp.float32) * scale
        )
        visible = (key_places[None, None, :] <= places[None, :, None]) & (
            key_places[None, None, :] >= starts[None, :, None]
        )
        masked = jnp.where(visible, scores, -jnp.inf)
        newest = jnp.maximum(running, jnp.max(masked, axis=2))
        factor = jnp.exp(running - newest)
        exponentials = jnp.where(visible, jnp.exp(masked - newest[:, :, None]), 0.0)
        totals = totals * factor + jnp.sum(exponentials, axis=2)
        summed = summed * factor[:, :, None] + jnp.einsum(
            "hqk,hkd->hqd", exponentials.astype(jnp.bfloat16), block_values,
            preferred_element_type=jnp.float32,
        )
        return (newest, totals, summed), None

    initial = (
        jnp.full((heads, count), -1e30, jnp.float32),
        jnp.zeros((heads, count), jnp.float32),
        jnp.zeros((heads, count, size), jnp.float32),
    )
    (running, totals, summed), unused = lax.scan(advance, initial, stacked)
    attended = (summed / totals[:, :, None]).astype(jnp.bfloat16)
    return attended.transpose(1, 0, 2).reshape(count, heads * size)


def in_vmem(count):
    return [pl.BlockSpec(memory_space=pltpu.VMEM)] * count


def per_device(activations, norm_gain, qkv_weight, doc_ids):
    rows, width = activations.shape
    span, local_heads, triple = qkv_weight.shape
    size = triple // 3
    pair = local_heads // 2
    block = 2 * rows
    toks = lax.axis_size("tok")
    tok, row, col = lax.axis_index("tok"), lax.axis_index("row"), lax.axis_index("col")
    chip, core = col >> 1, col & 1
    grid = [(r, c) for r in range(2) for c in range(4)]

    def by_col(value, flip):
        return lax.ppermute(value, "col", [(c, c ^ flip) for c in range(4)])

    def by_row(value):
        return lax.ppermute(value, "row", [(0, 1), (1, 0)])

    def ordered(index, own, other):
        first = index == 0
        return jnp.concatenate([jnp.where(first, own, other), jnp.where(first, other, own)])

    near = lax.ppermute(
        activations,
        ("row", "col"),
        [(r * 4 + c, (c // 2) * 4 + 2 * r + c % 2) for r, c in grid],
    )
    far = lax.ppermute(
        activations,
        ("row", "col"),
        [(r * 4 + c, (c // 2) * 4 + 2 * (1 - r) + c % 2) for r, c in grid],
    )
    widened = activations.astype(jnp.float32)
    squares = jnp.sum(widened * widened, axis=1)
    gain = norm_gain.astype(jnp.float32)
    message = jnp.concatenate([squares, gain])
    message, qkv_weight = lax.optimization_barrier((message, qkv_weight))
    flat_weight = qkv_weight.reshape(span, local_heads * triple)
    got = by_col(message, 1)
    squares = squares + got[:rows]
    gain = ordered(core, gain, got[rows:])
    got = by_col(jnp.concatenate([squares, gain]), 2)
    near, far, got, flat_weight = lax.optimization_barrier((near, far, got, flat_weight))
    near_other, far_other = by_col(near, 1), by_col(far, 1)
    squares = squares + got[:rows]
    gain = jnp.where(chip == row, gain, got[rows:]).reshape(2, 1, width)
    docs = doc_ids.astype(jnp.float32)
    got = by_row(jnp.concatenate([squares, docs]))
    squares = ordered(row, squares, got[:rows]).reshape(block, 1)
    block_docs = ordered(row, docs, got[rows:])
    places = tok * block + jnp.arange(block, dtype=jnp.int32)
    cosine, sine = rotary_tables(places, size)

    def projection(kernel, heads, normalising):
        normed_shape = (jax.ShapeDtypeStruct((2, block, width), jnp.bfloat16),)
        return pl.pallas_call(
            kernel,
            out_shape=(jax.ShapeDtypeStruct((heads, 3, block, size), jnp.float32),)
            + (normed_shape if normalising else ()),
            in_specs=[pl.BlockSpec(memory_space=pltpu.SMEM)]
            + in_vmem(6 if normalising else 1)
            + [pl.BlockSpec(memory_space=pl.ANY)]
            + in_vmem(2),
            out_specs=tuple(in_vmem(2 if normalising else 1)),
            scratch_shapes=[
                pltpu.VMEM((span, heads * triple), jnp.bfloat16),
                pltpu.SemaphoreType.DMA((2,)),
            ],
            compiler_params=pltpu.CompilerParams(vmem_limit_bytes=24 * MIB),
            cost_estimate=pl.CostEstimate(
                flops=2 * block * span * heads * triple,
                bytes_accessed=(2 + heads) * MIB,
                transcendentals=0,
            ),
        )

    away_head, own_head = (1 - row) * pair, row * pair
    away, normed = projection(normalise_project_kernel, 1, True)(
        jnp.stack([core, chip, away_head]), near, far, near_other, far_other, squares, gain,
        flat_weight, cosine, sine,
    )
    arrived = []
    for head in range(pair):
        if head > 0:
            (away,) = projection(project_kernel, 1, False)(
                (away_head + head).reshape(1), normed, flat_weight, cosine, sine
            )
        away, normed = lax.optimization_barrier((away.astype(jnp.float16), normed))
        arrived.append(by_row(away[0]))
    (own,) = projection(project_kernel, pair, False)(
        own_head.reshape(1), normed, flat_weight, cosine, sine
    )

    block_docs, own = lax.optimization_barrier((block_docs, own))
    all_docs = block_docs
    if toks == 4:
        for flip in (1, 2):
            got = lax.ppermute(all_docs, "tok", [(t, t ^ flip) for t in range(4)])
            all_docs = ordered(tok & flip, all_docs, got)
    else:
        all_docs = lax.all_gather(block_docs, "tok", axis=0, tiled=True)
    starts = jnp.sum((all_docs[None, :] < block_docs[:, None]).astype(jnp.int32), axis=1)
    scale = 1.0 / math.sqrt(size)

    queries, key_values = [], []
    for head in range(pair):
        query = (own[head, 0] + arrived[head][0].astype(jnp.float32)).astype(jnp.bfloat16)
        both = (own[head, 1:] + arrived[head][1:].astype(jnp.float32)).astype(jnp.bfloat16)
        if head + 1 < pair:
            query, both, arrived[head + 1] = lax.optimization_barrier(
                (query, both, arrived[head + 1])
            )
        queries.append(query)
        key_values.append(both)
    if toks == 4:
        received = [
            [lax.ppermute(key_values[head], "tok", [(t, t + s) for t in range(4 - s)]) for s in (1, 2, 3)]
            for head in range(pair)
        ]
        key_places = jnp.concatenate(
            [(tok - s) * block + jnp.arange(block, dtype=jnp.int32) for s in range(4)]
        )
        attend = pl.pallas_call(
            lambda *refs: attend_kernel(scale, *refs),
            out_shape=jax.ShapeDtypeStruct((block, size), jnp.bfloat16),
            in_specs=in_vmem(8),
            out_specs=in_vmem(1)[0],
            compiler_params=pltpu.CompilerParams(vmem_limit_bytes=24 * MIB),
            cost_estimate=pl.CostEstimate(
                flops=4 * block * 4 * block * size,
                bytes_accessed=2 * MIB,
                transcendentals=block * 4 * block,
            ),
        )
        attended = [
            attend(
                queries[head], key_values[head], *received[head],
                key_places.reshape(1, 4 * block), places.reshape(block, 1), starts.reshape(block, 1),
            )
            for head in range(pair)
        ]
    else:
        everything = lax.all_gather(jnp.stack(key_values), "tok", axis=2, tiled=True)
        together = attend_gathered(
            jnp.stack(queries), everything[:, 0], everything[:, 1], places, starts, scale
        )
        attended = [together[:, head * size : (head + 1) * size] for head in range(pair)]

    mine, theirs = [], []
    for one in attended:
        mine.append(jnp.where(row == 0, one[:rows], one[rows:]))
        theirs.append(by_row(jnp.where(row == 0, one[rows:], one[:rows])))
    return jnp.concatenate(
        [jnp.where(row == 0, a, b) for a, b in zip(mine + theirs, theirs + mine)], axis=1
    )


def solution(mesh):
    placed = (P(("tok", "row"), "col"), P("col"), P("row", "col", None), P(("tok", "row")))
    return jax.shard_map(
        per_device, mesh=mesh, in_specs=placed, out_specs=P(("tok", "row"), "col"), check_vma=False
    )
```

profile of v0, /device:TPU:24, one launch (start us, length us, event | category | flops | bytes accessed | tf_op | source)
XLA Modules:
  0.0 86.0 jit_solution(18020542533382394052)
XLA Ops:
  0.0 1.8 %collective-permute-start.1 = (bf16[176,1024]{1,0:T(8,128)(2,1)}, bf16[176,1024]{1,0:T(8,128)(2,1)S(1)}, u32[]{:S(2)}, u32[]{:S(2)}) collective-permute-start(bf16[176,1024]{1,0:T(8,128)(2,1)} %param.4), channel_id=1, source_target_pairs={{0,0},{1,1},{2,4},{3,5},{4,2},{5,3},{6,6},{7,7},{8,8},{9,9},{10,12... | collective-permute-start | bytes 1081352 | tf_op jit(solution)/shard_map/ppermute | solution.py:178
  1.8 3.3 %collective-permute-start.2 = (bf16[176,1024]{1,0:T(8,128)(2,1)}, bf16[176,1024]{1,0:T(8,128)(2,1)S(1)}, u32[]{:S(2)}, u32[]{:S(2)}) collective-permute-start(bf16[176,1024]{1,0:T(8,128)(2,1)} %param.4), channel_id=1, source_target_pairs={{0,2},{1,3},{2,6},{3,7},{4,0},{5,1},{6,4},{7,5},{8,10},{9,11},{10,... | collective-permute-start | bytes 1081352 | tf_op jit(solution)/shard_map/ppermute | solution.py:183
  5.1 1.2 %multiply_reduce_fusion = f32[176]{0:T(256)S(1)} fusion(bf16[176,1024]{1,0:T(8,128)(2,1)} %param.4), kind=kLoop, calls=%fused_computation.1 | loop fusion | flops 540496 | bytes 361152 | tf_op jit(solution)/shard_map/reduce_sum | solution.py:189
  6.2 0.7 convert_element_type.64
  7.1 0.7 fusion.4
  7.8 0.1 pad_maximum_fusion.cos_ref
  7.9 0.1 pad_maximum_fusion.1.sin_ref
  8.0 0.1 collective-permute-done
  8.3 0.1 concatenate.49
  8.4 0.1 pad_add_fusion.place_ref
  8.4 6.6 %copy.11 = bf16[256,8,4,384]{3,1,2,0:T(8,128)(2,1)} copy(bf16[256,8,4,384]{3,2,1,0:T(4,128)(2,1)} %bitcast.35) | data formatting | bytes 12582912
  15.2 2.0 %collective-permute-start.4 = (f32[352]{0:T(512)S(1)}, f32[352]{0:T(512)S(1)}, u32[]{:S(2)}, u32[]{:S(2)}) collective-permute-start(f32[352]{0:T(512)S(1)} %pad_maximum_fusion.6), channel_id=1, source_target_pairs={{0,4},{4,0},{1,5},{5,1},{2,6},{6,2},{3,7},{7,3},{8,12},{12,8},{9,1... | collective-permute-start | bytes 4232 | tf_op jit(solution)/shard_map/ppermute | solution.py:172
  17.2 0.5 collective-permute-start.6
  17.8 1.1 %collective-permute-done.4 = f32[352]{0:T(512)S(1)} collective-permute-done((f32[352]{0:T(512)S(1)}, f32[352]{0:T(512)S(1)}, u32[]{:S(2)}, u32[]{:S(2)}) %collective-permute-start.4) | collective-permute-done | bytes 1440 | tf_op jit(solution)/shard_map/ppermute | solution.py:172
  19.0 0.1 reshape.90.squares_ref
  19.1 0.1 pad_maximum_fusion.7
  19.2 0.2 collective-permute-done.6.b_far
  19.4 2.8 %copy-done = bf16[256,8,4,384]{3,1,2,0:T(8,128)(2,1)S(1)} copy-done((bf16[256,8,4,384]{3,1,2,0:T(8,128)(2,1)S(1)}, bf16[256,8,4,384]{3,1,2,0:T(8,128)(2,1)}, u32[]{:S(2)}) %copy-start) | copy-done | bytes 6291480
  22.2 2.1 %shard_map.46 = (f32[1,3,352,128]{3,2,1,0:T(8,128)S(1)}, bf16[2,352,1024]{2,1,0:T(8,128)(2,1)S(1)}) custom-call(s32[3]{0:T(128)S(1)} %pad_add_fusion.place_ref, bf16[176,1024]{1,0:T(8,128)(2,1)S(1)} %collective-permute-done.1.a_near, bf16[176,1024]{1,0:T(8,128)(2,1)S(1)} %collective-permute-done.2.a_far, ...), custom_call_target="tpu_custom_call" | custom-call | flops 553648128 | bytes 3145728 | tf_op jit(solution)/shard_map/pallas_call | solution.py:233
  24.4 0.6 copy-done.1
  25.0 1.2 %shard_map.47 = f32[1,3,352,128]{3,2,1,0:T(8,128)S(1)} custom-call(s32[1]{0:T(128)} %bitcast.1.place_ref, bf16[2,352,1024]{2,1,0:T(8,128)(2,1)S(1)} %get-tuple-element.31.normed_ref, bf16[2048,1536]{1,0:T(8,128)(2,1)S(1)} %bitcast.33, f32[352,128]{1,0:T(8,128)S(1)} %pad_maximum_fusion.cos_ref, f32[352,128]{1,0:T(8,128)S(1)} %pad_maximum_fusion.1.sin_ref), custom_call_target="tpu_custom_call" | custom-call | flops 553648128 | bytes 3145728 | tf_op jit(solution)/shard_map/pallas_call | solution.py:240
  26.2 2.0 %shard_map.48 = f32[2,3,352,128]{3,2,1,0:T(8,128)S(1)} custom-call(s32[1]{0:T(128)} %bitcast.place_ref, bf16[2,352,1024]{2,1,0:T(8,128)(2,1)S(1)} %get-tuple-element.31.normed_ref, bf16[2048,1536]{1,0:T(8,128)(2,1)S(1)} %bitcast.34, f32[352,128]{1,0:T(8,128)S(1)} %pad_maximum_fusion.cos_ref, f32[352,128]{1,0:T(8,128)S(1)} %pad_maximum_fusion.1.sin_ref), custom_call_target="tpu_custom_call" | custom-call | flops 1107296256 | bytes 4194304 | tf_op jit(solution)/shard_map/pallas_call | solution.py:245
  28.2 0.5 collective-permute-start.12
  28.7 3.1 %collective-permute-done.12 = f32[352]{0:T(512)S(1)} collective-permute-done((f32[352]{0:T(512)S(1)}, f32[352]{0:T(512)S(1)}, u32[]{:S(2)}, u32[]{:S(2)}) %collective-permute-start.12) | collective-permute-done | bytes 1440 | tf_op jit(solution)/shard_map/ppermute | solution.py:253
  31.9 0.1 pad_maximum_fusion.5
  32.0 0.3 collective-permute-start.13
  32.3 0.1 concatenate.58
  32.4 1.8 %collective-permute-start.7 = (f16[3,352,128]{2,1,0:T(8,128)(2,1)S(1)}, f16[3,352,128]{2,1,0:T(8,128)(2,1)S(1)}, u32[]{:S(2)}, u32[]{:S(2)}) collective-permute-start(f16[3,352,128]{2,1,0:T(8,128)(2,1)S(1)} %bitcast.37), channel_id=1, source_target_pairs={{0,4},{4,0},{1,5},{5,1},{2,6},{6,2},{3,7},{7,3},{8,12},{12,8},{9,1... | collective-permute-start | bytes 811016 | tf_op jit(solution)/shard_map/ppermute | solution.py:172
  34.2 0.3 collective-permute-start.8
  34.5 2.0 %collective-permute-done.13 = f32[704]{0:T(1024)S(1)} collective-permute-done((f32[704]{0:T(1024)S(1)}, f32[704]{0:T(1024)S(1)}, u32[]{:S(2)}, u32[]{:S(2)}) %collective-permute-start.13) | collective-permute-done | bytes 2848 | tf_op jit(solution)/shard_map/ppermute | solution.py:253
  36.5 0.1 pad_maximum_fusion.4
  36.6 0.4 convert_reduce_fusion
  37.0 0.1 reshape.91.refs_7_
  37.1 4.8 %collective-permute-done.7 = f16[3,352,128]{2,1,0:T(8,128)(2,1)S(1)} collective-permute-done((f16[3,352,128]{2,1,0:T(8,128)(2,1)S(1)}, f16[3,352,128]{2,1,0:T(8,128)(2,1)S(1)}, u32[]{:S(2)}, u32[]{:S(2)}) %collective-permute-start.7) | collective-permute-done | bytes 270368 | tf_op jit(solution)/shard_map/ppermute | solution.py:172
  42.0 3.4 %collective-permute-done.8 = f16[3,352,128]{2,1,0:T(8,128)(2,1)S(1)} collective-permute-done((f16[3,352,128]{2,1,0:T(8,128)(2,1)S(1)}, f16[3,352,128]{2,1,0:T(8,128)(2,1)S(1)}, u32[]{:S(2)}, u32[]{:S(2)}) %collective-permute-start.8) | collective-permute-done | bytes 270368 | tf_op jit(solution)/shard_map/ppermute | solution.py:172
  45.4 1.3 %collective-permute-start.15 = (bf16[2,352,128]{2,1,0:T(8,128)(2,1)S(1)}, bf16[2,352,128]{2,1,0:T(8,128)(2,1)S(1)}, u32[]{:S(2)}, u32[]{:S(2)}) collective-permute-start(bf16[2,352,128]{2,1,0:T(8,128)(2,1)S(1)} %fusion.refs_1_), channel_id=1, source_target_pairs={{0,8},{8,16},{16,24},{1,9},{9,17},{17,25},{2,10},{10,18},{18,26},{... | collective-permute-start | bytes 540680 | tf_op jit(solution)/shard_map/ppermute | solution.py:272
  46.7 1.3 %collective-permute-start.16 = (bf16[2,352,128]{2,1,0:T(8,128)(2,1)S(1)}, bf16[2,352,128]{2,1,0:T(8,128)(2,1)S(1)}, u32[]{:S(2)}, u32[]{:S(2)}) collective-permute-start(bf16[2,352,128]{2,1,0:T(8,128)(2,1)S(1)} %fusion.refs_1_), channel_id=1, source_target_pairs={{0,16},{8,24},{1,17},{9,25},{2,18},{10,26},{3,19},{11,27},{4,20},{... | collective-permute-start | bytes 540680 | tf_op jit(solution)/shard_map/ppermute | solution.py:272
  48.0 1.3 %collective-permute-start.17 = (bf16[2,352,128]{2,1,0:T(8,128)(2,1)S(1)}, bf16[2,352,128]{2,1,0:T(8,128)(2,1)S(1)}, u32[]{:S(2)}, u32[]{:S(2)}) collective-permute-start(bf16[2,352,128]{2,1,0:T(8,128)(2,1)S(1)} %fusion.refs_1_), channel_id=1, source_target_pairs={{0,24},{1,25},{2,26},{3,27},{4,28},{5,29},{6,30},{7,31}} | collective-permute-start | bytes 540680 | tf_op jit(solution)/shard_map/ppermute | solution.py:272
  49.3 1.3 %collective-permute-start.9 = (bf16[2,352,128]{2,1,0:T(8,128)(2,1)S(1)}, bf16[2,352,128]{2,1,0:T(8,128)(2,1)S(1)}, u32[]{:S(2)}, u32[]{:S(2)}) collective-permute-start(bf16[2,352,128]{2,1,0:T(8,128)(2,1)S(1)} %fusion.1.refs_1_), channel_id=1, source_target_pairs={{0,8},{8,16},{16,24},{1,9},{9,17},{17,25},{2,10},{10,18},{18,26},{... | collective-permute-start | bytes 540680 | tf_op jit(solution)/shard_map/ppermute | solution.py:272
  50.6 1.3 %collective-permute-start.10 = (bf16[2,352,128]{2,1,0:T(8,128)(2,1)S(1)}, bf16[2,352,128]{2,1,0:T(8,128)(2,1)S(1)}, u32[]{:S(2)}, u32[]{:S(2)}) collective-permute-start(bf16[2,352,128]{2,1,0:T(8,128)(2,1)S(1)} %fusion.1.refs_1_), channel_id=1, source_target_pairs={{0,16},{8,24},{1,17},{9,25},{2,18},{10,26},{3,19},{11,27},{4,20},{... | collective-permute-start | bytes 540680 | tf_op jit(solution)/shard_map/ppermute | solution.py:272
  51.9 6.0 %collective-permute-done.15.refs_2_ = bf16[2,352,128]{2,1,0:T(8,128)(2,1)S(1)} collective-permute-done((bf16[2,352,128]{2,1,0:T(8,128)(2,1)S(1)}, bf16[2,352,128]{2,1,0:T(8,128)(2,1)S(1)}, u32[]{:S(2)}, u32[]{:S(2)}) %collective-permute-start.15) | collective-permute-done | bytes 180256 | tf_op jit(solution)/shard_map/ppermute | solution.py:272
  57.9 1.3 %collective-permute-start.11 = (bf16[2,352,128]{2,1,0:T(8,128)(2,1)S(1)}, bf16[2,352,128]{2,1,0:T(8,128)(2,1)S(1)}, u32[]{:S(2)}, u32[]{:S(2)}) collective-permute-start(bf16[2,352,128]{2,1,0:T(8,128)(2,1)S(1)} %fusion.1.refs_1_), channel_id=1, source_target_pairs={{0,24},{1,25},{2,26},{3,27},{4,28},{5,29},{6,30},{7,31}} | collective-permute-start | bytes 540680 | tf_op jit(solution)/shard_map/ppermute | solution.py:272
  59.2 15.4 %collective-permute-done.16.refs_3_ = bf16[2,352,128]{2,1,0:T(8,128)(2,1)S(1)} collective-permute-done((bf16[2,352,128]{2,1,0:T(8,128)(2,1)S(1)}, bf16[2,352,128]{2,1,0:T(8,128)(2,1)S(1)}, u32[]{:S(2)}, u32[]{:S(2)}) %collective-permute-start.16) | collective-permute-done | bytes 180256 | tf_op jit(solution)/shard_map/ppermute | solution.py:272
  74.7 1.8 %shard_map.50 = bf16[352,128]{1,0:T(8,128)(2,1)S(1)} custom-call(bf16[352,128]{1,0:T(8,128)(2,1)S(1)} %fusion.2.refs_0_, bf16[2,352,128]{2,1,0:T(8,128)(2,1)S(1)} %fusion.refs_1_, bf16[2,352,128]{2,1,0:T(8,128)(2,1)S(1)} %collective-permute-done.15.refs_2_, bf16[2,352,128]{2,1,0:T(8,128)(2,1)S(1)} %collective-permute-done.16.refs_3_, ...), custom_call_target="tpu_custom_call" | custom-call | flops 253755392 | bytes 2097152 | tf_op jit(solution)/shard_map/pallas_call | solution.py:291
  76.5 2.9 %collective-permute-done.10.refs_3_ = bf16[2,352,128]{2,1,0:T(8,128)(2,1)S(1)} collective-permute-done((bf16[2,352,128]{2,1,0:T(8,128)(2,1)S(1)}, bf16[2,352,128]{2,1,0:T(8,128)(2,1)S(1)}, u32[]{:S(2)}, u32[]{:S(2)}) %collective-permute-start.10) | collective-permute-done | bytes 180256 | tf_op jit(solution)/shard_map/ppermute | solution.py:272
  79.4 1.8 %shard_map.49 = bf16[352,128]{1,0:T(8,128)(2,1)S(1)} custom-call(bf16[352,128]{1,0:T(8,128)(2,1)S(1)} %fusion.3.refs_0_, bf16[2,352,128]{2,1,0:T(8,128)(2,1)S(1)} %fusion.1.refs_1_, bf16[2,352,128]{2,1,0:T(8,128)(2,1)S(1)} %collective-permute-done.9.refs_2_, bf16[2,352,128]{2,1,0:T(8,128)(2,1)S(1)} %collective-permute-done.10.refs_3_, ...), custom_call_target="tpu_custom_call" | custom-call | flops 253755392 | bytes 2097152 | tf_op jit(solution)/shard_map/pallas_call | solution.py:291
  81.3 4.0 %collective-permute-done.14 = bf16[176,128]{1,0:T(8,128)(2,1)S(1)} collective-permute-done((bf16[176,128]{1,0:T(8,128)(2,1)S(1)}, bf16[176,128]{1,0:T(8,128)(2,1)S(1)}, u32[]{:S(2)}, u32[]{:S(2)}) %collective-permute-start.14) | collective-permute-done | bytes 45088 | tf_op jit(solution)/shard_map/ppermute | solution.py:172
  85.3 0.7 pad_maximum_fusion.2
  (47 shorter events, 1.1 us)
Async XLA Ops:
  0.0 8.2 %copy-start.2 = (bf16[1024]{0:T(1024)(128)(2,1)S(1)}, bf16[1024]{0:T(1024)(128)(2,1)}, u32[]{:S(2)}) copy-start(bf16[1024]{0:T(1024)(128)(2,1)} %param.5) | copy-start | bytes 6148
  0.0 15.1 %collective-permute-start.1 = (bf16[176,1024]{1,0:T(8,128)(2,1)}, bf16[176,1024]{1,0:T(8,128)(2,1)S(1)}, u32[]{:S(2)}, u32[]{:S(2)}) collective-permute-start(bf16[176,1024]{1,0:T(8,128)(2,1)} %param.4), channel_id=1, source_target_pairs={{0,0},{1,1},{2,4},{3,5},{4,2},{5,3},{6,6},{7,7},{8,8},{9,9},{10,12... | collective-permute-start | bytes 1081352 | tf_op jit(solution)/shard_map/ppermute | solution.py:178
  1.8 13.3 %collective-permute-start.2 = (bf16[176,1024]{1,0:T(8,128)(2,1)}, bf16[176,1024]{1,0:T(8,128)(2,1)S(1)}, u32[]{:S(2)}, u32[]{:S(2)}) collective-permute-start(bf16[176,1024]{1,0:T(8,128)(2,1)} %param.4), channel_id=1, source_target_pairs={{0,2},{1,3},{2,6},{3,7},{4,0},{5,1},{6,4},{7,5},{8,10},{9,11},{10,... | collective-permute-start | bytes 1081352 | tf_op jit(solution)/shard_map/ppermute | solution.py:183
  7.0 1.2 %collective-permute-start = (f32[1200]{0:T(1024)S(1)}, f32[1200]{0:T(1024)S(1)}, u32[]{:S(2)}, u32[]{:S(2)}) collective-permute-start(f32[1200]{0:T(1024)S(1)} %pad_maximum_fusion.3), channel_id=1, source_target_pairs={{0,1},{1,0},{2,3},{3,2},{4,5},{5,4},{6,7},{7,6},{8,9},{9,8},{10,11... | collective-permute-start | bytes 14408 | tf_op jit(solution)/shard_map/ppermute | solution.py:169
  8.3 6.7 %collective-permute-start.3 = (f32[2224]{0:T(1024)S(1)}, f32[2224]{0:T(1024)S(1)}, u32[]{:S(2)}, u32[]{:S(2)}) collective-permute-start(f32[2224]{0:T(1024)S(1)} %concatenate.49), channel_id=1, source_target_pairs={{0,2},{1,3},{2,0},{3,1},{4,6},{5,7},{6,4},{7,5},{8,10},{9,11},{10,... | collective-permute-start | bytes 26696 | tf_op jit(solution)/shard_map/ppermute | solution.py:169
  8.4 6.6 %copy-start.3 = (s32[176]{0:T(256)S(1)}, s32[176]{0:T(256)}, u32[]{:S(2)}) copy-start(s32[176]{0:T(256)} %param.7) | copy-start | bytes 2116
  15.2 3.6 %collective-permute-start.4 = (f32[352]{0:T(512)S(1)}, f32[352]{0:T(512)S(1)}, u32[]{:S(2)}, u32[]{:S(2)}) collective-permute-start(f32[352]{0:T(512)S(1)} %pad_maximum_fusion.6), channel_id=1, source_target_pairs={{0,4},{4,0},{1,5},{5,1},{2,6},{6,2},{3,7},{7,3},{8,12},{12,8},{9,1... | collective-permute-start | bytes 4232 | tf_op jit(solution)/shard_map/ppermute | solution.py:172
  17.2 1.9 %collective-permute-start.5 = (bf16[176,1024]{1,0:T(8,128)(2,1)S(1)}, bf16[176,1024]{1,0:T(8,128)(2,1)S(1)}, u32[]{:S(2)}, u32[]{:S(2)}) collective-permute-start(bf16[176,1024]{1,0:T(8,128)(2,1)S(1)} %collective-permute-done.1.a_near), channel_id=1, source_target_pairs={{0,1},{1,0},{2,3},{3,2},{4,5},{5,4},{6,7},{7,6},{8,9},{9,8},{10,11... | collective-permute-start | bytes 1081352 | tf_op jit(solution)/shard_map/ppermute | solution.py:169
  17.2 2.2 %collective-permute-start.6 = (bf16[176,1024]{1,0:T(8,128)(2,1)S(1)}, bf16[176,1024]{1,0:T(8,128)(2,1)S(1)}, u32[]{:S(2)}, u32[]{:S(2)}) collective-permute-start(bf16[176,1024]{1,0:T(8,128)(2,1)S(1)} %collective-permute-done.2.a_far), channel_id=1, source_target_pairs={{0,1},{1,0},{2,3},{3,2},{4,5},{5,4},{6,7},{7,6},{8,9},{9,8},{10,11... | collective-permute-start | bytes 1081352 | tf_op jit(solution)/shard_map/ppermute | solution.py:169
  19.4 2.8 %copy-start = (bf16[256,8,4,384]{3,1,2,0:T(8,128)(2,1)S(1)}, bf16[256,8,4,384]{3,1,2,0:T(8,128)(2,1)}, u32[]{:S(2)}) copy-start(bf16[256,8,4,384]{3,1,2,0:T(8,128)(2,1)} %copy.11) | copy-start | bytes 18874372
  22.2 2.8 %copy-start.1 = (bf16[256,8,4,384]{3,1,2,0:T(8,128)(2,1)S(1)}, bf16[256,8,4,384]{3,1,2,0:T(8,128)(2,1)}, u32[]{:S(2)}) copy-start(bf16[256,8,4,384]{3,1,2,0:T(8,128)(2,1)} %copy.11) | copy-start | bytes 18874372
  28.2 3.7 %collective-permute-start.12 = (f32[352]{0:T(512)S(1)}, f32[352]{0:T(512)S(1)}, u32[]{:S(2)}, u32[]{:S(2)}) collective-permute-start(f32[352]{0:T(512)S(1)} %pad_maximum_fusion.7), channel_id=1, source_target_pairs={{0,8},{8,0},{16,24},{24,16},{1,9},{9,1},{17,25},{25,17},{2,10},{10... | collective-permute-start | bytes 4232 | tf_op jit(solution)/shard_map/ppermute | solution.py:253
  32.0 4.5 %collective-permute-start.13 = (f32[704]{0:T(1024)S(1)}, f32[704]{0:T(1024)S(1)}, u32[]{:S(2)}, u32[]{:S(2)}) collective-permute-start(f32[704]{0:T(1024)S(1)} %pad_maximum_fusion.5), channel_id=1, source_target_pairs={{0,16},{8,24},{16,0},{24,8},{1,17},{9,25},{17,1},{25,9},{2,18},{10... | collective-permute-start | bytes 8456 | tf_op jit(solution)/shard_map/ppermute | solution.py:253
  32.4 9.5 %collective-permute-start.7 = (f16[3,352,128]{2,1,0:T(8,128)(2,1)S(1)}, f16[3,352,128]{2,1,0:T(8,128)(2,1)S(1)}, u32[]{:S(2)}, u32[]{:S(2)}) collective-permute-start(f16[3,352,128]{2,1,0:T(8,128)(2,1)S(1)} %bitcast.37), channel_id=1, source_target_pairs={{0,4},{4,0},{1,5},{5,1},{2,6},{6,2},{3,7},{7,3},{8,12},{12,8},{9,1... | collective-permute-start | bytes 811016 | tf_op jit(solution)/shard_map/ppermute | solution.py:172
  34.2 11.1 %collective-permute-start.8 = (f16[3,352,128]{2,1,0:T(8,128)(2,1)S(1)}, f16[3,352,128]{2,1,0:T(8,128)(2,1)S(1)}, u32[]{:S(2)}, u32[]{:S(2)}) collective-permute-start(f16[3,352,128]{2,1,0:T(8,128)(2,1)S(1)} %bitcast.36), channel_id=1, source_target_pairs={{0,4},{4,0},{1,5},{5,1},{2,6},{6,2},{3,7},{7,3},{8,12},{12,8},{9,1... | collective-permute-start | bytes 811016 | tf_op jit(solution)/shard_map/ppermute | solution.py:172
  45.4 12.5 %collective-permute-start.15 = (bf16[2,352,128]{2,1,0:T(8,128)(2,1)S(1)}, bf16[2,352,128]{2,1,0:T(8,128)(2,1)S(1)}, u32[]{:S(2)}, u32[]{:S(2)}) collective-permute-start(bf16[2,352,128]{2,1,0:T(8,128)(2,1)S(1)} %fusion.refs_1_), channel_id=1, source_target_pairs={{0,8},{8,16},{16,24},{1,9},{9,17},{17,25},{2,10},{10,18},{18,26},{... | collective-permute-start | bytes 540680 | tf_op jit(solution)/shard_map/ppermute | solution.py:272
  46.7 28.0 %collective-permute-start.16 = (bf16[2,352,128]{2,1,0:T(8,128)(2,1)S(1)}, bf16[2,352,128]{2,1,0:T(8,128)(2,1)S(1)}, u32[]{:S(2)}, u32[]{:S(2)}) collective-permute-start(bf16[2,352,128]{2,1,0:T(8,128)(2,1)S(1)} %fusion.refs_1_), channel_id=1, source_target_pairs={{0,16},{8,24},{1,17},{9,25},{2,18},{10,26},{3,19},{11,27},{4,20},{... | collective-permute-start | bytes 540680 | tf_op jit(solution)/shard_map/ppermute | solution.py:272
  48.0 26.7 %collective-permute-start.17 = (bf16[2,352,128]{2,1,0:T(8,128)(2,1)S(1)}, bf16[2,352,128]{2,1,0:T(8,128)(2,1)S(1)}, u32[]{:S(2)}, u32[]{:S(2)}) collective-permute-start(bf16[2,352,128]{2,1,0:T(8,128)(2,1)S(1)} %fusion.refs_1_), channel_id=1, source_target_pairs={{0,24},{1,25},{2,26},{3,27},{4,28},{5,29},{6,30},{7,31}} | collective-permute-start | bytes 540680 | tf_op jit(solution)/shard_map/ppermute | solution.py:272
  49.3 27.2 %collective-permute-start.9 = (bf16[2,352,128]{2,1,0:T(8,128)(2,1)S(1)}, bf16[2,352,128]{2,1,0:T(8,128)(2,1)S(1)}, u32[]{:S(2)}, u32[]{:S(2)}) collective-permute-start(bf16[2,352,128]{2,1,0:T(8,128)(2,1)S(1)} %fusion.1.refs_1_), channel_id=1, source_target_pairs={{0,8},{8,16},{16,24},{1,9},{9,17},{17,25},{2,10},{10,18},{18,26},{... | collective-permute-start | bytes 540680 | tf_op jit(solution)/shard_map/ppermute | solution.py:272
  50.6 28.8 %collective-permute-start.10 = (bf16[2,352,128]{2,1,0:T(8,128)(2,1)S(1)}, bf16[2,352,128]{2,1,0:T(8,128)(2,1)S(1)}, u32[]{:S(2)}, u32[]{:S(2)}) collective-permute-start(bf16[2,352,128]{2,1,0:T(8,128)(2,1)S(1)} %fusion.1.refs_1_), channel_id=1, source_target_pairs={{0,16},{8,24},{1,17},{9,25},{2,18},{10,26},{3,19},{11,27},{4,20},{... | collective-permute-start | bytes 540680 | tf_op jit(solution)/shard_map/ppermute | solution.py:272
  57.9 21.5 %collective-permute-start.11 = (bf16[2,352,128]{2,1,0:T(8,128)(2,1)S(1)}, bf16[2,352,128]{2,1,0:T(8,128)(2,1)S(1)}, u32[]{:S(2)}, u32[]{:S(2)}) collective-permute-start(bf16[2,352,128]{2,1,0:T(8,128)(2,1)S(1)} %fusion.1.refs_1_), channel_id=1, source_target_pairs={{0,24},{1,25},{2,26},{3,27},{4,28},{5,29},{6,30},{7,31}} | collective-permute-start | bytes 540680 | tf_op jit(solution)/shard_map/ppermute | solution.py:272
  76.5 4.8 %collective-permute-start.18 = (bf16[176,128]{1,0:T(8,128)(2,1)S(1)}, bf16[176,128]{1,0:T(8,128)(2,1)S(1)}, u32[]{:S(2)}, u32[]{:S(2)}) collective-permute-start(bf16[176,128]{1,0:T(8,128)(2,1)S(1)} %broadcast_select_fusion.3), channel_id=1, source_target_pairs={{0,4},{4,0},{1,5},{5,1},{2,6},{6,2},{3,7},{7,3},{8,12},{12,8},{9,1... | collective-permute-start | bytes 135176 | tf_op jit(solution)/shard_map/ppermute | solution.py:172
  81.2 4.1 %collective-permute-start.14 = (bf16[176,128]{1,0:T(8,128)(2,1)S(1)}, bf16[176,128]{1,0:T(8,128)(2,1)S(1)}, u32[]{:S(2)}, u32[]{:S(2)}) collective-permute-start(bf16[176,128]{1,0:T(8,128)(2,1)S(1)} %broadcast_select_fusion.6), channel_id=1, source_target_pairs={{0,4},{4,0},{1,5},{5,1},{2,6},{6,2},{3,7},{7,3},{8,12},{12,8},{9,1... | collective-permute-start | bytes 135176 | tf_op jit(solution)/shard_map/ppermute | solution.py:172
where the time goes:
time: 86.5 us; the launch traced here: 86 us
  waiting for transfers between devices  43.1 us (50%)
  starting transfers between devices  18.4 us (21%)
  local copies, waits for them, and re-layouts  10.5 us (12%)
  Pallas kernels  8.84 us (10%)
  other arithmetic  4.92 us (6%)
    ppermute x6, waiting for transfers between devices, per_device(): lax.ppermute(key_values[head], 'tok', [(t, t + s) for t in range(4 - s)])  24.3 us
    ppermute x5, waiting for transfers between devices, by_row(): return lax.ppermute(value, 'row', [(0, 1), (1, 0)])  13.3 us
    unnamed x9, local copies, waits for them, and re-layouts  10 us
    ppermute x6, starting transfers between devices, per_device(): lax.ppermute(key_values[head], 'tok', [(t, t + s) for t in range(4 - s)])  7.74 us
    ppermute x2, waiting for transfers between devices, per_device(): got = lax.ppermute(all_docs, 'tok', [(t, t ^ flip) for t in range(4)])  5.11 us
    ppermute x5, starting transfers between devices, by_row(): return lax.ppermute(value, 'row', [(0, 1), (1, 0)])  4.23 us
    pallas_call x2, Pallas kernels, per_device(): attend(queries[head], key_values[head], *received[head], key_places.resha...  3.54 us
    ppermute x1, starting transfers between devices, per_device(): lax.ppermute(activations, ('row', 'col'), [(r * 4 + c, c // 2 * 4 + 2 * (...  3.31 us
  transfers between devices with their start and end apart: 19, of which 11 were waited for; matrix products, arithmetic and copies ran while one was open for 13% of the time, Pallas kernels for 4%

commit v1 on v0

--- a/solution.py
+++ b/solution.py
@@ -194,15 +194,26 @@
     got = by_col(message, 1)
     squares = squares + got[:rows]
     gain = ordered(core, gain, got[rows:])
+    docs = doc_ids.astype(jnp.float32)
+    if toks == 4:
+        for flip in (1, 2):
+            other = lax.ppermute(docs, "tok", [(t, t ^ flip) for t in range(4)])
+            docs = ordered(tok & flip, docs, other)
     got = by_col(jnp.concatenate([squares, gain]), 2)
-    near, far, got, flat_weight = lax.optimization_barrier((near, far, got, flat_weight))
+    near, far, got, docs, flat_weight = lax.optimization_barrier(
+        (near, far, got, docs, flat_weight)
+    )
     near_other, far_other = by_col(near, 1), by_col(far, 1)
     squares = squares + got[:rows]
     gain = jnp.where(chip == row, gain, got[rows:]).reshape(2, 1, width)
-    docs = doc_ids.astype(jnp.float32)
     got = by_row(jnp.concatenate([squares, docs]))
     squares = ordered(row, squares, got[:rows]).reshape(block, 1)
-    block_docs = ordered(row, docs, got[rows:])
+    row_docs = [jnp.where(row == r, docs, got[rows:]).reshape(-1, rows) for r in range(2)]
+    all_docs = jnp.stack(row_docs, axis=1).reshape(-1)
+    if toks != 4:
+        all_docs = lax.all_gather(all_docs, "tok", axis=0, tiled=True)
+    block_docs = lax.dynamic_slice_in_dim(all_docs, tok * block, block, 0)
+    starts = jnp.sum((all_docs[None, :] < block_docs[:, None]).astype(jnp.int32), axis=1)
     places = tok * block + jnp.arange(block, dtype=jnp.int32)
     cosine, sine = rotary_tables(places, size)
 
@@ -214,7 +225,7 @@
             + (normed_shape if normalising else ()),
             in_specs=[pl.BlockSpec(memory_space=pltpu.SMEM)]
             + in_vmem(6 if normalising else 1)
-            + [pl.BlockSpec(memory_space=pl.ANY)]
+            + [pl.BlockSpec(memory_space=pltpu.HBM)]
             + in_vmem(2),
             out_specs=tuple(in_vmem(2 if normalising else 1)),
             scratch_shapes=[
@@ -222,11 +233,7 @@
                 pltpu.SemaphoreType.DMA((2,)),
             ],
             compiler_params=pltpu.CompilerParams(vmem_limit_bytes=24 * MIB),
-            cost_estimate=pl.CostEstimate(
-                flops=2 * block * span * heads * triple,
-                bytes_accessed=(2 + heads) * MIB,
-                transcendentals=0,
-            ),
+            cost_estimate=pl.CostEstimate(flops=0, bytes_accessed=0, transcendentals=0),
         )
 
     away_head, own_head = (1 - row) * pair, row * pair
@@ -246,32 +253,23 @@
         own_head.reshape(1), normed, flat_weight, cosine, sine
     )
 
-    block_docs, own = lax.optimization_barrier((block_docs, own))
-    all_docs = block_docs
+    scale = 1.0 / math.sqrt(size)
+
+    queries, key_values, received = [], [], []
+    for head in range(pair):
+        sums = arrived[head].astype(jnp.float32)
+        if toks == 4 and head > 0:
+            sums = jnp.where(tok < toks, sums, received[-1][0][0, 0, 0].astype(jnp.float32))
+        queries.append((own[head, 0] + sums[0]).astype(jnp.bfloat16))
+        key_values.append((own[head, 1:] + sums[1:]).astype(jnp.bfloat16))
+        if toks == 4:
+            received.append(
+                [
+                    lax.ppermute(key_values[head], "tok", [(t, t + s) for t in range(4 - s)])
+                    for s in (1, 2, 3)
+                ]
+            )
     if toks == 4:
-        for flip in (1, 2):
-            got = lax.ppermute(all_docs, "tok", [(t, t ^ flip) for t in range(4)])
-            all_docs = ordered(tok & flip, all_docs, got)
-    else:
-        all_docs = lax.all_gather(block_docs, "tok", axis=0, tiled=True)
-    starts = jnp.sum((all_docs[None, :] < block_docs[:, None]).astype(jnp.int32), axis=1)
-    scale = 1.0 / math.sqrt(size)
-
-    queries, key_values = [], []
-    for head in range(pair):
-        query = (own[head, 0] + arrived[head][0].astype(jnp.float32)).astype(jnp.bfloat16)
-        both = (own[head, 1:] + arrived[head][1:].astype(jnp.float32)).astype(jnp.bfloat16)
-        if head + 1 < pair:
-            query, both, arrived[head + 1] = lax.optimization_barrier(
-                (query, both, arrived[head + 1])
-            )
-        queries.append(query)
-        key_values.append(both)
-    if toks == 4:
-        received = [
-            [lax.ppermute(key_values[head], "tok", [(t, t + s) for t in range(4 - s)]) for s in (1, 2, 3)]
-            for head in range(pair)
-        ]
         key_places = jnp.concatenate(
             [(tok - s) * block + jnp.arange(block, dtype=jnp.int32) for s in range(4)]
         )

time: 86.5 us -> 83.8 us (0.969)
  waiting for transfers between devices: 43.1 us -> 35 us
  other arithmetic: 4.92 us -> 8.17 us
  local copies, waits for them, and re-layouts: 10.5 us -> 13.5 us
  starting transfers between devices: 18.4 us -> 16.9 us
    ppermute x5, waiting for transfers between devices: 13.3 us -> 7.35 us  [by_row(): return lax.ppermute(value, 'row', [(0, 1), (1, 0)])]
    ppermute x4, waiting for transfers between devices: 0.39 us -> 3.62 us  [by_col(): return lax.ppermute(value, 'col', [(c, c ^ flip) for c in range(4)])]
    ppermute x2, waiting for transfers between devices: 5.11 us -> 2.16 us  [per_device(): other = lax.ppermute(docs, 'tok', [(t, t ^ flip) for t in range(4)])]
    ppermute x6, waiting for transfers between devices: 24.3 us -> 21.8 us  [per_device(): lax.ppermute(key_values[head], 'tok', [(t, t + s) for t in range(4 - s)])]
    unnamed x9, local copies, waits for them, and re-layouts: 10 us -> 12.2 us
    ppermute x5, starting transfers between devices: 4.23 us -> 2.76 us  [by_row(): return lax.ppermute(value, 'row', [(0, 1), (1, 0)])]
    select_n x0 -> x2, other arithmetic: none -> 1.07 us  [the longest x1 0.99 us: per_device(): jnp.where(tok < toks, sums, received[-1][0][0, 0, 0].astype(jnp.float32))]
    convert_element_type x4 -> x5, other arithmetic: 0.13 us -> 1.14 us  [the longest x1 0.99 us: per_device(): sums = arrived[head].astype(jnp.float32)]
  transfers between devices with their start and end apart: 19 -> 19, of which waited for: 11 -> 7; matrix products, arithmetic and copies ran while one was open for 13% -> 18% of each run, Pallas kernels for 4% -> 8%
where the time goes in v1:
time: 83.8 us; the launch traced here: 83.3 us
  waiting for transfers between devices  35 us (42%)
  starting transfers between devices  16.9 us (20%)
  local copies, waits for them, and re-layouts  13.5 us (16%)
  Pallas kernels  8.77 us (10%)
  other arithmetic  8.17 us (10%)
  between operations  0.99 us (1%)
    ppermute x6, waiting for transfers between devices, per_device(): lax.ppermute(key_values[head], 'tok', [(t, t + s) for t in range(4 - s)])  21.8 us
    unnamed x9, local copies, waits for them, and re-layouts  12.2 us
    ppermute x6, starting transfers between devices, per_device(): lax.ppermute(key_values[head], 'tok', [(t, t + s) for t in range(4 - s)])  7.75 us
    ppermute x5, waiting for transfers between devices, by_row(): return lax.ppermute(value, 'row', [(0, 1), (1, 0)])  7.35 us
    ppermute x4, waiting for transfers between devices, by_col(): return lax.ppermute(value, 'col', [(c, c ^ flip) for c in range(4)])  3.62 us
    pallas_call x2, Pallas kernels, per_device(): attend(queries[head], key_values[head], *received[head], key_places.resha...  3.55 us
    ppermute x1, starting transfers between devices, per_device(): lax.ppermute(activations, ('row', 'col'), [(r * 4 + c, c // 2 * 4 + 2 * (...  3.31 us
    ppermute x5, starting transfers between devices, by_row(): return lax.ppermute(value, 'row', [(0, 1), (1, 0)])  2.76 us
  transfers between devices with their start and end apart: 19, of which 7 were waited for; matrix products, arithmetic and copies ran while one was open for 18% of the time, Pallas kernels for 8%

profile of v1, /device:TPU:24, one launch (start us, length us, event | category | flops | bytes accessed | tf_op | source)
XLA Modules:
  0.0 83.3 jit_solution(9566254206685536522)
XLA Ops:
  0.0 1.8 %collective-permute-start = (bf16[176,1024]{1,0:T(8,128)(2,1)}, bf16[176,1024]{1,0:T(8,128)(2,1)S(1)}, u32[]{:S(2)}, u32[]{:S(2)}) collective-permute-start(bf16[176,1024]{1,0:T(8,128)(2,1)} %param.4), channel_id=1, source_target_pairs={{0,0},{1,1},{2,4},{3,5},{4,2},{5,3},{6,6},{7,7},{8,8},{9,9},{10,12... | collective-permute-start | bytes 1081352 | tf_op jit(solution)/shard_map/ppermute | solution.py:178
  1.8 3.3 %collective-permute-start.1 = (bf16[176,1024]{1,0:T(8,128)(2,1)}, bf16[176,1024]{1,0:T(8,128)(2,1)S(1)}, u32[]{:S(2)}, u32[]{:S(2)}) collective-permute-start(bf16[176,1024]{1,0:T(8,128)(2,1)} %param.4), channel_id=1, source_target_pairs={{0,2},{1,3},{2,6},{3,7},{4,0},{5,1},{6,4},{7,5},{8,10},{9,11},{10,... | collective-permute-start | bytes 1081352 | tf_op jit(solution)/shard_map/ppermute | solution.py:183
  5.1 1.2 %multiply_reduce_fusion = f32[176]{0:T(256)S(1)} fusion(bf16[176,1024]{1,0:T(8,128)(2,1)} %param.4), kind=kLoop, calls=%fused_computation.1 | loop fusion | flops 540496 | bytes 361152 | tf_op jit(solution)/shard_map/reduce_sum | solution.py:189
  6.2 0.7 convert_element_type.57
  7.0 0.7 convert_element_type.58
  7.7 0.4 collective-permute-start.4
  8.2 0.7 fusion.6
  8.9 0.2 pad_maximum_fusion
  9.1 2.2 %collective-permute-done.4 = f32[176]{0:T(256)S(1)} collective-permute-done((f32[176]{0:T(256)S(1)}, f32[176]{0:T(256)S(1)}, u32[]{:S(2)}, u32[]{:S(2)}) %collective-permute-start.4) | collective-permute-done | bytes 736 | tf_op jit(solution)/shard_map/ppermute | solution.py:200
  11.4 0.3 collective-permute-start.5
  11.8 6.6 %copy.11 = bf16[256,8,4,384]{3,1,2,0:T(8,128)(2,1)} copy(bf16[256,8,4,384]{3,2,1,0:T(4,128)(2,1)} %bitcast.45) | data formatting | bytes 12582912
  18.5 0.1 concatenate.46
  18.7 3.6 %collective-permute-done.3 = f32[2224]{0:T(1024)S(1)} collective-permute-done((f32[2224]{0:T(1024)S(1)}, f32[2224]{0:T(1024)S(1)}, u32[]{:S(2)}, u32[]{:S(2)}) %collective-permute-start.3) | collective-permute-done | bytes 8928 | tf_op jit(solution)/shard_map/ppermute | solution.py:169
  22.4 0.5 collective-permute-start.7
  23.0 3.6 %collective-permute-done.8 = f32[880]{0:T(1024)S(1)} collective-permute-done((f32[880]{0:T(1024)S(1)}, f32[880]{0:T(1024)S(1)}, u32[]{:S(2)}, u32[]{:S(2)}) %collective-permute-start.8) | collective-permute-done | bytes 3552 | tf_op jit(solution)/shard_map/ppermute | solution.py:172
  26.7 0.1 reshape.88.squares_ref
  26.8 2.8 %copy-done = bf16[256,8,4,384]{3,1,2,0:T(8,128)(2,1)S(1)} copy-done((bf16[256,8,4,384]{3,1,2,0:T(8,128)(2,1)S(1)}, bf16[256,8,4,384]{3,1,2,0:T(8,128)(2,1)}, u32[]{:S(2)}) %copy-start) | copy-done | bytes 6291480
  29.6 2.1 %shard_map.46 = (f32[1,3,352,128]{3,2,1,0:T(8,128)S(1)}, bf16[2,352,1024]{2,1,0:T(8,128)(2,1)S(1)}) custom-call(s32[3]{0:T(128)S(1)} %pad_add_fusion.place_ref, bf16[176,1024]{1,0:T(8,128)(2,1)S(1)} %collective-permute-done.a_near, bf16[176,1024]{1,0:T(8,128)(2,1)S(1)} %collective-permute-done.1.a_far, bf16[176,1024]{1,0:T(8,128)(2,1)S(1)} %collective-permute-done.6.b_near, ...), custom_call_target="tpu_custom_call" | custom-call | tf_op jit(solution)/shard_map/pallas_call | solution.py:240
  31.9 0.1 concatenate.56
  32.0 0.1 stack_reshape.7
  32.1 0.1 stack_reshape.6
  32.2 2.8 %copy-done.1 = bf16[256,8,4,384]{3,1,2,0:T(8,128)(2,1)S(1)} copy-done((bf16[256,8,4,384]{3,1,2,0:T(8,128)(2,1)S(1)}, bf16[256,8,4,384]{3,1,2,0:T(8,128)(2,1)}, u32[]{:S(2)}) %copy-start.1) | copy-done | bytes 6291480
  35.0 1.2 %shard_map.47 = f32[1,3,352,128]{3,2,1,0:T(8,128)S(1)} custom-call(s32[1]{0:T(128)} %bitcast.1.place_ref, bf16[2,352,1024]{2,1,0:T(8,128)(2,1)S(1)} %get-tuple-element.28.normed_ref, bf16[2048,1536]{1,0:T(8,128)(2,1)S(1)} %bitcast.43, f32[352,128]{1,0:T(8,128)S(1)} %get-tuple-element.50.cos_ref, f32[352,128]{1,0:T(8,128)S(1)} %get-tuple-element.51.sin_ref), custom_call_target="tpu_custom_call" | custom-call | tf_op jit(solution)/shard_map/pallas_call | solution.py:247
  36.2 0.7 convert_element_type.62
  36.9 2.0 %collective-permute-start.14 = (f16[3,352,128]{2,1,0:T(8,128)(2,1)}, f16[3,352,128]{2,1,0:T(8,128)(2,1)}, u32[]{:S(2)}, u32[]{:S(2)}) collective-permute-start(f16[3,352,128]{2,1,0:T(8,128)(2,1)} %bitcast.13), channel_id=1, source_target_pairs={{0,4},{4,0},{1,5},{5,1},{2,6},{6,2},{3,7},{7,3},{8,12},{12,8},{9,1... | collective-permute-start | bytes 811016 | tf_op jit(solution)/shard_map/ppermute | solution.py:172
  38.9 2.0 %shard_map.48 = f32[2,3,352,128]{3,2,1,0:T(8,128)S(1)} custom-call(s32[1]{0:T(128)} %bitcast.place_ref, bf16[2,352,1024]{2,1,0:T(8,128)(2,1)S(1)} %get-tuple-element.28.normed_ref, bf16[2048,1536]{1,0:T(8,128)(2,1)S(1)} %bitcast.44, f32[352,128]{1,0:T(8,128)S(1)} %get-tuple-element.50.cos_ref, f32[352,128]{1,0:T(8,128)S(1)} %get-tuple-element.51.sin_ref), custom_call_target="tpu_custom_call" | custom-call | tf_op jit(solution)/shard_map/pallas_call | solution.py:252
  40.9 1.0 %convert_element_type.63 = f32[3,352,128]{2,1,0:T(8,128)S(1)} convert(f16[3,352,128]{2,1,0:T(8,128)(2,1)} %collective-permute-done.9) | non-fusion elementwise | flops 135168 | bytes 811008 | tf_op jit(solution)/shard_map/convert_element_type | solution.py:260
  41.9 1.3 %collective-permute-start.10 = (bf16[2,352,128]{2,1,0:T(8,128)(2,1)S(1)}, bf16[2,352,128]{2,1,0:T(8,128)(2,1)S(1)}, u32[]{:S(2)}, u32[]{:S(2)}) collective-permute-start(bf16[2,352,128]{2,1,0:T(8,128)(2,1)S(1)} %fusion.1.refs_1_), channel_id=1, source_target_pairs={{0,8},{8,16},{16,24},{1,9},{9,17},{17,25},{2,10},{10,18},{18,26},{... | collective-permute-start | bytes 540680 | tf_op jit(solution)/shard_map/ppermute | solution.py:268
  43.2 0.1 lt.21
  43.3 0.1 dynamic_slice.3
  43.4 0.4 convert_reduce_fusion
  43.8 0.1 reshape.89.refs_7_
  43.9 1.3 %collective-permute-start.11 = (bf16[2,352,128]{2,1,0:T(8,128)(2,1)S(1)}, bf16[2,352,128]{2,1,0:T(8,128)(2,1)S(1)}, u32[]{:S(2)}, u32[]{:S(2)}) collective-permute-start(bf16[2,352,128]{2,1,0:T(8,128)(2,1)S(1)} %fusion.1.refs_1_), channel_id=1, source_target_pairs={{0,16},{8,24},{1,17},{9,25},{2,18},{10,26},{3,19},{11,27},{4,20},{... | collective-permute-start | bytes 540680 | tf_op jit(solution)/shard_map/ppermute | solution.py:268
  45.2 1.3 %collective-permute-start.12 = (bf16[2,352,128]{2,1,0:T(8,128)(2,1)S(1)}, bf16[2,352,128]{2,1,0:T(8,128)(2,1)S(1)}, u32[]{:S(2)}, u32[]{:S(2)}) collective-permute-start(bf16[2,352,128]{2,1,0:T(8,128)(2,1)S(1)} %fusion.1.refs_1_), channel_id=1, source_target_pairs={{0,24},{1,25},{2,26},{3,27},{4,28},{5,29},{6,30},{7,31}} | collective-permute-start | bytes 540680 | tf_op jit(solution)/shard_map/ppermute | solution.py:268
  46.5 4.2 %collective-permute-done.10.refs_2_ = bf16[2,352,128]{2,1,0:T(8,128)(2,1)S(1)} collective-permute-done((bf16[2,352,128]{2,1,0:T(8,128)(2,1)S(1)}, bf16[2,352,128]{2,1,0:T(8,128)(2,1)S(1)}, u32[]{:S(2)}, u32[]{:S(2)}) %collective-permute-start.10) | collective-permute-done | bytes 180256 | tf_op jit(solution)/shard_map/ppermute | solution.py:268
  50.7 0.5 slice.93
  51.8 1.0 %convert_select_fusion = f32[3,352,128]{2,1,0:T(8,128)S(1)} fusion(f16[3,352,128]{2,1,0:T(8,128)(2,1)} %collective-permute-done.14, f32[]{:T(128)S(6)} %convert.1, pred[]{:T(512)S(6)} %lt.26), kind=kLoop, calls=%fused_computation.2 | loop fusion | flops 270336 | bytes 811013 | tf_op jit(solution)/shard_map/jit(_where)/select_n | solution.py:262
  52.9 1.3 %collective-permute-start.15 = (bf16[2,352,128]{2,1,0:T(8,128)(2,1)S(1)}, bf16[2,352,128]{2,1,0:T(8,128)(2,1)S(1)}, u32[]{:S(2)}, u32[]{:S(2)}) collective-permute-start(bf16[2,352,128]{2,1,0:T(8,128)(2,1)S(1)} %fusion.refs_1_), channel_id=1, source_target_pairs={{0,8},{8,16},{16,24},{1,9},{9,17},{17,25},{2,10},{10,18},{18,26},{... | collective-permute-start | bytes 540680 | tf_op jit(solution)/shard_map/ppermute | solution.py:268
  54.2 1.3 %collective-permute-start.16 = (bf16[2,352,128]{2,1,0:T(8,128)(2,1)S(1)}, bf16[2,352,128]{2,1,0:T(8,128)(2,1)S(1)}, u32[]{:S(2)}, u32[]{:S(2)}) collective-permute-start(bf16[2,352,128]{2,1,0:T(8,128)(2,1)S(1)} %fusion.refs_1_), channel_id=1, source_target_pairs={{0,16},{8,24},{1,17},{9,25},{2,18},{10,26},{3,19},{11,27},{4,20},{... | collective-permute-start | bytes 540680 | tf_op jit(solution)/shard_map/ppermute | solution.py:268
  55.5 1.3 %collective-permute-start.17 = (bf16[2,352,128]{2,1,0:T(8,128)(2,1)S(1)}, bf16[2,352,128]{2,1,0:T(8,128)(2,1)S(1)}, u32[]{:S(2)}, u32[]{:S(2)}) collective-permute-start(bf16[2,352,128]{2,1,0:T(8,128)(2,1)S(1)} %fusion.refs_1_), channel_id=1, source_target_pairs={{0,24},{1,25},{2,26},{3,27},{4,28},{5,29},{6,30},{7,31}} | collective-permute-start | bytes 540680 | tf_op jit(solution)/shard_map/ppermute | solution.py:268
  56.8 10.1 %collective-permute-done.11.refs_3_ = bf16[2,352,128]{2,1,0:T(8,128)(2,1)S(1)} collective-permute-done((bf16[2,352,128]{2,1,0:T(8,128)(2,1)S(1)}, bf16[2,352,128]{2,1,0:T(8,128)(2,1)S(1)}, u32[]{:S(2)}, u32[]{:S(2)}) %collective-permute-start.11) | collective-permute-done | bytes 180256 | tf_op jit(solution)/shard_map/ppermute | solution.py:268
  67.0 1.8 %shard_map.49 = bf16[352,128]{1,0:T(8,128)(2,1)S(1)} custom-call(bf16[352,128]{1,0:T(8,128)(2,1)S(1)} %get-tuple-element.31.refs_0_, bf16[2,352,128]{2,1,0:T(8,128)(2,1)S(1)} %fusion.1.refs_1_, bf16[2,352,128]{2,1,0:T(8,128)(2,1)S(1)} %collective-permute-done.10.refs_2_, bf16[2,352,128]{2,1,0:T(8,128)(2,1)S(1)} %collective-permute-done.11.refs_3_, ...), custom_call_target="tpu_custom_call" | custom-call | flops 253755392 | bytes 2097152 | tf_op jit(solution)/shard_map/pallas_call | solution.py:289
  68.8 0.4 collective-permute-start.13
  69.1 7.5 %collective-permute-done.16.refs_3_ = bf16[2,352,128]{2,1,0:T(8,128)(2,1)S(1)} collective-permute-done((bf16[2,352,128]{2,1,0:T(8,128)(2,1)S(1)}, bf16[2,352,128]{2,1,0:T(8,128)(2,1)S(1)}, u32[]{:S(2)}, u32[]{:S(2)}) %collective-permute-start.16) | collective-permute-done | bytes 180256 | tf_op jit(solution)/shard_map/ppermute | solution.py:268
  76.6 1.8 %shard_map.50 = bf16[352,128]{1,0:T(8,128)(2,1)S(1)} custom-call(bf16[352,128]{1,0:T(8,128)(2,1)S(1)} %get-tuple-element.32.refs_0_, bf16[2,352,128]{2,1,0:T(8,128)(2,1)S(1)} %fusion.refs_1_, bf16[2,352,128]{2,1,0:T(8,128)(2,1)S(1)} %collective-permute-done.15.refs_2_, bf16[2,352,128]{2,1,0:T(8,128)(2,1)S(1)} %collective-permute-done.16.refs_3_, ...), custom_call_target="tpu_custom_call" | custom-call | flops 253755392 | bytes 2097152 | tf_op jit(solution)/shard_map/pallas_call | solution.py:289
  78.4 0.3 collective-permute-start.18
  78.8 3.8 %collective-permute-done.18 = bf16[176,128]{1,0:T(8,128)(2,1)S(1)} collective-permute-done((bf16[176,128]{1,0:T(8,128)(2,1)S(1)}, bf16[176,128]{1,0:T(8,128)(2,1)S(1)}, u32[]{:S(2)}, u32[]{:S(2)}) %collective-permute-start.18) | collective-permute-done | bytes 45088 | tf_op jit(solution)/shard_map/ppermute | solution.py:172
  82.6 0.7 pad_maximum_fusion.2
  (54 shorter events, 1.2 us)
Async XLA Ops:
  0.0 11.3 %copy-start.3 = (s32[176]{0:T(256)S(1)}, s32[176]{0:T(256)}, u32[]{:S(2)}) copy-start(s32[176]{0:T(256)} %param.7) | copy-start | bytes 2116
  0.0 22.3 %collective-permute-start = (bf16[176,1024]{1,0:T(8,128)(2,1)}, bf16[176,1024]{1,0:T(8,128)(2,1)S(1)}, u32[]{:S(2)}, u32[]{:S(2)}) collective-permute-start(bf16[176,1024]{1,0:T(8,128)(2,1)} %param.4), channel_id=1, source_target_pairs={{0,0},{1,1},{2,4},{3,5},{4,2},{5,3},{6,6},{7,7},{8,8},{9,9},{10,12... | collective-permute-start | bytes 1081352 | tf_op jit(solution)/shard_map/ppermute | solution.py:178
  1.8 20.6 %collective-permute-start.1 = (bf16[176,1024]{1,0:T(8,128)(2,1)}, bf16[176,1024]{1,0:T(8,128)(2,1)S(1)}, u32[]{:S(2)}, u32[]{:S(2)}) collective-permute-start(bf16[176,1024]{1,0:T(8,128)(2,1)} %param.4), channel_id=1, source_target_pairs={{0,2},{1,3},{2,6},{3,7},{4,0},{5,1},{6,4},{7,5},{8,10},{9,11},{10,... | collective-permute-start | bytes 1081352 | tf_op jit(solution)/shard_map/ppermute | solution.py:183
  7.0 11.5 %collective-permute-start.2 = (f32[1200]{0:T(1024)S(1)}, f32[1200]{0:T(1024)S(1)}, u32[]{:S(2)}, u32[]{:S(2)}) collective-permute-start(f32[1200]{0:T(1024)S(1)} %pad_maximum_fusion.3), channel_id=1, source_target_pairs={{0,1},{1,0},{2,3},{3,2},{4,5},{5,4},{6,7},{7,6},{8,9},{9,8},{10,11... | collective-permute-start | bytes 14408 | tf_op jit(solution)/shard_map/ppermute | solution.py:169
  7.7 3.6 %collective-permute-start.4 = (f32[176]{0:T(256)S(1)}, f32[176]{0:T(256)S(1)}, u32[]{:S(2)}, u32[]{:S(2)}) collective-permute-start(f32[176]{0:T(256)S(1)} %convert_element_type.58), channel_id=1, source_target_pairs={{0,8},{8,0},{16,24},{24,16},{1,9},{9,1},{17,25},{25,17},{2,10},{10... | collective-permute-start | bytes 2120 | tf_op jit(solution)/shard_map/ppermute | solution.py:200
  11.4 7.0 %collective-permute-start.5 = (f32[352]{0:T(512)S(1)}, f32[352]{0:T(512)S(1)}, u32[]{:S(2)}, u32[]{:S(2)}) collective-permute-start(f32[352]{0:T(512)S(1)} %pad_maximum_fusion.7), channel_id=1, source_target_pairs={{0,16},{8,24},{16,0},{24,8},{1,17},{9,25},{17,1},{25,9},{2,18},{10... | collective-permute-start | bytes 4232 | tf_op jit(solution)/shard_map/ppermute | solution.py:200
  11.8 6.7 %copy-start.2 = (bf16[1024]{0:T(1024)(128)(2,1)S(1)}, bf16[1024]{0:T(1024)(128)(2,1)}, u32[]{:S(2)}) copy-start(bf16[1024]{0:T(1024)(128)(2,1)} %param.5) | copy-start | bytes 6148
  18.6 3.7 %collective-permute-start.3 = (f32[2224]{0:T(1024)S(1)}, f32[2224]{0:T(1024)S(1)}, u32[]{:S(2)}, u32[]{:S(2)}) collective-permute-start(f32[2224]{0:T(1024)S(1)} %concatenate.46), channel_id=1, source_target_pairs={{0,2},{1,3},{2,0},{3,1},{4,6},{5,7},{6,4},{7,5},{8,10},{9,11},{10,... | collective-permute-start | bytes 26696 | tf_op jit(solution)/shard_map/ppermute | solution.py:169
  22.4 4.4 %collective-permute-start.6 = (bf16[176,1024]{1,0:T(8,128)(2,1)S(1)}, bf16[176,1024]{1,0:T(8,128)(2,1)S(1)}, u32[]{:S(2)}, u32[]{:S(2)}) collective-permute-start(bf16[176,1024]{1,0:T(8,128)(2,1)S(1)} %collective-permute-done.a_near), channel_id=1, source_target_pairs={{0,1},{1,0},{2,3},{3,2},{4,5},{5,4},{6,7},{7,6},{8,9},{9,8},{10,11... | collective-permute-start | bytes 1081352 | tf_op jit(solution)/shard_map/ppermute | solution.py:169
  22.4 4.4 %collective-permute-start.7 = (bf16[176,1024]{1,0:T(8,128)(2,1)S(1)}, bf16[176,1024]{1,0:T(8,128)(2,1)S(1)}, u32[]{:S(2)}, u32[]{:S(2)}) collective-permute-start(bf16[176,1024]{1,0:T(8,128)(2,1)S(1)} %collective-permute-done.1.a_far), channel_id=1, source_target_pairs={{0,1},{1,0},{2,3},{3,2},{4,5},{5,4},{6,7},{7,6},{8,9},{9,8},{10,11... | collective-permute-start | bytes 1081352 | tf_op jit(solution)/shard_map/ppermute | solution.py:169
  23.0 3.6 %collective-permute-start.8 = (f32[880]{0:T(1024)S(1)}, f32[880]{0:T(1024)S(1)}, u32[]{:S(2)}, u32[]{:S(2)}) collective-permute-start(f32[880]{0:T(1024)S(1)} %pad_maximum_fusion.6), channel_id=1, source_target_pairs={{0,4},{4,0},{1,5},{5,1},{2,6},{6,2},{3,7},{7,3},{8,12},{12,8},{9,1... | collective-permute-start | bytes 10568 | tf_op jit(solution)/shard_map/ppermute | solution.py:172
  26.8 2.8 %copy-start = (bf16[256,8,4,384]{3,1,2,0:T(8,128)(2,1)S(1)}, bf16[256,8,4,384]{3,1,2,0:T(8,128)(2,1)}, u32[]{:S(2)}) copy-start(bf16[256,8,4,384]{3,1,2,0:T(8,128)(2,1)} %copy.11) | copy-start | bytes 18874372
  31.8 9.1 %collective-permute-start.9 = (f16[3,352,128]{2,1,0:T(8,128)(2,1)S(1)}, f16[3,352,128]{2,1,0:T(8,128)(2,1)}, u32[]{:S(2)}, u32[]{:S(2)}) collective-permute-start(f16[3,352,128]{2,1,0:T(8,128)(2,1)S(1)} %bitcast.46), channel_id=1, source_target_pairs={{0,4},{4,0},{1,5},{5,1},{2,6},{6,2},{3,7},{7,3},{8,12},{12,8},{9,1... | collective-permute-start | bytes 811016 | tf_op jit(solution)/shard_map/ppermute | solution.py:172
  32.2 2.8 %copy-start.1 = (bf16[256,8,4,384]{3,1,2,0:T(8,128)(2,1)S(1)}, bf16[256,8,4,384]{3,1,2,0:T(8,128)(2,1)}, u32[]{:S(2)}) copy-start(bf16[256,8,4,384]{3,1,2,0:T(8,128)(2,1)} %copy.11) | copy-start | bytes 18874372
  36.9 14.9 %collective-permute-start.14 = (f16[3,352,128]{2,1,0:T(8,128)(2,1)}, f16[3,352,128]{2,1,0:T(8,128)(2,1)}, u32[]{:S(2)}, u32[]{:S(2)}) collective-permute-start(f16[3,352,128]{2,1,0:T(8,128)(2,1)} %bitcast.13), channel_id=1, source_target_pairs={{0,4},{4,0},{1,5},{5,1},{2,6},{6,2},{3,7},{7,3},{8,12},{12,8},{9,1... | collective-permute-start | bytes 811016 | tf_op jit(solution)/shard_map/ppermute | solution.py:172
  41.9 8.7 %collective-permute-start.10 = (bf16[2,352,128]{2,1,0:T(8,128)(2,1)S(1)}, bf16[2,352,128]{2,1,0:T(8,128)(2,1)S(1)}, u32[]{:S(2)}, u32[]{:S(2)}) collective-permute-start(bf16[2,352,128]{2,1,0:T(8,128)(2,1)S(1)} %fusion.1.refs_1_), channel_id=1, source_target_pairs={{0,8},{8,16},{16,24},{1,9},{9,17},{17,25},{2,10},{10,18},{18,26},{... | collective-permute-start | bytes 540680 | tf_op jit(solution)/shard_map/ppermute | solution.py:268
  43.9 23.1 %collective-permute-start.11 = (bf16[2,352,128]{2,1,0:T(8,128)(2,1)S(1)}, bf16[2,352,128]{2,1,0:T(8,128)(2,1)S(1)}, u32[]{:S(2)}, u32[]{:S(2)}) collective-permute-start(bf16[2,352,128]{2,1,0:T(8,128)(2,1)S(1)} %fusion.1.refs_1_), channel_id=1, source_target_pairs={{0,16},{8,24},{1,17},{9,25},{2,18},{10,26},{3,19},{11,27},{4,20},{... | collective-permute-start | bytes 540680 | tf_op jit(solution)/shard_map/ppermute | solution.py:268
  45.2 21.8 %collective-permute-start.12 = (bf16[2,352,128]{2,1,0:T(8,128)(2,1)S(1)}, bf16[2,352,128]{2,1,0:T(8,128)(2,1)S(1)}, u32[]{:S(2)}, u32[]{:S(2)}) collective-permute-start(bf16[2,352,128]{2,1,0:T(8,128)(2,1)S(1)} %fusion.1.refs_1_), channel_id=1, source_target_pairs={{0,24},{1,25},{2,26},{3,27},{4,28},{5,29},{6,30},{7,31}} | collective-permute-start | bytes 540680 | tf_op jit(solution)/shard_map/ppermute | solution.py:268
  52.9 16.3 %collective-permute-start.15 = (bf16[2,352,128]{2,1,0:T(8,128)(2,1)S(1)}, bf16[2,352,128]{2,1,0:T(8,128)(2,1)S(1)}, u32[]{:S(2)}, u32[]{:S(2)}) collective-permute-start(bf16[2,352,128]{2,1,0:T(8,128)(2,1)S(1)} %fusion.refs_1_), channel_id=1, source_target_pairs={{0,8},{8,16},{16,24},{1,9},{9,17},{17,25},{2,10},{10,18},{18,26},{... | collective-permute-start | bytes 540680 | tf_op jit(solution)/shard_map/ppermute | solution.py:268
  54.2 22.4 %collective-permute-start.16 = (bf16[2,352,128]{2,1,0:T(8,128)(2,1)S(1)}, bf16[2,352,128]{2,1,0:T(8,128)(2,1)S(1)}, u32[]{:S(2)}, u32[]{:S(2)}) collective-permute-start(bf16[2,352,128]{2,1,0:T(8,128)(2,1)S(1)} %fusion.refs_1_), channel_id=1, source_target_pairs={{0,16},{8,24},{1,17},{9,25},{2,18},{10,26},{3,19},{11,27},{4,20},{... | collective-permute-start | bytes 540680 | tf_op jit(solution)/shard_map/ppermute | solution.py:268
  55.5 21.1 %collective-permute-start.17 = (bf16[2,352,128]{2,1,0:T(8,128)(2,1)S(1)}, bf16[2,352,128]{2,1,0:T(8,128)(2,1)S(1)}, u32[]{:S(2)}, u32[]{:S(2)}) collective-permute-start(bf16[2,352,128]{2,1,0:T(8,128)(2,1)S(1)} %fusion.refs_1_), channel_id=1, source_target_pairs={{0,24},{1,25},{2,26},{3,27},{4,28},{5,29},{6,30},{7,31}} | collective-permute-start | bytes 540680 | tf_op jit(solution)/shard_map/ppermute | solution.py:268
  68.8 10.0 %collective-permute-start.13 = (bf16[176,128]{1,0:T(8,128)(2,1)S(1)}, bf16[176,128]{1,0:T(8,128)(2,1)S(1)}, u32[]{:S(2)}, u32[]{:S(2)}) collective-permute-start(bf16[176,128]{1,0:T(8,128)(2,1)S(1)} %broadcast_select_fusion.6), channel_id=1, source_target_pairs={{0,4},{4,0},{1,5},{5,1},{2,6},{6,2},{3,7},{7,3},{8,12},{12,8},{9,1... | collective-permute-start | bytes 135176 | tf_op jit(solution)/shard_map/ppermute | solution.py:172
  78.4 4.1 %collective-permute-start.18 = (bf16[176,128]{1,0:T(8,128)(2,1)S(1)}, bf16[176,128]{1,0:T(8,128)(2,1)S(1)}, u32[]{:S(2)}, u32[]{:S(2)}) collective-permute-start(bf16[176,128]{1,0:T(8,128)(2,1)S(1)} %broadcast_select_fusion.3), channel_id=1, source_target_pairs={{0,4},{4,0},{1,5},{5,1},{2,6},{6,2},{3,7},{7,3},{8,12},{12,8},{9,1... | collective-permute-start | bytes 135176 | tf_op jit(solution)/shard_map/ppermute | solution.py:172

commit v2 on v1

--- a/solution.py
+++ b/solution.py
@@ -8,6 +8,8 @@
 from jax.sharding import PartitionSpec as P
 
 EPS = 1e-05
+LOW = -1e30
+EXTRA = 16
 MIB = 1 << 20
 
 
@@ -37,8 +39,9 @@
     ]
 
 
-def project_heads(normed_ref, copies, weight_buffer, cos_ref, sin_ref, out_ref):
-    heads, size = out_ref.shape[0], out_ref.shape[3]
+def project_heads(normed_ref, copies, weight_buffer, cos_ref, sin_ref, doc_rows, out_ref):
+    heads, size = out_ref.shape[0], out_ref.shape[2]
+    block, extra = cos_ref.shape[0], doc_rows.shape[0]
     depth = weight_buffer.shape[0] // 2
     for copy in copies:
         copy.wait()
@@ -49,11 +52,13 @@
         ) + jnp.dot(
             normed_ref[1], weight_buffer[depth:, columns], preferred_element_type=jnp.float32
         )
-        for kind in range(3):
+        for kind, at in ((0, 2 * block + extra), (1, 0), (2, block)):
             piece = part[:, kind * size : (kind + 1) * size]
             if kind < 2:
                 piece = piece * cos_ref[...] + pltpu.roll(piece, size // 2, 1) * sin_ref[...]
-            out_ref[head, kind] = piece
+            out_ref[head, at : at + block, :] = piece
+        for at in (2 * block, 3 * block + extra):
+            out_ref[head, at : at + extra, :] = doc_rows
 
 
 def normalise_project_kernel(
@@ -74,40 +79,143 @@
             normed_ref[half, at, :] = (shard[...].astype(jnp.float32) * factor * gain).astype(
                 jnp.bfloat16
             )
-    project_heads(normed_ref, copies, weight_buffer, cos_ref, sin_ref, out_ref)
+    nothing = jnp.zeros((EXTRA, out_ref.shape[2]), jnp.float32)
+    project_heads(normed_ref, copies, weight_buffer, cos_ref, sin_ref, nothing, out_ref)
 
 
 def project_kernel(
-    place_ref, normed_ref, weight_hbm, cos_ref, sin_ref, out_ref, weight_buffer, semaphores
+    place_ref, normed_ref, docs_ref, weight_hbm, cos_ref, sin_ref, out_ref, weight_buffer,
+    semaphores,
 ):
     copies = weight_copies(
         place_ref[0], 3 * cos_ref.shape[1], weight_hbm, weight_buffer, semaphores
     )
     for copy in copies:
         copy.start()
-    project_heads(normed_ref, copies, weight_buffer, cos_ref, sin_ref, out_ref)
-
-
-def attend_kernel(scale, query_ref, *refs):
-    key_value_refs, (key_place_ref, place_ref, start_ref, out_ref) = refs[:-4], refs[-4:]
-    key_places = key_place_ref[...]
-    visible = (key_places <= place_ref[...]) & (key_places >= start_ref[...])
-    keys = jnp.concatenate([ref[0] for ref in key_value_refs], axis=0)
-    values = jnp.concatenate([ref[1] for ref in key_value_refs], axis=0)
+    project_heads(normed_ref, copies, weight_buffer, cos_ref, sin_ref, docs_ref[...], out_ref)
+
+
+def as_column(rows, count):
+    lanes = rows.shape[1]
+    pieces = []
+    for begin in range(0, count, lanes):
+        held = min(lanes, count - begin)
+        at = lax.broadcasted_iota(jnp.int32, (held, lanes), 0)
+        diagonal = at == lax.broadcasted_iota(jnp.int32, (held, lanes), 1)
+        row = rows[begin // lanes : begin // lanes + 1, :]
+        pieces.append(jnp.sum(jnp.where(diagonal, row, 0.0), axis=1, keepdims=True))
+    return jnp.concatenate(pieces, axis=0)
+
+
+def as_rows(column, lanes):
+    count = column.shape[0]
+    rows = []
+    for begin in range(0, count, lanes):
+        held = min(lanes, count - begin)
+        at = lax.broadcasted_iota(jnp.int32, (held, lanes), 0)
+        diagonal = at == lax.broadcasted_iota(jnp.int32, (held, lanes), 1)
+        rows.append(
+            jnp.sum(jnp.where(diagonal, column[begin : begin + held], 0.0), axis=0, keepdims=True)
+        )
+    return rows
+
+
+def as_lanes(rows, count):
+    lanes = rows.shape[1]
+    return jnp.concatenate(
+        [
+            rows[begin // lanes : begin // lanes + 1, : min(lanes, count - begin)]
+            for begin in range(0, count, lanes)
+        ],
+        axis=1,
+    )
+
+
+def softmax_part(scale, query, query_docs, messages, causal):
+    block = (messages[0].shape[0] - EXTRA) // 2
+    keys = jnp.concatenate([message[:block] for message in messages], axis=0)
+    values = jnp.concatenate([message[block : 2 * block] for message in messages], axis=0)
+    key_docs = jnp.concatenate(
+        [as_lanes(message[2 * block :].astype(jnp.float32), block) for message in messages], axis=1
+    )
+    visible = query_docs == key_docs
+    if causal:
+        shape = (query.shape[0], keys.shape[0])
+        query_places = lax.broadcasted_iota(jnp.int32, shape, 0)
+        key_places = lax.broadcasted_iota(jnp.int32, shape, 1)
+        visible &= (key_places <= query_places) | (key_places >= block)
     scores = (
-        lax.dot_general(
-            query_ref[...], keys, (((1,), (1,)), ((), ())), preferred_element_type=jnp.float32
-        )
+        lax.dot_general(query, keys, (((1,), (1,)), ((), ())), preferred_element_type=jnp.float32)
         * scale
     )
-    masked = jnp.where(visible, scores, -1e30)
-    top = jnp.max(masked, axis=1, keepdims=True)
-    exponentials = jnp.where(visible, jnp.exp(masked - top), 0.0)
+    top = jnp.max(jnp.where(visible, scores, LOW), axis=1, keepdims=True)
+    exponentials = jnp.where(visible, jnp.exp(scores - top), 0.0)
     total = jnp.sum(exponentials, axis=1, keepdims=True)
-    summed = jnp.dot(
-        exponentials.astype(jnp.bfloat16), values, preferred_element_type=jnp.float32
-    )
-    out_ref[...] = (summed / total).astype(jnp.bfloat16)
+    summed = jnp.dot(exponentials.astype(jnp.bfloat16), values, preferred_element_type=jnp.float32)
+    some = total > 0.0
+    safe = jnp.where(some, total, 1.0)
+    return summed / safe, jnp.where(some, top + jnp.log(safe), LOW)
+
+
+def guest_kernel(
+    scale, tok_ref, query_one, query_two, up_first, up_second, down_first, down_second, out_ref
+):
+    block = query_one.shape[0] - EXTRA
+    size = query_one.shape[1]
+    at_two = tok_ref[0] == 2
+    messages = [
+        jnp.where(at_two, up_first[...], down_first[...]),
+        jnp.where(at_two, up_second[...], down_second[...]),
+    ]
+    for index, query_ref in enumerate((query_one, query_two)):
+        docs = as_column(query_ref[block:, :].astype(jnp.float32), block)
+        output, logs = softmax_part(scale, query_ref[:block, :], docs, messages, False)
+        out_ref[index, :block, :] = output.astype(jnp.bfloat16)
+        high = logs.astype(jnp.bfloat16).astype(jnp.float32)
+        middle = (logs - high).astype(jnp.bfloat16).astype(jnp.float32)
+        rows = as_rows(high, size) + as_rows(middle, size) + as_rows(logs - high - middle, size)
+        rows.append(jnp.zeros((EXTRA - len(rows), size), jnp.float32))
+        out_ref[index, block:, :] = jnp.concatenate(rows, axis=0).astype(jnp.bfloat16)
+
+
+def own_kernel(
+    scale, query_a, own_a, one_up_a, two_up_a, query_b, own_b, one_up_b, unused, out_ref, logs_ref
+):
+    block = query_a.shape[0] - EXTRA
+    for index, (query_ref, refs) in enumerate(
+        ((query_a, (own_a, one_up_a, two_up_a)), (query_b, (own_b, one_up_b)))
+    ):
+        docs = as_column(query_ref[block:, :].astype(jnp.float32), block)
+        output, logs = softmax_part(
+            scale, query_ref[:block, :], docs, [ref[...] for ref in refs], True
+        )
+        out_ref[index] = output
+        logs_ref[index] = logs
+
+
+def merge_kernel(place_ref, out_ref, logs_ref, one_ref, two_ref, mine_ref, theirs_ref):
+    block, size = out_ref.shape[1:]
+    groups = pl.cdiv(block, size)
+    tok, row = place_ref[0], place_ref[1]
+    rows = block // 2
+    at_two, at_three = tok == 2, tok == 3
+
+    def joined(index, message, present):
+        logs = logs_ref[index]
+        tile = message[block:].astype(jnp.float32)
+        guest = sum(as_column(tile[k * groups : (k + 1) * groups], block) for k in range(3))
+        guest = jnp.where(present, guest, LOW)
+        top = jnp.maximum(logs, guest)
+        weight, guest_weight = jnp.exp(logs - top), jnp.exp(guest - top)
+        output = out_ref[index] * weight + message[:block].astype(jnp.float32) * guest_weight
+        return (output / (weight + guest_weight)).astype(jnp.bfloat16)
+
+    first = joined(0, one_ref[...], at_three)
+    second = joined(1, jnp.where(at_two, one_ref[...], two_ref[...]), at_two | at_three)
+    for index, output in enumerate((first, second)):
+        columns = slice(index * size, (index + 1) * size)
+        mine_ref[:, columns] = jnp.where(row == 0, output[:rows], output[rows:])
+        theirs_ref[:, columns] = jnp.where(row == 0, output[rows:], output[:rows])
 
 
 def attend_gathered(query, keys, values, places, starts, scale):
@@ -194,37 +302,30 @@
     got = by_col(message, 1)
     squares = squares + got[:rows]
     gain = ordered(core, gain, got[rows:])
-    docs = doc_ids.astype(jnp.float32)
-    if toks == 4:
-        for flip in (1, 2):
-            other = lax.ppermute(docs, "tok", [(t, t ^ flip) for t in range(4)])
-            docs = ordered(tok & flip, docs, other)
     got = by_col(jnp.concatenate([squares, gain]), 2)
-    near, far, got, docs, flat_weight = lax.optimization_barrier(
-        (near, far, got, docs, flat_weight)
-    )
+    near, far, got, flat_weight = lax.optimization_barrier((near, far, got, flat_weight))
     near_other, far_other = by_col(near, 1), by_col(far, 1)
     squares = squares + got[:rows]
     gain = jnp.where(chip == row, gain, got[rows:]).reshape(2, 1, width)
-    got = by_row(jnp.concatenate([squares, docs]))
+    codes = doc_ids.astype(jnp.float32) + 1.0
+    got = by_row(jnp.concatenate([squares, codes]))
     squares = ordered(row, squares, got[:rows]).reshape(block, 1)
-    row_docs = [jnp.where(row == r, docs, got[rows:]).reshape(-1, rows) for r in range(2)]
-    all_docs = jnp.stack(row_docs, axis=1).reshape(-1)
-    if toks != 4:
-        all_docs = lax.all_gather(all_docs, "tok", axis=0, tiled=True)
-    block_docs = lax.dynamic_slice_in_dim(all_docs, tok * block, block, 0)
-    starts = jnp.sum((all_docs[None, :] < block_docs[:, None]).astype(jnp.int32), axis=1)
+    codes = ordered(row, codes, got[rows:])
+    doc_rows = jnp.pad(codes, (0, EXTRA * size - block)).reshape(EXTRA, size)
     places = tok * block + jnp.arange(block, dtype=jnp.int32)
     cosine, sine = rotary_tables(places, size)
+
+    taller = 3 * block + 2 * EXTRA
+    break_at = 2 * block + EXTRA
 
     def projection(kernel, heads, normalising):
         normed_shape = (jax.ShapeDtypeStruct((2, block, width), jnp.bfloat16),)
         return pl.pallas_call(
             kernel,
-            out_shape=(jax.ShapeDtypeStruct((heads, 3, block, size), jnp.float32),)
+            out_shape=(jax.ShapeDtypeStruct((heads, taller, size), jnp.float32),)
             + (normed_shape if normalising else ()),
             in_specs=[pl.BlockSpec(memory_space=pltpu.SMEM)]
-            + in_vmem(6 if normalising else 1)
+            + in_vmem(6 if normalising else 2)
             + [pl.BlockSpec(memory_space=pltpu.HBM)]
             + in_vmem(2),
             out_specs=tuple(in_vmem(2 if normalising else 1)),
@@ -232,7 +333,7 @@
                 pltpu.VMEM((span, heads * triple), jnp.bfloat16),
                 pltpu.SemaphoreType.DMA((2,)),
             ],
-            compiler_params=pltpu.CompilerParams(vmem_limit_bytes=24 * MIB),
+            compiler_params=pltpu.CompilerParams(vmem_limit_bytes=12 * MIB),
             cost_estimate=pl.CostEstimate(flops=0, bytes_accessed=0, transcendentals=0),
         )
 
@@ -245,66 +346,80 @@
     for head in range(pair):
         if head > 0:
             (away,) = projection(project_kernel, 1, False)(
-                (away_head + head).reshape(1), normed, flat_weight, cosine, sine
+                (away_head + head).reshape(1), normed, jnp.zeros_like(doc_rows), flat_weight,
+                cosine, sine,
             )
         away, normed = lax.optimization_barrier((away.astype(jnp.float16), normed))
         arrived.append(by_row(away[0]))
     (own,) = projection(project_kernel, pair, False)(
-        own_head.reshape(1), normed, flat_weight, cosine, sine
-    )
-
+        own_head.reshape(1), normed, doc_rows, flat_weight, cosine, sine
+    )
     scale = 1.0 / math.sqrt(size)
 
-    queries, key_values, received = [], [], []
-    for head in range(pair):
-        sums = arrived[head].astype(jnp.float32)
-        if toks == 4 and head > 0:
-            sums = jnp.where(tok < toks, sums, received[-1][0][0, 0, 0].astype(jnp.float32))
-        queries.append((own[head, 0] + sums[0]).astype(jnp.bfloat16))
-        key_values.append((own[head, 1:] + sums[1:]).astype(jnp.bfloat16))
-        if toks == 4:
-            received.append(
-                [
-                    lax.ppermute(key_values[head], "tok", [(t, t + s) for t in range(4 - s)])
-                    for s in (1, 2, 3)
-                ]
-            )
-    if toks == 4:
-        key_places = jnp.concatenate(
-            [(tok - s) * block + jnp.arange(block, dtype=jnp.int32) for s in range(4)]
-        )
-        attend = pl.pallas_call(
-            lambda *refs: attend_kernel(scale, *refs),
-            out_shape=jax.ShapeDtypeStruct((block, size), jnp.bfloat16),
-            in_specs=in_vmem(8),
+    def along_tok(value, pairs):
+        return lax.ppermute(value, "tok", pairs)
+
+    def summed(head, begin, end):
+        return own[head, begin:end] + arrived[head][begin:end].astype(jnp.float32)
+
+    if toks == 4 and pair == 2:
+        keys_a = summed(0, 0, break_at).astype(jnp.bfloat16)
+        query_a = summed(0, break_at, taller).astype(jnp.bfloat16)
+        one_up_a = along_tok(keys_a, [(0, 1), (1, 2), (2, 3)])
+        two_up_a = along_tok(keys_a, [(0, 2)])
+        keys_b = jnp.where(
+            tok < toks, summed(1, 0, break_at), one_up_a.astype(jnp.float32)
+        ).astype(jnp.bfloat16)
+        query_b = summed(1, break_at, taller).astype(jnp.bfloat16)
+        guest_one = along_tok(jnp.where(tok == 3, query_a, query_b), [(2, 1), (3, 2)])
+        guest_two = along_tok(query_b, [(3, 1)])
+        one_up_b = along_tok(keys_b, [(0, 1), (2, 3)])
+        guests = pl.pallas_call(
+            lambda *refs: guest_kernel(scale, *refs),
+            out_shape=jax.ShapeDtypeStruct((2, block + EXTRA, size), jnp.bfloat16),
+            in_specs=[pl.BlockSpec(memory_space=pltpu.SMEM)] + in_vmem(6),
             out_specs=in_vmem(1)[0],
-            compiler_params=pltpu.CompilerParams(vmem_limit_bytes=24 * MIB),
-            cost_estimate=pl.CostEstimate(
-                flops=4 * block * 4 * block * size,
-                bytes_accessed=2 * MIB,
-                transcendentals=block * 4 * block,
+            compiler_params=pltpu.CompilerParams(vmem_limit_bytes=16 * MIB),
+        )(tok.reshape(1), guest_one, guest_two, two_up_a, one_up_a, one_up_b, keys_b)
+        from_one = along_tok(guests[0], [(1, 2), (2, 3)])
+        from_two = along_tok(guests[1], [(1, 3)])
+        output, logs = pl.pallas_call(
+            lambda *refs: own_kernel(scale, *refs),
+            out_shape=(
+                jax.ShapeDtypeStruct((2, block, size), jnp.float32),
+                jax.ShapeDtypeStruct((2, block, 1), jnp.float32),
             ),
-        )
-        attended = [
-            attend(
-                queries[head], key_values[head], *received[head],
-                key_places.reshape(1, 4 * block), places.reshape(block, 1), starts.reshape(block, 1),
-            )
-            for head in range(pair)
-        ]
+            in_specs=in_vmem(7) + [pl.BlockSpec(memory_space=pl.ANY)],
+            out_specs=tuple(in_vmem(2)),
+            compiler_params=pltpu.CompilerParams(vmem_limit_bytes=16 * MIB),
+            cost_estimate=pl.CostEstimate(flops=0, bytes_accessed=0, transcendentals=0),
+        )(query_a, keys_a, one_up_a, two_up_a, query_b, keys_b, one_up_b, guests)
+        half_shape = jax.ShapeDtypeStruct((rows, 2 * size), jnp.bfloat16)
+        mine, theirs = pl.pallas_call(
+            merge_kernel,
+            out_shape=(half_shape, half_shape),
+            in_specs=[pl.BlockSpec(memory_space=pltpu.SMEM)] + in_vmem(4),
+            out_specs=tuple(in_vmem(2)),
+            compiler_params=pltpu.CompilerParams(vmem_limit_bytes=16 * MIB),
+        )(jnp.stack([tok, row]), output, logs, from_one, from_two)
     else:
-        everything = lax.all_gather(jnp.stack(key_values), "tok", axis=2, tiled=True)
+        sums = jnp.stack([summed(head, 0, taller) for head in range(pair)]).astype(jnp.bfloat16)
+        everything = lax.all_gather(sums[:, : 2 * block], "tok", axis=0, tiled=False)
+        everything = everything.transpose(1, 0, 2, 3)
+        all_codes = lax.all_gather(codes, "tok", axis=0, tiled=True)
+        starts = jnp.sum((all_codes[None, :] < codes[:, None]).astype(jnp.int32), axis=1)
         together = attend_gathered(
-            jnp.stack(queries), everything[:, 0], everything[:, 1], places, starts, scale
-        )
-        attended = [together[:, head * size : (head + 1) * size] for head in range(pair)]
-
-    mine, theirs = [], []
-    for one in attended:
-        mine.append(jnp.where(row == 0, one[:rows], one[rows:]))
-        theirs.append(by_row(jnp.where(row == 0, one[rows:], one[:rows])))
+            sums[:, break_at : break_at + block],
+            everything[:, :, :block].reshape(pair, toks * block, size),
+            everything[:, :, block:].reshape(pair, toks * block, size),
+            places, starts, scale,
+        )
+        mine = jnp.where(row == 0, together[:rows], together[rows:])
+        theirs = jnp.where(row == 0, together[rows:], together[:rows])
+
+    theirs = by_row(theirs)
     return jnp.concatenate(
-        [jnp.where(row == 0, a, b) for a, b in zip(mine + theirs, theirs + mine)], axis=1
+        [jnp.where(row == 0, mine, theirs), jnp.where(row == 0, theirs, mine)], axis=1
     )
 
 

time: 83.8 us -> 66.9 us (0.80)
  waiting for transfers between devices: 35 us -> 17.7 us
  local copies, waits for them, and re-layouts: 13.5 us -> 8.19 us
  starting transfers between devices: 16.9 us -> 22.2 us
  Pallas kernels: 8.77 us -> 10.3 us
    ppermute x8 -> x7, waiting for transfers between devices: 24 us -> 9.44 us  [along_tok(): return lax.ppermute(value, 'tok', pairs)]
    unnamed x9 -> x11, local copies, waits for them, and re-layouts: 12.2 us -> 7.92 us
    ppermute x8 -> x7, starting transfers between devices: 8.54 us -> 11.7 us  [along_tok(): return lax.ppermute(value, 'tok', pairs)]
    ppermute x4, waiting for transfers between devices: 3.62 us -> 0.86 us  [by_col(): return lax.ppermute(value, 'col', [(c, c ^ flip) for c in range(4)])]
    ppermute x5 -> x4, starting transfers between devices: 2.76 us -> 4.92 us  [by_row(): return lax.ppermute(value, 'row', [(0, 1), (1, 0)])]
    pallas_call x2 -> x3, Pallas kernels: 3.55 us -> 5.04 us  [the longest x1 1.94 us: per_device(): pl.pallas_call(lambda *refs: own_kernel(scale, *refs), out_shape=(jax.Sha...]
    convert_element_type x5 -> x2, other arithmetic: 1.82 us -> 1.95 us  [the longest x1 0.99 us: per_device(): keys_b = jnp.where(tok < toks, summed(1, 0, break_at), one_up_a.astype(jn...]
    ppermute x5 -> x4, waiting for transfers between devices: 7.35 us -> 7.42 us  [by_row(): return lax.ppermute(value, 'row', [(0, 1), (1, 0)])]
  transfers between devices with their start and end apart: 19 -> 17, of which waited for: 7 -> 11; matrix products, arithmetic and copies ran while one was open for 18% -> 17% of each run, Pallas kernels for 8% -> 8%
where the time goes in v2:
time: 66.9 us; the launch traced here: 66.4 us
  starting transfers between devices  22.2 us (33%)
  waiting for transfers between devices  17.7 us (26%)
  Pallas kernels  10.3 us (15%)
  local copies, waits for them, and re-layouts  8.19 us (12%)
  other arithmetic  7.77 us (12%)
    ppermute x7, starting transfers between devices, along_tok(): return lax.ppermute(value, 'tok', pairs)  11.7 us
    ppermute x7, waiting for transfers between devices, along_tok(): return lax.ppermute(value, 'tok', pairs)  9.44 us
    unnamed x11, local copies, waits for them, and re-layouts  7.92 us
    ppermute x4, waiting for transfers between devices, by_row(): return lax.ppermute(value, 'row', [(0, 1), (1, 0)])  7.42 us
    ppermute x4, starting transfers between devices, by_row(): return lax.ppermute(value, 'row', [(0, 1), (1, 0)])  4.92 us
    ppermute x1, starting transfers between devices, per_device(): lax.ppermute(activations, ('row', 'col'), [(r * 4 + c, c // 2 * 4 + 2 * (...  3.31 us
    pallas_call x1, Pallas kernels, per_device(): projection(normalise_project_kernel, 1, True)  2.11 us
    pallas_call x1, Pallas kernels, per_device(): projection(project_kernel, pair, False)  1.95 us
  transfers between devices with their start and end apart: 17, of which 11 were waited for; matrix products, arithmetic and copies ran while one was open for 17% of the time, Pallas kernels for 8%

profile of v2, /device:TPU:24, one launch (start us, length us, event | category | flops | bytes accessed | tf_op | source)
XLA Modules:
  0.0 66.4 jit_solution(9941429487241351517)
XLA Ops:
  0.0 1.8 %collective-permute-start = (bf16[176,1024]{1,0:T(8,128)(2,1)}, bf16[176,1024]{1,0:T(8,128)(2,1)S(1)}, u32[]{:S(2)}, u32[]{:S(2)}) collective-permute-start(bf16[176,1024]{1,0:T(8,128)(2,1)} %param.4), channel_id=1, source_target_pairs={{0,0},{1,1},{2,4},{3,5},{4,2},{5,3},{6,6},{7,7},{8,8},{9,9},{10,12... | collective-permute-start | bytes 1081352 | tf_op jit(solution)/shard_map/ppermute | solution.py:286
  1.8 3.3 %collective-permute-start.1 = (bf16[176,1024]{1,0:T(8,128)(2,1)}, bf16[176,1024]{1,0:T(8,128)(2,1)S(1)}, u32[]{:S(2)}, u32[]{:S(2)}) collective-permute-start(bf16[176,1024]{1,0:T(8,128)(2,1)} %param.4), channel_id=1, source_target_pairs={{0,2},{1,3},{2,6},{3,7},{4,0},{5,1},{6,4},{7,5},{8,10},{9,11},{10,... | collective-permute-start | bytes 1081352 | tf_op jit(solution)/shard_map/ppermute | solution.py:291
  5.1 1.2 %multiply_reduce_fusion = f32[176]{0:T(256)S(1)} fusion(bf16[176,1024]{1,0:T(8,128)(2,1)} %param.4), kind=kLoop, calls=%fused_computation | loop fusion | flops 540496 | bytes 361152 | tf_op jit(solution)/shard_map/reduce_sum | solution.py:297
  6.2 0.7 %convert_element_type.59 = f32[1024]{0:T(1024)S(1)} convert(bf16[1024]{0:T(1024)(128)(2,1)} %param.5) | non-fusion elementwise | flops 1024 | bytes 6144 | tf_op jit(solution)/shard_map/convert_element_type | solution.py:298
  7.0 0.7 %convert_add_fusion = f32[176]{0:T(256)S(1)} fusion(s32[176]{0:T(256)} %param.7), kind=kLoop, calls=%fused_computation.36 | loop fusion | flops 352 | bytes 1408 | tf_op jit(solution)/shard_map/add | solution.py:310
  7.7 0.7 %fusion.9 = (f32[352,64]{1,0:T(8,128)S(1)}, f32[352,64]{1,0:T(8,128)S(1)}, f32[352,64]{1,0:T(8,128)S(1)}) fusion(f32[64]{0:T(128)S(1)} %negate_power_fusion, f32[352]{0:T(512)S(1)} %add_convert_fusion), kind=kLoop, calls=%fused_computation.24 | loop fusion | flops 45056 | bytes 272000 | tf_op jit(solution)/shard_map/neg | solution.py:24
  8.4 0.2 pad_maximum_fusion
  8.7 0.1 concatenate.40
  8.8 0.1 pad_add_fusion.1.place_ref
  8.9 4.0 %copy.6 = bf16[256,8,4,384]{3,1,2,0:T(8,128)(2,1)S(1)} copy(bf16[256,8,4,384]{3,2,1,0:T(4,128)(2,1)} %bitcast.51) | data formatting | bytes 12582912
  12.9 0.7 %collective-permute-done.3 = f32[2224]{0:T(1024)S(1)} collective-permute-done((f32[2224]{0:T(1024)S(1)}, f32[2224]{0:T(1024)S(1)}, u32[]{:S(2)}, u32[]{:S(2)}) %collective-permute-start.3) | collective-permute-done | bytes 8928 | tf_op jit(solution)/shard_map/ppermute | solution.py:277
  13.8 1.8 %collective-permute-start.6 = (f32[352]{0:T(512)S(1)}, f32[352]{0:T(512)S(1)}, u32[]{:S(2)}, u32[]{:S(2)}) collective-permute-start(f32[352]{0:T(512)S(1)} %pad_maximum_fusion.4), channel_id=1, source_target_pairs={{0,4},{4,0},{1,5},{5,1},{2,6},{6,2},{3,7},{7,3},{8,12},{12,8},{9,1... | collective-permute-start | bytes 4232 | tf_op jit(solution)/shard_map/ppermute | solution.py:280
  15.6 0.5 collective-permute-start.5
  16.1 1.3 %collective-permute-done.6 = f32[352]{0:T(512)S(1)} collective-permute-done((f32[352]{0:T(512)S(1)}, f32[352]{0:T(512)S(1)}, u32[]{:S(2)}, u32[]{:S(2)}) %collective-permute-start.6) | collective-permute-done | bytes 1440 | tf_op jit(solution)/shard_map/ppermute | solution.py:280
  17.5 0.1 reshape.70.squares_ref
  17.6 0.1 collective-permute-done.5.b_far
  17.7 2.1 %shard_map.46 = (f32[1,1088,128]{2,1,0:T(8,128)S(1)}, bf16[2,352,1024]{2,1,0:T(8,128)(2,1)S(1)}) custom-call(s32[3]{0:T(128)S(1)} %pad_add_fusion.1.place_ref, bf16[176,1024]{1,0:T(8,128)(2,1)S(1)} %collective-permute-done.a_near, bf16[176,1024]{1,0:T(8,128)(2,1)S(1)} %collective-permute-done.1.a_far, bf16[176,1024]{1,0:T(8,128)(2,1)S(1)} %collective-permute-done.4.b_near, ...), custom_call_target="tpu_custom_call" | custom-call | tf_op jit(solution)/shard_map/pallas_call | solution.py:341
  19.9 1.7 %collective-permute-start.7 = (f16[1088,128]{1,0:T(8,128)(2,1)S(1)}, f16[1088,128]{1,0:T(8,128)(2,1)}, u32[]{:S(2)}, u32[]{:S(2)}) collective-permute-start(f16[1088,128]{1,0:T(8,128)(2,1)S(1)} %bitcast.52), channel_id=1, source_target_pairs={{0,4},{4,0},{1,5},{5,1},{2,6},{6,2},{3,7},{7,3},{8,12},{12,8},{9,1... | collective-permute-start | bytes 835592 | tf_op jit(solution)/shard_map/ppermute | solution.py:280
  21.7 0.1 fusion.10.docs_ref
  21.8 2.8 %copy-done.1 = bf16[256,8,4,384]{3,1,2,0:T(8,128)(2,1)S(1)} copy-done((bf16[256,8,4,384]{3,1,2,0:T(8,128)(2,1)S(1)}, bf16[256,8,4,384]{3,1,2,0:T(8,128)(2,1)}, u32[]{:S(2)}) %copy-start.1) | copy-done | bytes 6291480
  24.5 1.2 %shard_map.47 = f32[1,1088,128]{2,1,0:T(8,128)S(1)} custom-call(s32[1]{0:T(128)} %bitcast.3.place_ref, bf16[2,352,1024]{2,1,0:T(8,128)(2,1)S(1)} %get-tuple-element.30.normed_ref, f32[16,128]{1,0:T(8,128)S(1)} %broadcast_in_dim.2.docs_ref, bf16[2048,1536]{1,0:T(8,128)(2,1)S(1)} %bitcast.49, f32[352,128]{1,0:T(8,128)S(1)} %get-tuple-element.55.cos_ref, ...), custom_call_target="tpu_custom_call" | custom-call | tf_op jit(solution)/shard_map/pallas_call | solution.py:348
  25.8 0.4 collective-permute-start.10
  26.2 1.2 %copy-done.2 = bf16[256,8,4,384]{3,1,2,0:T(8,128)(2,1)S(1)} copy-done((bf16[256,8,4,384]{3,1,2,0:T(8,128)(2,1)S(1)}, bf16[256,8,4,384]{3,1,2,0:T(8,128)(2,1)}, u32[]{:S(2)}) %copy-start.2) | copy-done | bytes 6291480
  27.3 2.0 %shard_map.48 = f32[2,1088,128]{2,1,0:T(8,128)S(1)} custom-call(s32[1]{0:T(128)} %bitcast.2.place_ref, bf16[2,352,1024]{2,1,0:T(8,128)(2,1)S(1)} %get-tuple-element.30.normed_ref, f32[16,128]{1,0:T(8,128)S(1)} %fusion.10.docs_ref, bf16[2048,1536]{1,0:T(8,128)(2,1)S(1)} %bitcast.50, f32[352,128]{1,0:T(8,128)S(1)} %get-tuple-element.55.cos_ref, ...), custom_call_target="tpu_custom_call" | custom-call | tf_op jit(solution)/shard_map/pallas_call | solution.py:354
  29.3 0.3 collective-permute-done.7
  29.6 1.0 %fusion.4.refs_1_ = bf16[720,128]{1,0:T(8,128)(2,1)S(1)} fusion(f32[2,1088,128]{2,1,0:T(8,128)S(1)} %shard_map.48, f16[1088,128]{1,0:T(8,128)(2,1)} %collective-permute-done.7), kind=kLoop, calls=%fused_computation.7 | loop fusion | flops 276480 | bytes 737280 | tf_op jit(solution)/shard_map/convert_element_type | solution.py:366
  30.6 1.3 %collective-permute-start.8 = (bf16[720,128]{1,0:T(8,128)(2,1)S(1)}, bf16[720,128]{1,0:T(8,128)(2,1)S(1)}, u32[]{:S(2)}, u32[]{:S(2)}) collective-permute-start(bf16[720,128]{1,0:T(8,128)(2,1)S(1)} %fusion.4.refs_1_), channel_id=1, source_target_pairs={{0,8},{8,16},{16,24},{1,9},{9,17},{17,25},{2,10},{10,18},{18,26},{... | collective-permute-start | bytes 552968 | tf_op jit(solution)/shard_map/ppermute | solution.py:360
  31.9 0.7 %collective-permute-start.9 = (bf16[720,128]{1,0:T(8,128)(2,1)S(1)}, bf16[720,128]{1,0:T(8,128)(2,1)S(1)}, u32[]{:S(2)}, u32[]{:S(2)}) collective-permute-start(bf16[720,128]{1,0:T(8,128)(2,1)S(1)} %fusion.4.refs_1_), channel_id=1, source_target_pairs={{0,16},{1,17},{2,18},{3,19},{4,20},{5,21},{6,22},{7,23}} | collective-permute-start | bytes 552968 | tf_op jit(solution)/shard_map/ppermute | solution.py:360
  32.6 2.2 %collective-permute-done.10 = f16[1088,128]{1,0:T(8,128)(2,1)} collective-permute-done((f16[1088,128]{1,0:T(8,128)(2,1)S(1)}, f16[1088,128]{1,0:T(8,128)(2,1)}, u32[]{:S(2)}, u32[]{:S(2)}) %collective-permute-start.10) | collective-permute-done | bytes 278560 | tf_op jit(solution)/shard_map/ppermute | solution.py:280
  34.8 3.2 %collective-permute-done.8.refs_4_.refs_2_ = bf16[720,128]{1,0:T(8,128)(2,1)S(1)} collective-permute-done((bf16[720,128]{1,0:T(8,128)(2,1)S(1)}, bf16[720,128]{1,0:T(8,128)(2,1)S(1)}, u32[]{:S(2)}, u32[]{:S(2)}) %collective-permute-start.8) | collective-permute-done | bytes 184352 | tf_op jit(solution)/shard_map/ppermute | solution.py:360
  38.0 1.0 %fusion.2.refs_6_.refs_5_ = bf16[720,128]{1,0:T(8,128)(2,1)S(1)} fusion(f32[2,1088,128]{2,1,0:T(8,128)S(1)} %shard_map.48, bf16[720,128]{1,0:T(8,128)(2,1)S(1)} %collective-permute-done.8.refs_4_.refs_2_, f16[1088,128]{1,0:T(8,128)(2,1)} %collective-permute-done.10, pred[]{:T(512)S(6)} %lt.3), kind=kLoop, calls=%fused_computation.4 | loop fusion | flops 460800 | bytes 921601 | tf_op jit(solution)/shard_map/convert_element_type | solution.py:372
  39.0 1.3 %collective-permute-start.11 = (bf16[720,128]{1,0:T(8,128)(2,1)S(1)}, bf16[720,128]{1,0:T(8,128)(2,1)S(1)}, u32[]{:S(2)}, u32[]{:S(2)}) collective-permute-start(bf16[720,128]{1,0:T(8,128)(2,1)S(1)} %fusion.2.refs_6_.refs_5_), channel_id=1, source_target_pairs={{0,8},{16,24},{1,9},{17,25},{2,10},{18,26},{3,11},{19,27},{4,12},{... | collective-permute-start | bytes 552968 | tf_op jit(solution)/shard_map/ppermute | solution.py:360
  40.3 1.0 %broadcast_select_fusion = (bf16[368,128]{1,0:T(8,128)(2,1)S(1)}, bf16[368,128]{1,0:T(8,128)(2,1)S(1)}, bf16[368,128]{1,0:T(8,128)(2,1)S(1)}) fusion(pred[]{:T(512)S(6)} %eq.18, f16[1088,128]{1,0:T(8,128)(2,1)} %collective-permute-done.10, f32[2,1088,128]{2,1,0:T(8,128)S(1)} %shard_map.48, f16[1088,128]{1,0:T(8,128)(2,1)} %collective-permute-done.7), kind=kLoop, calls=%fused_computation.21 | loop fusion | flops 329728 | bytes 847873 | tf_op jit(solution)/shard_map/jit(_where)/select_n | solution.py:374
  41.3 4.6 %collective-permute-start.12 = (bf16[368,128]{1,0:T(8,128)(2,1)S(1)}, bf16[368,128]{1,0:T(8,128)(2,1)S(1)}, u32[]{:S(2)}, u32[]{:S(2)}) collective-permute-start(bf16[368,128]{1,0:T(8,128)(2,1)S(1)} %get-tuple-element.37), channel_id=1, source_target_pairs={{16,8},{24,16},{17,9},{25,17},{18,10},{26,18},{19,11},{27,19},{20,... | collective-permute-start | bytes 282632 | tf_op jit(solution)/shard_map/ppermute | solution.py:360
  45.9 1.3 %collective-permute-start.13 = (bf16[368,128]{1,0:T(8,128)(2,1)S(1)}, bf16[368,128]{1,0:T(8,128)(2,1)S(1)}, u32[]{:S(2)}, u32[]{:S(2)}) collective-permute-start(bf16[368,128]{1,0:T(8,128)(2,1)S(1)} %get-tuple-element.38.refs_4_), channel_id=1, source_target_pairs={{24,8},{25,9},{26,10},{27,11},{28,12},{29,13},{30,14},{31,15}} | collective-permute-start | bytes 282632 | tf_op jit(solution)/shard_map/ppermute | solution.py:360
  47.2 0.8 %collective-permute-done.12.refs_1_ = bf16[368,128]{1,0:T(8,128)(2,1)S(1)} collective-permute-done((bf16[368,128]{1,0:T(8,128)(2,1)S(1)}, bf16[368,128]{1,0:T(8,128)(2,1)S(1)}, u32[]{:S(2)}, u32[]{:S(2)}) %collective-permute-start.12) | collective-permute-done | bytes 94240 | tf_op jit(solution)/shard_map/ppermute | solution.py:360
  48.0 1.3 %collective-permute-done.13.refs_2_ = bf16[368,128]{1,0:T(8,128)(2,1)S(1)} collective-permute-done((bf16[368,128]{1,0:T(8,128)(2,1)S(1)}, bf16[368,128]{1,0:T(8,128)(2,1)S(1)}, u32[]{:S(2)}, u32[]{:S(2)}) %collective-permute-start.13) | collective-permute-done | bytes 94240 | tf_op jit(solution)/shard_map/ppermute | solution.py:360
  49.3 1.9 %shard_map.49.refs_7_ = bf16[2,368,128]{2,1,0:T(8,128)(2,1)S(1)} custom-call(s32[1]{0:T(128)} %bitcast.refs_0_, bf16[368,128]{1,0:T(8,128)(2,1)S(1)} %collective-permute-done.12.refs_1_, bf16[368,128]{1,0:T(8,128)(2,1)S(1)} %collective-permute-done.13.refs_2_, bf16[720,128]{1,0:T(8,128)(2,1)S(1)} %collective-permute-done.9.refs_3_, ...), custom_call_target="tpu_custom_call" | custom-call | tf_op jit(solution)/shard_map/pallas_call | solution.py:377
  51.2 1.3 %collective-permute-start.14 = (bf16[368,128]{1,0:T(8,128)(2,1)S(1)}, bf16[368,128]{1,0:T(8,128)(2,1)S(1)}, u32[]{:S(2)}, u32[]{:S(2)}) collective-permute-start(bf16[368,128]{1,0:T(8,128)(2,1)S(1)} %get-tuple-element.41), channel_id=1, source_target_pairs={{8,16},{16,24},{9,17},{17,25},{10,18},{18,26},{11,19},{19,27},{12,... | collective-permute-start | bytes 282632 | tf_op jit(solution)/shard_map/ppermute | solution.py:360
  52.5 1.3 %collective-permute-start.15 = (bf16[368,128]{1,0:T(8,128)(2,1)S(1)}, bf16[368,128]{1,0:T(8,128)(2,1)S(1)}, u32[]{:S(2)}, u32[]{:S(2)}) collective-permute-start(bf16[368,128]{1,0:T(8,128)(2,1)S(1)} %get-tuple-element.40), channel_id=1, source_target_pairs={{8,24},{9,25},{10,26},{11,27},{12,28},{13,29},{14,30},{15,31}} | collective-permute-start | bytes 282632 | tf_op jit(solution)/shard_map/ppermute | solution.py:360
  53.8 0.1 pad_add_fusion.place_ref
  53.9 1.9 %shard_map.50 = (f32[2,352,128]{2,1,0:T(8,128)S(1)}, f32[2,352,1]{2,1,0:T(8,128)S(1)}) custom-call(bf16[368,128]{1,0:T(8,128)(2,1)S(1)} %get-tuple-element.39.refs_0_, bf16[720,128]{1,0:T(8,128)(2,1)S(1)} %fusion.4.refs_1_, bf16[720,128]{1,0:T(8,128)(2,1)S(1)} %collective-permute-done.8.refs_4_.refs_2_, bf16[720,128]{1,0:T(8,128)(2,1)S(1)} %collective-permute-done.9.refs_3_, ...), custom_call_target="tpu_custom_call" | custom-call | tf_op jit(solution)/shard_map/pallas_call | solution.py:386
  55.8 1.8 %collective-permute-done.14.one_ref = bf16[368,128]{1,0:T(8,128)(2,1)S(1)} collective-permute-done((bf16[368,128]{1,0:T(8,128)(2,1)S(1)}, bf16[368,128]{1,0:T(8,128)(2,1)S(1)}, u32[]{:S(2)}, u32[]{:S(2)}) %collective-permute-start.14) | collective-permute-done | bytes 94240 | tf_op jit(solution)/shard_map/ppermute | solution.py:360
  57.7 2.2 %collective-permute-done.15.two_ref = bf16[368,128]{1,0:T(8,128)(2,1)S(1)} collective-permute-done((bf16[368,128]{1,0:T(8,128)(2,1)S(1)}, bf16[368,128]{1,0:T(8,128)(2,1)S(1)}, u32[]{:S(2)}, u32[]{:S(2)}) %collective-permute-start.15) | collective-permute-done | bytes 94240 | tf_op jit(solution)/shard_map/ppermute | solution.py:360
  59.9 1.2 %shard_map.51 = (bf16[176,256]{1,0:T(8,128)(2,1)S(1)}, bf16[176,256]{1,0:T(8,128)(2,1)S(1)}) custom-call(s32[2]{0:T(128)S(1)} %pad_add_fusion.place_ref, f32[2,352,128]{2,1,0:T(8,128)S(1)} %get-tuple-element.33.out_ref, f32[2,352,1]{2,1,0:T(8,128)S(1)} %get-tuple-element.34.logs_ref, bf16[368,128]{1,0:T(8,128)(2,1)S(1)} %collective-permute-done.14.one_ref, ...), custom_call_target="tpu_custom_call" | custom-call | tf_op jit(solution)/shard_map/pallas_call | solution.py:398
  61.1 1.0 %collective-permute-start.16 = (bf16[176,256]{1,0:T(8,128)(2,1)S(1)}, bf16[176,256]{1,0:T(8,128)(2,1)S(1)}, u32[]{:S(2)}, u32[]{:S(2)}) collective-permute-start(bf16[176,256]{1,0:T(8,128)(2,1)S(1)} %get-tuple-element.36), channel_id=1, source_target_pairs={{0,4},{4,0},{1,5},{5,1},{2,6},{6,2},{3,7},{7,3},{8,12},{12,8},{9,1... | collective-permute-start | bytes 270344 | tf_op jit(solution)/shard_map/ppermute | solution.py:280
  62.1 3.6 %collective-permute-done.16 = bf16[176,256]{1,0:T(8,128)(2,1)S(1)} collective-permute-done((bf16[176,256]{1,0:T(8,128)(2,1)S(1)}, bf16[176,256]{1,0:T(8,128)(2,1)S(1)}, u32[]{:S(2)}, u32[]{:S(2)}) %collective-permute-start.16) | collective-permute-done | bytes 90144 | tf_op jit(solution)/shard_map/ppermute | solution.py:280
  65.7 0.7 %pad_maximum_fusion.2 = bf16[176,512]{1,0:T(8,128)(2,1)} fusion(bf16[176,256]{1,0:T(8,128)(2,1)S(1)} %get-tuple-element.43, bf16[176,256]{1,0:T(8,128)(2,1)S(1)} %get-tuple-element.42), kind=kLoop, calls=%fused_computation.18 | loop fusion | flops 360448 | bytes 360448 | tf_op jit(solution)/shard_map/concatenate | solution.py:421
  (33 shorter events, 0.6 us)
Async XLA Ops:
  0.0 8.6 %copy-start.3 = (bf16[1024]{0:T(1024)(128)(2,1)S(1)}, bf16[1024]{0:T(1024)(128)(2,1)}, u32[]{:S(2)}) copy-start(bf16[1024]{0:T(1024)(128)(2,1)} %param.5) | copy-start | bytes 6148
  0.0 13.6 %collective-permute-start = (bf16[176,1024]{1,0:T(8,128)(2,1)}, bf16[176,1024]{1,0:T(8,128)(2,1)S(1)}, u32[]{:S(2)}, u32[]{:S(2)}) collective-permute-start(bf16[176,1024]{1,0:T(8,128)(2,1)} %param.4), channel_id=1, source_target_pairs={{0,0},{1,1},{2,4},{3,5},{4,2},{5,3},{6,6},{7,7},{8,8},{9,9},{10,12... | collective-permute-start | bytes 1081352 | tf_op jit(solution)/shard_map/ppermute | solution.py:286
  1.8 11.8 %collective-permute-start.1 = (bf16[176,1024]{1,0:T(8,128)(2,1)}, bf16[176,1024]{1,0:T(8,128)(2,1)S(1)}, u32[]{:S(2)}, u32[]{:S(2)}) collective-permute-start(bf16[176,1024]{1,0:T(8,128)(2,1)} %param.4), channel_id=1, source_target_pairs={{0,2},{1,3},{2,6},{3,7},{4,0},{5,1},{6,4},{7,5},{8,10},{9,11},{10,... | collective-permute-start | bytes 1081352 | tf_op jit(solution)/shard_map/ppermute | solution.py:291
  7.0 1.6 %collective-permute-start.2 = (f32[1200]{0:T(1024)S(1)}, f32[1200]{0:T(1024)S(1)}, u32[]{:S(2)}, u32[]{:S(2)}) collective-permute-start(f32[1200]{0:T(1024)S(1)} %pad_maximum_fusion.3), channel_id=1, source_target_pairs={{0,1},{1,0},{2,3},{3,2},{4,5},{5,4},{6,7},{7,6},{8,9},{9,8},{10,11... | collective-permute-start | bytes 14408 | tf_op jit(solution)/shard_map/ppermute | solution.py:277
  8.8 4.8 %collective-permute-start.3 = (f32[2224]{0:T(1024)S(1)}, f32[2224]{0:T(1024)S(1)}, u32[]{:S(2)}, u32[]{:S(2)}) collective-permute-start(f32[2224]{0:T(1024)S(1)} %concatenate.40), channel_id=1, source_target_pairs={{0,2},{1,3},{2,0},{3,1},{4,6},{5,7},{6,4},{7,5},{8,10},{9,11},{10,... | collective-permute-start | bytes 26696 | tf_op jit(solution)/shard_map/ppermute | solution.py:277
  8.9 8.5 %copy-start.4 = (s32[176]{0:T(256)S(1)}, s32[176]{0:T(256)}, u32[]{:S(2)}) copy-start(s32[176]{0:T(256)} %param.7) | copy-start | bytes 2116
  12.9 7.0 %copy-start = (bf16[256,8,4,384]{3,1,2,0:T(8,128)(2,1)}, bf16[256,8,4,384]{3,1,2,0:T(8,128)(2,1)S(1)}, u32[]{:S(2)}) copy-start(bf16[256,8,4,384]{3,1,2,0:T(8,128)(2,1)S(1)} %copy.6) | copy-start | bytes 18874372
  13.8 3.6 %collective-permute-start.6 = (f32[352]{0:T(512)S(1)}, f32[352]{0:T(512)S(1)}, u32[]{:S(2)}, u32[]{:S(2)}) collective-permute-start(f32[352]{0:T(512)S(1)} %pad_maximum_fusion.4), channel_id=1, source_target_pairs={{0,4},{4,0},{1,5},{5,1},{2,6},{6,2},{3,7},{7,3},{8,12},{12,8},{9,1... | collective-permute-start | bytes 4232 | tf_op jit(solution)/shard_map/ppermute | solution.py:280
  15.6 2.1 %collective-permute-start.4 = (bf16[176,1024]{1,0:T(8,128)(2,1)S(1)}, bf16[176,1024]{1,0:T(8,128)(2,1)S(1)}, u32[]{:S(2)}, u32[]{:S(2)}) collective-permute-start(bf16[176,1024]{1,0:T(8,128)(2,1)S(1)} %collective-permute-done.a_near), channel_id=1, source_target_pairs={{0,1},{1,0},{2,3},{3,2},{4,5},{5,4},{6,7},{7,6},{8,9},{9,8},{10,11... | collective-permute-start | bytes 1081352 | tf_op jit(solution)/shard_map/ppermute | solution.py:277
  15.6 2.2 %collective-permute-start.5 = (bf16[176,1024]{1,0:T(8,128)(2,1)S(1)}, bf16[176,1024]{1,0:T(8,128)(2,1)S(1)}, u32[]{:S(2)}, u32[]{:S(2)}) collective-permute-start(bf16[176,1024]{1,0:T(8,128)(2,1)S(1)} %collective-permute-done.1.a_far), channel_id=1, source_target_pairs={{0,1},{1,0},{2,3},{3,2},{4,5},{5,4},{6,7},{7,6},{8,9},{9,8},{10,11... | collective-permute-start | bytes 1081352 | tf_op jit(solution)/shard_map/ppermute | solution.py:277
  19.9 9.7 %collective-permute-start.7 = (f16[1088,128]{1,0:T(8,128)(2,1)S(1)}, f16[1088,128]{1,0:T(8,128)(2,1)}, u32[]{:S(2)}, u32[]{:S(2)}) collective-permute-start(f16[1088,128]{1,0:T(8,128)(2,1)S(1)} %bitcast.52), channel_id=1, source_target_pairs={{0,4},{4,0},{1,5},{5,1},{2,6},{6,2},{3,7},{7,3},{8,12},{12,8},{9,1... | collective-permute-start | bytes 835592 | tf_op jit(solution)/shard_map/ppermute | solution.py:280
  21.7 2.8 %copy-start.1 = (bf16[256,8,4,384]{3,1,2,0:T(8,128)(2,1)S(1)}, bf16[256,8,4,384]{3,1,2,0:T(8,128)(2,1)}, u32[]{:S(2)}) copy-start(bf16[256,8,4,384]{3,1,2,0:T(8,128)(2,1)} %copy-done) | copy-start | bytes 18874372
  24.5 2.8 %copy-start.2 = (bf16[256,8,4,384]{3,1,2,0:T(8,128)(2,1)S(1)}, bf16[256,8,4,384]{3,1,2,0:T(8,128)(2,1)}, u32[]{:S(2)}) copy-start(bf16[256,8,4,384]{3,1,2,0:T(8,128)(2,1)} %copy-done) | copy-start | bytes 18874372
  25.8 9.0 %collective-permute-start.10 = (f16[1088,128]{1,0:T(8,128)(2,1)S(1)}, f16[1088,128]{1,0:T(8,128)(2,1)}, u32[]{:S(2)}, u32[]{:S(2)}) collective-permute-start(f16[1088,128]{1,0:T(8,128)(2,1)S(1)} %bitcast.53), channel_id=1, source_target_pairs={{0,4},{4,0},{1,5},{5,1},{2,6},{6,2},{3,7},{7,3},{8,12},{12,8},{9,1... | collective-permute-start | bytes 835592 | tf_op jit(solution)/shard_map/ppermute | solution.py:280
  30.6 7.4 %collective-permute-start.8 = (bf16[720,128]{1,0:T(8,128)(2,1)S(1)}, bf16[720,128]{1,0:T(8,128)(2,1)S(1)}, u32[]{:S(2)}, u32[]{:S(2)}) collective-permute-start(bf16[720,128]{1,0:T(8,128)(2,1)S(1)} %fusion.4.refs_1_), channel_id=1, source_target_pairs={{0,8},{8,16},{16,24},{1,9},{9,17},{17,25},{2,10},{10,18},{18,26},{... | collective-permute-start | bytes 552968 | tf_op jit(solution)/shard_map/ppermute | solution.py:360
  31.9 17.4 %collective-permute-start.9 = (bf16[720,128]{1,0:T(8,128)(2,1)S(1)}, bf16[720,128]{1,0:T(8,128)(2,1)S(1)}, u32[]{:S(2)}, u32[]{:S(2)}) collective-permute-start(bf16[720,128]{1,0:T(8,128)(2,1)S(1)} %fusion.4.refs_1_), channel_id=1, source_target_pairs={{0,16},{1,17},{2,18},{3,19},{4,20},{5,21},{6,22},{7,23}} | collective-permute-start | bytes 552968 | tf_op jit(solution)/shard_map/ppermute | solution.py:360
  39.0 10.3 %collective-permute-start.11 = (bf16[720,128]{1,0:T(8,128)(2,1)S(1)}, bf16[720,128]{1,0:T(8,128)(2,1)S(1)}, u32[]{:S(2)}, u32[]{:S(2)}) collective-permute-start(bf16[720,128]{1,0:T(8,128)(2,1)S(1)} %fusion.2.refs_6_.refs_5_), channel_id=1, source_target_pairs={{0,8},{16,24},{1,9},{17,25},{2,10},{18,26},{3,11},{19,27},{4,12},{... | collective-permute-start | bytes 552968 | tf_op jit(solution)/shard_map/ppermute | solution.py:360
  41.3 6.7 %collective-permute-start.12 = (bf16[368,128]{1,0:T(8,128)(2,1)S(1)}, bf16[368,128]{1,0:T(8,128)(2,1)S(1)}, u32[]{:S(2)}, u32[]{:S(2)}) collective-permute-start(bf16[368,128]{1,0:T(8,128)(2,1)S(1)} %get-tuple-element.37), channel_id=1, source_target_pairs={{16,8},{24,16},{17,9},{25,17},{18,10},{26,18},{19,11},{27,19},{20,... | collective-permute-start | bytes 282632 | tf_op jit(solution)/shard_map/ppermute | solution.py:360
  45.9 3.5 %collective-permute-start.13 = (bf16[368,128]{1,0:T(8,128)(2,1)S(1)}, bf16[368,128]{1,0:T(8,128)(2,1)S(1)}, u32[]{:S(2)}, u32[]{:S(2)}) collective-permute-start(bf16[368,128]{1,0:T(8,128)(2,1)S(1)} %get-tuple-element.38.refs_4_), channel_id=1, source_target_pairs={{24,8},{25,9},{26,10},{27,11},{28,12},{29,13},{30,14},{31,15}} | collective-permute-start | bytes 282632 | tf_op jit(solution)/shard_map/ppermute | solution.py:360
  51.2 6.5 %collective-permute-start.14 = (bf16[368,128]{1,0:T(8,128)(2,1)S(1)}, bf16[368,128]{1,0:T(8,128)(2,1)S(1)}, u32[]{:S(2)}, u32[]{:S(2)}) collective-permute-start(bf16[368,128]{1,0:T(8,128)(2,1)S(1)} %get-tuple-element.41), channel_id=1, source_target_pairs={{8,16},{16,24},{9,17},{17,25},{10,18},{18,26},{11,19},{19,27},{12,... | collective-permute-start | bytes 282632 | tf_op jit(solution)/shard_map/ppermute | solution.py:360
  52.5 7.4 %collective-permute-start.15 = (bf16[368,128]{1,0:T(8,128)(2,1)S(1)}, bf16[368,128]{1,0:T(8,128)(2,1)S(1)}, u32[]{:S(2)}, u32[]{:S(2)}) collective-permute-start(bf16[368,128]{1,0:T(8,128)(2,1)S(1)} %get-tuple-element.40), channel_id=1, source_target_pairs={{8,24},{9,25},{10,26},{11,27},{12,28},{13,29},{14,30},{15,31}} | collective-permute-start | bytes 282632 | tf_op jit(solution)/shard_map/ppermute | solution.py:360
  61.1 4.6 %collective-permute-start.16 = (bf16[176,256]{1,0:T(8,128)(2,1)S(1)}, bf16[176,256]{1,0:T(8,128)(2,1)S(1)}, u32[]{:S(2)}, u32[]{:S(2)}) collective-permute-start(bf16[176,256]{1,0:T(8,128)(2,1)S(1)} %get-tuple-element.36), channel_id=1, source_target_pairs={{0,4},{4,0},{1,5},{5,1},{2,6},{6,2},{3,7},{7,3},{8,12},{12,8},{9,1... | collective-permute-start | bytes 270344 | tf_op jit(solution)/shard_map/ppermute | solution.py:280

commit v3 on v2

--- a/solution.py
+++ b/solution.py
@@ -157,65 +157,95 @@
     return summed / safe, jnp.where(some, top + jnp.log(safe), LOW)
 
 
-def guest_kernel(
-    scale, tok_ref, query_one, query_two, up_first, up_second, down_first, down_second, out_ref
+def as_message(output, logs, size):
+    high = logs.astype(jnp.bfloat16).astype(jnp.float32)
+    middle = (logs - high).astype(jnp.bfloat16).astype(jnp.float32)
+    rows = as_rows(high, size) + as_rows(middle, size) + as_rows(logs - high - middle, size)
+    rows.append(jnp.zeros((EXTRA - len(rows), size), jnp.float32))
+    return jnp.concatenate([output] + rows, axis=0).astype(jnp.bfloat16)
+
+
+def parted(row, value):
+    rows = value.shape[0] // 2
+    first = row == 0
+    return (
+        jnp.where(first, value[:rows], value[rows:]),
+        jnp.where(first, value[rows:], value[:rows]),
+    )
+
+
+def guest_kernel(scale, here, place_ref, *refs):
+    count = len(refs) - 3
+    query_refs, message_refs, out_ref = refs[:count], refs[count:-1], refs[-1]
+
+    @pl.when(place_ref[0] == here)
+    def attend():
+        messages = [ref[...] for ref in message_refs]
+        for index, query_ref in enumerate(query_refs):
+            block, size = query_ref.shape[0] - EXTRA, query_ref.shape[1]
+            docs = as_column(query_ref[block:, :].astype(jnp.float32), block)
+            output, logs = softmax_part(scale, query_ref[:block, :], docs, messages, False)
+            for owner, (a, b) in enumerate(
+                zip(parted(place_ref[1], output), parted(place_ref[1], logs))
+            ):
+                out_ref[index, owner] = as_message(a, b, size)
+
+
+def own_kernel(
+    scale, place_ref, query_down, own_down, one_down, query_up, own_up, one_up, two_up, unused_ref,
+    mine_ref, logs_ref, theirs_ref,
 ):
-    block = query_one.shape[0] - EXTRA
-    size = query_one.shape[1]
-    at_two = tok_ref[0] == 2
-    messages = [
-        jnp.where(at_two, up_first[...], down_first[...]),
-        jnp.where(at_two, up_second[...], down_second[...]),
-    ]
-    for index, query_ref in enumerate((query_one, query_two)):
-        docs = as_column(query_ref[block:, :].astype(jnp.float32), block)
-        output, logs = softmax_part(scale, query_ref[:block, :], docs, messages, False)
-        out_ref[index, :block, :] = output.astype(jnp.bfloat16)
-        high = logs.astype(jnp.bfloat16).astype(jnp.float32)
-        middle = (logs - high).astype(jnp.bfloat16).astype(jnp.float32)
-        rows = as_rows(high, size) + as_rows(middle, size) + as_rows(logs - high - middle, size)
-        rows.append(jnp.zeros((EXTRA - len(rows), size), jnp.float32))
-        out_ref[index, block:, :] = jnp.concatenate(rows, axis=0).astype(jnp.bfloat16)
-
-
-def own_kernel(
-    scale, query_a, own_a, one_up_a, two_up_a, query_b, own_b, one_up_b, unused, out_ref, logs_ref
-):
-    block = query_a.shape[0] - EXTRA
+    block, size = query_down.shape[0] - EXTRA, query_down.shape[1]
     for index, (query_ref, refs) in enumerate(
-        ((query_a, (own_a, one_up_a, two_up_a)), (query_b, (own_b, one_up_b)))
+        ((query_down, (own_down, one_down)), (query_up, (own_up, one_up, two_up)))
     ):
         docs = as_column(query_ref[block:, :].astype(jnp.float32), block)
         output, logs = softmax_part(
             scale, query_ref[:block, :], docs, [ref[...] for ref in refs], True
         )
-        out_ref[index] = output
-        logs_ref[index] = logs
-
-
-def merge_kernel(place_ref, out_ref, logs_ref, one_ref, two_ref, mine_ref, theirs_ref):
-    block, size = out_ref.shape[1:]
-    groups = pl.cdiv(block, size)
+        mine, theirs = parted(place_ref[1], output)
+        my_logs, their_logs = parted(place_ref[1], logs)
+        mine_ref[index] = mine
+        logs_ref[index] = my_logs
+        theirs_ref[index] = as_message(theirs, their_logs, size)
+
+
+def merge_kernel(
+    place_ref, mine_ref, logs_ref, partner_ref, two_same, two_cross, three_same, three_cross,
+    up_same, up_cross, out_ref,
+):
+    rows, size = mine_ref.shape[1:]
+    groups = pl.cdiv(rows, size)
     tok, row = place_ref[0], place_ref[1]
-    rows = block // 2
-    at_two, at_three = tok == 2, tok == 3
-
-    def joined(index, message, present):
-        logs = logs_ref[index]
-        tile = message[block:].astype(jnp.float32)
-        guest = sum(as_column(tile[k * groups : (k + 1) * groups], block) for k in range(3))
-        guest = jnp.where(present, guest, LOW)
+
+    def logs_of(message):
+        tile = message[rows:].astype(jnp.float32)
+        return sum(as_column(tile[k * groups : (k + 1) * groups], rows) for k in range(3))
+
+    def joined(output, logs, message, present):
+        guest = jnp.where(present, logs_of(message), LOW)
         top = jnp.maximum(logs, guest)
         weight, guest_weight = jnp.exp(logs - top), jnp.exp(guest - top)
-        output = out_ref[index] * weight + message[:block].astype(jnp.float32) * guest_weight
-        return (output / (weight + guest_weight)).astype(jnp.bfloat16)
-
-    first = joined(0, one_ref[...], at_three)
-    second = joined(1, jnp.where(at_two, one_ref[...], two_ref[...]), at_two | at_three)
-    for index, output in enumerate((first, second)):
-        columns = slice(index * size, (index + 1) * size)
-        mine_ref[:, columns] = jnp.where(row == 0, output[:rows], output[rows:])
-        theirs_ref[:, columns] = jnp.where(row == 0, output[rows:], output[:rows])
+        total = output * weight + message[:rows].astype(jnp.float32) * guest_weight
+        return (total / (weight + guest_weight)).astype(jnp.bfloat16)
+
+    at_two, at_three = tok == 2, tok == 3
+    for mine, two, three, up in (
+        (True, two_same, three_same, up_same),
+        (False, two_cross, three_cross, up_cross),
+    ):
+        begin = jnp.where(row == 0, 0, 1) if mine else jnp.where(row == 0, 1, 0)
+        down = jnp.where(at_two, two[...], three[...])
+        for index, (message, present) in enumerate(
+            ((down, at_two | at_three), (up[...], at_three))
+        ):
+            if mine:
+                output, logs = mine_ref[index], logs_ref[index]
+            else:
+                partner = partner_ref[index]
+                output, logs = partner[:rows].astype(jnp.float32), logs_of(partner)
+            at = pl.ds(pl.multiple_of((2 * begin + index) * size, size), size)
+            out_ref[:, at] = joined(output, logs, message, present)
 
 
 def attend_gathered(query, keys, values, places, starts, scale):
@@ -363,59 +393,84 @@
         return own[head, begin:end] + arrived[head][begin:end].astype(jnp.float32)
 
     if toks == 4 and pair == 2:
-        keys_a = summed(0, 0, break_at).astype(jnp.bfloat16)
-        query_a = summed(0, break_at, taller).astype(jnp.bfloat16)
-        one_up_a = along_tok(keys_a, [(0, 1), (1, 2), (2, 3)])
-        two_up_a = along_tok(keys_a, [(0, 2)])
-        keys_b = jnp.where(
-            tok < toks, summed(1, 0, break_at), one_up_a.astype(jnp.float32)
-        ).astype(jnp.bfloat16)
-        query_b = summed(1, break_at, taller).astype(jnp.bfloat16)
-        guest_one = along_tok(jnp.where(tok == 3, query_a, query_b), [(2, 1), (3, 2)])
-        guest_two = along_tok(query_b, [(3, 1)])
-        one_up_b = along_tok(keys_b, [(0, 1), (2, 3)])
-        guests = pl.pallas_call(
-            lambda *refs: guest_kernel(scale, *refs),
-            out_shape=jax.ShapeDtypeStruct((2, block + EXTRA, size), jnp.bfloat16),
-            in_specs=[pl.BlockSpec(memory_space=pltpu.SMEM)] + in_vmem(6),
+        places = jnp.stack([tok, row])
+
+        def returned(value, pairs):
+            across = [(2 * a + r, 2 * b + 1 - r) for a, b in pairs for r in range(2)]
+            return along_tok(value[0], pairs), lax.ppermute(value[1], ("tok", "row"), across)
+
+        def guests(here, queries, messages):
+            shape = (len(queries), 2, rows + EXTRA, size)
+            return pl.pallas_call(
+                lambda *refs: guest_kernel(scale, here, *refs),
+                out_shape=jax.ShapeDtypeStruct(shape, jnp.bfloat16),
+                in_specs=[pl.BlockSpec(memory_space=pltpu.SMEM)] + in_vmem(len(queries) + 2),
+                out_specs=in_vmem(1)[0],
+                compiler_params=pltpu.CompilerParams(vmem_limit_bytes=16 * MIB),
+            )(places, *queries, *messages)
+
+        query_down = summed(0, break_at, taller).astype(jnp.bfloat16)
+        keys_down = summed(0, 0, break_at).astype(jnp.bfloat16)
+        from_three = along_tok(query_down, [(3, 1)])
+        from_two = along_tok(query_down, [(2, 1)])
+        one_down = along_tok(keys_down, [(0, 1), (2, 3)])
+
+        arrived[1] = jnp.where(
+            tok < toks,
+            arrived[1].astype(jnp.float32),
+            jnp.broadcast_to(from_two[:1].astype(jnp.float32), arrived[1].shape),
+        )
+        keys_up = summed(1, 0, break_at).astype(jnp.bfloat16)
+        query_up = summed(1, break_at, taller).astype(jnp.bfloat16)
+        two_up = along_tok(keys_up, [(0, 2)])
+        three_up = along_tok(query_up, [(3, 2)])
+        one_up = along_tok(keys_up, [(0, 1), (1, 2), (2, 3)])
+
+        down = guests(1, [from_two, from_three], [one_down, keys_down])
+        three_same, three_cross = returned(down[1], [(1, 3)])
+        two_same, two_cross = returned(down[0], [(1, 2)])
+        up = guests(2, [three_up], [two_up, one_up])
+        up_same, up_cross = returned(up[0], [(2, 3)])
+
+        mine, logs, theirs = pl.pallas_call(
+            lambda *refs: own_kernel(scale, *refs),
+            out_shape=(
+                jax.ShapeDtypeStruct((2, rows, size), jnp.float32),
+                jax.ShapeDtypeStruct((2, rows, 1), jnp.float32),
+                jax.ShapeDtypeStruct((2, rows + EXTRA, size), jnp.bfloat16),
+            ),
+            in_specs=[pl.BlockSpec(memory_space=pltpu.SMEM)]
+            + in_vmem(7)
+            + [pl.BlockSpec(memory_space=pl.ANY)],
+            out_specs=tuple(in_vmem(3)),
+            compiler_params=pltpu.CompilerParams(vmem_limit_bytes=16 * MIB),
+            cost_estimate=pl.CostEstimate(flops=0, bytes_accessed=0, transcendentals=0),
+        )(places, query_down, keys_down, one_down, query_up, keys_up, one_up, two_up, up)
+        partner = by_row(theirs)
+        return pl.pallas_call(
+            merge_kernel,
+            out_shape=jax.ShapeDtypeStruct((rows, local_heads * size), jnp.bfloat16),
+            in_specs=[pl.BlockSpec(memory_space=pltpu.SMEM)] + in_vmem(9),
             out_specs=in_vmem(1)[0],
             compiler_params=pltpu.CompilerParams(vmem_limit_bytes=16 * MIB),
-        )(tok.reshape(1), guest_one, guest_two, two_up_a, one_up_a, one_up_b, keys_b)
-        from_one = along_tok(guests[0], [(1, 2), (2, 3)])
-        from_two = along_tok(guests[1], [(1, 3)])
-        output, logs = pl.pallas_call(
-            lambda *refs: own_kernel(scale, *refs),
-            out_shape=(
-                jax.ShapeDtypeStruct((2, block, size), jnp.float32),
-                jax.ShapeDtypeStruct((2, block, 1), jnp.float32),
-            ),
-            in_specs=in_vmem(7) + [pl.BlockSpec(memory_space=pl.ANY)],
-            out_specs=tuple(in_vmem(2)),
-            compiler_params=pltpu.CompilerParams(vmem_limit_bytes=16 * MIB),
-            cost_estimate=pl.CostEstimate(flops=0, bytes_accessed=0, transcendentals=0),
-        )(query_a, keys_a, one_up_a, two_up_a, query_b, keys_b, one_up_b, guests)
-        half_shape = jax.ShapeDtypeStruct((rows, 2 * size), jnp.bfloat16)
-        mine, theirs = pl.pallas_call(
-            merge_kernel,
-            out_shape=(half_shape, half_shape),
-            in_specs=[pl.BlockSpec(memory_space=pltpu.SMEM)] + in_vmem(4),
-            out_specs=tuple(in_vmem(2)),
-            compiler_params=pltpu.CompilerParams(vmem_limit_bytes=16 * MIB),
-        )(jnp.stack([tok, row]), output, logs, from_one, from_two)
-    else:
-        sums = jnp.stack([summed(head, 0, taller) for head in range(pair)]).astype(jnp.bfloat16)
-        everything = lax.all_gather(sums[:, : 2 * block], "tok", axis=0, tiled=False)
-        everything = everything.transpose(1, 0, 2, 3)
-        all_codes = lax.all_gather(codes, "tok", axis=0, tiled=True)
-        starts = jnp.sum((all_codes[None, :] < codes[:, None]).astype(jnp.int32), axis=1)
-        together = attend_gathered(
-            sums[:, break_at : break_at + block],
-            everything[:, :, :block].reshape(pair, toks * block, size),
-            everything[:, :, block:].reshape(pair, toks * block, size),
-            places, starts, scale,
-        )
-        mine = jnp.where(row == 0, together[:rows], together[rows:])
-        theirs = jnp.where(row == 0, together[rows:], together[:rows])
+        )(
+            places, mine, logs, partner, two_same, two_cross, three_same, three_cross, up_same,
+            up_cross,
+        )
+
+    sums = jnp.stack([summed(head, 0, taller) for head in range(pair)]).astype(jnp.bfloat16)
+    everything = lax.all_gather(sums[:, : 2 * block], "tok", axis=0, tiled=False)
+    everything = everything.transpose(1, 0, 2, 3)
+    all_codes = lax.all_gather(codes, "tok", axis=0, tiled=True)
+    starts = jnp.sum((all_codes[None, :] < codes[:, None]).astype(jnp.int32), axis=1)
+    together = attend_gathered(
+        sums[:, break_at : break_at + block],
+        everything[:, :, :block].reshape(pair, toks * block, size),
+        everything[:, :, block:].reshape(pair, toks * block, size),
+        places, starts, scale,
+    )
+    mine = jnp.where(row == 0, together[:rows], together[rows:])
+    theirs = jnp.where(row == 0, together[rows:], together[:rows])
 
     theirs = by_row(theirs)
     return jnp.concatenate(

time: 66.9 us -> 66.5 us (level)
  starting transfers between devices: 22.2 us -> 29.2 us
  waiting for transfers between devices: 17.7 us -> 11.7 us
  other arithmetic: 7.77 us -> 5.77 us
  Pallas kernels: 10.3 us -> 11.3 us
    ppermute x7 -> x9, waiting for transfers between devices: 9.44 us -> 4.34 us  [along_tok(): return lax.ppermute(value, 'tok', pairs)]
    ppermute x4, waiting for transfers between devices: 7.42 us -> 3.09 us  [by_row(): return lax.ppermute(value, 'row', [(0, 1), (1, 0)])]
    ppermute x7 -> x9, starting transfers between devices: 11.7 us -> 15.8 us  [along_tok(): return lax.ppermute(value, 'tok', pairs)]
    ppermute x0 -> x3, waiting for transfers between devices: none -> 3.42 us  [returned(): lax.ppermute(value[1], ('tok', 'row'), across)]
    ppermute x0 -> x3, starting transfers between devices: none -> 3.25 us  [returned(): lax.ppermute(value[1], ('tok', 'row'), across)]
    convert_element_type x2 -> x3, other arithmetic: 1.95 us -> 0.15 us  [the longest x1 0.1 us: per_device(): keys_up = summed(1, 0, break_at).astype(jnp.bfloat16)]
    convert_element_type x2, other arithmetic: 0.08 us -> 1.54 us  [per_device(): away, normed = lax.optimization_barrier((away.astype(jnp.float16), normed))]
    select_n x2 -> x1, other arithmetic: 1.01 us -> 0.04 us  [per_device(): jnp.where(tok < toks, arrived[1].astype(jnp.float32), jnp.broadcast_to(fr...]
  transfers between devices with their start and end apart: 17 -> 22, of which waited for: 11 -> 10; matrix products, arithmetic and copies ran while one was open for 17% -> 14% of each run, Pallas kernels for 8% -> 11%
where the time goes in v3:
time: 66.5 us; the launch traced here: 66 us
  starting transfers between devices  29.2 us (44%)
  waiting for transfers between devices  11.7 us (18%)
  Pallas kernels  11.3 us (17%)
  local copies, waits for them, and re-layouts  7.63 us (11%)
  other arithmetic  5.77 us (9%)
    ppermute x9, starting transfers between devices, along_tok(): return lax.ppermute(value, 'tok', pairs)  15.8 us
    unnamed x11, local copies, waits for them, and re-layouts  7.35 us
    ppermute x4, starting transfers between devices, by_row(): return lax.ppermute(value, 'row', [(0, 1), (1, 0)])  4.57 us
    ppermute x9, waiting for transfers between devices, along_tok(): return lax.ppermute(value, 'tok', pairs)  4.34 us
    ppermute x3, waiting for transfers between devices, returned(): lax.ppermute(value[1], ('tok', 'row'), across)  3.42 us
    ppermute x1, starting transfers between devices, per_device(): lax.ppermute(activations, ('row', 'col'), [(r * 4 + c, c // 2 * 4 + 2 * (...  3.31 us
    ppermute x3, starting transfers between devices, returned(): lax.ppermute(value[1], ('tok', 'row'), across)  3.25 us
    ppermute x4, waiting for transfers between devices, by_row(): return lax.ppermute(value, 'row', [(0, 1), (1, 0)])  3.09 us
  transfers between devices with their start and end apart: 22, of which 10 were waited for; matrix products, arithmetic and copies ran while one was open for 14% of the time, Pallas kernels for 11%

profile of v3, /device:TPU:24, one launch (start us, length us, event | category | flops | bytes accessed | tf_op | source)
XLA Modules:
  0.0 66.0 jit_solution(122563182511619563)
XLA Ops:
  0.0 1.8 %collective-permute-start = (bf16[176,1024]{1,0:T(8,128)(2,1)}, bf16[176,1024]{1,0:T(8,128)(2,1)S(1)}, u32[]{:S(2)}, u32[]{:S(2)}) collective-permute-start(bf16[176,1024]{1,0:T(8,128)(2,1)} %param.4), channel_id=1, source_target_pairs={{0,0},{1,1},{2,4},{3,5},{4,2},{5,3},{6,6},{7,7},{8,8},{9,9},{10,12... | collective-permute-start | bytes 1081352 | tf_op jit(solution)/shard_map/ppermute | solution.py:316
  1.8 3.3 %collective-permute-start.1 = (bf16[176,1024]{1,0:T(8,128)(2,1)}, bf16[176,1024]{1,0:T(8,128)(2,1)S(1)}, u32[]{:S(2)}, u32[]{:S(2)}) collective-permute-start(bf16[176,1024]{1,0:T(8,128)(2,1)} %param.4), channel_id=1, source_target_pairs={{0,2},{1,3},{2,6},{3,7},{4,0},{5,1},{6,4},{7,5},{8,10},{9,11},{10,... | collective-permute-start | bytes 1081352 | tf_op jit(solution)/shard_map/ppermute | solution.py:321
  5.1 1.2 %multiply_reduce_fusion = f32[176]{0:T(256)S(1)} fusion(bf16[176,1024]{1,0:T(8,128)(2,1)} %param.4), kind=kLoop, calls=%fused_computation | loop fusion | flops 540496 | bytes 361152 | tf_op jit(solution)/shard_map/reduce_sum | solution.py:327
  6.2 0.7 %convert_element_type.54 = f32[1024]{0:T(1024)S(1)} convert(bf16[1024]{0:T(1024)(128)(2,1)} %param.5) | non-fusion elementwise | flops 1024 | bytes 6144 | tf_op jit(solution)/shard_map/convert_element_type | solution.py:328
  7.0 0.7 %convert_add_fusion = f32[176]{0:T(256)S(1)} fusion(s32[176]{0:T(256)} %param.7), kind=kLoop, calls=%fused_computation.36 | loop fusion | flops 352 | bytes 1408 | tf_op jit(solution)/shard_map/add | solution.py:340
  7.7 0.7 %fusion.6 = (f32[352,64]{1,0:T(8,128)S(1)}, f32[352,64]{1,0:T(8,128)S(1)}, f32[352,64]{1,0:T(8,128)S(1)}) fusion(f32[64]{0:T(128)S(1)} %negate_power_fusion, f32[352]{0:T(512)S(1)} %add_convert_fusion), kind=kLoop, calls=%fused_computation.18 | loop fusion | flops 45056 | bytes 272000 | tf_op jit(solution)/shard_map/neg | solution.py:24
  8.4 0.2 pad_maximum_fusion
  8.9 4.0 %copy.6 = bf16[256,8,4,384]{3,1,2,0:T(8,128)(2,1)S(1)} copy(bf16[256,8,4,384]{3,2,1,0:T(4,128)(2,1)} %bitcast.56) | data formatting | bytes 12582912
  12.9 0.7 %collective-permute-done.3 = f32[2224]{0:T(1024)S(1)} collective-permute-done((f32[2224]{0:T(1024)S(1)}, f32[2224]{0:T(1024)S(1)}, u32[]{:S(2)}, u32[]{:S(2)}) %collective-permute-start.3) | collective-permute-done | bytes 8928 | tf_op jit(solution)/shard_map/ppermute | solution.py:307
  13.8 1.8 %collective-permute-start.6 = (f32[352]{0:T(512)S(1)}, f32[352]{0:T(512)S(1)}, u32[]{:S(2)}, u32[]{:S(2)}) collective-permute-start(f32[352]{0:T(512)S(1)} %pad_maximum_fusion.3), channel_id=1, source_target_pairs={{0,4},{4,0},{1,5},{5,1},{2,6},{6,2},{3,7},{7,3},{8,12},{12,8},{9,1... | collective-permute-start | bytes 4232 | tf_op jit(solution)/shard_map/ppermute | solution.py:310
  15.6 0.5 collective-permute-start.5
  16.1 1.3 %collective-permute-done.6 = f32[352]{0:T(512)S(1)} collective-permute-done((f32[352]{0:T(512)S(1)}, f32[352]{0:T(512)S(1)}, u32[]{:S(2)}, u32[]{:S(2)}) %collective-permute-start.6) | collective-permute-done | bytes 1440 | tf_op jit(solution)/shard_map/ppermute | solution.py:310
  17.5 0.1 reshape.82.squares_ref
  17.6 0.1 collective-permute-done.5.b_far
  17.7 2.1 %shard_map.46 = (f32[1,1088,128]{2,1,0:T(8,128)S(1)}, bf16[2,352,1024]{2,1,0:T(8,128)(2,1)S(1)}) custom-call(s32[3]{0:T(128)S(1)} %pad_add_fusion.1.place_ref, bf16[176,1024]{1,0:T(8,128)(2,1)S(1)} %collective-permute-done.a_near, bf16[176,1024]{1,0:T(8,128)(2,1)S(1)} %collective-permute-done.1.a_far, bf16[176,1024]{1,0:T(8,128)(2,1)S(1)} %collective-permute-done.4.b_near, ...), custom_call_target="tpu_custom_call" | custom-call | tf_op jit(solution)/shard_map/pallas_call | solution.py:371
  19.9 0.8 %convert_element_type.58 = f16[1,1088,128]{2,1,0:T(8,128)(2,1)} convert(f32[1,1088,128]{2,1,0:T(8,128)S(1)} %get-tuple-element.26) | non-fusion elementwise | flops 139264 | bytes 835584 | tf_op jit(solution)/shard_map/convert_element_type | solution.py:382
  20.6 1.7 %collective-permute-start.7 = (f16[1088,128]{1,0:T(8,128)(2,1)}, f16[1088,128]{1,0:T(8,128)(2,1)S(1)}, u32[]{:S(2)}, u32[]{:S(2)}) collective-permute-start(f16[1088,128]{1,0:T(8,128)(2,1)} %bitcast.12), channel_id=1, source_target_pairs={{0,4},{4,0},{1,5},{5,1},{2,6},{6,2},{3,7},{7,3},{8,12},{12,8},{9,1... | collective-permute-start | bytes 835592 | tf_op jit(solution)/shard_map/ppermute | solution.py:310
  22.4 2.8 %copy-done.1 = bf16[256,8,4,384]{3,1,2,0:T(8,128)(2,1)S(1)} copy-done((bf16[256,8,4,384]{3,1,2,0:T(8,128)(2,1)S(1)}, bf16[256,8,4,384]{3,1,2,0:T(8,128)(2,1)}, u32[]{:S(2)}) %copy-start.1) | copy-done | bytes 6291480
  25.2 1.2 %shard_map.47 = f32[1,1088,128]{2,1,0:T(8,128)S(1)} custom-call(s32[1]{0:T(128)} %bitcast.3.place_ref, bf16[2,352,1024]{2,1,0:T(8,128)(2,1)S(1)} %get-tuple-element.29.normed_ref, f32[16,128]{1,0:T(8,128)S(1)} %broadcast_in_dim.15.docs_ref, bf16[2048,1536]{1,0:T(8,128)(2,1)S(1)} %bitcast.54, f32[352,128]{1,0:T(8,128)S(1)} %get-tuple-element.54.cos_ref, ...), custom_call_target="tpu_custom_call" | custom-call | tf_op jit(solution)/shard_map/pallas_call | solution.py:378
  26.4 0.8 %convert_element_type.59 = f16[1,1088,128]{2,1,0:T(8,128)(2,1)} convert(f32[1,1088,128]{2,1,0:T(8,128)S(1)} %shard_map.47) | non-fusion elementwise | flops 139264 | bytes 835584 | tf_op jit(solution)/shard_map/convert_element_type | solution.py:382
  27.1 0.3 collective-permute-start.9
  27.5 0.6 copy-done.2
  28.1 2.0 %shard_map.48 = f32[2,1088,128]{2,1,0:T(8,128)S(1)} custom-call(s32[1]{0:T(128)} %bitcast.2.place_ref, bf16[2,352,1024]{2,1,0:T(8,128)(2,1)S(1)} %get-tuple-element.29.normed_ref, f32[16,128]{1,0:T(8,128)S(1)} %fusion.7.docs_ref, bf16[2048,1536]{1,0:T(8,128)(2,1)S(1)} %bitcast.55, f32[352,128]{1,0:T(8,128)S(1)} %get-tuple-element.54.cos_ref, ...), custom_call_target="tpu_custom_call" | custom-call | tf_op jit(solution)/shard_map/pallas_call | solution.py:384
  30.0 0.3 collective-permute-done.7
  30.4 0.7 %collective-permute-start.10 = (bf16[368,128]{1,0:T(8,128)(2,1)S(1)}, bf16[368,128]{1,0:T(8,128)(2,1)S(1)}, u32[]{:S(2)}, u32[]{:S(2)}) collective-permute-start(bf16[368,128]{1,0:T(8,128)(2,1)S(1)} %fusion.5.refs_1_), channel_id=1, source_target_pairs={{16,8},{17,9},{18,10},{19,11},{20,12},{21,13},{22,14},{23,15}} | collective-permute-start | bytes 282632 | tf_op jit(solution)/shard_map/ppermute | solution.py:390
  31.1 2.9 %collective-permute-start.15 = (bf16[368,128]{1,0:T(8,128)(2,1)S(1)}, bf16[368,128]{1,0:T(8,128)(2,1)S(1)}, u32[]{:S(2)}, u32[]{:S(2)}) collective-permute-start(bf16[368,128]{1,0:T(8,128)(2,1)S(1)} %fusion.5.refs_1_), channel_id=1, source_target_pairs={{24,8},{25,9},{26,10},{27,11},{28,12},{29,13},{30,14},{31,15}} | collective-permute-start | bytes 282632 | tf_op jit(solution)/shard_map/ppermute | solution.py:390
  34.0 1.5 %collective-permute-done.9 = f16[1088,128]{1,0:T(8,128)(2,1)S(1)} collective-permute-done((f16[1088,128]{1,0:T(8,128)(2,1)}, f16[1088,128]{1,0:T(8,128)(2,1)S(1)}, u32[]{:S(2)}, u32[]{:S(2)}) %collective-permute-start.9) | collective-permute-done | bytes 278560 | tf_op jit(solution)/shard_map/ppermute | solution.py:310
  35.6 0.1 fusion
  35.7 1.3 %collective-permute-start.8 = (bf16[720,128]{1,0:T(8,128)(2,1)S(1)}, bf16[720,128]{1,0:T(8,128)(2,1)S(1)}, u32[]{:S(2)}, u32[]{:S(2)}) collective-permute-start(bf16[720,128]{1,0:T(8,128)(2,1)S(1)} %get-tuple-element.36.refs_2_.refs_4_), channel_id=1, source_target_pairs={{0,8},{16,24},{1,9},{17,25},{2,10},{18,26},{3,11},{19,27},{4,12},{... | collective-permute-start | bytes 552968 | tf_op jit(solution)/shard_map/ppermute | solution.py:390
  37.0 1.3 %collective-permute-start.11 = (bf16[720,128]{1,0:T(8,128)(2,1)S(1)}, bf16[720,128]{1,0:T(8,128)(2,1)S(1)}, u32[]{:S(2)}, u32[]{:S(2)}) collective-permute-start(bf16[720,128]{1,0:T(8,128)(2,1)S(1)} %get-tuple-element.35.refs_5_), channel_id=1, source_target_pairs={{0,8},{8,16},{16,24},{1,9},{9,17},{17,25},{2,10},{10,18},{18,26},{... | collective-permute-start | bytes 552968 | tf_op jit(solution)/shard_map/ppermute | solution.py:390
  38.3 0.7 %collective-permute-start.12 = (bf16[720,128]{1,0:T(8,128)(2,1)S(1)}, bf16[720,128]{1,0:T(8,128)(2,1)S(1)}, u32[]{:S(2)}, u32[]{:S(2)}) collective-permute-start(bf16[720,128]{1,0:T(8,128)(2,1)S(1)} %get-tuple-element.35.refs_5_), channel_id=1, source_target_pairs={{0,16},{1,17},{2,18},{3,19},{4,20},{5,21},{6,22},{7,23}} | collective-permute-start | bytes 552968 | tf_op jit(solution)/shard_map/ppermute | solution.py:390
  39.0 5.8 %collective-permute-start.13 = (bf16[368,128]{1,0:T(8,128)(2,1)S(1)}, bf16[368,128]{1,0:T(8,128)(2,1)S(1)}, u32[]{:S(2)}, u32[]{:S(2)}) collective-permute-start(bf16[368,128]{1,0:T(8,128)(2,1)S(1)} %fusion.3.refs_4_), channel_id=1, source_target_pairs={{24,16},{25,17},{26,18},{27,19},{28,20},{29,21},{30,22},{31,23}} | collective-permute-start | bytes 282632 | tf_op jit(solution)/shard_map/ppermute | solution.py:390
  44.8 0.6 shard_map.51
  45.4 0.7 %collective-permute-start.16 = (bf16[192,128]{1,0:T(8,128)(2,1)S(1)}, bf16[192,128]{1,0:T(8,128)(2,1)S(1)}, u32[]{:S(2)}, u32[]{:S(2)}) collective-permute-start(bf16[192,128]{1,0:T(8,128)(2,1)S(1)} %get-tuple-element.40), channel_id=1, source_target_pairs={{8,16},{9,17},{10,18},{11,19},{12,20},{13,21},{14,22},{15,23}} | collective-permute-start | bytes 147464 | tf_op jit(solution)/shard_map/ppermute | solution.py:390
  46.1 0.7 %collective-permute-start.17 = (bf16[192,128]{1,0:T(8,128)(2,1)S(1)}, bf16[192,128]{1,0:T(8,128)(2,1)S(1)}, u32[]{:S(2)}, u32[]{:S(2)}) collective-permute-start(bf16[192,128]{1,0:T(8,128)(2,1)S(1)} %get-tuple-element.39), channel_id=1, source_target_pairs={{8,20},{12,16},{9,21},{13,17},{10,22},{14,18},{11,23},{15,19}} | collective-permute-start | bytes 147464 | tf_op jit(solution)/shard_map/ppermute | solution.py:400
  46.7 0.2 collective-permute-done.13.refs_1_
  46.9 0.7 %shard_map.49.refs_8_ = bf16[1,2,192,128]{3,2,1,0:T(8,128)(2,1)S(1)} custom-call(s32[2]{0:T(128)S(1)} %pad_add_fusion.refs_0_.place_ref, bf16[368,128]{1,0:T(8,128)(2,1)S(1)} %collective-permute-done.13.refs_1_, bf16[720,128]{1,0:T(8,128)(2,1)S(1)} %collective-permute-done.12.refs_2_.refs_7_, bf16[720,128]{1,0:T(8,128)(2,1)S(1)} %collective-permute-done.11.refs_3_.refs_6_), custom_call_target="tpu_custom_call" | custom-call | tf_op jit(solution)/shard_map/pallas_call | solution.py:404
  47.7 2.7 %shard_map.50 = (f32[2,176,128]{2,1,0:T(8,128)S(1)}, f32[2,176,1]{2,1,0:T(8,128)S(1)}, bf16[2,192,128]{2,1,0:T(8,128)(2,1)S(1)}) custom-call(s32[2]{0:T(128)S(1)} %pad_add_fusion.refs_0_.place_ref, bf16[368,128]{1,0:T(8,128)(2,1)S(1)} %fusion.5.refs_1_, bf16[720,128]{1,0:T(8,128)(2,1)S(1)} %get-tuple-element.36.refs_2_.refs_4_, ...), custom_call_target="tpu_custom_call" | custom-call | tf_op jit(solution)/shard_map/pallas_call | solution.py:435
  50.4 0.8 %collective-permute-start.14 = (bf16[2,192,128]{2,1,0:T(8,128)(2,1)S(1)}, bf16[2,192,128]{2,1,0:T(8,128)(2,1)S(1)}, u32[]{:S(2)}, u32[]{:S(2)}) collective-permute-start(bf16[2,192,128]{2,1,0:T(8,128)(2,1)S(1)} %get-tuple-element.34), channel_id=1, source_target_pairs={{0,4},{4,0},{1,5},{5,1},{2,6},{6,2},{3,7},{7,3},{8,12},{12,8},{9,1... | collective-permute-start | bytes 294920 | tf_op jit(solution)/shard_map/ppermute | solution.py:310
  51.2 1.3 %collective-permute-start.18 = (bf16[192,128]{1,0:T(8,128)(2,1)S(1)}, bf16[192,128]{1,0:T(8,128)(2,1)S(1)}, u32[]{:S(2)}, u32[]{:S(2)}) collective-permute-start(bf16[192,128]{1,0:T(8,128)(2,1)S(1)} %get-tuple-element.38), channel_id=1, source_target_pairs={{8,24},{9,25},{10,26},{11,27},{12,28},{13,29},{14,30},{15,31}} | collective-permute-start | bytes 147464 | tf_op jit(solution)/shard_map/ppermute | solution.py:390
  52.5 1.3 %collective-permute-start.19 = (bf16[192,128]{1,0:T(8,128)(2,1)S(1)}, bf16[192,128]{1,0:T(8,128)(2,1)S(1)}, u32[]{:S(2)}, u32[]{:S(2)}) collective-permute-start(bf16[192,128]{1,0:T(8,128)(2,1)S(1)} %get-tuple-element.37), channel_id=1, source_target_pairs={{8,28},{12,24},{9,29},{13,25},{10,30},{14,26},{11,31},{15,27}} | collective-permute-start | bytes 147464 | tf_op jit(solution)/shard_map/ppermute | solution.py:400
  53.8 1.3 %collective-permute-start.20 = (bf16[192,128]{1,0:T(8,128)(2,1)S(1)}, bf16[192,128]{1,0:T(8,128)(2,1)S(1)}, u32[]{:S(2)}, u32[]{:S(2)}) collective-permute-start(bf16[192,128]{1,0:T(8,128)(2,1)S(1)} %get-tuple-element.42), channel_id=1, source_target_pairs={{16,24},{17,25},{18,26},{19,27},{20,28},{21,29},{22,30},{23,31}} | collective-permute-start | bytes 147464 | tf_op jit(solution)/shard_map/ppermute | solution.py:390
  55.1 1.3 %collective-permute-start.21 = (bf16[192,128]{1,0:T(8,128)(2,1)S(1)}, bf16[192,128]{1,0:T(8,128)(2,1)S(1)}, u32[]{:S(2)}, u32[]{:S(2)}) collective-permute-start(bf16[192,128]{1,0:T(8,128)(2,1)S(1)} %get-tuple-element.41), channel_id=1, source_target_pairs={{16,28},{20,24},{17,29},{21,25},{18,30},{22,26},{19,31},{23,27}} | collective-permute-start | bytes 147464 | tf_op jit(solution)/shard_map/ppermute | solution.py:400
  56.4 2.8 %collective-permute-done.18.three_same = bf16[192,128]{1,0:T(8,128)(2,1)S(1)} collective-permute-done((bf16[192,128]{1,0:T(8,128)(2,1)S(1)}, bf16[192,128]{1,0:T(8,128)(2,1)S(1)}, u32[]{:S(2)}, u32[]{:S(2)}) %collective-permute-start.18) | collective-permute-done | bytes 49184 | tf_op jit(solution)/shard_map/ppermute | solution.py:390
  59.1 1.7 %collective-permute-done.19.three_cross = bf16[192,128]{1,0:T(8,128)(2,1)S(1)} collective-permute-done((bf16[192,128]{1,0:T(8,128)(2,1)S(1)}, bf16[192,128]{1,0:T(8,128)(2,1)S(1)}, u32[]{:S(2)}, u32[]{:S(2)}) %collective-permute-start.19) | collective-permute-done | bytes 49184 | tf_op jit(solution)/shard_map/ppermute | solution.py:400
  60.8 1.3 %collective-permute-done.20.up_same = bf16[192,128]{1,0:T(8,128)(2,1)S(1)} collective-permute-done((bf16[192,128]{1,0:T(8,128)(2,1)S(1)}, bf16[192,128]{1,0:T(8,128)(2,1)S(1)}, u32[]{:S(2)}, u32[]{:S(2)}) %collective-permute-start.20) | collective-permute-done | bytes 49184 | tf_op jit(solution)/shard_map/ppermute | solution.py:390
  62.2 1.7 %collective-permute-done.21.up_cross = bf16[192,128]{1,0:T(8,128)(2,1)S(1)} collective-permute-done((bf16[192,128]{1,0:T(8,128)(2,1)S(1)}, bf16[192,128]{1,0:T(8,128)(2,1)S(1)}, u32[]{:S(2)}, u32[]{:S(2)}) %collective-permute-start.21) | collective-permute-done | bytes 49184 | tf_op jit(solution)/shard_map/ppermute | solution.py:400
  63.9 2.0 %shard_map.52 = bf16[176,512]{1,0:T(8,128)(2,1)} custom-call(s32[2]{0:T(128)S(1)} %pad_add_fusion.refs_0_.place_ref, f32[2,176,128]{2,1,0:T(8,128)S(1)} %get-tuple-element.32.mine_ref, f32[2,176,1]{2,1,0:T(8,128)S(1)} %get-tuple-element.33.logs_ref, bf16[2,192,128]{2,1,0:T(8,128)(2,1)S(1)} %collective-permute-done.14.partner_ref, ...), custom_call_target="tpu_custom_call" | custom-call | tf_op jit(solution)/shard_map/pallas_call | solution.py:450
  (45 shorter events, 1.0 us)
Async XLA Ops:
  0.0 8.6 %copy-start.3 = (bf16[1024]{0:T(1024)(128)(2,1)S(1)}, bf16[1024]{0:T(1024)(128)(2,1)}, u32[]{:S(2)}) copy-start(bf16[1024]{0:T(1024)(128)(2,1)} %param.5) | copy-start | bytes 6148
  0.0 13.6 %collective-permute-start = (bf16[176,1024]{1,0:T(8,128)(2,1)}, bf16[176,1024]{1,0:T(8,128)(2,1)S(1)}, u32[]{:S(2)}, u32[]{:S(2)}) collective-permute-start(bf16[176,1024]{1,0:T(8,128)(2,1)} %param.4), channel_id=1, source_target_pairs={{0,0},{1,1},{2,4},{3,5},{4,2},{5,3},{6,6},{7,7},{8,8},{9,9},{10,12... | collective-permute-start | bytes 1081352 | tf_op jit(solution)/shard_map/ppermute | solution.py:316
  1.8 11.8 %collective-permute-start.1 = (bf16[176,1024]{1,0:T(8,128)(2,1)}, bf16[176,1024]{1,0:T(8,128)(2,1)S(1)}, u32[]{:S(2)}, u32[]{:S(2)}) collective-permute-start(bf16[176,1024]{1,0:T(8,128)(2,1)} %param.4), channel_id=1, source_target_pairs={{0,2},{1,3},{2,6},{3,7},{4,0},{5,1},{6,4},{7,5},{8,10},{9,11},{10,... | collective-permute-start | bytes 1081352 | tf_op jit(solution)/shard_map/ppermute | solution.py:321
  7.0 1.6 %collective-permute-start.2 = (f32[1200]{0:T(1024)S(1)}, f32[1200]{0:T(1024)S(1)}, u32[]{:S(2)}, u32[]{:S(2)}) collective-permute-start(f32[1200]{0:T(1024)S(1)} %pad_maximum_fusion.2), channel_id=1, source_target_pairs={{0,1},{1,0},{2,3},{3,2},{4,5},{5,4},{6,7},{7,6},{8,9},{9,8},{10,11... | collective-permute-start | bytes 14408 | tf_op jit(solution)/shard_map/ppermute | solution.py:307
  8.8 4.8 %collective-permute-start.3 = (f32[2224]{0:T(1024)S(1)}, f32[2224]{0:T(1024)S(1)}, u32[]{:S(2)}, u32[]{:S(2)}) collective-permute-start(f32[2224]{0:T(1024)S(1)} %concatenate.37), channel_id=1, source_target_pairs={{0,2},{1,3},{2,0},{3,1},{4,6},{5,7},{6,4},{7,5},{8,10},{9,11},{10,... | collective-permute-start | bytes 26696 | tf_op jit(solution)/shard_map/ppermute | solution.py:307
  8.9 8.5 %copy-start.4 = (s32[176]{0:T(256)S(1)}, s32[176]{0:T(256)}, u32[]{:S(2)}) copy-start(s32[176]{0:T(256)} %param.7) | copy-start | bytes 2116
  12.9 7.0 %copy-start = (bf16[256,8,4,384]{3,1,2,0:T(8,128)(2,1)}, bf16[256,8,4,384]{3,1,2,0:T(8,128)(2,1)S(1)}, u32[]{:S(2)}) copy-start(bf16[256,8,4,384]{3,1,2,0:T(8,128)(2,1)S(1)} %copy.6) | copy-start | bytes 18874372
  13.8 3.6 %collective-permute-start.6 = (f32[352]{0:T(512)S(1)}, f32[352]{0:T(512)S(1)}, u32[]{:S(2)}, u32[]{:S(2)}) collective-permute-start(f32[352]{0:T(512)S(1)} %pad_maximum_fusion.3), channel_id=1, source_target_pairs={{0,4},{4,0},{1,5},{5,1},{2,6},{6,2},{3,7},{7,3},{8,12},{12,8},{9,1... | collective-permute-start | bytes 4232 | tf_op jit(solution)/shard_map/ppermute | solution.py:310
  15.6 2.1 %collective-permute-start.4 = (bf16[176,1024]{1,0:T(8,128)(2,1)S(1)}, bf16[176,1024]{1,0:T(8,128)(2,1)S(1)}, u32[]{:S(2)}, u32[]{:S(2)}) collective-permute-start(bf16[176,1024]{1,0:T(8,128)(2,1)S(1)} %collective-permute-done.a_near), channel_id=1, source_target_pairs={{0,1},{1,0},{2,3},{3,2},{4,5},{5,4},{6,7},{7,6},{8,9},{9,8},{10,11... | collective-permute-start | bytes 1081352 | tf_op jit(solution)/shard_map/ppermute | solution.py:307
  15.6 2.2 %collective-permute-start.5 = (bf16[176,1024]{1,0:T(8,128)(2,1)S(1)}, bf16[176,1024]{1,0:T(8,128)(2,1)S(1)}, u32[]{:S(2)}, u32[]{:S(2)}) collective-permute-start(bf16[176,1024]{1,0:T(8,128)(2,1)S(1)} %collective-permute-done.1.a_far), channel_id=1, source_target_pairs={{0,1},{1,0},{2,3},{3,2},{4,5},{5,4},{6,7},{7,6},{8,9},{9,8},{10,11... | collective-permute-start | bytes 1081352 | tf_op jit(solution)/shard_map/ppermute | solution.py:307
  20.6 9.7 %collective-permute-start.7 = (f16[1088,128]{1,0:T(8,128)(2,1)}, f16[1088,128]{1,0:T(8,128)(2,1)S(1)}, u32[]{:S(2)}, u32[]{:S(2)}) collective-permute-start(f16[1088,128]{1,0:T(8,128)(2,1)} %bitcast.12), channel_id=1, source_target_pairs={{0,4},{4,0},{1,5},{5,1},{2,6},{6,2},{3,7},{7,3},{8,12},{12,8},{9,1... | collective-permute-start | bytes 835592 | tf_op jit(solution)/shard_map/ppermute | solution.py:310
  22.4 2.8 %copy-start.1 = (bf16[256,8,4,384]{3,1,2,0:T(8,128)(2,1)S(1)}, bf16[256,8,4,384]{3,1,2,0:T(8,128)(2,1)}, u32[]{:S(2)}) copy-start(bf16[256,8,4,384]{3,1,2,0:T(8,128)(2,1)} %copy-done) | copy-start | bytes 18874372
  25.2 2.9 %copy-start.2 = (bf16[256,8,4,384]{3,1,2,0:T(8,128)(2,1)S(1)}, bf16[256,8,4,384]{3,1,2,0:T(8,128)(2,1)}, u32[]{:S(2)}) copy-start(bf16[256,8,4,384]{3,1,2,0:T(8,128)(2,1)} %copy-done) | copy-start | bytes 18874372
  27.1 8.4 %collective-permute-start.9 = (f16[1088,128]{1,0:T(8,128)(2,1)}, f16[1088,128]{1,0:T(8,128)(2,1)S(1)}, u32[]{:S(2)}, u32[]{:S(2)}) collective-permute-start(f16[1088,128]{1,0:T(8,128)(2,1)} %bitcast.15), channel_id=1, source_target_pairs={{0,4},{4,0},{1,5},{5,1},{2,6},{6,2},{3,7},{7,3},{8,12},{12,8},{9,1... | collective-permute-start | bytes 835592 | tf_op jit(solution)/shard_map/ppermute | solution.py:310
  30.4 3.6 %collective-permute-start.10 = (bf16[368,128]{1,0:T(8,128)(2,1)S(1)}, bf16[368,128]{1,0:T(8,128)(2,1)S(1)}, u32[]{:S(2)}, u32[]{:S(2)}) collective-permute-start(bf16[368,128]{1,0:T(8,128)(2,1)S(1)} %fusion.5.refs_1_), channel_id=1, source_target_pairs={{16,8},{17,9},{18,10},{19,11},{20,12},{21,13},{22,14},{23,15}} | collective-permute-start | bytes 282632 | tf_op jit(solution)/shard_map/ppermute | solution.py:390
  31.1 13.7 %collective-permute-start.15 = (bf16[368,128]{1,0:T(8,128)(2,1)S(1)}, bf16[368,128]{1,0:T(8,128)(2,1)S(1)}, u32[]{:S(2)}, u32[]{:S(2)}) collective-permute-start(bf16[368,128]{1,0:T(8,128)(2,1)S(1)} %fusion.5.refs_1_), channel_id=1, source_target_pairs={{24,8},{25,9},{26,10},{27,11},{28,12},{29,13},{30,14},{31,15}} | collective-permute-start | bytes 282632 | tf_op jit(solution)/shard_map/ppermute | solution.py:390
  35.7 9.1 %collective-permute-start.8 = (bf16[720,128]{1,0:T(8,128)(2,1)S(1)}, bf16[720,128]{1,0:T(8,128)(2,1)S(1)}, u32[]{:S(2)}, u32[]{:S(2)}) collective-permute-start(bf16[720,128]{1,0:T(8,128)(2,1)S(1)} %get-tuple-element.36.refs_2_.refs_4_), channel_id=1, source_target_pairs={{0,8},{16,24},{1,9},{17,25},{2,10},{18,26},{3,11},{19,27},{4,12},{... | collective-permute-start | bytes 552968 | tf_op jit(solution)/shard_map/ppermute | solution.py:390
  37.0 9.9 %collective-permute-start.11 = (bf16[720,128]{1,0:T(8,128)(2,1)S(1)}, bf16[720,128]{1,0:T(8,128)(2,1)S(1)}, u32[]{:S(2)}, u32[]{:S(2)}) collective-permute-start(bf16[720,128]{1,0:T(8,128)(2,1)S(1)} %get-tuple-element.35.refs_5_), channel_id=1, source_target_pairs={{0,8},{8,16},{16,24},{1,9},{9,17},{17,25},{2,10},{10,18},{18,26},{... | collective-permute-start | bytes 552968 | tf_op jit(solution)/shard_map/ppermute | solution.py:390
  38.3 8.7 %collective-permute-start.12 = (bf16[720,128]{1,0:T(8,128)(2,1)S(1)}, bf16[720,128]{1,0:T(8,128)(2,1)S(1)}, u32[]{:S(2)}, u32[]{:S(2)}) collective-permute-start(bf16[720,128]{1,0:T(8,128)(2,1)S(1)} %get-tuple-element.35.refs_5_), channel_id=1, source_target_pairs={{0,16},{1,17},{2,18},{3,19},{4,20},{5,21},{6,22},{7,23}} | collective-permute-start | bytes 552968 | tf_op jit(solution)/shard_map/ppermute | solution.py:390
  39.0 8.0 %collective-permute-start.13 = (bf16[368,128]{1,0:T(8,128)(2,1)S(1)}, bf16[368,128]{1,0:T(8,128)(2,1)S(1)}, u32[]{:S(2)}, u32[]{:S(2)}) collective-permute-start(bf16[368,128]{1,0:T(8,128)(2,1)S(1)} %fusion.3.refs_4_), channel_id=1, source_target_pairs={{24,16},{25,17},{26,18},{27,19},{28,20},{29,21},{30,22},{31,23}} | collective-permute-start | bytes 282632 | tf_op jit(solution)/shard_map/ppermute | solution.py:390
  45.4 8.4 %collective-permute-start.16 = (bf16[192,128]{1,0:T(8,128)(2,1)S(1)}, bf16[192,128]{1,0:T(8,128)(2,1)S(1)}, u32[]{:S(2)}, u32[]{:S(2)}) collective-permute-start(bf16[192,128]{1,0:T(8,128)(2,1)S(1)} %get-tuple-element.40), channel_id=1, source_target_pairs={{8,16},{9,17},{10,18},{11,19},{12,20},{13,21},{14,22},{15,23}} | collective-permute-start | bytes 147464 | tf_op jit(solution)/shard_map/ppermute | solution.py:390
  46.1 9.0 %collective-permute-start.17 = (bf16[192,128]{1,0:T(8,128)(2,1)S(1)}, bf16[192,128]{1,0:T(8,128)(2,1)S(1)}, u32[]{:S(2)}, u32[]{:S(2)}) collective-permute-start(bf16[192,128]{1,0:T(8,128)(2,1)S(1)} %get-tuple-element.39), channel_id=1, source_target_pairs={{8,20},{12,16},{9,21},{13,17},{10,22},{14,18},{11,23},{15,19}} | collective-permute-start | bytes 147464 | tf_op jit(solution)/shard_map/ppermute | solution.py:400
  50.4 13.5 %collective-permute-start.14 = (bf16[2,192,128]{2,1,0:T(8,128)(2,1)S(1)}, bf16[2,192,128]{2,1,0:T(8,128)(2,1)S(1)}, u32[]{:S(2)}, u32[]{:S(2)}) collective-permute-start(bf16[2,192,128]{2,1,0:T(8,128)(2,1)S(1)} %get-tuple-element.34), channel_id=1, source_target_pairs={{0,4},{4,0},{1,5},{5,1},{2,6},{6,2},{3,7},{7,3},{8,12},{12,8},{9,1... | collective-permute-start | bytes 294920 | tf_op jit(solution)/shard_map/ppermute | solution.py:310
  51.2 8.0 %collective-permute-start.18 = (bf16[192,128]{1,0:T(8,128)(2,1)S(1)}, bf16[192,128]{1,0:T(8,128)(2,1)S(1)}, u32[]{:S(2)}, u32[]{:S(2)}) collective-permute-start(bf16[192,128]{1,0:T(8,128)(2,1)S(1)} %get-tuple-element.38), channel_id=1, source_target_pairs={{8,24},{9,25},{10,26},{11,27},{12,28},{13,29},{14,30},{15,31}} | collective-permute-start | bytes 147464 | tf_op jit(solution)/shard_map/ppermute | solution.py:390
  52.5 8.4 %collective-permute-start.19 = (bf16[192,128]{1,0:T(8,128)(2,1)S(1)}, bf16[192,128]{1,0:T(8,128)(2,1)S(1)}, u32[]{:S(2)}, u32[]{:S(2)}) collective-permute-start(bf16[192,128]{1,0:T(8,128)(2,1)S(1)} %get-tuple-element.37), channel_id=1, source_target_pairs={{8,28},{12,24},{9,29},{13,25},{10,30},{14,26},{11,31},{15,27}} | collective-permute-start | bytes 147464 | tf_op jit(solution)/shard_map/ppermute | solution.py:400
  53.8 8.4 %collective-permute-start.20 = (bf16[192,128]{1,0:T(8,128)(2,1)S(1)}, bf16[192,128]{1,0:T(8,128)(2,1)S(1)}, u32[]{:S(2)}, u32[]{:S(2)}) collective-permute-start(bf16[192,128]{1,0:T(8,128)(2,1)S(1)} %get-tuple-element.42), channel_id=1, source_target_pairs={{16,24},{17,25},{18,26},{19,27},{20,28},{21,29},{22,30},{23,31}} | collective-permute-start | bytes 147464 | tf_op jit(solution)/shard_map/ppermute | solution.py:390
  55.1 8.8 %collective-permute-start.21 = (bf16[192,128]{1,0:T(8,128)(2,1)S(1)}, bf16[192,128]{1,0:T(8,128)(2,1)S(1)}, u32[]{:S(2)}, u32[]{:S(2)}) collective-permute-start(bf16[192,128]{1,0:T(8,128)(2,1)S(1)} %get-tuple-element.41), channel_id=1, source_target_pairs={{16,28},{20,24},{17,29},{21,25},{18,30},{22,26},{19,31},{23,27}} | collective-permute-start | bytes 147464 | tf_op jit(solution)/shard_map/ppermute | solution.py:400

commit v4 on v3

--- a/solution.py
+++ b/solution.py
@@ -39,8 +39,8 @@
     ]
 
 
-def project_heads(normed_ref, copies, weight_buffer, cos_ref, sin_ref, doc_rows, out_ref):
-    heads, size = out_ref.shape[0], out_ref.shape[2]
+def project_heads(normed_ref, copies, weight_buffer, cos_ref, sin_ref, doc_rows, out_refs):
+    heads, size = len(out_refs), cos_ref.shape[1]
     block, extra = cos_ref.shape[0], doc_rows.shape[0]
     depth = weight_buffer.shape[0] // 2
     for copy in copies:
@@ -56,9 +56,9 @@
             piece = part[:, kind * size : (kind + 1) * size]
             if kind < 2:
                 piece = piece * cos_ref[...] + pltpu.roll(piece, size // 2, 1) * sin_ref[...]
-            out_ref[head, at : at + block, :] = piece
+            out_refs[head][at : at + block, :] = piece
         for at in (2 * block, 3 * block + extra):
-            out_ref[head, at : at + extra, :] = doc_rows
+            out_refs[head][at : at + extra, :] = doc_rows
 
 
 def normalise_project_kernel(
@@ -79,20 +79,20 @@
             normed_ref[half, at, :] = (shard[...].astype(jnp.float32) * factor * gain).astype(
                 jnp.bfloat16
             )
-    nothing = jnp.zeros((EXTRA, out_ref.shape[2]), jnp.float32)
-    project_heads(normed_ref, copies, weight_buffer, cos_ref, sin_ref, nothing, out_ref)
-
-
-def project_kernel(
-    place_ref, normed_ref, docs_ref, weight_hbm, cos_ref, sin_ref, out_ref, weight_buffer,
-    semaphores,
-):
+    nothing = jnp.zeros((EXTRA, out_ref.shape[1]), jnp.float32)
+    project_heads(normed_ref, copies, weight_buffer, cos_ref, sin_ref, nothing, [out_ref])
+
+
+def project_kernel(place_ref, normed_ref, docs_ref, weight_hbm, cos_ref, sin_ref, *refs):
+    out_refs, (weight_buffer, semaphores) = refs[:-2], refs[-2:]
     copies = weight_copies(
         place_ref[0], 3 * cos_ref.shape[1], weight_hbm, weight_buffer, semaphores
     )
     for copy in copies:
         copy.start()
-    project_heads(normed_ref, copies, weight_buffer, cos_ref, sin_ref, docs_ref[...], out_ref)
+    project_heads(
+        normed_ref, copies, weight_buffer, cos_ref, sin_ref, docs_ref[...], out_refs
+    )
 
 
 def as_column(rows, count):
@@ -158,11 +158,18 @@
 
 
 def as_message(output, logs, size):
-    high = logs.astype(jnp.bfloat16).astype(jnp.float32)
-    middle = (logs - high).astype(jnp.bfloat16).astype(jnp.float32)
-    rows = as_rows(high, size) + as_rows(middle, size) + as_rows(logs - high - middle, size)
-    rows.append(jnp.zeros((EXTRA - len(rows), size), jnp.float32))
-    return jnp.concatenate([output] + rows, axis=0).astype(jnp.bfloat16)
+    along = jnp.concatenate(as_rows(logs, size), axis=0)
+    high = along.astype(jnp.bfloat16).astype(jnp.float32)
+    middle = (along - high).astype(jnp.bfloat16).astype(jnp.float32)
+    pieces = [output, high, middle, along - high - middle]
+    pieces.append(jnp.zeros((EXTRA - 3 * along.shape[0], size), jnp.float32))
+    return jnp.concatenate(pieces, axis=0).astype(jnp.bfloat16)
+
+
+def logs_of(message, rows):
+    tile = message[rows:].astype(jnp.float32)
+    groups = pl.cdiv(rows, tile.shape[1])
+    return as_column(sum(tile[k * groups : (k + 1) * groups] for k in range(3)), rows)
 
 
 def parted(row, value):
@@ -174,76 +181,84 @@
     )
 
 
-def guest_kernel(scale, here, place_ref, *refs):
-    count = len(refs) - 3
-    query_refs, message_refs, out_ref = refs[:count], refs[count:-1], refs[-1]
-
-    @pl.when(place_ref[0] == here)
+def guests_into(scale, row, query_refs, messages, out_ref):
+    for index, query_ref in enumerate(query_refs):
+        block, size = query_ref.shape[0] - EXTRA, query_ref.shape[1]
+        docs = as_column(query_ref[block:, :].astype(jnp.float32), block)
+        output, logs = softmax_part(scale, query_ref[:block, :], docs, messages, False)
+        for owner, (a, b) in enumerate(zip(parted(row, output), parted(row, logs))):
+            out_ref[index, owner] = as_message(a, b, size)
+
+
+def guests_down_kernel(
+    scale, place_ref, query_two, query_three, first, second, out_ref
+):
+    @pl.when(place_ref[0] == 1)
     def attend():
-        messages = [ref[...] for ref in message_refs]
-        for index, query_ref in enumerate(query_refs):
-            block, size = query_ref.shape[0] - EXTRA, query_ref.shape[1]
-            docs = as_column(query_ref[block:, :].astype(jnp.float32), block)
-            output, logs = softmax_part(scale, query_ref[:block, :], docs, messages, False)
-            for owner, (a, b) in enumerate(
-                zip(parted(place_ref[1], output), parted(place_ref[1], logs))
-            ):
-                out_ref[index, owner] = as_message(a, b, size)
-
-
-def own_kernel(
-    scale, place_ref, query_down, own_down, one_down, query_up, own_up, one_up, two_up, unused_ref,
-    mine_ref, logs_ref, theirs_ref,
+        guests_into(scale, place_ref[1], (query_two, query_three), [first[...], second[...]], out_ref)
+
+
+def guests_up_kernel(
+    scale, place_ref, query_three, first, second, down_ref, unused_ref, out_ref
 ):
-    block, size = query_down.shape[0] - EXTRA, query_down.shape[1]
-    for index, (query_ref, refs) in enumerate(
-        ((query_down, (own_down, one_down)), (query_up, (own_up, one_up, two_up)))
-    ):
-        docs = as_column(query_ref[block:, :].astype(jnp.float32), block)
-        output, logs = softmax_part(
-            scale, query_ref[:block, :], docs, [ref[...] for ref in refs], True
-        )
-        mine, theirs = parted(place_ref[1], output)
-        my_logs, their_logs = parted(place_ref[1], logs)
-        mine_ref[index] = mine
-        logs_ref[index] = my_logs
-        theirs_ref[index] = as_message(theirs, their_logs, size)
+    @pl.when(place_ref[0] == 1)
+    def forward():
+        out_ref[...] = down_ref[...]
+
+    @pl.when(place_ref[0] == 2)
+    def attend():
+        guests_into(scale, place_ref[1], (query_three,), [first[...], second[...]], out_ref)
+
+
+def own_kernel(scale, place_ref, query_ref, *refs):
+    message_refs, (mine_ref, logs_ref, theirs_ref) = refs[:-3], refs[-3:]
+    block, size = query_ref.shape[0] - EXTRA, query_ref.shape[1]
+    docs = as_column(query_ref[block:, :].astype(jnp.float32), block)
+    output, logs = softmax_part(
+        scale, query_ref[:block, :], docs, [ref[...] for ref in message_refs], True
+    )
+    mine_ref[...], theirs = parted(place_ref[1], output)
+    logs_ref[...], their_logs = parted(place_ref[1], logs)
+    theirs_ref[...] = as_message(theirs, their_logs, size)
+
+
+def own_up_kernel(scale, place_ref, query_ref, own, one, two, before_ref, mine, logs, theirs_ref):
+    theirs_ref[0] = before_ref[...]
+    own_kernel(scale, place_ref, query_ref, own, one, two, mine, logs, theirs_ref.at[1])
 
 
 def merge_kernel(
-    place_ref, mine_ref, logs_ref, partner_ref, two_same, two_cross, three_same, three_cross,
-    up_same, up_cross, out_ref,
+    place_ref, mine_down, logs_down, mine_up, logs_up, partner_ref, three_same, three_cross,
+    next_same, next_cross, out_ref,
 ):
-    rows, size = mine_ref.shape[1:]
-    groups = pl.cdiv(rows, size)
+    rows, size = mine_down.shape
     tok, row = place_ref[0], place_ref[1]
-
-    def logs_of(message):
-        tile = message[rows:].astype(jnp.float32)
-        return sum(as_column(tile[k * groups : (k + 1) * groups], rows) for k in range(3))
+    at_two, at_three = tok == 2, tok == 3
 
     def joined(output, logs, message, present):
-        guest = jnp.where(present, logs_of(message), LOW)
+        guest = jnp.where(present, logs_of(message, rows), LOW)
         top = jnp.maximum(logs, guest)
         weight, guest_weight = jnp.exp(logs - top), jnp.exp(guest - top)
         total = output * weight + message[:rows].astype(jnp.float32) * guest_weight
         return (total / (weight + guest_weight)).astype(jnp.bfloat16)
 
-    at_two, at_three = tok == 2, tok == 3
-    for mine, two, three, up in (
-        (True, two_same, three_same, up_same),
-        (False, two_cross, three_cross, up_cross),
+    for mine, three, following in (
+        (True, three_same, next_same),
+        (False, three_cross, next_cross),
     ):
         begin = jnp.where(row == 0, 0, 1) if mine else jnp.where(row == 0, 1, 0)
-        down = jnp.where(at_two, two[...], three[...])
-        for index, (message, present) in enumerate(
-            ((down, at_two | at_three), (up[...], at_three))
+        down = jnp.where(at_two, following[...], three[...])
+        for index, (message, present, output_ref, logs_ref) in enumerate(
+            (
+                (down, at_two | at_three, mine_down, logs_down),
+                (following[...], at_three, mine_up, logs_up),
+            )
         ):
             if mine:
-                output, logs = mine_ref[index], logs_ref[index]
+                output, logs = output_ref[...], logs_ref[...]
             else:
                 partner = partner_ref[index]
-                output, logs = partner[:rows].astype(jnp.float32), logs_of(partner)
+                output, logs = partner[:rows].astype(jnp.float32), logs_of(partner, rows)
             at = pl.ds(pl.multiple_of((2 * begin + index) * size, size), size)
             out_ref[:, at] = joined(output, logs, message, present)
 
@@ -332,15 +347,19 @@
     got = by_col(message, 1)
     squares = squares + got[:rows]
     gain = ordered(core, gain, got[rows:])
-    got = by_col(jnp.concatenate([squares, gain]), 2)
-    near, far, got, flat_weight = lax.optimization_barrier((near, far, got, flat_weight))
+    codes = doc_ids.astype(jnp.float32) + 1.0
+    message = jnp.concatenate([squares, gain])
+    by_chip = by_col(message, 2)
+    by_row_only = by_row(jnp.concatenate([squares, codes]))
+    by_both = lax.ppermute(
+        squares, ("row", "col"), [(r * 4 + c, (1 - r) * 4 + (c ^ 2)) for r, c in grid]
+    )
+    near, far, by_chip, flat_weight = lax.optimization_barrier((near, far, by_chip, flat_weight))
     near_other, far_other = by_col(near, 1), by_col(far, 1)
-    squares = squares + got[:rows]
-    gain = jnp.where(chip == row, gain, got[rows:]).reshape(2, 1, width)
-    codes = doc_ids.astype(jnp.float32) + 1.0
-    got = by_row(jnp.concatenate([squares, codes]))
-    squares = ordered(row, squares, got[:rows]).reshape(block, 1)
-    codes = ordered(row, codes, got[rows:])
+    gain = jnp.where(chip == row, gain, by_chip[rows:]).reshape(2, 1, width)
+    squares = ordered(row, squares + by_chip[:rows], by_row_only[:rows] + by_both)
+    squares = squares.reshape(block, 1)
+    codes = ordered(row, codes, by_row_only[rows:])
     doc_rows = jnp.pad(codes, (0, EXTRA * size - block)).reshape(EXTRA, size)
     places = tok * block + jnp.arange(block, dtype=jnp.int32)
     cosine, sine = rotary_tables(places, size)
@@ -352,13 +371,13 @@
         normed_shape = (jax.ShapeDtypeStruct((2, block, width), jnp.bfloat16),)
         return pl.pallas_call(
             kernel,
-            out_shape=(jax.ShapeDtypeStruct((heads, taller, size), jnp.float32),)
+            out_shape=(jax.ShapeDtypeStruct((taller, size), jnp.float32),) * heads
             + (normed_shape if normalising else ()),
             in_specs=[pl.BlockSpec(memory_space=pltpu.SMEM)]
             + in_vmem(6 if normalising else 2)
             + [pl.BlockSpec(memory_space=pltpu.HBM)]
             + in_vmem(2),
-            out_specs=tuple(in_vmem(2 if normalising else 1)),
+            out_specs=tuple(in_vmem(heads + 1 if normalising else heads)),
             scratch_shapes=[
                 pltpu.VMEM((span, heads * triple), jnp.bfloat16),
                 pltpu.SemaphoreType.DMA((2,)),
@@ -380,8 +399,8 @@
                 cosine, sine,
             )
         away, normed = lax.optimization_barrier((away.astype(jnp.float16), normed))
-        arrived.append(by_row(away[0]))
-    (own,) = projection(project_kernel, pair, False)(
+        arrived.append(by_row(away))
+    own = projection(project_kernel, pair, False)(
         own_head.reshape(1), normed, doc_rows, flat_weight, cosine, sine
     )
     scale = 1.0 / math.sqrt(size)
@@ -390,7 +409,7 @@
         return lax.ppermute(value, "tok", pairs)
 
     def summed(head, begin, end):
-        return own[head, begin:end] + arrived[head][begin:end].astype(jnp.float32)
+        return own[head][begin:end] + arrived[head][begin:end].astype(jnp.float32)
 
     if toks == 4 and pair == 2:
         places = jnp.stack([tok, row])
@@ -399,15 +418,23 @@
             across = [(2 * a + r, 2 * b + 1 - r) for a, b in pairs for r in range(2)]
             return along_tok(value[0], pairs), lax.ppermute(value[1], ("tok", "row"), across)
 
-        def guests(here, queries, messages):
-            shape = (len(queries), 2, rows + EXTRA, size)
+        def on_place(kernel, out_shape, ins, unused=0):
             return pl.pallas_call(
-                lambda *refs: guest_kernel(scale, here, *refs),
-                out_shape=jax.ShapeDtypeStruct(shape, jnp.bfloat16),
-                in_specs=[pl.BlockSpec(memory_space=pltpu.SMEM)] + in_vmem(len(queries) + 2),
-                out_specs=in_vmem(1)[0],
+                kernel,
+                out_shape=out_shape,
+                in_specs=[pl.BlockSpec(memory_space=pltpu.SMEM)]
+                + in_vmem(ins - unused)
+                + [pl.BlockSpec(memory_space=pl.ANY)] * unused,
+                out_specs=jax.tree.map(lambda unused: in_vmem(1)[0], out_shape),
                 compiler_params=pltpu.CompilerParams(vmem_limit_bytes=16 * MIB),
-            )(places, *queries, *messages)
+                cost_estimate=pl.CostEstimate(flops=0, bytes_accessed=0, transcendentals=0),
+            )
+
+        half_message = (rows + EXTRA, size)
+        own_shapes = (
+            jax.ShapeDtypeStruct((rows, size), jnp.float32),
+            jax.ShapeDtypeStruct((rows, 1), jnp.float32),
+        )
 
         query_down = summed(0, break_at, taller).astype(jnp.bfloat16)
         keys_down = summed(0, 0, break_at).astype(jnp.bfloat16)
@@ -426,36 +453,35 @@
         three_up = along_tok(query_up, [(3, 2)])
         one_up = along_tok(keys_up, [(0, 1), (1, 2), (2, 3)])
 
-        down = guests(1, [from_two, from_three], [one_down, keys_down])
+        down = on_place(
+            lambda *refs: guests_down_kernel(scale, *refs),
+            jax.ShapeDtypeStruct((2, 2) + half_message, jnp.bfloat16),
+            4,
+        )(places, from_two, from_three, one_down, keys_down)
         three_same, three_cross = returned(down[1], [(1, 3)])
-        two_same, two_cross = returned(down[0], [(1, 2)])
-        up = guests(2, [three_up], [two_up, one_up])
-        up_same, up_cross = returned(up[0], [(2, 3)])
-
-        mine, logs, theirs = pl.pallas_call(
+        mine_down, logs_down, theirs = on_place(
             lambda *refs: own_kernel(scale, *refs),
-            out_shape=(
-                jax.ShapeDtypeStruct((2, rows, size), jnp.float32),
-                jax.ShapeDtypeStruct((2, rows, 1), jnp.float32),
-                jax.ShapeDtypeStruct((2, rows + EXTRA, size), jnp.bfloat16),
-            ),
-            in_specs=[pl.BlockSpec(memory_space=pltpu.SMEM)]
-            + in_vmem(7)
-            + [pl.BlockSpec(memory_space=pl.ANY)],
-            out_specs=tuple(in_vmem(3)),
-            compiler_params=pltpu.CompilerParams(vmem_limit_bytes=16 * MIB),
-            cost_estimate=pl.CostEstimate(flops=0, bytes_accessed=0, transcendentals=0),
-        )(places, query_down, keys_down, one_down, query_up, keys_up, one_up, two_up, up)
+            own_shapes + (jax.ShapeDtypeStruct(half_message, jnp.bfloat16),),
+            3,
+        )(places, query_down, keys_down, one_down)
+        mine_up, logs_up, theirs = on_place(
+            lambda *refs: own_up_kernel(scale, *refs),
+            own_shapes + (jax.ShapeDtypeStruct((2,) + half_message, jnp.bfloat16),),
+            5,
+        )(places, query_up, keys_up, one_up, two_up, theirs)
         partner = by_row(theirs)
-        return pl.pallas_call(
-            merge_kernel,
-            out_shape=jax.ShapeDtypeStruct((rows, local_heads * size), jnp.bfloat16),
-            in_specs=[pl.BlockSpec(memory_space=pltpu.SMEM)] + in_vmem(9),
-            out_specs=in_vmem(1)[0],
-            compiler_params=pltpu.CompilerParams(vmem_limit_bytes=16 * MIB),
+        up = on_place(
+            lambda *refs: guests_up_kernel(scale, *refs),
+            jax.ShapeDtypeStruct((1, 2) + half_message, jnp.bfloat16),
+            5,
+            1,
+        )(places, three_up, two_up, one_up, down[:1], mine_up)
+        next_same, next_cross = returned(up[0], [(1, 2), (2, 3)])
+        return on_place(
+            merge_kernel, jax.ShapeDtypeStruct((rows, local_heads * size), jnp.bfloat16), 9
         )(
-            places, mine, logs, partner, two_same, two_cross, three_same, three_cross, up_same,
-            up_cross,
+            places, mine_down, logs_down, mine_up, logs_up, partner, three_same, three_cross,
+            next_same, next_cross,
         )
 
     sums = jnp.stack([summed(head, 0, taller) for head in range(pair)]).astype(jnp.bfloat16)

time: 66.5 us -> 67.8 us (1.020)
  the two profiles are of different devices: /device:TPU:24 before, /device:TPU:16 now
where the time goes in v4:
time: 67.8 us; the launch traced here: 67.3 us
  starting transfers between devices  28.5 us (42%)
  Pallas kernels  13 us (19%)
  waiting for transfers between devices  10.7 us (16%)
  local copies, waits for them, and re-layouts  9.66 us (14%)
  other arithmetic  5 us (7%)
    ppermute x8, starting transfers between devices, along_tok(): return lax.ppermute(value, 'tok', pairs)  14.1 us
    unnamed x9, local copies, waits for them, and re-layouts  9.37 us
    ppermute x8, waiting for transfers between devices, along_tok(): return lax.ppermute(value, 'tok', pairs)  5.82 us
    ppermute x4, starting transfers between devices, by_row(): return lax.ppermute(value, 'row', [(0, 1), (1, 0)])  4.79 us
    ppermute x1, starting transfers between devices, per_device(): lax.ppermute(activations, ('row', 'col'), [(r * 4 + c, c // 2 * 4 + 2 * (...  3.31 us
    ppermute x2, starting transfers between devices, returned(): lax.ppermute(value[1], ('tok', 'row'), across)  2.58 us
    ppermute x2, waiting for transfers between devices, returned(): lax.ppermute(value[1], ('tok', 'row'), across)  2.31 us
    pallas_call x1, Pallas kernels, per_device(): projection(normalise_project_kernel, 1, True)  2.13 us
  transfers between devices with their start and end apart: 21, of which 8 were waited for; matrix products, arithmetic and copies ran while one was open for 14% of the time, Pallas kernels for 14%

profile of v4, /device:TPU:16, one launch (start us, length us, event | category | flops | bytes accessed | tf_op | source)
XLA Modules:
  0.0 67.3 jit_solution(18336355810459554836)
XLA Ops:
  0.0 1.6 %collective-permute-start = (bf16[176,1024]{1,0:T(8,128)(2,1)}, bf16[176,1024]{1,0:T(8,128)(2,1)S(1)}, u32[]{:S(2)}, u32[]{:S(2)}) collective-permute-start(bf16[176,1024]{1,0:T(8,128)(2,1)} %param.4), channel_id=1, source_target_pairs={{0,0},{1,1},{2,4},{3,5},{4,2},{5,3},{6,6},{7,7},{8,8},{9,9},{10,12... | collective-permute-start | bytes 1081352 | tf_op jit(solution)/shard_map/ppermute | solution.py:331
  1.6 3.3 %collective-permute-start.1 = (bf16[176,1024]{1,0:T(8,128)(2,1)}, bf16[176,1024]{1,0:T(8,128)(2,1)S(1)}, u32[]{:S(2)}, u32[]{:S(2)}) collective-permute-start(bf16[176,1024]{1,0:T(8,128)(2,1)} %param.4), channel_id=1, source_target_pairs={{0,2},{1,3},{2,6},{3,7},{4,0},{5,1},{6,4},{7,5},{8,10},{9,11},{10,... | collective-permute-start | bytes 1081352 | tf_op jit(solution)/shard_map/ppermute | solution.py:336
  4.9 1.2 %multiply_reduce_fusion = f32[176]{0:T(256)S(1)} fusion(bf16[176,1024]{1,0:T(8,128)(2,1)} %param.4), kind=kLoop, calls=%fused_computation | loop fusion | flops 540496 | bytes 361152 | tf_op jit(solution)/shard_map/reduce_sum | solution.py:342
  6.1 0.7 %convert_element_type.54 = f32[1024]{0:T(1024)S(1)} convert(bf16[1024]{0:T(1024)(128)(2,1)} %param.5) | non-fusion elementwise | flops 1024 | bytes 6144 | tf_op jit(solution)/shard_map/convert_element_type | solution.py:343
  6.9 0.7 %convert_add_fusion = f32[176]{0:T(256)S(1)} fusion(s32[176]{0:T(256)} %param.7), kind=kLoop, calls=%fused_computation.29 | loop fusion | flops 352 | bytes 1408 | tf_op jit(solution)/shard_map/add | solution.py:350
  7.6 0.7 %fusion.2 = (f32[352,64]{1,0:T(8,128)S(1)}, f32[352,64]{1,0:T(8,128)S(1)}, f32[352,64]{1,0:T(8,128)S(1)}) fusion(f32[64]{0:T(128)S(1)} %negate_power_fusion, f32[352]{0:T(512)S(1)} %add_convert_fusion.2), kind=kLoop, calls=%fused_computation.12 | loop fusion | flops 45056 | bytes 272000 | tf_op jit(solution)/shard_map/neg | solution.py:24
  8.3 0.2 pad_maximum_fusion
  8.5 0.8 %slice_select_fusion = (f32[1024]{0:T(1024)S(1)}, f32[1024]{0:T(1024)S(1)}) fusion(f32[1200]{0:T(1024)S(1)} %collective-permute-done.2, bf16[1024]{0:T(1024)(128)(2,1)} %param.5, pred[]{:T(512)S(6)} %eq.10), kind=kLoop, calls=%fused_computation.22 | loop fusion | flops 3072 | bytes 14337 | tf_op jit(solution)/shard_map/jit(_where)/select_n | solution.py:329
  9.3 0.1 concatenate.37
  9.3 0.1 pad_maximum_fusion.3
  9.4 2.0 %collective-permute-start.6 = (f32[352]{0:T(512)S(1)}, f32[352]{0:T(512)S(1)}, u32[]{:S(2)}, u32[]{:S(2)}) collective-permute-start(f32[352]{0:T(512)S(1)} %pad_maximum_fusion.3), channel_id=1, source_target_pairs={{0,4},{4,0},{1,5},{5,1},{2,6},{6,2},{3,7},{7,3},{8,12},{12,8},{9,1... | collective-permute-start | bytes 4232 | tf_op jit(solution)/shard_map/ppermute | solution.py:325
  11.4 0.1 pad_add_fusion.1.place_ref
  11.5 1.5 %collective-permute-start.7 = (f32[176]{0:T(256)S(1)}, f32[176]{0:T(256)S(1)}, u32[]{:S(2)}, u32[]{:S(2)}) collective-permute-start(f32[176]{0:T(256)S(1)} %slice_add_fusion.2), channel_id=1, source_target_pairs={{0,6},{1,7},{2,4},{3,5},{4,2},{5,3},{6,0},{7,1},{8,14},{9,15},{10,... | collective-permute-start | bytes 2120 | tf_op jit(solution)/shard_map/ppermute | solution.py:354
  13.0 4.0 %copy.6 = bf16[256,8,4,384]{3,1,2,0:T(8,128)(2,1)S(1)} copy(bf16[256,8,4,384]{3,2,1,0:T(4,128)(2,1)} %bitcast.30) | data formatting | bytes 12582912
  17.1 0.5 collective-permute-start.5
  17.8 0.1 reshape.78.squares_ref
  17.9 0.8 %collective-permute-done.4.b_near = bf16[176,1024]{1,0:T(8,128)(2,1)S(1)} collective-permute-done((bf16[176,1024]{1,0:T(8,128)(2,1)S(1)}, bf16[176,1024]{1,0:T(8,128)(2,1)S(1)}, u32[]{:S(2)}, u32[]{:S(2)}) %collective-permute-start.4) | collective-permute-done | bytes 360480 | tf_op jit(solution)/shard_map/ppermute | solution.py:322
  18.7 0.5 collective-permute-done.5.b_far
  19.2 2.1 %shard_map.46 = (f32[1088,128]{1,0:T(8,128)S(1)}, bf16[2,352,1024]{2,1,0:T(8,128)(2,1)S(1)}) custom-call(s32[3]{0:T(128)S(1)} %pad_add_fusion.1.place_ref, bf16[176,1024]{1,0:T(8,128)(2,1)S(1)} %collective-permute-done.a_near, bf16[176,1024]{1,0:T(8,128)(2,1)S(1)} %collective-permute-done.1.a_far, bf16[176,1024]{1,0:T(8,128)(2,1)S(1)} %collective-permute-done.4.b_near, ...), custom_call_target="tpu_custom_call" | custom-call | tf_op jit(solution)/shard_map/pallas_call | solution.py:390
  21.4 2.6 %copy-done = bf16[256,8,4,384]{3,1,2,0:T(8,128)(2,1)} copy-done((bf16[256,8,4,384]{3,1,2,0:T(8,128)(2,1)}, bf16[256,8,4,384]{3,1,2,0:T(8,128)(2,1)S(1)}, u32[]{:S(2)}) %copy-start) | copy-done | bytes 6291480
  24.0 0.1 collective-permute-start.8
  24.1 0.1 pad_add_fusion.refs_0_.place_ref
  24.3 2.8 %copy-done.1 = bf16[256,8,4,384]{3,1,2,0:T(8,128)(2,1)S(1)} copy-done((bf16[256,8,4,384]{3,1,2,0:T(8,128)(2,1)S(1)}, bf16[256,8,4,384]{3,1,2,0:T(8,128)(2,1)}, u32[]{:S(2)}) %copy-start.1) | copy-done | bytes 6291480
  27.1 1.2 %shard_map.47 = f32[1088,128]{1,0:T(8,128)S(1)} custom-call(s32[1]{0:T(128)} %bitcast.3.place_ref, bf16[2,352,1024]{2,1,0:T(8,128)(2,1)S(1)} %get-tuple-element.34.normed_ref, f32[16,128]{1,0:T(8,128)S(1)} %broadcast_in_dim.15.docs_ref, bf16[2048,1536]{1,0:T(8,128)(2,1)S(1)} %bitcast.28, f32[352,128]{1,0:T(8,128)S(1)} %get-tuple-element.60.cos_ref, ...), custom_call_target="tpu_custom_call" | custom-call | tf_op jit(solution)/shard_map/pallas_call | solution.py:397
  28.3 2.1 %collective-permute-start.10 = (f16[1088,128]{1,0:T(8,128)(2,1)S(1)}, f16[1088,128]{1,0:T(8,128)(2,1)S(1)}, u32[]{:S(2)}, u32[]{:S(2)}) collective-permute-start(f16[1088,128]{1,0:T(8,128)(2,1)S(1)} %convert_element_type.59), channel_id=1, source_target_pairs={{0,4},{4,0},{1,5},{5,1},{2,6},{6,2},{3,7},{7,3},{8,12},{12,8},{9,1... | collective-permute-start | bytes 835592 | tf_op jit(solution)/shard_map/ppermute | solution.py:325
  30.4 2.0 %shard_map.48 = (f32[1088,128]{1,0:T(8,128)S(1)}, f32[1088,128]{1,0:T(8,128)S(1)}) custom-call(s32[1]{0:T(128)} %bitcast.2.place_ref, bf16[2,352,1024]{2,1,0:T(8,128)(2,1)S(1)} %get-tuple-element.34.normed_ref, f32[16,128]{1,0:T(8,128)S(1)} %fusion.3.docs_ref, bf16[2048,1536]{1,0:T(8,128)(2,1)S(1)} %bitcast.29, f32[352,128]{1,0:T(8,128)S(1)} %get-tuple-element.60.cos_ref, ...), custom_call_target="tpu_custom_call" | custom-call | tf_op jit(solution)/shard_map/pallas_call | solution.py:403
  32.4 1.3 %collective-permute-done.8 = f16[1088,128]{1,0:T(8,128)(2,1)S(1)} collective-permute-done((f16[1088,128]{1,0:T(8,128)(2,1)S(1)}, f16[1088,128]{1,0:T(8,128)(2,1)S(1)}, u32[]{:S(2)}, u32[]{:S(2)}) %collective-permute-start.8) | collective-permute-done | bytes 278560 | tf_op jit(solution)/shard_map/ppermute | solution.py:325
  33.6 2.4 %collective-permute-start.11 = (bf16[368,128]{1,0:T(8,128)(2,1)S(1)}, bf16[368,128]{1,0:T(8,128)(2,1)S(1)}, u32[]{:S(2)}, u32[]{:S(2)}) collective-permute-start(bf16[368,128]{1,0:T(8,128)(2,1)S(1)} %add_convert_fusion.1.refs_1_), channel_id=1, source_target_pairs={{16,8},{17,9},{18,10},{19,11},{20,12},{21,13},{22,14},{23,15}} | collective-permute-start | bytes 282632 | tf_op jit(solution)/shard_map/ppermute | solution.py:409
  36.0 0.7 collective-permute-start.15
  36.7 4.0 %collective-permute-start.9 = (bf16[720,128]{1,0:T(8,128)(2,1)S(1)}, bf16[720,128]{1,0:T(8,128)(2,1)S(1)}, u32[]{:S(2)}, u32[]{:S(2)}) collective-permute-start(bf16[720,128]{1,0:T(8,128)(2,1)S(1)} %add_convert_fusion.refs_2_.refs_4_), channel_id=1, source_target_pairs={{0,8},{16,24},{1,9},{17,25},{2,10},{18,26},{3,11},{19,27},{4,12},{... | collective-permute-start | bytes 552968 | tf_op jit(solution)/shard_map/ppermute | solution.py:409
  40.9 1.9 %collective-permute-start.12 = (bf16[720,128]{1,0:T(8,128)(2,1)S(1)}, bf16[720,128]{1,0:T(8,128)(2,1)S(1)}, u32[]{:S(2)}, u32[]{:S(2)}) collective-permute-start(bf16[720,128]{1,0:T(8,128)(2,1)S(1)} %fusion.refs_2_), channel_id=1, source_target_pairs={{0,8},{8,16},{16,24},{1,9},{9,17},{17,25},{2,10},{10,18},{18,26},{... | collective-permute-start | bytes 552968 | tf_op jit(solution)/shard_map/ppermute | solution.py:409
  42.8 1.3 %collective-permute-start.13 = (bf16[720,128]{1,0:T(8,128)(2,1)S(1)}, bf16[720,128]{1,0:T(8,128)(2,1)S(1)}, u32[]{:S(2)}, u32[]{:S(2)}) collective-permute-start(bf16[720,128]{1,0:T(8,128)(2,1)S(1)} %fusion.refs_2_), channel_id=1, source_target_pairs={{0,16},{1,17},{2,18},{3,19},{4,20},{5,21},{6,22},{7,23}} | collective-permute-start | bytes 552968 | tf_op jit(solution)/shard_map/ppermute | solution.py:409
  44.1 1.3 %collective-permute-start.18 = (bf16[368,128]{1,0:T(8,128)(2,1)S(1)}, bf16[368,128]{1,0:T(8,128)(2,1)S(1)}, u32[]{:S(2)}, u32[]{:S(2)}) collective-permute-start(bf16[368,128]{1,0:T(8,128)(2,1)S(1)} %fusion.1.refs_1_), channel_id=1, source_target_pairs={{24,16},{25,17},{26,18},{27,19},{28,20},{29,21},{30,22},{31,23}} | collective-permute-start | bytes 282632 | tf_op jit(solution)/shard_map/ppermute | solution.py:409
  45.5 0.3 collective-permute-done.9.refs_3_
  45.7 0.5 shard_map.51
  46.3 0.7 collective-permute-start.16
  47.0 0.7 collective-permute-start.17
  47.7 1.7 %shard_map.49 = (f32[176,128]{1,0:T(8,128)S(1)}, f32[176,1]{1,0:T(8,128)S(1)}, bf16[192,128]{1,0:T(8,128)(2,1)S(1)}) custom-call(s32[2]{0:T(128)S(1)} %pad_add_fusion.refs_0_.place_ref, bf16[368,128]{1,0:T(8,128)(2,1)S(1)} %add_convert_fusion.1.refs_1_, bf16[720,128]{1,0:T(8,128)(2,1)S(1)} %add_convert_fusion.refs_2_.refs_4_, ...), custom_call_target="tpu_custom_call" | custom-call | tf_op jit(solution)/shard_map/pallas_call | solution.py:462
  49.4 0.8 %collective-permute-done.12.refs_3_ = bf16[720,128]{1,0:T(8,128)(2,1)S(1)} collective-permute-done((bf16[720,128]{1,0:T(8,128)(2,1)S(1)}, bf16[720,128]{1,0:T(8,128)(2,1)S(1)}, u32[]{:S(2)}, u32[]{:S(2)}) %collective-permute-start.12) | collective-permute-done | bytes 184352 | tf_op jit(solution)/shard_map/ppermute | solution.py:409
  50.2 2.1 %collective-permute-done.13.refs_4_.refs_2_ = bf16[720,128]{1,0:T(8,128)(2,1)S(1)} collective-permute-done((bf16[720,128]{1,0:T(8,128)(2,1)S(1)}, bf16[720,128]{1,0:T(8,128)(2,1)S(1)}, u32[]{:S(2)}, u32[]{:S(2)}) %collective-permute-start.13) | collective-permute-done | bytes 184352 | tf_op jit(solution)/shard_map/ppermute | solution.py:409
  52.3 2.1 %shard_map.50 = (f32[176,128]{1,0:T(8,128)S(1)}, f32[176,1]{1,0:T(8,128)S(1)}, bf16[2,192,128]{2,1,0:T(8,128)(2,1)S(1)}) custom-call(s32[2]{0:T(128)S(1)} %pad_add_fusion.refs_0_.place_ref, bf16[368,128]{1,0:T(8,128)(2,1)S(1)} %fusion.1.refs_1_, bf16[720,128]{1,0:T(8,128)(2,1)S(1)} %fusion.refs_2_, bf16[720,128]{1,0:T(8,128)(2,1)S(1)} %collective-permute-done.12.refs_3_, ...), custom_call_target="tpu_custom_call" | custom-call | tf_op jit(solution)/shard_map/pallas_call | solution.py:467
  54.3 0.7 collective-permute-start.14
  55.0 1.7 %shard_map.52 = bf16[1,2,192,128]{3,2,1,0:T(8,128)(2,1)S(1)} custom-call(s32[2]{0:T(128)S(1)} %pad_add_fusion.refs_0_.place_ref, bf16[368,128]{1,0:T(8,128)(2,1)S(1)} %collective-permute-done.18.refs_1_, bf16[720,128]{1,0:T(8,128)(2,1)S(1)} %collective-permute-done.13.refs_4_.refs_2_, bf16[720,128]{1,0:T(8,128)(2,1)S(1)} %collective-permute-done.12.refs_3_, ...), custom_call_target="tpu_custom_call" | custom-call | tf_op jit(solution)/shard_map/pallas_call | solution.py:473
  56.7 1.9 %collective-permute-start.19 = (bf16[192,128]{1,0:T(8,128)(2,1)S(1)}, bf16[192,128]{1,0:T(8,128)(2,1)S(1)}, u32[]{:S(2)}, u32[]{:S(2)}) collective-permute-start(bf16[192,128]{1,0:T(8,128)(2,1)S(1)} %get-tuple-element.48), channel_id=1, source_target_pairs={{8,16},{16,24},{9,17},{17,25},{10,18},{18,26},{11,19},{19,27},{12,... | collective-permute-start | bytes 147464 | tf_op jit(solution)/shard_map/ppermute | solution.py:409
  58.6 1.9 %collective-permute-start.20 = (bf16[192,128]{1,0:T(8,128)(2,1)S(1)}, bf16[192,128]{1,0:T(8,128)(2,1)S(1)}, u32[]{:S(2)}, u32[]{:S(2)}) collective-permute-start(bf16[192,128]{1,0:T(8,128)(2,1)S(1)} %get-tuple-element.47), channel_id=1, source_target_pairs={{8,20},{12,16},{16,28},{20,24},{9,21},{13,17},{17,29},{21,25},{10,... | collective-permute-start | bytes 147464 | tf_op jit(solution)/shard_map/ppermute | solution.py:419
  60.6 2.6 %collective-permute-done.19.next_same = bf16[192,128]{1,0:T(8,128)(2,1)S(1)} collective-permute-done((bf16[192,128]{1,0:T(8,128)(2,1)S(1)}, bf16[192,128]{1,0:T(8,128)(2,1)S(1)}, u32[]{:S(2)}, u32[]{:S(2)}) %collective-permute-start.19) | collective-permute-done | bytes 49184 | tf_op jit(solution)/shard_map/ppermute | solution.py:409
  63.2 2.3 %collective-permute-done.20.next_cross = bf16[192,128]{1,0:T(8,128)(2,1)S(1)} collective-permute-done((bf16[192,128]{1,0:T(8,128)(2,1)S(1)}, bf16[192,128]{1,0:T(8,128)(2,1)S(1)}, u32[]{:S(2)}, u32[]{:S(2)}) %collective-permute-start.20) | collective-permute-done | bytes 49184 | tf_op jit(solution)/shard_map/ppermute | solution.py:419
  65.5 1.8 %shard_map.53 = bf16[176,512]{1,0:T(8,128)(2,1)} custom-call(s32[2]{0:T(128)S(1)} %pad_add_fusion.refs_0_.place_ref, f32[176,128]{1,0:T(8,128)S(1)} %get-tuple-element.37.mine_down, f32[176,1]{1,0:T(8,128)S(1)} %get-tuple-element.38.logs_down, f32[176,128]{1,0:T(8,128)S(1)} %get-tuple-element.42.refs_5_.mine_up, f32[176,1]{1,0:T(8,128)S(1)} %get-tuple-element.43.logs_up, ...), custom_call_target="tpu_custom_call" | custom-call | tf_op jit(solution)/shard_map/pallas_call | solution.py:480
  (43 shorter events, 0.8 us)
Async XLA Ops:
  0.0 17.0 %collective-permute-start = (bf16[176,1024]{1,0:T(8,128)(2,1)}, bf16[176,1024]{1,0:T(8,128)(2,1)S(1)}, u32[]{:S(2)}, u32[]{:S(2)}) collective-permute-start(bf16[176,1024]{1,0:T(8,128)(2,1)} %param.4), channel_id=1, source_target_pairs={{0,0},{1,1},{2,4},{3,5},{4,2},{5,3},{6,6},{7,7},{8,8},{9,9},{10,12... | collective-permute-start | bytes 1081352 | tf_op jit(solution)/shard_map/ppermute | solution.py:331
  1.6 15.3 %collective-permute-start.1 = (bf16[176,1024]{1,0:T(8,128)(2,1)}, bf16[176,1024]{1,0:T(8,128)(2,1)S(1)}, u32[]{:S(2)}, u32[]{:S(2)}) collective-permute-start(bf16[176,1024]{1,0:T(8,128)(2,1)} %param.4), channel_id=1, source_target_pairs={{0,2},{1,3},{2,6},{3,7},{4,0},{5,1},{6,4},{7,5},{8,10},{9,11},{10,... | collective-permute-start | bytes 1081352 | tf_op jit(solution)/shard_map/ppermute | solution.py:336
  6.9 1.6 %collective-permute-start.2 = (f32[1200]{0:T(1024)S(1)}, f32[1200]{0:T(1024)S(1)}, u32[]{:S(2)}, u32[]{:S(2)}) collective-permute-start(f32[1200]{0:T(1024)S(1)} %pad_maximum_fusion.2), channel_id=1, source_target_pairs={{0,1},{1,0},{2,3},{3,2},{4,5},{5,4},{6,7},{7,6},{8,9},{9,8},{10,11... | collective-permute-start | bytes 14408 | tf_op jit(solution)/shard_map/ppermute | solution.py:322
  9.3 7.6 %collective-permute-start.3 = (f32[2224]{0:T(1024)S(1)}, f32[2224]{0:T(1024)S(1)}, u32[]{:S(2)}, u32[]{:S(2)}) collective-permute-start(f32[2224]{0:T(1024)S(1)} %concatenate.37), channel_id=1, source_target_pairs={{0,2},{1,3},{2,0},{3,1},{4,6},{5,7},{6,4},{7,5},{8,10},{9,11},{10,... | collective-permute-start | bytes 26696 | tf_op jit(solution)/shard_map/ppermute | solution.py:322
  9.4 8.1 %collective-permute-start.6 = (f32[352]{0:T(512)S(1)}, f32[352]{0:T(512)S(1)}, u32[]{:S(2)}, u32[]{:S(2)}) collective-permute-start(f32[352]{0:T(512)S(1)} %pad_maximum_fusion.3), channel_id=1, source_target_pairs={{0,4},{4,0},{1,5},{5,1},{2,6},{6,2},{3,7},{7,3},{8,12},{12,8},{9,1... | collective-permute-start | bytes 4232 | tf_op jit(solution)/shard_map/ppermute | solution.py:325
  11.5 6.1 %collective-permute-start.7 = (f32[176]{0:T(256)S(1)}, f32[176]{0:T(256)S(1)}, u32[]{:S(2)}, u32[]{:S(2)}) collective-permute-start(f32[176]{0:T(256)S(1)} %slice_add_fusion.2), channel_id=1, source_target_pairs={{0,6},{1,7},{2,4},{3,5},{4,2},{5,3},{6,0},{7,1},{8,14},{9,15},{10,... | collective-permute-start | bytes 2120 | tf_op jit(solution)/shard_map/ppermute | solution.py:354
  13.0 4.6 %copy-start.3 = (s32[176]{0:T(256)S(1)}, s32[176]{0:T(256)}, u32[]{:S(2)}) copy-start(s32[176]{0:T(256)} %param.7) | copy-start | bytes 2116
  17.0 1.7 %collective-permute-start.4 = (bf16[176,1024]{1,0:T(8,128)(2,1)S(1)}, bf16[176,1024]{1,0:T(8,128)(2,1)S(1)}, u32[]{:S(2)}, u32[]{:S(2)}) collective-permute-start(bf16[176,1024]{1,0:T(8,128)(2,1)S(1)} %collective-permute-done.a_near), channel_id=1, source_target_pairs={{0,1},{1,0},{2,3},{3,2},{4,5},{5,4},{6,7},{7,6},{8,9},{9,8},{10,11... | collective-permute-start | bytes 1081352 | tf_op jit(solution)/shard_map/ppermute | solution.py:322
  17.1 2.2 %collective-permute-start.5 = (bf16[176,1024]{1,0:T(8,128)(2,1)S(1)}, bf16[176,1024]{1,0:T(8,128)(2,1)S(1)}, u32[]{:S(2)}, u32[]{:S(2)}) collective-permute-start(bf16[176,1024]{1,0:T(8,128)(2,1)S(1)} %collective-permute-done.1.a_far), channel_id=1, source_target_pairs={{0,1},{1,0},{2,3},{3,2},{4,5},{5,4},{6,7},{7,6},{8,9},{9,8},{10,11... | collective-permute-start | bytes 1081352 | tf_op jit(solution)/shard_map/ppermute | solution.py:322
  21.4 2.6 %copy-start = (bf16[256,8,4,384]{3,1,2,0:T(8,128)(2,1)}, bf16[256,8,4,384]{3,1,2,0:T(8,128)(2,1)S(1)}, u32[]{:S(2)}) copy-start(bf16[256,8,4,384]{3,1,2,0:T(8,128)(2,1)S(1)} %copy.6) | copy-start | bytes 18874372
  24.0 9.6 %collective-permute-start.8 = (f16[1088,128]{1,0:T(8,128)(2,1)S(1)}, f16[1088,128]{1,0:T(8,128)(2,1)S(1)}, u32[]{:S(2)}, u32[]{:S(2)}) collective-permute-start(f16[1088,128]{1,0:T(8,128)(2,1)S(1)} %convert_element_type.58), channel_id=1, source_target_pairs={{0,4},{4,0},{1,5},{5,1},{2,6},{6,2},{3,7},{7,3},{8,12},{12,8},{9,1... | collective-permute-start | bytes 835592 | tf_op jit(solution)/shard_map/ppermute | solution.py:325
  24.3 2.8 %copy-start.1 = (bf16[256,8,4,384]{3,1,2,0:T(8,128)(2,1)S(1)}, bf16[256,8,4,384]{3,1,2,0:T(8,128)(2,1)}, u32[]{:S(2)}) copy-start(bf16[256,8,4,384]{3,1,2,0:T(8,128)(2,1)} %copy-done) | copy-start | bytes 18874372
  27.1 3.3 %copy-start.2 = (bf16[256,8,4,384]{3,1,2,0:T(8,128)(2,1)S(1)}, bf16[256,8,4,384]{3,1,2,0:T(8,128)(2,1)}, u32[]{:S(2)}) copy-start(bf16[256,8,4,384]{3,1,2,0:T(8,128)(2,1)} %copy-done) | copy-start | bytes 18874372
  28.3 12.5 %collective-permute-start.10 = (f16[1088,128]{1,0:T(8,128)(2,1)S(1)}, f16[1088,128]{1,0:T(8,128)(2,1)S(1)}, u32[]{:S(2)}, u32[]{:S(2)}) collective-permute-start(f16[1088,128]{1,0:T(8,128)(2,1)S(1)} %convert_element_type.59), channel_id=1, source_target_pairs={{0,4},{4,0},{1,5},{5,1},{2,6},{6,2},{3,7},{7,3},{8,12},{12,8},{9,1... | collective-permute-start | bytes 835592 | tf_op jit(solution)/shard_map/ppermute | solution.py:325
  33.6 7.1 %collective-permute-start.11 = (bf16[368,128]{1,0:T(8,128)(2,1)S(1)}, bf16[368,128]{1,0:T(8,128)(2,1)S(1)}, u32[]{:S(2)}, u32[]{:S(2)}) collective-permute-start(bf16[368,128]{1,0:T(8,128)(2,1)S(1)} %add_convert_fusion.1.refs_1_), channel_id=1, source_target_pairs={{16,8},{17,9},{18,10},{19,11},{20,12},{21,13},{22,14},{23,15}} | collective-permute-start | bytes 282632 | tf_op jit(solution)/shard_map/ppermute | solution.py:409
  36.0 9.4 %collective-permute-start.15 = (bf16[368,128]{1,0:T(8,128)(2,1)S(1)}, bf16[368,128]{1,0:T(8,128)(2,1)S(1)}, u32[]{:S(2)}, u32[]{:S(2)}) collective-permute-start(bf16[368,128]{1,0:T(8,128)(2,1)S(1)} %add_convert_fusion.1.refs_1_), channel_id=1, source_target_pairs={{24,8},{25,9},{26,10},{27,11},{28,12},{29,13},{30,14},{31,15}} | collective-permute-start | bytes 282632 | tf_op jit(solution)/shard_map/ppermute | solution.py:409
  36.7 9.0 %collective-permute-start.9 = (bf16[720,128]{1,0:T(8,128)(2,1)S(1)}, bf16[720,128]{1,0:T(8,128)(2,1)S(1)}, u32[]{:S(2)}, u32[]{:S(2)}) collective-permute-start(bf16[720,128]{1,0:T(8,128)(2,1)S(1)} %add_convert_fusion.refs_2_.refs_4_), channel_id=1, source_target_pairs={{0,8},{16,24},{1,9},{17,25},{2,10},{18,26},{3,11},{19,27},{4,12},{... | collective-permute-start | bytes 552968 | tf_op jit(solution)/shard_map/ppermute | solution.py:409
  40.9 9.3 %collective-permute-start.12 = (bf16[720,128]{1,0:T(8,128)(2,1)S(1)}, bf16[720,128]{1,0:T(8,128)(2,1)S(1)}, u32[]{:S(2)}, u32[]{:S(2)}) collective-permute-start(bf16[720,128]{1,0:T(8,128)(2,1)S(1)} %fusion.refs_2_), channel_id=1, source_target_pairs={{0,8},{8,16},{16,24},{1,9},{9,17},{17,25},{2,10},{10,18},{18,26},{... | collective-permute-start | bytes 552968 | tf_op jit(solution)/shard_map/ppermute | solution.py:409
  42.8 9.5 %collective-permute-start.13 = (bf16[720,128]{1,0:T(8,128)(2,1)S(1)}, bf16[720,128]{1,0:T(8,128)(2,1)S(1)}, u32[]{:S(2)}, u32[]{:S(2)}) collective-permute-start(bf16[720,128]{1,0:T(8,128)(2,1)S(1)} %fusion.refs_2_), channel_id=1, source_target_pairs={{0,16},{1,17},{2,18},{3,19},{4,20},{5,21},{6,22},{7,23}} | collective-permute-start | bytes 552968 | tf_op jit(solution)/shard_map/ppermute | solution.py:409
  44.1 10.8 %collective-permute-start.18 = (bf16[368,128]{1,0:T(8,128)(2,1)S(1)}, bf16[368,128]{1,0:T(8,128)(2,1)S(1)}, u32[]{:S(2)}, u32[]{:S(2)}) collective-permute-start(bf16[368,128]{1,0:T(8,128)(2,1)S(1)} %fusion.1.refs_1_), channel_id=1, source_target_pairs={{24,16},{25,17},{26,18},{27,19},{28,20},{29,21},{30,22},{31,23}} | collective-permute-start | bytes 282632 | tf_op jit(solution)/shard_map/ppermute | solution.py:409
  46.3 14.2 %collective-permute-start.16 = (bf16[192,128]{1,0:T(8,128)(2,1)S(1)}, bf16[192,128]{1,0:T(8,128)(2,1)S(1)}, u32[]{:S(2)}, u32[]{:S(2)}) collective-permute-start(bf16[192,128]{1,0:T(8,128)(2,1)S(1)} %get-tuple-element.46), channel_id=1, source_target_pairs={{8,24},{9,25},{10,26},{11,27},{12,28},{13,29},{14,30},{15,31}} | collective-permute-start | bytes 147464 | tf_op jit(solution)/shard_map/ppermute | solution.py:409
  47.0 13.6 %collective-permute-start.17 = (bf16[192,128]{1,0:T(8,128)(2,1)S(1)}, bf16[192,128]{1,0:T(8,128)(2,1)S(1)}, u32[]{:S(2)}, u32[]{:S(2)}) collective-permute-start(bf16[192,128]{1,0:T(8,128)(2,1)S(1)} %get-tuple-element.45), channel_id=1, source_target_pairs={{8,28},{12,24},{9,29},{13,25},{10,30},{14,26},{11,31},{15,27}} | collective-permute-start | bytes 147464 | tf_op jit(solution)/shard_map/ppermute | solution.py:419
  54.3 11.2 %collective-permute-start.14 = (bf16[2,192,128]{2,1,0:T(8,128)(2,1)S(1)}, bf16[2,192,128]{2,1,0:T(8,128)(2,1)S(1)}, u32[]{:S(2)}, u32[]{:S(2)}) collective-permute-start(bf16[2,192,128]{2,1,0:T(8,128)(2,1)S(1)} %get-tuple-element.44), channel_id=1, source_target_pairs={{0,4},{4,0},{1,5},{5,1},{2,6},{6,2},{3,7},{7,3},{8,12},{12,8},{9,1... | collective-permute-start | bytes 294920 | tf_op jit(solution)/shard_map/ppermute | solution.py:325
  56.7 6.5 %collective-permute-start.19 = (bf16[192,128]{1,0:T(8,128)(2,1)S(1)}, bf16[192,128]{1,0:T(8,128)(2,1)S(1)}, u32[]{:S(2)}, u32[]{:S(2)}) collective-permute-start(bf16[192,128]{1,0:T(8,128)(2,1)S(1)} %get-tuple-element.48), channel_id=1, source_target_pairs={{8,16},{16,24},{9,17},{17,25},{10,18},{18,26},{11,19},{19,27},{12,... | collective-permute-start | bytes 147464 | tf_op jit(solution)/shard_map/ppermute | solution.py:409
  58.6 6.9 %collective-permute-start.20 = (bf16[192,128]{1,0:T(8,128)(2,1)S(1)}, bf16[192,128]{1,0:T(8,128)(2,1)S(1)}, u32[]{:S(2)}, u32[]{:S(2)}) collective-permute-start(bf16[192,128]{1,0:T(8,128)(2,1)S(1)} %get-tuple-element.47), channel_id=1, source_target_pairs={{8,20},{12,16},{16,28},{20,24},{9,21},{13,17},{17,29},{21,25},{10,... | collective-permute-start | bytes 147464 | tf_op jit(solution)/shard_map/ppermute | solution.py:419

commit v5 on v4

--- a/solution.py
+++ b/solution.py
@@ -25,52 +25,36 @@
     )
 
 
-def weight_copies(first_head, triple, weight_hbm, weight_buffer, semaphores):
-    depth = weight_buffer.shape[0] // 2
-    columns = weight_buffer.shape[1]
-    first = pl.multiple_of(first_head * triple, 128)
-    return [
-        pltpu.make_async_copy(
-            weight_hbm.at[pl.ds(half * depth, depth), pl.ds(first, columns)],
-            weight_buffer.at[pl.ds(half * depth, depth), :],
-            semaphores.at[half],
-        )
-        for half in range(2)
-    ]
-
-
-def project_heads(normed_ref, copies, weight_buffer, cos_ref, sin_ref, doc_rows, out_refs):
-    heads, size = len(out_refs), cos_ref.shape[1]
-    block, extra = cos_ref.shape[0], doc_rows.shape[0]
-    depth = weight_buffer.shape[0] // 2
-    for copy in copies:
-        copy.wait()
-    for head in range(heads):
-        columns = slice(head * 3 * size, (head + 1) * 3 * size)
-        part = jnp.dot(
-            normed_ref[0], weight_buffer[:depth, columns], preferred_element_type=jnp.float32
-        ) + jnp.dot(
-            normed_ref[1], weight_buffer[depth:, columns], preferred_element_type=jnp.float32
-        )
-        for kind, at in ((0, 2 * block + extra), (1, 0), (2, block)):
-            piece = part[:, kind * size : (kind + 1) * size]
-            if kind < 2:
-                piece = piece * cos_ref[...] + pltpu.roll(piece, size // 2, 1) * sin_ref[...]
-            out_refs[head][at : at + block, :] = piece
-        for at in (2 * block, 3 * block + extra):
-            out_refs[head][at : at + extra, :] = doc_rows
+def project_chunks(normed_ref, first_column, weight_ref, cos_ref, sin_ref, doc_rows, out_refs):
+    block, size = cos_ref.shape
+    extra = doc_rows.shape[0]
+    depth = weight_ref.shape[0] // 2
+
+    def product(column, width):
+        at = pl.ds(pl.multiple_of(first_column + column * size, size), width * size)
+        return jnp.dot(
+            normed_ref[0], weight_ref[:depth, at], preferred_element_type=jnp.float32
+        ) + jnp.dot(normed_ref[1], weight_ref[depth:, at], preferred_element_type=jnp.float32)
+
+    def rotated(piece):
+        return piece * cos_ref[...] + pltpu.roll(piece, size // 2, 1) * sin_ref[...]
+
+    for chunk, out_ref in out_refs:
+        both = product(4 if chunk == 0 else 1, 2)
+        out_ref[:block, :] = rotated(both[:, :size])
+        out_ref[block : 2 * block, :] = both[:, size:]
+        out_ref[2 * block : 2 * block + extra, :] = doc_rows
+        out_ref[2 * block + extra : 3 * block + extra, :] = rotated(product(0 if chunk == 0 else 3, 1))
+        out_ref[3 * block + extra :, :] = doc_rows
 
 
 def normalise_project_kernel(
-    place_ref, a_near, a_far, b_near, b_far, squares_ref, gain_ref, weight_hbm, cos_ref, sin_ref,
-    out_ref, normed_ref, weight_buffer, semaphores,
+    place_ref, a_near, a_far, b_near, b_far, squares_ref, gain_ref, weight_ref, cos_ref, sin_ref,
+    out_ref, normed_ref,
 ):
     rows = a_near.shape[0]
     features = 2 * gain_ref.shape[0] * gain_ref.shape[2]
-    core, near_row, head = place_ref[0], place_ref[1], place_ref[2]
-    copies = weight_copies(head, 3 * cos_ref.shape[1], weight_hbm, weight_buffer, semaphores)
-    for copy in copies:
-        copy.start()
+    core, near_row = place_ref[0], place_ref[1]
     for shards, half in (((a_near, a_far), core), ((b_near, b_far), 1 - core)):
         gain = gain_ref[half]
         for shard, row in zip(shards, (near_row, 1 - near_row)):
@@ -80,18 +64,16 @@
                 jnp.bfloat16
             )
     nothing = jnp.zeros((EXTRA, out_ref.shape[1]), jnp.float32)
-    project_heads(normed_ref, copies, weight_buffer, cos_ref, sin_ref, nothing, [out_ref])
-
-
-def project_kernel(place_ref, normed_ref, docs_ref, weight_hbm, cos_ref, sin_ref, *refs):
-    out_refs, (weight_buffer, semaphores) = refs[:-2], refs[-2:]
-    copies = weight_copies(
-        place_ref[0], 3 * cos_ref.shape[1], weight_hbm, weight_buffer, semaphores
-    )
-    for copy in copies:
-        copy.start()
-    project_heads(
-        normed_ref, copies, weight_buffer, cos_ref, sin_ref, docs_ref[...], out_refs
+    project_chunks(
+        normed_ref, place_ref[2], weight_ref, cos_ref, sin_ref, nothing, [(0, out_ref)]
+    )
+
+
+def project_kernel(
+    chunks, place_ref, normed_ref, docs_ref, weight_ref, cos_ref, sin_ref, *out_refs
+):
+    project_chunks(
+        normed_ref, place_ref[0], weight_ref, cos_ref, sin_ref, docs_ref[...], list(zip(chunks, out_refs))
     )
 
 
@@ -131,12 +113,20 @@
     )
 
 
-def softmax_part(scale, query, query_docs, messages, causal):
+def softmax_part(scale, query_message, messages, causal):
+    valid = [present for message, present in messages]
+    messages = [message for message, present in messages]
+    query = query_message[:-EXTRA]
+    query_docs = as_column(query_message[-EXTRA:].astype(jnp.float32), query.shape[0])
     block = (messages[0].shape[0] - EXTRA) // 2
     keys = jnp.concatenate([message[:block] for message in messages], axis=0)
     values = jnp.concatenate([message[block : 2 * block] for message in messages], axis=0)
     key_docs = jnp.concatenate(
-        [as_lanes(message[2 * block :].astype(jnp.float32), block) for message in messages], axis=1
+        [
+            jnp.where(present, as_lanes(message[2 * block :].astype(jnp.float32), block), 0.0)
+            for message, present in zip(messages, valid)
+        ],
+        axis=1,
     )
     visible = query_docs == key_docs
     if causal:
@@ -181,50 +171,63 @@
     )
 
 
-def guests_into(scale, row, query_refs, messages, out_ref):
-    for index, query_ref in enumerate(query_refs):
-        block, size = query_ref.shape[0] - EXTRA, query_ref.shape[1]
-        docs = as_column(query_ref[block:, :].astype(jnp.float32), block)
-        output, logs = softmax_part(scale, query_ref[:block, :], docs, messages, False)
+def guests_into(scale, row, queries, messages, out_ref):
+    for index, query in enumerate(queries):
+        output, logs = softmax_part(scale, query, [(m, True) for m in messages], False)
         for owner, (a, b) in enumerate(zip(parted(row, output), parted(row, logs))):
-            out_ref[index, owner] = as_message(a, b, size)
-
-
-def guests_down_kernel(
-    scale, place_ref, query_two, query_three, first, second, out_ref
-):
+            out_ref[index, owner] = as_message(a, b, query.shape[1])
+
+
+def guests_down_kernel(scale, place_ref, one_ref, two_ref, first_ref, own_ref, unused_ref, out_ref):
     @pl.when(place_ref[0] == 1)
     def attend():
-        guests_into(scale, place_ref[1], (query_two, query_three), [first[...], second[...]], out_ref)
-
-
-def guests_up_kernel(
-    scale, place_ref, query_three, first, second, down_ref, unused_ref, out_ref
-):
+        height = first_ref.shape[0]
+        queries = [ref[(height - EXTRA) // 2 :, :] for ref in (one_ref, two_ref)]
+        guests_into(
+            scale, place_ref[1], queries, [first_ref[...], own_ref[:height, :]], out_ref
+        )
+
+
+def guests_up_kernel(scale, place_ref, query_ref, first_ref, second_ref, down_ref, out_ref):
     @pl.when(place_ref[0] == 1)
     def forward():
-        out_ref[...] = down_ref[...]
+        out_ref[...] = down_ref[:1]
 
     @pl.when(place_ref[0] == 2)
     def attend():
-        guests_into(scale, place_ref[1], (query_three,), [first[...], second[...]], out_ref)
-
-
-def own_kernel(scale, place_ref, query_ref, *refs):
-    message_refs, (mine_ref, logs_ref, theirs_ref) = refs[:-3], refs[-3:]
-    block, size = query_ref.shape[0] - EXTRA, query_ref.shape[1]
-    docs = as_column(query_ref[block:, :].astype(jnp.float32), block)
-    output, logs = softmax_part(
-        scale, query_ref[:block, :], docs, [ref[...] for ref in message_refs], True
-    )
-    mine_ref[...], theirs = parted(place_ref[1], output)
-    logs_ref[...], their_logs = parted(place_ref[1], logs)
-    theirs_ref[...] = as_message(theirs, their_logs, size)
-
-
-def own_up_kernel(scale, place_ref, query_ref, own, one, two, before_ref, mine, logs, theirs_ref):
-    theirs_ref[0] = before_ref[...]
-    own_kernel(scale, place_ref, query_ref, own, one, two, mine, logs, theirs_ref.at[1])
+        query = query_ref[(query_ref.shape[0] - EXTRA) // 2 :, :]
+        guests_into(scale, place_ref[1], [query], [first_ref[...], second_ref[...]], out_ref)
+
+
+def own_part(scale, row, query, messages, mine_ref, logs_ref):
+    output, logs = softmax_part(scale, query, messages, True)
+    mine_ref[...], theirs = parted(row, output)
+    logs_ref[...], their_logs = parted(row, logs)
+    return as_message(theirs, their_logs, query.shape[1])
+
+
+def own_up_kernel(
+    scale, place_ref, query_chunk, own_chunk, one_up, from_one, from_zero, mine, logs, theirs_ref
+):
+    tok = place_ref[0]
+    height = from_one.shape[0]
+    previous = jnp.where(tok == 1, one_up[...], from_one[...])
+    messages = [
+        (own_chunk[:height, :], True), (previous, tok > 0), (from_zero[...], tok == 2)
+    ]
+    theirs_ref[...] = own_part(
+        scale, place_ref[1], query_chunk[height:, :], messages, mine, logs
+    )
+
+
+def own_down_kernel(
+    scale, place_ref, query_chunk, own_chunk, previous, before_ref, unused_ref, mine, logs, theirs_ref
+):
+    tok = place_ref[0]
+    height = previous.shape[0]
+    messages = [(own_chunk[:height, :], True), (previous[...], (tok == 1) | (tok == 3))]
+    theirs_ref[0] = own_part(scale, place_ref[1], query_chunk[height:, :], messages, mine, logs)
+    theirs_ref[1] = before_ref[...]
 
 
 def merge_kernel(
@@ -239,7 +242,8 @@
         guest = jnp.where(present, logs_of(message, rows), LOW)
         top = jnp.maximum(logs, guest)
         weight, guest_weight = jnp.exp(logs - top), jnp.exp(guest - top)
-        total = output * weight + message[:rows].astype(jnp.float32) * guest_weight
+        guest_output = jnp.where(present, message[:rows].astype(jnp.float32), 0.0)
+        total = output * weight + guest_output * guest_weight
         return (total / (weight + guest_weight)).astype(jnp.bfloat16)
 
     for mine, three, following in (
@@ -348,18 +352,14 @@
     squares = squares + got[:rows]
     gain = ordered(core, gain, got[rows:])
     codes = doc_ids.astype(jnp.float32) + 1.0
-    message = jnp.concatenate([squares, gain])
-    by_chip = by_col(message, 2)
-    by_row_only = by_row(jnp.concatenate([squares, codes]))
-    by_both = lax.ppermute(
-        squares, ("row", "col"), [(r * 4 + c, (1 - r) * 4 + (c ^ 2)) for r, c in grid]
-    )
-    near, far, by_chip, flat_weight = lax.optimization_barrier((near, far, by_chip, flat_weight))
+    got = by_row(jnp.concatenate([squares, codes]))
+    got, flat_weight = lax.optimization_barrier((got, flat_weight))
+    squares = ordered(row, squares, got[:rows])
+    codes = ordered(row, codes, got[rows:])
+    got = by_col(jnp.concatenate([squares, gain]), 2)
     near_other, far_other = by_col(near, 1), by_col(far, 1)
-    gain = jnp.where(chip == row, gain, by_chip[rows:]).reshape(2, 1, width)
-    squares = ordered(row, squares + by_chip[:rows], by_row_only[:rows] + by_both)
-    squares = squares.reshape(block, 1)
-    codes = ordered(row, codes, by_row_only[rows:])
+    squares = (squares + got[:block]).reshape(block, 1)
+    gain = jnp.where(chip == row, gain, got[block:]).reshape(2, 1, width)
     doc_rows = jnp.pad(codes, (0, EXTRA * size - block)).reshape(EXTRA, size)
     places = tok * block + jnp.arange(block, dtype=jnp.int32)
     cosine, sine = rotary_tables(places, size)
@@ -367,56 +367,51 @@
     taller = 3 * block + 2 * EXTRA
     break_at = 2 * block + EXTRA
 
-    def projection(kernel, heads, normalising):
+    flat_weight = pltpu.with_memory_space_constraint(flat_weight, pltpu.VMEM)
+
+    def projection(kernel, chunks, normalising):
         normed_shape = (jax.ShapeDtypeStruct((2, block, width), jnp.bfloat16),)
         return pl.pallas_call(
             kernel,
-            out_shape=(jax.ShapeDtypeStruct((taller, size), jnp.float32),) * heads
+            out_shape=(jax.ShapeDtypeStruct((taller, size), jnp.float32),) * chunks
             + (normed_shape if normalising else ()),
-            in_specs=[pl.BlockSpec(memory_space=pltpu.SMEM)]
-            + in_vmem(6 if normalising else 2)
-            + [pl.BlockSpec(memory_space=pltpu.HBM)]
-            + in_vmem(2),
-            out_specs=tuple(in_vmem(heads + 1 if normalising else heads)),
-            scratch_shapes=[
-                pltpu.VMEM((span, heads * triple), jnp.bfloat16),
-                pltpu.SemaphoreType.DMA((2,)),
-            ],
+            in_specs=[pl.BlockSpec(memory_space=pltpu.SMEM)] + in_vmem(9 if normalising else 5),
+            out_specs=tuple(in_vmem(chunks + 1 if normalising else chunks)),
             compiler_params=pltpu.CompilerParams(vmem_limit_bytes=12 * MIB),
             cost_estimate=pl.CostEstimate(flops=0, bytes_accessed=0, transcendentals=0),
         )
 
-    away_head, own_head = (1 - row) * pair, row * pair
+    away_column, own_column = (1 - row) * (pair * triple), row * (pair * triple)
     away, normed = projection(normalise_project_kernel, 1, True)(
-        jnp.stack([core, chip, away_head]), near, far, near_other, far_other, squares, gain,
+        jnp.stack([core, chip, away_column]), near, far, near_other, far_other, squares, gain,
         flat_weight, cosine, sine,
     )
-    arrived = []
-    for head in range(pair):
-        if head > 0:
-            (away,) = projection(project_kernel, 1, False)(
-                (away_head + head).reshape(1), normed, jnp.zeros_like(doc_rows), flat_weight,
-                cosine, sine,
-            )
-        away, normed = lax.optimization_barrier((away.astype(jnp.float16), normed))
-        arrived.append(by_row(away))
-    own = projection(project_kernel, pair, False)(
-        own_head.reshape(1), normed, doc_rows, flat_weight, cosine, sine
+    arrived = [by_row(away.astype(jnp.float16))]
+    (away,) = projection(lambda *refs: project_kernel((1,), *refs), 1, False)(
+        away_column.reshape(1), normed, jnp.zeros_like(doc_rows), flat_weight, cosine, sine
+    )
+    arrived.append(by_row(away.astype(jnp.float16)))
+    own = projection(lambda *refs: project_kernel((0, 1), *refs), 2, False)(
+        own_column.reshape(1), normed, doc_rows, flat_weight, cosine, sine
     )
     scale = 1.0 / math.sqrt(size)
 
-    def along_tok(value, pairs):
-        return lax.ppermute(value, "tok", pairs)
-
-    def summed(head, begin, end):
-        return own[head][begin:end] + arrived[head][begin:end].astype(jnp.float32)
-
-    if toks == 4 and pair == 2:
+    def summed(chunk):
+        return (own[chunk] + arrived[chunk].astype(jnp.float32)).astype(jnp.bfloat16)
+
+    if toks == 4:
         places = jnp.stack([tok, row])
 
-        def returned(value, pairs):
-            across = [(2 * a + r, 2 * b + 1 - r) for a, b in pairs for r in range(2)]
-            return along_tok(value[0], pairs), lax.ppermute(value[1], ("tok", "row"), across)
+        def along_tok(value, targets):
+            return lax.ppermute(value, "tok", list(enumerate(targets)))
+
+        def returned(value, targets):
+            across = [(2 * t + r, 2 * to + 1 - r) for t, to in enumerate(targets) for r in range(2)]
+            return along_tok(value[0], targets), lax.ppermute(value[1], ("tok", "row"), across)
+
+        def keys_or_query(chunk, query_from):
+            begin = jnp.where(tok == query_from, taller - break_at, 0)
+            return lax.dynamic_slice_in_dim(chunk, begin.astype(jnp.uint32), break_at, 0)
 
         def on_place(kernel, out_shape, ins, unused=0):
             return pl.pallas_call(
@@ -436,47 +431,44 @@
             jax.ShapeDtypeStruct((rows, 1), jnp.float32),
         )
 
-        query_down = summed(0, break_at, taller).astype(jnp.bfloat16)
-        keys_down = summed(0, 0, break_at).astype(jnp.bfloat16)
-        from_three = along_tok(query_down, [(3, 1)])
-        from_two = along_tok(query_down, [(2, 1)])
-        one_down = along_tok(keys_down, [(0, 1), (2, 3)])
-
+        chunk_one = summed(0)
+        from_zero = along_tok(keys_or_query(chunk_one, 2), (2, 0, 1, 3))
+        from_one = along_tok(keys_or_query(chunk_one, 3), (0, 2, 3, 1))
+        one_up = along_tok(chunk_one[:break_at], (1, 0, 3, 2))
+        across = by_col(chunk_one[:EXTRA], 1)
         arrived[1] = jnp.where(
             tok < toks,
             arrived[1].astype(jnp.float32),
-            jnp.broadcast_to(from_two[:1].astype(jnp.float32), arrived[1].shape),
-        )
-        keys_up = summed(1, 0, break_at).astype(jnp.bfloat16)
-        query_up = summed(1, break_at, taller).astype(jnp.bfloat16)
-        two_up = along_tok(keys_up, [(0, 2)])
-        three_up = along_tok(query_up, [(3, 2)])
-        one_up = along_tok(keys_up, [(0, 1), (1, 2), (2, 3)])
-
+            jnp.broadcast_to(across[:1].astype(jnp.float32), arrived[1].shape),
+        )
+        chunk_two = summed(1)
+        neighbour = along_tok(keys_or_query(chunk_two, 3), (1, 0, 3, 2))
+
+        mine_up, logs_up, theirs = on_place(
+            lambda *refs: own_up_kernel(scale, *refs),
+            own_shapes + (jax.ShapeDtypeStruct(half_message, jnp.bfloat16),),
+            5,
+        )(places, chunk_two, chunk_one, one_up, from_one, from_zero)
         down = on_place(
             lambda *refs: guests_down_kernel(scale, *refs),
             jax.ShapeDtypeStruct((2, 2) + half_message, jnp.bfloat16),
-            4,
-        )(places, from_two, from_three, one_down, keys_down)
-        three_same, three_cross = returned(down[1], [(1, 3)])
-        mine_down, logs_down, theirs = on_place(
-            lambda *refs: own_kernel(scale, *refs),
-            own_shapes + (jax.ShapeDtypeStruct(half_message, jnp.bfloat16),),
-            3,
-        )(places, query_down, keys_down, one_down)
-        mine_up, logs_up, theirs = on_place(
-            lambda *refs: own_up_kernel(scale, *refs),
-            own_shapes + (jax.ShapeDtypeStruct((2,) + half_message, jnp.bfloat16),),
             5,
-        )(places, query_up, keys_up, one_up, two_up, theirs)
-        partner = by_row(theirs)
+            1,
+        )(places, from_zero, from_one, neighbour, chunk_two, mine_up)
         up = on_place(
             lambda *refs: guests_up_kernel(scale, *refs),
             jax.ShapeDtypeStruct((1, 2) + half_message, jnp.bfloat16),
+            4,
+        )(places, neighbour, from_zero, from_one, down)
+        three_same, three_cross = returned(down[1], (2, 3, 0, 1))
+        next_same, next_cross = returned(up[0], (1, 2, 3, 0))
+        mine_down, logs_down, theirs = on_place(
+            lambda *refs: own_down_kernel(scale, *refs),
+            own_shapes + (jax.ShapeDtypeStruct((2,) + half_message, jnp.bfloat16),),
             5,
             1,
-        )(places, three_up, two_up, one_up, down[:1], mine_up)
-        next_same, next_cross = returned(up[0], [(1, 2), (2, 3)])
+        )(places, chunk_one, chunk_two, neighbour, theirs, up)
+        partner = by_row(theirs)
         return on_place(
             merge_kernel, jax.ShapeDtypeStruct((rows, local_heads * size), jnp.bfloat16), 9
         )(
@@ -484,13 +476,13 @@
             next_same, next_cross,
         )
 
-    sums = jnp.stack([summed(head, 0, taller) for head in range(pair)]).astype(jnp.bfloat16)
-    everything = lax.all_gather(sums[:, : 2 * block], "tok", axis=0, tiled=False)
-    everything = everything.transpose(1, 0, 2, 3)
+    chunks = [summed(0), summed(1)]
+    keys = jnp.stack([chunks[1][: 2 * block], chunks[0][: 2 * block]])
+    everything = lax.all_gather(keys, "tok", axis=0, tiled=False).transpose(1, 0, 2, 3)
     all_codes = lax.all_gather(codes, "tok", axis=0, tiled=True)
     starts = jnp.sum((all_codes[None, :] < codes[:, None]).astype(jnp.int32), axis=1)
     together = attend_gathered(
-        sums[:, break_at : break_at + block],
+        jnp.stack([chunk[break_at : break_at + block] for chunk in chunks]),
         everything[:, :, :block].reshape(pair, toks * block, size),
         everything[:, :, block:].reshape(pair, toks * block, size),
         places, starts, scale,

time: 67.8 us -> 81.7 us (1.21)
  the two profiles are of different devices: /device:TPU:16 before, /device:TPU:0 now
where the time goes in v5:
time: 81.7 us; the launch traced here: 81.1 us
  starting transfers between devices  27 us (33%)
  local copies, waits for them, and re-layouts  19.8 us (24%)
  waiting for transfers between devices  16.1 us (20%)
  Pallas kernels  11.3 us (14%)
  other arithmetic  6.68 us (8%)
    unnamed x29, local copies, waits for them, and re-layouts  19.3 us
    ppermute x6, starting transfers between devices, along_tok(): return lax.ppermute(value, 'tok', list(enumerate(targets)))  13 us
    ppermute x6, waiting for transfers between devices, along_tok(): return lax.ppermute(value, 'tok', list(enumerate(targets)))  6.52 us
    ppermute x1, starting transfers between devices, per_device(): lax.ppermute(activations, ('row', 'col'), [(r * 4 + c, c // 2 * 4 + 2 * (...  4.75 us
    ppermute x2, waiting for transfers between devices, returned(): lax.ppermute(value[1], ('tok', 'row'), across)  4.47 us
    ppermute x2, starting transfers between devices, returned(): lax.ppermute(value[1], ('tok', 'row'), across)  3.7 us
    ppermute x4, waiting for transfers between devices, by_row(): return lax.ppermute(value, 'row', [(0, 1), (1, 0)])  3.5 us
    ppermute x4, starting transfers between devices, by_row(): return lax.ppermute(value, 'row', [(0, 1), (1, 0)])  3.24 us
  transfers between devices with their start and end apart: 19, of which 7 were waited for; matrix products, arithmetic and copies ran while one was open for 16% of the time, Pallas kernels for 6%

profile of v5, /device:TPU:0, one launch (start us, length us, event | category | flops | bytes accessed | tf_op | source)
XLA Modules:
  0.0 81.1 jit_solution(686610811197226708)
XLA Ops:
  0.0 1.6 %collective-permute-start = (bf16[176,1024]{1,0:T(8,128)(2,1)}, bf16[176,1024]{1,0:T(8,128)(2,1)S(1)}, u32[]{:S(2)}, u32[]{:S(2)}) collective-permute-start(bf16[176,1024]{1,0:T(8,128)(2,1)} %param.4), channel_id=1, source_target_pairs={{0,0},{1,1},{2,4},{3,5},{4,2},{5,3},{6,6},{7,7},{8,8},{9,9},{10,12... | collective-permute-start | bytes 1081352 | tf_op jit(solution)/shard_map/ppermute | solution.py:335
  1.6 4.8 %collective-permute-start.1 = (bf16[176,1024]{1,0:T(8,128)(2,1)}, bf16[176,1024]{1,0:T(8,128)(2,1)S(1)}, u32[]{:S(2)}, u32[]{:S(2)}) collective-permute-start(bf16[176,1024]{1,0:T(8,128)(2,1)} %param.4), channel_id=1, source_target_pairs={{0,2},{1,3},{2,6},{3,7},{4,0},{5,1},{6,4},{7,5},{8,10},{9,11},{10,... | collective-permute-start | bytes 1081352 | tf_op jit(solution)/shard_map/ppermute | solution.py:340
  6.4 1.2 %multiply_reduce_fusion = f32[176]{0:T(256)S(1)} fusion(bf16[176,1024]{1,0:T(8,128)(2,1)} %param.4), kind=kLoop, calls=%fused_computation | loop fusion | flops 540496 | bytes 361152 | tf_op jit(solution)/shard_map/reduce_sum | solution.py:346
  7.6 0.7 convert_element_type.52
  8.3 0.7 convert_add_fusion
  9.0 0.7 fusion
  9.7 0.9 %pad_maximum_fusion = (f32[352,128]{1,0:T(8,128)}, f32[352,128]{1,0:T(8,128)}) fusion(f32[352,64]{1,0:T(8,128)S(1)} %get-tuple-element.48, f32[352,64]{1,0:T(8,128)S(1)} %get-tuple-element.47, f32[352,64]{1,0:T(8,128)S(1)} %get-tuple-element.46), kind=kLoop, calls=%fused_computation.5 | loop fusion | flops 90112 | bytes 630784 | tf_op jit(solution)/shard_map/concatenate | solution.py:23
  10.6 6.6 %copy.6 = bf16[256,8,4,384]{3,1,2,0:T(8,128)(2,1)} copy(bf16[256,8,4,384]{3,2,1,0:T(4,128)(2,1)} %bitcast.31) | data formatting | bytes 12582912
  17.5 3.5 %collective-permute-done.5 = f32[352]{0:T(512)S(1)} collective-permute-done((f32[352]{0:T(512)S(1)}, f32[352]{0:T(512)S(1)}, u32[]{:S(2)}, u32[]{:S(2)}) %collective-permute-start.5) | collective-permute-done | bytes 1440 | tf_op jit(solution)/shard_map/ppermute | solution.py:329
  21.3 0.7 copy-done.6
  22.0 0.5 collective-permute-start.3
  22.5 0.7 copy-done.8
  23.2 1.6 %collective-permute-done.6 = f32[2400]{0:T(1024)S(1)} collective-permute-done((f32[2400]{0:T(1024)S(1)}, f32[2400]{0:T(1024)S(1)}, u32[]{:S(2)}, u32[]{:S(2)}) %collective-permute-start.6) | collective-permute-done | bytes 9632 | tf_op jit(solution)/shard_map/ppermute | solution.py:326
  25.1 2.8 %copy-done = bf16[256,8,4,384]{3,1,2,0:T(8,128)(2,1)S(1)} copy-done((bf16[256,8,4,384]{3,1,2,0:T(8,128)(2,1)S(1)}, bf16[256,8,4,384]{3,1,2,0:T(8,128)(2,1)}, u32[]{:S(2)}) %copy-start) | copy-done | bytes 6291480
  27.9 0.9 %copy-done.2 = f32[352,128]{1,0:T(8,128)S(1)} copy-done((f32[352,128]{1,0:T(8,128)S(1)}, f32[352,128]{1,0:T(8,128)}, u32[]{:S(2)}) %copy-start.2) | copy-done | bytes 180248
  28.8 0.9 %copy-done.4 = f32[352,128]{1,0:T(8,128)S(1)} copy-done((f32[352,128]{1,0:T(8,128)S(1)}, f32[352,128]{1,0:T(8,128)}, u32[]{:S(2)}) %copy-start.4) | copy-done | bytes 180248
  29.8 1.0 %copy-done.7 = bf16[176,1024]{1,0:T(8,128)(2,1)S(1)} copy-done((bf16[176,1024]{1,0:T(8,128)(2,1)S(1)}, bf16[176,1024]{1,0:T(8,128)(2,1)}, u32[]{:S(2)}) %copy-start.7) | copy-done | bytes 360472
  30.7 1.0 %copy-done.9 = bf16[176,1024]{1,0:T(8,128)(2,1)S(1)} copy-done((bf16[176,1024]{1,0:T(8,128)(2,1)S(1)}, bf16[176,1024]{1,0:T(8,128)(2,1)}, u32[]{:S(2)}) %copy-start.9) | copy-done | bytes 360472
  31.7 1.9 %shard_map.46 = (f32[1088,128]{1,0:T(8,128)S(1)}, bf16[2,352,1024]{2,1,0:T(8,128)(2,1)S(1)}) custom-call(s32[3]{0:T(128)S(1)} %pad_add_fusion.1.place_ref, bf16[176,1024]{1,0:T(8,128)(2,1)S(1)} %copy-done.7, bf16[176,1024]{1,0:T(8,128)(2,1)S(1)} %copy-done.9, bf16[176,1024]{1,0:T(8,128)(2,1)S(1)} %collective-permute-done.2.b_near, ...), custom_call_target="tpu_custom_call" | custom-call | tf_op jit(solution)/shard_map/pallas_call | solution.py:385
  33.6 0.8 convert_element_type.56
  34.4 0.7 collective-permute-start.7
  35.1 2.8 %copy-done.1 = bf16[256,8,4,384]{3,1,2,0:T(8,128)(2,1)S(1)} copy-done((bf16[256,8,4,384]{3,1,2,0:T(8,128)(2,1)S(1)}, bf16[256,8,4,384]{3,1,2,0:T(8,128)(2,1)}, u32[]{:S(2)}) %copy-start.1) | copy-done | bytes 6291480
  37.9 0.9 %copy-done.3 = f32[352,128]{1,0:T(8,128)S(1)} copy-done((f32[352,128]{1,0:T(8,128)S(1)}, f32[352,128]{1,0:T(8,128)}, u32[]{:S(2)}) %copy-start.3) | copy-done | bytes 180248
  38.8 0.9 %copy-done.5 = f32[352,128]{1,0:T(8,128)S(1)} copy-done((f32[352,128]{1,0:T(8,128)S(1)}, f32[352,128]{1,0:T(8,128)}, u32[]{:S(2)}) %copy-start.5) | copy-done | bytes 180248
  39.8 1.0 %shard_map.48 = f32[1088,128]{1,0:T(8,128)S(1)} custom-call(s32[1]{0:T(128)} %bitcast.5.refs_0_, bf16[2,352,1024]{2,1,0:T(8,128)(2,1)S(1)} %get-tuple-element.23.refs_1_, f32[16,128]{1,0:T(8,128)S(1)} %broadcast_in_dim.15.refs_2_, bf16[2048,1536]{1,0:T(8,128)(2,1)S(1)} %bitcast.27, f32[352,128]{1,0:T(8,128)S(1)} %copy-done.3, f32[352,128]{1,0:T(8,128)S(1)} %copy-done.5), custom_call_target="tpu_custom_call" | custom-call | tf_op jit(solution)/shard_map/pallas_call | solution.py:390
  40.8 1.4 %collective-permute-start.8 = (f16[1088,128]{1,0:T(8,128)(2,1)S(1)}, f16[1088,128]{1,0:T(8,128)(2,1)S(1)}, u32[]{:S(2)}, u32[]{:S(2)}) collective-permute-start(f16[1088,128]{1,0:T(8,128)(2,1)S(1)} %convert_element_type.59), channel_id=1, source_target_pairs={{0,4},{4,0},{1,5},{5,1},{2,6},{6,2},{3,7},{7,3},{8,12},{12,8},{9,1... | collective-permute-start | bytes 835592 | tf_op jit(solution)/shard_map/ppermute | solution.py:329
  42.2 1.7 %shard_map.47 = (f32[1088,128]{1,0:T(8,128)S(1)}, f32[1088,128]{1,0:T(8,128)S(1)}) custom-call(s32[1]{0:T(128)} %bitcast.2.refs_0_, bf16[2,352,1024]{2,1,0:T(8,128)(2,1)S(1)} %get-tuple-element.23.refs_1_, f32[16,128]{1,0:T(8,128)S(1)} %fusion.1.refs_2_, bf16[2048,1536]{1,0:T(8,128)(2,1)S(1)} %bitcast.30, f32[352,128]{1,0:T(8,128)S(1)} %copy-done.3, ...), custom_call_target="tpu_custom_call" | custom-call | tf_op jit(solution)/shard_map/pallas_call | solution.py:394
  44.0 1.0 %add_convert_fusion.1.refs_2_.refs_1_ = bf16[1088,128]{1,0:T(8,128)(2,1)S(1)} fusion(f32[1088,128]{1,0:T(8,128)S(1)} %get-tuple-element.24, f16[1088,128]{1,0:T(8,128)(2,1)} %collective-permute-done.7), kind=kLoop, calls=%fused_computation.2 | loop fusion | flops 417792 | bytes 1114112 | tf_op jit(solution)/shard_map/convert_element_type | solution.py:400
  45.1 0.1 constant_dynamic-slice_fusion
  45.2 1.6 %collective-permute-start.11 = (bf16[720,128]{1,0:T(8,128)(2,1)S(1)}, bf16[720,128]{1,0:T(8,128)(2,1)S(1)}, u32[]{:S(2)}, u32[]{:S(2)}) collective-permute-start(bf16[720,128]{1,0:T(8,128)(2,1)S(1)} %get-tuple-element.35), channel_id=1, source_target_pairs={{0,8},{8,0},{16,24},{24,16},{1,9},{9,1},{17,25},{25,17},{2,10},{10... | collective-permute-start | bytes 552968 | tf_op jit(solution)/shard_map/ppermute | solution.py:406
  46.9 0.7 collective-permute-start.12
  47.5 6.2 %collective-permute-start.13 = (bf16[720,128]{1,0:T(8,128)(2,1)S(1)}, bf16[720,128]{1,0:T(8,128)(2,1)S(1)}, u32[]{:S(2)}, u32[]{:S(2)}) collective-permute-start(bf16[720,128]{1,0:T(8,128)(2,1)S(1)} %get-tuple-element.33), channel_id=1, source_target_pairs={{0,16},{8,0},{16,8},{24,24},{1,17},{9,1},{17,9},{25,25},{2,18},{10... | collective-permute-start | bytes 552968 | tf_op jit(solution)/shard_map/ppermute | solution.py:406
  53.9 0.2 collective-permute-start.10
  54.2 5.1 %collective-permute-done.13.refs_5_.refs_1_.refs_2_ = bf16[720,128]{1,0:T(8,128)(2,1)S(1)} collective-permute-done((bf16[720,128]{1,0:T(8,128)(2,1)S(1)}, bf16[720,128]{1,0:T(8,128)(2,1)S(1)}, u32[]{:S(2)}, u32[]{:S(2)}) %collective-permute-start.13) | collective-permute-done | bytes 184352 | tf_op jit(solution)/shard_map/ppermute | solution.py:406
  59.3 2.1 %shard_map.49 = (f32[176,128]{1,0:T(8,128)S(1)}, f32[176,1]{1,0:T(8,128)S(1)}, bf16[192,128]{1,0:T(8,128)(2,1)S(1)}) custom-call(s32[2]{0:T(128)S(1)} %pad_add_fusion.refs_0_.place_ref, bf16[1088,128]{1,0:T(8,128)(2,1)S(1)} %add_convert_fusion.refs_1_.refs_4_.refs_2_, bf16[1088,128]{1,0:T(8,128)(2,1)S(1)} %add_convert_fusion.1.refs_2_.refs_1_, ...), custom_call_target="tpu_custom_call" | custom-call | tf_op jit(solution)/shard_map/pallas_call | solution.py:447
  61.4 1.1 %collective-permute-done.10.refs_3_.refs_1_ = bf16[720,128]{1,0:T(8,128)(2,1)S(1)} collective-permute-done((bf16[720,128]{1,0:T(8,128)(2,1)S(1)}, bf16[720,128]{1,0:T(8,128)(2,1)S(1)}, u32[]{:S(2)}, u32[]{:S(2)}) %collective-permute-start.10) | collective-permute-done | bytes 184352 | tf_op jit(solution)/shard_map/ppermute | solution.py:406
  62.5 0.5 shard_map.50.refs_4_
  63.1 0.6 shard_map.51.refs_5_
  63.7 1.7 %shard_map.52 = (f32[176,128]{1,0:T(8,128)S(1)}, f32[176,1]{1,0:T(8,128)S(1)}, bf16[2,192,128]{2,1,0:T(8,128)(2,1)S(1)}) custom-call(s32[2]{0:T(128)S(1)} %pad_add_fusion.refs_0_.place_ref, bf16[1088,128]{1,0:T(8,128)(2,1)S(1)} %add_convert_fusion.1.refs_2_.refs_1_, bf16[1088,128]{1,0:T(8,128)(2,1)S(1)} %add_convert_fusion.refs_1_.refs_4_.refs_2_, ...), custom_call_target="tpu_custom_call" | custom-call | tf_op jit(solution)/shard_map/pallas_call | solution.py:465
  65.3 1.2 %collective-permute-start.14 = (bf16[2,192,128]{2,1,0:T(8,128)(2,1)S(1)}, bf16[2,192,128]{2,1,0:T(8,128)(2,1)S(1)}, u32[]{:S(2)}, u32[]{:S(2)}) collective-permute-start(bf16[2,192,128]{2,1,0:T(8,128)(2,1)S(1)} %get-tuple-element.32), channel_id=1, source_target_pairs={{0,4},{4,0},{1,5},{5,1},{2,6},{6,2},{3,7},{7,3},{8,12},{12,8},{9,1... | collective-permute-start | bytes 294920 | tf_op jit(solution)/shard_map/ppermute | solution.py:329
  66.5 4.2 %collective-permute-start.17 = (bf16[192,128]{1,0:T(8,128)(2,1)S(1)}, bf16[192,128]{1,0:T(8,128)(2,1)S(1)}, u32[]{:S(2)}, u32[]{:S(2)}) collective-permute-start(bf16[192,128]{1,0:T(8,128)(2,1)S(1)} %get-tuple-element.39), channel_id=1, source_target_pairs={{0,8},{8,16},{16,24},{24,0},{1,9},{9,17},{17,25},{25,1},{2,10},{10... | collective-permute-start | bytes 147464 | tf_op jit(solution)/shard_map/ppermute | solution.py:406
  70.7 0.4 collective-permute-start.18
  71.1 0.2 collective-permute-start.15
  71.3 3.3 %collective-permute-start.16 = (bf16[192,128]{1,0:T(8,128)(2,1)S(1)}, bf16[192,128]{1,0:T(8,128)(2,1)S(1)}, u32[]{:S(2)}, u32[]{:S(2)}) collective-permute-start(bf16[192,128]{1,0:T(8,128)(2,1)S(1)} %get-tuple-element.36), channel_id=1, source_target_pairs={{0,20},{4,16},{8,28},{12,24},{16,4},{20,0},{24,12},{28,8},{1,21},{... | collective-permute-start | bytes 147464 | tf_op jit(solution)/shard_map/ppermute | solution.py:410
  74.6 2.9 %collective-permute-done.18.next_cross = bf16[192,128]{1,0:T(8,128)(2,1)S(1)} collective-permute-done((bf16[192,128]{1,0:T(8,128)(2,1)S(1)}, bf16[192,128]{1,0:T(8,128)(2,1)S(1)}, u32[]{:S(2)}, u32[]{:S(2)}) %collective-permute-start.18) | collective-permute-done | bytes 49184 | tf_op jit(solution)/shard_map/ppermute | solution.py:410
  77.5 0.3 collective-permute-done.15.three_same
  77.8 1.6 %collective-permute-done.16.three_cross = bf16[192,128]{1,0:T(8,128)(2,1)S(1)} collective-permute-done((bf16[192,128]{1,0:T(8,128)(2,1)S(1)}, bf16[192,128]{1,0:T(8,128)(2,1)S(1)}, u32[]{:S(2)}, u32[]{:S(2)}) %collective-permute-start.16) | collective-permute-done | bytes 49184 | tf_op jit(solution)/shard_map/ppermute | solution.py:410
  79.4 1.8 %shard_map.53 = bf16[176,512]{1,0:T(8,128)(2,1)} custom-call(s32[2]{0:T(128)S(1)} %pad_add_fusion.refs_0_.place_ref, f32[176,128]{1,0:T(8,128)S(1)} %get-tuple-element.29.mine_down, f32[176,1]{1,0:T(8,128)S(1)} %get-tuple-element.30.logs_down, f32[176,128]{1,0:T(8,128)S(1)} %get-tuple-element.28.refs_5_.mine_up, f32[176,1]{1,0:T(8,128)S(1)} %get-tuple-element.31.logs_up, ...), custom_call_target="tpu_custom_call" | custom-call | tf_op jit(solution)/shard_map/pallas_call | solution.py:472
  (59 shorter events, 1.3 us)
Async XLA Ops:
  0.0 21.2 %collective-permute-start = (bf16[176,1024]{1,0:T(8,128)(2,1)}, bf16[176,1024]{1,0:T(8,128)(2,1)S(1)}, u32[]{:S(2)}, u32[]{:S(2)}) collective-permute-start(bf16[176,1024]{1,0:T(8,128)(2,1)} %param.4), channel_id=1, source_target_pairs={{0,0},{1,1},{2,4},{3,5},{4,2},{5,3},{6,6},{7,7},{8,8},{9,9},{10,12... | collective-permute-start | bytes 1081352 | tf_op jit(solution)/shard_map/ppermute | solution.py:335
  1.6 20.4 %collective-permute-start.1 = (bf16[176,1024]{1,0:T(8,128)(2,1)}, bf16[176,1024]{1,0:T(8,128)(2,1)S(1)}, u32[]{:S(2)}, u32[]{:S(2)}) collective-permute-start(bf16[176,1024]{1,0:T(8,128)(2,1)} %param.4), channel_id=1, source_target_pairs={{0,2},{1,3},{2,6},{3,7},{4,0},{5,1},{6,4},{7,5},{8,10},{9,11},{10,... | collective-permute-start | bytes 1081352 | tf_op jit(solution)/shard_map/ppermute | solution.py:340
  8.3 9.0 %collective-permute-start.4 = (f32[1200]{0:T(1024)S(1)}, f32[1200]{0:T(1024)S(1)}, u32[]{:S(2)}, u32[]{:S(2)}) collective-permute-start(f32[1200]{0:T(1024)S(1)} %pad_maximum_fusion.2), channel_id=1, source_target_pairs={{0,1},{1,0},{2,3},{3,2},{4,5},{5,4},{6,7},{7,6},{8,9},{9,8},{10,11... | collective-permute-start | bytes 14408 | tf_op jit(solution)/shard_map/ppermute | solution.py:326
  10.6 6.7 %copy-start.10 = (bf16[1024]{0:T(1024)(128)(2,1)S(1)}, bf16[1024]{0:T(1024)(128)(2,1)}, u32[]{:S(2)}) copy-start(bf16[1024]{0:T(1024)(128)(2,1)} %param.5) | copy-start | bytes 6148
  10.6 10.3 %copy-start.11 = (s32[176]{0:T(256)S(1)}, s32[176]{0:T(256)}, u32[]{:S(2)}) copy-start(s32[176]{0:T(256)} %param.7) | copy-start | bytes 2116
  17.4 3.6 %collective-permute-start.5 = (f32[352]{0:T(512)S(1)}, f32[352]{0:T(512)S(1)}, u32[]{:S(2)}, u32[]{:S(2)}) collective-permute-start(f32[352]{0:T(512)S(1)} %pad_maximum_fusion.3), channel_id=1, source_target_pairs={{0,4},{4,0},{1,5},{5,1},{2,6},{6,2},{3,7},{7,3},{8,12},{12,8},{9,1... | collective-permute-start | bytes 4232 | tf_op jit(solution)/shard_map/ppermute | solution.py:329
  21.1 3.7 %collective-permute-start.6 = (f32[2400]{0:T(1024)S(1)}, f32[2400]{0:T(1024)S(1)}, u32[]{:S(2)}, u32[]{:S(2)}) collective-permute-start(f32[2400]{0:T(1024)S(1)} %concatenate.39), channel_id=1, source_target_pairs={{0,2},{1,3},{2,0},{3,1},{4,6},{5,7},{6,4},{7,5},{8,10},{9,11},{10,... | collective-permute-start | bytes 28808 | tf_op jit(solution)/shard_map/ppermute | solution.py:326
  21.2 3.9 %collective-permute-start.2 = (bf16[176,1024]{1,0:T(8,128)(2,1)S(1)}, bf16[176,1024]{1,0:T(8,128)(2,1)S(1)}, u32[]{:S(2)}, u32[]{:S(2)}) collective-permute-start(bf16[176,1024]{1,0:T(8,128)(2,1)S(1)} %collective-permute-done.a_near), channel_id=1, source_target_pairs={{0,1},{1,0},{2,3},{3,2},{4,5},{5,4},{6,7},{7,6},{8,9},{9,8},{10,11... | collective-permute-start | bytes 1081352 | tf_op jit(solution)/shard_map/ppermute | solution.py:326
  21.2 0.8 copy-start.6
  22.0 3.1 %collective-permute-start.3 = (bf16[176,1024]{1,0:T(8,128)(2,1)S(1)}, bf16[176,1024]{1,0:T(8,128)(2,1)S(1)}, u32[]{:S(2)}, u32[]{:S(2)}) collective-permute-start(bf16[176,1024]{1,0:T(8,128)(2,1)S(1)} %collective-permute-done.1.a_far), channel_id=1, source_target_pairs={{0,1},{1,0},{2,3},{3,2},{4,5},{5,4},{6,7},{7,6},{8,9},{9,8},{10,11... | collective-permute-start | bytes 1081352 | tf_op jit(solution)/shard_map/ppermute | solution.py:326
  22.5 0.7 copy-start.8
  25.1 2.8 %copy-start = (bf16[256,8,4,384]{3,1,2,0:T(8,128)(2,1)S(1)}, bf16[256,8,4,384]{3,1,2,0:T(8,128)(2,1)}, u32[]{:S(2)}) copy-start(bf16[256,8,4,384]{3,1,2,0:T(8,128)(2,1)} %copy.6) | copy-start | bytes 18874372
  27.9 0.9 %copy-start.2 = (f32[352,128]{1,0:T(8,128)S(1)}, f32[352,128]{1,0:T(8,128)}, u32[]{:S(2)}) copy-start(f32[352,128]{1,0:T(8,128)} %get-tuple-element.51.cos_ref.refs_4_) | copy-start | bytes 540676
  28.8 0.9 %copy-start.4 = (f32[352,128]{1,0:T(8,128)S(1)}, f32[352,128]{1,0:T(8,128)}, u32[]{:S(2)}) copy-start(f32[352,128]{1,0:T(8,128)} %get-tuple-element.52.sin_ref.refs_5_) | copy-start | bytes 540676
  29.7 1.0 %copy-start.7 = (bf16[176,1024]{1,0:T(8,128)(2,1)S(1)}, bf16[176,1024]{1,0:T(8,128)(2,1)}, u32[]{:S(2)}) copy-start(bf16[176,1024]{1,0:T(8,128)(2,1)} %copy-done.6) | copy-start | bytes 1081348
  30.7 1.0 %copy-start.9 = (bf16[176,1024]{1,0:T(8,128)(2,1)S(1)}, bf16[176,1024]{1,0:T(8,128)(2,1)}, u32[]{:S(2)}) copy-start(bf16[176,1024]{1,0:T(8,128)(2,1)} %copy-done.8) | copy-start | bytes 1081348
  31.7 10.5 %slice-start = ((s8[6291456]{0:T(1024)(128)(4,1)}), s8[2097152]{0:T(1024)(128)(4,1)S(1)}, s32[]{:S(2)}) async-start(s8[6291456]{0:T(1024)(128)(4,1)} %bitcast.28), calls=%async_computation | async-start | bytes 4194304
  34.4 9.6 %collective-permute-start.7 = (f16[1088,128]{1,0:T(8,128)(2,1)}, f16[1088,128]{1,0:T(8,128)(2,1)}, u32[]{:S(2)}, u32[]{:S(2)}) collective-permute-start(f16[1088,128]{1,0:T(8,128)(2,1)} %convert_element_type.56), channel_id=1, source_target_pairs={{0,4},{4,0},{1,5},{5,1},{2,6},{6,2},{3,7},{7,3},{8,12},{12,8},{9,1... | collective-permute-start | bytes 835592 | tf_op jit(solution)/shard_map/ppermute | solution.py:329
  35.1 2.8 %copy-start.1 = (bf16[256,8,4,384]{3,1,2,0:T(8,128)(2,1)S(1)}, bf16[256,8,4,384]{3,1,2,0:T(8,128)(2,1)}, u32[]{:S(2)}) copy-start(bf16[256,8,4,384]{3,1,2,0:T(8,128)(2,1)} %copy.6) | copy-start | bytes 18874372
  37.9 0.9 %copy-start.3 = (f32[352,128]{1,0:T(8,128)S(1)}, f32[352,128]{1,0:T(8,128)}, u32[]{:S(2)}) copy-start(f32[352,128]{1,0:T(8,128)} %get-tuple-element.51.cos_ref.refs_4_) | copy-start | bytes 540676
  38.8 0.9 %copy-start.5 = (f32[352,128]{1,0:T(8,128)S(1)}, f32[352,128]{1,0:T(8,128)}, u32[]{:S(2)}) copy-start(f32[352,128]{1,0:T(8,128)} %get-tuple-element.52.sin_ref.refs_5_) | copy-start | bytes 540676
  39.8 2.5 %slice-start.1 = ((s8[6291456]{0:T(1024)(128)(4,1)}), s8[4194304]{0:T(1024)(128)(4,1)S(1)}, s32[]{:S(2)}) async-start(s8[6291456]{0:T(1024)(128)(4,1)} %bitcast.28), calls=%async_computation.1 | async-start | bytes 8388608
  40.8 13.0 %collective-permute-start.8 = (f16[1088,128]{1,0:T(8,128)(2,1)S(1)}, f16[1088,128]{1,0:T(8,128)(2,1)S(1)}, u32[]{:S(2)}, u32[]{:S(2)}) collective-permute-start(f16[1088,128]{1,0:T(8,128)(2,1)S(1)} %convert_element_type.59), channel_id=1, source_target_pairs={{0,4},{4,0},{1,5},{5,1},{2,6},{6,2},{3,7},{7,3},{8,12},{12,8},{9,1... | collective-permute-start | bytes 835592 | tf_op jit(solution)/shard_map/ppermute | solution.py:329
  45.0 8.7 %collective-permute-start.9 = (bf16[16,128]{1,0:T(8,128)(2,1)S(1)}, bf16[16,128]{1,0:T(8,128)(2,1)S(1)}, u32[]{:S(2)}, u32[]{:S(2)}) collective-permute-start(bf16[16,128]{1,0:T(8,128)(2,1)S(1)} %slice.66), channel_id=1, source_target_pairs={{0,1},{1,0},{2,3},{3,2},{4,5},{5,4},{6,7},{7,6},{8,9},{9,8},{10,11... | collective-permute-start | bytes 12296 | tf_op jit(solution)/shard_map/ppermute | solution.py:326
  45.2 9.0 %collective-permute-start.11 = (bf16[720,128]{1,0:T(8,128)(2,1)S(1)}, bf16[720,128]{1,0:T(8,128)(2,1)S(1)}, u32[]{:S(2)}, u32[]{:S(2)}) collective-permute-start(bf16[720,128]{1,0:T(8,128)(2,1)S(1)} %get-tuple-element.35), channel_id=1, source_target_pairs={{0,8},{8,0},{16,24},{24,16},{1,9},{9,1},{17,25},{25,17},{2,10},{10... | collective-permute-start | bytes 552968 | tf_op jit(solution)/shard_map/ppermute | solution.py:406
  46.9 7.3 %collective-permute-start.12 = (bf16[720,128]{1,0:T(8,128)(2,1)S(1)}, bf16[720,128]{1,0:T(8,128)(2,1)S(1)}, u32[]{:S(2)}, u32[]{:S(2)}) collective-permute-start(bf16[720,128]{1,0:T(8,128)(2,1)S(1)} %get-tuple-element.34), channel_id=1, source_target_pairs={{0,0},{8,16},{16,24},{24,8},{1,1},{9,17},{17,25},{25,9},{2,2},{10,... | collective-permute-start | bytes 552968 | tf_op jit(solution)/shard_map/ppermute | solution.py:406
  47.5 11.8 %collective-permute-start.13 = (bf16[720,128]{1,0:T(8,128)(2,1)S(1)}, bf16[720,128]{1,0:T(8,128)(2,1)S(1)}, u32[]{:S(2)}, u32[]{:S(2)}) collective-permute-start(bf16[720,128]{1,0:T(8,128)(2,1)S(1)} %get-tuple-element.33), channel_id=1, source_target_pairs={{0,16},{8,0},{16,8},{24,24},{1,17},{9,1},{17,9},{25,25},{2,18},{10... | collective-permute-start | bytes 552968 | tf_op jit(solution)/shard_map/ppermute | solution.py:406
  53.9 8.6 %collective-permute-start.10 = (bf16[720,128]{1,0:T(8,128)(2,1)S(1)}, bf16[720,128]{1,0:T(8,128)(2,1)S(1)}, u32[]{:S(2)}, u32[]{:S(2)}) collective-permute-start(bf16[720,128]{1,0:T(8,128)(2,1)S(1)} %constant_dynamic-slice_fusion.2), channel_id=1, source_target_pairs={{0,8},{8,0},{16,24},{24,16},{1,9},{9,1},{17,25},{25,17},{2,10},{10... | collective-permute-start | bytes 552968 | tf_op jit(solution)/shard_map/ppermute | solution.py:406
  65.3 14.0 %collective-permute-start.14 = (bf16[2,192,128]{2,1,0:T(8,128)(2,1)S(1)}, bf16[2,192,128]{2,1,0:T(8,128)(2,1)S(1)}, u32[]{:S(2)}, u32[]{:S(2)}) collective-permute-start(bf16[2,192,128]{2,1,0:T(8,128)(2,1)S(1)} %get-tuple-element.32), channel_id=1, source_target_pairs={{0,4},{4,0},{1,5},{5,1},{2,6},{6,2},{3,7},{7,3},{8,12},{12,8},{9,1... | collective-permute-start | bytes 294920 | tf_op jit(solution)/shard_map/ppermute | solution.py:329
  66.5 8.1 %collective-permute-start.17 = (bf16[192,128]{1,0:T(8,128)(2,1)S(1)}, bf16[192,128]{1,0:T(8,128)(2,1)S(1)}, u32[]{:S(2)}, u32[]{:S(2)}) collective-permute-start(bf16[192,128]{1,0:T(8,128)(2,1)S(1)} %get-tuple-element.39), channel_id=1, source_target_pairs={{0,8},{8,16},{16,24},{24,0},{1,9},{9,17},{17,25},{25,1},{2,10},{10... | collective-permute-start | bytes 147464 | tf_op jit(solution)/shard_map/ppermute | solution.py:406
  70.7 6.8 %collective-permute-start.18 = (bf16[192,128]{1,0:T(8,128)(2,1)S(1)}, bf16[192,128]{1,0:T(8,128)(2,1)S(1)}, u32[]{:S(2)}, u32[]{:S(2)}) collective-permute-start(bf16[192,128]{1,0:T(8,128)(2,1)S(1)} %get-tuple-element.38), channel_id=1, source_target_pairs={{0,12},{4,8},{8,20},{12,16},{16,28},{20,24},{24,4},{28,0},{1,13},{... | collective-permute-start | bytes 147464 | tf_op jit(solution)/shard_map/ppermute | solution.py:410
  71.1 6.6 %collective-permute-start.15 = (bf16[192,128]{1,0:T(8,128)(2,1)S(1)}, bf16[192,128]{1,0:T(8,128)(2,1)S(1)}, u32[]{:S(2)}, u32[]{:S(2)}) collective-permute-start(bf16[192,128]{1,0:T(8,128)(2,1)S(1)} %get-tuple-element.37), channel_id=1, source_target_pairs={{0,16},{8,24},{16,0},{24,8},{1,17},{9,25},{17,1},{25,9},{2,18},{10... | collective-permute-start | bytes 147464 | tf_op jit(solution)/shard_map/ppermute | solution.py:406
  71.3 8.0 %collective-permute-start.16 = (bf16[192,128]{1,0:T(8,128)(2,1)S(1)}, bf16[192,128]{1,0:T(8,128)(2,1)S(1)}, u32[]{:S(2)}, u32[]{:S(2)}) collective-permute-start(bf16[192,128]{1,0:T(8,128)(2,1)S(1)} %get-tuple-element.36), channel_id=1, source_target_pairs={{0,20},{4,16},{8,28},{12,24},{16,4},{20,0},{24,12},{28,8},{1,21},{... | collective-permute-start | bytes 147464 | tf_op jit(solution)/shard_map/ppermute | solution.py:410

commit v6 on v5

v6 whole, which is shorter than its diff:
```python
import math

import jax
import jax.numpy as jnp
from jax import lax
from jax.experimental import pallas as pl
from jax.experimental.pallas import tpu as pltpu
from jax.sharding import PartitionSpec as P

EPS = 1e-05
LOW = -1e30
EXTRA = 16
MIB = 1 << 20
KEY_COLUMNS = ((4, 2), (1, 2))
QUERY_COLUMNS = ((0, 1), (3, 1))


def rotary_tables(places, head_size):
    half = head_size // 2
    spacing = jnp.arange(half).astype(jnp.float32) * (2.0 / head_size)
    inverse = jnp.power(10000.0, -spacing)
    angles = places.astype(jnp.float32)[:, None] * inverse[None, :]
    cosine, sine = jnp.cos(angles), jnp.sin(angles)
    return (
        jnp.concatenate([cosine, cosine], axis=1),
        jnp.concatenate([-sine, sine], axis=1),
    )


def weight_copies(first_column, chunks, size, weight_hbm, weight_buffer, semaphores):
    copies = []
    for index, chunk in enumerate(chunks):
        for part, (column, width) in enumerate((KEY_COLUMNS[chunk], QUERY_COLUMNS[chunk])):
            source = pl.ds(pl.multiple_of(first_column + column * size, size), width * size)
            target = pl.ds((3 * index + 2 * part) * size, width * size)
            copies.append(
                pltpu.make_async_copy(
                    weight_hbm.at[:, source], weight_buffer.at[:, target], semaphores.at[2 * index + part]
                )
            )
    return copies


def project_chunks(normed_ref, copies, weight_buffer, cos_ref, sin_ref, doc_rows, out_refs):
    block, size = cos_ref.shape
    extra = doc_rows.shape[0]
    depth = weight_buffer.shape[0] // 2

    def product(begin, width):
        at = slice(begin * size, (begin + width) * size)
        return jnp.dot(
            normed_ref[0], weight_buffer[:depth, at], preferred_element_type=jnp.float32
        ) + jnp.dot(normed_ref[1], weight_buffer[depth:, at], preferred_element_type=jnp.float32)

    def rotated(piece):
        return piece * cos_ref[...] + pltpu.roll(piece, size // 2, 1) * sin_ref[...]

    for index, out_ref in enumerate(out_refs):
        copies[2 * index].wait()
        both = product(3 * index, 2)
        out_ref[:block, :] = rotated(both[:, :size])
        out_ref[block : 2 * block, :] = both[:, size:]
        out_ref[2 * block : 2 * block + extra, :] = doc_rows
        copies[2 * index + 1].wait()
        out_ref[2 * block + extra : 3 * block + extra, :] = rotated(product(3 * index + 2, 1))
        out_ref[3 * block + extra :, :] = doc_rows


def normalise_project_kernel(
    place_ref, a_near, a_far, b_near, b_far, squares_ref, gain_ref, cos_ref, sin_ref, weight_hbm,
    out_ref, normed_ref, weight_buffer, semaphores,
):
    rows = a_near.shape[0]
    features = 2 * gain_ref.shape[0] * gain_ref.shape[2]
    core, near_row = place_ref[0], place_ref[1]
    copies = weight_copies(
        place_ref[2], (0,), cos_ref.shape[1], weight_hbm, weight_buffer, semaphores
    )
    for copy in copies:
        copy.start()
    for shards, half in (((a_near, a_far), core), ((b_near, b_far), 1 - core)):
        gain = gain_ref[half]
        for shard, row in zip(shards, (near_row, 1 - near_row)):
            at = pl.ds(pl.multiple_of(row * rows, 16), rows)
            factor = lax.rsqrt(squares_ref[at, :] / features + EPS)
            normed_ref[half, at, :] = (shard[...].astype(jnp.float32) * factor * gain).astype(
                jnp.bfloat16
            )
    nothing = jnp.zeros((EXTRA, out_ref.shape[1]), jnp.float32)
    project_chunks(normed_ref, copies, weight_buffer, cos_ref, sin_ref, nothing, [out_ref])


def project_kernel(chunks, place_ref, normed_ref, docs_ref, cos_ref, sin_ref, weight_hbm, *refs):
    out_refs, (weight_buffer, semaphores) = refs[:-2], refs[-2:]
    copies = weight_copies(
        place_ref[0], chunks, cos_ref.shape[1], weight_hbm, weight_buffer, semaphores
    )
    for copy in copies:
        copy.start()
    project_chunks(
        normed_ref, copies, weight_buffer, cos_ref, sin_ref, docs_ref[...], out_refs
    )


def as_column(rows, count):
    lanes = rows.shape[1]
    pieces = []
    for begin in range(0, count, lanes):
        held = min(lanes, count - begin)
        at = lax.broadcasted_iota(jnp.int32, (held, lanes), 0)
        diagonal = at == lax.broadcasted_iota(jnp.int32, (held, lanes), 1)
        row = rows[begin // lanes : begin // lanes + 1, :]
        pieces.append(jnp.sum(jnp.where(diagonal, row, 0.0), axis=1, keepdims=True))
    return jnp.concatenate(pieces, axis=0)


def as_rows(column, lanes):
    count = column.shape[0]
    rows = []
    for begin in range(0, count, lanes):
        held = min(lanes, count - begin)
        at = lax.broadcasted_iota(jnp.int32, (held, lanes), 0)
        diagonal = at == lax.broadcasted_iota(jnp.int32, (held, lanes), 1)
        rows.append(
            jnp.sum(jnp.where(diagonal, column[begin : begin + held], 0.0), axis=0, keepdims=True)
        )
    return rows


def as_lanes(rows, count):
    lanes = rows.shape[1]
    return jnp.concatenate(
        [
            rows[begin // lanes : begin // lanes + 1, : min(lanes, count - begin)]
            for begin in range(0, count, lanes)
        ],
        axis=1,
    )


def softmax_part(scale, query_message, messages, causal):
    valid = [present for message, present in messages]
    messages = [message for message, present in messages]
    query = query_message[:-EXTRA]
    query_docs = as_column(query_message[-EXTRA:].astype(jnp.float32), query.shape[0])
    block = (messages[0].shape[0] - EXTRA) // 2
    keys = jnp.concatenate([message[:block] for message in messages], axis=0)
    values = jnp.concatenate([message[block : 2 * block] for message in messages], axis=0)
    key_docs = jnp.concatenate(
        [
            jnp.where(present, as_lanes(message[2 * block :].astype(jnp.float32), block), 0.0)
            for message, present in zip(messages, valid)
        ],
        axis=1,
    )
    visible = query_docs == key_docs
    if causal:
        shape = (query.shape[0], keys.shape[0])
        query_places = lax.broadcasted_iota(jnp.int32, shape, 0)
        key_places = lax.broadcasted_iota(jnp.int32, shape, 1)
        visible &= (key_places <= query_places) | (key_places >= block)
    scores = (
        lax.dot_general(query, keys, (((1,), (1,)), ((), ())), preferred_element_type=jnp.float32)
        * scale
    )
    top = jnp.max(jnp.where(visible, scores, LOW), axis=1, keepdims=True)
    exponentials = jnp.where(visible, jnp.exp(scores - top), 0.0)
    total = jnp.sum(exponentials, axis=1, keepdims=True)
    summed = jnp.dot(exponentials.astype(jnp.bfloat16), values, preferred_element_type=jnp.float32)
    some = total > 0.0
    safe = jnp.where(some, total, 1.0)
    return summed / safe, jnp.where(some, top + jnp.log(safe), LOW)


def as_message(output, logs, size):
    along = jnp.concatenate(as_rows(logs, size), axis=0)
    high = along.astype(jnp.bfloat16).astype(jnp.float32)
    middle = (along - high).astype(jnp.bfloat16).astype(jnp.float32)
    pieces = [output, high, middle, along - high - middle]
    pieces.append(jnp.zeros((EXTRA - 3 * along.shape[0], size), jnp.float32))
    return jnp.concatenate(pieces, axis=0).astype(jnp.bfloat16)


def logs_of(message, rows):
    tile = message[rows:].astype(jnp.float32)
    groups = pl.cdiv(rows, tile.shape[1])
    return as_column(sum(tile[k * groups : (k + 1) * groups] for k in range(3)), rows)


def parted(row, value):
    rows = value.shape[0] // 2
    first = row == 0
    return (
        jnp.where(first, value[:rows], value[rows:]),
        jnp.where(first, value[rows:], value[:rows]),
    )


def guest_kernel(
    scale, place_ref, one_ref, two_ref, first_ref, own_chunk, out_ref
):
    height = first_ref.shape[0]
    size = first_ref.shape[1]
    begin = (height - EXTRA) // 2

    def attend(index, query, messages):
        output, logs = softmax_part(scale, query, [(m, True) for m in messages], False)
        out_ref[index] = as_message(output, logs, size)

    @pl.when(place_ref[0] == 1)
    def down():
        keys = [first_ref[...], own_chunk[:height, :]]
        attend(0, two_ref[begin:, :], keys)
        attend(1, one_ref[begin:, :], keys)

    @pl.when(place_ref[0] == 2)
    def up():
        attend(0, first_ref[begin:, :], [one_ref[...], two_ref[...]])


def own_kernel(
    scale, place_ref, chunk_one, chunk_two, from_two_away, swapped, neighbour, one_up, unused_ref,
    out_ref, logs_ref,
):
    tok = place_ref[0]
    height = neighbour.shape[0]
    odd = (tok == 1) | (tok == 3)
    down = [(chunk_two[:height, :], True), (neighbour[...], odd)]
    up = [
        (chunk_one[:height, :], True),
        (jnp.where(tok == 2, swapped[...], one_up[...]), tok > 0),
        (from_two_away[...], tok == 2),
    ]
    for index, (query, messages) in enumerate(
        ((chunk_one[height:, :], down), (chunk_two[height:, :], up))
    ):
        out_ref[index], logs_ref[index] = softmax_part(scale, query, messages, True)


def merge_kernel(place_ref, out_ref, logs_ref, next_ref, three_ref, mine_ref, theirs_ref):
    block, size = out_ref.shape[1:]
    tok, row = place_ref[0], place_ref[1]
    at_two, at_three = tok == 2, tok == 3

    def joined(index, message, present):
        logs = logs_ref[index]
        guest = jnp.where(present, logs_of(message, block), LOW)
        top = jnp.maximum(logs, guest)
        weight, guest_weight = jnp.exp(logs - top), jnp.exp(guest - top)
        guest_output = jnp.where(present, message[:block].astype(jnp.float32), 0.0)
        output = out_ref[index] * weight + guest_output * guest_weight
        return (output / (weight + guest_weight)).astype(jnp.bfloat16)

    down = joined(0, jnp.where(at_two, next_ref[...], three_ref[...]), at_two | at_three)
    up = joined(1, next_ref[...], at_three)
    for index, output in enumerate((down, up)):
        columns = slice(index * size, (index + 1) * size)
        mine_ref[:, columns], theirs_ref[:, columns] = parted(row, output)


def attend_gathered(query, keys, values, places, starts, scale):
    heads, count, size = query.shape
    chunk = math.gcd(keys.shape[1], 1024)
    rounds = keys.shape[1] // chunk
    stacked = (
        keys.reshape(heads, rounds, chunk, size).transpose(1, 0, 2, 3),
        values.reshape(heads, rounds, chunk, size).transpose(1, 0, 2, 3),
        jnp.arange(rounds * chunk, dtype=jnp.int32).reshape(rounds, chunk),
    )

    def advance(state, blocks):
        running, totals, summed = state
        block_keys, block_values, key_places = blocks
        scores = (
            jnp.einsum("hqd,hkd->hqk", query, block_keys, preferred_element_type=jnp.float32) * scale
        )
        visible = (key_places[None, None, :] <= places[None, :, None]) & (
            key_places[None, None, :] >= starts[None, :, None]
        )
        masked = jnp.where(visible, scores, -jnp.inf)
        newest = jnp.maximum(running, jnp.max(masked, axis=2))
        factor = jnp.exp(running - newest)
        exponentials = jnp.where(visible, jnp.exp(masked - newest[:, :, None]), 0.0)
        totals = totals * factor + jnp.sum(exponentials, axis=2)
        summed = summed * factor[:, :, None] + jnp.einsum(
            "hqk,hkd->hqd", exponentials.astype(jnp.bfloat16), block_values,
            preferred_element_type=jnp.float32,
        )
        return (newest, totals, summed), None

    initial = (
        jnp.full((heads, count), -1e30, jnp.float32),
        jnp.zeros((heads, count), jnp.float32),
        jnp.zeros((heads, count, size), jnp.float32),
    )
    (running, totals, summed), unused = lax.scan(advance, initial, stacked)
    attended = (summed / totals[:, :, None]).astype(jnp.bfloat16)
    return attended.transpose(1, 0, 2).reshape(count, heads * size)


def in_vmem(count):
    return [pl.BlockSpec(memory_space=pltpu.VMEM)] * count


def per_device(activations, norm_gain, qkv_weight, doc_ids):
    rows, width = activations.shape
    span, local_heads, triple = qkv_weight.shape
    size = triple // 3
    pair = local_heads // 2
    block = 2 * rows
    toks = lax.axis_size("tok")
    tok, row, col = lax.axis_index("tok"), lax.axis_index("row"), lax.axis_index("col")
    chip, core = col >> 1, col & 1
    grid = [(r, c) for r in range(2) for c in range(4)]

    def by_col(value, flip):
        return lax.ppermute(value, "col", [(c, c ^ flip) for c in range(4)])

    def by_row(value):
        return lax.ppermute(value, "row", [(0, 1), (1, 0)])

    def ordered(index, own, other):
        first = index == 0
        return jnp.concatenate([jnp.where(first, own, other), jnp.where(first, other, own)])

    near = lax.ppermute(
        activations,
        ("row", "col"),
        [(r * 4 + c, (c // 2) * 4 + 2 * r + c % 2) for r, c in grid],
    )
    far = lax.ppermute(
        activations,
        ("row", "col"),
        [(r * 4 + c, (c // 2) * 4 + 2 * (1 - r) + c % 2) for r, c in grid],
    )
    widened = activations.astype(jnp.float32)
    squares = jnp.sum(widened * widened, axis=1)
    gain = norm_gain.astype(jnp.float32)
    message = jnp.concatenate([squares, gain])
    message, qkv_weight = lax.optimization_barrier((message, qkv_weight))
    flat_weight = qkv_weight.reshape(span, local_heads * triple)
    got = by_col(message, 1)
    squares = squares + got[:rows]
    gain = ordered(core, gain, got[rows:])
    got = by_col(jnp.concatenate([squares, gain]), 2)
    near, far, got, flat_weight = lax.optimization_barrier((near, far, got, flat_weight))
    near_other, far_other = by_col(near, 1), by_col(far, 1)
    squares = squares + got[:rows]
    gain = jnp.where(chip == row, gain, got[rows:]).reshape(2, 1, width)
    codes = doc_ids.astype(jnp.float32) + 1.0
    got = by_row(jnp.concatenate([squares, codes]))
    squares = ordered(row, squares, got[:rows]).reshape(block, 1)
    codes = ordered(row, codes, got[rows:])
    doc_rows = jnp.pad(codes, (0, EXTRA * size - block)).reshape(EXTRA, size)
    places = tok * block + jnp.arange(block, dtype=jnp.int32)
    cosine, sine = rotary_tables(places, size)

    taller = 3 * block + 2 * EXTRA
    break_at = 2 * block + EXTRA

    def projection(kernel, chunks, normalising):
        normed_shape = (jax.ShapeDtypeStruct((2, block, width), jnp.bfloat16),)
        return pl.pallas_call(
            kernel,
            out_shape=(jax.ShapeDtypeStruct((taller, size), jnp.float32),) * chunks
            + (normed_shape if normalising else ()),
            in_specs=[pl.BlockSpec(memory_space=pltpu.SMEM)]
            + in_vmem(8 if normalising else 4)
            + [pl.BlockSpec(memory_space=pltpu.HBM)],
            out_specs=tuple(in_vmem(chunks + 1 if normalising else chunks)),
            scratch_shapes=[
                pltpu.VMEM((span, chunks * triple), jnp.bfloat16),
                pltpu.SemaphoreType.DMA((2 * chunks,)),
            ],
            compiler_params=pltpu.CompilerParams(vmem_limit_bytes=6 * MIB),
            cost_estimate=pl.CostEstimate(flops=0, bytes_accessed=0, transcendentals=0),
        )

    away_column, own_column = (1 - row) * (pair * triple), row * (pair * triple)
    away, normed = projection(normalise_project_kernel, 1, True)(
        jnp.stack([core, chip, away_column]), near, far, near_other, far_other, squares, gain,
        cosine, sine, flat_weight,
    )
    arrived = [by_row(away.astype(jnp.float16))]
    (away,) = projection(lambda *refs: project_kernel((1,), *refs), 1, False)(
        away_column.reshape(1), normed, jnp.zeros_like(doc_rows), cosine, sine, flat_weight
    )
    arrived.append(by_row(away.astype(jnp.float16)))
    own = projection(lambda *refs: project_kernel((0, 1), *refs), 2, False)(
        own_column.reshape(1), normed, doc_rows, cosine, sine, flat_weight
    )
    scale = 1.0 / math.sqrt(size)

    def summed(chunk):
        return (own[chunk] + arrived[chunk].astype(jnp.float32)).astype(jnp.bfloat16)

    def gathered_attention():
        chunks = [summed(0), summed(1)]
        keys = jnp.stack([chunks[1][: 2 * block], chunks[0][: 2 * block]])
        everything = lax.all_gather(keys, "tok", axis=0, tiled=False).transpose(1, 0, 2, 3)
        all_codes = lax.all_gather(codes, "tok", axis=0, tiled=True)
        starts = jnp.sum((all_codes[None, :] < codes[:, None]).astype(jnp.int32), axis=1)
        together = attend_gathered(
            jnp.stack([chunk[break_at : break_at + block] for chunk in chunks]),
            everything[:, :, :block].reshape(pair, toks * block, size),
            everything[:, :, block:].reshape(pair, toks * block, size),
            places, starts, scale,
        )
        return parted(row, together)

    if toks == 4:
        places = jnp.stack([tok, row])

        def along_tok(value, pairs):
            return lax.ppermute(value, "tok", pairs)

        def keys_or_query(chunk, query_from):
            begin = jnp.where(tok == query_from, taller - break_at, 0)
            return lax.dynamic_slice_in_dim(chunk, begin.astype(jnp.uint32), break_at, 0)

        def on_place(kernel, out_shape, ins, unused=0):
            return pl.pallas_call(
                kernel,
                out_shape=out_shape,
                in_specs=[pl.BlockSpec(memory_space=pltpu.SMEM)]
                + in_vmem(ins - unused)
                + [pl.BlockSpec(memory_space=pl.ANY)] * unused,
                out_specs=jax.tree.map(lambda unused: in_vmem(1)[0], out_shape),
                compiler_params=pltpu.CompilerParams(vmem_limit_bytes=16 * MIB),
                cost_estimate=pl.CostEstimate(flops=0, bytes_accessed=0, transcendentals=0),
            )

        chunk_one = summed(0)
        two_away = along_tok(keys_or_query(chunk_one, 3), [(3, 1), (0, 2)])
        swapped = along_tok(keys_or_query(chunk_one, 2), [(2, 1), (1, 2)])
        across = by_col(chunk_one[:EXTRA], 1)
        arrived[1] = jnp.where(
            tok < toks,
            arrived[1].astype(jnp.float32),
            jnp.broadcast_to(across[:1].astype(jnp.float32), arrived[1].shape),
        )
        chunk_two = summed(1)
        neighbour = along_tok(keys_or_query(chunk_two, 3), [(0, 1), (2, 3), (3, 2)])
        one_up = along_tok(chunk_one[:break_at], [(0, 1), (2, 3)])

        guests = on_place(
            lambda *refs: guest_kernel(scale, *refs),
            jax.ShapeDtypeStruct((2, block + EXTRA, size), jnp.bfloat16),
            4,
        )(places, two_away, swapped, neighbour, chunk_two)
        from_next = along_tok(guests[0], [(1, 2), (2, 3)])
        from_three = along_tok(guests[1], [(1, 3)])
        output, logs = on_place(
            lambda *refs: own_kernel(scale, *refs),
            (
                jax.ShapeDtypeStruct((2, block, size), jnp.float32),
                jax.ShapeDtypeStruct((2, block, 1), jnp.float32),
            ),
            7,
            1,
        )(places, chunk_one, chunk_two, two_away, swapped, neighbour, one_up, guests)
        half = jax.ShapeDtypeStruct((rows, pair * size), jnp.bfloat16)
        mine, theirs = on_place(merge_kernel, (half, half), 4)(
            places, output, logs, from_next, from_three
        )
    else:
        mine, theirs = gathered_attention()

    theirs = by_row(theirs)
    return jnp.concatenate(
        [jnp.where(row == 0, mine, theirs), jnp.where(row == 0, theirs, mine)], axis=1
    )


def solution(mesh):
    placed = (P(("tok", "row"), "col"), P("col"), P("row", "col", None), P(("tok", "row")))
    return jax.shard_map(
        per_device, mesh=mesh, in_specs=placed, out_specs=P(("tok", "row"), "col"), check_vma=False
    )
```

time: 81.7 us -> 66.2 us (0.81)
  the two profiles are of different devices: /device:TPU:0 before, /device:TPU:24 now
where the time goes in v6:
time: 66.2 us; the launch traced here: 65.8 us
  starting transfers between devices  21.2 us (32%)
  waiting for transfers between devices  14.8 us (22%)
  Pallas kernels  13.7 us (21%)
  local copies, waits for them, and re-layouts  10 us (15%)
  other arithmetic  5.67 us (9%)
    ppermute x6, waiting for transfers between devices, along_tok(): return lax.ppermute(value, 'tok', pairs)  10.3 us
    ppermute x6, starting transfers between devices, along_tok(): return lax.ppermute(value, 'tok', pairs)  10.1 us
    unnamed x9, local copies, waits for them, and re-layouts  9.6 us
    ppermute x4, starting transfers between devices, by_row(): return lax.ppermute(value, 'row', [(0, 1), (1, 0)])  5.65 us
    pallas_call x1, Pallas kernels, per_device(): projection(lambda *refs: project_kernel((0, 1), *refs), 2, False)  4.21 us
    ppermute x4, waiting for transfers between devices, by_row(): return lax.ppermute(value, 'row', [(0, 1), (1, 0)])  4.17 us
    ppermute x1, starting transfers between devices, per_device(): lax.ppermute(activations, ('row', 'col'), [(r * 4 + c, c // 2 * 4 + 2 * (...  3.31 us
    pallas_call x1, Pallas kernels, per_device(): projection(normalise_project_kernel, 1, True)  3.06 us
  transfers between devices with their start and end apart: 17, of which 7 were waited for; matrix products, arithmetic and copies ran while one was open for 14% of the time, Pallas kernels for 15%

profile of v6, /device:TPU:24, one launch (start us, length us, event | category | flops | bytes accessed | tf_op | source)
XLA Modules:
  0.0 65.8 jit_solution(9919904606426770186)
XLA Ops:
  0.0 1.6 %collective-permute-start = (bf16[176,1024]{1,0:T(8,128)(2,1)}, bf16[176,1024]{1,0:T(8,128)(2,1)S(1)}, u32[]{:S(2)}, u32[]{:S(2)}) collective-permute-start(bf16[176,1024]{1,0:T(8,128)(2,1)} %param.4), channel_id=1, source_target_pairs={{0,0},{1,1},{2,4},{3,5},{4,2},{5,3},{6,6},{7,7},{8,8},{9,9},{10,12... | collective-permute-start | bytes 1081352 | tf_op jit(solution)/shard_map/ppermute | solution.py:326
  1.6 3.3 %collective-permute-start.1 = (bf16[176,1024]{1,0:T(8,128)(2,1)}, bf16[176,1024]{1,0:T(8,128)(2,1)S(1)}, u32[]{:S(2)}, u32[]{:S(2)}) collective-permute-start(bf16[176,1024]{1,0:T(8,128)(2,1)} %param.4), channel_id=1, source_target_pairs={{0,2},{1,3},{2,6},{3,7},{4,0},{5,1},{6,4},{7,5},{8,10},{9,11},{10,... | collective-permute-start | bytes 1081352 | tf_op jit(solution)/shard_map/ppermute | solution.py:331
  4.9 1.2 %multiply_reduce_fusion = f32[176]{0:T(256)S(1)} fusion(bf16[176,1024]{1,0:T(8,128)(2,1)} %param.4), kind=kLoop, calls=%fused_computation | loop fusion | flops 540496 | bytes 361152 | tf_op jit(solution)/shard_map/reduce_sum | solution.py:337
  6.1 0.7 %convert_element_type.52 = f32[1024]{0:T(1024)S(1)} convert(bf16[1024]{0:T(1024)(128)(2,1)} %param.5) | non-fusion elementwise | flops 1024 | bytes 6144 | tf_op jit(solution)/shard_map/convert_element_type | solution.py:338
  6.8 0.1 pad_maximum_fusion.3
  6.9 0.7 %convert_add_fusion = f32[176]{0:T(256)S(1)} fusion(s32[176]{0:T(256)} %param.7), kind=kLoop, calls=%fused_computation.27 | loop fusion | flops 352 | bytes 1408 | tf_op jit(solution)/shard_map/add | solution.py:350
  7.6 0.7 %fusion = (f32[352,64]{1,0:T(8,128)S(1)}, f32[352,64]{1,0:T(8,128)S(1)}, f32[352,64]{1,0:T(8,128)S(1)}) fusion(f32[64]{0:T(128)S(1)} %negate_power_fusion, f32[352]{0:T(512)S(1)} %add_convert_fusion.2), kind=kLoop, calls=%fused_computation.12 | loop fusion | flops 45056 | bytes 272000 | tf_op jit(solution)/shard_map/neg | solution.py:26
  8.3 0.2 pad_maximum_fusion
  8.5 0.8 %slice_select_fusion = (f32[1024]{0:T(1024)S(1)}, f32[1024]{0:T(1024)S(1)}) fusion(f32[1200]{0:T(1024)S(1)} %collective-permute-done.2, bf16[1024]{0:T(1024)(128)(2,1)} %param.5, pred[]{:T(512)S(6)} %eq.20), kind=kLoop, calls=%fused_computation.18 | loop fusion | flops 3072 | bytes 14337 | tf_op jit(solution)/shard_map/jit(_where)/select_n | solution.py:324
  9.3 0.1 concatenate.40
  9.4 0.1 pad_add_fusion.1.place_ref
  9.4 4.0 %copy.6 = bf16[256,8,4,384]{3,1,2,0:T(8,128)(2,1)S(1)} copy(bf16[256,8,4,384]{3,2,1,0:T(4,128)(2,1)} %bitcast.25) | data formatting | bytes 12582912
  13.5 0.1 slice.39
  13.6 0.1 pad_maximum_fusion.4
  13.6 2.0 %collective-permute-start.6 = (f32[352]{0:T(512)S(1)}, f32[352]{0:T(512)S(1)}, u32[]{:S(2)}, u32[]{:S(2)}) collective-permute-start(f32[352]{0:T(512)S(1)} %pad_maximum_fusion.4), channel_id=1, source_target_pairs={{0,4},{4,0},{1,5},{5,1},{2,6},{6,2},{3,7},{7,3},{8,12},{12,8},{9,1... | collective-permute-start | bytes 4232 | tf_op jit(solution)/shard_map/ppermute | solution.py:320
  15.6 0.5 collective-permute-start.5
  16.1 1.1 %collective-permute-done.6 = f32[352]{0:T(512)S(1)} collective-permute-done((f32[352]{0:T(512)S(1)}, f32[352]{0:T(512)S(1)}, u32[]{:S(2)}, u32[]{:S(2)}) %collective-permute-start.6) | collective-permute-done | bytes 1440 | tf_op jit(solution)/shard_map/ppermute | solution.py:320
  17.2 0.1 broadcast_select_fusion.4
  17.3 0.1 pad_maximum_fusion.5
  17.4 0.1 reshape.67.squares_ref
  17.5 0.3 collective-permute-done.5.b_far
  17.8 3.1 %shard_map.46 = (f32[1088,128]{1,0:T(8,128)S(1)}, bf16[2,352,1024]{2,1,0:T(8,128)(2,1)S(1)}) custom-call(s32[3]{0:T(128)S(1)} %pad_add_fusion.1.place_ref, bf16[176,1024]{1,0:T(8,128)(2,1)S(1)} %collective-permute-done.a_near, bf16[176,1024]{1,0:T(8,128)(2,1)S(1)} %collective-permute-done.1.a_far, bf16[176,1024]{1,0:T(8,128)(2,1)S(1)} %collective-permute-done.4.b_near, ...), custom_call_target="tpu_custom_call" | custom-call | tf_op jit(solution)/shard_map/pallas_call | solution.py:380
  20.9 2.6 %copy-done = bf16[256,8,4,384]{3,1,2,0:T(8,128)(2,1)} copy-done((bf16[256,8,4,384]{3,1,2,0:T(8,128)(2,1)}, bf16[256,8,4,384]{3,1,2,0:T(8,128)(2,1)S(1)}, u32[]{:S(2)}) %copy-start) | copy-done | bytes 6291480
  23.5 1.7 %collective-permute-start.7 = (f16[1088,128]{1,0:T(8,128)(2,1)S(1)}, f16[1088,128]{1,0:T(8,128)(2,1)S(1)}, u32[]{:S(2)}, u32[]{:S(2)}) collective-permute-start(f16[1088,128]{1,0:T(8,128)(2,1)S(1)} %convert_element_type.56), channel_id=1, source_target_pairs={{0,4},{4,0},{1,5},{5,1},{2,6},{6,2},{3,7},{7,3},{8,12},{12,8},{9,1... | collective-permute-start | bytes 835592 | tf_op jit(solution)/shard_map/ppermute | solution.py:320
  25.3 0.1 fusion.1.refs_2_
  25.3 2.8 %copy-done.1 = bf16[256,8,4,384]{3,1,2,0:T(8,128)(2,1)S(1)} copy-done((bf16[256,8,4,384]{3,1,2,0:T(8,128)(2,1)S(1)}, bf16[256,8,4,384]{3,1,2,0:T(8,128)(2,1)}, u32[]{:S(2)}) %copy-start.1) | copy-done | bytes 6291480
  28.1 2.1 %shard_map.48 = f32[1088,128]{1,0:T(8,128)S(1)} custom-call(s32[1]{0:T(128)} %bitcast.5.refs_0_, bf16[2,352,1024]{2,1,0:T(8,128)(2,1)S(1)} %get-tuple-element.25.refs_1_, f32[16,128]{1,0:T(8,128)S(1)} %broadcast_in_dim.15.refs_2_, f32[352,128]{1,0:T(8,128)S(1)} %get-tuple-element.51.cos_ref.refs_3_, f32[352,128]{1,0:T(8,128)S(1)} %get-tuple-element.52.sin_ref.refs_4_, ...), custom_call_target="tpu_custom_call" | custom-call | tf_op jit(solution)/shard_map/pallas_call | solution.py:385
  30.3 0.4 collective-permute-start.8
  30.7 0.2 copy-done.2
  30.9 4.2 %shard_map.47 = (f32[1088,128]{1,0:T(8,128)S(1)}, f32[1088,128]{1,0:T(8,128)S(1)}) custom-call(s32[1]{0:T(128)} %bitcast.2.refs_0_, bf16[2,352,1024]{2,1,0:T(8,128)(2,1)S(1)} %get-tuple-element.25.refs_1_, f32[16,128]{1,0:T(8,128)S(1)} %fusion.1.refs_2_, f32[352,128]{1,0:T(8,128)S(1)} %get-tuple-element.51.cos_ref.refs_3_, ...), custom_call_target="tpu_custom_call" | custom-call | tf_op jit(solution)/shard_map/pallas_call | solution.py:389
  35.3 0.1 fusion.3
  35.4 2.3 %collective-permute-start.10 = (bf16[720,128]{1,0:T(8,128)(2,1)S(1)}, bf16[720,128]{1,0:T(8,128)(2,1)S(1)}, u32[]{:S(2)}, u32[]{:S(2)}) collective-permute-start(bf16[720,128]{1,0:T(8,128)(2,1)S(1)} %get-tuple-element.35), channel_id=1, source_target_pairs={{24,8},{0,16},{25,9},{1,17},{26,10},{2,18},{27,11},{3,19},{28,12},... | collective-permute-start | bytes 552968 | tf_op jit(solution)/shard_map/ppermute | solution.py:415
  37.7 0.7 %collective-permute-start.11 = (bf16[720,128]{1,0:T(8,128)(2,1)S(1)}, bf16[720,128]{1,0:T(8,128)(2,1)S(1)}, u32[]{:S(2)}, u32[]{:S(2)}) collective-permute-start(bf16[720,128]{1,0:T(8,128)(2,1)S(1)} %get-tuple-element.34), channel_id=1, source_target_pairs={{16,8},{8,16},{17,9},{9,17},{18,10},{10,18},{19,11},{11,19},{20,12... | collective-permute-start | bytes 552968 | tf_op jit(solution)/shard_map/ppermute | solution.py:415
  38.4 0.1 add_convert_fusion.refs_4_.refs_2_
  38.6 3.1 %collective-permute-start.12 = (bf16[720,128]{1,0:T(8,128)(2,1)S(1)}, bf16[720,128]{1,0:T(8,128)(2,1)S(1)}, u32[]{:S(2)}, u32[]{:S(2)}) collective-permute-start(bf16[720,128]{1,0:T(8,128)(2,1)S(1)} %constant_dynamic-slice_fusion), channel_id=1, source_target_pairs={{0,8},{16,24},{24,16},{1,9},{17,25},{25,17},{2,10},{18,26},{26,18}... | collective-permute-start | bytes 552968 | tf_op jit(solution)/shard_map/ppermute | solution.py:415
  41.6 0.1 pad_add_fusion.refs_0_.place_ref
  41.7 1.3 %collective-permute-start.13 = (bf16[720,128]{1,0:T(8,128)(2,1)S(1)}, bf16[720,128]{1,0:T(8,128)(2,1)S(1)}, u32[]{:S(2)}, u32[]{:S(2)}) collective-permute-start(bf16[720,128]{1,0:T(8,128)(2,1)S(1)} %get-tuple-element.33), channel_id=1, source_target_pairs={{0,8},{16,24},{1,9},{17,25},{2,10},{18,26},{3,11},{19,27},{4,12},{... | collective-permute-start | bytes 552968 | tf_op jit(solution)/shard_map/ppermute | solution.py:415
  43.0 4.9 %collective-permute-done.12.refs_3_.refs_5_ = bf16[720,128]{1,0:T(8,128)(2,1)S(1)} collective-permute-done((bf16[720,128]{1,0:T(8,128)(2,1)S(1)}, bf16[720,128]{1,0:T(8,128)(2,1)S(1)}, u32[]{:S(2)}, u32[]{:S(2)}) %collective-permute-start.12) | collective-permute-done | bytes 184352 | tf_op jit(solution)/shard_map/ppermute | solution.py:415
  47.9 0.6 shard_map.49.refs_7_
  48.5 1.3 %collective-permute-start.14 = (bf16[368,128]{1,0:T(8,128)(2,1)S(1)}, bf16[368,128]{1,0:T(8,128)(2,1)S(1)}, u32[]{:S(2)}, u32[]{:S(2)}) collective-permute-start(bf16[368,128]{1,0:T(8,128)(2,1)S(1)} %get-tuple-element.37), channel_id=1, source_target_pairs={{8,16},{16,24},{9,17},{17,25},{10,18},{18,26},{11,19},{19,27},{12,... | collective-permute-start | bytes 282632 | tf_op jit(solution)/shard_map/ppermute | solution.py:415
  49.8 1.5 %collective-permute-start.15 = (bf16[368,128]{1,0:T(8,128)(2,1)S(1)}, bf16[368,128]{1,0:T(8,128)(2,1)S(1)}, u32[]{:S(2)}, u32[]{:S(2)}) collective-permute-start(bf16[368,128]{1,0:T(8,128)(2,1)S(1)} %get-tuple-element.36), channel_id=1, source_target_pairs={{8,24},{9,25},{10,26},{11,27},{12,28},{13,29},{14,30},{15,31}} | collective-permute-start | bytes 282632 | tf_op jit(solution)/shard_map/ppermute | solution.py:415
  51.3 2.7 %shard_map.50 = (f32[2,352,128]{2,1,0:T(8,128)S(1)}, f32[2,352,1]{2,1,0:T(8,128)S(1)}) custom-call(s32[2]{0:T(128)S(1)} %pad_add_fusion.refs_0_.place_ref, bf16[1088,128]{1,0:T(8,128)(2,1)S(1)} %add_convert_fusion.1.refs_1_, bf16[1088,128]{1,0:T(8,128)(2,1)S(1)} %add_convert_fusion.refs_4_.refs_2_, ...), custom_call_target="tpu_custom_call" | custom-call | tf_op jit(solution)/shard_map/pallas_call | solution.py:453
  54.0 2.2 %collective-permute-done.14.next_ref = bf16[368,128]{1,0:T(8,128)(2,1)S(1)} collective-permute-done((bf16[368,128]{1,0:T(8,128)(2,1)S(1)}, bf16[368,128]{1,0:T(8,128)(2,1)S(1)}, u32[]{:S(2)}, u32[]{:S(2)}) %collective-permute-start.14) | collective-permute-done | bytes 94240 | tf_op jit(solution)/shard_map/ppermute | solution.py:415
  56.2 3.2 %collective-permute-done.15.three_ref = bf16[368,128]{1,0:T(8,128)(2,1)S(1)} collective-permute-done((bf16[368,128]{1,0:T(8,128)(2,1)S(1)}, bf16[368,128]{1,0:T(8,128)(2,1)S(1)}, u32[]{:S(2)}, u32[]{:S(2)}) %collective-permute-start.15) | collective-permute-done | bytes 94240 | tf_op jit(solution)/shard_map/ppermute | solution.py:415
  59.4 1.1 %shard_map.51 = (bf16[176,256]{1,0:T(8,128)(2,1)S(1)}, bf16[176,256]{1,0:T(8,128)(2,1)S(1)}) custom-call(s32[2]{0:T(128)S(1)} %pad_add_fusion.refs_0_.place_ref, f32[2,352,128]{2,1,0:T(8,128)S(1)} %get-tuple-element.29.out_ref, f32[2,352,1]{2,1,0:T(8,128)S(1)} %get-tuple-element.30.logs_ref, bf16[368,128]{1,0:T(8,128)(2,1)S(1)} %collective-permute-done.14.next_ref, ...), custom_call_target="tpu_custom_call" | custom-call | tf_op jit(solution)/shard_map/pallas_call | solution.py:463
  60.5 1.5 %collective-permute-start.16 = (bf16[176,256]{1,0:T(8,128)(2,1)S(1)}, bf16[176,256]{1,0:T(8,128)(2,1)S(1)}, u32[]{:S(2)}, u32[]{:S(2)}) collective-permute-start(bf16[176,256]{1,0:T(8,128)(2,1)S(1)} %get-tuple-element.32), channel_id=1, source_target_pairs={{0,4},{4,0},{1,5},{5,1},{2,6},{6,2},{3,7},{7,3},{8,12},{12,8},{9,1... | collective-permute-start | bytes 270344 | tf_op jit(solution)/shard_map/ppermute | solution.py:320
  62.0 3.1 %collective-permute-done.16 = bf16[176,256]{1,0:T(8,128)(2,1)S(1)} collective-permute-done((bf16[176,256]{1,0:T(8,128)(2,1)S(1)}, bf16[176,256]{1,0:T(8,128)(2,1)S(1)}, u32[]{:S(2)}, u32[]{:S(2)}) %collective-permute-start.16) | collective-permute-done | bytes 90144 | tf_op jit(solution)/shard_map/ppermute | solution.py:320
  65.1 0.7 %pad_maximum_fusion.2 = bf16[176,512]{1,0:T(8,128)(2,1)} fusion(bf16[176,256]{1,0:T(8,128)(2,1)S(1)} %get-tuple-element.39, bf16[176,256]{1,0:T(8,128)(2,1)S(1)} %get-tuple-element.38), kind=kLoop, calls=%fused_computation.7 | loop fusion | flops 360448 | bytes 360448 | tf_op jit(solution)/shard_map/concatenate | solution.py:470
  (34 shorter events, 0.5 us)
Async XLA Ops:
  0.0 13.5 %collective-permute-start = (bf16[176,1024]{1,0:T(8,128)(2,1)}, bf16[176,1024]{1,0:T(8,128)(2,1)S(1)}, u32[]{:S(2)}, u32[]{:S(2)}) collective-permute-start(bf16[176,1024]{1,0:T(8,128)(2,1)} %param.4), channel_id=1, source_target_pairs={{0,0},{1,1},{2,4},{3,5},{4,2},{5,3},{6,6},{7,7},{8,8},{9,9},{10,12... | collective-permute-start | bytes 1081352 | tf_op jit(solution)/shard_map/ppermute | solution.py:326
  1.6 11.8 %collective-permute-start.1 = (bf16[176,1024]{1,0:T(8,128)(2,1)}, bf16[176,1024]{1,0:T(8,128)(2,1)S(1)}, u32[]{:S(2)}, u32[]{:S(2)}) collective-permute-start(bf16[176,1024]{1,0:T(8,128)(2,1)} %param.4), channel_id=1, source_target_pairs={{0,2},{1,3},{2,6},{3,7},{4,0},{5,1},{6,4},{7,5},{8,10},{9,11},{10,... | collective-permute-start | bytes 1081352 | tf_op jit(solution)/shard_map/ppermute | solution.py:331
  6.9 1.6 %collective-permute-start.2 = (f32[1200]{0:T(1024)S(1)}, f32[1200]{0:T(1024)S(1)}, u32[]{:S(2)}, u32[]{:S(2)}) collective-permute-start(f32[1200]{0:T(1024)S(1)} %pad_maximum_fusion.3), channel_id=1, source_target_pairs={{0,1},{1,0},{2,3},{3,2},{4,5},{5,4},{6,7},{7,6},{8,9},{9,8},{10,11... | collective-permute-start | bytes 14408 | tf_op jit(solution)/shard_map/ppermute | solution.py:317
  9.3 4.1 %collective-permute-start.3 = (f32[2224]{0:T(1024)S(1)}, f32[2224]{0:T(1024)S(1)}, u32[]{:S(2)}, u32[]{:S(2)}) collective-permute-start(f32[2224]{0:T(1024)S(1)} %concatenate.40), channel_id=1, source_target_pairs={{0,2},{1,3},{2,0},{3,1},{4,6},{5,7},{6,4},{7,5},{8,10},{9,11},{10,... | collective-permute-start | bytes 26696 | tf_op jit(solution)/shard_map/ppermute | solution.py:317
  9.4 7.8 %copy-start.3 = (s32[176]{0:T(256)S(1)}, s32[176]{0:T(256)}, u32[]{:S(2)}) copy-start(s32[176]{0:T(256)} %param.7) | copy-start | bytes 2116
  13.6 3.6 %collective-permute-start.6 = (f32[352]{0:T(512)S(1)}, f32[352]{0:T(512)S(1)}, u32[]{:S(2)}, u32[]{:S(2)}) collective-permute-start(f32[352]{0:T(512)S(1)} %pad_maximum_fusion.4), channel_id=1, source_target_pairs={{0,4},{4,0},{1,5},{5,1},{2,6},{6,2},{3,7},{7,3},{8,12},{12,8},{9,1... | collective-permute-start | bytes 4232 | tf_op jit(solution)/shard_map/ppermute | solution.py:320
  15.6 1.9 %collective-permute-start.4 = (bf16[176,1024]{1,0:T(8,128)(2,1)S(1)}, bf16[176,1024]{1,0:T(8,128)(2,1)S(1)}, u32[]{:S(2)}, u32[]{:S(2)}) collective-permute-start(bf16[176,1024]{1,0:T(8,128)(2,1)S(1)} %collective-permute-done.a_near), channel_id=1, source_target_pairs={{0,1},{1,0},{2,3},{3,2},{4,5},{5,4},{6,7},{7,6},{8,9},{9,8},{10,11... | collective-permute-start | bytes 1081352 | tf_op jit(solution)/shard_map/ppermute | solution.py:317
  15.6 2.2 %collective-permute-start.5 = (bf16[176,1024]{1,0:T(8,128)(2,1)S(1)}, bf16[176,1024]{1,0:T(8,128)(2,1)S(1)}, u32[]{:S(2)}, u32[]{:S(2)}) collective-permute-start(bf16[176,1024]{1,0:T(8,128)(2,1)S(1)} %collective-permute-done.1.a_far), channel_id=1, source_target_pairs={{0,1},{1,0},{2,3},{3,2},{4,5},{5,4},{6,7},{7,6},{8,9},{9,8},{10,11... | collective-permute-start | bytes 1081352 | tf_op jit(solution)/shard_map/ppermute | solution.py:317
  20.8 2.6 %copy-start = (bf16[256,8,4,384]{3,1,2,0:T(8,128)(2,1)}, bf16[256,8,4,384]{3,1,2,0:T(8,128)(2,1)S(1)}, u32[]{:S(2)}) copy-start(bf16[256,8,4,384]{3,1,2,0:T(8,128)(2,1)S(1)} %copy.6) | copy-start | bytes 18874372
  23.5 11.6 %collective-permute-start.7 = (f16[1088,128]{1,0:T(8,128)(2,1)S(1)}, f16[1088,128]{1,0:T(8,128)(2,1)S(1)}, u32[]{:S(2)}, u32[]{:S(2)}) collective-permute-start(f16[1088,128]{1,0:T(8,128)(2,1)S(1)} %convert_element_type.56), channel_id=1, source_target_pairs={{0,4},{4,0},{1,5},{5,1},{2,6},{6,2},{3,7},{7,3},{8,12},{12,8},{9,1... | collective-permute-start | bytes 835592 | tf_op jit(solution)/shard_map/ppermute | solution.py:320
  25.3 2.8 %copy-start.1 = (bf16[256,8,4,384]{3,1,2,0:T(8,128)(2,1)S(1)}, bf16[256,8,4,384]{3,1,2,0:T(8,128)(2,1)}, u32[]{:S(2)}) copy-start(bf16[256,8,4,384]{3,1,2,0:T(8,128)(2,1)} %copy-done) | copy-start | bytes 18874372
  28.1 2.8 %copy-start.2 = (bf16[256,8,4,384]{3,1,2,0:T(8,128)(2,1)S(1)}, bf16[256,8,4,384]{3,1,2,0:T(8,128)(2,1)}, u32[]{:S(2)}) copy-start(bf16[256,8,4,384]{3,1,2,0:T(8,128)(2,1)} %copy-done) | copy-start | bytes 18874372
  30.3 8.1 %collective-permute-start.8 = (f16[1088,128]{1,0:T(8,128)(2,1)S(1)}, f16[1088,128]{1,0:T(8,128)(2,1)S(1)}, u32[]{:S(2)}, u32[]{:S(2)}) collective-permute-start(f16[1088,128]{1,0:T(8,128)(2,1)S(1)} %convert_element_type.59), channel_id=1, source_target_pairs={{0,4},{4,0},{1,5},{5,1},{2,6},{6,2},{3,7},{7,3},{8,12},{12,8},{9,1... | collective-permute-start | bytes 835592 | tf_op jit(solution)/shard_map/ppermute | solution.py:320
  35.2 3.1 %collective-permute-start.9 = (bf16[16,128]{1,0:T(8,128)(2,1)S(1)}, bf16[16,128]{1,0:T(8,128)(2,1)S(1)}, u32[]{:S(2)}, u32[]{:S(2)}) collective-permute-start(bf16[16,128]{1,0:T(8,128)(2,1)S(1)} %slice.49), channel_id=1, source_target_pairs={{0,1},{1,0},{2,3},{3,2},{4,5},{5,4},{6,7},{7,6},{8,9},{9,8},{10,11... | collective-permute-start | bytes 12296 | tf_op jit(solution)/shard_map/ppermute | solution.py:317
  35.4 7.6 %collective-permute-start.10 = (bf16[720,128]{1,0:T(8,128)(2,1)S(1)}, bf16[720,128]{1,0:T(8,128)(2,1)S(1)}, u32[]{:S(2)}, u32[]{:S(2)}) collective-permute-start(bf16[720,128]{1,0:T(8,128)(2,1)S(1)} %get-tuple-element.35), channel_id=1, source_target_pairs={{24,8},{0,16},{25,9},{1,17},{26,10},{2,18},{27,11},{3,19},{28,12},... | collective-permute-start | bytes 552968 | tf_op jit(solution)/shard_map/ppermute | solution.py:415
  37.7 5.3 %collective-permute-start.11 = (bf16[720,128]{1,0:T(8,128)(2,1)S(1)}, bf16[720,128]{1,0:T(8,128)(2,1)S(1)}, u32[]{:S(2)}, u32[]{:S(2)}) collective-permute-start(bf16[720,128]{1,0:T(8,128)(2,1)S(1)} %get-tuple-element.34), channel_id=1, source_target_pairs={{16,8},{8,16},{17,9},{9,17},{18,10},{10,18},{19,11},{11,19},{20,12... | collective-permute-start | bytes 552968 | tf_op jit(solution)/shard_map/ppermute | solution.py:415
  38.6 9.4 %collective-permute-start.12 = (bf16[720,128]{1,0:T(8,128)(2,1)S(1)}, bf16[720,128]{1,0:T(8,128)(2,1)S(1)}, u32[]{:S(2)}, u32[]{:S(2)}) collective-permute-start(bf16[720,128]{1,0:T(8,128)(2,1)S(1)} %constant_dynamic-slice_fusion), channel_id=1, source_target_pairs={{0,8},{16,24},{24,16},{1,9},{17,25},{25,17},{2,10},{18,26},{26,18}... | collective-permute-start | bytes 552968 | tf_op jit(solution)/shard_map/ppermute | solution.py:415
  41.7 9.6 %collective-permute-start.13 = (bf16[720,128]{1,0:T(8,128)(2,1)S(1)}, bf16[720,128]{1,0:T(8,128)(2,1)S(1)}, u32[]{:S(2)}, u32[]{:S(2)}) collective-permute-start(bf16[720,128]{1,0:T(8,128)(2,1)S(1)} %get-tuple-element.33), channel_id=1, source_target_pairs={{0,8},{16,24},{1,9},{17,25},{2,10},{18,26},{3,11},{19,27},{4,12},{... | collective-permute-start | bytes 552968 | tf_op jit(solution)/shard_map/ppermute | solution.py:415
  48.5 7.7 %collective-permute-start.14 = (bf16[368,128]{1,0:T(8,128)(2,1)S(1)}, bf16[368,128]{1,0:T(8,128)(2,1)S(1)}, u32[]{:S(2)}, u32[]{:S(2)}) collective-permute-start(bf16[368,128]{1,0:T(8,128)(2,1)S(1)} %get-tuple-element.37), channel_id=1, source_target_pairs={{8,16},{16,24},{9,17},{17,25},{10,18},{18,26},{11,19},{19,27},{12,... | collective-permute-start | bytes 282632 | tf_op jit(solution)/shard_map/ppermute | solution.py:415
  49.8 9.6 %collective-permute-start.15 = (bf16[368,128]{1,0:T(8,128)(2,1)S(1)}, bf16[368,128]{1,0:T(8,128)(2,1)S(1)}, u32[]{:S(2)}, u32[]{:S(2)}) collective-permute-start(bf16[368,128]{1,0:T(8,128)(2,1)S(1)} %get-tuple-element.36), channel_id=1, source_target_pairs={{8,24},{9,25},{10,26},{11,27},{12,28},{13,29},{14,30},{15,31}} | collective-permute-start | bytes 282632 | tf_op jit(solution)/shard_map/ppermute | solution.py:415
  60.5 4.6 %collective-permute-start.16 = (bf16[176,256]{1,0:T(8,128)(2,1)S(1)}, bf16[176,256]{1,0:T(8,128)(2,1)S(1)}, u32[]{:S(2)}, u32[]{:S(2)}) collective-permute-start(bf16[176,256]{1,0:T(8,128)(2,1)S(1)} %get-tuple-element.32), channel_id=1, source_target_pairs={{0,4},{4,0},{1,5},{5,1},{2,6},{6,2},{3,7},{7,3},{8,12},{12,8},{9,1... | collective-permute-start | bytes 270344 | tf_op jit(solution)/shard_map/ppermute | solution.py:320

commit v7 on v6

--- a/solution.py
+++ b/solution.py
@@ -11,8 +11,6 @@
 LOW = -1e30
 EXTRA = 16
 MIB = 1 << 20
-KEY_COLUMNS = ((4, 2), (1, 2))
-QUERY_COLUMNS = ((0, 1), (3, 1))
 
 
 def rotary_tables(places, head_size):
@@ -27,55 +25,45 @@
     )
 
 
-def weight_copies(first_column, chunks, size, weight_hbm, weight_buffer, semaphores):
-    copies = []
-    for index, chunk in enumerate(chunks):
-        for part, (column, width) in enumerate((KEY_COLUMNS[chunk], QUERY_COLUMNS[chunk])):
-            source = pl.ds(pl.multiple_of(first_column + column * size, size), width * size)
-            target = pl.ds((3 * index + 2 * part) * size, width * size)
-            copies.append(
-                pltpu.make_async_copy(
-                    weight_hbm.at[:, source], weight_buffer.at[:, target], semaphores.at[2 * index + part]
-                )
-            )
-    return copies
-
-
-def project_chunks(normed_ref, copies, weight_buffer, cos_ref, sin_ref, doc_rows, out_refs):
+def project_chunk(normed_ref, weight_ref, key_column, query_column, cos_ref, sin_ref, doc_rows, out_ref):
     block, size = cos_ref.shape
     extra = doc_rows.shape[0]
-    depth = weight_buffer.shape[0] // 2
-
-    def product(begin, width):
-        at = slice(begin * size, (begin + width) * size)
+    depth = weight_ref.shape[0] // 2
+
+    def product(column, width):
+        at = pl.ds(column if isinstance(column, int) else pl.multiple_of(column, size), width)
         return jnp.dot(
-            normed_ref[0], weight_buffer[:depth, at], preferred_element_type=jnp.float32
-        ) + jnp.dot(normed_ref[1], weight_buffer[depth:, at], preferred_element_type=jnp.float32)
+            normed_ref[0], weight_ref[:depth, at], preferred_element_type=jnp.float32
+        ) + jnp.dot(normed_ref[1], weight_ref[depth:, at], preferred_element_type=jnp.float32)
 
     def rotated(piece):
         return piece * cos_ref[...] + pltpu.roll(piece, size // 2, 1) * sin_ref[...]
 
-    for index, out_ref in enumerate(out_refs):
-        copies[2 * index].wait()
-        both = product(3 * index, 2)
-        out_ref[:block, :] = rotated(both[:, :size])
-        out_ref[block : 2 * block, :] = both[:, size:]
-        out_ref[2 * block : 2 * block + extra, :] = doc_rows
-        copies[2 * index + 1].wait()
-        out_ref[2 * block + extra : 3 * block + extra, :] = rotated(product(3 * index + 2, 1))
-        out_ref[3 * block + extra :, :] = doc_rows
+    both = product(key_column, 2 * size)
+    out_ref[:block, :] = rotated(both[:, :size])
+    out_ref[block : 2 * block, :] = both[:, size:]
+    out_ref[2 * block : 2 * block + extra, :] = doc_rows
+    out_ref[2 * block + extra : 3 * block + extra, :] = rotated(product(query_column, size))
+    out_ref[3 * block + extra :, :] = doc_rows
 
 
 def normalise_project_kernel(
-    place_ref, a_near, a_far, b_near, b_far, squares_ref, gain_ref, cos_ref, sin_ref, weight_hbm,
-    out_ref, normed_ref, weight_buffer, semaphores,
+    place_ref, a_near, a_far, b_near, b_far, squares_ref, gain_ref, cos_ref, sin_ref, weight_ref,
+    out_ref, normed_ref, rest_hbm, semaphores,
 ):
-    rows = a_near.shape[0]
+    rows, size = a_near.shape[0], cos_ref.shape[1]
     features = 2 * gain_ref.shape[0] * gain_ref.shape[2]
-    core, near_row = place_ref[0], place_ref[1]
-    copies = weight_copies(
-        place_ref[2], (0,), cos_ref.shape[1], weight_hbm, weight_buffer, semaphores
-    )
+    core, near_row, away, own = place_ref[0], place_ref[1], place_ref[2], place_ref[3]
+    copies = [
+        pltpu.make_async_copy(
+            weight_ref.at[:, pl.ds(pl.multiple_of(source, size), width)],
+            rest_hbm.at[:, pl.ds(target, width)],
+            semaphores.at[index],
+        )
+        for index, (source, target, width) in enumerate(
+            ((away + size, 0, 3 * size), (own, 3 * size, 6 * size))
+        )
+    ]
     for copy in copies:
         copy.start()
     for shards, half in (((a_near, a_far), core), ((b_near, b_far), 1 - core)):
@@ -86,20 +74,26 @@
             normed_ref[half, at, :] = (shard[...].astype(jnp.float32) * factor * gain).astype(
                 jnp.bfloat16
             )
-    nothing = jnp.zeros((EXTRA, out_ref.shape[1]), jnp.float32)
-    project_chunks(normed_ref, copies, weight_buffer, cos_ref, sin_ref, nothing, [out_ref])
-
-
-def project_kernel(chunks, place_ref, normed_ref, docs_ref, cos_ref, sin_ref, weight_hbm, *refs):
-    out_refs, (weight_buffer, semaphores) = refs[:-2], refs[-2:]
-    copies = weight_copies(
-        place_ref[0], chunks, cos_ref.shape[1], weight_hbm, weight_buffer, semaphores
+    nothing = jnp.zeros((EXTRA, size), jnp.float32)
+    project_chunk(
+        normed_ref, weight_ref, away + 4 * size, away, cos_ref, sin_ref, nothing, out_ref
     )
     for copy in copies:
-        copy.start()
-    project_chunks(
-        normed_ref, copies, weight_buffer, cos_ref, sin_ref, docs_ref[...], out_refs
-    )
+        copy.wait()
+
+
+def project_kernel(first, columns, normed_ref, docs_ref, cos_ref, sin_ref, rest_hbm, *refs):
+    out_refs, (weight_buffer, semaphore) = refs[:-2], refs[-2:]
+    copy = pltpu.make_async_copy(
+        rest_hbm.at[:, pl.ds(first, weight_buffer.shape[1])], weight_buffer, semaphore
+    )
+    copy.start()
+    copy.wait()
+    for (key_column, query_column), out_ref in zip(columns, out_refs):
+        project_chunk(
+            normed_ref, weight_buffer, key_column, query_column, cos_ref, sin_ref, docs_ref[...],
+            out_ref,
+        )
 
 
 def as_column(rows, count):
@@ -197,40 +191,38 @@
 
 
 def guest_kernel(
-    scale, place_ref, one_ref, two_ref, first_ref, own_chunk, out_ref
+    scale, place_ref, two_away, swapped, neighbour, chunk_one, chunk_two, out_ref
 ):
-    height = first_ref.shape[0]
-    size = first_ref.shape[1]
+    height, size = neighbour.shape
     begin = (height - EXTRA) // 2
 
     def attend(index, query, messages):
         output, logs = softmax_part(scale, query, [(m, True) for m in messages], False)
         out_ref[index] = as_message(output, logs, size)
 
+    @pl.when(place_ref[0] == 0)
+    def one_up():
+        attend(0, neighbour[begin:, :], [chunk_one[:height, :]])
+
     @pl.when(place_ref[0] == 1)
     def down():
-        keys = [first_ref[...], own_chunk[:height, :]]
-        attend(0, two_ref[begin:, :], keys)
-        attend(1, one_ref[begin:, :], keys)
+        keys = [neighbour[...], chunk_two[:height, :]]
+        attend(1, two_away[begin:, :], keys)
+        attend(0, swapped[begin:, :], keys)
 
     @pl.when(place_ref[0] == 2)
-    def up():
-        attend(0, first_ref[begin:, :], [one_ref[...], two_ref[...]])
+    def three_up():
+        attend(0, neighbour[begin:, :], [two_away[...], swapped[...], chunk_one[:height, :]])
 
 
 def own_kernel(
-    scale, place_ref, chunk_one, chunk_two, from_two_away, swapped, neighbour, one_up, unused_ref,
-    out_ref, logs_ref,
+    scale, place_ref, chunk_one, chunk_two, two_away, swapped, neighbour, unused_ref, out_ref,
+    logs_ref,
 ):
     tok = place_ref[0]
     height = neighbour.shape[0]
-    odd = (tok == 1) | (tok == 3)
-    down = [(chunk_two[:height, :], True), (neighbour[...], odd)]
-    up = [
-        (chunk_one[:height, :], True),
-        (jnp.where(tok == 2, swapped[...], one_up[...]), tok > 0),
-        (from_two_away[...], tok == 2),
-    ]
+    down = [(chunk_two[:height, :], True), (neighbour[...], (tok == 1) | (tok == 3))]
+    up = [(chunk_one[:height, :], True), (swapped[...], tok == 2), (two_away[...], tok == 2)]
     for index, (query, messages) in enumerate(
         ((chunk_one[height:, :], down), (chunk_two[height:, :], up))
     ):
@@ -252,7 +244,7 @@
         return (output / (weight + guest_weight)).astype(jnp.bfloat16)
 
     down = joined(0, jnp.where(at_two, next_ref[...], three_ref[...]), at_two | at_three)
-    up = joined(1, next_ref[...], at_three)
+    up = joined(1, next_ref[...], (tok == 1) | at_three)
     for index, output in enumerate((down, up)):
         columns = slice(index * size, (index + 1) * size)
         mine_ref[:, columns], theirs_ref[:, columns] = parted(row, output)
@@ -358,37 +350,46 @@
     taller = 3 * block + 2 * EXTRA
     break_at = 2 * block + EXTRA
 
-    def projection(kernel, chunks, normalising):
-        normed_shape = (jax.ShapeDtypeStruct((2, block, width), jnp.bfloat16),)
+    partial_sums = jax.ShapeDtypeStruct((taller, size), jnp.float32)
+    no_cost = pl.CostEstimate(flops=0, bytes_accessed=0, transcendentals=0)
+    away, normed, rest = pl.pallas_call(
+        normalise_project_kernel,
+        out_shape=(
+            partial_sums,
+            jax.ShapeDtypeStruct((2, block, width), jnp.bfloat16),
+            pltpu.HBM((span, 3 * triple), jnp.bfloat16),
+        ),
+        in_specs=[pl.BlockSpec(memory_space=pltpu.SMEM)] + in_vmem(9),
+        out_specs=tuple(in_vmem(2)) + (pl.BlockSpec(memory_space=pltpu.HBM),),
+        scratch_shapes=[pltpu.SemaphoreType.DMA((2,))],
+        compiler_params=pltpu.CompilerParams(vmem_limit_bytes=12 * MIB),
+        cost_estimate=no_cost,
+    )(
+        jnp.stack([core, chip, (1 - row) * (pair * triple), row * (pair * triple)]),
+        near, far, near_other, far_other, squares, gain, cosine, sine, flat_weight,
+    )
+
+    def projection(first, columns, doc_rows):
+        chunks = len(columns)
         return pl.pallas_call(
-            kernel,
-            out_shape=(jax.ShapeDtypeStruct((taller, size), jnp.float32),) * chunks
-            + (normed_shape if normalising else ()),
-            in_specs=[pl.BlockSpec(memory_space=pltpu.SMEM)]
-            + in_vmem(8 if normalising else 4)
-            + [pl.BlockSpec(memory_space=pltpu.HBM)],
-            out_specs=tuple(in_vmem(chunks + 1 if normalising else chunks)),
+            lambda *refs: project_kernel(first, columns, *refs),
+            out_shape=(partial_sums,) * chunks,
+            in_specs=in_vmem(4) + [pl.BlockSpec(memory_space=pltpu.HBM)],
+            out_specs=tuple(in_vmem(chunks)),
             scratch_shapes=[
                 pltpu.VMEM((span, chunks * triple), jnp.bfloat16),
-                pltpu.SemaphoreType.DMA((2 * chunks,)),
+                pltpu.SemaphoreType.DMA(()),
             ],
-            compiler_params=pltpu.CompilerParams(vmem_limit_bytes=6 * MIB),
-            cost_estimate=pl.CostEstimate(flops=0, bytes_accessed=0, transcendentals=0),
-        )
-
-    away_column, own_column = (1 - row) * (pair * triple), row * (pair * triple)
-    away, normed = projection(normalise_project_kernel, 1, True)(
-        jnp.stack([core, chip, away_column]), near, far, near_other, far_other, squares, gain,
-        cosine, sine, flat_weight,
-    )
+            compiler_params=pltpu.CompilerParams(vmem_limit_bytes=8 * MIB),
+            cost_estimate=no_cost,
+        )(
+            normed, doc_rows, cosine, sine, pltpu.with_memory_space_constraint(rest, pltpu.HBM)
+        )
+
     arrived = [by_row(away.astype(jnp.float16))]
-    (away,) = projection(lambda *refs: project_kernel((1,), *refs), 1, False)(
-        away_column.reshape(1), normed, jnp.zeros_like(doc_rows), cosine, sine, flat_weight
-    )
+    (away,) = projection(0, [(0, 2 * size)], jnp.zeros_like(doc_rows))
     arrived.append(by_row(away.astype(jnp.float16)))
-    own = projection(lambda *refs: project_kernel((0, 1), *refs), 2, False)(
-        own_column.reshape(1), normed, doc_rows, cosine, sine, flat_weight
-    )
+    own = projection(triple, [(4 * size, 0), (size, 3 * size)], doc_rows)
     scale = 1.0 / math.sqrt(size)
 
     def summed(chunk):
@@ -414,8 +415,8 @@
         def along_tok(value, pairs):
             return lax.ppermute(value, "tok", pairs)
 
-        def keys_or_query(chunk, query_from):
-            begin = jnp.where(tok == query_from, taller - break_at, 0)
+        def keys_or_query(chunk, is_query):
+            begin = jnp.where(is_query, taller - break_at, 0)
             return lax.dynamic_slice_in_dim(chunk, begin.astype(jnp.uint32), break_at, 0)
 
         def on_place(kernel, out_shape, ins, unused=0):
@@ -431,8 +432,8 @@
             )
 
         chunk_one = summed(0)
-        two_away = along_tok(keys_or_query(chunk_one, 3), [(3, 1), (0, 2)])
-        swapped = along_tok(keys_or_query(chunk_one, 2), [(2, 1), (1, 2)])
+        two_away = along_tok(keys_or_query(chunk_one, tok == 3), [(3, 1), (0, 2)])
+        swapped = along_tok(keys_or_query(chunk_one, tok == 2), [(2, 1), (1, 2)])
         across = by_col(chunk_one[:EXTRA], 1)
         arrived[1] = jnp.where(
             tok < toks,
@@ -440,25 +441,25 @@
             jnp.broadcast_to(across[:1].astype(jnp.float32), arrived[1].shape),
         )
         chunk_two = summed(1)
-        neighbour = along_tok(keys_or_query(chunk_two, 3), [(0, 1), (2, 3), (3, 2)])
-        one_up = along_tok(chunk_one[:break_at], [(0, 1), (2, 3)])
-
+        neighbour = along_tok(
+            keys_or_query(chunk_two, (tok & 1) == 1), [(0, 1), (1, 0), (2, 3), (3, 2)]
+        )
         guests = on_place(
             lambda *refs: guest_kernel(scale, *refs),
             jax.ShapeDtypeStruct((2, block + EXTRA, size), jnp.bfloat16),
-            4,
-        )(places, two_away, swapped, neighbour, chunk_two)
-        from_next = along_tok(guests[0], [(1, 2), (2, 3)])
+            5,
+        )(places, two_away, swapped, neighbour, chunk_one, chunk_two)
         from_three = along_tok(guests[1], [(1, 3)])
+        from_next = along_tok(guests[0], [(0, 1), (1, 2), (2, 3)])
         output, logs = on_place(
             lambda *refs: own_kernel(scale, *refs),
             (
                 jax.ShapeDtypeStruct((2, block, size), jnp.float32),
                 jax.ShapeDtypeStruct((2, block, 1), jnp.float32),
             ),
-            7,
+            6,
             1,
-        )(places, chunk_one, chunk_two, two_away, swapped, neighbour, one_up, guests)
+        )(places, chunk_one, chunk_two, two_away, swapped, neighbour, guests)
         half = jax.ShapeDtypeStruct((rows, pair * size), jnp.bfloat16)
         mine, theirs = on_place(merge_kernel, (half, half), 4)(
             places, output, logs, from_next, from_three

time: 66.2 us -> 63.3 us (0.956)
  local copies, waits for them, and re-layouts: 10 us -> 4.41 us
  waiting for transfers between devices: 14.8 us -> 20 us
  starting transfers between devices: 21.2 us -> 17.7 us
  Pallas kernels: 13.7 us -> 14.4 us
    unnamed x9 -> x3, local copies, waits for them, and re-layouts: 9.6 us -> 3.97 us
    ppermute x6 -> x5, starting transfers between devices: 10.1 us -> 6.2 us  [along_tok(): return lax.ppermute(value, 'tok', pairs)]
    ppermute x4, waiting for transfers between devices: 4.17 us -> 6.98 us  [by_row(): return lax.ppermute(value, 'row', [(0, 1), (1, 0)])]
    ppermute x6 -> x5, waiting for transfers between devices: 10.3 us -> 12.7 us  [along_tok(): return lax.ppermute(value, 'tok', pairs)]
    pallas_call x3, Pallas kernels: 9.37 us -> 10.1 us  [the longest x2 6.07 us: projection(): pl.pallas_call(lambda *refs: project_kernel(first, columns, *refs), out_s...]
  transfers between devices with their start and end apart: 17 -> 16, of which waited for: 7 -> 10; matrix products, arithmetic and copies ran while one was open for 14% -> 15% of each run, Pallas kernels for 15% -> 14%
where the time goes in v7:
time: 63.3 us; the launch traced here: 62.5 us
  waiting for transfers between devices  20 us (32%)
  starting transfers between devices  17.7 us (28%)
  Pallas kernels  14.4 us (23%)
  other arithmetic  5.66 us (9%)
  local copies, waits for them, and re-layouts  4.41 us (7%)
    ppermute x5, waiting for transfers between devices, along_tok(): return lax.ppermute(value, 'tok', pairs)  12.7 us
    ppermute x4, waiting for transfers between devices, by_row(): return lax.ppermute(value, 'row', [(0, 1), (1, 0)])  6.98 us
    ppermute x5, starting transfers between devices, along_tok(): return lax.ppermute(value, 'tok', pairs)  6.2 us
    pallas_call x2, Pallas kernels, projection(): pl.pallas_call(lambda *refs: project_kernel(first, columns, *refs), out_s...  6.07 us
    ppermute x4, starting transfers between devices, by_row(): return lax.ppermute(value, 'row', [(0, 1), (1, 0)])  5.95 us
    pallas_call x1, Pallas kernels, per_device(): pl.pallas_call(normalise_project_kernel, out_shape=(partial_sums, jax.Sha...  4.05 us
    unnamed x3, local copies, waits for them, and re-layouts  3.97 us
    ppermute x1, starting transfers between devices, per_device(): lax.ppermute(activations, ('row', 'col'), [(r * 4 + c, c // 2 * 4 + 2 * (...  3.31 us
  transfers between devices with their start and end apart: 16, of which 10 were waited for; matrix products, arithmetic and copies ran while one was open for 15% of the time, Pallas kernels for 14%

profile of v7, /device:TPU:24, one launch (start us, length us, event | category | flops | bytes accessed | tf_op | source)
XLA Modules:
  0.0 62.5 jit_solution(2814236420216891496)
XLA Ops:
  0.0 1.6 %collective-permute-start = (bf16[176,1024]{1,0:T(8,128)(2,1)}, bf16[176,1024]{1,0:T(8,128)(2,1)S(1)}, u32[]{:S(2)}, u32[]{:S(2)}) collective-permute-start(bf16[176,1024]{1,0:T(8,128)(2,1)} %param.4), channel_id=1, source_target_pairs={{0,0},{1,1},{2,4},{3,5},{4,2},{5,3},{6,6},{7,7},{8,8},{9,9},{10,12... | collective-permute-start | bytes 1081352 | tf_op jit(solution)/shard_map/ppermute | solution.py:318
  1.6 3.3 %collective-permute-start.1 = (bf16[176,1024]{1,0:T(8,128)(2,1)}, bf16[176,1024]{1,0:T(8,128)(2,1)S(1)}, u32[]{:S(2)}, u32[]{:S(2)}) collective-permute-start(bf16[176,1024]{1,0:T(8,128)(2,1)} %param.4), channel_id=1, source_target_pairs={{0,2},{1,3},{2,6},{3,7},{4,0},{5,1},{6,4},{7,5},{8,10},{9,11},{10,... | collective-permute-start | bytes 1081352 | tf_op jit(solution)/shard_map/ppermute | solution.py:323
  4.9 1.2 %multiply_reduce_fusion = f32[176]{0:T(256)S(1)} fusion(bf16[176,1024]{1,0:T(8,128)(2,1)} %param.4), kind=kLoop, calls=%fused_computation | loop fusion | flops 540496 | bytes 361152 | tf_op jit(solution)/shard_map/reduce_sum | solution.py:329
  6.1 0.7 %convert_element_type.54 = f32[1024]{0:T(1024)S(1)} convert(bf16[1024]{0:T(1024)(128)(2,1)} %param.5) | non-fusion elementwise | flops 1024 | bytes 6144 | tf_op jit(solution)/shard_map/convert_element_type | solution.py:330
  6.8 0.1 pad_maximum_fusion.3
  6.9 0.7 %convert_add_fusion = f32[176]{0:T(256)S(1)} fusion(s32[176]{0:T(256)} %param.7), kind=kLoop, calls=%fused_computation.27 | loop fusion | flops 352 | bytes 1408 | tf_op jit(solution)/shard_map/add | solution.py:342
  7.6 0.7 %fusion = (f32[352,64]{1,0:T(8,128)S(1)}, f32[352,64]{1,0:T(8,128)S(1)}, f32[352,64]{1,0:T(8,128)S(1)}) fusion(f32[64]{0:T(128)S(1)} %negate_power_fusion, f32[352]{0:T(512)S(1)} %add_convert_fusion.2), kind=kLoop, calls=%fused_computation.12 | loop fusion | flops 45056 | bytes 272000 | tf_op jit(solution)/shard_map/neg | solution.py:24
  8.3 0.2 pad_maximum_fusion
  8.5 0.8 %slice_select_fusion = (f32[1024]{0:T(1024)S(1)}, f32[1024]{0:T(1024)S(1)}) fusion(f32[1200]{0:T(1024)S(1)} %collective-permute-done.2, bf16[1024]{0:T(1024)(128)(2,1)} %param.5, pred[]{:T(512)S(6)} %eq.22), kind=kLoop, calls=%fused_computation.18 | loop fusion | flops 3072 | bytes 14337 | tf_op jit(solution)/shard_map/jit(_where)/select_n | solution.py:316
  9.3 0.1 concatenate.40
  9.4 0.1 pad_add_fusion.1.place_ref
  9.4 4.0 %copy.6 = bf16[256,8,4,384]{3,1,2,0:T(8,128)(2,1)S(1)} copy(bf16[256,8,4,384]{3,2,1,0:T(4,128)(2,1)} %bitcast.23) | data formatting | bytes 12582912
  13.5 0.1 slice.36
  13.6 0.1 pad_maximum_fusion.4
  13.6 2.0 %collective-permute-start.6 = (f32[352]{0:T(512)S(1)}, f32[352]{0:T(512)S(1)}, u32[]{:S(2)}, u32[]{:S(2)}) collective-permute-start(f32[352]{0:T(512)S(1)} %pad_maximum_fusion.4), channel_id=1, source_target_pairs={{0,4},{4,0},{1,5},{5,1},{2,6},{6,2},{3,7},{7,3},{8,12},{12,8},{9,1... | collective-permute-start | bytes 4232 | tf_op jit(solution)/shard_map/ppermute | solution.py:312
  15.6 0.5 collective-permute-start.5
  16.1 1.1 %collective-permute-done.6 = f32[352]{0:T(512)S(1)} collective-permute-done((f32[352]{0:T(512)S(1)}, f32[352]{0:T(512)S(1)}, u32[]{:S(2)}, u32[]{:S(2)}) %collective-permute-start.6) | collective-permute-done | bytes 1440 | tf_op jit(solution)/shard_map/ppermute | solution.py:312
  17.2 0.1 broadcast_select_fusion.4
  17.3 0.1 pad_maximum_fusion.5
  17.4 0.1 reshape.62.squares_ref
  17.5 0.3 collective-permute-done.5.b_far
  17.8 4.1 %shard_map.46 = (f32[1088,128]{1,0:T(8,128)S(1)}, bf16[2,352,1024]{2,1,0:T(8,128)(2,1)S(1)}, bf16[2048,1152]{1,0:T(8,128)(2,1)}) custom-call(s32[4]{0:T(128)S(1)} %pad_add_fusion.1.place_ref, bf16[176,1024]{1,0:T(8,128)(2,1)S(1)} %collective-permute-done.a_near, bf16[176,1024]{1,0:T(8,128)(2,1)S(1)} %collective-permute-done.1.a_far, ...), custom_call_target="tpu_custom_call" | custom-call | tf_op jit(solution)/shard_map/pallas_call | solution.py:355
  21.9 1.8 %collective-permute-start.7 = (f16[1088,128]{1,0:T(8,128)(2,1)S(1)}, f16[1088,128]{1,0:T(8,128)(2,1)S(1)}, u32[]{:S(2)}, u32[]{:S(2)}) collective-permute-start(f16[1088,128]{1,0:T(8,128)(2,1)S(1)} %convert_element_type.58), channel_id=1, source_target_pairs={{0,4},{4,0},{1,5},{5,1},{2,6},{6,2},{3,7},{7,3},{8,12},{12,8},{9,1... | collective-permute-start | bytes 835592 | tf_op jit(solution)/shard_map/ppermute | solution.py:312
  23.6 0.1 fusion.1.refs_1_
  23.7 2.4 %shard_map.48 = f32[1088,128]{1,0:T(8,128)S(1)} custom-call(bf16[2,352,1024]{2,1,0:T(8,128)(2,1)S(1)} %get-tuple-element.26.refs_0_, f32[16,128]{1,0:T(8,128)S(1)} %broadcast_in_dim.15.refs_1_, f32[352,128]{1,0:T(8,128)S(1)} %get-tuple-element.52.cos_ref.refs_2_, f32[352,128]{1,0:T(8,128)S(1)} %get-tuple-element.53.sin_ref.refs_3_, ...), custom_call_target="tpu_custom_call" | custom-call | tf_op jit(solution)/shard_map/pallas_call | solution.py:374
  26.2 0.4 collective-permute-start.8
  26.6 3.7 %shard_map.47 = (f32[1088,128]{1,0:T(8,128)S(1)}, f32[1088,128]{1,0:T(8,128)S(1)}) custom-call(bf16[2,352,1024]{2,1,0:T(8,128)(2,1)S(1)} %get-tuple-element.26.refs_0_, f32[16,128]{1,0:T(8,128)S(1)} %fusion.1.refs_1_, f32[352,128]{1,0:T(8,128)S(1)} %get-tuple-element.52.cos_ref.refs_2_, f32[352,128]{1,0:T(8,128)S(1)} %get-tuple-element.53.sin_ref.refs_3_, ...), custom_call_target="tpu_custom_call" | custom-call | tf_op jit(solution)/shard_map/pallas_call | solution.py:374
  30.3 1.2 %collective-permute-done.7 = f16[1088,128]{1,0:T(8,128)(2,1)S(1)} collective-permute-done((f16[1088,128]{1,0:T(8,128)(2,1)S(1)}, f16[1088,128]{1,0:T(8,128)(2,1)S(1)}, u32[]{:S(2)}, u32[]{:S(2)}) %collective-permute-start.7) | collective-permute-done | bytes 278560 | tf_op jit(solution)/shard_map/ppermute | solution.py:312
  31.5 0.1 collective-permute-start.9
  31.6 0.1 constant_dynamic-slice_fusion.1
  31.7 2.2 %collective-permute-start.10 = (bf16[720,128]{1,0:T(8,128)(2,1)S(1)}, bf16[720,128]{1,0:T(8,128)(2,1)S(1)}, u32[]{:S(2)}, u32[]{:S(2)}) collective-permute-start(bf16[720,128]{1,0:T(8,128)(2,1)S(1)} %get-tuple-element.36), channel_id=1, source_target_pairs={{24,8},{0,16},{25,9},{1,17},{26,10},{2,18},{27,11},{3,19},{28,12},... | collective-permute-start | bytes 552968 | tf_op jit(solution)/shard_map/ppermute | solution.py:416
  34.0 0.7 %collective-permute-start.11 = (bf16[720,128]{1,0:T(8,128)(2,1)S(1)}, bf16[720,128]{1,0:T(8,128)(2,1)S(1)}, u32[]{:S(2)}, u32[]{:S(2)}) collective-permute-start(bf16[720,128]{1,0:T(8,128)(2,1)S(1)} %get-tuple-element.35), channel_id=1, source_target_pairs={{16,8},{8,16},{17,9},{9,17},{18,10},{10,18},{19,11},{11,19},{20,12... | collective-permute-start | bytes 552968 | tf_op jit(solution)/shard_map/ppermute | solution.py:416
  34.7 1.9 %collective-permute-done.8 = f16[1088,128]{1,0:T(8,128)(2,1)S(1)} collective-permute-done((f16[1088,128]{1,0:T(8,128)(2,1)S(1)}, f16[1088,128]{1,0:T(8,128)(2,1)S(1)}, u32[]{:S(2)}, u32[]{:S(2)}) %collective-permute-start.8) | collective-permute-done | bytes 278560 | tf_op jit(solution)/shard_map/ppermute | solution.py:312
  36.6 0.1 add_convert_fusion.refs_5_.refs_2_
  36.8 0.5 collective-permute-start.12
  37.3 0.1 pad_add_fusion.refs_0_.place_ref
  37.4 1.6 %collective-permute-done.10.refs_1_.refs_3_ = bf16[720,128]{1,0:T(8,128)(2,1)S(1)} collective-permute-done((bf16[720,128]{1,0:T(8,128)(2,1)S(1)}, bf16[720,128]{1,0:T(8,128)(2,1)S(1)}, u32[]{:S(2)}, u32[]{:S(2)}) %collective-permute-start.10) | collective-permute-done | bytes 184352 | tf_op jit(solution)/shard_map/ppermute | solution.py:416
  39.0 3.7 %collective-permute-done.12.refs_3_.refs_5_ = bf16[720,128]{1,0:T(8,128)(2,1)S(1)} collective-permute-done((bf16[720,128]{1,0:T(8,128)(2,1)S(1)}, bf16[720,128]{1,0:T(8,128)(2,1)S(1)}, u32[]{:S(2)}, u32[]{:S(2)}) %collective-permute-start.12) | collective-permute-done | bytes 184352 | tf_op jit(solution)/shard_map/ppermute | solution.py:416
  42.7 0.6 shard_map.49.refs_6_
  43.3 1.3 %collective-permute-start.13 = (bf16[368,128]{1,0:T(8,128)(2,1)S(1)}, bf16[368,128]{1,0:T(8,128)(2,1)S(1)}, u32[]{:S(2)}, u32[]{:S(2)}) collective-permute-start(bf16[368,128]{1,0:T(8,128)(2,1)S(1)} %get-tuple-element.38), channel_id=1, source_target_pairs={{0,8},{8,16},{16,24},{1,9},{9,17},{17,25},{2,10},{10,18},{18,26},{... | collective-permute-start | bytes 282632 | tf_op jit(solution)/shard_map/ppermute | solution.py:416
  44.6 1.5 %collective-permute-start.14 = (bf16[368,128]{1,0:T(8,128)(2,1)S(1)}, bf16[368,128]{1,0:T(8,128)(2,1)S(1)}, u32[]{:S(2)}, u32[]{:S(2)}) collective-permute-start(bf16[368,128]{1,0:T(8,128)(2,1)S(1)} %get-tuple-element.37), channel_id=1, source_target_pairs={{8,24},{9,25},{10,26},{11,27},{12,28},{13,29},{14,30},{15,31}} | collective-permute-start | bytes 282632 | tf_op jit(solution)/shard_map/ppermute | solution.py:416
  46.1 2.7 %shard_map.50 = (f32[2,352,128]{2,1,0:T(8,128)S(1)}, f32[2,352,1]{2,1,0:T(8,128)S(1)}) custom-call(s32[2]{0:T(128)S(1)} %pad_add_fusion.refs_0_.place_ref, bf16[1088,128]{1,0:T(8,128)(2,1)S(1)} %add_convert_fusion.1.refs_4_.refs_1_, bf16[1088,128]{1,0:T(8,128)(2,1)S(1)} %add_convert_fusion.refs_5_.refs_2_, ...), custom_call_target="tpu_custom_call" | custom-call | tf_op jit(solution)/shard_map/pallas_call | solution.py:454
  48.7 4.2 %collective-permute-done.13.next_ref = bf16[368,128]{1,0:T(8,128)(2,1)S(1)} collective-permute-done((bf16[368,128]{1,0:T(8,128)(2,1)S(1)}, bf16[368,128]{1,0:T(8,128)(2,1)S(1)}, u32[]{:S(2)}, u32[]{:S(2)}) %collective-permute-start.13) | collective-permute-done | bytes 94240 | tf_op jit(solution)/shard_map/ppermute | solution.py:416
  52.9 3.2 %collective-permute-done.14.three_ref = bf16[368,128]{1,0:T(8,128)(2,1)S(1)} collective-permute-done((bf16[368,128]{1,0:T(8,128)(2,1)S(1)}, bf16[368,128]{1,0:T(8,128)(2,1)S(1)}, u32[]{:S(2)}, u32[]{:S(2)}) %collective-permute-start.14) | collective-permute-done | bytes 94240 | tf_op jit(solution)/shard_map/ppermute | solution.py:416
  56.1 1.1 %shard_map.51 = (bf16[176,256]{1,0:T(8,128)(2,1)S(1)}, bf16[176,256]{1,0:T(8,128)(2,1)S(1)}) custom-call(s32[2]{0:T(128)S(1)} %pad_add_fusion.refs_0_.place_ref, f32[2,352,128]{2,1,0:T(8,128)S(1)} %get-tuple-element.31.out_ref, f32[2,352,1]{2,1,0:T(8,128)S(1)} %get-tuple-element.32.logs_ref, bf16[368,128]{1,0:T(8,128)(2,1)S(1)} %collective-permute-done.13.next_ref, ...), custom_call_target="tpu_custom_call" | custom-call | tf_op jit(solution)/shard_map/pallas_call | solution.py:464
  57.2 1.8 %collective-permute-start.15 = (bf16[176,256]{1,0:T(8,128)(2,1)S(1)}, bf16[176,256]{1,0:T(8,128)(2,1)S(1)}, u32[]{:S(2)}, u32[]{:S(2)}) collective-permute-start(bf16[176,256]{1,0:T(8,128)(2,1)S(1)} %get-tuple-element.34), channel_id=1, source_target_pairs={{0,4},{4,0},{1,5},{5,1},{2,6},{6,2},{3,7},{7,3},{8,12},{12,8},{9,1... | collective-permute-start | bytes 270344 | tf_op jit(solution)/shard_map/ppermute | solution.py:312
  59.0 2.8 %collective-permute-done.15 = bf16[176,256]{1,0:T(8,128)(2,1)S(1)} collective-permute-done((bf16[176,256]{1,0:T(8,128)(2,1)S(1)}, bf16[176,256]{1,0:T(8,128)(2,1)S(1)}, u32[]{:S(2)}, u32[]{:S(2)}) %collective-permute-start.15) | collective-permute-done | bytes 90144 | tf_op jit(solution)/shard_map/ppermute | solution.py:312
  61.8 0.7 %pad_maximum_fusion.2 = bf16[176,512]{1,0:T(8,128)(2,1)} fusion(bf16[176,256]{1,0:T(8,128)(2,1)S(1)} %get-tuple-element.40, bf16[176,256]{1,0:T(8,128)(2,1)S(1)} %get-tuple-element.39), kind=kLoop, calls=%fused_computation.7 | loop fusion | flops 360448 | bytes 360448 | tf_op jit(solution)/shard_map/concatenate | solution.py:471
  (26 shorter events, 0.4 us)
Async XLA Ops:
  0.0 13.5 %collective-permute-start = (bf16[176,1024]{1,0:T(8,128)(2,1)}, bf16[176,1024]{1,0:T(8,128)(2,1)S(1)}, u32[]{:S(2)}, u32[]{:S(2)}) collective-permute-start(bf16[176,1024]{1,0:T(8,128)(2,1)} %param.4), channel_id=1, source_target_pairs={{0,0},{1,1},{2,4},{3,5},{4,2},{5,3},{6,6},{7,7},{8,8},{9,9},{10,12... | collective-permute-start | bytes 1081352 | tf_op jit(solution)/shard_map/ppermute | solution.py:318
  1.6 11.8 %collective-permute-start.1 = (bf16[176,1024]{1,0:T(8,128)(2,1)}, bf16[176,1024]{1,0:T(8,128)(2,1)S(1)}, u32[]{:S(2)}, u32[]{:S(2)}) collective-permute-start(bf16[176,1024]{1,0:T(8,128)(2,1)} %param.4), channel_id=1, source_target_pairs={{0,2},{1,3},{2,6},{3,7},{4,0},{5,1},{6,4},{7,5},{8,10},{9,11},{10,... | collective-permute-start | bytes 1081352 | tf_op jit(solution)/shard_map/ppermute | solution.py:323
  6.9 1.6 %collective-permute-start.2 = (f32[1200]{0:T(1024)S(1)}, f32[1200]{0:T(1024)S(1)}, u32[]{:S(2)}, u32[]{:S(2)}) collective-permute-start(f32[1200]{0:T(1024)S(1)} %pad_maximum_fusion.3), channel_id=1, source_target_pairs={{0,1},{1,0},{2,3},{3,2},{4,5},{5,4},{6,7},{7,6},{8,9},{9,8},{10,11... | collective-permute-start | bytes 14408 | tf_op jit(solution)/shard_map/ppermute | solution.py:309
  9.3 4.1 %collective-permute-start.3 = (f32[2224]{0:T(1024)S(1)}, f32[2224]{0:T(1024)S(1)}, u32[]{:S(2)}, u32[]{:S(2)}) collective-permute-start(f32[2224]{0:T(1024)S(1)} %concatenate.40), channel_id=1, source_target_pairs={{0,2},{1,3},{2,0},{3,1},{4,6},{5,7},{6,4},{7,5},{8,10},{9,11},{10,... | collective-permute-start | bytes 26696 | tf_op jit(solution)/shard_map/ppermute | solution.py:309
  9.4 7.8 %copy-start = (s32[176]{0:T(256)S(1)}, s32[176]{0:T(256)}, u32[]{:S(2)}) copy-start(s32[176]{0:T(256)} %param.7) | copy-start | bytes 2116
  13.6 3.6 %collective-permute-start.6 = (f32[352]{0:T(512)S(1)}, f32[352]{0:T(512)S(1)}, u32[]{:S(2)}, u32[]{:S(2)}) collective-permute-start(f32[352]{0:T(512)S(1)} %pad_maximum_fusion.4), channel_id=1, source_target_pairs={{0,4},{4,0},{1,5},{5,1},{2,6},{6,2},{3,7},{7,3},{8,12},{12,8},{9,1... | collective-permute-start | bytes 4232 | tf_op jit(solution)/shard_map/ppermute | solution.py:312
  15.6 1.9 %collective-permute-start.4 = (bf16[176,1024]{1,0:T(8,128)(2,1)S(1)}, bf16[176,1024]{1,0:T(8,128)(2,1)S(1)}, u32[]{:S(2)}, u32[]{:S(2)}) collective-permute-start(bf16[176,1024]{1,0:T(8,128)(2,1)S(1)} %collective-permute-done.a_near), channel_id=1, source_target_pairs={{0,1},{1,0},{2,3},{3,2},{4,5},{5,4},{6,7},{7,6},{8,9},{9,8},{10,11... | collective-permute-start | bytes 1081352 | tf_op jit(solution)/shard_map/ppermute | solution.py:309
  15.6 2.2 %collective-permute-start.5 = (bf16[176,1024]{1,0:T(8,128)(2,1)S(1)}, bf16[176,1024]{1,0:T(8,128)(2,1)S(1)}, u32[]{:S(2)}, u32[]{:S(2)}) collective-permute-start(bf16[176,1024]{1,0:T(8,128)(2,1)S(1)} %collective-permute-done.1.a_far), channel_id=1, source_target_pairs={{0,1},{1,0},{2,3},{3,2},{4,5},{5,4},{6,7},{7,6},{8,9},{9,8},{10,11... | collective-permute-start | bytes 1081352 | tf_op jit(solution)/shard_map/ppermute | solution.py:309
  21.9 9.6 %collective-permute-start.7 = (f16[1088,128]{1,0:T(8,128)(2,1)S(1)}, f16[1088,128]{1,0:T(8,128)(2,1)S(1)}, u32[]{:S(2)}, u32[]{:S(2)}) collective-permute-start(f16[1088,128]{1,0:T(8,128)(2,1)S(1)} %convert_element_type.58), channel_id=1, source_target_pairs={{0,4},{4,0},{1,5},{5,1},{2,6},{6,2},{3,7},{7,3},{8,12},{12,8},{9,1... | collective-permute-start | bytes 835592 | tf_op jit(solution)/shard_map/ppermute | solution.py:312
  26.2 10.4 %collective-permute-start.8 = (f16[1088,128]{1,0:T(8,128)(2,1)S(1)}, f16[1088,128]{1,0:T(8,128)(2,1)S(1)}, u32[]{:S(2)}, u32[]{:S(2)}) collective-permute-start(f16[1088,128]{1,0:T(8,128)(2,1)S(1)} %convert_element_type.61), channel_id=1, source_target_pairs={{0,4},{4,0},{1,5},{5,1},{2,6},{6,2},{3,7},{7,3},{8,12},{12,8},{9,1... | collective-permute-start | bytes 835592 | tf_op jit(solution)/shard_map/ppermute | solution.py:312
  31.5 3.1 %collective-permute-start.9 = (bf16[16,128]{1,0:T(8,128)(2,1)S(1)}, bf16[16,128]{1,0:T(8,128)(2,1)S(1)}, u32[]{:S(2)}, u32[]{:S(2)}) collective-permute-start(bf16[16,128]{1,0:T(8,128)(2,1)S(1)} %slice.45), channel_id=1, source_target_pairs={{0,1},{1,0},{2,3},{3,2},{4,5},{5,4},{6,7},{7,6},{8,9},{9,8},{10,11... | collective-permute-start | bytes 12296 | tf_op jit(solution)/shard_map/ppermute | solution.py:309
  31.7 7.2 %collective-permute-start.10 = (bf16[720,128]{1,0:T(8,128)(2,1)S(1)}, bf16[720,128]{1,0:T(8,128)(2,1)S(1)}, u32[]{:S(2)}, u32[]{:S(2)}) collective-permute-start(bf16[720,128]{1,0:T(8,128)(2,1)S(1)} %get-tuple-element.36), channel_id=1, source_target_pairs={{24,8},{0,16},{25,9},{1,17},{26,10},{2,18},{27,11},{3,19},{28,12},... | collective-permute-start | bytes 552968 | tf_op jit(solution)/shard_map/ppermute | solution.py:416
  34.0 5.0 %collective-permute-start.11 = (bf16[720,128]{1,0:T(8,128)(2,1)S(1)}, bf16[720,128]{1,0:T(8,128)(2,1)S(1)}, u32[]{:S(2)}, u32[]{:S(2)}) collective-permute-start(bf16[720,128]{1,0:T(8,128)(2,1)S(1)} %get-tuple-element.35), channel_id=1, source_target_pairs={{16,8},{8,16},{17,9},{9,17},{18,10},{10,18},{19,11},{11,19},{20,12... | collective-permute-start | bytes 552968 | tf_op jit(solution)/shard_map/ppermute | solution.py:416
  36.8 5.9 %collective-permute-start.12 = (bf16[720,128]{1,0:T(8,128)(2,1)S(1)}, bf16[720,128]{1,0:T(8,128)(2,1)S(1)}, u32[]{:S(2)}, u32[]{:S(2)}) collective-permute-start(bf16[720,128]{1,0:T(8,128)(2,1)S(1)} %constant_dynamic-slice_fusion), channel_id=1, source_target_pairs={{0,8},{8,0},{16,24},{24,16},{1,9},{9,1},{17,25},{25,17},{2,10},{10... | collective-permute-start | bytes 552968 | tf_op jit(solution)/shard_map/ppermute | solution.py:416
  43.3 9.6 %collective-permute-start.13 = (bf16[368,128]{1,0:T(8,128)(2,1)S(1)}, bf16[368,128]{1,0:T(8,128)(2,1)S(1)}, u32[]{:S(2)}, u32[]{:S(2)}) collective-permute-start(bf16[368,128]{1,0:T(8,128)(2,1)S(1)} %get-tuple-element.38), channel_id=1, source_target_pairs={{0,8},{8,16},{16,24},{1,9},{9,17},{17,25},{2,10},{10,18},{18,26},{... | collective-permute-start | bytes 282632 | tf_op jit(solution)/shard_map/ppermute | solution.py:416
  44.6 11.5 %collective-permute-start.14 = (bf16[368,128]{1,0:T(8,128)(2,1)S(1)}, bf16[368,128]{1,0:T(8,128)(2,1)S(1)}, u32[]{:S(2)}, u32[]{:S(2)}) collective-permute-start(bf16[368,128]{1,0:T(8,128)(2,1)S(1)} %get-tuple-element.37), channel_id=1, source_target_pairs={{8,24},{9,25},{10,26},{11,27},{12,28},{13,29},{14,30},{15,31}} | collective-permute-start | bytes 282632 | tf_op jit(solution)/shard_map/ppermute | solution.py:416
  57.2 4.6 %collective-permute-start.15 = (bf16[176,256]{1,0:T(8,128)(2,1)S(1)}, bf16[176,256]{1,0:T(8,128)(2,1)S(1)}, u32[]{:S(2)}, u32[]{:S(2)}) collective-permute-start(bf16[176,256]{1,0:T(8,128)(2,1)S(1)} %get-tuple-element.34), channel_id=1, source_target_pairs={{0,4},{4,0},{1,5},{5,1},{2,6},{6,2},{3,7},{7,3},{8,12},{12,8},{9,1... | collective-permute-start | bytes 270344 | tf_op jit(solution)/shard_map/ppermute | solution.py:312

commit v8 on v7

--- a/solution.py
+++ b/solution.py
@@ -8,9 +8,11 @@
 from jax.sharding import PartitionSpec as P
 
 EPS = 1e-05
+LOG2_E = math.log2(math.e)
 LOW = -1e30
 EXTRA = 16
 MIB = 1 << 20
+CHUNKS = ((4, 0), (1, 3))
 
 
 def rotary_tables(places, head_size):
@@ -49,23 +51,15 @@
 
 def normalise_project_kernel(
     place_ref, a_near, a_far, b_near, b_far, squares_ref, gain_ref, cos_ref, sin_ref, weight_ref,
-    out_ref, normed_ref, rest_hbm, semaphores,
+    one_ref, two_ref, normed_ref, own_hbm, semaphore,
 ):
     rows, size = a_near.shape[0], cos_ref.shape[1]
     features = 2 * gain_ref.shape[0] * gain_ref.shape[2]
     core, near_row, away, own = place_ref[0], place_ref[1], place_ref[2], place_ref[3]
-    copies = [
-        pltpu.make_async_copy(
-            weight_ref.at[:, pl.ds(pl.multiple_of(source, size), width)],
-            rest_hbm.at[:, pl.ds(target, width)],
-            semaphores.at[index],
-        )
-        for index, (source, target, width) in enumerate(
-            ((away + size, 0, 3 * size), (own, 3 * size, 6 * size))
-        )
-    ]
-    for copy in copies:
-        copy.start()
+    copy = pltpu.make_async_copy(
+        weight_ref.at[:, pl.ds(pl.multiple_of(own, size), 6 * size)], own_hbm, semaphore
+    )
+    copy.start()
     for shards, half in (((a_near, a_far), core), ((b_near, b_far), 1 - core)):
         gain = gain_ref[half]
         for shard, row in zip(shards, (near_row, 1 - near_row)):
@@ -75,24 +69,25 @@
                 jnp.bfloat16
             )
     nothing = jnp.zeros((EXTRA, size), jnp.float32)
-    project_chunk(
-        normed_ref, weight_ref, away + 4 * size, away, cos_ref, sin_ref, nothing, out_ref
-    )
-    for copy in copies:
-        copy.wait()
-
-
-def project_kernel(first, columns, normed_ref, docs_ref, cos_ref, sin_ref, rest_hbm, *refs):
-    out_refs, (weight_buffer, semaphore) = refs[:-2], refs[-2:]
-    copy = pltpu.make_async_copy(
-        rest_hbm.at[:, pl.ds(first, weight_buffer.shape[1])], weight_buffer, semaphore
-    )
+    for chunk, (keys, query) in enumerate(CHUNKS):
+        project_chunk(
+            normed_ref, weight_ref, away + keys * size, away + query * size, cos_ref, sin_ref, nothing,
+            (one_ref, two_ref)[chunk],
+        )
+    copy.wait()
+
+
+def project_kernel(
+    normed_ref, docs_ref, cos_ref, sin_ref, own_hbm, one_ref, two_ref, weight_buffer, semaphore
+):
+    copy = pltpu.make_async_copy(own_hbm, weight_buffer, semaphore)
     copy.start()
     copy.wait()
-    for (key_column, query_column), out_ref in zip(columns, out_refs):
+    size = cos_ref.shape[1]
+    for chunk, (keys, query) in enumerate(CHUNKS):
         project_chunk(
-            normed_ref, weight_buffer, key_column, query_column, cos_ref, sin_ref, docs_ref[...],
-            out_ref,
+            normed_ref, weight_buffer, keys * size, query * size, cos_ref, sin_ref, docs_ref[...],
+            (one_ref, two_ref)[chunk],
         )
 
 
@@ -153,17 +148,16 @@
         query_places = lax.broadcasted_iota(jnp.int32, shape, 0)
         key_places = lax.broadcasted_iota(jnp.int32, shape, 1)
         visible &= (key_places <= query_places) | (key_places >= block)
-    scores = (
-        lax.dot_general(query, keys, (((1,), (1,)), ((), ())), preferred_element_type=jnp.float32)
-        * scale
+    scores = lax.dot_general(
+        query, keys, (((1,), (1,)), ((), ())), preferred_element_type=jnp.float32
     )
     top = jnp.max(jnp.where(visible, scores, LOW), axis=1, keepdims=True)
-    exponentials = jnp.where(visible, jnp.exp(scores - top), 0.0)
+    exponentials = jnp.where(visible, jnp.exp2((scores - top) * (scale * LOG2_E)), 0.0)
     total = jnp.sum(exponentials, axis=1, keepdims=True)
     summed = jnp.dot(exponentials.astype(jnp.bfloat16), values, preferred_element_type=jnp.float32)
     some = total > 0.0
     safe = jnp.where(some, total, 1.0)
-    return summed / safe, jnp.where(some, top + jnp.log(safe), LOW)
+    return summed / safe, jnp.where(some, top * scale + jnp.log(safe), LOW)
 
 
 def as_message(output, logs, size):
@@ -229,7 +223,9 @@
         out_ref[index], logs_ref[index] = softmax_part(scale, query, messages, True)
 
 
-def merge_kernel(place_ref, out_ref, logs_ref, next_ref, three_ref, mine_ref, theirs_ref):
+def merge_kernel(
+    place_ref, out_ref, logs_ref, two_below_ref, one_ref, below_ref, mine_ref, theirs_ref
+):
     block, size = out_ref.shape[1:]
     tok, row = place_ref[0], place_ref[1]
     at_two, at_three = tok == 2, tok == 3
@@ -243,8 +239,8 @@
         output = out_ref[index] * weight + guest_output * guest_weight
         return (output / (weight + guest_weight)).astype(jnp.bfloat16)
 
-    down = joined(0, jnp.where(at_two, next_ref[...], three_ref[...]), at_two | at_three)
-    up = joined(1, next_ref[...], (tok == 1) | at_three)
+    down = joined(0, jnp.where(at_two, one_ref[...], two_below_ref[...]), at_two | at_three)
+    up = joined(1, below_ref[...], (tok == 1) | at_three)
     for index, output in enumerate((down, up)):
         columns = slice(index * size, (index + 1) * size)
         mine_ref[:, columns], theirs_ref[:, columns] = parted(row, output)
@@ -352,44 +348,38 @@
 
     partial_sums = jax.ShapeDtypeStruct((taller, size), jnp.float32)
     no_cost = pl.CostEstimate(flops=0, bytes_accessed=0, transcendentals=0)
-    away, normed, rest = pl.pallas_call(
+    *away, normed, own_weight = pl.pallas_call(
         normalise_project_kernel,
         out_shape=(
             partial_sums,
+            partial_sums,
             jax.ShapeDtypeStruct((2, block, width), jnp.bfloat16),
-            pltpu.HBM((span, 3 * triple), jnp.bfloat16),
+            pltpu.HBM((span, pair * triple), jnp.bfloat16),
         ),
         in_specs=[pl.BlockSpec(memory_space=pltpu.SMEM)] + in_vmem(9),
-        out_specs=tuple(in_vmem(2)) + (pl.BlockSpec(memory_space=pltpu.HBM),),
-        scratch_shapes=[pltpu.SemaphoreType.DMA((2,))],
+        out_specs=tuple(in_vmem(3)) + (pl.BlockSpec(memory_space=pltpu.HBM),),
+        scratch_shapes=[pltpu.SemaphoreType.DMA(())],
         compiler_params=pltpu.CompilerParams(vmem_limit_bytes=12 * MIB),
         cost_estimate=no_cost,
     )(
         jnp.stack([core, chip, (1 - row) * (pair * triple), row * (pair * triple)]),
         near, far, near_other, far_other, squares, gain, cosine, sine, flat_weight,
     )
-
-    def projection(first, columns, doc_rows):
-        chunks = len(columns)
-        return pl.pallas_call(
-            lambda *refs: project_kernel(first, columns, *refs),
-            out_shape=(partial_sums,) * chunks,
-            in_specs=in_vmem(4) + [pl.BlockSpec(memory_space=pltpu.HBM)],
-            out_specs=tuple(in_vmem(chunks)),
-            scratch_shapes=[
-                pltpu.VMEM((span, chunks * triple), jnp.bfloat16),
-                pltpu.SemaphoreType.DMA(()),
-            ],
-            compiler_params=pltpu.CompilerParams(vmem_limit_bytes=8 * MIB),
-            cost_estimate=no_cost,
-        )(
-            normed, doc_rows, cosine, sine, pltpu.with_memory_space_constraint(rest, pltpu.HBM)
-        )
-
-    arrived = [by_row(away.astype(jnp.float16))]
-    (away,) = projection(0, [(0, 2 * size)], jnp.zeros_like(doc_rows))
-    arrived.append(by_row(away.astype(jnp.float16)))
-    own = projection(triple, [(4 * size, 0), (size, 3 * size)], doc_rows)
+    arrived = [by_row(chunk.astype(jnp.float16)) for chunk in away]
+    own = pl.pallas_call(
+        project_kernel,
+        out_shape=(partial_sums, partial_sums),
+        in_specs=in_vmem(4) + [pl.BlockSpec(memory_space=pltpu.HBM)],
+        out_specs=tuple(in_vmem(2)),
+        scratch_shapes=[
+            pltpu.VMEM((span, pair * triple), jnp.bfloat16),
+            pltpu.SemaphoreType.DMA(()),
+        ],
+        compiler_params=pltpu.CompilerParams(vmem_limit_bytes=8 * MIB),
+        cost_estimate=no_cost,
+    )(
+        normed, doc_rows, cosine, sine, pltpu.with_memory_space_constraint(own_weight, pltpu.HBM)
+    )
     scale = 1.0 / math.sqrt(size)
 
     def summed(chunk):
@@ -432,8 +422,8 @@
             )
 
         chunk_one = summed(0)
-        two_away = along_tok(keys_or_query(chunk_one, tok == 3), [(3, 1), (0, 2)])
-        swapped = along_tok(keys_or_query(chunk_one, tok == 2), [(2, 1), (1, 2)])
+        two_away = along_tok(keys_or_query(chunk_one, tok == 3), [(0, 2), (3, 1), (1, 0), (2, 3)])
+        swapped = along_tok(keys_or_query(chunk_one, tok == 2), [(1, 2), (2, 1), (0, 0), (3, 3)])
         across = by_col(chunk_one[:EXTRA], 1)
         arrived[1] = jnp.where(
             tok < toks,
@@ -449,8 +439,9 @@
             jax.ShapeDtypeStruct((2, block + EXTRA, size), jnp.bfloat16),
             5,
         )(places, two_away, swapped, neighbour, chunk_one, chunk_two)
-        from_three = along_tok(guests[1], [(1, 3)])
-        from_next = along_tok(guests[0], [(0, 1), (1, 2), (2, 3)])
+        from_two_below = along_tok(guests[1], [(t, t ^ 2) for t in range(4)])
+        from_one = along_tok(guests[0], [(t, t ^ 3) for t in range(4)])
+        from_below = along_tok(guests[0], [(t, t ^ 1) for t in range(4)])
         output, logs = on_place(
             lambda *refs: own_kernel(scale, *refs),
             (
@@ -461,8 +452,8 @@
             1,
         )(places, chunk_one, chunk_two, two_away, swapped, neighbour, guests)
         half = jax.ShapeDtypeStruct((rows, pair * size), jnp.bfloat16)
-        mine, theirs = on_place(merge_kernel, (half, half), 4)(
-            places, output, logs, from_next, from_three
+        mine, theirs = on_place(merge_kernel, (half, half), 5)(
+            places, output, logs, from_two_below, from_one, from_below
         )
     else:
         mine, theirs = gathered_attention()

time: 63.3 us -> 64.7 us (1.022)
  the two profiles are of different devices: /device:TPU:24 before, /device:TPU:0 now
where the time goes in v8:
time: 64.7 us; the launch traced here: 64.4 us
  starting transfers between devices  24.4 us (38%)
  waiting for transfers between devices  17.2 us (27%)
  Pallas kernels  11.4 us (18%)
  other arithmetic  6.63 us (10%)
  local copies, waits for them, and re-layouts  4.41 us (7%)
    ppermute x6, starting transfers between devices, along_tok(): return lax.ppermute(value, 'tok', pairs)  11.5 us
    ppermute x6, waiting for transfers between devices, along_tok(): return lax.ppermute(value, 'tok', pairs)  8.81 us
    ppermute x4, waiting for transfers between devices, by_row(): return lax.ppermute(value, 'row', [(0, 1), (1, 0)])  8.04 us
    ppermute x4, starting transfers between devices, by_row(): return lax.ppermute(value, 'row', [(0, 1), (1, 0)])  5.98 us
    ppermute x1, starting transfers between devices, per_device(): lax.ppermute(activations, ('row', 'col'), [(r * 4 + c, c // 2 * 4 + 2 * (...  4.75 us
    unnamed x3, local copies, waits for them, and re-layouts  3.97 us
    pallas_call x1, Pallas kernels, per_device(): pl.pallas_call(project_kernel, out_shape=(partial_sums, partial_sums), in...  3.65 us
    pallas_call x1, Pallas kernels, per_device(): pl.pallas_call(normalise_project_kernel, out_shape=(partial_sums, partial...  2.68 us
  transfers between devices with their start and end apart: 17, of which 10 were waited for; matrix products, arithmetic and copies ran while one was open for 16% of the time, Pallas kernels for 10%

profile of v8, /device:TPU:0, one launch (start us, length us, event | category | flops | bytes accessed | tf_op | source)
XLA Modules:
  0.0 64.4 jit_solution(18255195708444238633)
XLA Ops:
  0.0 1.6 %collective-permute-start = (bf16[176,1024]{1,0:T(8,128)(2,1)}, bf16[176,1024]{1,0:T(8,128)(2,1)S(1)}, u32[]{:S(2)}, u32[]{:S(2)}) collective-permute-start(bf16[176,1024]{1,0:T(8,128)(2,1)} %param.4), channel_id=1, source_target_pairs={{0,0},{1,1},{2,4},{3,5},{4,2},{5,3},{6,6},{7,7},{8,8},{9,9},{10,12... | collective-permute-start | bytes 1081352 | tf_op jit(solution)/shard_map/ppermute | solution.py:314
  1.6 4.8 %collective-permute-start.1 = (bf16[176,1024]{1,0:T(8,128)(2,1)}, bf16[176,1024]{1,0:T(8,128)(2,1)S(1)}, u32[]{:S(2)}, u32[]{:S(2)}) collective-permute-start(bf16[176,1024]{1,0:T(8,128)(2,1)} %param.4), channel_id=1, source_target_pairs={{0,2},{1,3},{2,6},{3,7},{4,0},{5,1},{6,4},{7,5},{8,10},{9,11},{10,... | collective-permute-start | bytes 1081352 | tf_op jit(solution)/shard_map/ppermute | solution.py:319
  6.4 1.2 %multiply_reduce_fusion = f32[176]{0:T(256)S(1)} fusion(bf16[176,1024]{1,0:T(8,128)(2,1)} %param.4), kind=kLoop, calls=%fused_computation | loop fusion | flops 540496 | bytes 361152 | tf_op jit(solution)/shard_map/reduce_sum | solution.py:325
  7.6 0.7 %convert_element_type.54 = f32[1024]{0:T(1024)S(1)} convert(bf16[1024]{0:T(1024)(128)(2,1)} %param.5) | non-fusion elementwise | flops 1024 | bytes 6144 | tf_op jit(solution)/shard_map/convert_element_type | solution.py:326
  8.2 0.1 pad_maximum_fusion.3
  8.3 0.7 %convert_add_fusion = f32[176]{0:T(256)S(1)} fusion(s32[176]{0:T(256)} %param.7), kind=kLoop, calls=%fused_computation.27 | loop fusion | flops 352 | bytes 1408 | tf_op jit(solution)/shard_map/add | solution.py:338
  9.0 0.7 %fusion = (f32[352,64]{1,0:T(8,128)S(1)}, f32[352,64]{1,0:T(8,128)S(1)}, f32[352,64]{1,0:T(8,128)S(1)}) fusion(f32[64]{0:T(128)S(1)} %negate_power_fusion, f32[352]{0:T(512)S(1)} %add_convert_fusion.2), kind=kLoop, calls=%fused_computation.12 | loop fusion | flops 45056 | bytes 272000 | tf_op jit(solution)/shard_map/neg | solution.py:26
  9.7 0.2 pad_maximum_fusion
  10.0 0.8 %slice_select_fusion = (f32[1024]{0:T(1024)S(1)}, f32[1024]{0:T(1024)S(1)}) fusion(f32[1200]{0:T(1024)S(1)} %collective-permute-done.2, bf16[1024]{0:T(1024)(128)(2,1)} %param.5, pred[]{:T(512)S(6)} %eq.22), kind=kLoop, calls=%fused_computation.18 | loop fusion | flops 3072 | bytes 14337 | tf_op jit(solution)/shard_map/jit(_where)/select_n | solution.py:312
  10.7 0.1 concatenate.40
  10.8 0.1 pad_add_fusion.1.place_ref
  10.9 4.0 %copy.6 = bf16[256,8,4,384]{3,1,2,0:T(8,128)(2,1)S(1)} copy(bf16[256,8,4,384]{3,2,1,0:T(4,128)(2,1)} %bitcast.23) | data formatting | bytes 12582912
  14.9 0.1 slice.37
  15.0 0.1 pad_maximum_fusion.4
  15.1 2.0 %collective-permute-start.6 = (f32[352]{0:T(512)S(1)}, f32[352]{0:T(512)S(1)}, u32[]{:S(2)}, u32[]{:S(2)}) collective-permute-start(f32[352]{0:T(512)S(1)} %pad_maximum_fusion.4), channel_id=1, source_target_pairs={{0,4},{4,0},{1,5},{5,1},{2,6},{6,2},{3,7},{7,3},{8,12},{12,8},{9,1... | collective-permute-start | bytes 4232 | tf_op jit(solution)/shard_map/ppermute | solution.py:308
  17.0 0.5 collective-permute-start.5
  17.6 1.1 %collective-permute-done.6 = f32[352]{0:T(512)S(1)} collective-permute-done((f32[352]{0:T(512)S(1)}, f32[352]{0:T(512)S(1)}, u32[]{:S(2)}, u32[]{:S(2)}) %collective-permute-start.6) | collective-permute-done | bytes 1440 | tf_op jit(solution)/shard_map/ppermute | solution.py:308
  18.7 0.1 broadcast_select_fusion.4
  18.7 0.1 pad_maximum_fusion.5
  18.8 0.1 reshape.62.squares_ref
  18.9 0.3 collective-permute-done.5.b_far
  19.2 2.7 %shard_map.46 = (f32[1088,128]{1,0:T(8,128)S(1)}, f32[1088,128]{1,0:T(8,128)S(1)}, bf16[2,352,1024]{2,1,0:T(8,128)(2,1)S(1)}, bf16[2048,768]{1,0:T(8,128)(2,1)}) custom-call(s32[4]{0:T(128)S(1)} %pad_add_fusion.1.place_ref, bf16[176,1024]{1,0:T(8,128)(2,1)S(1)} %collective-permute-done.a_near, bf16[176,1024]{1,0:T(8,128)(2,1)S(1)} %collective-permute-done.1.a_far, ...), custom_call_target="tpu_custom_call" | custom-call | tf_op jit(solution)/shard_map/pallas_call | solution.py:351
  22.0 1.8 %collective-permute-start.7 = (f16[1088,128]{1,0:T(8,128)(2,1)S(1)}, f16[1088,128]{1,0:T(8,128)(2,1)}, u32[]{:S(2)}, u32[]{:S(2)}) collective-permute-start(f16[1088,128]{1,0:T(8,128)(2,1)S(1)} %convert_element_type.58), channel_id=1, source_target_pairs={{0,4},{4,0},{1,5},{5,1},{2,6},{6,2},{3,7},{7,3},{8,12},{12,8},{9,1... | collective-permute-start | bytes 835592 | tf_op jit(solution)/shard_map/ppermute | solution.py:308
  23.7 0.1 fusion.1.docs_ref
  23.8 0.4 collective-permute-start.8
  24.2 3.7 %shard_map.47 = (f32[1088,128]{1,0:T(8,128)S(1)}, f32[1088,128]{1,0:T(8,128)S(1)}) custom-call(bf16[2,352,1024]{2,1,0:T(8,128)(2,1)S(1)} %get-tuple-element.27.normed_ref, f32[16,128]{1,0:T(8,128)S(1)} %fusion.1.docs_ref, f32[352,128]{1,0:T(8,128)S(1)} %get-tuple-element.54.cos_ref, f32[352,128]{1,0:T(8,128)S(1)} %get-tuple-element.55.sin_ref, ...), custom_call_target="tpu_custom_call" | custom-call | tf_op jit(solution)/shard_map/pallas_call | solution.py:369
  27.9 3.7 %collective-permute-done.7 = f16[1088,128]{1,0:T(8,128)(2,1)} collective-permute-done((f16[1088,128]{1,0:T(8,128)(2,1)S(1)}, f16[1088,128]{1,0:T(8,128)(2,1)}, u32[]{:S(2)}, u32[]{:S(2)}) %collective-permute-start.7) | collective-permute-done | bytes 278560 | tf_op jit(solution)/shard_map/ppermute | solution.py:308
  31.6 1.0 %add_convert_fusion.1.refs_4_.refs_1_ = bf16[1088,128]{1,0:T(8,128)(2,1)S(1)} fusion(f32[1088,128]{1,0:T(8,128)S(1)} %get-tuple-element.29, f16[1088,128]{1,0:T(8,128)(2,1)} %collective-permute-done.7), kind=kLoop, calls=%fused_computation.2 | loop fusion | flops 417792 | bytes 1114112 | tf_op jit(solution)/shard_map/convert_element_type | solution.py:386
  32.7 0.1 collective-permute-start.9
  32.8 0.1 constant_dynamic-slice_fusion.1
  32.9 2.6 %collective-permute-start.10 = (bf16[720,128]{1,0:T(8,128)(2,1)S(1)}, bf16[720,128]{1,0:T(8,128)(2,1)S(1)}, u32[]{:S(2)}, u32[]{:S(2)}) collective-permute-start(bf16[720,128]{1,0:T(8,128)(2,1)S(1)} %get-tuple-element.38), channel_id=1, source_target_pairs={{0,16},{24,8},{8,0},{16,24},{1,17},{25,9},{9,1},{17,25},{2,18},{26... | collective-permute-start | bytes 552968 | tf_op jit(solution)/shard_map/ppermute | solution.py:406
  35.5 0.7 %collective-permute-start.11 = (bf16[720,128]{1,0:T(8,128)(2,1)S(1)}, bf16[720,128]{1,0:T(8,128)(2,1)S(1)}, u32[]{:S(2)}, u32[]{:S(2)}) collective-permute-start(bf16[720,128]{1,0:T(8,128)(2,1)S(1)} %get-tuple-element.37), channel_id=1, source_target_pairs={{8,16},{16,8},{0,0},{24,24},{9,17},{17,9},{1,1},{25,25},{10,18},{1... | collective-permute-start | bytes 552968 | tf_op jit(solution)/shard_map/ppermute | solution.py:406
  36.2 0.5 collective-permute-done.8
  36.7 0.1 add_convert_fusion.refs_5_.refs_2_
  36.8 3.0 %collective-permute-start.12 = (bf16[720,128]{1,0:T(8,128)(2,1)S(1)}, bf16[720,128]{1,0:T(8,128)(2,1)S(1)}, u32[]{:S(2)}, u32[]{:S(2)}) collective-permute-start(bf16[720,128]{1,0:T(8,128)(2,1)S(1)} %constant_dynamic-slice_fusion), channel_id=1, source_target_pairs={{0,8},{8,0},{16,24},{24,16},{1,9},{9,1},{17,25},{25,17},{2,10},{10... | collective-permute-start | bytes 552968 | tf_op jit(solution)/shard_map/ppermute | solution.py:406
  39.8 0.1 pad_add_fusion.refs_0_.place_ref
  39.9 0.3 collective-permute-done.10.refs_1_.refs_3_
  40.2 4.3 %collective-permute-done.12.refs_3_.refs_5_ = bf16[720,128]{1,0:T(8,128)(2,1)S(1)} collective-permute-done((bf16[720,128]{1,0:T(8,128)(2,1)S(1)}, bf16[720,128]{1,0:T(8,128)(2,1)S(1)}, u32[]{:S(2)}, u32[]{:S(2)}) %collective-permute-start.12) | collective-permute-done | bytes 184352 | tf_op jit(solution)/shard_map/ppermute | solution.py:406
  44.6 1.6 %shard_map.48.refs_6_ = bf16[2,368,128]{2,1,0:T(8,128)(2,1)S(1)} custom-call(s32[2]{0:T(128)S(1)} %pad_add_fusion.refs_0_.place_ref, bf16[720,128]{1,0:T(8,128)(2,1)S(1)} %collective-permute-done.10.refs_1_.refs_3_, bf16[720,128]{1,0:T(8,128)(2,1)S(1)} %collective-permute-done.11.refs_2_.refs_4_, ...), custom_call_target="tpu_custom_call" | custom-call | tf_op jit(solution)/shard_map/pallas_call | solution.py:437
  46.1 3.5 %collective-permute-start.13 = (bf16[368,128]{1,0:T(8,128)(2,1)S(1)}, bf16[368,128]{1,0:T(8,128)(2,1)S(1)}, u32[]{:S(2)}, u32[]{:S(2)}) collective-permute-start(bf16[368,128]{1,0:T(8,128)(2,1)S(1)} %get-tuple-element.40), channel_id=1, source_target_pairs={{0,16},{8,24},{16,0},{24,8},{1,17},{9,25},{17,1},{25,9},{2,18},{10... | collective-permute-start | bytes 282632 | tf_op jit(solution)/shard_map/ppermute | solution.py:406
  49.7 1.7 %collective-permute-start.14 = (bf16[368,128]{1,0:T(8,128)(2,1)S(1)}, bf16[368,128]{1,0:T(8,128)(2,1)S(1)}, u32[]{:S(2)}, u32[]{:S(2)}) collective-permute-start(bf16[368,128]{1,0:T(8,128)(2,1)S(1)} %get-tuple-element.39), channel_id=1, source_target_pairs={{0,24},{8,16},{16,8},{24,0},{1,25},{9,17},{17,9},{25,1},{2,26},{10... | collective-permute-start | bytes 282632 | tf_op jit(solution)/shard_map/ppermute | solution.py:406
  51.3 2.5 %shard_map.49 = (f32[2,352,128]{2,1,0:T(8,128)S(1)}, f32[2,352,1]{2,1,0:T(8,128)S(1)}) custom-call(s32[2]{0:T(128)S(1)} %pad_add_fusion.refs_0_.place_ref, bf16[1088,128]{1,0:T(8,128)(2,1)S(1)} %add_convert_fusion.1.refs_4_.refs_1_, bf16[1088,128]{1,0:T(8,128)(2,1)S(1)} %add_convert_fusion.refs_5_.refs_2_, ...), custom_call_target="tpu_custom_call" | custom-call | tf_op jit(solution)/shard_map/pallas_call | solution.py:445
  53.8 3.4 %collective-permute-done.13.two_below_ref = bf16[368,128]{1,0:T(8,128)(2,1)S(1)} collective-permute-done((bf16[368,128]{1,0:T(8,128)(2,1)S(1)}, bf16[368,128]{1,0:T(8,128)(2,1)S(1)}, u32[]{:S(2)}, u32[]{:S(2)}) %collective-permute-start.13) | collective-permute-done | bytes 94240 | tf_op jit(solution)/shard_map/ppermute | solution.py:406
  57.2 0.8 %collective-permute-done.15.below_ref = bf16[368,128]{1,0:T(8,128)(2,1)S(1)} collective-permute-done((bf16[368,128]{1,0:T(8,128)(2,1)S(1)}, bf16[368,128]{1,0:T(8,128)(2,1)S(1)}, u32[]{:S(2)}, u32[]{:S(2)}) %collective-permute-start.15) | collective-permute-done | bytes 94240 | tf_op jit(solution)/shard_map/ppermute | solution.py:406
  58.0 1.1 %shard_map.50 = (bf16[176,256]{1,0:T(8,128)(2,1)S(1)}, bf16[176,256]{1,0:T(8,128)(2,1)S(1)}) custom-call(s32[2]{0:T(128)S(1)} %pad_add_fusion.refs_0_.place_ref, f32[2,352,128]{2,1,0:T(8,128)S(1)} %get-tuple-element.33.out_ref, f32[2,352,1]{2,1,0:T(8,128)S(1)} %get-tuple-element.34.logs_ref, bf16[368,128]{1,0:T(8,128)(2,1)S(1)} %collective-permute-done.13.two_below_ref, ...), custom_call_target="tpu_custom_call" | custom-call | tf_op jit(solution)/shard_map/pallas_call | solution.py:455
  59.1 1.9 %collective-permute-start.16 = (bf16[176,256]{1,0:T(8,128)(2,1)S(1)}, bf16[176,256]{1,0:T(8,128)(2,1)S(1)}, u32[]{:S(2)}, u32[]{:S(2)}) collective-permute-start(bf16[176,256]{1,0:T(8,128)(2,1)S(1)} %get-tuple-element.36), channel_id=1, source_target_pairs={{0,4},{4,0},{1,5},{5,1},{2,6},{6,2},{3,7},{7,3},{8,12},{12,8},{9,1... | collective-permute-start | bytes 270344 | tf_op jit(solution)/shard_map/ppermute | solution.py:308
  60.9 2.7 %collective-permute-done.16 = bf16[176,256]{1,0:T(8,128)(2,1)S(1)} collective-permute-done((bf16[176,256]{1,0:T(8,128)(2,1)S(1)}, bf16[176,256]{1,0:T(8,128)(2,1)S(1)}, u32[]{:S(2)}, u32[]{:S(2)}) %collective-permute-start.16) | collective-permute-done | bytes 90144 | tf_op jit(solution)/shard_map/ppermute | solution.py:308
  63.7 0.7 %pad_maximum_fusion.2 = bf16[176,512]{1,0:T(8,128)(2,1)} fusion(bf16[176,256]{1,0:T(8,128)(2,1)S(1)} %get-tuple-element.42, bf16[176,256]{1,0:T(8,128)(2,1)S(1)} %get-tuple-element.41), kind=kLoop, calls=%fused_computation.7 | loop fusion | flops 360448 | bytes 360448 | tf_op jit(solution)/shard_map/concatenate | solution.py:462
  (26 shorter events, 0.3 us)
Async XLA Ops:
  0.0 14.9 %collective-permute-start = (bf16[176,1024]{1,0:T(8,128)(2,1)}, bf16[176,1024]{1,0:T(8,128)(2,1)S(1)}, u32[]{:S(2)}, u32[]{:S(2)}) collective-permute-start(bf16[176,1024]{1,0:T(8,128)(2,1)} %param.4), channel_id=1, source_target_pairs={{0,0},{1,1},{2,4},{3,5},{4,2},{5,3},{6,6},{7,7},{8,8},{9,9},{10,12... | collective-permute-start | bytes 1081352 | tf_op jit(solution)/shard_map/ppermute | solution.py:314
  1.6 13.3 %collective-permute-start.1 = (bf16[176,1024]{1,0:T(8,128)(2,1)}, bf16[176,1024]{1,0:T(8,128)(2,1)S(1)}, u32[]{:S(2)}, u32[]{:S(2)}) collective-permute-start(bf16[176,1024]{1,0:T(8,128)(2,1)} %param.4), channel_id=1, source_target_pairs={{0,2},{1,3},{2,6},{3,7},{4,0},{5,1},{6,4},{7,5},{8,10},{9,11},{10,... | collective-permute-start | bytes 1081352 | tf_op jit(solution)/shard_map/ppermute | solution.py:319
  8.3 1.6 %collective-permute-start.2 = (f32[1200]{0:T(1024)S(1)}, f32[1200]{0:T(1024)S(1)}, u32[]{:S(2)}, u32[]{:S(2)}) collective-permute-start(f32[1200]{0:T(1024)S(1)} %pad_maximum_fusion.3), channel_id=1, source_target_pairs={{0,1},{1,0},{2,3},{3,2},{4,5},{5,4},{6,7},{7,6},{8,9},{9,8},{10,11... | collective-permute-start | bytes 14408 | tf_op jit(solution)/shard_map/ppermute | solution.py:305
  10.8 4.1 %collective-permute-start.3 = (f32[2224]{0:T(1024)S(1)}, f32[2224]{0:T(1024)S(1)}, u32[]{:S(2)}, u32[]{:S(2)}) collective-permute-start(f32[2224]{0:T(1024)S(1)} %concatenate.40), channel_id=1, source_target_pairs={{0,2},{1,3},{2,0},{3,1},{4,6},{5,7},{6,4},{7,5},{8,10},{9,11},{10,... | collective-permute-start | bytes 26696 | tf_op jit(solution)/shard_map/ppermute | solution.py:305
  10.9 7.8 %copy-start = (s32[176]{0:T(256)S(1)}, s32[176]{0:T(256)}, u32[]{:S(2)}) copy-start(s32[176]{0:T(256)} %param.7) | copy-start | bytes 2116
  15.1 3.6 %collective-permute-start.6 = (f32[352]{0:T(512)S(1)}, f32[352]{0:T(512)S(1)}, u32[]{:S(2)}, u32[]{:S(2)}) collective-permute-start(f32[352]{0:T(512)S(1)} %pad_maximum_fusion.4), channel_id=1, source_target_pairs={{0,4},{4,0},{1,5},{5,1},{2,6},{6,2},{3,7},{7,3},{8,12},{12,8},{9,1... | collective-permute-start | bytes 4232 | tf_op jit(solution)/shard_map/ppermute | solution.py:308
  17.0 1.9 %collective-permute-start.4 = (bf16[176,1024]{1,0:T(8,128)(2,1)S(1)}, bf16[176,1024]{1,0:T(8,128)(2,1)S(1)}, u32[]{:S(2)}, u32[]{:S(2)}) collective-permute-start(bf16[176,1024]{1,0:T(8,128)(2,1)S(1)} %collective-permute-done.a_near), channel_id=1, source_target_pairs={{0,1},{1,0},{2,3},{3,2},{4,5},{5,4},{6,7},{7,6},{8,9},{9,8},{10,11... | collective-permute-start | bytes 1081352 | tf_op jit(solution)/shard_map/ppermute | solution.py:305
  17.0 2.2 %collective-permute-start.5 = (bf16[176,1024]{1,0:T(8,128)(2,1)S(1)}, bf16[176,1024]{1,0:T(8,128)(2,1)S(1)}, u32[]{:S(2)}, u32[]{:S(2)}) collective-permute-start(bf16[176,1024]{1,0:T(8,128)(2,1)S(1)} %collective-permute-done.1.a_far), channel_id=1, source_target_pairs={{0,1},{1,0},{2,3},{3,2},{4,5},{5,4},{6,7},{7,6},{8,9},{9,8},{10,11... | collective-permute-start | bytes 1081352 | tf_op jit(solution)/shard_map/ppermute | solution.py:305
  22.0 9.7 %collective-permute-start.7 = (f16[1088,128]{1,0:T(8,128)(2,1)S(1)}, f16[1088,128]{1,0:T(8,128)(2,1)}, u32[]{:S(2)}, u32[]{:S(2)}) collective-permute-start(f16[1088,128]{1,0:T(8,128)(2,1)S(1)} %convert_element_type.58), channel_id=1, source_target_pairs={{0,4},{4,0},{1,5},{5,1},{2,6},{6,2},{3,7},{7,3},{8,12},{12,8},{9,1... | collective-permute-start | bytes 835592 | tf_op jit(solution)/shard_map/ppermute | solution.py:308
  23.8 12.8 %collective-permute-start.8 = (f16[1088,128]{1,0:T(8,128)(2,1)S(1)}, f16[1088,128]{1,0:T(8,128)(2,1)S(1)}, u32[]{:S(2)}, u32[]{:S(2)}) collective-permute-start(f16[1088,128]{1,0:T(8,128)(2,1)S(1)} %convert_element_type.61), channel_id=1, source_target_pairs={{0,4},{4,0},{1,5},{5,1},{2,6},{6,2},{3,7},{7,3},{8,12},{12,8},{9,1... | collective-permute-start | bytes 835592 | tf_op jit(solution)/shard_map/ppermute | solution.py:308
  32.7 3.5 %collective-permute-start.9 = (bf16[16,128]{1,0:T(8,128)(2,1)S(1)}, bf16[16,128]{1,0:T(8,128)(2,1)S(1)}, u32[]{:S(2)}, u32[]{:S(2)}) collective-permute-start(bf16[16,128]{1,0:T(8,128)(2,1)S(1)} %slice.46), channel_id=1, source_target_pairs={{0,1},{1,0},{2,3},{3,2},{4,5},{5,4},{6,7},{7,6},{8,9},{9,8},{10,11... | collective-permute-start | bytes 12296 | tf_op jit(solution)/shard_map/ppermute | solution.py:305
  32.9 7.3 %collective-permute-start.10 = (bf16[720,128]{1,0:T(8,128)(2,1)S(1)}, bf16[720,128]{1,0:T(8,128)(2,1)S(1)}, u32[]{:S(2)}, u32[]{:S(2)}) collective-permute-start(bf16[720,128]{1,0:T(8,128)(2,1)S(1)} %get-tuple-element.38), channel_id=1, source_target_pairs={{0,16},{24,8},{8,0},{16,24},{1,17},{25,9},{9,1},{17,25},{2,18},{26... | collective-permute-start | bytes 552968 | tf_op jit(solution)/shard_map/ppermute | solution.py:406
  35.5 4.7 %collective-permute-start.11 = (bf16[720,128]{1,0:T(8,128)(2,1)S(1)}, bf16[720,128]{1,0:T(8,128)(2,1)S(1)}, u32[]{:S(2)}, u32[]{:S(2)}) collective-permute-start(bf16[720,128]{1,0:T(8,128)(2,1)S(1)} %get-tuple-element.37), channel_id=1, source_target_pairs={{8,16},{16,8},{0,0},{24,24},{9,17},{17,9},{1,1},{25,25},{10,18},{1... | collective-permute-start | bytes 552968 | tf_op jit(solution)/shard_map/ppermute | solution.py:406
  36.8 7.7 %collective-permute-start.12 = (bf16[720,128]{1,0:T(8,128)(2,1)S(1)}, bf16[720,128]{1,0:T(8,128)(2,1)S(1)}, u32[]{:S(2)}, u32[]{:S(2)}) collective-permute-start(bf16[720,128]{1,0:T(8,128)(2,1)S(1)} %constant_dynamic-slice_fusion), channel_id=1, source_target_pairs={{0,8},{8,0},{16,24},{24,16},{1,9},{9,1},{17,25},{25,17},{2,10},{10... | collective-permute-start | bytes 552968 | tf_op jit(solution)/shard_map/ppermute | solution.py:406
  46.1 11.1 %collective-permute-start.13 = (bf16[368,128]{1,0:T(8,128)(2,1)S(1)}, bf16[368,128]{1,0:T(8,128)(2,1)S(1)}, u32[]{:S(2)}, u32[]{:S(2)}) collective-permute-start(bf16[368,128]{1,0:T(8,128)(2,1)S(1)} %get-tuple-element.40), channel_id=1, source_target_pairs={{0,16},{8,24},{16,0},{24,8},{1,17},{9,25},{17,1},{25,9},{2,18},{10... | collective-permute-start | bytes 282632 | tf_op jit(solution)/shard_map/ppermute | solution.py:406
  49.7 7.6 %collective-permute-start.14 = (bf16[368,128]{1,0:T(8,128)(2,1)S(1)}, bf16[368,128]{1,0:T(8,128)(2,1)S(1)}, u32[]{:S(2)}, u32[]{:S(2)}) collective-permute-start(bf16[368,128]{1,0:T(8,128)(2,1)S(1)} %get-tuple-element.39), channel_id=1, source_target_pairs={{0,24},{8,16},{16,8},{24,0},{1,25},{9,17},{17,9},{25,1},{2,26},{10... | collective-permute-start | bytes 282632 | tf_op jit(solution)/shard_map/ppermute | solution.py:406
  51.3 6.6 %collective-permute-start.15 = (bf16[368,128]{1,0:T(8,128)(2,1)S(1)}, bf16[368,128]{1,0:T(8,128)(2,1)S(1)}, u32[]{:S(2)}, u32[]{:S(2)}) collective-permute-start(bf16[368,128]{1,0:T(8,128)(2,1)S(1)} %get-tuple-element.39), channel_id=1, source_target_pairs={{0,8},{8,0},{16,24},{24,16},{1,9},{9,1},{17,25},{25,17},{2,10},{10... | collective-permute-start | bytes 282632 | tf_op jit(solution)/shard_map/ppermute | solution.py:406
  59.1 4.6 %collective-permute-start.16 = (bf16[176,256]{1,0:T(8,128)(2,1)S(1)}, bf16[176,256]{1,0:T(8,128)(2,1)S(1)}, u32[]{:S(2)}, u32[]{:S(2)}) collective-permute-start(bf16[176,256]{1,0:T(8,128)(2,1)S(1)} %get-tuple-element.36), channel_id=1, source_target_pairs={{0,4},{4,0},{1,5},{5,1},{2,6},{6,2},{3,7},{7,3},{8,12},{12,8},{9,1... | collective-permute-start | bytes 270344 | tf_op jit(solution)/shard_map/ppermute | solution.py:308

commit v9 on v8

--- a/solution.py
+++ b/solution.py
@@ -184,15 +184,34 @@
     )
 
 
+def joined(first, second):
+    (output, logs), (other, other_logs) = first, second
+    top = jnp.maximum(logs, other_logs)
+    weight, other_weight = jnp.exp(logs - top), jnp.exp(other_logs - top)
+    total = weight + other_weight
+    return (output * weight + other * other_weight) / total, top + jnp.log(total)
+
+
+def own_block_kernel(scale, place_ref, chunk_one, chunk_two, out_ref, logs_ref):
+    for index, (queries, keys) in enumerate(((chunk_one, chunk_two), (chunk_two, chunk_one))):
+        height = keys.shape[0] - out_ref.shape[1] - EXTRA
+        out_ref[index], logs_ref[index] = softmax_part(
+            scale, queries[height:, :], [(keys[:height, :], True)], True
+        )
+
+
 def guest_kernel(
-    scale, place_ref, two_away, swapped, neighbour, chunk_one, chunk_two, out_ref
+    scale, place_ref, swapped, two_away, neighbour, chunk_one, chunk_two, unused_ref, out_ref
 ):
     height, size = neighbour.shape
     begin = (height - EXTRA) // 2
 
     def attend(index, query, messages):
         output, logs = softmax_part(scale, query, [(m, True) for m in messages], False)
-        out_ref[index] = as_message(output, logs, size)
+        for owner, (a, b) in enumerate(
+            zip(parted(place_ref[1], output), parted(place_ref[1], logs))
+        ):
+            out_ref[index, owner] = as_message(a, b, size)
 
     @pl.when(place_ref[0] == 0)
     def one_up():
@@ -209,41 +228,59 @@
         attend(0, neighbour[begin:, :], [two_away[...], swapped[...], chunk_one[:height, :]])
 
 
-def own_kernel(
-    scale, place_ref, chunk_one, chunk_two, two_away, swapped, neighbour, unused_ref, out_ref,
-    logs_ref,
+def own_rest_kernel(
+    scale, place_ref, own_out, own_logs, chunk_one, chunk_two, swapped, two_away, neighbour,
+    unused_ref, mine_ref, logs_ref, theirs_ref, out_buffer, logs_buffer,
 ):
-    tok = place_ref[0]
-    height = neighbour.shape[0]
-    down = [(chunk_two[:height, :], True), (neighbour[...], (tok == 1) | (tok == 3))]
-    up = [(chunk_one[:height, :], True), (swapped[...], tok == 2), (two_away[...], tok == 2)]
-    for index, (query, messages) in enumerate(
-        ((chunk_one[height:, :], down), (chunk_two[height:, :], up))
-    ):
-        out_ref[index], logs_ref[index] = softmax_part(scale, query, messages, True)
+    tok, row = place_ref[0], place_ref[1]
+    height, size = neighbour.shape
+    out_buffer[...] = own_out[...]
+    logs_buffer[...] = own_logs[...]
+
+    def add(index, query, messages):
+        part = softmax_part(scale, query, [(m, True) for m in messages], False)
+        out_buffer[index], logs_buffer[index] = joined(
+            (own_out[index], own_logs[index]), part
+        )
+
+    @pl.when((tok == 1) | (tok == 3))
+    def down():
+        add(0, chunk_one[height:, :], [neighbour[...]])
+
+    @pl.when(tok == 2)
+    def up():
+        add(1, chunk_two[height:, :], [swapped[...], two_away[...]])
+
+    for index in range(2):
+        mine_ref[index], theirs = parted(row, out_buffer[index])
+        logs_ref[index], their_logs = parted(row, logs_buffer[index])
+        theirs_ref[index] = as_message(theirs, their_logs, size)
 
 
 def merge_kernel(
-    place_ref, out_ref, logs_ref, two_below_ref, one_ref, below_ref, mine_ref, theirs_ref
+    place_ref, mine_ref, logs_ref, partner_ref, three_same, three_cross, below_same, below_cross,
+    out_ref,
 ):
-    block, size = out_ref.shape[1:]
+    rows, size = mine_ref.shape[1:]
     tok, row = place_ref[0], place_ref[1]
-    at_two, at_three = tok == 2, tok == 3
-
-    def joined(index, message, present):
-        logs = logs_ref[index]
-        guest = jnp.where(present, logs_of(message, block), LOW)
-        top = jnp.maximum(logs, guest)
-        weight, guest_weight = jnp.exp(logs - top), jnp.exp(guest - top)
-        guest_output = jnp.where(present, message[:block].astype(jnp.float32), 0.0)
-        output = out_ref[index] * weight + guest_output * guest_weight
-        return (output / (weight + guest_weight)).astype(jnp.bfloat16)
-
-    down = joined(0, jnp.where(at_two, one_ref[...], two_below_ref[...]), at_two | at_three)
-    up = joined(1, below_ref[...], (tok == 1) | at_three)
-    for index, output in enumerate((down, up)):
-        columns = slice(index * size, (index + 1) * size)
-        mine_ref[:, columns], theirs_ref[:, columns] = parted(row, output)
+
+    def from_message(message):
+        return message[:rows].astype(jnp.float32), logs_of(message, rows)
+
+    def present(message, condition):
+        output, logs = from_message(message)
+        return jnp.where(condition, output, 0.0), jnp.where(condition, logs, LOW)
+
+    for mine, three, below in ((True, three_same, below_same), (False, three_cross, below_cross)):
+        begin = jnp.where(row == 0, 0, 2) if mine else jnp.where(row == 0, 2, 0)
+        guests = (
+            present(jnp.where(tok == 2, below[...], three[...]), tok >= 2),
+            present(below[...], (tok == 1) | (tok == 3)),
+        )
+        for index, guest in enumerate(guests):
+            own = (mine_ref[index], logs_ref[index]) if mine else from_message(partner_ref[index])
+            at = pl.ds(pl.multiple_of((begin + index) * size, size), size)
+            out_ref[:, at] = joined(own, guest)[0].astype(jnp.bfloat16)
 
 
 def attend_gathered(query, keys, values, places, starts, scale):
@@ -409,7 +446,7 @@
             begin = jnp.where(is_query, taller - break_at, 0)
             return lax.dynamic_slice_in_dim(chunk, begin.astype(jnp.uint32), break_at, 0)
 
-        def on_place(kernel, out_shape, ins, unused=0):
+        def on_place(kernel, out_shape, ins, unused=0, scratch=()):
             return pl.pallas_call(
                 kernel,
                 out_shape=out_shape,
@@ -417,6 +454,7 @@
                 + in_vmem(ins - unused)
                 + [pl.BlockSpec(memory_space=pl.ANY)] * unused,
                 out_specs=jax.tree.map(lambda unused: in_vmem(1)[0], out_shape),
+                scratch_shapes=scratch,
                 compiler_params=pltpu.CompilerParams(vmem_limit_bytes=16 * MIB),
                 cost_estimate=pl.CostEstimate(flops=0, bytes_accessed=0, transcendentals=0),
             )
@@ -434,30 +472,50 @@
         neighbour = along_tok(
             keys_or_query(chunk_two, (tok & 1) == 1), [(0, 1), (1, 0), (2, 3), (3, 2)]
         )
+        part_shapes = (
+            jax.ShapeDtypeStruct((2, block, size), jnp.float32),
+            jax.ShapeDtypeStruct((2, block, 1), jnp.float32),
+        )
+        own_out, own_logs = on_place(
+            lambda *refs: own_block_kernel(scale, *refs), part_shapes, 2
+        )(places, chunk_one, chunk_two)
+        half_message = (rows + EXTRA, size)
         guests = on_place(
             lambda *refs: guest_kernel(scale, *refs),
-            jax.ShapeDtypeStruct((2, block + EXTRA, size), jnp.bfloat16),
-            5,
-        )(places, two_away, swapped, neighbour, chunk_one, chunk_two)
-        from_two_below = along_tok(guests[1], [(t, t ^ 2) for t in range(4)])
-        from_one = along_tok(guests[0], [(t, t ^ 3) for t in range(4)])
-        from_below = along_tok(guests[0], [(t, t ^ 1) for t in range(4)])
-        output, logs = on_place(
-            lambda *refs: own_kernel(scale, *refs),
-            (
-                jax.ShapeDtypeStruct((2, block, size), jnp.float32),
-                jax.ShapeDtypeStruct((2, block, 1), jnp.float32),
-            ),
+            jax.ShapeDtypeStruct((2, 2) + half_message, jnp.bfloat16),
             6,
             1,
-        )(places, chunk_one, chunk_two, two_away, swapped, neighbour, guests)
-        half = jax.ShapeDtypeStruct((rows, pair * size), jnp.bfloat16)
-        mine, theirs = on_place(merge_kernel, (half, half), 5)(
-            places, output, logs, from_two_below, from_one, from_below
-        )
-    else:
-        mine, theirs = gathered_attention()
-
+        )(places, swapped, two_away, neighbour, chunk_one, chunk_two, own_logs)
+
+        def returned(value, targets):
+            across = [
+                (2 * t + r, 2 * to + (1 - r if t != to else r))
+                for t, to in enumerate(targets)
+                for r in range(2)
+            ]
+            return [
+                along_tok(value[0], list(enumerate(targets))),
+                lax.ppermute(value[1], ("tok", "row"), across),
+            ]
+
+        from_three = returned(guests[1], (0, 3, 2, 1))
+        from_below = returned(guests[0], (1, 2, 3, 0))
+        mine, logs, theirs = on_place(
+            lambda *refs: own_rest_kernel(scale, *refs),
+            (
+                jax.ShapeDtypeStruct((2, rows, size), jnp.float32),
+                jax.ShapeDtypeStruct((2, rows, 1), jnp.float32),
+                jax.ShapeDtypeStruct((2,) + half_message, jnp.bfloat16),
+            ),
+            8,
+            1,
+            [pltpu.VMEM(shape.shape, shape.dtype) for shape in part_shapes],
+        )(places, own_out, own_logs, chunk_one, chunk_two, swapped, two_away, neighbour, guests)
+        return on_place(
+            merge_kernel, jax.ShapeDtypeStruct((rows, local_heads * size), jnp.bfloat16), 7
+        )(places, mine, logs, by_row(theirs), *from_three, *from_below)
+
+    mine, theirs = gathered_attention()
     theirs = by_row(theirs)
     return jnp.concatenate(
         [jnp.where(row == 0, mine, theirs), jnp.where(row == 0, theirs, mine)], axis=1

time: 64.7 us -> 69.5 us (1.074)
  starting transfers between devices: 24.4 us -> 29.3 us
  other arithmetic: 6.63 us -> 5.93 us
  Pallas kernels: 11.4 us -> 12.1 us
    ppermute x0 -> x2, waiting for transfers between devices: none -> 4.5 us  [returned(): lax.ppermute(value[1], ('tok', 'row'), across)]
    ppermute x4, waiting for transfers between devices: 8.04 us -> 4.85 us  [by_row(): return lax.ppermute(value, 'row', [(0, 1), (1, 0)])]
    ppermute x6 -> x5, starting transfers between devices: 11.5 us -> 14.4 us  [along_tok(): return lax.ppermute(value, 'tok', pairs)]
    ppermute x0 -> x2, starting transfers between devices: none -> 1.96 us  [returned(): lax.ppermute(value[1], ('tok', 'row'), across)]
    ppermute x6 -> x5, waiting for transfers between devices: 8.81 us -> 7.51 us  [along_tok(): return lax.ppermute(value, 'tok', pairs)]
    pallas_call x2 -> x3, Pallas kernels: 3.55 us -> 4.38 us  [the longest x1 1.87 us: per_device(): on_place(lambda *refs: own_block_kernel(scale, *refs), part_shapes, 2)]
  transfers between devices with their start and end apart: 17 -> 18, of which waited for: 10 -> 8; matrix products, arithmetic and copies ran while one was open for 16% -> 15% of each run, Pallas kernels for 10% -> 8%
where the time goes in v9:
time: 69.5 us; the launch traced here: 69.2 us
  starting transfers between devices  29.3 us (42%)
  waiting for transfers between devices  17.2 us (25%)
  Pallas kernels  12.1 us (17%)
  other arithmetic  5.93 us (9%)
  local copies, waits for them, and re-layouts  4.41 us (6%)
    ppermute x5, starting transfers between devices, along_tok(): return lax.ppermute(value, 'tok', pairs)  14.4 us
    ppermute x5, waiting for transfers between devices, along_tok(): return lax.ppermute(value, 'tok', pairs)  7.51 us
    ppermute x4, starting transfers between devices, by_row(): return lax.ppermute(value, 'row', [(0, 1), (1, 0)])  5.97 us
    ppermute x4, waiting for transfers between devices, by_row(): return lax.ppermute(value, 'row', [(0, 1), (1, 0)])  4.85 us
    ppermute x1, starting transfers between devices, per_device(): lax.ppermute(activations, ('row', 'col'), [(r * 4 + c, c // 2 * 4 + 2 * (...  4.75 us
    ppermute x2, waiting for transfers between devices, returned(): lax.ppermute(value[1], ('tok', 'row'), across)  4.5 us
    unnamed x3, local copies, waits for them, and re-layouts  3.97 us
    pallas_call x1, Pallas kernels, per_device(): pl.pallas_call(project_kernel, out_shape=(partial_sums, partial_sums), in...  3.65 us
  transfers between devices with their start and end apart: 18, of which 8 were waited for; matrix products, arithmetic and copies ran while one was open for 15% of the time, Pallas kernels for 8%

profile of v9, /device:TPU:0, one launch (start us, length us, event | category | flops | bytes accessed | tf_op | source)
XLA Modules:
  0.0 69.2 jit_solution(6253760275177272913)
XLA Ops:
  0.0 1.6 %collective-permute-start = (bf16[176,1024]{1,0:T(8,128)(2,1)}, bf16[176,1024]{1,0:T(8,128)(2,1)S(1)}, u32[]{:S(2)}, u32[]{:S(2)}) collective-permute-start(bf16[176,1024]{1,0:T(8,128)(2,1)} %param.4), channel_id=1, source_target_pairs={{0,0},{1,1},{2,4},{3,5},{4,2},{5,3},{6,6},{7,7},{8,8},{9,9},{10,12... | collective-permute-start | bytes 1081352 | tf_op jit(solution)/shard_map/ppermute | solution.py:351
  1.6 4.8 %collective-permute-start.1 = (bf16[176,1024]{1,0:T(8,128)(2,1)}, bf16[176,1024]{1,0:T(8,128)(2,1)S(1)}, u32[]{:S(2)}, u32[]{:S(2)}) collective-permute-start(bf16[176,1024]{1,0:T(8,128)(2,1)} %param.4), channel_id=1, source_target_pairs={{0,2},{1,3},{2,6},{3,7},{4,0},{5,1},{6,4},{7,5},{8,10},{9,11},{10,... | collective-permute-start | bytes 1081352 | tf_op jit(solution)/shard_map/ppermute | solution.py:356
  6.4 1.2 %multiply_reduce_fusion = f32[176]{0:T(256)S(1)} fusion(bf16[176,1024]{1,0:T(8,128)(2,1)} %param.4), kind=kLoop, calls=%fused_computation | loop fusion | flops 540496 | bytes 361152 | tf_op jit(solution)/shard_map/reduce_sum | solution.py:362
  7.6 0.7 convert_element_type.54
  8.2 0.1 pad_maximum_fusion.2
  8.3 0.7 convert_add_fusion
  9.0 0.7 %fusion = (f32[352,64]{1,0:T(8,128)S(1)}, f32[352,64]{1,0:T(8,128)S(1)}, f32[352,64]{1,0:T(8,128)S(1)}) fusion(f32[64]{0:T(128)S(1)} %negate_power_fusion, f32[352]{0:T(512)S(1)} %add_convert_fusion.2), kind=kLoop, calls=%fused_computation.7 | loop fusion | flops 45056 | bytes 272000 | tf_op jit(solution)/shard_map/neg | solution.py:26
  9.7 0.2 pad_maximum_fusion
  10.0 0.8 %slice_select_fusion = (f32[1024]{0:T(1024)S(1)}, f32[1024]{0:T(1024)S(1)}) fusion(f32[1200]{0:T(1024)S(1)} %collective-permute-done.2, bf16[1024]{0:T(1024)(128)(2,1)} %param.5, pred[]{:T(512)S(6)} %eq.19), kind=kLoop, calls=%fused_computation.17 | loop fusion | flops 3072 | bytes 14337 | tf_op jit(solution)/shard_map/jit(_where)/select_n | solution.py:349
  10.7 0.1 concatenate.37
  10.8 0.1 pad_add_fusion.1.place_ref
  10.9 4.0 %copy.6 = bf16[256,8,4,384]{3,1,2,0:T(8,128)(2,1)S(1)} copy(bf16[256,8,4,384]{3,2,1,0:T(4,128)(2,1)} %bitcast.27) | data formatting | bytes 12582912
  14.9 0.1 slice.52
  15.0 0.1 pad_maximum_fusion.3
  15.1 2.0 %collective-permute-start.6 = (f32[352]{0:T(512)S(1)}, f32[352]{0:T(512)S(1)}, u32[]{:S(2)}, u32[]{:S(2)}) collective-permute-start(f32[352]{0:T(512)S(1)} %pad_maximum_fusion.3), channel_id=1, source_target_pairs={{0,4},{4,0},{1,5},{5,1},{2,6},{6,2},{3,7},{7,3},{8,12},{12,8},{9,1... | collective-permute-start | bytes 4232 | tf_op jit(solution)/shard_map/ppermute | solution.py:345
  17.0 0.5 collective-permute-start.5
  17.6 1.1 %collective-permute-done.6 = f32[352]{0:T(512)S(1)} collective-permute-done((f32[352]{0:T(512)S(1)}, f32[352]{0:T(512)S(1)}, u32[]{:S(2)}, u32[]{:S(2)}) %collective-permute-start.6) | collective-permute-done | bytes 1440 | tf_op jit(solution)/shard_map/ppermute | solution.py:345
  18.7 0.1 broadcast_select_fusion.2
  18.7 0.1 pad_maximum_fusion.4
  18.8 0.1 reshape.70.squares_ref
  18.9 0.3 collective-permute-done.5.b_far
  19.2 2.7 %shard_map.46 = (f32[1088,128]{1,0:T(8,128)S(1)}, f32[1088,128]{1,0:T(8,128)S(1)}, bf16[2,352,1024]{2,1,0:T(8,128)(2,1)S(1)}, bf16[2048,768]{1,0:T(8,128)(2,1)}) custom-call(s32[4]{0:T(128)S(1)} %pad_add_fusion.1.place_ref, bf16[176,1024]{1,0:T(8,128)(2,1)S(1)} %collective-permute-done.a_near, bf16[176,1024]{1,0:T(8,128)(2,1)S(1)} %collective-permute-done.1.a_far, ...), custom_call_target="tpu_custom_call" | custom-call | tf_op jit(solution)/shard_map/pallas_call | solution.py:388
  22.0 1.8 %collective-permute-start.7 = (f16[1088,128]{1,0:T(8,128)(2,1)S(1)}, f16[1088,128]{1,0:T(8,128)(2,1)}, u32[]{:S(2)}, u32[]{:S(2)}) collective-permute-start(f16[1088,128]{1,0:T(8,128)(2,1)S(1)} %convert_element_type.58), channel_id=1, source_target_pairs={{0,4},{4,0},{1,5},{5,1},{2,6},{6,2},{3,7},{7,3},{8,12},{12,8},{9,1... | collective-permute-start | bytes 835592 | tf_op jit(solution)/shard_map/ppermute | solution.py:345
  23.7 0.1 fusion.1.docs_ref
  23.8 0.4 collective-permute-start.8
  24.2 3.7 %shard_map.47 = (f32[1088,128]{1,0:T(8,128)S(1)}, f32[1088,128]{1,0:T(8,128)S(1)}) custom-call(bf16[2,352,1024]{2,1,0:T(8,128)(2,1)S(1)} %get-tuple-element.28.normed_ref, f32[16,128]{1,0:T(8,128)S(1)} %fusion.1.docs_ref, f32[352,128]{1,0:T(8,128)S(1)} %get-tuple-element.56.cos_ref, f32[352,128]{1,0:T(8,128)S(1)} %get-tuple-element.57.sin_ref, ...), custom_call_target="tpu_custom_call" | custom-call | tf_op jit(solution)/shard_map/pallas_call | solution.py:406
  27.9 3.7 %collective-permute-done.7 = f16[1088,128]{1,0:T(8,128)(2,1)} collective-permute-done((f16[1088,128]{1,0:T(8,128)(2,1)S(1)}, f16[1088,128]{1,0:T(8,128)(2,1)}, u32[]{:S(2)}, u32[]{:S(2)}) %collective-permute-start.7) | collective-permute-done | bytes 278560 | tf_op jit(solution)/shard_map/ppermute | solution.py:345
  31.6 1.0 %add_convert_fusion.1.refs_1_.refs_4_.refs_3_ = bf16[1088,128]{1,0:T(8,128)(2,1)S(1)} fusion(f32[1088,128]{1,0:T(8,128)S(1)} %get-tuple-element.30, f16[1088,128]{1,0:T(8,128)(2,1)} %collective-permute-done.7), kind=kLoop, calls=%fused_computation.2 | loop fusion | flops 417792 | bytes 1114112 | tf_op jit(solution)/shard_map/convert_element_type | solution.py:423
  32.7 0.1 collective-permute-start.9
  32.8 0.1 constant_dynamic-slice_fusion.1
  32.9 0.7 collective-permute-start.10
  33.6 4.3 %collective-permute-start.11 = (bf16[720,128]{1,0:T(8,128)(2,1)S(1)}, bf16[720,128]{1,0:T(8,128)(2,1)S(1)}, u32[]{:S(2)}, u32[]{:S(2)}) collective-permute-start(bf16[720,128]{1,0:T(8,128)(2,1)S(1)} %get-tuple-element.39), channel_id=1, source_target_pairs={{0,16},{24,8},{8,0},{16,24},{1,17},{25,9},{9,1},{17,25},{2,18},{26... | collective-permute-start | bytes 552968 | tf_op jit(solution)/shard_map/ppermute | solution.py:443
  37.9 0.1 add_convert_fusion.refs_2_.refs_5_.refs_4_
  38.1 0.4 collective-permute-start.12
  38.5 0.1 pad_add_fusion.refs_0_.place_ref
  38.6 1.9 %shard_map.48 = (f32[2,352,128]{2,1,0:T(8,128)S(1)}, f32[2,352,1]{2,1,0:T(8,128)S(1)}) custom-call(s32[2]{0:T(128)S(1)} %pad_add_fusion.refs_0_.place_ref, bf16[1088,128]{1,0:T(8,128)(2,1)S(1)} %add_convert_fusion.1.refs_1_.refs_4_.refs_3_, bf16[1088,128]{1,0:T(8,128)(2,1)S(1)} %add_convert_fusion.refs_2_.refs_5_.refs_4_), custom_call_target="tpu_custom_call" | custom-call | tf_op jit(solution)/shard_map/pallas_call | solution.py:479
  40.4 3.0 %collective-permute-done.11.refs_2_.refs_6_ = bf16[720,128]{1,0:T(8,128)(2,1)S(1)} collective-permute-done((bf16[720,128]{1,0:T(8,128)(2,1)S(1)}, bf16[720,128]{1,0:T(8,128)(2,1)S(1)}, u32[]{:S(2)}, u32[]{:S(2)}) %collective-permute-start.11) | collective-permute-done | bytes 184352 | tf_op jit(solution)/shard_map/ppermute | solution.py:443
  43.4 3.5 %collective-permute-done.12.refs_3_.refs_7_ = bf16[720,128]{1,0:T(8,128)(2,1)S(1)} collective-permute-done((bf16[720,128]{1,0:T(8,128)(2,1)S(1)}, bf16[720,128]{1,0:T(8,128)(2,1)S(1)}, u32[]{:S(2)}, u32[]{:S(2)}) %collective-permute-start.12) | collective-permute-done | bytes 184352 | tf_op jit(solution)/shard_map/ppermute | solution.py:443
  47.0 1.4 %shard_map.49.refs_8_ = bf16[2,2,192,128]{3,2,1,0:T(8,128)(2,1)S(1)} custom-call(s32[2]{0:T(128)S(1)} %pad_add_fusion.refs_0_.place_ref, bf16[720,128]{1,0:T(8,128)(2,1)S(1)} %collective-permute-done.10.refs_1_.refs_5_, bf16[720,128]{1,0:T(8,128)(2,1)S(1)} %collective-permute-done.11.refs_2_.refs_6_, ...), custom_call_target="tpu_custom_call" | custom-call | tf_op jit(solution)/shard_map/pallas_call | solution.py:483
  48.3 0.7 %shard_map.50 = (f32[2,176,128]{2,1,0:T(8,128)S(1)}, f32[2,176,1]{2,1,0:T(8,128)S(1)}, bf16[2,192,128]{2,1,0:T(8,128)(2,1)S(1)}) custom-call(s32[2]{0:T(128)S(1)} %pad_add_fusion.refs_0_.place_ref, f32[2,352,128]{2,1,0:T(8,128)S(1)} %get-tuple-element.34.refs_1_, f32[2,352,1]{2,1,0:T(8,128)S(1)} %get-tuple-element.35.refs_6_.refs_2_, ...), custom_call_target="tpu_custom_call" | custom-call | tf_op jit(solution)/shard_map/pallas_call | solution.py:503
  49.1 1.9 %collective-permute-start.13 = (bf16[2,192,128]{2,1,0:T(8,128)(2,1)S(1)}, bf16[2,192,128]{2,1,0:T(8,128)(2,1)S(1)}, u32[]{:S(2)}, u32[]{:S(2)}) collective-permute-start(bf16[2,192,128]{2,1,0:T(8,128)(2,1)S(1)} %get-tuple-element.38), channel_id=1, source_target_pairs={{0,4},{4,0},{1,5},{5,1},{2,6},{6,2},{3,7},{7,3},{8,12},{12,8},{9,1... | collective-permute-start | bytes 294920 | tf_op jit(solution)/shard_map/ppermute | solution.py:345
  51.0 0.7 collective-permute-start.14
  51.6 0.7 collective-permute-start.15
  52.3 8.3 %collective-permute-start.16 = (bf16[192,128]{1,0:T(8,128)(2,1)S(1)}, bf16[192,128]{1,0:T(8,128)(2,1)S(1)}, u32[]{:S(2)}, u32[]{:S(2)}) collective-permute-start(bf16[192,128]{1,0:T(8,128)(2,1)S(1)} %get-tuple-element.42), channel_id=1, source_target_pairs={{0,8},{8,16},{16,24},{24,0},{1,9},{9,17},{17,25},{25,1},{2,10},{10... | collective-permute-start | bytes 147464 | tf_op jit(solution)/shard_map/ppermute | solution.py:443
  60.6 1.3 %collective-permute-start.17 = (bf16[192,128]{1,0:T(8,128)(2,1)S(1)}, bf16[192,128]{1,0:T(8,128)(2,1)S(1)}, u32[]{:S(2)}, u32[]{:S(2)}) collective-permute-start(bf16[192,128]{1,0:T(8,128)(2,1)S(1)} %get-tuple-element.41), channel_id=1, source_target_pairs={{0,12},{4,8},{8,20},{12,16},{16,28},{20,24},{24,4},{28,0},{1,13},{... | collective-permute-start | bytes 147464 | tf_op jit(solution)/shard_map/ppermute | solution.py:498
  61.9 1.0 %collective-permute-done.16.below_same = bf16[192,128]{1,0:T(8,128)(2,1)S(1)} collective-permute-done((bf16[192,128]{1,0:T(8,128)(2,1)S(1)}, bf16[192,128]{1,0:T(8,128)(2,1)S(1)}, u32[]{:S(2)}, u32[]{:S(2)}) %collective-permute-start.16) | collective-permute-done | bytes 49184 | tf_op jit(solution)/shard_map/ppermute | solution.py:443
  62.9 4.5 %collective-permute-done.17.below_cross = bf16[192,128]{1,0:T(8,128)(2,1)S(1)} collective-permute-done((bf16[192,128]{1,0:T(8,128)(2,1)S(1)}, bf16[192,128]{1,0:T(8,128)(2,1)S(1)}, u32[]{:S(2)}, u32[]{:S(2)}) %collective-permute-start.17) | collective-permute-done | bytes 49184 | tf_op jit(solution)/shard_map/ppermute | solution.py:498
  67.4 1.8 %shard_map.51 = bf16[176,512]{1,0:T(8,128)(2,1)} custom-call(s32[2]{0:T(128)S(1)} %pad_add_fusion.refs_0_.place_ref, f32[2,176,128]{2,1,0:T(8,128)S(1)} %get-tuple-element.36.mine_ref, f32[2,176,1]{2,1,0:T(8,128)S(1)} %get-tuple-element.37.logs_ref, bf16[2,192,128]{2,1,0:T(8,128)(2,1)S(1)} %collective-permute-done.13.partner_ref, ...), custom_call_target="tpu_custom_call" | custom-call | tf_op jit(solution)/shard_map/pallas_call | solution.py:514
  (27 shorter events, 0.3 us)
Async XLA Ops:
  0.0 14.9 %collective-permute-start = (bf16[176,1024]{1,0:T(8,128)(2,1)}, bf16[176,1024]{1,0:T(8,128)(2,1)S(1)}, u32[]{:S(2)}, u32[]{:S(2)}) collective-permute-start(bf16[176,1024]{1,0:T(8,128)(2,1)} %param.4), channel_id=1, source_target_pairs={{0,0},{1,1},{2,4},{3,5},{4,2},{5,3},{6,6},{7,7},{8,8},{9,9},{10,12... | collective-permute-start | bytes 1081352 | tf_op jit(solution)/shard_map/ppermute | solution.py:351
  1.6 13.3 %collective-permute-start.1 = (bf16[176,1024]{1,0:T(8,128)(2,1)}, bf16[176,1024]{1,0:T(8,128)(2,1)S(1)}, u32[]{:S(2)}, u32[]{:S(2)}) collective-permute-start(bf16[176,1024]{1,0:T(8,128)(2,1)} %param.4), channel_id=1, source_target_pairs={{0,2},{1,3},{2,6},{3,7},{4,0},{5,1},{6,4},{7,5},{8,10},{9,11},{10,... | collective-permute-start | bytes 1081352 | tf_op jit(solution)/shard_map/ppermute | solution.py:356
  8.3 1.6 %collective-permute-start.2 = (f32[1200]{0:T(1024)S(1)}, f32[1200]{0:T(1024)S(1)}, u32[]{:S(2)}, u32[]{:S(2)}) collective-permute-start(f32[1200]{0:T(1024)S(1)} %pad_maximum_fusion.2), channel_id=1, source_target_pairs={{0,1},{1,0},{2,3},{3,2},{4,5},{5,4},{6,7},{7,6},{8,9},{9,8},{10,11... | collective-permute-start | bytes 14408 | tf_op jit(solution)/shard_map/ppermute | solution.py:342
  10.8 4.1 %collective-permute-start.3 = (f32[2224]{0:T(1024)S(1)}, f32[2224]{0:T(1024)S(1)}, u32[]{:S(2)}, u32[]{:S(2)}) collective-permute-start(f32[2224]{0:T(1024)S(1)} %concatenate.37), channel_id=1, source_target_pairs={{0,2},{1,3},{2,0},{3,1},{4,6},{5,7},{6,4},{7,5},{8,10},{9,11},{10,... | collective-permute-start | bytes 26696 | tf_op jit(solution)/shard_map/ppermute | solution.py:342
  10.9 7.8 %copy-start = (s32[176]{0:T(256)S(1)}, s32[176]{0:T(256)}, u32[]{:S(2)}) copy-start(s32[176]{0:T(256)} %param.7) | copy-start | bytes 2116
  15.1 3.6 %collective-permute-start.6 = (f32[352]{0:T(512)S(1)}, f32[352]{0:T(512)S(1)}, u32[]{:S(2)}, u32[]{:S(2)}) collective-permute-start(f32[352]{0:T(512)S(1)} %pad_maximum_fusion.3), channel_id=1, source_target_pairs={{0,4},{4,0},{1,5},{5,1},{2,6},{6,2},{3,7},{7,3},{8,12},{12,8},{9,1... | collective-permute-start | bytes 4232 | tf_op jit(solution)/shard_map/ppermute | solution.py:345
  17.0 1.9 %collective-permute-start.4 = (bf16[176,1024]{1,0:T(8,128)(2,1)S(1)}, bf16[176,1024]{1,0:T(8,128)(2,1)S(1)}, u32[]{:S(2)}, u32[]{:S(2)}) collective-permute-start(bf16[176,1024]{1,0:T(8,128)(2,1)S(1)} %collective-permute-done.a_near), channel_id=1, source_target_pairs={{0,1},{1,0},{2,3},{3,2},{4,5},{5,4},{6,7},{7,6},{8,9},{9,8},{10,11... | collective-permute-start | bytes 1081352 | tf_op jit(solution)/shard_map/ppermute | solution.py:342
  17.0 2.2 %collective-permute-start.5 = (bf16[176,1024]{1,0:T(8,128)(2,1)S(1)}, bf16[176,1024]{1,0:T(8,128)(2,1)S(1)}, u32[]{:S(2)}, u32[]{:S(2)}) collective-permute-start(bf16[176,1024]{1,0:T(8,128)(2,1)S(1)} %collective-permute-done.1.a_far), channel_id=1, source_target_pairs={{0,1},{1,0},{2,3},{3,2},{4,5},{5,4},{6,7},{7,6},{8,9},{9,8},{10,11... | collective-permute-start | bytes 1081352 | tf_op jit(solution)/shard_map/ppermute | solution.py:342
  22.0 9.7 %collective-permute-start.7 = (f16[1088,128]{1,0:T(8,128)(2,1)S(1)}, f16[1088,128]{1,0:T(8,128)(2,1)}, u32[]{:S(2)}, u32[]{:S(2)}) collective-permute-start(f16[1088,128]{1,0:T(8,128)(2,1)S(1)} %convert_element_type.58), channel_id=1, source_target_pairs={{0,4},{4,0},{1,5},{5,1},{2,6},{6,2},{3,7},{7,3},{8,12},{12,8},{9,1... | collective-permute-start | bytes 835592 | tf_op jit(solution)/shard_map/ppermute | solution.py:345
  23.8 14.1 %collective-permute-start.8 = (f16[1088,128]{1,0:T(8,128)(2,1)S(1)}, f16[1088,128]{1,0:T(8,128)(2,1)S(1)}, u32[]{:S(2)}, u32[]{:S(2)}) collective-permute-start(f16[1088,128]{1,0:T(8,128)(2,1)S(1)} %convert_element_type.61), channel_id=1, source_target_pairs={{0,4},{4,0},{1,5},{5,1},{2,6},{6,2},{3,7},{7,3},{8,12},{12,8},{9,1... | collective-permute-start | bytes 835592 | tf_op jit(solution)/shard_map/ppermute | solution.py:345
  32.7 5.2 %collective-permute-start.9 = (bf16[16,128]{1,0:T(8,128)(2,1)S(1)}, bf16[16,128]{1,0:T(8,128)(2,1)S(1)}, u32[]{:S(2)}, u32[]{:S(2)}) collective-permute-start(bf16[16,128]{1,0:T(8,128)(2,1)S(1)} %slice.63), channel_id=1, source_target_pairs={{0,1},{1,0},{2,3},{3,2},{4,5},{5,4},{6,7},{7,6},{8,9},{9,8},{10,11... | collective-permute-start | bytes 12296 | tf_op jit(solution)/shard_map/ppermute | solution.py:342
  32.9 7.6 %collective-permute-start.10 = (bf16[720,128]{1,0:T(8,128)(2,1)S(1)}, bf16[720,128]{1,0:T(8,128)(2,1)S(1)}, u32[]{:S(2)}, u32[]{:S(2)}) collective-permute-start(bf16[720,128]{1,0:T(8,128)(2,1)S(1)} %get-tuple-element.40), channel_id=1, source_target_pairs={{8,16},{16,8},{0,0},{24,24},{9,17},{17,9},{1,1},{25,25},{10,18},{1... | collective-permute-start | bytes 552968 | tf_op jit(solution)/shard_map/ppermute | solution.py:443
  33.6 9.9 %collective-permute-start.11 = (bf16[720,128]{1,0:T(8,128)(2,1)S(1)}, bf16[720,128]{1,0:T(8,128)(2,1)S(1)}, u32[]{:S(2)}, u32[]{:S(2)}) collective-permute-start(bf16[720,128]{1,0:T(8,128)(2,1)S(1)} %get-tuple-element.39), channel_id=1, source_target_pairs={{0,16},{24,8},{8,0},{16,24},{1,17},{25,9},{9,1},{17,25},{2,18},{26... | collective-permute-start | bytes 552968 | tf_op jit(solution)/shard_map/ppermute | solution.py:443
  38.1 8.9 %collective-permute-start.12 = (bf16[720,128]{1,0:T(8,128)(2,1)S(1)}, bf16[720,128]{1,0:T(8,128)(2,1)S(1)}, u32[]{:S(2)}, u32[]{:S(2)}) collective-permute-start(bf16[720,128]{1,0:T(8,128)(2,1)S(1)} %constant_dynamic-slice_fusion), channel_id=1, source_target_pairs={{0,8},{8,0},{16,24},{24,16},{1,9},{9,1},{17,25},{25,17},{2,10},{10... | collective-permute-start | bytes 552968 | tf_op jit(solution)/shard_map/ppermute | solution.py:443
  49.1 18.3 %collective-permute-start.13 = (bf16[2,192,128]{2,1,0:T(8,128)(2,1)S(1)}, bf16[2,192,128]{2,1,0:T(8,128)(2,1)S(1)}, u32[]{:S(2)}, u32[]{:S(2)}) collective-permute-start(bf16[2,192,128]{2,1,0:T(8,128)(2,1)S(1)} %get-tuple-element.38), channel_id=1, source_target_pairs={{0,4},{4,0},{1,5},{5,1},{2,6},{6,2},{3,7},{7,3},{8,12},{12,8},{9,1... | collective-permute-start | bytes 294920 | tf_op jit(solution)/shard_map/ppermute | solution.py:345
  51.0 10.9 %collective-permute-start.14 = (bf16[192,128]{1,0:T(8,128)(2,1)S(1)}, bf16[192,128]{1,0:T(8,128)(2,1)S(1)}, u32[]{:S(2)}, u32[]{:S(2)}) collective-permute-start(bf16[192,128]{1,0:T(8,128)(2,1)S(1)} %get-tuple-element.44), channel_id=1, source_target_pairs={{0,0},{8,24},{16,16},{24,8},{1,1},{9,25},{17,17},{25,9},{2,2},{10,... | collective-permute-start | bytes 147464 | tf_op jit(solution)/shard_map/ppermute | solution.py:443
  51.6 10.3 %collective-permute-start.15 = (bf16[192,128]{1,0:T(8,128)(2,1)S(1)}, bf16[192,128]{1,0:T(8,128)(2,1)S(1)}, u32[]{:S(2)}, u32[]{:S(2)}) collective-permute-start(bf16[192,128]{1,0:T(8,128)(2,1)S(1)} %get-tuple-element.43), channel_id=1, source_target_pairs={{0,0},{4,4},{8,28},{12,24},{16,16},{20,20},{24,12},{28,8},{1,1},{5... | collective-permute-start | bytes 147464 | tf_op jit(solution)/shard_map/ppermute | solution.py:498
  52.3 10.6 %collective-permute-start.16 = (bf16[192,128]{1,0:T(8,128)(2,1)S(1)}, bf16[192,128]{1,0:T(8,128)(2,1)S(1)}, u32[]{:S(2)}, u32[]{:S(2)}) collective-permute-start(bf16[192,128]{1,0:T(8,128)(2,1)S(1)} %get-tuple-element.42), channel_id=1, source_target_pairs={{0,8},{8,16},{16,24},{24,0},{1,9},{9,17},{17,25},{25,1},{2,10},{10... | collective-permute-start | bytes 147464 | tf_op jit(solution)/shard_map/ppermute | solution.py:443
  60.6 6.8 %collective-permute-start.17 = (bf16[192,128]{1,0:T(8,128)(2,1)S(1)}, bf16[192,128]{1,0:T(8,128)(2,1)S(1)}, u32[]{:S(2)}, u32[]{:S(2)}) collective-permute-start(bf16[192,128]{1,0:T(8,128)(2,1)S(1)} %get-tuple-element.41), channel_id=1, source_target_pairs={{0,12},{4,8},{8,20},{12,16},{16,28},{20,24},{24,4},{28,0},{1,13},{... | collective-permute-start | bytes 147464 | tf_op jit(solution)/shard_map/ppermute | solution.py:498

commit v10 on v8

--- a/solution.py
+++ b/solution.py
@@ -184,8 +184,24 @@
     )
 
 
+def joined(first, second):
+    (output, logs), (other, other_logs) = first, second
+    top = jnp.maximum(logs, other_logs)
+    weight, other_weight = jnp.exp(logs - top), jnp.exp(other_logs - top)
+    total = weight + other_weight
+    return (output * weight + other * other_weight) / total, top + jnp.log(total)
+
+
+def own_block_kernel(scale, place_ref, chunk_one, chunk_two, out_ref, logs_ref):
+    for index, (queries, keys) in enumerate(((chunk_one, chunk_two), (chunk_two, chunk_one))):
+        height = keys.shape[0] - out_ref.shape[1] - EXTRA
+        out_ref[index], logs_ref[index] = softmax_part(
+            scale, queries[height:, :], [(keys[:height, :], True)], True
+        )
+
+
 def guest_kernel(
-    scale, place_ref, two_away, swapped, neighbour, chunk_one, chunk_two, out_ref
+    scale, place_ref, two_away, swapped, neighbour, chunk_one, chunk_two, unused_ref, out_ref
 ):
     height, size = neighbour.shape
     begin = (height - EXTRA) // 2
@@ -209,38 +225,42 @@
         attend(0, neighbour[begin:, :], [two_away[...], swapped[...], chunk_one[:height, :]])
 
 
-def own_kernel(
-    scale, place_ref, chunk_one, chunk_two, two_away, swapped, neighbour, unused_ref, out_ref,
-    logs_ref,
+def own_rest_kernel(
+    scale, place_ref, own_out, own_logs, chunk_one, chunk_two, two_away, swapped, neighbour,
+    unused_ref, out_ref, logs_ref,
 ):
     tok = place_ref[0]
     height = neighbour.shape[0]
-    down = [(chunk_two[:height, :], True), (neighbour[...], (tok == 1) | (tok == 3))]
-    up = [(chunk_one[:height, :], True), (swapped[...], tok == 2), (two_away[...], tok == 2)]
-    for index, (query, messages) in enumerate(
-        ((chunk_one[height:, :], down), (chunk_two[height:, :], up))
-    ):
-        out_ref[index], logs_ref[index] = softmax_part(scale, query, messages, True)
+    out_ref[...] = own_out[...]
+    logs_ref[...] = own_logs[...]
+
+    def add(index, query, messages):
+        part = softmax_part(scale, query, [(m, True) for m in messages], False)
+        out_ref[index], logs_ref[index] = joined((own_out[index], own_logs[index]), part)
+
+    @pl.when((tok == 1) | (tok == 3))
+    def down():
+        add(0, chunk_one[height:, :], [neighbour[...]])
+
+    @pl.when(tok == 2)
+    def up():
+        add(1, chunk_two[height:, :], [swapped[...], two_away[...]])
 
 
 def merge_kernel(
-    place_ref, out_ref, logs_ref, two_below_ref, one_ref, below_ref, mine_ref, theirs_ref
+    place_ref, out_ref, logs_ref, two_below_ref, below_ref, mine_ref, theirs_ref
 ):
     block, size = out_ref.shape[1:]
     tok, row = place_ref[0], place_ref[1]
-    at_two, at_three = tok == 2, tok == 3
-
-    def joined(index, message, present):
-        logs = logs_ref[index]
-        guest = jnp.where(present, logs_of(message, block), LOW)
-        top = jnp.maximum(logs, guest)
-        weight, guest_weight = jnp.exp(logs - top), jnp.exp(guest - top)
-        guest_output = jnp.where(present, message[:block].astype(jnp.float32), 0.0)
-        output = out_ref[index] * weight + guest_output * guest_weight
-        return (output / (weight + guest_weight)).astype(jnp.bfloat16)
-
-    down = joined(0, jnp.where(at_two, one_ref[...], two_below_ref[...]), at_two | at_three)
-    up = joined(1, below_ref[...], (tok == 1) | at_three)
+
+    def with_guest(index, message, present):
+        guest = jnp.where(present, message[:block].astype(jnp.float32), 0.0)
+        guest_logs = jnp.where(present, logs_of(message, block), LOW)
+        output, logs = joined((out_ref[index], logs_ref[index]), (guest, guest_logs))
+        return output.astype(jnp.bfloat16)
+
+    down = with_guest(0, jnp.where(tok == 2, below_ref[...], two_below_ref[...]), tok >= 2)
+    up = with_guest(1, below_ref[...], (tok == 1) | (tok == 3))
     for index, output in enumerate((down, up)):
         columns = slice(index * size, (index + 1) * size)
         mine_ref[:, columns], theirs_ref[:, columns] = parted(row, output)
@@ -434,30 +454,30 @@
         neighbour = along_tok(
             keys_or_query(chunk_two, (tok & 1) == 1), [(0, 1), (1, 0), (2, 3), (3, 2)]
         )
+        part_shapes = (
+            jax.ShapeDtypeStruct((2, block, size), jnp.float32),
+            jax.ShapeDtypeStruct((2, block, 1), jnp.float32),
+        )
+        own_out, own_logs = on_place(
+            lambda *refs: own_block_kernel(scale, *refs), part_shapes, 2
+        )(places, chunk_one, chunk_two)
         guests = on_place(
             lambda *refs: guest_kernel(scale, *refs),
             jax.ShapeDtypeStruct((2, block + EXTRA, size), jnp.bfloat16),
-            5,
-        )(places, two_away, swapped, neighbour, chunk_one, chunk_two)
-        from_two_below = along_tok(guests[1], [(t, t ^ 2) for t in range(4)])
-        from_one = along_tok(guests[0], [(t, t ^ 3) for t in range(4)])
-        from_below = along_tok(guests[0], [(t, t ^ 1) for t in range(4)])
-        output, logs = on_place(
-            lambda *refs: own_kernel(scale, *refs),
-            (
-                jax.ShapeDtypeStruct((2, block, size), jnp.float32),
-                jax.ShapeDtypeStruct((2, block, 1), jnp.float32),
-            ),
             6,
             1,
-        )(places, chunk_one, chunk_two, two_away, swapped, neighbour, guests)
+        )(places, two_away, swapped, neighbour, chunk_one, chunk_two, own_logs)
+        from_two_below = along_tok(guests[1], [(1, 3), (0, 1), (2, 0), (3, 2)])
+        from_below = along_tok(guests[0], [(0, 1), (1, 2), (2, 3), (3, 0)])
+        output, logs = on_place(
+            lambda *refs: own_rest_kernel(scale, *refs), part_shapes, 8, 1
+        )(places, own_out, own_logs, chunk_one, chunk_two, two_away, swapped, neighbour, guests)
         half = jax.ShapeDtypeStruct((rows, pair * size), jnp.bfloat16)
-        mine, theirs = on_place(merge_kernel, (half, half), 5)(
-            places, output, logs, from_two_below, from_one, from_below
+        mine, theirs = on_place(merge_kernel, (half, half), 4)(
+            places, output, logs, from_two_below, from_below
         )
     else:
         mine, theirs = gathered_attention()
-
     theirs = by_row(theirs)
     return jnp.concatenate(
         [jnp.where(row == 0, mine, theirs), jnp.where(row == 0, theirs, mine)], axis=1

time: 64.7 us -> 62.3 us (0.963)
  starting transfers between devices: 24.4 us -> 22.1 us
    ppermute x6 -> x5, starting transfers between devices: 11.5 us -> 9.17 us  [along_tok(): return lax.ppermute(value, 'tok', pairs)]
    ppermute x6 -> x5, waiting for transfers between devices: 8.81 us -> 8.89 us  [along_tok(): return lax.ppermute(value, 'tok', pairs)]
    pallas_call x2 -> x3, Pallas kernels: 3.55 us -> 3.53 us  [the longest x1 1.87 us: per_device(): on_place(lambda *refs: own_block_kernel(scale, *refs), part_shapes, 2)]
  transfers between devices with their start and end apart: 17 -> 16, of which waited for: 10 -> 9; matrix products, arithmetic and copies ran while one was open for 16% -> 16% of each run, Pallas kernels for 10% -> 10%
where the time goes in v10:
time: 62.3 us; the launch traced here: 62 us
  starting transfers between devices  22.1 us (35%)
  waiting for transfers between devices  17.3 us (28%)
  Pallas kernels  11.2 us (18%)
  other arithmetic  6.63 us (11%)
  local copies, waits for them, and re-layouts  4.41 us (7%)
    ppermute x5, starting transfers between devices, along_tok(): return lax.ppermute(value, 'tok', pairs)  9.17 us
    ppermute x5, waiting for transfers between devices, along_tok(): return lax.ppermute(value, 'tok', pairs)  8.89 us
    ppermute x4, waiting for transfers between devices, by_row(): return lax.ppermute(value, 'row', [(0, 1), (1, 0)])  8.05 us
    ppermute x4, starting transfers between devices, by_row(): return lax.ppermute(value, 'row', [(0, 1), (1, 0)])  5.97 us
    ppermute x1, starting transfers between devices, per_device(): lax.ppermute(activations, ('row', 'col'), [(r * 4 + c, c // 2 * 4 + 2 * (...  4.75 us
    unnamed x3, local copies, waits for them, and re-layouts  3.97 us
    pallas_call x1, Pallas kernels, per_device(): pl.pallas_call(project_kernel, out_shape=(partial_sums, partial_sums), in...  3.65 us
    pallas_call x1, Pallas kernels, per_device(): pl.pallas_call(normalise_project_kernel, out_shape=(partial_sums, partial...  2.68 us
  transfers between devices with their start and end apart: 16, of which 9 were waited for; matrix products, arithmetic and copies ran while one was open for 16% of the time, Pallas kernels for 10%

profile of v10, /device:TPU:0, one launch (start us, length us, event | category | flops | bytes accessed | tf_op | source)
XLA Modules:
  0.0 62.0 jit_solution(13365723019584335723)
XLA Ops:
  0.0 1.6 %collective-permute-start = (bf16[176,1024]{1,0:T(8,128)(2,1)}, bf16[176,1024]{1,0:T(8,128)(2,1)S(1)}, u32[]{:S(2)}, u32[]{:S(2)}) collective-permute-start(bf16[176,1024]{1,0:T(8,128)(2,1)} %param.4), channel_id=1, source_target_pairs={{0,0},{1,1},{2,4},{3,5},{4,2},{5,3},{6,6},{7,7},{8,8},{9,9},{10,12... | collective-permute-start | bytes 1081352 | tf_op jit(solution)/shard_map/ppermute | solution.py:334
  1.6 4.8 %collective-permute-start.1 = (bf16[176,1024]{1,0:T(8,128)(2,1)}, bf16[176,1024]{1,0:T(8,128)(2,1)S(1)}, u32[]{:S(2)}, u32[]{:S(2)}) collective-permute-start(bf16[176,1024]{1,0:T(8,128)(2,1)} %param.4), channel_id=1, source_target_pairs={{0,2},{1,3},{2,6},{3,7},{4,0},{5,1},{6,4},{7,5},{8,10},{9,11},{10,... | collective-permute-start | bytes 1081352 | tf_op jit(solution)/shard_map/ppermute | solution.py:339
  6.4 1.2 %multiply_reduce_fusion = f32[176]{0:T(256)S(1)} fusion(bf16[176,1024]{1,0:T(8,128)(2,1)} %param.4), kind=kLoop, calls=%fused_computation | loop fusion | flops 540496 | bytes 361152 | tf_op jit(solution)/shard_map/reduce_sum | solution.py:345
  7.6 0.7 %convert_element_type.54 = f32[1024]{0:T(1024)S(1)} convert(bf16[1024]{0:T(1024)(128)(2,1)} %param.5) | non-fusion elementwise | flops 1024 | bytes 6144 | tf_op jit(solution)/shard_map/convert_element_type | solution.py:346
  8.2 0.1 pad_maximum_fusion.3
  8.3 0.7 %convert_add_fusion = f32[176]{0:T(256)S(1)} fusion(s32[176]{0:T(256)} %param.7), kind=kLoop, calls=%fused_computation.27 | loop fusion | flops 352 | bytes 1408 | tf_op jit(solution)/shard_map/add | solution.py:358
  9.0 0.7 %fusion = (f32[352,64]{1,0:T(8,128)S(1)}, f32[352,64]{1,0:T(8,128)S(1)}, f32[352,64]{1,0:T(8,128)S(1)}) fusion(f32[64]{0:T(128)S(1)} %negate_power_fusion, f32[352]{0:T(512)S(1)} %add_convert_fusion.2), kind=kLoop, calls=%fused_computation.12 | loop fusion | flops 45056 | bytes 272000 | tf_op jit(solution)/shard_map/neg | solution.py:26
  9.7 0.2 pad_maximum_fusion
  10.0 0.8 %slice_select_fusion = (f32[1024]{0:T(1024)S(1)}, f32[1024]{0:T(1024)S(1)}) fusion(f32[1200]{0:T(1024)S(1)} %collective-permute-done.2, bf16[1024]{0:T(1024)(128)(2,1)} %param.5, pred[]{:T(512)S(6)} %eq.22), kind=kLoop, calls=%fused_computation.18 | loop fusion | flops 3072 | bytes 14337 | tf_op jit(solution)/shard_map/jit(_where)/select_n | solution.py:332
  10.7 0.1 concatenate.40
  10.8 0.1 pad_add_fusion.1.place_ref
  10.9 4.0 %copy.6 = bf16[256,8,4,384]{3,1,2,0:T(8,128)(2,1)S(1)} copy(bf16[256,8,4,384]{3,2,1,0:T(4,128)(2,1)} %bitcast.23) | data formatting | bytes 12582912
  14.9 0.1 slice.36
  15.0 0.1 pad_maximum_fusion.4
  15.1 2.0 %collective-permute-start.6 = (f32[352]{0:T(512)S(1)}, f32[352]{0:T(512)S(1)}, u32[]{:S(2)}, u32[]{:S(2)}) collective-permute-start(f32[352]{0:T(512)S(1)} %pad_maximum_fusion.4), channel_id=1, source_target_pairs={{0,4},{4,0},{1,5},{5,1},{2,6},{6,2},{3,7},{7,3},{8,12},{12,8},{9,1... | collective-permute-start | bytes 4232 | tf_op jit(solution)/shard_map/ppermute | solution.py:328
  17.0 0.5 collective-permute-start.5
  17.6 1.1 %collective-permute-done.6 = f32[352]{0:T(512)S(1)} collective-permute-done((f32[352]{0:T(512)S(1)}, f32[352]{0:T(512)S(1)}, u32[]{:S(2)}, u32[]{:S(2)}) %collective-permute-start.6) | collective-permute-done | bytes 1440 | tf_op jit(solution)/shard_map/ppermute | solution.py:328
  18.7 0.1 broadcast_select_fusion.4
  18.7 0.1 pad_maximum_fusion.5
  18.8 0.1 reshape.62.squares_ref
  18.9 0.3 collective-permute-done.5.b_far
  19.2 2.7 %shard_map.46 = (f32[1088,128]{1,0:T(8,128)S(1)}, f32[1088,128]{1,0:T(8,128)S(1)}, bf16[2,352,1024]{2,1,0:T(8,128)(2,1)S(1)}, bf16[2048,768]{1,0:T(8,128)(2,1)}) custom-call(s32[4]{0:T(128)S(1)} %pad_add_fusion.1.place_ref, bf16[176,1024]{1,0:T(8,128)(2,1)S(1)} %collective-permute-done.a_near, bf16[176,1024]{1,0:T(8,128)(2,1)S(1)} %collective-permute-done.1.a_far, ...), custom_call_target="tpu_custom_call" | custom-call | tf_op jit(solution)/shard_map/pallas_call | solution.py:371
  22.0 1.8 %collective-permute-start.7 = (f16[1088,128]{1,0:T(8,128)(2,1)S(1)}, f16[1088,128]{1,0:T(8,128)(2,1)}, u32[]{:S(2)}, u32[]{:S(2)}) collective-permute-start(f16[1088,128]{1,0:T(8,128)(2,1)S(1)} %convert_element_type.58), channel_id=1, source_target_pairs={{0,4},{4,0},{1,5},{5,1},{2,6},{6,2},{3,7},{7,3},{8,12},{12,8},{9,1... | collective-permute-start | bytes 835592 | tf_op jit(solution)/shard_map/ppermute | solution.py:328
  23.7 0.1 fusion.1.docs_ref
  23.8 0.4 collective-permute-start.8
  24.2 3.7 %shard_map.47 = (f32[1088,128]{1,0:T(8,128)S(1)}, f32[1088,128]{1,0:T(8,128)S(1)}) custom-call(bf16[2,352,1024]{2,1,0:T(8,128)(2,1)S(1)} %get-tuple-element.29.normed_ref, f32[16,128]{1,0:T(8,128)S(1)} %fusion.1.docs_ref, f32[352,128]{1,0:T(8,128)S(1)} %get-tuple-element.58.cos_ref, f32[352,128]{1,0:T(8,128)S(1)} %get-tuple-element.59.sin_ref, ...), custom_call_target="tpu_custom_call" | custom-call | tf_op jit(solution)/shard_map/pallas_call | solution.py:389
  27.9 3.7 %collective-permute-done.7 = f16[1088,128]{1,0:T(8,128)(2,1)} collective-permute-done((f16[1088,128]{1,0:T(8,128)(2,1)S(1)}, f16[1088,128]{1,0:T(8,128)(2,1)}, u32[]{:S(2)}, u32[]{:S(2)}) %collective-permute-start.7) | collective-permute-done | bytes 278560 | tf_op jit(solution)/shard_map/ppermute | solution.py:328
  31.6 1.0 %add_convert_fusion.1.refs_1_.refs_4_.refs_3_ = bf16[1088,128]{1,0:T(8,128)(2,1)S(1)} fusion(f32[1088,128]{1,0:T(8,128)S(1)} %get-tuple-element.31, f16[1088,128]{1,0:T(8,128)(2,1)} %collective-permute-done.7), kind=kLoop, calls=%fused_computation.2 | loop fusion | flops 417792 | bytes 1114112 | tf_op jit(solution)/shard_map/convert_element_type | solution.py:406
  32.7 0.1 collective-permute-start.9
  32.8 0.1 constant_dynamic-slice_fusion.1
  32.9 2.6 %collective-permute-start.10 = (bf16[720,128]{1,0:T(8,128)(2,1)S(1)}, bf16[720,128]{1,0:T(8,128)(2,1)S(1)}, u32[]{:S(2)}, u32[]{:S(2)}) collective-permute-start(bf16[720,128]{1,0:T(8,128)(2,1)S(1)} %get-tuple-element.42), channel_id=1, source_target_pairs={{0,16},{24,8},{8,0},{16,24},{1,17},{25,9},{9,1},{17,25},{2,18},{26... | collective-permute-start | bytes 552968 | tf_op jit(solution)/shard_map/ppermute | solution.py:426
  35.5 0.7 %collective-permute-start.11 = (bf16[720,128]{1,0:T(8,128)(2,1)S(1)}, bf16[720,128]{1,0:T(8,128)(2,1)S(1)}, u32[]{:S(2)}, u32[]{:S(2)}) collective-permute-start(bf16[720,128]{1,0:T(8,128)(2,1)S(1)} %get-tuple-element.41), channel_id=1, source_target_pairs={{8,16},{16,8},{0,0},{24,24},{9,17},{17,9},{1,1},{25,25},{10,18},{1... | collective-permute-start | bytes 552968 | tf_op jit(solution)/shard_map/ppermute | solution.py:426
  36.2 0.5 collective-permute-done.8
  36.7 0.1 add_convert_fusion.refs_2_.refs_5_.refs_4_
  36.8 3.0 %collective-permute-start.12 = (bf16[720,128]{1,0:T(8,128)(2,1)S(1)}, bf16[720,128]{1,0:T(8,128)(2,1)S(1)}, u32[]{:S(2)}, u32[]{:S(2)}) collective-permute-start(bf16[720,128]{1,0:T(8,128)(2,1)S(1)} %constant_dynamic-slice_fusion), channel_id=1, source_target_pairs={{0,8},{8,0},{16,24},{24,16},{1,9},{9,1},{17,25},{25,17},{2,10},{10... | collective-permute-start | bytes 552968 | tf_op jit(solution)/shard_map/ppermute | solution.py:426
  39.8 0.1 pad_add_fusion.refs_0_.place_ref
  39.9 1.9 %shard_map.48 = (f32[2,352,128]{2,1,0:T(8,128)S(1)}, f32[2,352,1]{2,1,0:T(8,128)S(1)}) custom-call(s32[2]{0:T(128)S(1)} %pad_add_fusion.refs_0_.place_ref, bf16[1088,128]{1,0:T(8,128)(2,1)S(1)} %add_convert_fusion.1.refs_1_.refs_4_.refs_3_, bf16[1088,128]{1,0:T(8,128)(2,1)S(1)} %add_convert_fusion.refs_2_.refs_5_.refs_4_), custom_call_target="tpu_custom_call" | custom-call | tf_op jit(solution)/shard_map/pallas_call | solution.py:461
  41.8 2.8 %collective-permute-done.12.refs_3_.refs_7_ = bf16[720,128]{1,0:T(8,128)(2,1)S(1)} collective-permute-done((bf16[720,128]{1,0:T(8,128)(2,1)S(1)}, bf16[720,128]{1,0:T(8,128)(2,1)S(1)}, u32[]{:S(2)}, u32[]{:S(2)}) %collective-permute-start.12) | collective-permute-done | bytes 184352 | tf_op jit(solution)/shard_map/ppermute | solution.py:426
  44.6 1.4 %shard_map.49.refs_8_ = bf16[2,368,128]{2,1,0:T(8,128)(2,1)S(1)} custom-call(s32[2]{0:T(128)S(1)} %pad_add_fusion.refs_0_.place_ref, bf16[720,128]{1,0:T(8,128)(2,1)S(1)} %collective-permute-done.10.refs_1_.refs_5_, bf16[720,128]{1,0:T(8,128)(2,1)S(1)} %collective-permute-done.11.refs_2_.refs_6_, ...), custom_call_target="tpu_custom_call" | custom-call | tf_op jit(solution)/shard_map/pallas_call | solution.py:464
  46.0 2.8 %collective-permute-start.13 = (bf16[368,128]{1,0:T(8,128)(2,1)S(1)}, bf16[368,128]{1,0:T(8,128)(2,1)S(1)}, u32[]{:S(2)}, u32[]{:S(2)}) collective-permute-start(bf16[368,128]{1,0:T(8,128)(2,1)S(1)} %get-tuple-element.44), channel_id=1, source_target_pairs={{8,24},{0,8},{16,0},{24,16},{9,25},{1,9},{17,1},{25,17},{10,26},{2... | collective-permute-start | bytes 282632 | tf_op jit(solution)/shard_map/ppermute | solution.py:426
  48.8 0.1 collective-permute-start.14
  48.9 0.6 shard_map.50
  49.5 2.9 %collective-permute-done.13.two_below_ref = bf16[368,128]{1,0:T(8,128)(2,1)S(1)} collective-permute-done((bf16[368,128]{1,0:T(8,128)(2,1)S(1)}, bf16[368,128]{1,0:T(8,128)(2,1)S(1)}, u32[]{:S(2)}, u32[]{:S(2)}) %collective-permute-start.13) | collective-permute-done | bytes 94240 | tf_op jit(solution)/shard_map/ppermute | solution.py:426
  52.4 3.2 %collective-permute-done.14.below_ref = bf16[368,128]{1,0:T(8,128)(2,1)S(1)} collective-permute-done((bf16[368,128]{1,0:T(8,128)(2,1)S(1)}, bf16[368,128]{1,0:T(8,128)(2,1)S(1)}, u32[]{:S(2)}, u32[]{:S(2)}) %collective-permute-start.14) | collective-permute-done | bytes 94240 | tf_op jit(solution)/shard_map/ppermute | solution.py:426
  55.6 1.1 %shard_map.51 = (bf16[176,256]{1,0:T(8,128)(2,1)S(1)}, bf16[176,256]{1,0:T(8,128)(2,1)S(1)}) custom-call(s32[2]{0:T(128)S(1)} %pad_add_fusion.refs_0_.place_ref, f32[2,352,128]{2,1,0:T(8,128)S(1)} %get-tuple-element.37.out_ref, f32[2,352,1]{2,1,0:T(8,128)S(1)} %get-tuple-element.38.logs_ref, bf16[368,128]{1,0:T(8,128)(2,1)S(1)} %collective-permute-done.13.two_below_ref, ...), custom_call_target="tpu_custom_call" | custom-call | tf_op jit(solution)/shard_map/pallas_call | solution.py:476
  56.7 1.9 %collective-permute-start.15 = (bf16[176,256]{1,0:T(8,128)(2,1)S(1)}, bf16[176,256]{1,0:T(8,128)(2,1)S(1)}, u32[]{:S(2)}, u32[]{:S(2)}) collective-permute-start(bf16[176,256]{1,0:T(8,128)(2,1)S(1)} %get-tuple-element.40), channel_id=1, source_target_pairs={{0,4},{4,0},{1,5},{5,1},{2,6},{6,2},{3,7},{7,3},{8,12},{12,8},{9,1... | collective-permute-start | bytes 270344 | tf_op jit(solution)/shard_map/ppermute | solution.py:328
  58.5 2.7 %collective-permute-done.15 = bf16[176,256]{1,0:T(8,128)(2,1)S(1)} collective-permute-done((bf16[176,256]{1,0:T(8,128)(2,1)S(1)}, bf16[176,256]{1,0:T(8,128)(2,1)S(1)}, u32[]{:S(2)}, u32[]{:S(2)}) %collective-permute-start.15) | collective-permute-done | bytes 90144 | tf_op jit(solution)/shard_map/ppermute | solution.py:328
  61.3 0.7 %pad_maximum_fusion.2 = bf16[176,512]{1,0:T(8,128)(2,1)} fusion(bf16[176,256]{1,0:T(8,128)(2,1)S(1)} %get-tuple-element.46, bf16[176,256]{1,0:T(8,128)(2,1)S(1)} %get-tuple-element.45), kind=kLoop, calls=%fused_computation.7 | loop fusion | flops 360448 | bytes 360448 | tf_op jit(solution)/shard_map/concatenate | solution.py:482
  (25 shorter events, 0.3 us)
Async XLA Ops:
  0.0 14.9 %collective-permute-start = (bf16[176,1024]{1,0:T(8,128)(2,1)}, bf16[176,1024]{1,0:T(8,128)(2,1)S(1)}, u32[]{:S(2)}, u32[]{:S(2)}) collective-permute-start(bf16[176,1024]{1,0:T(8,128)(2,1)} %param.4), channel_id=1, source_target_pairs={{0,0},{1,1},{2,4},{3,5},{4,2},{5,3},{6,6},{7,7},{8,8},{9,9},{10,12... | collective-permute-start | bytes 1081352 | tf_op jit(solution)/shard_map/ppermute | solution.py:334
  1.6 13.3 %collective-permute-start.1 = (bf16[176,1024]{1,0:T(8,128)(2,1)}, bf16[176,1024]{1,0:T(8,128)(2,1)S(1)}, u32[]{:S(2)}, u32[]{:S(2)}) collective-permute-start(bf16[176,1024]{1,0:T(8,128)(2,1)} %param.4), channel_id=1, source_target_pairs={{0,2},{1,3},{2,6},{3,7},{4,0},{5,1},{6,4},{7,5},{8,10},{9,11},{10,... | collective-permute-start | bytes 1081352 | tf_op jit(solution)/shard_map/ppermute | solution.py:339
  8.3 1.6 %collective-permute-start.2 = (f32[1200]{0:T(1024)S(1)}, f32[1200]{0:T(1024)S(1)}, u32[]{:S(2)}, u32[]{:S(2)}) collective-permute-start(f32[1200]{0:T(1024)S(1)} %pad_maximum_fusion.3), channel_id=1, source_target_pairs={{0,1},{1,0},{2,3},{3,2},{4,5},{5,4},{6,7},{7,6},{8,9},{9,8},{10,11... | collective-permute-start | bytes 14408 | tf_op jit(solution)/shard_map/ppermute | solution.py:325
  10.8 4.1 %collective-permute-start.3 = (f32[2224]{0:T(1024)S(1)}, f32[2224]{0:T(1024)S(1)}, u32[]{:S(2)}, u32[]{:S(2)}) collective-permute-start(f32[2224]{0:T(1024)S(1)} %concatenate.40), channel_id=1, source_target_pairs={{0,2},{1,3},{2,0},{3,1},{4,6},{5,7},{6,4},{7,5},{8,10},{9,11},{10,... | collective-permute-start | bytes 26696 | tf_op jit(solution)/shard_map/ppermute | solution.py:325
  10.9 7.8 %copy-start = (s32[176]{0:T(256)S(1)}, s32[176]{0:T(256)}, u32[]{:S(2)}) copy-start(s32[176]{0:T(256)} %param.7) | copy-start | bytes 2116
  15.1 3.6 %collective-permute-start.6 = (f32[352]{0:T(512)S(1)}, f32[352]{0:T(512)S(1)}, u32[]{:S(2)}, u32[]{:S(2)}) collective-permute-start(f32[352]{0:T(512)S(1)} %pad_maximum_fusion.4), channel_id=1, source_target_pairs={{0,4},{4,0},{1,5},{5,1},{2,6},{6,2},{3,7},{7,3},{8,12},{12,8},{9,1... | collective-permute-start | bytes 4232 | tf_op jit(solution)/shard_map/ppermute | solution.py:328
  17.0 1.9 %collective-permute-start.4 = (bf16[176,1024]{1,0:T(8,128)(2,1)S(1)}, bf16[176,1024]{1,0:T(8,128)(2,1)S(1)}, u32[]{:S(2)}, u32[]{:S(2)}) collective-permute-start(bf16[176,1024]{1,0:T(8,128)(2,1)S(1)} %collective-permute-done.a_near), channel_id=1, source_target_pairs={{0,1},{1,0},{2,3},{3,2},{4,5},{5,4},{6,7},{7,6},{8,9},{9,8},{10,11... | collective-permute-start | bytes 1081352 | tf_op jit(solution)/shard_map/ppermute | solution.py:325
  17.0 2.2 %collective-permute-start.5 = (bf16[176,1024]{1,0:T(8,128)(2,1)S(1)}, bf16[176,1024]{1,0:T(8,128)(2,1)S(1)}, u32[]{:S(2)}, u32[]{:S(2)}) collective-permute-start(bf16[176,1024]{1,0:T(8,128)(2,1)S(1)} %collective-permute-done.1.a_far), channel_id=1, source_target_pairs={{0,1},{1,0},{2,3},{3,2},{4,5},{5,4},{6,7},{7,6},{8,9},{9,8},{10,11... | collective-permute-start | bytes 1081352 | tf_op jit(solution)/shard_map/ppermute | solution.py:325
  22.0 9.7 %collective-permute-start.7 = (f16[1088,128]{1,0:T(8,128)(2,1)S(1)}, f16[1088,128]{1,0:T(8,128)(2,1)}, u32[]{:S(2)}, u32[]{:S(2)}) collective-permute-start(f16[1088,128]{1,0:T(8,128)(2,1)S(1)} %convert_element_type.58), channel_id=1, source_target_pairs={{0,4},{4,0},{1,5},{5,1},{2,6},{6,2},{3,7},{7,3},{8,12},{12,8},{9,1... | collective-permute-start | bytes 835592 | tf_op jit(solution)/shard_map/ppermute | solution.py:328
  23.8 12.8 %collective-permute-start.8 = (f16[1088,128]{1,0:T(8,128)(2,1)S(1)}, f16[1088,128]{1,0:T(8,128)(2,1)S(1)}, u32[]{:S(2)}, u32[]{:S(2)}) collective-permute-start(f16[1088,128]{1,0:T(8,128)(2,1)S(1)} %convert_element_type.61), channel_id=1, source_target_pairs={{0,4},{4,0},{1,5},{5,1},{2,6},{6,2},{3,7},{7,3},{8,12},{12,8},{9,1... | collective-permute-start | bytes 835592 | tf_op jit(solution)/shard_map/ppermute | solution.py:328
  32.7 3.5 %collective-permute-start.9 = (bf16[16,128]{1,0:T(8,128)(2,1)S(1)}, bf16[16,128]{1,0:T(8,128)(2,1)S(1)}, u32[]{:S(2)}, u32[]{:S(2)}) collective-permute-start(bf16[16,128]{1,0:T(8,128)(2,1)S(1)} %slice.45), channel_id=1, source_target_pairs={{0,1},{1,0},{2,3},{3,2},{4,5},{5,4},{6,7},{7,6},{8,9},{9,8},{10,11... | collective-permute-start | bytes 12296 | tf_op jit(solution)/shard_map/ppermute | solution.py:325
  32.9 8.9 %collective-permute-start.10 = (bf16[720,128]{1,0:T(8,128)(2,1)S(1)}, bf16[720,128]{1,0:T(8,128)(2,1)S(1)}, u32[]{:S(2)}, u32[]{:S(2)}) collective-permute-start(bf16[720,128]{1,0:T(8,128)(2,1)S(1)} %get-tuple-element.42), channel_id=1, source_target_pairs={{0,16},{24,8},{8,0},{16,24},{1,17},{25,9},{9,1},{17,25},{2,18},{26... | collective-permute-start | bytes 552968 | tf_op jit(solution)/shard_map/ppermute | solution.py:426
  35.5 6.3 %collective-permute-start.11 = (bf16[720,128]{1,0:T(8,128)(2,1)S(1)}, bf16[720,128]{1,0:T(8,128)(2,1)S(1)}, u32[]{:S(2)}, u32[]{:S(2)}) collective-permute-start(bf16[720,128]{1,0:T(8,128)(2,1)S(1)} %get-tuple-element.41), channel_id=1, source_target_pairs={{8,16},{16,8},{0,0},{24,24},{9,17},{17,9},{1,1},{25,25},{10,18},{1... | collective-permute-start | bytes 552968 | tf_op jit(solution)/shard_map/ppermute | solution.py:426
  36.8 7.7 %collective-permute-start.12 = (bf16[720,128]{1,0:T(8,128)(2,1)S(1)}, bf16[720,128]{1,0:T(8,128)(2,1)S(1)}, u32[]{:S(2)}, u32[]{:S(2)}) collective-permute-start(bf16[720,128]{1,0:T(8,128)(2,1)S(1)} %constant_dynamic-slice_fusion), channel_id=1, source_target_pairs={{0,8},{8,0},{16,24},{24,16},{1,9},{9,1},{17,25},{25,17},{2,10},{10... | collective-permute-start | bytes 552968 | tf_op jit(solution)/shard_map/ppermute | solution.py:426
  46.0 6.4 %collective-permute-start.13 = (bf16[368,128]{1,0:T(8,128)(2,1)S(1)}, bf16[368,128]{1,0:T(8,128)(2,1)S(1)}, u32[]{:S(2)}, u32[]{:S(2)}) collective-permute-start(bf16[368,128]{1,0:T(8,128)(2,1)S(1)} %get-tuple-element.44), channel_id=1, source_target_pairs={{8,24},{0,8},{16,0},{24,16},{9,25},{1,9},{17,1},{25,17},{10,26},{2... | collective-permute-start | bytes 282632 | tf_op jit(solution)/shard_map/ppermute | solution.py:426
  48.8 6.8 %collective-permute-start.14 = (bf16[368,128]{1,0:T(8,128)(2,1)S(1)}, bf16[368,128]{1,0:T(8,128)(2,1)S(1)}, u32[]{:S(2)}, u32[]{:S(2)}) collective-permute-start(bf16[368,128]{1,0:T(8,128)(2,1)S(1)} %get-tuple-element.43), channel_id=1, source_target_pairs={{0,8},{8,16},{16,24},{24,0},{1,9},{9,17},{17,25},{25,1},{2,10},{10... | collective-permute-start | bytes 282632 | tf_op jit(solution)/shard_map/ppermute | solution.py:426
  56.7 4.6 %collective-permute-start.15 = (bf16[176,256]{1,0:T(8,128)(2,1)S(1)}, bf16[176,256]{1,0:T(8,128)(2,1)S(1)}, u32[]{:S(2)}, u32[]{:S(2)}) collective-permute-start(bf16[176,256]{1,0:T(8,128)(2,1)S(1)} %get-tuple-element.40), channel_id=1, source_target_pairs={{0,4},{4,0},{1,5},{5,1},{2,6},{6,2},{3,7},{7,3},{8,12},{12,8},{9,1... | collective-permute-start | bytes 270344 | tf_op jit(solution)/shard_map/ppermute | solution.py:328

commit v11 on v10

--- a/solution.py
+++ b/solution.py
@@ -15,10 +15,10 @@
 CHUNKS = ((4, 0), (1, 3))
 
 
-def rotary_tables(places, head_size):
+def rotary_tables(places, head_size, always):
     half = head_size // 2
     spacing = jnp.arange(half).astype(jnp.float32) * (2.0 / head_size)
-    inverse = jnp.power(10000.0, -spacing)
+    inverse = jnp.where(always, jnp.power(10000.0, -spacing), 0.0)
     angles = places.astype(jnp.float32)[:, None] * inverse[None, :]
     cosine, sine = jnp.cos(angles), jnp.sin(angles)
     return (
@@ -212,7 +212,7 @@
 
     @pl.when(place_ref[0] == 0)
     def one_up():
-        attend(0, neighbour[begin:, :], [chunk_one[:height, :]])
+        attend(1, neighbour[begin:, :], [chunk_one[:height, :]])
 
     @pl.when(place_ref[0] == 1)
     def down():
@@ -248,7 +248,7 @@
 
 
 def merge_kernel(
-    place_ref, out_ref, logs_ref, two_below_ref, below_ref, mine_ref, theirs_ref
+    place_ref, out_ref, logs_ref, first_ref, below_ref, mine_ref, theirs_ref
 ):
     block, size = out_ref.shape[1:]
     tok, row = place_ref[0], place_ref[1]
@@ -259,8 +259,8 @@
         output, logs = joined((out_ref[index], logs_ref[index]), (guest, guest_logs))
         return output.astype(jnp.bfloat16)
 
-    down = with_guest(0, jnp.where(tok == 2, below_ref[...], two_below_ref[...]), tok >= 2)
-    up = with_guest(1, below_ref[...], (tok == 1) | (tok == 3))
+    down = with_guest(0, jnp.where(tok == 2, below_ref[...], first_ref[...]), tok >= 2)
+    up = with_guest(1, jnp.where(tok == 1, first_ref[...], below_ref[...]), (tok == 1) | (tok == 3))
     for index, output in enumerate((down, up)):
         columns = slice(index * size, (index + 1) * size)
         mine_ref[:, columns], theirs_ref[:, columns] = parted(row, output)
@@ -350,18 +350,18 @@
     got = by_col(message, 1)
     squares = squares + got[:rows]
     gain = ordered(core, gain, got[rows:])
-    got = by_col(jnp.concatenate([squares, gain]), 2)
-    near, far, got, flat_weight = lax.optimization_barrier((near, far, got, flat_weight))
+    by_chip = by_col(jnp.concatenate([squares, gain]), 2)
+    near, far, by_chip, flat_weight = lax.optimization_barrier((near, far, by_chip, flat_weight))
     near_other, far_other = by_col(near, 1), by_col(far, 1)
-    squares = squares + got[:rows]
-    gain = jnp.where(chip == row, gain, got[rows:]).reshape(2, 1, width)
+    squares = squares + by_chip[:rows]
+    gain = jnp.where(chip == row, gain, by_chip[rows:]).reshape(2, 1, width)
     codes = doc_ids.astype(jnp.float32) + 1.0
     got = by_row(jnp.concatenate([squares, codes]))
     squares = ordered(row, squares, got[:rows]).reshape(block, 1)
     codes = ordered(row, codes, got[rows:])
     doc_rows = jnp.pad(codes, (0, EXTRA * size - block)).reshape(EXTRA, size)
     places = tok * block + jnp.arange(block, dtype=jnp.int32)
-    cosine, sine = rotary_tables(places, size)
+    cosine, sine = rotary_tables(places, size, near[0, : size // 2].astype(jnp.float32) < 1e30)
 
     taller = 3 * block + 2 * EXTRA
     break_at = 2 * block + EXTRA
@@ -467,14 +467,14 @@
             6,
             1,
         )(places, two_away, swapped, neighbour, chunk_one, chunk_two, own_logs)
-        from_two_below = along_tok(guests[1], [(1, 3), (0, 1), (2, 0), (3, 2)])
-        from_below = along_tok(guests[0], [(0, 1), (1, 2), (2, 3), (3, 0)])
+        from_first = along_tok(guests[1], [(0, 1), (1, 3), (2, 0), (3, 2)])
+        from_below = along_tok(guests[0], [(1, 2), (2, 3)])
         output, logs = on_place(
             lambda *refs: own_rest_kernel(scale, *refs), part_shapes, 8, 1
         )(places, own_out, own_logs, chunk_one, chunk_two, two_away, swapped, neighbour, guests)
         half = jax.ShapeDtypeStruct((rows, pair * size), jnp.bfloat16)
         mine, theirs = on_place(merge_kernel, (half, half), 4)(
-            places, output, logs, from_two_below, from_below
+            places, output, logs, from_first, from_below
         )
     else:
         mine, theirs = gathered_attention()

time: 62.3 us -> 58.2 us (0.934)
  the two profiles are of different devices: /device:TPU:0 before, /device:TPU:24 now
where the time goes in v11:
time: 58.2 us; the launch traced here: 57.5 us
  waiting for transfers between devices  19.3 us (33%)
  starting transfers between devices  16.8 us (29%)
  Pallas kernels  11.1 us (19%)
  other arithmetic  5.65 us (10%)
  local copies, waits for them, and re-layouts  4.41 us (8%)
    ppermute x4, waiting for transfers between devices, by_row(): return lax.ppermute(value, 'row', [(0, 1), (1, 0)])  10.5 us
    ppermute x5, waiting for transfers between devices, along_tok(): return lax.ppermute(value, 'tok', pairs)  7.81 us
    ppermute x4, starting transfers between devices, by_row(): return lax.ppermute(value, 'row', [(0, 1), (1, 0)])  5.85 us
    ppermute x5, starting transfers between devices, along_tok(): return lax.ppermute(value, 'tok', pairs)  5.67 us
    unnamed x3, local copies, waits for them, and re-layouts  3.97 us
    pallas_call x1, Pallas kernels, per_device(): pl.pallas_call(project_kernel, out_shape=(partial_sums, partial_sums), in...  3.66 us
    ppermute x1, starting transfers between devices, per_device(): lax.ppermute(activations, ('row', 'col'), [(r * 4 + c, c // 2 * 4 + 2 * (...  3.31 us
    pallas_call x1, Pallas kernels, per_device(): pl.pallas_call(normalise_project_kernel, out_shape=(partial_sums, partial...  2.69 us
  transfers between devices with their start and end apart: 16, of which 10 were waited for; matrix products, arithmetic and copies ran while one was open for 16% of the time, Pallas kernels for 12%

profile of v11, /device:TPU:24, one launch (start us, length us, event | category | flops | bytes accessed | tf_op | source)
XLA Modules:
  0.0 57.5 jit_solution(9511294899319382145)
XLA Ops:
  0.0 1.6 %collective-permute-start = (bf16[176,1024]{1,0:T(8,128)(2,1)}, bf16[176,1024]{1,0:T(8,128)(2,1)S(1)}, u32[]{:S(2)}, u32[]{:S(2)}) collective-permute-start(bf16[176,1024]{1,0:T(8,128)(2,1)} %param.4), channel_id=1, source_target_pairs={{0,0},{1,1},{2,4},{3,5},{4,2},{5,3},{6,6},{7,7},{8,8},{9,9},{10,12... | collective-permute-start | bytes 1081352 | tf_op jit(solution)/shard_map/ppermute | solution.py:334
  1.6 3.3 %collective-permute-start.1 = (bf16[176,1024]{1,0:T(8,128)(2,1)}, bf16[176,1024]{1,0:T(8,128)(2,1)S(1)}, u32[]{:S(2)}, u32[]{:S(2)}) collective-permute-start(bf16[176,1024]{1,0:T(8,128)(2,1)} %param.4), channel_id=1, source_target_pairs={{0,2},{1,3},{2,6},{3,7},{4,0},{5,1},{6,4},{7,5},{8,10},{9,11},{10,... | collective-permute-start | bytes 1081352 | tf_op jit(solution)/shard_map/ppermute | solution.py:339
  4.9 1.2 %multiply_reduce_fusion = f32[176]{0:T(256)S(1)} fusion(bf16[176,1024]{1,0:T(8,128)(2,1)} %param.4), kind=kLoop, calls=%fused_computation | loop fusion | flops 540496 | bytes 361152 | tf_op jit(solution)/shard_map/reduce_sum | solution.py:345
  6.1 0.7 %convert_element_type.61 = f32[1024]{0:T(1024)S(1)} convert(bf16[1024]{0:T(1024)(128)(2,1)} %param.5) | non-fusion elementwise | flops 1024 | bytes 6144 | tf_op jit(solution)/shard_map/convert_element_type | solution.py:346
  6.8 0.1 pad_maximum_fusion.3
  6.9 0.7 %convert_add_fusion = f32[176]{0:T(256)S(1)} fusion(s32[176]{0:T(256)} %param.7), kind=kLoop, calls=%fused_computation.28 | loop fusion | flops 352 | bytes 1408 | tf_op jit(solution)/shard_map/add | solution.py:358
  7.6 0.5 collective-permute-done.2
  8.0 0.8 %slice_select_fusion = (f32[1024]{0:T(1024)S(1)}, f32[1024]{0:T(1024)S(1)}) fusion(f32[1200]{0:T(1024)S(1)} %collective-permute-done.2, bf16[1024]{0:T(1024)(128)(2,1)} %param.5, pred[]{:T(512)S(6)} %eq.22), kind=kLoop, calls=%fused_computation.18 | loop fusion | flops 3072 | bytes 14337 | tf_op jit(solution)/shard_map/jit(_where)/select_n | solution.py:332
  8.8 0.1 concatenate.40
  8.9 0.1 pad_add_fusion.1.place_ref
  9.0 4.0 %copy.6 = bf16[256,8,4,384]{3,1,2,0:T(8,128)(2,1)S(1)} copy(bf16[256,8,4,384]{3,2,1,0:T(4,128)(2,1)} %bitcast.25) | data formatting | bytes 12582912
  12.9 0.5 collective-permute-done.3
  13.5 0.1 slice.39
  13.6 0.1 pad_maximum_fusion.4
  13.7 1.8 %collective-permute-start.6 = (f32[352]{0:T(512)S(1)}, f32[352]{0:T(512)S(1)}, u32[]{:S(2)}, u32[]{:S(2)}) collective-permute-start(f32[352]{0:T(512)S(1)} %pad_maximum_fusion.4), channel_id=1, source_target_pairs={{0,4},{4,0},{1,5},{5,1},{2,6},{6,2},{3,7},{7,3},{8,12},{12,8},{9,1... | collective-permute-start | bytes 4232 | tf_op jit(solution)/shard_map/ppermute | solution.py:328
  15.5 0.2 collective-permute-start.5
  15.7 0.7 %fusion = (f32[352,64]{1,0:T(8,128)S(1)}, f32[352,64]{1,0:T(8,128)S(1)}, f32[352,64]{1,0:T(8,128)S(1)}) fusion(f32[64]{0:T(128)S(1)} %fusion.2, f32[352]{0:T(512)S(1)} %add_convert_fusion.2), kind=kLoop, calls=%fused_computation.12 | loop fusion | flops 45056 | bytes 272000 | tf_op jit(solution)/shard_map/neg | solution.py:26
  16.4 0.2 pad_maximum_fusion
  16.6 0.7 %collective-permute-done.6 = f32[352]{0:T(512)S(1)} collective-permute-done((f32[352]{0:T(512)S(1)}, f32[352]{0:T(512)S(1)}, u32[]{:S(2)}, u32[]{:S(2)}) %collective-permute-start.6) | collective-permute-done | bytes 1440 | tf_op jit(solution)/shard_map/ppermute | solution.py:328
  17.3 0.1 broadcast_select_fusion.4
  17.4 0.1 pad_maximum_fusion.5
  17.4 0.1 reshape.71.squares_ref
  17.6 2.7 %shard_map.46 = (f32[1088,128]{1,0:T(8,128)S(1)}, f32[1088,128]{1,0:T(8,128)S(1)}, bf16[2,352,1024]{2,1,0:T(8,128)(2,1)S(1)}, bf16[2048,768]{1,0:T(8,128)(2,1)}) custom-call(s32[4]{0:T(128)S(1)} %pad_add_fusion.1.place_ref, bf16[176,1024]{1,0:T(8,128)(2,1)S(1)} %collective-permute-done.a_near, bf16[176,1024]{1,0:T(8,128)(2,1)S(1)} %collective-permute-done.1.a_far, ...), custom_call_target="tpu_custom_call" | custom-call | tf_op jit(solution)/shard_map/pallas_call | solution.py:371
  20.3 1.9 %collective-permute-start.7 = (f16[1088,128]{1,0:T(8,128)(2,1)S(1)}, f16[1088,128]{1,0:T(8,128)(2,1)S(1)}, u32[]{:S(2)}, u32[]{:S(2)}) collective-permute-start(f16[1088,128]{1,0:T(8,128)(2,1)S(1)} %convert_element_type.66), channel_id=1, source_target_pairs={{0,4},{4,0},{1,5},{5,1},{2,6},{6,2},{3,7},{7,3},{8,12},{12,8},{9,1... | collective-permute-start | bytes 835592 | tf_op jit(solution)/shard_map/ppermute | solution.py:328
  22.2 0.1 fusion.1.docs_ref
  22.3 0.3 collective-permute-start.8
  22.6 3.7 %shard_map.47 = (f32[1088,128]{1,0:T(8,128)S(1)}, f32[1088,128]{1,0:T(8,128)S(1)}) custom-call(bf16[2,352,1024]{2,1,0:T(8,128)(2,1)S(1)} %get-tuple-element.29.normed_ref, f32[16,128]{1,0:T(8,128)S(1)} %fusion.1.docs_ref, f32[352,128]{1,0:T(8,128)S(1)} %get-tuple-element.58.cos_ref, f32[352,128]{1,0:T(8,128)S(1)} %get-tuple-element.59.sin_ref, ...), custom_call_target="tpu_custom_call" | custom-call | tf_op jit(solution)/shard_map/pallas_call | solution.py:389
  26.3 3.7 %collective-permute-done.7 = f16[1088,128]{1,0:T(8,128)(2,1)S(1)} collective-permute-done((f16[1088,128]{1,0:T(8,128)(2,1)S(1)}, f16[1088,128]{1,0:T(8,128)(2,1)S(1)}, u32[]{:S(2)}, u32[]{:S(2)}) %collective-permute-start.7) | collective-permute-done | bytes 278560 | tf_op jit(solution)/shard_map/ppermute | solution.py:328
  30.1 0.1 constant_dynamic-slice_fusion.1
  30.2 0.4 collective-permute-start.10
  30.6 0.7 %collective-permute-start.11 = (bf16[720,128]{1,0:T(8,128)(2,1)S(1)}, bf16[720,128]{1,0:T(8,128)(2,1)S(1)}, u32[]{:S(2)}, u32[]{:S(2)}) collective-permute-start(bf16[720,128]{1,0:T(8,128)(2,1)S(1)} %get-tuple-element.41), channel_id=1, source_target_pairs={{8,16},{16,8},{0,0},{24,24},{9,17},{17,9},{1,1},{25,25},{10,18},{1... | collective-permute-start | bytes 552968 | tf_op jit(solution)/shard_map/ppermute | solution.py:426
  31.3 3.4 %collective-permute-done.8 = f16[1088,128]{1,0:T(8,128)(2,1)S(1)} collective-permute-done((f16[1088,128]{1,0:T(8,128)(2,1)S(1)}, f16[1088,128]{1,0:T(8,128)(2,1)S(1)}, u32[]{:S(2)}, u32[]{:S(2)}) %collective-permute-start.8) | collective-permute-done | bytes 278560 | tf_op jit(solution)/shard_map/ppermute | solution.py:328
  34.7 0.1 add_convert_fusion.refs_2_.refs_5_.refs_4_
  34.9 0.5 collective-permute-start.12
  35.4 0.1 pad_add_fusion.refs_0_.place_ref
  35.5 1.9 %shard_map.48 = (f32[2,352,128]{2,1,0:T(8,128)S(1)}, f32[2,352,1]{2,1,0:T(8,128)S(1)}) custom-call(s32[2]{0:T(128)S(1)} %pad_add_fusion.refs_0_.place_ref, bf16[1088,128]{1,0:T(8,128)(2,1)S(1)} %add_convert_fusion.1.refs_1_.refs_4_.refs_3_, bf16[1088,128]{1,0:T(8,128)(2,1)S(1)} %add_convert_fusion.refs_2_.refs_5_.refs_4_), custom_call_target="tpu_custom_call" | custom-call | tf_op jit(solution)/shard_map/pallas_call | solution.py:461
  37.3 0.4 collective-permute-done.10.refs_1_.refs_5_
  37.7 3.5 %collective-permute-done.12.refs_3_.refs_7_ = bf16[720,128]{1,0:T(8,128)(2,1)S(1)} collective-permute-done((bf16[720,128]{1,0:T(8,128)(2,1)S(1)}, bf16[720,128]{1,0:T(8,128)(2,1)S(1)}, u32[]{:S(2)}, u32[]{:S(2)}) %collective-permute-start.12) | collective-permute-done | bytes 184352 | tf_op jit(solution)/shard_map/ppermute | solution.py:426
  41.2 0.6 shard_map.49.refs_8_
  41.8 2.8 %collective-permute-start.13 = (bf16[368,128]{1,0:T(8,128)(2,1)S(1)}, bf16[368,128]{1,0:T(8,128)(2,1)S(1)}, u32[]{:S(2)}, u32[]{:S(2)}) collective-permute-start(bf16[368,128]{1,0:T(8,128)(2,1)S(1)} %get-tuple-element.44), channel_id=1, source_target_pairs={{0,8},{8,24},{16,0},{24,16},{1,9},{9,25},{17,1},{25,17},{2,10},{10... | collective-permute-start | bytes 282632 | tf_op jit(solution)/shard_map/ppermute | solution.py:426
  44.7 1.3 %collective-permute-start.14 = (bf16[368,128]{1,0:T(8,128)(2,1)S(1)}, bf16[368,128]{1,0:T(8,128)(2,1)S(1)}, u32[]{:S(2)}, u32[]{:S(2)}) collective-permute-start(bf16[368,128]{1,0:T(8,128)(2,1)S(1)} %get-tuple-element.43), channel_id=1, source_target_pairs={{8,16},{16,24},{9,17},{17,25},{10,18},{18,26},{11,19},{19,27},{12,... | collective-permute-start | bytes 282632 | tf_op jit(solution)/shard_map/ppermute | solution.py:426
  46.0 1.2 %shard_map.50 = (f32[2,352,128]{2,1,0:T(8,128)S(1)}, f32[2,352,1]{2,1,0:T(8,128)S(1)}) custom-call(s32[2]{0:T(128)S(1)} %pad_add_fusion.refs_0_.place_ref, f32[2,352,128]{2,1,0:T(8,128)S(1)} %get-tuple-element.35.refs_1_, f32[2,352,1]{2,1,0:T(8,128)S(1)} %get-tuple-element.36.refs_6_.refs_2_, ...), custom_call_target="tpu_custom_call" | custom-call | tf_op jit(solution)/shard_map/pallas_call | solution.py:472
  47.2 0.5 collective-permute-done.13.first_ref
  47.7 3.4 %collective-permute-done.14.below_ref = bf16[368,128]{1,0:T(8,128)(2,1)S(1)} collective-permute-done((bf16[368,128]{1,0:T(8,128)(2,1)S(1)}, bf16[368,128]{1,0:T(8,128)(2,1)S(1)}, u32[]{:S(2)}, u32[]{:S(2)}) %collective-permute-start.14) | collective-permute-done | bytes 94240 | tf_op jit(solution)/shard_map/ppermute | solution.py:426
  51.1 1.1 %shard_map.51 = (bf16[176,256]{1,0:T(8,128)(2,1)S(1)}, bf16[176,256]{1,0:T(8,128)(2,1)S(1)}) custom-call(s32[2]{0:T(128)S(1)} %pad_add_fusion.refs_0_.place_ref, f32[2,352,128]{2,1,0:T(8,128)S(1)} %get-tuple-element.37.out_ref, f32[2,352,1]{2,1,0:T(8,128)S(1)} %get-tuple-element.38.logs_ref, bf16[368,128]{1,0:T(8,128)(2,1)S(1)} %collective-permute-done.13.first_ref, ...), custom_call_target="tpu_custom_call" | custom-call | tf_op jit(solution)/shard_map/pallas_call | solution.py:476
  52.2 1.9 %collective-permute-start.15 = (bf16[176,256]{1,0:T(8,128)(2,1)S(1)}, bf16[176,256]{1,0:T(8,128)(2,1)S(1)}, u32[]{:S(2)}, u32[]{:S(2)}) collective-permute-start(bf16[176,256]{1,0:T(8,128)(2,1)S(1)} %get-tuple-element.40), channel_id=1, source_target_pairs={{0,4},{4,0},{1,5},{5,1},{2,6},{6,2},{3,7},{7,3},{8,12},{12,8},{9,1... | collective-permute-start | bytes 270344 | tf_op jit(solution)/shard_map/ppermute | solution.py:328
  54.1 2.7 %collective-permute-done.15 = bf16[176,256]{1,0:T(8,128)(2,1)S(1)} collective-permute-done((bf16[176,256]{1,0:T(8,128)(2,1)S(1)}, bf16[176,256]{1,0:T(8,128)(2,1)S(1)}, u32[]{:S(2)}, u32[]{:S(2)}) %collective-permute-start.15) | collective-permute-done | bytes 90144 | tf_op jit(solution)/shard_map/ppermute | solution.py:328
  56.8 0.7 %pad_maximum_fusion.2 = bf16[176,512]{1,0:T(8,128)(2,1)} fusion(bf16[176,256]{1,0:T(8,128)(2,1)S(1)} %get-tuple-element.46, bf16[176,256]{1,0:T(8,128)(2,1)S(1)} %get-tuple-element.45), kind=kLoop, calls=%fused_computation.7 | loop fusion | flops 360448 | bytes 360448 | tf_op jit(solution)/shard_map/concatenate | solution.py:482
  (25 shorter events, 0.4 us)
Async XLA Ops:
  0.0 13.5 %collective-permute-start = (bf16[176,1024]{1,0:T(8,128)(2,1)}, bf16[176,1024]{1,0:T(8,128)(2,1)S(1)}, u32[]{:S(2)}, u32[]{:S(2)}) collective-permute-start(bf16[176,1024]{1,0:T(8,128)(2,1)} %param.4), channel_id=1, source_target_pairs={{0,0},{1,1},{2,4},{3,5},{4,2},{5,3},{6,6},{7,7},{8,8},{9,9},{10,12... | collective-permute-start | bytes 1081352 | tf_op jit(solution)/shard_map/ppermute | solution.py:334
  1.6 11.8 %collective-permute-start.1 = (bf16[176,1024]{1,0:T(8,128)(2,1)}, bf16[176,1024]{1,0:T(8,128)(2,1)S(1)}, u32[]{:S(2)}, u32[]{:S(2)}) collective-permute-start(bf16[176,1024]{1,0:T(8,128)(2,1)} %param.4), channel_id=1, source_target_pairs={{0,2},{1,3},{2,6},{3,7},{4,0},{5,1},{6,4},{7,5},{8,10},{9,11},{10,... | collective-permute-start | bytes 1081352 | tf_op jit(solution)/shard_map/ppermute | solution.py:339
  6.9 1.2 %collective-permute-start.2 = (f32[1200]{0:T(1024)S(1)}, f32[1200]{0:T(1024)S(1)}, u32[]{:S(2)}, u32[]{:S(2)}) collective-permute-start(f32[1200]{0:T(1024)S(1)} %pad_maximum_fusion.3), channel_id=1, source_target_pairs={{0,1},{1,0},{2,3},{3,2},{4,5},{5,4},{6,7},{7,6},{8,9},{9,8},{10,11... | collective-permute-start | bytes 14408 | tf_op jit(solution)/shard_map/ppermute | solution.py:325
  8.9 4.6 %collective-permute-start.3 = (f32[2224]{0:T(1024)S(1)}, f32[2224]{0:T(1024)S(1)}, u32[]{:S(2)}, u32[]{:S(2)}) collective-permute-start(f32[2224]{0:T(1024)S(1)} %concatenate.40), channel_id=1, source_target_pairs={{0,2},{1,3},{2,0},{3,1},{4,6},{5,7},{6,4},{7,5},{8,10},{9,11},{10,... | collective-permute-start | bytes 26696 | tf_op jit(solution)/shard_map/ppermute | solution.py:325
  9.0 8.3 %copy-start = (s32[176]{0:T(256)S(1)}, s32[176]{0:T(256)}, u32[]{:S(2)}) copy-start(s32[176]{0:T(256)} %param.7) | copy-start | bytes 2116
  13.6 4.0 %collective-permute-start.4 = (bf16[176,1024]{1,0:T(8,128)(2,1)S(1)}, bf16[176,1024]{1,0:T(8,128)(2,1)S(1)}, u32[]{:S(2)}, u32[]{:S(2)}) collective-permute-start(bf16[176,1024]{1,0:T(8,128)(2,1)S(1)} %collective-permute-done.a_near), channel_id=1, source_target_pairs={{0,1},{1,0},{2,3},{3,2},{4,5},{5,4},{6,7},{7,6},{8,9},{9,8},{10,11... | collective-permute-start | bytes 1081352 | tf_op jit(solution)/shard_map/ppermute | solution.py:325
  13.7 3.6 %collective-permute-start.6 = (f32[352]{0:T(512)S(1)}, f32[352]{0:T(512)S(1)}, u32[]{:S(2)}, u32[]{:S(2)}) collective-permute-start(f32[352]{0:T(512)S(1)} %pad_maximum_fusion.4), channel_id=1, source_target_pairs={{0,4},{4,0},{1,5},{5,1},{2,6},{6,2},{3,7},{7,3},{8,12},{12,8},{9,1... | collective-permute-start | bytes 4232 | tf_op jit(solution)/shard_map/ppermute | solution.py:328
  15.5 2.1 %collective-permute-start.5 = (bf16[176,1024]{1,0:T(8,128)(2,1)S(1)}, bf16[176,1024]{1,0:T(8,128)(2,1)S(1)}, u32[]{:S(2)}, u32[]{:S(2)}) collective-permute-start(bf16[176,1024]{1,0:T(8,128)(2,1)S(1)} %collective-permute-done.1.a_far), channel_id=1, source_target_pairs={{0,1},{1,0},{2,3},{3,2},{4,5},{5,4},{6,7},{7,6},{8,9},{9,8},{10,11... | collective-permute-start | bytes 1081352 | tf_op jit(solution)/shard_map/ppermute | solution.py:325
  20.3 9.6 %collective-permute-start.7 = (f16[1088,128]{1,0:T(8,128)(2,1)S(1)}, f16[1088,128]{1,0:T(8,128)(2,1)S(1)}, u32[]{:S(2)}, u32[]{:S(2)}) collective-permute-start(f16[1088,128]{1,0:T(8,128)(2,1)S(1)} %convert_element_type.66), channel_id=1, source_target_pairs={{0,4},{4,0},{1,5},{5,1},{2,6},{6,2},{3,7},{7,3},{8,12},{12,8},{9,1... | collective-permute-start | bytes 835592 | tf_op jit(solution)/shard_map/ppermute | solution.py:328
  22.3 12.4 %collective-permute-start.8 = (f16[1088,128]{1,0:T(8,128)(2,1)S(1)}, f16[1088,128]{1,0:T(8,128)(2,1)S(1)}, u32[]{:S(2)}, u32[]{:S(2)}) collective-permute-start(f16[1088,128]{1,0:T(8,128)(2,1)S(1)} %convert_element_type.69), channel_id=1, source_target_pairs={{0,4},{4,0},{1,5},{5,1},{2,6},{6,2},{3,7},{7,3},{8,12},{12,8},{9,1... | collective-permute-start | bytes 835592 | tf_op jit(solution)/shard_map/ppermute | solution.py:328
  30.0 1.3 %collective-permute-start.9 = (bf16[16,128]{1,0:T(8,128)(2,1)S(1)}, bf16[16,128]{1,0:T(8,128)(2,1)S(1)}, u32[]{:S(2)}, u32[]{:S(2)}) collective-permute-start(bf16[16,128]{1,0:T(8,128)(2,1)S(1)} %slice.49), channel_id=1, source_target_pairs={{0,1},{1,0},{2,3},{3,2},{4,5},{5,4},{6,7},{7,6},{8,9},{9,8},{10,11... | collective-permute-start | bytes 12296 | tf_op jit(solution)/shard_map/ppermute | solution.py:325
  30.2 7.5 %collective-permute-start.10 = (bf16[720,128]{1,0:T(8,128)(2,1)S(1)}, bf16[720,128]{1,0:T(8,128)(2,1)S(1)}, u32[]{:S(2)}, u32[]{:S(2)}) collective-permute-start(bf16[720,128]{1,0:T(8,128)(2,1)S(1)} %get-tuple-element.42), channel_id=1, source_target_pairs={{0,16},{24,8},{8,0},{16,24},{1,17},{25,9},{9,1},{17,25},{2,18},{26... | collective-permute-start | bytes 552968 | tf_op jit(solution)/shard_map/ppermute | solution.py:426
  30.6 7.1 %collective-permute-start.11 = (bf16[720,128]{1,0:T(8,128)(2,1)S(1)}, bf16[720,128]{1,0:T(8,128)(2,1)S(1)}, u32[]{:S(2)}, u32[]{:S(2)}) collective-permute-start(bf16[720,128]{1,0:T(8,128)(2,1)S(1)} %get-tuple-element.41), channel_id=1, source_target_pairs={{8,16},{16,8},{0,0},{24,24},{9,17},{17,9},{1,1},{25,25},{10,18},{1... | collective-permute-start | bytes 552968 | tf_op jit(solution)/shard_map/ppermute | solution.py:426
  34.9 6.4 %collective-permute-start.12 = (bf16[720,128]{1,0:T(8,128)(2,1)S(1)}, bf16[720,128]{1,0:T(8,128)(2,1)S(1)}, u32[]{:S(2)}, u32[]{:S(2)}) collective-permute-start(bf16[720,128]{1,0:T(8,128)(2,1)S(1)} %constant_dynamic-slice_fusion), channel_id=1, source_target_pairs={{0,8},{8,0},{16,24},{24,16},{1,9},{9,1},{17,25},{25,17},{2,10},{10... | collective-permute-start | bytes 552968 | tf_op jit(solution)/shard_map/ppermute | solution.py:426
  41.8 5.9 %collective-permute-start.13 = (bf16[368,128]{1,0:T(8,128)(2,1)S(1)}, bf16[368,128]{1,0:T(8,128)(2,1)S(1)}, u32[]{:S(2)}, u32[]{:S(2)}) collective-permute-start(bf16[368,128]{1,0:T(8,128)(2,1)S(1)} %get-tuple-element.44), channel_id=1, source_target_pairs={{0,8},{8,24},{16,0},{24,16},{1,9},{9,25},{17,1},{25,17},{2,10},{10... | collective-permute-start | bytes 282632 | tf_op jit(solution)/shard_map/ppermute | solution.py:426
  44.7 6.5 %collective-permute-start.14 = (bf16[368,128]{1,0:T(8,128)(2,1)S(1)}, bf16[368,128]{1,0:T(8,128)(2,1)S(1)}, u32[]{:S(2)}, u32[]{:S(2)}) collective-permute-start(bf16[368,128]{1,0:T(8,128)(2,1)S(1)} %get-tuple-element.43), channel_id=1, source_target_pairs={{8,16},{16,24},{9,17},{17,25},{10,18},{18,26},{11,19},{19,27},{12,... | collective-permute-start | bytes 282632 | tf_op jit(solution)/shard_map/ppermute | solution.py:426
  52.2 4.6 %collective-permute-start.15 = (bf16[176,256]{1,0:T(8,128)(2,1)S(1)}, bf16[176,256]{1,0:T(8,128)(2,1)S(1)}, u32[]{:S(2)}, u32[]{:S(2)}) collective-permute-start(bf16[176,256]{1,0:T(8,128)(2,1)S(1)} %get-tuple-element.40), channel_id=1, source_target_pairs={{0,4},{4,0},{1,5},{5,1},{2,6},{6,2},{3,7},{7,3},{8,12},{12,8},{9,1... | collective-permute-start | bytes 270344 | tf_op jit(solution)/shard_map/ppermute | solution.py:328

commit v12 on v11

--- a/solution.py
+++ b/solution.py
@@ -151,13 +151,12 @@
     scores = lax.dot_general(
         query, keys, (((1,), (1,)), ((), ())), preferred_element_type=jnp.float32
     )
-    top = jnp.max(jnp.where(visible, scores, LOW), axis=1, keepdims=True)
-    exponentials = jnp.where(visible, jnp.exp2((scores - top) * (scale * LOG2_E)), 0.0)
+    masked = jnp.where(visible, scores, LOW)
+    top = jnp.max(masked, axis=1, keepdims=True)
+    exponentials = jnp.exp2((masked - top) * (scale * LOG2_E))
     total = jnp.sum(exponentials, axis=1, keepdims=True)
     summed = jnp.dot(exponentials.astype(jnp.bfloat16), values, preferred_element_type=jnp.float32)
-    some = total > 0.0
-    safe = jnp.where(some, total, 1.0)
-    return summed / safe, jnp.where(some, top * scale + jnp.log(safe), LOW)
+    return summed / total, jnp.where(top > LOW / 2, top * scale + jnp.log(total), LOW)
 
 
 def as_message(output, logs, size):
@@ -345,20 +344,21 @@
     squares = jnp.sum(widened * widened, axis=1)
     gain = norm_gain.astype(jnp.float32)
     message = jnp.concatenate([squares, gain])
-    message, qkv_weight = lax.optimization_barrier((message, qkv_weight))
-    flat_weight = qkv_weight.reshape(span, local_heads * triple)
     got = by_col(message, 1)
     squares = squares + got[:rows]
     gain = ordered(core, gain, got[rows:])
+    codes = doc_ids.astype(jnp.float32) + 1.0
+    message = jnp.concatenate([squares, codes])
+    message, qkv_weight = lax.optimization_barrier((message, qkv_weight))
+    flat_weight = qkv_weight.reshape(span, local_heads * triple)
+    got = by_row(message)
+    got, flat_weight, near, far = lax.optimization_barrier((got, flat_weight, near, far))
+    squares = ordered(row, squares, got[:rows])
+    codes = ordered(row, codes, got[rows:])
     by_chip = by_col(jnp.concatenate([squares, gain]), 2)
-    near, far, by_chip, flat_weight = lax.optimization_barrier((near, far, by_chip, flat_weight))
     near_other, far_other = by_col(near, 1), by_col(far, 1)
-    squares = squares + by_chip[:rows]
-    gain = jnp.where(chip == row, gain, by_chip[rows:]).reshape(2, 1, width)
-    codes = doc_ids.astype(jnp.float32) + 1.0
-    got = by_row(jnp.concatenate([squares, codes]))
-    squares = ordered(row, squares, got[:rows]).reshape(block, 1)
-    codes = ordered(row, codes, got[rows:])
+    squares = (squares + by_chip[:block]).reshape(block, 1)
+    gain = jnp.where(chip == row, gain, by_chip[block:]).reshape(2, 1, width)
     doc_rows = jnp.pad(codes, (0, EXTRA * size - block)).reshape(EXTRA, size)
     places = tok * block + jnp.arange(block, dtype=jnp.int32)
     cosine, sine = rotary_tables(places, size, near[0, : size // 2].astype(jnp.float32) < 1e30)

time: 58.2 us -> 63.3 us (1.088)
  local copies, waits for them, and re-layouts: 4.41 us -> 9.83 us
    unnamed x3 -> x5, local copies, waits for them, and re-layouts: 3.97 us -> 9.39 us
    ppermute x5, starting transfers between devices: 0.35 us -> 2.36 us  [by_col(): return lax.ppermute(value, 'col', [(c, c ^ flip) for c in range(4)])]
    ppermute x4, starting transfers between devices: 5.85 us -> 4.12 us  [by_row(): return lax.ppermute(value, 'row', [(0, 1), (1, 0)])]
    ppermute x4, waiting for transfers between devices: 10.5 us -> 9.66 us  [by_row(): return lax.ppermute(value, 'row', [(0, 1), (1, 0)])]
  transfers between devices with their start and end apart: 16 -> 16, of which waited for: 10 -> 9; matrix products, arithmetic and copies ran while one was open for 16% -> 19% of each run, Pallas kernels for 12% -> 11%
where the time goes in v12:
time: 63.3 us; the launch traced here: 62.6 us
  waiting for transfers between devices  18.8 us (30%)
  starting transfers between devices  17 us (27%)
  Pallas kernels  11 us (17%)
  local copies, waits for them, and re-layouts  9.83 us (16%)
  other arithmetic  5.68 us (9%)
    ppermute x4, waiting for transfers between devices, by_row(): return lax.ppermute(value, 'row', [(0, 1), (1, 0)])  9.66 us
    unnamed x5, local copies, waits for them, and re-layouts  9.39 us
    ppermute x5, waiting for transfers between devices, along_tok(): return lax.ppermute(value, 'tok', pairs)  7.95 us
    ppermute x5, starting transfers between devices, along_tok(): return lax.ppermute(value, 'tok', pairs)  5.58 us
    ppermute x4, starting transfers between devices, by_row(): return lax.ppermute(value, 'row', [(0, 1), (1, 0)])  4.12 us
    pallas_call x1, Pallas kernels, per_device(): pl.pallas_call(project_kernel, out_shape=(partial_sums, partial_sums), in...  3.66 us
    ppermute x1, starting transfers between devices, per_device(): lax.ppermute(activations, ('row', 'col'), [(r * 4 + c, c // 2 * 4 + 2 * (...  3.31 us
    pallas_call x1, Pallas kernels, per_device(): pl.pallas_call(normalise_project_kernel, out_shape=(partial_sums, partial...  2.68 us
  transfers between devices with their start and end apart: 16, of which 9 were waited for; matrix products, arithmetic and copies ran while one was open for 19% of the time, Pallas kernels for 11%

profile of v12, /device:TPU:24, one launch (start us, length us, event | category | flops | bytes accessed | tf_op | source)
XLA Modules:
  0.0 62.6 jit_solution(3201864061678943699)
XLA Ops:
  0.0 1.6 %collective-permute-start.2 = (bf16[176,1024]{1,0:T(8,128)(2,1)}, bf16[176,1024]{1,0:T(8,128)(2,1)S(1)}, u32[]{:S(2)}, u32[]{:S(2)}) collective-permute-start(bf16[176,1024]{1,0:T(8,128)(2,1)} %param.4), channel_id=1, source_target_pairs={{0,0},{1,1},{2,4},{3,5},{4,2},{5,3},{6,6},{7,7},{8,8},{9,9},{10,12... | collective-permute-start | bytes 1081352 | tf_op jit(solution)/shard_map/ppermute | solution.py:333
  1.6 3.3 %collective-permute-start.3 = (bf16[176,1024]{1,0:T(8,128)(2,1)}, bf16[176,1024]{1,0:T(8,128)(2,1)S(1)}, u32[]{:S(2)}, u32[]{:S(2)}) collective-permute-start(bf16[176,1024]{1,0:T(8,128)(2,1)} %param.4), channel_id=1, source_target_pairs={{0,2},{1,3},{2,6},{3,7},{4,0},{5,1},{6,4},{7,5},{8,10},{9,11},{10,... | collective-permute-start | bytes 1081352 | tf_op jit(solution)/shard_map/ppermute | solution.py:338
  4.9 1.2 %multiply_reduce_fusion = f32[176]{0:T(256)S(1)} fusion(bf16[176,1024]{1,0:T(8,128)(2,1)} %param.4), kind=kLoop, calls=%fused_computation | loop fusion | flops 540496 | bytes 361152 | tf_op jit(solution)/shard_map/reduce_sum | solution.py:344
  6.1 0.7 %convert_element_type.61 = f32[1024]{0:T(1024)S(1)} convert(bf16[1024]{0:T(1024)(128)(2,1)} %param.5) | non-fusion elementwise | flops 1024 | bytes 6144 | tf_op jit(solution)/shard_map/convert_element_type | solution.py:345
  6.8 0.1 pad_maximum_fusion.3
  6.9 0.7 %convert_add_fusion = f32[176]{0:T(256)S(1)} fusion(s32[176]{0:T(256)} %param.7), kind=kLoop, calls=%fused_computation.28 | loop fusion | flops 352 | bytes 1408 | tf_op jit(solution)/shard_map/add | solution.py:350
  7.6 0.1 pad_add_fusion.1.place_ref
  7.7 0.4 collective-permute-done
  8.0 0.1 pad_maximum_fusion.4
  8.1 0.8 %slice_select_fusion = (f32[1024]{0:T(1024)S(1)}, f32[1024]{0:T(1024)S(1)}) fusion(f32[1200]{0:T(1024)S(1)} %collective-permute-done, bf16[1024]{0:T(1024)(128)(2,1)} %param.5, pred[]{:T(512)S(6)} %eq.22), kind=kLoop, calls=%fused_computation.18 | loop fusion | flops 3072 | bytes 14337 | tf_op jit(solution)/shard_map/jit(_where)/select_n | solution.py:331
  8.9 6.6 %copy.6 = bf16[256,8,4,384]{3,1,2,0:T(8,128)(2,1)} copy(bf16[256,8,4,384]{3,2,1,0:T(4,128)(2,1)} %bitcast.25) | data formatting | bytes 12582912
  15.5 0.2 collective-permute-start.4
  15.8 0.1 concatenate.42
  15.9 1.8 %collective-permute-start.6 = (f32[2400]{0:T(1024)S(1)}, f32[2400]{0:T(1024)S(1)}, u32[]{:S(2)}, u32[]{:S(2)}) collective-permute-start(f32[2400]{0:T(1024)S(1)} %concatenate.42), channel_id=1, source_target_pairs={{0,2},{1,3},{2,0},{3,1},{4,6},{5,7},{6,4},{7,5},{8,10},{9,11},{10,... | collective-permute-start | bytes 28808 | tf_op jit(solution)/shard_map/ppermute | solution.py:324
  17.8 0.2 collective-permute-start.5
  18.0 0.7 %fusion = (f32[352,64]{1,0:T(8,128)S(1)}, f32[352,64]{1,0:T(8,128)S(1)}, f32[352,64]{1,0:T(8,128)S(1)}) fusion(f32[64]{0:T(128)S(1)} %fusion.2, f32[352]{0:T(512)S(1)} %add_convert_fusion.2), kind=kLoop, calls=%fused_computation.12 | loop fusion | flops 45056 | bytes 272000 | tf_op jit(solution)/shard_map/neg | solution.py:26
  18.7 0.2 pad_maximum_fusion
  18.8 0.8 %collective-permute-done.6 = f32[2400]{0:T(1024)S(1)} collective-permute-done((f32[2400]{0:T(1024)S(1)}, f32[2400]{0:T(1024)S(1)}, u32[]{:S(2)}, u32[]{:S(2)}) %collective-permute-start.6) | collective-permute-done | bytes 9632 | tf_op jit(solution)/shard_map/ppermute | solution.py:324
  19.6 0.1 slice_add_fusion
  19.7 0.1 reshape.71.squares_ref
  19.9 2.8 %copy-done = bf16[256,8,4,384]{3,1,2,0:T(8,128)(2,1)S(1)} copy-done((bf16[256,8,4,384]{3,1,2,0:T(8,128)(2,1)S(1)}, bf16[256,8,4,384]{3,1,2,0:T(8,128)(2,1)}, u32[]{:S(2)}) %copy-start) | copy-done | bytes 6291480
  22.7 2.7 %shard_map.46 = (f32[1088,128]{1,0:T(8,128)S(1)}, f32[1088,128]{1,0:T(8,128)S(1)}, bf16[2,352,1024]{2,1,0:T(8,128)(2,1)S(1)}, bf16[2048,768]{1,0:T(8,128)(2,1)}) custom-call(s32[4]{0:T(128)S(1)} %pad_add_fusion.1.place_ref, bf16[176,1024]{1,0:T(8,128)(2,1)S(1)} %collective-permute-done.2.a_near, bf16[176,1024]{1,0:T(8,128)(2,1)S(1)} %collective-permute-done.3.a_far, ...), custom_call_target="tpu_custom_call" | custom-call | tf_op jit(solution)/shard_map/pallas_call | solution.py:371
  25.4 1.9 %collective-permute-start.7 = (f16[1088,128]{1,0:T(8,128)(2,1)S(1)}, f16[1088,128]{1,0:T(8,128)(2,1)S(1)}, u32[]{:S(2)}, u32[]{:S(2)}) collective-permute-start(f16[1088,128]{1,0:T(8,128)(2,1)S(1)} %convert_element_type.66), channel_id=1, source_target_pairs={{0,4},{4,0},{1,5},{5,1},{2,6},{6,2},{3,7},{7,3},{8,12},{12,8},{9,1... | collective-permute-start | bytes 835592 | tf_op jit(solution)/shard_map/ppermute | solution.py:327
  27.4 0.1 fusion.1.docs_ref
  27.5 0.2 collective-permute-start.8
  27.7 3.7 %shard_map.47 = (f32[1088,128]{1,0:T(8,128)S(1)}, f32[1088,128]{1,0:T(8,128)S(1)}) custom-call(bf16[2,352,1024]{2,1,0:T(8,128)(2,1)S(1)} %get-tuple-element.29.normed_ref, f32[16,128]{1,0:T(8,128)S(1)} %fusion.1.docs_ref, f32[352,128]{1,0:T(8,128)S(1)} %get-tuple-element.58.cos_ref, f32[352,128]{1,0:T(8,128)S(1)} %get-tuple-element.59.sin_ref, ...), custom_call_target="tpu_custom_call" | custom-call | tf_op jit(solution)/shard_map/pallas_call | solution.py:389
  31.4 3.7 %collective-permute-done.7 = f16[1088,128]{1,0:T(8,128)(2,1)S(1)} collective-permute-done((f16[1088,128]{1,0:T(8,128)(2,1)S(1)}, f16[1088,128]{1,0:T(8,128)(2,1)S(1)}, u32[]{:S(2)}, u32[]{:S(2)}) %collective-permute-start.7) | collective-permute-done | bytes 278560 | tf_op jit(solution)/shard_map/ppermute | solution.py:327
  35.1 0.1 add_convert_fusion.1.refs_1_.refs_4_.refs_3_
  35.3 0.1 constant_dynamic-slice_fusion.1
  35.4 0.4 collective-permute-start.10
  35.8 0.7 %collective-permute-start.11 = (bf16[720,128]{1,0:T(8,128)(2,1)S(1)}, bf16[720,128]{1,0:T(8,128)(2,1)S(1)}, u32[]{:S(2)}, u32[]{:S(2)}) collective-permute-start(bf16[720,128]{1,0:T(8,128)(2,1)S(1)} %get-tuple-element.41), channel_id=1, source_target_pairs={{8,16},{16,8},{0,0},{24,24},{9,17},{17,9},{1,1},{25,25},{10,18},{1... | collective-permute-start | bytes 552968 | tf_op jit(solution)/shard_map/ppermute | solution.py:426
  36.4 3.3 %collective-permute-done.8 = f16[1088,128]{1,0:T(8,128)(2,1)S(1)} collective-permute-done((f16[1088,128]{1,0:T(8,128)(2,1)S(1)}, f16[1088,128]{1,0:T(8,128)(2,1)S(1)}, u32[]{:S(2)}, u32[]{:S(2)}) %collective-permute-start.8) | collective-permute-done | bytes 278560 | tf_op jit(solution)/shard_map/ppermute | solution.py:327
  39.8 0.1 add_convert_fusion.refs_2_.refs_5_.refs_4_
  39.9 0.5 collective-permute-start.12
  40.5 0.1 pad_add_fusion.refs_0_.place_ref
  40.5 1.8 %shard_map.48 = (f32[2,352,128]{2,1,0:T(8,128)S(1)}, f32[2,352,1]{2,1,0:T(8,128)S(1)}) custom-call(s32[2]{0:T(128)S(1)} %pad_add_fusion.refs_0_.place_ref, bf16[1088,128]{1,0:T(8,128)(2,1)S(1)} %add_convert_fusion.1.refs_1_.refs_4_.refs_3_, bf16[1088,128]{1,0:T(8,128)(2,1)S(1)} %add_convert_fusion.refs_2_.refs_5_.refs_4_), custom_call_target="tpu_custom_call" | custom-call | tf_op jit(solution)/shard_map/pallas_call | solution.py:461
  42.4 0.5 collective-permute-done.10.refs_1_.refs_5_
  42.9 3.5 %collective-permute-done.12.refs_3_.refs_7_ = bf16[720,128]{1,0:T(8,128)(2,1)S(1)} collective-permute-done((bf16[720,128]{1,0:T(8,128)(2,1)S(1)}, bf16[720,128]{1,0:T(8,128)(2,1)S(1)}, u32[]{:S(2)}, u32[]{:S(2)}) %collective-permute-start.12) | collective-permute-done | bytes 184352 | tf_op jit(solution)/shard_map/ppermute | solution.py:426
  46.4 0.6 shard_map.49.refs_8_
  47.0 2.7 %collective-permute-start.13 = (bf16[368,128]{1,0:T(8,128)(2,1)S(1)}, bf16[368,128]{1,0:T(8,128)(2,1)S(1)}, u32[]{:S(2)}, u32[]{:S(2)}) collective-permute-start(bf16[368,128]{1,0:T(8,128)(2,1)S(1)} %get-tuple-element.44), channel_id=1, source_target_pairs={{0,8},{8,24},{16,0},{24,16},{1,9},{9,25},{17,1},{25,17},{2,10},{10... | collective-permute-start | bytes 282632 | tf_op jit(solution)/shard_map/ppermute | solution.py:426
  49.7 1.3 %collective-permute-start.14 = (bf16[368,128]{1,0:T(8,128)(2,1)S(1)}, bf16[368,128]{1,0:T(8,128)(2,1)S(1)}, u32[]{:S(2)}, u32[]{:S(2)}) collective-permute-start(bf16[368,128]{1,0:T(8,128)(2,1)S(1)} %get-tuple-element.43), channel_id=1, source_target_pairs={{8,16},{16,24},{9,17},{17,25},{10,18},{18,26},{11,19},{19,27},{12,... | collective-permute-start | bytes 282632 | tf_op jit(solution)/shard_map/ppermute | solution.py:426
  51.0 1.2 %shard_map.50 = (f32[2,352,128]{2,1,0:T(8,128)S(1)}, f32[2,352,1]{2,1,0:T(8,128)S(1)}) custom-call(s32[2]{0:T(128)S(1)} %pad_add_fusion.refs_0_.place_ref, f32[2,352,128]{2,1,0:T(8,128)S(1)} %get-tuple-element.35.refs_1_, f32[2,352,1]{2,1,0:T(8,128)S(1)} %get-tuple-element.36.refs_6_.refs_2_, ...), custom_call_target="tpu_custom_call" | custom-call | tf_op jit(solution)/shard_map/pallas_call | solution.py:472
  52.3 0.5 collective-permute-done.13.first_ref
  52.7 3.5 %collective-permute-done.14.below_ref = bf16[368,128]{1,0:T(8,128)(2,1)S(1)} collective-permute-done((bf16[368,128]{1,0:T(8,128)(2,1)S(1)}, bf16[368,128]{1,0:T(8,128)(2,1)S(1)}, u32[]{:S(2)}, u32[]{:S(2)}) %collective-permute-start.14) | collective-permute-done | bytes 94240 | tf_op jit(solution)/shard_map/ppermute | solution.py:426
  56.2 1.1 %shard_map.51 = (bf16[176,256]{1,0:T(8,128)(2,1)S(1)}, bf16[176,256]{1,0:T(8,128)(2,1)S(1)}) custom-call(s32[2]{0:T(128)S(1)} %pad_add_fusion.refs_0_.place_ref, f32[2,352,128]{2,1,0:T(8,128)S(1)} %get-tuple-element.37.out_ref, f32[2,352,1]{2,1,0:T(8,128)S(1)} %get-tuple-element.38.logs_ref, bf16[368,128]{1,0:T(8,128)(2,1)S(1)} %collective-permute-done.13.first_ref, ...), custom_call_target="tpu_custom_call" | custom-call | tf_op jit(solution)/shard_map/pallas_call | solution.py:476
  57.3 2.0 %collective-permute-start.15 = (bf16[176,256]{1,0:T(8,128)(2,1)S(1)}, bf16[176,256]{1,0:T(8,128)(2,1)S(1)}, u32[]{:S(2)}, u32[]{:S(2)}) collective-permute-start(bf16[176,256]{1,0:T(8,128)(2,1)S(1)} %get-tuple-element.40), channel_id=1, source_target_pairs={{0,4},{4,0},{1,5},{5,1},{2,6},{6,2},{3,7},{7,3},{8,12},{12,8},{9,1... | collective-permute-start | bytes 270344 | tf_op jit(solution)/shard_map/ppermute | solution.py:327
  59.2 2.6 %collective-permute-done.15 = bf16[176,256]{1,0:T(8,128)(2,1)S(1)} collective-permute-done((bf16[176,256]{1,0:T(8,128)(2,1)S(1)}, bf16[176,256]{1,0:T(8,128)(2,1)S(1)}, u32[]{:S(2)}, u32[]{:S(2)}) %collective-permute-start.15) | collective-permute-done | bytes 90144 | tf_op jit(solution)/shard_map/ppermute | solution.py:327
  61.9 0.7 %pad_maximum_fusion.2 = bf16[176,512]{1,0:T(8,128)(2,1)} fusion(bf16[176,256]{1,0:T(8,128)(2,1)S(1)} %get-tuple-element.46, bf16[176,256]{1,0:T(8,128)(2,1)S(1)} %get-tuple-element.45), kind=kLoop, calls=%fused_computation.7 | loop fusion | flops 360448 | bytes 360448 | tf_op jit(solution)/shard_map/concatenate | solution.py:482
  (26 shorter events, 0.5 us)
Async XLA Ops:
  0.0 15.5 %collective-permute-start.2 = (bf16[176,1024]{1,0:T(8,128)(2,1)}, bf16[176,1024]{1,0:T(8,128)(2,1)S(1)}, u32[]{:S(2)}, u32[]{:S(2)}) collective-permute-start(bf16[176,1024]{1,0:T(8,128)(2,1)} %param.4), channel_id=1, source_target_pairs={{0,0},{1,1},{2,4},{3,5},{4,2},{5,3},{6,6},{7,7},{8,8},{9,9},{10,12... | collective-permute-start | bytes 1081352 | tf_op jit(solution)/shard_map/ppermute | solution.py:333
  1.6 13.9 %collective-permute-start.3 = (bf16[176,1024]{1,0:T(8,128)(2,1)}, bf16[176,1024]{1,0:T(8,128)(2,1)S(1)}, u32[]{:S(2)}, u32[]{:S(2)}) collective-permute-start(bf16[176,1024]{1,0:T(8,128)(2,1)} %param.4), channel_id=1, source_target_pairs={{0,2},{1,3},{2,6},{3,7},{4,0},{5,1},{6,4},{7,5},{8,10},{9,11},{10,... | collective-permute-start | bytes 1081352 | tf_op jit(solution)/shard_map/ppermute | solution.py:338
  6.9 1.2 %collective-permute-start = (f32[1200]{0:T(1024)S(1)}, f32[1200]{0:T(1024)S(1)}, u32[]{:S(2)}, u32[]{:S(2)}) collective-permute-start(f32[1200]{0:T(1024)S(1)} %pad_maximum_fusion.3), channel_id=1, source_target_pairs={{0,1},{1,0},{2,3},{3,2},{4,5},{5,4},{6,7},{7,6},{8,9},{9,8},{10,11... | collective-permute-start | bytes 14408 | tf_op jit(solution)/shard_map/ppermute | solution.py:324
  8.1 7.4 %collective-permute-start.1 = (f32[352]{0:T(512)S(1)}, f32[352]{0:T(512)S(1)}, u32[]{:S(2)}, u32[]{:S(2)}) collective-permute-start(f32[352]{0:T(512)S(1)} %pad_maximum_fusion.4), channel_id=1, source_target_pairs={{0,4},{4,0},{1,5},{5,1},{2,6},{6,2},{3,7},{7,3},{8,12},{12,8},{9,1... | collective-permute-start | bytes 4232 | tf_op jit(solution)/shard_map/ppermute | solution.py:327
  8.9 6.9 %copy-start.1 = (s32[176]{0:T(256)S(1)}, s32[176]{0:T(256)}, u32[]{:S(2)}) copy-start(s32[176]{0:T(256)} %param.7) | copy-start | bytes 2116
  15.5 4.4 %collective-permute-start.4 = (bf16[176,1024]{1,0:T(8,128)(2,1)S(1)}, bf16[176,1024]{1,0:T(8,128)(2,1)S(1)}, u32[]{:S(2)}, u32[]{:S(2)}) collective-permute-start(bf16[176,1024]{1,0:T(8,128)(2,1)S(1)} %collective-permute-done.2.a_near), channel_id=1, source_target_pairs={{0,1},{1,0},{2,3},{3,2},{4,5},{5,4},{6,7},{7,6},{8,9},{9,8},{10,11... | collective-permute-start | bytes 1081352 | tf_op jit(solution)/shard_map/ppermute | solution.py:324
  15.9 3.7 %collective-permute-start.6 = (f32[2400]{0:T(1024)S(1)}, f32[2400]{0:T(1024)S(1)}, u32[]{:S(2)}, u32[]{:S(2)}) collective-permute-start(f32[2400]{0:T(1024)S(1)} %concatenate.42), channel_id=1, source_target_pairs={{0,2},{1,3},{2,0},{3,1},{4,6},{5,7},{6,4},{7,5},{8,10},{9,11},{10,... | collective-permute-start | bytes 28808 | tf_op jit(solution)/shard_map/ppermute | solution.py:324
  17.8 2.2 %collective-permute-start.5 = (bf16[176,1024]{1,0:T(8,128)(2,1)S(1)}, bf16[176,1024]{1,0:T(8,128)(2,1)S(1)}, u32[]{:S(2)}, u32[]{:S(2)}) collective-permute-start(bf16[176,1024]{1,0:T(8,128)(2,1)S(1)} %collective-permute-done.3.a_far), channel_id=1, source_target_pairs={{0,1},{1,0},{2,3},{3,2},{4,5},{5,4},{6,7},{7,6},{8,9},{9,8},{10,11... | collective-permute-start | bytes 1081352 | tf_op jit(solution)/shard_map/ppermute | solution.py:324
  19.9 2.8 %copy-start = (bf16[256,8,4,384]{3,1,2,0:T(8,128)(2,1)S(1)}, bf16[256,8,4,384]{3,1,2,0:T(8,128)(2,1)}, u32[]{:S(2)}) copy-start(bf16[256,8,4,384]{3,1,2,0:T(8,128)(2,1)} %copy.6) | copy-start | bytes 18874372
  25.4 9.6 %collective-permute-start.7 = (f16[1088,128]{1,0:T(8,128)(2,1)S(1)}, f16[1088,128]{1,0:T(8,128)(2,1)S(1)}, u32[]{:S(2)}, u32[]{:S(2)}) collective-permute-start(f16[1088,128]{1,0:T(8,128)(2,1)S(1)} %convert_element_type.66), channel_id=1, source_target_pairs={{0,4},{4,0},{1,5},{5,1},{2,6},{6,2},{3,7},{7,3},{8,12},{12,8},{9,1... | collective-permute-start | bytes 835592 | tf_op jit(solution)/shard_map/ppermute | solution.py:327
  27.5 12.3 %collective-permute-start.8 = (f16[1088,128]{1,0:T(8,128)(2,1)S(1)}, f16[1088,128]{1,0:T(8,128)(2,1)S(1)}, u32[]{:S(2)}, u32[]{:S(2)}) collective-permute-start(f16[1088,128]{1,0:T(8,128)(2,1)S(1)} %convert_element_type.69), channel_id=1, source_target_pairs={{0,4},{4,0},{1,5},{5,1},{2,6},{6,2},{3,7},{7,3},{8,12},{12,8},{9,1... | collective-permute-start | bytes 835592 | tf_op jit(solution)/shard_map/ppermute | solution.py:327
  35.2 1.3 %collective-permute-start.9 = (bf16[16,128]{1,0:T(8,128)(2,1)S(1)}, bf16[16,128]{1,0:T(8,128)(2,1)S(1)}, u32[]{:S(2)}, u32[]{:S(2)}) collective-permute-start(bf16[16,128]{1,0:T(8,128)(2,1)S(1)} %slice.51), channel_id=1, source_target_pairs={{0,1},{1,0},{2,3},{3,2},{4,5},{5,4},{6,7},{7,6},{8,9},{9,8},{10,11... | collective-permute-start | bytes 12296 | tf_op jit(solution)/shard_map/ppermute | solution.py:324
  35.4 7.5 %collective-permute-start.10 = (bf16[720,128]{1,0:T(8,128)(2,1)S(1)}, bf16[720,128]{1,0:T(8,128)(2,1)S(1)}, u32[]{:S(2)}, u32[]{:S(2)}) collective-permute-start(bf16[720,128]{1,0:T(8,128)(2,1)S(1)} %get-tuple-element.42), channel_id=1, source_target_pairs={{0,16},{24,8},{8,0},{16,24},{1,17},{25,9},{9,1},{17,25},{2,18},{26... | collective-permute-start | bytes 552968 | tf_op jit(solution)/shard_map/ppermute | solution.py:426
  35.8 7.1 %collective-permute-start.11 = (bf16[720,128]{1,0:T(8,128)(2,1)S(1)}, bf16[720,128]{1,0:T(8,128)(2,1)S(1)}, u32[]{:S(2)}, u32[]{:S(2)}) collective-permute-start(bf16[720,128]{1,0:T(8,128)(2,1)S(1)} %get-tuple-element.41), channel_id=1, source_target_pairs={{8,16},{16,8},{0,0},{24,24},{9,17},{17,9},{1,1},{25,25},{10,18},{1... | collective-permute-start | bytes 552968 | tf_op jit(solution)/shard_map/ppermute | solution.py:426
  39.9 6.5 %collective-permute-start.12 = (bf16[720,128]{1,0:T(8,128)(2,1)S(1)}, bf16[720,128]{1,0:T(8,128)(2,1)S(1)}, u32[]{:S(2)}, u32[]{:S(2)}) collective-permute-start(bf16[720,128]{1,0:T(8,128)(2,1)S(1)} %constant_dynamic-slice_fusion), channel_id=1, source_target_pairs={{0,8},{8,0},{16,24},{24,16},{1,9},{9,1},{17,25},{25,17},{2,10},{10... | collective-permute-start | bytes 552968 | tf_op jit(solution)/shard_map/ppermute | solution.py:426
  47.0 5.7 %collective-permute-start.13 = (bf16[368,128]{1,0:T(8,128)(2,1)S(1)}, bf16[368,128]{1,0:T(8,128)(2,1)S(1)}, u32[]{:S(2)}, u32[]{:S(2)}) collective-permute-start(bf16[368,128]{1,0:T(8,128)(2,1)S(1)} %get-tuple-element.44), channel_id=1, source_target_pairs={{0,8},{8,24},{16,0},{24,16},{1,9},{9,25},{17,1},{25,17},{2,10},{10... | collective-permute-start | bytes 282632 | tf_op jit(solution)/shard_map/ppermute | solution.py:426
  49.7 6.5 %collective-permute-start.14 = (bf16[368,128]{1,0:T(8,128)(2,1)S(1)}, bf16[368,128]{1,0:T(8,128)(2,1)S(1)}, u32[]{:S(2)}, u32[]{:S(2)}) collective-permute-start(bf16[368,128]{1,0:T(8,128)(2,1)S(1)} %get-tuple-element.43), channel_id=1, source_target_pairs={{8,16},{16,24},{9,17},{17,25},{10,18},{18,26},{11,19},{19,27},{12,... | collective-permute-start | bytes 282632 | tf_op jit(solution)/shard_map/ppermute | solution.py:426
  57.3 4.6 %collective-permute-start.15 = (bf16[176,256]{1,0:T(8,128)(2,1)S(1)}, bf16[176,256]{1,0:T(8,128)(2,1)S(1)}, u32[]{:S(2)}, u32[]{:S(2)}) collective-permute-start(bf16[176,256]{1,0:T(8,128)(2,1)S(1)} %get-tuple-element.40), channel_id=1, source_target_pairs={{0,4},{4,0},{1,5},{5,1},{2,6},{6,2},{3,7},{7,3},{8,12},{12,8},{9,1... | collective-permute-start | bytes 270344 | tf_op jit(solution)/shard_map/ppermute | solution.py:327

commit v13 on v11

--- a/solution.py
+++ b/solution.py
@@ -151,13 +151,12 @@
     scores = lax.dot_general(
         query, keys, (((1,), (1,)), ((), ())), preferred_element_type=jnp.float32
     )
-    top = jnp.max(jnp.where(visible, scores, LOW), axis=1, keepdims=True)
-    exponentials = jnp.where(visible, jnp.exp2((scores - top) * (scale * LOG2_E)), 0.0)
+    masked = jnp.where(visible, scores, LOW)
+    top = jnp.max(masked, axis=1, keepdims=True)
+    exponentials = jnp.exp2((masked - top) * (scale * LOG2_E))
     total = jnp.sum(exponentials, axis=1, keepdims=True)
     summed = jnp.dot(exponentials.astype(jnp.bfloat16), values, preferred_element_type=jnp.float32)
-    some = total > 0.0
-    safe = jnp.where(some, total, 1.0)
-    return summed / safe, jnp.where(some, top * scale + jnp.log(safe), LOW)
+    return summed / total, jnp.where(top > LOW / 2, top * scale + jnp.log(total), LOW)
 
 
 def as_message(output, logs, size):
@@ -444,7 +443,7 @@
         chunk_one = summed(0)
         two_away = along_tok(keys_or_query(chunk_one, tok == 3), [(0, 2), (3, 1), (1, 0), (2, 3)])
         swapped = along_tok(keys_or_query(chunk_one, tok == 2), [(1, 2), (2, 1), (0, 0), (3, 3)])
-        across = by_col(chunk_one[:EXTRA], 1)
+        across = by_col(chunk_one[:EXTRA], 2)
         arrived[1] = jnp.where(
             tok < toks,
             arrived[1].astype(jnp.float32),

time: 58.2 us -> 57.6 us (0.990)
    ppermute x5, starting transfers between devices: 0.35 us -> 2.2 us  [by_col(): return lax.ppermute(value, 'col', [(c, c ^ flip) for c in range(4)])]
    ppermute x4, starting transfers between devices: 5.85 us -> 4.02 us  [by_row(): return lax.ppermute(value, 'row', [(0, 1), (1, 0)])]
    ppermute x4, waiting for transfers between devices: 10.5 us -> 9.9 us  [by_row(): return lax.ppermute(value, 'row', [(0, 1), (1, 0)])]
  transfers between devices with their start and end apart: 16 -> 16, of which waited for: 10 -> 11; matrix products, arithmetic and copies ran while one was open for 16% -> 16% of each run, Pallas kernels for 12% -> 12%
where the time goes in v13:
time: 57.6 us; the launch traced here: 57.1 us
  waiting for transfers between devices  18.8 us (33%)
  starting transfers between devices  17 us (30%)
  Pallas kernels  11 us (19%)
  other arithmetic  5.65 us (10%)
  local copies, waits for them, and re-layouts  4.4 us (8%)
    ppermute x4, waiting for transfers between devices, by_row(): return lax.ppermute(value, 'row', [(0, 1), (1, 0)])  9.9 us
    ppermute x5, waiting for transfers between devices, along_tok(): return lax.ppermute(value, 'tok', pairs)  7.29 us
    ppermute x5, starting transfers between devices, along_tok(): return lax.ppermute(value, 'tok', pairs)  5.8 us
    ppermute x4, starting transfers between devices, by_row(): return lax.ppermute(value, 'row', [(0, 1), (1, 0)])  4.02 us
    unnamed x3, local copies, waits for them, and re-layouts  3.97 us
    pallas_call x1, Pallas kernels, per_device(): pl.pallas_call(project_kernel, out_shape=(partial_sums, partial_sums), in...  3.66 us
    ppermute x1, starting transfers between devices, per_device(): lax.ppermute(activations, ('row', 'col'), [(r * 4 + c, c // 2 * 4 + 2 * (...  3.31 us
    pallas_call x1, Pallas kernels, per_device(): pl.pallas_call(normalise_project_kernel, out_shape=(partial_sums, partial...  2.69 us
  transfers between devices with their start and end apart: 16, of which 11 were waited for; matrix products, arithmetic and copies ran while one was open for 16% of the time, Pallas kernels for 12%

profile of v13, /device:TPU:24, one launch (start us, length us, event | category | flops | bytes accessed | tf_op | source)
XLA Modules:
  0.0 57.1 jit_solution(2758421777378063804)
XLA Ops:
  0.0 1.6 %collective-permute-start = (bf16[176,1024]{1,0:T(8,128)(2,1)}, bf16[176,1024]{1,0:T(8,128)(2,1)S(1)}, u32[]{:S(2)}, u32[]{:S(2)}) collective-permute-start(bf16[176,1024]{1,0:T(8,128)(2,1)} %param.4), channel_id=1, source_target_pairs={{0,0},{1,1},{2,4},{3,5},{4,2},{5,3},{6,6},{7,7},{8,8},{9,9},{10,12... | collective-permute-start | bytes 1081352 | tf_op jit(solution)/shard_map/ppermute | solution.py:333
  1.6 3.3 %collective-permute-start.1 = (bf16[176,1024]{1,0:T(8,128)(2,1)}, bf16[176,1024]{1,0:T(8,128)(2,1)S(1)}, u32[]{:S(2)}, u32[]{:S(2)}) collective-permute-start(bf16[176,1024]{1,0:T(8,128)(2,1)} %param.4), channel_id=1, source_target_pairs={{0,2},{1,3},{2,6},{3,7},{4,0},{5,1},{6,4},{7,5},{8,10},{9,11},{10,... | collective-permute-start | bytes 1081352 | tf_op jit(solution)/shard_map/ppermute | solution.py:338
  4.9 1.2 %multiply_reduce_fusion = f32[176]{0:T(256)S(1)} fusion(bf16[176,1024]{1,0:T(8,128)(2,1)} %param.4), kind=kLoop, calls=%fused_computation | loop fusion | flops 540496 | bytes 361152 | tf_op jit(solution)/shard_map/reduce_sum | solution.py:344
  6.1 0.7 %convert_element_type.61 = f32[1024]{0:T(1024)S(1)} convert(bf16[1024]{0:T(1024)(128)(2,1)} %param.5) | non-fusion elementwise | flops 1024 | bytes 6144 | tf_op jit(solution)/shard_map/convert_element_type | solution.py:345
  6.8 0.1 pad_maximum_fusion.3
  6.9 0.7 %convert_add_fusion = f32[176]{0:T(256)S(1)} fusion(s32[176]{0:T(256)} %param.7), kind=kLoop, calls=%fused_computation.28 | loop fusion | flops 352 | bytes 1408 | tf_op jit(solution)/shard_map/add | solution.py:357
  7.6 0.5 collective-permute-done.2
  8.0 0.8 %slice_select_fusion = (f32[1024]{0:T(1024)S(1)}, f32[1024]{0:T(1024)S(1)}) fusion(f32[1200]{0:T(1024)S(1)} %collective-permute-done.2, bf16[1024]{0:T(1024)(128)(2,1)} %param.5, pred[]{:T(512)S(6)} %eq.22), kind=kLoop, calls=%fused_computation.18 | loop fusion | flops 3072 | bytes 14337 | tf_op jit(solution)/shard_map/jit(_where)/select_n | solution.py:331
  8.8 0.1 concatenate.40
  8.9 0.1 pad_add_fusion.1.place_ref
  9.0 4.0 %copy.6 = bf16[256,8,4,384]{3,1,2,0:T(8,128)(2,1)S(1)} copy(bf16[256,8,4,384]{3,2,1,0:T(4,128)(2,1)} %bitcast.25) | data formatting | bytes 12582912
  12.9 0.5 collective-permute-done.3
  13.5 0.1 slice.39
  13.6 0.1 pad_maximum_fusion.4
  13.7 1.8 %collective-permute-start.6 = (f32[352]{0:T(512)S(1)}, f32[352]{0:T(512)S(1)}, u32[]{:S(2)}, u32[]{:S(2)}) collective-permute-start(f32[352]{0:T(512)S(1)} %pad_maximum_fusion.4), channel_id=1, source_target_pairs={{0,4},{4,0},{1,5},{5,1},{2,6},{6,2},{3,7},{7,3},{8,12},{12,8},{9,1... | collective-permute-start | bytes 4232 | tf_op jit(solution)/shard_map/ppermute | solution.py:327
  15.5 0.2 collective-permute-start.5
  15.7 0.7 %fusion = (f32[352,64]{1,0:T(8,128)S(1)}, f32[352,64]{1,0:T(8,128)S(1)}, f32[352,64]{1,0:T(8,128)S(1)}) fusion(f32[64]{0:T(128)S(1)} %fusion.2, f32[352]{0:T(512)S(1)} %add_convert_fusion.2), kind=kLoop, calls=%fused_computation.12 | loop fusion | flops 45056 | bytes 272000 | tf_op jit(solution)/shard_map/neg | solution.py:26
  16.4 0.2 pad_maximum_fusion
  16.6 0.7 %collective-permute-done.6 = f32[352]{0:T(512)S(1)} collective-permute-done((f32[352]{0:T(512)S(1)}, f32[352]{0:T(512)S(1)}, u32[]{:S(2)}, u32[]{:S(2)}) %collective-permute-start.6) | collective-permute-done | bytes 1440 | tf_op jit(solution)/shard_map/ppermute | solution.py:327
  17.4 0.1 pad_maximum_fusion.5
  17.4 0.1 reshape.71.squares_ref
  17.6 2.7 %shard_map.46 = (f32[1088,128]{1,0:T(8,128)S(1)}, f32[1088,128]{1,0:T(8,128)S(1)}, bf16[2,352,1024]{2,1,0:T(8,128)(2,1)S(1)}, bf16[2048,768]{1,0:T(8,128)(2,1)}) custom-call(s32[4]{0:T(128)S(1)} %pad_add_fusion.1.place_ref, bf16[176,1024]{1,0:T(8,128)(2,1)S(1)} %collective-permute-done.a_near, bf16[176,1024]{1,0:T(8,128)(2,1)S(1)} %collective-permute-done.1.a_far, ...), custom_call_target="tpu_custom_call" | custom-call | tf_op jit(solution)/shard_map/pallas_call | solution.py:370
  20.3 1.9 %collective-permute-start.7 = (f16[1088,128]{1,0:T(8,128)(2,1)S(1)}, f16[1088,128]{1,0:T(8,128)(2,1)S(1)}, u32[]{:S(2)}, u32[]{:S(2)}) collective-permute-start(f16[1088,128]{1,0:T(8,128)(2,1)S(1)} %convert_element_type.66), channel_id=1, source_target_pairs={{0,4},{4,0},{1,5},{5,1},{2,6},{6,2},{3,7},{7,3},{8,12},{12,8},{9,1... | collective-permute-start | bytes 835592 | tf_op jit(solution)/shard_map/ppermute | solution.py:327
  22.2 0.1 fusion.1.docs_ref
  22.3 0.3 collective-permute-start.8
  22.6 3.7 %shard_map.47 = (f32[1088,128]{1,0:T(8,128)S(1)}, f32[1088,128]{1,0:T(8,128)S(1)}) custom-call(bf16[2,352,1024]{2,1,0:T(8,128)(2,1)S(1)} %get-tuple-element.29.normed_ref, f32[16,128]{1,0:T(8,128)S(1)} %fusion.1.docs_ref, f32[352,128]{1,0:T(8,128)S(1)} %get-tuple-element.58.cos_ref, f32[352,128]{1,0:T(8,128)S(1)} %get-tuple-element.59.sin_ref, ...), custom_call_target="tpu_custom_call" | custom-call | tf_op jit(solution)/shard_map/pallas_call | solution.py:388
  26.3 3.7 %collective-permute-done.7 = f16[1088,128]{1,0:T(8,128)(2,1)S(1)} collective-permute-done((f16[1088,128]{1,0:T(8,128)(2,1)S(1)}, f16[1088,128]{1,0:T(8,128)(2,1)S(1)}, u32[]{:S(2)}, u32[]{:S(2)}) %collective-permute-start.7) | collective-permute-done | bytes 278560 | tf_op jit(solution)/shard_map/ppermute | solution.py:327
  30.0 1.9 %collective-permute-start.9 = (bf16[16,128]{1,0:T(8,128)(2,1)S(1)}, bf16[16,128]{1,0:T(8,128)(2,1)S(1)}, u32[]{:S(2)}, u32[]{:S(2)}) collective-permute-start(bf16[16,128]{1,0:T(8,128)(2,1)S(1)} %slice.49), channel_id=1, source_target_pairs={{0,2},{1,3},{2,0},{3,1},{4,6},{5,7},{6,4},{7,5},{8,10},{9,11},{10,... | collective-permute-start | bytes 12296 | tf_op jit(solution)/shard_map/ppermute | solution.py:324
  31.9 0.1 constant_dynamic-slice_fusion.1
  32.0 0.4 collective-permute-start.10
  32.4 0.7 %collective-permute-start.11 = (bf16[720,128]{1,0:T(8,128)(2,1)S(1)}, bf16[720,128]{1,0:T(8,128)(2,1)S(1)}, u32[]{:S(2)}, u32[]{:S(2)}) collective-permute-start(bf16[720,128]{1,0:T(8,128)(2,1)S(1)} %get-tuple-element.41), channel_id=1, source_target_pairs={{8,16},{16,8},{0,0},{24,24},{9,17},{17,9},{1,1},{25,25},{10,18},{1... | collective-permute-start | bytes 552968 | tf_op jit(solution)/shard_map/ppermute | solution.py:425
  33.1 0.6 %collective-permute-done.9 = bf16[16,128]{1,0:T(8,128)(2,1)S(1)} collective-permute-done((bf16[16,128]{1,0:T(8,128)(2,1)S(1)}, bf16[16,128]{1,0:T(8,128)(2,1)S(1)}, u32[]{:S(2)}, u32[]{:S(2)}) %collective-permute-start.9) | collective-permute-done | bytes 4128 | tf_op jit(solution)/shard_map/ppermute | solution.py:324
  33.7 1.0 %collective-permute-done.8 = f16[1088,128]{1,0:T(8,128)(2,1)S(1)} collective-permute-done((f16[1088,128]{1,0:T(8,128)(2,1)S(1)}, f16[1088,128]{1,0:T(8,128)(2,1)S(1)}, u32[]{:S(2)}, u32[]{:S(2)}) %collective-permute-start.8) | collective-permute-done | bytes 278560 | tf_op jit(solution)/shard_map/ppermute | solution.py:327
  34.7 0.1 add_convert_fusion.refs_2_.refs_5_.refs_4_
  34.9 1.4 %collective-permute-start.12 = (bf16[720,128]{1,0:T(8,128)(2,1)S(1)}, bf16[720,128]{1,0:T(8,128)(2,1)S(1)}, u32[]{:S(2)}, u32[]{:S(2)}) collective-permute-start(bf16[720,128]{1,0:T(8,128)(2,1)S(1)} %constant_dynamic-slice_fusion), channel_id=1, source_target_pairs={{0,8},{8,0},{16,24},{24,16},{1,9},{9,1},{17,25},{25,17},{2,10},{10... | collective-permute-start | bytes 552968 | tf_op jit(solution)/shard_map/ppermute | solution.py:425
  36.3 0.1 pad_add_fusion.refs_0_.place_ref
  36.4 1.8 %shard_map.48 = (f32[2,352,128]{2,1,0:T(8,128)S(1)}, f32[2,352,1]{2,1,0:T(8,128)S(1)}) custom-call(s32[2]{0:T(128)S(1)} %pad_add_fusion.refs_0_.place_ref, bf16[1088,128]{1,0:T(8,128)(2,1)S(1)} %add_convert_fusion.1.refs_1_.refs_4_.refs_3_, bf16[1088,128]{1,0:T(8,128)(2,1)S(1)} %add_convert_fusion.refs_2_.refs_5_.refs_4_), custom_call_target="tpu_custom_call" | custom-call | tf_op jit(solution)/shard_map/pallas_call | solution.py:460
  38.2 0.6 %collective-permute-done.10.refs_1_.refs_5_ = bf16[720,128]{1,0:T(8,128)(2,1)S(1)} collective-permute-done((bf16[720,128]{1,0:T(8,128)(2,1)S(1)}, bf16[720,128]{1,0:T(8,128)(2,1)S(1)}, u32[]{:S(2)}, u32[]{:S(2)}) %collective-permute-start.10) | collective-permute-done | bytes 184352 | tf_op jit(solution)/shard_map/ppermute | solution.py:425
  38.9 2.7 %collective-permute-done.12.refs_3_.refs_7_ = bf16[720,128]{1,0:T(8,128)(2,1)S(1)} collective-permute-done((bf16[720,128]{1,0:T(8,128)(2,1)S(1)}, bf16[720,128]{1,0:T(8,128)(2,1)S(1)}, u32[]{:S(2)}, u32[]{:S(2)}) %collective-permute-start.12) | collective-permute-done | bytes 184352 | tf_op jit(solution)/shard_map/ppermute | solution.py:425
  41.6 0.6 shard_map.49.refs_8_
  42.2 2.0 %collective-permute-start.13 = (bf16[368,128]{1,0:T(8,128)(2,1)S(1)}, bf16[368,128]{1,0:T(8,128)(2,1)S(1)}, u32[]{:S(2)}, u32[]{:S(2)}) collective-permute-start(bf16[368,128]{1,0:T(8,128)(2,1)S(1)} %get-tuple-element.44), channel_id=1, source_target_pairs={{0,8},{8,24},{16,0},{24,16},{1,9},{9,25},{17,1},{25,17},{2,10},{10... | collective-permute-start | bytes 282632 | tf_op jit(solution)/shard_map/ppermute | solution.py:425
  44.2 1.3 %collective-permute-start.14 = (bf16[368,128]{1,0:T(8,128)(2,1)S(1)}, bf16[368,128]{1,0:T(8,128)(2,1)S(1)}, u32[]{:S(2)}, u32[]{:S(2)}) collective-permute-start(bf16[368,128]{1,0:T(8,128)(2,1)S(1)} %get-tuple-element.43), channel_id=1, source_target_pairs={{8,16},{16,24},{9,17},{17,25},{10,18},{18,26},{11,19},{19,27},{12,... | collective-permute-start | bytes 282632 | tf_op jit(solution)/shard_map/ppermute | solution.py:425
  45.5 1.2 %shard_map.50 = (f32[2,352,128]{2,1,0:T(8,128)S(1)}, f32[2,352,1]{2,1,0:T(8,128)S(1)}) custom-call(s32[2]{0:T(128)S(1)} %pad_add_fusion.refs_0_.place_ref, f32[2,352,128]{2,1,0:T(8,128)S(1)} %get-tuple-element.35.refs_1_, f32[2,352,1]{2,1,0:T(8,128)S(1)} %get-tuple-element.36.refs_6_.refs_2_, ...), custom_call_target="tpu_custom_call" | custom-call | tf_op jit(solution)/shard_map/pallas_call | solution.py:471
  46.8 1.3 %collective-permute-done.13.first_ref = bf16[368,128]{1,0:T(8,128)(2,1)S(1)} collective-permute-done((bf16[368,128]{1,0:T(8,128)(2,1)S(1)}, bf16[368,128]{1,0:T(8,128)(2,1)S(1)}, u32[]{:S(2)}, u32[]{:S(2)}) %collective-permute-start.13) | collective-permute-done | bytes 94240 | tf_op jit(solution)/shard_map/ppermute | solution.py:425
  48.1 2.6 %collective-permute-done.14.below_ref = bf16[368,128]{1,0:T(8,128)(2,1)S(1)} collective-permute-done((bf16[368,128]{1,0:T(8,128)(2,1)S(1)}, bf16[368,128]{1,0:T(8,128)(2,1)S(1)}, u32[]{:S(2)}, u32[]{:S(2)}) %collective-permute-start.14) | collective-permute-done | bytes 94240 | tf_op jit(solution)/shard_map/ppermute | solution.py:425
  50.7 1.1 %shard_map.51 = (bf16[176,256]{1,0:T(8,128)(2,1)S(1)}, bf16[176,256]{1,0:T(8,128)(2,1)S(1)}) custom-call(s32[2]{0:T(128)S(1)} %pad_add_fusion.refs_0_.place_ref, f32[2,352,128]{2,1,0:T(8,128)S(1)} %get-tuple-element.37.out_ref, f32[2,352,1]{2,1,0:T(8,128)S(1)} %get-tuple-element.38.logs_ref, bf16[368,128]{1,0:T(8,128)(2,1)S(1)} %collective-permute-done.13.first_ref, ...), custom_call_target="tpu_custom_call" | custom-call | tf_op jit(solution)/shard_map/pallas_call | solution.py:475
  51.8 4.5 %collective-permute-done.15 = bf16[176,256]{1,0:T(8,128)(2,1)S(1)} collective-permute-done((bf16[176,256]{1,0:T(8,128)(2,1)S(1)}, bf16[176,256]{1,0:T(8,128)(2,1)S(1)}, u32[]{:S(2)}, u32[]{:S(2)}) %collective-permute-start.15) | collective-permute-done | bytes 90144 | tf_op jit(solution)/shard_map/ppermute | solution.py:327
  56.4 0.7 %pad_maximum_fusion.2 = bf16[176,512]{1,0:T(8,128)(2,1)} fusion(bf16[176,256]{1,0:T(8,128)(2,1)S(1)} %get-tuple-element.46, bf16[176,256]{1,0:T(8,128)(2,1)S(1)} %get-tuple-element.45), kind=kLoop, calls=%fused_computation.7 | loop fusion | flops 360448 | bytes 360448 | tf_op jit(solution)/shard_map/concatenate | solution.py:481
  (25 shorter events, 0.5 us)
Async XLA Ops:
  0.0 13.5 %collective-permute-start = (bf16[176,1024]{1,0:T(8,128)(2,1)}, bf16[176,1024]{1,0:T(8,128)(2,1)S(1)}, u32[]{:S(2)}, u32[]{:S(2)}) collective-permute-start(bf16[176,1024]{1,0:T(8,128)(2,1)} %param.4), channel_id=1, source_target_pairs={{0,0},{1,1},{2,4},{3,5},{4,2},{5,3},{6,6},{7,7},{8,8},{9,9},{10,12... | collective-permute-start | bytes 1081352 | tf_op jit(solution)/shard_map/ppermute | solution.py:333
  1.6 11.8 %collective-permute-start.1 = (bf16[176,1024]{1,0:T(8,128)(2,1)}, bf16[176,1024]{1,0:T(8,128)(2,1)S(1)}, u32[]{:S(2)}, u32[]{:S(2)}) collective-permute-start(bf16[176,1024]{1,0:T(8,128)(2,1)} %param.4), channel_id=1, source_target_pairs={{0,2},{1,3},{2,6},{3,7},{4,0},{5,1},{6,4},{7,5},{8,10},{9,11},{10,... | collective-permute-start | bytes 1081352 | tf_op jit(solution)/shard_map/ppermute | solution.py:338
  6.9 1.2 %collective-permute-start.2 = (f32[1200]{0:T(1024)S(1)}, f32[1200]{0:T(1024)S(1)}, u32[]{:S(2)}, u32[]{:S(2)}) collective-permute-start(f32[1200]{0:T(1024)S(1)} %pad_maximum_fusion.3), channel_id=1, source_target_pairs={{0,1},{1,0},{2,3},{3,2},{4,5},{5,4},{6,7},{7,6},{8,9},{9,8},{10,11... | collective-permute-start | bytes 14408 | tf_op jit(solution)/shard_map/ppermute | solution.py:324
  8.9 4.6 %collective-permute-start.3 = (f32[2224]{0:T(1024)S(1)}, f32[2224]{0:T(1024)S(1)}, u32[]{:S(2)}, u32[]{:S(2)}) collective-permute-start(f32[2224]{0:T(1024)S(1)} %concatenate.40), channel_id=1, source_target_pairs={{0,2},{1,3},{2,0},{3,1},{4,6},{5,7},{6,4},{7,5},{8,10},{9,11},{10,... | collective-permute-start | bytes 26696 | tf_op jit(solution)/shard_map/ppermute | solution.py:324
  9.0 8.3 %copy-start = (s32[176]{0:T(256)S(1)}, s32[176]{0:T(256)}, u32[]{:S(2)}) copy-start(s32[176]{0:T(256)} %param.7) | copy-start | bytes 2116
  13.6 4.0 %collective-permute-start.4 = (bf16[176,1024]{1,0:T(8,128)(2,1)S(1)}, bf16[176,1024]{1,0:T(8,128)(2,1)S(1)}, u32[]{:S(2)}, u32[]{:S(2)}) collective-permute-start(bf16[176,1024]{1,0:T(8,128)(2,1)S(1)} %collective-permute-done.a_near), channel_id=1, source_target_pairs={{0,1},{1,0},{2,3},{3,2},{4,5},{5,4},{6,7},{7,6},{8,9},{9,8},{10,11... | collective-permute-start | bytes 1081352 | tf_op jit(solution)/shard_map/ppermute | solution.py:324
  13.7 3.6 %collective-permute-start.6 = (f32[352]{0:T(512)S(1)}, f32[352]{0:T(512)S(1)}, u32[]{:S(2)}, u32[]{:S(2)}) collective-permute-start(f32[352]{0:T(512)S(1)} %pad_maximum_fusion.4), channel_id=1, source_target_pairs={{0,4},{4,0},{1,5},{5,1},{2,6},{6,2},{3,7},{7,3},{8,12},{12,8},{9,1... | collective-permute-start | bytes 4232 | tf_op jit(solution)/shard_map/ppermute | solution.py:327
  15.5 2.1 %collective-permute-start.5 = (bf16[176,1024]{1,0:T(8,128)(2,1)S(1)}, bf16[176,1024]{1,0:T(8,128)(2,1)S(1)}, u32[]{:S(2)}, u32[]{:S(2)}) collective-permute-start(bf16[176,1024]{1,0:T(8,128)(2,1)S(1)} %collective-permute-done.1.a_far), channel_id=1, source_target_pairs={{0,1},{1,0},{2,3},{3,2},{4,5},{5,4},{6,7},{7,6},{8,9},{9,8},{10,11... | collective-permute-start | bytes 1081352 | tf_op jit(solution)/shard_map/ppermute | solution.py:324
  20.3 9.6 %collective-permute-start.7 = (f16[1088,128]{1,0:T(8,128)(2,1)S(1)}, f16[1088,128]{1,0:T(8,128)(2,1)S(1)}, u32[]{:S(2)}, u32[]{:S(2)}) collective-permute-start(f16[1088,128]{1,0:T(8,128)(2,1)S(1)} %convert_element_type.66), channel_id=1, source_target_pairs={{0,4},{4,0},{1,5},{5,1},{2,6},{6,2},{3,7},{7,3},{8,12},{12,8},{9,1... | collective-permute-start | bytes 835592 | tf_op jit(solution)/shard_map/ppermute | solution.py:327
  22.3 12.4 %collective-permute-start.8 = (f16[1088,128]{1,0:T(8,128)(2,1)S(1)}, f16[1088,128]{1,0:T(8,128)(2,1)S(1)}, u32[]{:S(2)}, u32[]{:S(2)}) collective-permute-start(f16[1088,128]{1,0:T(8,128)(2,1)S(1)} %convert_element_type.69), channel_id=1, source_target_pairs={{0,4},{4,0},{1,5},{5,1},{2,6},{6,2},{3,7},{7,3},{8,12},{12,8},{9,1... | collective-permute-start | bytes 835592 | tf_op jit(solution)/shard_map/ppermute | solution.py:327
  30.0 3.7 %collective-permute-start.9 = (bf16[16,128]{1,0:T(8,128)(2,1)S(1)}, bf16[16,128]{1,0:T(8,128)(2,1)S(1)}, u32[]{:S(2)}, u32[]{:S(2)}) collective-permute-start(bf16[16,128]{1,0:T(8,128)(2,1)S(1)} %slice.49), channel_id=1, source_target_pairs={{0,2},{1,3},{2,0},{3,1},{4,6},{5,7},{6,4},{7,5},{8,10},{9,11},{10,... | collective-permute-start | bytes 12296 | tf_op jit(solution)/shard_map/ppermute | solution.py:324
  32.0 6.8 %collective-permute-start.10 = (bf16[720,128]{1,0:T(8,128)(2,1)S(1)}, bf16[720,128]{1,0:T(8,128)(2,1)S(1)}, u32[]{:S(2)}, u32[]{:S(2)}) collective-permute-start(bf16[720,128]{1,0:T(8,128)(2,1)S(1)} %get-tuple-element.42), channel_id=1, source_target_pairs={{0,16},{24,8},{8,0},{16,24},{1,17},{25,9},{9,1},{17,25},{2,18},{26... | collective-permute-start | bytes 552968 | tf_op jit(solution)/shard_map/ppermute | solution.py:425
  32.4 6.4 %collective-permute-start.11 = (bf16[720,128]{1,0:T(8,128)(2,1)S(1)}, bf16[720,128]{1,0:T(8,128)(2,1)S(1)}, u32[]{:S(2)}, u32[]{:S(2)}) collective-permute-start(bf16[720,128]{1,0:T(8,128)(2,1)S(1)} %get-tuple-element.41), channel_id=1, source_target_pairs={{8,16},{16,8},{0,0},{24,24},{9,17},{17,9},{1,1},{25,25},{10,18},{1... | collective-permute-start | bytes 552968 | tf_op jit(solution)/shard_map/ppermute | solution.py:425
  34.9 6.7 %collective-permute-start.12 = (bf16[720,128]{1,0:T(8,128)(2,1)S(1)}, bf16[720,128]{1,0:T(8,128)(2,1)S(1)}, u32[]{:S(2)}, u32[]{:S(2)}) collective-permute-start(bf16[720,128]{1,0:T(8,128)(2,1)S(1)} %constant_dynamic-slice_fusion), channel_id=1, source_target_pairs={{0,8},{8,0},{16,24},{24,16},{1,9},{9,1},{17,25},{25,17},{2,10},{10... | collective-permute-start | bytes 552968 | tf_op jit(solution)/shard_map/ppermute | solution.py:425
  42.2 5.9 %collective-permute-start.13 = (bf16[368,128]{1,0:T(8,128)(2,1)S(1)}, bf16[368,128]{1,0:T(8,128)(2,1)S(1)}, u32[]{:S(2)}, u32[]{:S(2)}) collective-permute-start(bf16[368,128]{1,0:T(8,128)(2,1)S(1)} %get-tuple-element.44), channel_id=1, source_target_pairs={{0,8},{8,24},{16,0},{24,16},{1,9},{9,25},{17,1},{25,17},{2,10},{10... | collective-permute-start | bytes 282632 | tf_op jit(solution)/shard_map/ppermute | solution.py:425
  44.2 6.5 %collective-permute-start.14 = (bf16[368,128]{1,0:T(8,128)(2,1)S(1)}, bf16[368,128]{1,0:T(8,128)(2,1)S(1)}, u32[]{:S(2)}, u32[]{:S(2)}) collective-permute-start(bf16[368,128]{1,0:T(8,128)(2,1)S(1)} %get-tuple-element.43), channel_id=1, source_target_pairs={{8,16},{16,24},{9,17},{17,25},{10,18},{18,26},{11,19},{19,27},{12,... | collective-permute-start | bytes 282632 | tf_op jit(solution)/shard_map/ppermute | solution.py:425
  51.8 4.6 %collective-permute-start.15 = (bf16[176,256]{1,0:T(8,128)(2,1)S(1)}, bf16[176,256]{1,0:T(8,128)(2,1)S(1)}, u32[]{:S(2)}, u32[]{:S(2)}) collective-permute-start(bf16[176,256]{1,0:T(8,128)(2,1)S(1)} %get-tuple-element.40), channel_id=1, source_target_pairs={{0,4},{4,0},{1,5},{5,1},{2,6},{6,2},{3,7},{7,3},{8,12},{12,8},{9,1... | collective-permute-start | bytes 270344 | tf_op jit(solution)/shard_map/ppermute | solution.py:327

commit v14 on v13

--- a/solution.py
+++ b/solution.py
@@ -443,7 +443,7 @@
         chunk_one = summed(0)
         two_away = along_tok(keys_or_query(chunk_one, tok == 3), [(0, 2), (3, 1), (1, 0), (2, 3)])
         swapped = along_tok(keys_or_query(chunk_one, tok == 2), [(1, 2), (2, 1), (0, 0), (3, 3)])
-        across = by_col(chunk_one[:EXTRA], 2)
+        across = lax.ppermute(chunk_one[:EXTRA], ("tok", "row", "col"), [(2, 3)])
         arrived[1] = jnp.where(
             tok < toks,
             arrived[1].astype(jnp.float32),

time: 57.6 us -> 56.6 us (0.983)
  waiting for transfers between devices: 18.8 us -> 17.9 us
    ppermute x5 -> x4, starting transfers between devices: 2.2 us -> 0.27 us  [by_col(): return lax.ppermute(value, 'col', [(c, c ^ flip) for c in range(4)])]
    ppermute x4, starting transfers between devices: 4.02 us -> 5.93 us  [by_row(): return lax.ppermute(value, 'row', [(0, 1), (1, 0)])]
    ppermute x5, starting transfers between devices: 5.8 us -> 4.68 us  [along_tok(): return lax.ppermute(value, 'tok', pairs)]
    ppermute x0 -> x1, starting transfers between devices: none -> 0.66 us  [per_device(): across = lax.ppermute(chunk_one[:EXTRA], ('tok', 'row', 'col'), [(2, 3)])]
    ppermute x5 -> x4, waiting for transfers between devices: 1.57 us -> 0.99 us  [by_col(): return lax.ppermute(value, 'col', [(c, c ^ flip) for c in range(4)])]
  transfers between devices with their start and end apart: 16 -> 16, of which waited for: 11 -> 9; matrix products, arithmetic and copies ran while one was open for 16% -> 17% of each run, Pallas kernels for 12% -> 12%
where the time goes in v14:
time: 56.6 us; the launch traced here: 55.7 us
  waiting for transfers between devices  17.9 us (32%)
  starting transfers between devices  16.5 us (29%)
  Pallas kernels  11 us (19%)
  other arithmetic  5.65 us (10%)
  local copies, waits for them, and re-layouts  4.41 us (8%)
    ppermute x4, waiting for transfers between devices, by_row(): return lax.ppermute(value, 'row', [(0, 1), (1, 0)])  9.82 us
    ppermute x5, waiting for transfers between devices, along_tok(): return lax.ppermute(value, 'tok', pairs)  7.08 us
    ppermute x4, starting transfers between devices, by_row(): return lax.ppermute(value, 'row', [(0, 1), (1, 0)])  5.93 us
    ppermute x5, starting transfers between devices, along_tok(): return lax.ppermute(value, 'tok', pairs)  4.68 us
    unnamed x3, local copies, waits for them, and re-layouts  3.97 us
    pallas_call x1, Pallas kernels, per_device(): pl.pallas_call(project_kernel, out_shape=(partial_sums, partial_sums), in...  3.66 us
    ppermute x1, starting transfers between devices, per_device(): lax.ppermute(activations, ('row', 'col'), [(r * 4 + c, c // 2 * 4 + 2 * (...  3.31 us
    pallas_call x1, Pallas kernels, per_device(): pl.pallas_call(normalise_project_kernel, out_shape=(partial_sums, partial...  2.69 us
  transfers between devices with their start and end apart: 16, of which 9 were waited for; matrix products, arithmetic and copies ran while one was open for 17% of the time, Pallas kernels for 12%

profile of v14, /device:TPU:24, one launch (start us, length us, event | category | flops | bytes accessed | tf_op | source)
XLA Modules:
  0.0 55.7 jit_solution(17943201422945369028)
XLA Ops:
  0.0 1.6 %collective-permute-start = (bf16[176,1024]{1,0:T(8,128)(2,1)}, bf16[176,1024]{1,0:T(8,128)(2,1)S(1)}, u32[]{:S(2)}, u32[]{:S(2)}) collective-permute-start(bf16[176,1024]{1,0:T(8,128)(2,1)} %param.4), channel_id=1, source_target_pairs={{0,0},{1,1},{2,4},{3,5},{4,2},{5,3},{6,6},{7,7},{8,8},{9,9},{10,12... | collective-permute-start | bytes 1081352 | tf_op jit(solution)/shard_map/ppermute | solution.py:333
  1.6 3.3 %collective-permute-start.1 = (bf16[176,1024]{1,0:T(8,128)(2,1)}, bf16[176,1024]{1,0:T(8,128)(2,1)S(1)}, u32[]{:S(2)}, u32[]{:S(2)}) collective-permute-start(bf16[176,1024]{1,0:T(8,128)(2,1)} %param.4), channel_id=1, source_target_pairs={{0,2},{1,3},{2,6},{3,7},{4,0},{5,1},{6,4},{7,5},{8,10},{9,11},{10,... | collective-permute-start | bytes 1081352 | tf_op jit(solution)/shard_map/ppermute | solution.py:338
  4.9 1.2 %multiply_reduce_fusion = f32[176]{0:T(256)S(1)} fusion(bf16[176,1024]{1,0:T(8,128)(2,1)} %param.4), kind=kLoop, calls=%fused_computation | loop fusion | flops 540496 | bytes 361152 | tf_op jit(solution)/shard_map/reduce_sum | solution.py:344
  6.1 0.7 %convert_element_type.61 = f32[1024]{0:T(1024)S(1)} convert(bf16[1024]{0:T(1024)(128)(2,1)} %param.5) | non-fusion elementwise | flops 1024 | bytes 6144 | tf_op jit(solution)/shard_map/convert_element_type | solution.py:345
  6.8 0.1 pad_maximum_fusion.3
  6.9 0.7 %convert_add_fusion = f32[176]{0:T(256)S(1)} fusion(s32[176]{0:T(256)} %param.7), kind=kLoop, calls=%fused_computation.28 | loop fusion | flops 352 | bytes 1408 | tf_op jit(solution)/shard_map/add | solution.py:357
  7.6 0.5 collective-permute-done.2
  8.0 0.8 %slice_select_fusion = (f32[1024]{0:T(1024)S(1)}, f32[1024]{0:T(1024)S(1)}) fusion(f32[1200]{0:T(1024)S(1)} %collective-permute-done.2, bf16[1024]{0:T(1024)(128)(2,1)} %param.5, pred[]{:T(512)S(6)} %eq.22), kind=kLoop, calls=%fused_computation.18 | loop fusion | flops 3072 | bytes 14337 | tf_op jit(solution)/shard_map/jit(_where)/select_n | solution.py:331
  8.8 0.1 concatenate.40
  8.9 0.1 pad_add_fusion.1.place_ref
  9.0 4.0 %copy.6 = bf16[256,8,4,384]{3,1,2,0:T(8,128)(2,1)S(1)} copy(bf16[256,8,4,384]{3,2,1,0:T(4,128)(2,1)} %bitcast.25) | data formatting | bytes 12582912
  12.9 0.5 collective-permute-done.3
  13.5 0.1 slice.39
  13.6 0.1 pad_maximum_fusion.4
  13.7 1.8 %collective-permute-start.6 = (f32[352]{0:T(512)S(1)}, f32[352]{0:T(512)S(1)}, u32[]{:S(2)}, u32[]{:S(2)}) collective-permute-start(f32[352]{0:T(512)S(1)} %pad_maximum_fusion.4), channel_id=1, source_target_pairs={{0,4},{4,0},{1,5},{5,1},{2,6},{6,2},{3,7},{7,3},{8,12},{12,8},{9,1... | collective-permute-start | bytes 4232 | tf_op jit(solution)/shard_map/ppermute | solution.py:327
  15.5 0.2 collective-permute-start.5
  15.7 0.7 %fusion = (f32[352,64]{1,0:T(8,128)S(1)}, f32[352,64]{1,0:T(8,128)S(1)}, f32[352,64]{1,0:T(8,128)S(1)}) fusion(f32[64]{0:T(128)S(1)} %fusion.2, f32[352]{0:T(512)S(1)} %add_convert_fusion.2), kind=kLoop, calls=%fused_computation.12 | loop fusion | flops 45056 | bytes 272000 | tf_op jit(solution)/shard_map/neg | solution.py:26
  16.4 0.2 pad_maximum_fusion
  16.6 0.7 %collective-permute-done.6 = f32[352]{0:T(512)S(1)} collective-permute-done((f32[352]{0:T(512)S(1)}, f32[352]{0:T(512)S(1)}, u32[]{:S(2)}, u32[]{:S(2)}) %collective-permute-start.6) | collective-permute-done | bytes 1440 | tf_op jit(solution)/shard_map/ppermute | solution.py:327
  17.3 0.1 broadcast_select_fusion.4
  17.4 0.1 pad_maximum_fusion.5
  17.4 0.1 reshape.71.squares_ref
  17.6 2.7 %shard_map.46 = (f32[1088,128]{1,0:T(8,128)S(1)}, f32[1088,128]{1,0:T(8,128)S(1)}, bf16[2,352,1024]{2,1,0:T(8,128)(2,1)S(1)}, bf16[2048,768]{1,0:T(8,128)(2,1)}) custom-call(s32[4]{0:T(128)S(1)} %pad_add_fusion.1.place_ref, bf16[176,1024]{1,0:T(8,128)(2,1)S(1)} %collective-permute-done.a_near, bf16[176,1024]{1,0:T(8,128)(2,1)S(1)} %collective-permute-done.1.a_far, ...), custom_call_target="tpu_custom_call" | custom-call | tf_op jit(solution)/shard_map/pallas_call | solution.py:370
  20.3 1.9 %collective-permute-start.7 = (f16[1088,128]{1,0:T(8,128)(2,1)S(1)}, f16[1088,128]{1,0:T(8,128)(2,1)S(1)}, u32[]{:S(2)}, u32[]{:S(2)}) collective-permute-start(f16[1088,128]{1,0:T(8,128)(2,1)S(1)} %convert_element_type.66), channel_id=1, source_target_pairs={{0,4},{4,0},{1,5},{5,1},{2,6},{6,2},{3,7},{7,3},{8,12},{12,8},{9,1... | collective-permute-start | bytes 835592 | tf_op jit(solution)/shard_map/ppermute | solution.py:327
  22.2 0.1 fusion.1.docs_ref
  22.3 0.3 collective-permute-start.8
  22.6 3.7 %shard_map.47 = (f32[1088,128]{1,0:T(8,128)S(1)}, f32[1088,128]{1,0:T(8,128)S(1)}) custom-call(bf16[2,352,1024]{2,1,0:T(8,128)(2,1)S(1)} %get-tuple-element.29.normed_ref, f32[16,128]{1,0:T(8,128)S(1)} %fusion.1.docs_ref, f32[352,128]{1,0:T(8,128)S(1)} %get-tuple-element.58.cos_ref, f32[352,128]{1,0:T(8,128)S(1)} %get-tuple-element.59.sin_ref, ...), custom_call_target="tpu_custom_call" | custom-call | tf_op jit(solution)/shard_map/pallas_call | solution.py:388
  26.3 3.7 %collective-permute-done.7 = f16[1088,128]{1,0:T(8,128)(2,1)S(1)} collective-permute-done((f16[1088,128]{1,0:T(8,128)(2,1)S(1)}, f16[1088,128]{1,0:T(8,128)(2,1)S(1)}, u32[]{:S(2)}, u32[]{:S(2)}) %collective-permute-start.7) | collective-permute-done | bytes 278560 | tf_op jit(solution)/shard_map/ppermute | solution.py:327
  30.0 0.7 %collective-permute-start.9 = (bf16[16,128]{1,0:T(8,128)(2,1)S(1)}, bf16[16,128]{1,0:T(8,128)(2,1)S(1)}, u32[]{:S(2)}, u32[]{:S(2)}) collective-permute-start(bf16[16,128]{1,0:T(8,128)(2,1)S(1)} %slice.49), channel_id=1, source_target_pairs={{2,3}} | collective-permute-start | bytes 12296 | tf_op jit(solution)/shard_map/ppermute | solution.py:446
  30.7 0.1 constant_dynamic-slice_fusion.1
  30.8 0.4 collective-permute-start.10
  31.2 0.7 %collective-permute-start.11 = (bf16[720,128]{1,0:T(8,128)(2,1)S(1)}, bf16[720,128]{1,0:T(8,128)(2,1)S(1)}, u32[]{:S(2)}, u32[]{:S(2)}) collective-permute-start(bf16[720,128]{1,0:T(8,128)(2,1)S(1)} %get-tuple-element.41), channel_id=1, source_target_pairs={{8,16},{16,8},{0,0},{24,24},{9,17},{17,9},{1,1},{25,25},{10,18},{1... | collective-permute-start | bytes 552968 | tf_op jit(solution)/shard_map/ppermute | solution.py:425
  31.9 2.8 %collective-permute-done.8 = f16[1088,128]{1,0:T(8,128)(2,1)S(1)} collective-permute-done((f16[1088,128]{1,0:T(8,128)(2,1)S(1)}, f16[1088,128]{1,0:T(8,128)(2,1)S(1)}, u32[]{:S(2)}, u32[]{:S(2)}) %collective-permute-start.8) | collective-permute-done | bytes 278560 | tf_op jit(solution)/shard_map/ppermute | solution.py:327
  34.7 0.1 add_convert_fusion.refs_2_.refs_5_.refs_4_
  34.9 0.5 collective-permute-start.12
  35.4 0.1 pad_add_fusion.refs_0_.place_ref
  35.5 1.8 %shard_map.48 = (f32[2,352,128]{2,1,0:T(8,128)S(1)}, f32[2,352,1]{2,1,0:T(8,128)S(1)}) custom-call(s32[2]{0:T(128)S(1)} %pad_add_fusion.refs_0_.place_ref, bf16[1088,128]{1,0:T(8,128)(2,1)S(1)} %add_convert_fusion.1.refs_1_.refs_4_.refs_3_, bf16[1088,128]{1,0:T(8,128)(2,1)S(1)} %add_convert_fusion.refs_2_.refs_5_.refs_4_), custom_call_target="tpu_custom_call" | custom-call | tf_op jit(solution)/shard_map/pallas_call | solution.py:460
  37.3 3.1 %collective-permute-done.12.refs_3_.refs_7_ = bf16[720,128]{1,0:T(8,128)(2,1)S(1)} collective-permute-done((bf16[720,128]{1,0:T(8,128)(2,1)S(1)}, bf16[720,128]{1,0:T(8,128)(2,1)S(1)}, u32[]{:S(2)}, u32[]{:S(2)}) %collective-permute-start.12) | collective-permute-done | bytes 184352 | tf_op jit(solution)/shard_map/ppermute | solution.py:425
  40.5 0.6 %shard_map.49.refs_8_ = bf16[2,368,128]{2,1,0:T(8,128)(2,1)S(1)} custom-call(s32[2]{0:T(128)S(1)} %pad_add_fusion.refs_0_.place_ref, bf16[720,128]{1,0:T(8,128)(2,1)S(1)} %collective-permute-done.10.refs_1_.refs_5_, bf16[720,128]{1,0:T(8,128)(2,1)S(1)} %collective-permute-done.11.refs_2_.refs_6_, ...), custom_call_target="tpu_custom_call" | custom-call | tf_op jit(solution)/shard_map/pallas_call | solution.py:463
  41.1 1.8 %collective-permute-start.13 = (bf16[368,128]{1,0:T(8,128)(2,1)S(1)}, bf16[368,128]{1,0:T(8,128)(2,1)S(1)}, u32[]{:S(2)}, u32[]{:S(2)}) collective-permute-start(bf16[368,128]{1,0:T(8,128)(2,1)S(1)} %get-tuple-element.44), channel_id=1, source_target_pairs={{0,8},{8,24},{16,0},{24,16},{1,9},{9,25},{17,1},{25,17},{2,10},{10... | collective-permute-start | bytes 282632 | tf_op jit(solution)/shard_map/ppermute | solution.py:425
  42.9 1.3 %collective-permute-start.14 = (bf16[368,128]{1,0:T(8,128)(2,1)S(1)}, bf16[368,128]{1,0:T(8,128)(2,1)S(1)}, u32[]{:S(2)}, u32[]{:S(2)}) collective-permute-start(bf16[368,128]{1,0:T(8,128)(2,1)S(1)} %get-tuple-element.43), channel_id=1, source_target_pairs={{8,16},{16,24},{9,17},{17,25},{10,18},{18,26},{11,19},{19,27},{12,... | collective-permute-start | bytes 282632 | tf_op jit(solution)/shard_map/ppermute | solution.py:425
  44.2 1.2 %shard_map.50 = (f32[2,352,128]{2,1,0:T(8,128)S(1)}, f32[2,352,1]{2,1,0:T(8,128)S(1)}) custom-call(s32[2]{0:T(128)S(1)} %pad_add_fusion.refs_0_.place_ref, f32[2,352,128]{2,1,0:T(8,128)S(1)} %get-tuple-element.35.refs_1_, f32[2,352,1]{2,1,0:T(8,128)S(1)} %get-tuple-element.36.refs_6_.refs_2_, ...), custom_call_target="tpu_custom_call" | custom-call | tf_op jit(solution)/shard_map/pallas_call | solution.py:471
  45.4 1.6 %collective-permute-done.13.first_ref = bf16[368,128]{1,0:T(8,128)(2,1)S(1)} collective-permute-done((bf16[368,128]{1,0:T(8,128)(2,1)S(1)}, bf16[368,128]{1,0:T(8,128)(2,1)S(1)}, u32[]{:S(2)}, u32[]{:S(2)}) %collective-permute-start.13) | collective-permute-done | bytes 94240 | tf_op jit(solution)/shard_map/ppermute | solution.py:425
  47.0 2.3 %collective-permute-done.14.below_ref = bf16[368,128]{1,0:T(8,128)(2,1)S(1)} collective-permute-done((bf16[368,128]{1,0:T(8,128)(2,1)S(1)}, bf16[368,128]{1,0:T(8,128)(2,1)S(1)}, u32[]{:S(2)}, u32[]{:S(2)}) %collective-permute-start.14) | collective-permute-done | bytes 94240 | tf_op jit(solution)/shard_map/ppermute | solution.py:425
  49.4 1.1 %shard_map.51 = (bf16[176,256]{1,0:T(8,128)(2,1)S(1)}, bf16[176,256]{1,0:T(8,128)(2,1)S(1)}) custom-call(s32[2]{0:T(128)S(1)} %pad_add_fusion.refs_0_.place_ref, f32[2,352,128]{2,1,0:T(8,128)S(1)} %get-tuple-element.37.out_ref, f32[2,352,1]{2,1,0:T(8,128)S(1)} %get-tuple-element.38.logs_ref, bf16[368,128]{1,0:T(8,128)(2,1)S(1)} %collective-permute-done.13.first_ref, ...), custom_call_target="tpu_custom_call" | custom-call | tf_op jit(solution)/shard_map/pallas_call | solution.py:475
  50.4 2.0 %collective-permute-start.15 = (bf16[176,256]{1,0:T(8,128)(2,1)S(1)}, bf16[176,256]{1,0:T(8,128)(2,1)S(1)}, u32[]{:S(2)}, u32[]{:S(2)}) collective-permute-start(bf16[176,256]{1,0:T(8,128)(2,1)S(1)} %get-tuple-element.40), channel_id=1, source_target_pairs={{0,4},{4,0},{1,5},{5,1},{2,6},{6,2},{3,7},{7,3},{8,12},{12,8},{9,1... | collective-permute-start | bytes 270344 | tf_op jit(solution)/shard_map/ppermute | solution.py:327
  52.4 2.6 %collective-permute-done.15 = bf16[176,256]{1,0:T(8,128)(2,1)S(1)} collective-permute-done((bf16[176,256]{1,0:T(8,128)(2,1)S(1)}, bf16[176,256]{1,0:T(8,128)(2,1)S(1)}, u32[]{:S(2)}, u32[]{:S(2)}) %collective-permute-start.15) | collective-permute-done | bytes 90144 | tf_op jit(solution)/shard_map/ppermute | solution.py:327
  55.0 0.7 %pad_maximum_fusion.2 = bf16[176,512]{1,0:T(8,128)(2,1)} fusion(bf16[176,256]{1,0:T(8,128)(2,1)S(1)} %get-tuple-element.46, bf16[176,256]{1,0:T(8,128)(2,1)S(1)} %get-tuple-element.45), kind=kLoop, calls=%fused_computation.7 | loop fusion | flops 360448 | bytes 360448 | tf_op jit(solution)/shard_map/concatenate | solution.py:481
  (25 shorter events, 0.4 us)
Async XLA Ops:
  0.0 13.5 %collective-permute-start = (bf16[176,1024]{1,0:T(8,128)(2,1)}, bf16[176,1024]{1,0:T(8,128)(2,1)S(1)}, u32[]{:S(2)}, u32[]{:S(2)}) collective-permute-start(bf16[176,1024]{1,0:T(8,128)(2,1)} %param.4), channel_id=1, source_target_pairs={{0,0},{1,1},{2,4},{3,5},{4,2},{5,3},{6,6},{7,7},{8,8},{9,9},{10,12... | collective-permute-start | bytes 1081352 | tf_op jit(solution)/shard_map/ppermute | solution.py:333
  1.6 11.8 %collective-permute-start.1 = (bf16[176,1024]{1,0:T(8,128)(2,1)}, bf16[176,1024]{1,0:T(8,128)(2,1)S(1)}, u32[]{:S(2)}, u32[]{:S(2)}) collective-permute-start(bf16[176,1024]{1,0:T(8,128)(2,1)} %param.4), channel_id=1, source_target_pairs={{0,2},{1,3},{2,6},{3,7},{4,0},{5,1},{6,4},{7,5},{8,10},{9,11},{10,... | collective-permute-start | bytes 1081352 | tf_op jit(solution)/shard_map/ppermute | solution.py:338
  6.9 1.2 %collective-permute-start.2 = (f32[1200]{0:T(1024)S(1)}, f32[1200]{0:T(1024)S(1)}, u32[]{:S(2)}, u32[]{:S(2)}) collective-permute-start(f32[1200]{0:T(1024)S(1)} %pad_maximum_fusion.3), channel_id=1, source_target_pairs={{0,1},{1,0},{2,3},{3,2},{4,5},{5,4},{6,7},{7,6},{8,9},{9,8},{10,11... | collective-permute-start | bytes 14408 | tf_op jit(solution)/shard_map/ppermute | solution.py:324
  8.9 4.6 %collective-permute-start.3 = (f32[2224]{0:T(1024)S(1)}, f32[2224]{0:T(1024)S(1)}, u32[]{:S(2)}, u32[]{:S(2)}) collective-permute-start(f32[2224]{0:T(1024)S(1)} %concatenate.40), channel_id=1, source_target_pairs={{0,2},{1,3},{2,0},{3,1},{4,6},{5,7},{6,4},{7,5},{8,10},{9,11},{10,... | collective-permute-start | bytes 26696 | tf_op jit(solution)/shard_map/ppermute | solution.py:324
  9.0 8.3 %copy-start = (s32[176]{0:T(256)S(1)}, s32[176]{0:T(256)}, u32[]{:S(2)}) copy-start(s32[176]{0:T(256)} %param.7) | copy-start | bytes 2116
  13.6 4.0 %collective-permute-start.4 = (bf16[176,1024]{1,0:T(8,128)(2,1)S(1)}, bf16[176,1024]{1,0:T(8,128)(2,1)S(1)}, u32[]{:S(2)}, u32[]{:S(2)}) collective-permute-start(bf16[176,1024]{1,0:T(8,128)(2,1)S(1)} %collective-permute-done.a_near), channel_id=1, source_target_pairs={{0,1},{1,0},{2,3},{3,2},{4,5},{5,4},{6,7},{7,6},{8,9},{9,8},{10,11... | collective-permute-start | bytes 1081352 | tf_op jit(solution)/shard_map/ppermute | solution.py:324
  13.7 3.6 %collective-permute-start.6 = (f32[352]{0:T(512)S(1)}, f32[352]{0:T(512)S(1)}, u32[]{:S(2)}, u32[]{:S(2)}) collective-permute-start(f32[352]{0:T(512)S(1)} %pad_maximum_fusion.4), channel_id=1, source_target_pairs={{0,4},{4,0},{1,5},{5,1},{2,6},{6,2},{3,7},{7,3},{8,12},{12,8},{9,1... | collective-permute-start | bytes 4232 | tf_op jit(solution)/shard_map/ppermute | solution.py:327
  15.5 2.1 %collective-permute-start.5 = (bf16[176,1024]{1,0:T(8,128)(2,1)S(1)}, bf16[176,1024]{1,0:T(8,128)(2,1)S(1)}, u32[]{:S(2)}, u32[]{:S(2)}) collective-permute-start(bf16[176,1024]{1,0:T(8,128)(2,1)S(1)} %collective-permute-done.1.a_far), channel_id=1, source_target_pairs={{0,1},{1,0},{2,3},{3,2},{4,5},{5,4},{6,7},{7,6},{8,9},{9,8},{10,11... | collective-permute-start | bytes 1081352 | tf_op jit(solution)/shard_map/ppermute | solution.py:324
  20.3 9.6 %collective-permute-start.7 = (f16[1088,128]{1,0:T(8,128)(2,1)S(1)}, f16[1088,128]{1,0:T(8,128)(2,1)S(1)}, u32[]{:S(2)}, u32[]{:S(2)}) collective-permute-start(f16[1088,128]{1,0:T(8,128)(2,1)S(1)} %convert_element_type.66), channel_id=1, source_target_pairs={{0,4},{4,0},{1,5},{5,1},{2,6},{6,2},{3,7},{7,3},{8,12},{12,8},{9,1... | collective-permute-start | bytes 835592 | tf_op jit(solution)/shard_map/ppermute | solution.py:327
  22.3 12.4 %collective-permute-start.8 = (f16[1088,128]{1,0:T(8,128)(2,1)S(1)}, f16[1088,128]{1,0:T(8,128)(2,1)S(1)}, u32[]{:S(2)}, u32[]{:S(2)}) collective-permute-start(f16[1088,128]{1,0:T(8,128)(2,1)S(1)} %convert_element_type.69), channel_id=1, source_target_pairs={{0,4},{4,0},{1,5},{5,1},{2,6},{6,2},{3,7},{7,3},{8,12},{12,8},{9,1... | collective-permute-start | bytes 835592 | tf_op jit(solution)/shard_map/ppermute | solution.py:327
  30.0 1.8 %collective-permute-start.9 = (bf16[16,128]{1,0:T(8,128)(2,1)S(1)}, bf16[16,128]{1,0:T(8,128)(2,1)S(1)}, u32[]{:S(2)}, u32[]{:S(2)}) collective-permute-start(bf16[16,128]{1,0:T(8,128)(2,1)S(1)} %slice.49), channel_id=1, source_target_pairs={{2,3}} | collective-permute-start | bytes 12296 | tf_op jit(solution)/shard_map/ppermute | solution.py:446
  30.8 6.5 %collective-permute-start.10 = (bf16[720,128]{1,0:T(8,128)(2,1)S(1)}, bf16[720,128]{1,0:T(8,128)(2,1)S(1)}, u32[]{:S(2)}, u32[]{:S(2)}) collective-permute-start(bf16[720,128]{1,0:T(8,128)(2,1)S(1)} %get-tuple-element.42), channel_id=1, source_target_pairs={{0,16},{24,8},{8,0},{16,24},{1,17},{25,9},{9,1},{17,25},{2,18},{26... | collective-permute-start | bytes 552968 | tf_op jit(solution)/shard_map/ppermute | solution.py:425
  31.2 6.1 %collective-permute-start.11 = (bf16[720,128]{1,0:T(8,128)(2,1)S(1)}, bf16[720,128]{1,0:T(8,128)(2,1)S(1)}, u32[]{:S(2)}, u32[]{:S(2)}) collective-permute-start(bf16[720,128]{1,0:T(8,128)(2,1)S(1)} %get-tuple-element.41), channel_id=1, source_target_pairs={{8,16},{16,8},{0,0},{24,24},{9,17},{17,9},{1,1},{25,25},{10,18},{1... | collective-permute-start | bytes 552968 | tf_op jit(solution)/shard_map/ppermute | solution.py:425
  34.9 5.6 %collective-permute-start.12 = (bf16[720,128]{1,0:T(8,128)(2,1)S(1)}, bf16[720,128]{1,0:T(8,128)(2,1)S(1)}, u32[]{:S(2)}, u32[]{:S(2)}) collective-permute-start(bf16[720,128]{1,0:T(8,128)(2,1)S(1)} %constant_dynamic-slice_fusion), channel_id=1, source_target_pairs={{0,8},{8,0},{16,24},{24,16},{1,9},{9,1},{17,25},{25,17},{2,10},{10... | collective-permute-start | bytes 552968 | tf_op jit(solution)/shard_map/ppermute | solution.py:425
  41.1 6.0 %collective-permute-start.13 = (bf16[368,128]{1,0:T(8,128)(2,1)S(1)}, bf16[368,128]{1,0:T(8,128)(2,1)S(1)}, u32[]{:S(2)}, u32[]{:S(2)}) collective-permute-start(bf16[368,128]{1,0:T(8,128)(2,1)S(1)} %get-tuple-element.44), channel_id=1, source_target_pairs={{0,8},{8,24},{16,0},{24,16},{1,9},{9,25},{17,1},{25,17},{2,10},{10... | collective-permute-start | bytes 282632 | tf_op jit(solution)/shard_map/ppermute | solution.py:425
  42.9 6.5 %collective-permute-start.14 = (bf16[368,128]{1,0:T(8,128)(2,1)S(1)}, bf16[368,128]{1,0:T(8,128)(2,1)S(1)}, u32[]{:S(2)}, u32[]{:S(2)}) collective-permute-start(bf16[368,128]{1,0:T(8,128)(2,1)S(1)} %get-tuple-element.43), channel_id=1, source_target_pairs={{8,16},{16,24},{9,17},{17,25},{10,18},{18,26},{11,19},{19,27},{12,... | collective-permute-start | bytes 282632 | tf_op jit(solution)/shard_map/ppermute | solution.py:425
  50.4 4.6 %collective-permute-start.15 = (bf16[176,256]{1,0:T(8,128)(2,1)S(1)}, bf16[176,256]{1,0:T(8,128)(2,1)S(1)}, u32[]{:S(2)}, u32[]{:S(2)}) collective-permute-start(bf16[176,256]{1,0:T(8,128)(2,1)S(1)} %get-tuple-element.40), channel_id=1, source_target_pairs={{0,4},{4,0},{1,5},{5,1},{2,6},{6,2},{3,7},{7,3},{8,12},{12,8},{9,1... | collective-permute-start | bytes 270344 | tf_op jit(solution)/shard_map/ppermute | solution.py:327

commit v15 on v14

--- a/solution.py
+++ b/solution.py
@@ -27,25 +27,39 @@
     )
 
 
-def project_chunk(normed_ref, weight_ref, key_column, query_column, cos_ref, sin_ref, doc_rows, out_ref):
+def project_chunk(
+    normed, place, weight_ref, key_column, query_column, cos_ref, sin_ref, doc_rows, out_ref
+):
+    core, near_row = place
     block, size = cos_ref.shape
-    extra = doc_rows.shape[0]
+    rows, extra = block // 2, doc_rows.shape[0]
     depth = weight_ref.shape[0] // 2
 
     def product(column, width):
         at = pl.ds(column if isinstance(column, int) else pl.multiple_of(column, size), width)
-        return jnp.dot(
-            normed_ref[0], weight_ref[:depth, at], preferred_element_type=jnp.float32
-        ) + jnp.dot(normed_ref[1], weight_ref[depth:, at], preferred_element_type=jnp.float32)
-
-    def rotated(piece):
-        return piece * cos_ref[...] + pltpu.roll(piece, size // 2, 1) * sin_ref[...]
+        return sum(
+            jnp.dot(
+                normed[index],
+                weight_ref[pl.ds(pl.multiple_of(half * depth, depth), depth), at],
+                preferred_element_type=jnp.float32,
+            )
+            for index, half in enumerate((core, 1 - core))
+        )
+
+    def store(begin, piece, rotating):
+        for index, row in enumerate((near_row, 1 - near_row)):
+            part = piece[index * rows : (index + 1) * rows]
+            if rotating:
+                at = pl.ds(pl.multiple_of(row * rows, 8), rows)
+                part = part * cos_ref[at, :] + pltpu.roll(part, size // 2, 1) * sin_ref[at, :]
+            out_ref[pl.ds(pl.multiple_of(row * rows + begin, 8), rows), :] = part
 
     both = product(key_column, 2 * size)
-    out_ref[:block, :] = rotated(both[:, :size])
-    out_ref[block : 2 * block, :] = both[:, size:]
+    query = product(query_column, size)
+    store(0, both[:, :size], True)
+    store(block, both[:, size:], False)
+    store(2 * block + extra, query, True)
     out_ref[2 * block : 2 * block + extra, :] = doc_rows
-    out_ref[2 * block + extra : 3 * block + extra, :] = rotated(product(query_column, size))
     out_ref[3 * block + extra :, :] = doc_rows
 
 
@@ -60,25 +74,36 @@
         weight_ref.at[:, pl.ds(pl.multiple_of(own, size), 6 * size)], own_hbm, semaphore
     )
     copy.start()
+    factors = [
+        lax.rsqrt(squares_ref[pl.ds(pl.multiple_of(row * rows, 8), rows), :] / features + EPS)
+        for row in (near_row, 1 - near_row)
+    ]
+    normed = []
     for shards, half in (((a_near, a_far), core), ((b_near, b_far), 1 - core)):
         gain = gain_ref[half]
-        for shard, row in zip(shards, (near_row, 1 - near_row)):
-            at = pl.ds(pl.multiple_of(row * rows, 16), rows)
-            factor = lax.rsqrt(squares_ref[at, :] / features + EPS)
-            normed_ref[half, at, :] = (shard[...].astype(jnp.float32) * factor * gain).astype(
-                jnp.bfloat16
+        normed.append(
+            jnp.concatenate(
+                [
+                    (shard[...].astype(jnp.float32) * factor * gain).astype(jnp.bfloat16)
+                    for shard, factor in zip(shards, factors)
+                ],
+                axis=0,
             )
+        )
+    for index in range(2):
+        normed_ref[index] = normed[index]
     nothing = jnp.zeros((EXTRA, size), jnp.float32)
     for chunk, (keys, query) in enumerate(CHUNKS):
         project_chunk(
-            normed_ref, weight_ref, away + keys * size, away + query * size, cos_ref, sin_ref, nothing,
-            (one_ref, two_ref)[chunk],
+            normed, (core, near_row), weight_ref, away + keys * size, away + query * size, cos_ref,
+            sin_ref, nothing, (one_ref, two_ref)[chunk],
         )
     copy.wait()
 
 
 def project_kernel(
-    normed_ref, docs_ref, cos_ref, sin_ref, own_hbm, one_ref, two_ref, weight_buffer, semaphore
+    place_ref, normed_ref, docs_ref, cos_ref, sin_ref, own_hbm, one_ref, two_ref, weight_buffer,
+    semaphore,
 ):
     copy = pltpu.make_async_copy(own_hbm, weight_buffer, semaphore)
     copy.start()
@@ -86,8 +111,8 @@
     size = cos_ref.shape[1]
     for chunk, (keys, query) in enumerate(CHUNKS):
         project_chunk(
-            normed_ref, weight_buffer, keys * size, query * size, cos_ref, sin_ref, docs_ref[...],
-            (one_ref, two_ref)[chunk],
+            normed_ref, (place_ref[0], place_ref[1]), weight_buffer, keys * size, query * size, cos_ref,
+            sin_ref, docs_ref[...], (one_ref, two_ref)[chunk],
         )
 
 
@@ -388,7 +413,9 @@
     own = pl.pallas_call(
         project_kernel,
         out_shape=(partial_sums, partial_sums),
-        in_specs=in_vmem(4) + [pl.BlockSpec(memory_space=pltpu.HBM)],
+        in_specs=[pl.BlockSpec(memory_space=pltpu.SMEM)]
+        + in_vmem(4)
+        + [pl.BlockSpec(memory_space=pltpu.HBM)],
         out_specs=tuple(in_vmem(2)),
         scratch_shapes=[
             pltpu.VMEM((span, pair * triple), jnp.bfloat16),
@@ -397,7 +424,8 @@
         compiler_params=pltpu.CompilerParams(vmem_limit_bytes=8 * MIB),
         cost_estimate=no_cost,
     )(
-        normed, doc_rows, cosine, sine, pltpu.with_memory_space_constraint(own_weight, pltpu.HBM)
+        jnp.stack([core, chip]), normed, doc_rows, cosine, sine,
+        pltpu.with_memory_space_constraint(own_weight, pltpu.HBM),
     )
     scale = 1.0 / math.sqrt(size)
 

time: 56.6 us -> 58.3 us (1.030)
  Pallas kernels: 11 us -> 12.9 us
  waiting for transfers between devices: 17.9 us -> 17.1 us
  starting transfers between devices: 16.5 us -> 17.2 us
    pallas_call x1, Pallas kernels: 2.69 us -> 3.98 us  [per_device(): pl.pallas_call(normalise_project_kernel, out_shape=(partial_sums, partial...]
    ppermute x4, waiting for transfers between devices: 9.82 us -> 8.77 us  [by_row(): return lax.ppermute(value, 'row', [(0, 1), (1, 0)])]
    ppermute x5, starting transfers between devices: 4.68 us -> 5.4 us  [along_tok(): return lax.ppermute(value, 'tok', pairs)]
    pallas_call x1, Pallas kernels: 3.66 us -> 4.24 us  [per_device(): pl.pallas_call(project_kernel, out_shape=(partial_sums, partial_sums), in...]
  transfers between devices with their start and end apart: 16 -> 16, of which waited for: 9 -> 10; matrix products, arithmetic and copies ran while one was open for 17% -> 16% of each run, Pallas kernels for 12% -> 13%
where the time goes in v15:
time: 58.3 us; the launch traced here: 57.6 us
  starting transfers between devices  17.2 us (30%)
  waiting for transfers between devices  17.1 us (29%)
  Pallas kernels  12.9 us (22%)
  other arithmetic  5.73 us (10%)
  local copies, waits for them, and re-layouts  4.41 us (8%)
    ppermute x4, waiting for transfers between devices, by_row(): return lax.ppermute(value, 'row', [(0, 1), (1, 0)])  8.77 us
    ppermute x5, waiting for transfers between devices, along_tok(): return lax.ppermute(value, 'tok', pairs)  7.3 us
    ppermute x4, starting transfers between devices, by_row(): return lax.ppermute(value, 'row', [(0, 1), (1, 0)])  5.69 us
    ppermute x5, starting transfers between devices, along_tok(): return lax.ppermute(value, 'tok', pairs)  5.4 us
    pallas_call x1, Pallas kernels, per_device(): pl.pallas_call(project_kernel, out_shape=(partial_sums, partial_sums), in...  4.24 us
    pallas_call x1, Pallas kernels, per_device(): pl.pallas_call(normalise_project_kernel, out_shape=(partial_sums, partial...  3.98 us
    unnamed x3, local copies, waits for them, and re-layouts  3.97 us
    ppermute x1, starting transfers between devices, per_device(): lax.ppermute(activations, ('row', 'col'), [(r * 4 + c, c // 2 * 4 + 2 * (...  3.31 us
  transfers between devices with their start and end apart: 16, of which 10 were waited for; matrix products, arithmetic and copies ran while one was open for 16% of the time, Pallas kernels for 13%

profile of v15, /device:TPU:24, one launch (start us, length us, event | category | flops | bytes accessed | tf_op | source)
XLA Modules:
  0.0 57.6 jit_solution(10878758862005072380)
XLA Ops:
  0.0 1.6 %collective-permute-start = (bf16[176,1024]{1,0:T(8,128)(2,1)}, bf16[176,1024]{1,0:T(8,128)(2,1)S(1)}, u32[]{:S(2)}, u32[]{:S(2)}) collective-permute-start(bf16[176,1024]{1,0:T(8,128)(2,1)} %param.4), channel_id=1, source_target_pairs={{0,0},{1,1},{2,4},{3,5},{4,2},{5,3},{6,6},{7,7},{8,8},{9,9},{10,12... | collective-permute-start | bytes 1081352 | tf_op jit(solution)/shard_map/ppermute | solution.py:358
  1.6 3.3 %collective-permute-start.1 = (bf16[176,1024]{1,0:T(8,128)(2,1)}, bf16[176,1024]{1,0:T(8,128)(2,1)S(1)}, u32[]{:S(2)}, u32[]{:S(2)}) collective-permute-start(bf16[176,1024]{1,0:T(8,128)(2,1)} %param.4), channel_id=1, source_target_pairs={{0,2},{1,3},{2,6},{3,7},{4,0},{5,1},{6,4},{7,5},{8,10},{9,11},{10,... | collective-permute-start | bytes 1081352 | tf_op jit(solution)/shard_map/ppermute | solution.py:363
  4.9 1.2 %multiply_reduce_fusion = f32[176]{0:T(256)S(1)} fusion(bf16[176,1024]{1,0:T(8,128)(2,1)} %param.4), kind=kLoop, calls=%fused_computation | loop fusion | flops 540496 | bytes 361152 | tf_op jit(solution)/shard_map/reduce_sum | solution.py:369
  6.1 0.7 %convert_element_type.61 = f32[1024]{0:T(1024)S(1)} convert(bf16[1024]{0:T(1024)(128)(2,1)} %param.5) | non-fusion elementwise | flops 1024 | bytes 6144 | tf_op jit(solution)/shard_map/convert_element_type | solution.py:370
  6.8 0.1 pad_maximum_fusion.3
  6.9 0.7 %convert_add_fusion = f32[176]{0:T(256)S(1)} fusion(s32[176]{0:T(256)} %param.7), kind=kLoop, calls=%fused_computation.28 | loop fusion | flops 352 | bytes 1408 | tf_op jit(solution)/shard_map/add | solution.py:382
  7.6 0.5 collective-permute-done.2
  8.0 0.8 %slice_select_fusion = (f32[1024]{0:T(1024)S(1)}, f32[1024]{0:T(1024)S(1)}) fusion(f32[1200]{0:T(1024)S(1)} %collective-permute-done.2, bf16[1024]{0:T(1024)(128)(2,1)} %param.5, pred[]{:T(512)S(6)} %eq.22), kind=kLoop, calls=%fused_computation.18 | loop fusion | flops 3072 | bytes 14337 | tf_op jit(solution)/shard_map/jit(_where)/select_n | solution.py:356
  8.8 0.1 concatenate.40
  8.9 0.1 pad_add_fusion.2.place_ref
  9.0 4.0 %copy.6 = bf16[256,8,4,384]{3,1,2,0:T(8,128)(2,1)S(1)} copy(bf16[256,8,4,384]{3,2,1,0:T(4,128)(2,1)} %bitcast.25) | data formatting | bytes 12582912
  12.9 0.5 collective-permute-done.3
  13.6 0.5 collective-permute-start.5
  14.1 0.1 pad_maximum_fusion.4
  14.2 1.8 %collective-permute-start.6 = (f32[352]{0:T(512)S(1)}, f32[352]{0:T(512)S(1)}, u32[]{:S(2)}, u32[]{:S(2)}) collective-permute-start(f32[352]{0:T(512)S(1)} %pad_maximum_fusion.4), channel_id=1, source_target_pairs={{0,4},{4,0},{1,5},{5,1},{2,6},{6,2},{3,7},{7,3},{8,12},{12,8},{9,1... | collective-permute-start | bytes 4232 | tf_op jit(solution)/shard_map/ppermute | solution.py:352
  15.9 0.7 %fusion = (f32[352,64]{1,0:T(8,128)S(1)}, f32[352,64]{1,0:T(8,128)S(1)}, f32[352,64]{1,0:T(8,128)S(1)}) fusion(f32[64]{0:T(128)S(1)} %fusion.2, f32[352]{0:T(512)S(1)} %add_convert_fusion.2), kind=kLoop, calls=%fused_computation.12 | loop fusion | flops 45056 | bytes 272000 | tf_op jit(solution)/shard_map/neg | solution.py:26
  16.7 0.2 pad_maximum_fusion
  16.8 0.9 %collective-permute-done.6 = f32[352]{0:T(512)S(1)} collective-permute-done((f32[352]{0:T(512)S(1)}, f32[352]{0:T(512)S(1)}, u32[]{:S(2)}, u32[]{:S(2)}) %collective-permute-start.6) | collective-permute-done | bytes 1440 | tf_op jit(solution)/shard_map/ppermute | solution.py:352
  17.8 0.1 pad_maximum_fusion.5
  17.9 0.1 reshape.71.squares_ref
  18.0 4.0 %shard_map.46 = (f32[1088,128]{1,0:T(8,128)S(1)}, f32[1088,128]{1,0:T(8,128)S(1)}, bf16[2,352,1024]{2,1,0:T(8,128)(2,1)S(1)}, bf16[2048,768]{1,0:T(8,128)(2,1)}) custom-call(s32[4]{0:T(128)S(1)} %pad_add_fusion.2.place_ref, bf16[176,1024]{1,0:T(8,128)(2,1)S(1)} %collective-permute-done.a_near, bf16[176,1024]{1,0:T(8,128)(2,1)S(1)} %collective-permute-done.1.a_far, ...), custom_call_target="tpu_custom_call" | custom-call | tf_op jit(solution)/shard_map/pallas_call | solution.py:395
  22.1 1.8 %collective-permute-start.7 = (f16[1088,128]{1,0:T(8,128)(2,1)S(1)}, f16[1088,128]{1,0:T(8,128)(2,1)S(1)}, u32[]{:S(2)}, u32[]{:S(2)}) collective-permute-start(f16[1088,128]{1,0:T(8,128)(2,1)S(1)} %convert_element_type.66), channel_id=1, source_target_pairs={{0,4},{4,0},{1,5},{5,1},{2,6},{6,2},{3,7},{7,3},{8,12},{12,8},{9,1... | collective-permute-start | bytes 835592 | tf_op jit(solution)/shard_map/ppermute | solution.py:352
  23.9 0.1 pad_add_fusion.1.place_ref
  24.0 0.1 fusion.1.docs_ref
  24.1 0.3 collective-permute-start.8
  24.4 4.2 %shard_map.47 = (f32[1088,128]{1,0:T(8,128)S(1)}, f32[1088,128]{1,0:T(8,128)S(1)}) custom-call(s32[2]{0:T(128)S(1)} %pad_add_fusion.1.place_ref, bf16[2,352,1024]{2,1,0:T(8,128)(2,1)S(1)} %get-tuple-element.29.normed_ref, f32[16,128]{1,0:T(8,128)S(1)} %fusion.1.docs_ref, f32[352,128]{1,0:T(8,128)S(1)} %get-tuple-element.58.cos_ref, ...), custom_call_target="tpu_custom_call" | custom-call | tf_op jit(solution)/shard_map/pallas_call | solution.py:413
  28.7 3.1 %collective-permute-done.7 = f16[1088,128]{1,0:T(8,128)(2,1)S(1)} collective-permute-done((f16[1088,128]{1,0:T(8,128)(2,1)S(1)}, f16[1088,128]{1,0:T(8,128)(2,1)S(1)}, u32[]{:S(2)}, u32[]{:S(2)}) %collective-permute-start.7) | collective-permute-done | bytes 278560 | tf_op jit(solution)/shard_map/ppermute | solution.py:352
  31.8 0.7 %collective-permute-start.9 = (bf16[16,128]{1,0:T(8,128)(2,1)S(1)}, bf16[16,128]{1,0:T(8,128)(2,1)S(1)}, u32[]{:S(2)}, u32[]{:S(2)}) collective-permute-start(bf16[16,128]{1,0:T(8,128)(2,1)S(1)} %slice.49), channel_id=1, source_target_pairs={{2,3}} | collective-permute-start | bytes 12296 | tf_op jit(solution)/shard_map/ppermute | solution.py:474
  32.5 0.1 constant_dynamic-slice_fusion.1
  32.6 0.4 collective-permute-start.10
  33.0 0.7 %collective-permute-start.11 = (bf16[720,128]{1,0:T(8,128)(2,1)S(1)}, bf16[720,128]{1,0:T(8,128)(2,1)S(1)}, u32[]{:S(2)}, u32[]{:S(2)}) collective-permute-start(bf16[720,128]{1,0:T(8,128)(2,1)S(1)} %get-tuple-element.41), channel_id=1, source_target_pairs={{8,16},{16,8},{0,0},{24,24},{9,17},{17,9},{1,1},{25,25},{10,18},{1... | collective-permute-start | bytes 552968 | tf_op jit(solution)/shard_map/ppermute | solution.py:453
  33.7 2.0 %collective-permute-done.8 = f16[1088,128]{1,0:T(8,128)(2,1)S(1)} collective-permute-done((f16[1088,128]{1,0:T(8,128)(2,1)S(1)}, f16[1088,128]{1,0:T(8,128)(2,1)S(1)}, u32[]{:S(2)}, u32[]{:S(2)}) %collective-permute-start.8) | collective-permute-done | bytes 278560 | tf_op jit(solution)/shard_map/ppermute | solution.py:352
  35.6 0.1 add_convert_fusion.refs_2_.refs_5_.refs_4_
  35.8 1.1 %collective-permute-start.12 = (bf16[720,128]{1,0:T(8,128)(2,1)S(1)}, bf16[720,128]{1,0:T(8,128)(2,1)S(1)}, u32[]{:S(2)}, u32[]{:S(2)}) collective-permute-start(bf16[720,128]{1,0:T(8,128)(2,1)S(1)} %constant_dynamic-slice_fusion), channel_id=1, source_target_pairs={{0,8},{8,0},{16,24},{24,16},{1,9},{9,1},{17,25},{25,17},{2,10},{10... | collective-permute-start | bytes 552968 | tf_op jit(solution)/shard_map/ppermute | solution.py:453
  36.8 0.1 pad_add_fusion.refs_0_.place_ref
  36.9 1.8 %shard_map.48 = (f32[2,352,128]{2,1,0:T(8,128)S(1)}, f32[2,352,1]{2,1,0:T(8,128)S(1)}) custom-call(s32[2]{0:T(128)S(1)} %pad_add_fusion.refs_0_.place_ref, bf16[1088,128]{1,0:T(8,128)(2,1)S(1)} %add_convert_fusion.1.refs_1_.refs_4_.refs_3_, bf16[1088,128]{1,0:T(8,128)(2,1)S(1)} %add_convert_fusion.refs_2_.refs_5_.refs_4_), custom_call_target="tpu_custom_call" | custom-call | tf_op jit(solution)/shard_map/pallas_call | solution.py:488
  38.8 1.1 %collective-permute-done.10.refs_1_.refs_5_ = bf16[720,128]{1,0:T(8,128)(2,1)S(1)} collective-permute-done((bf16[720,128]{1,0:T(8,128)(2,1)S(1)}, bf16[720,128]{1,0:T(8,128)(2,1)S(1)}, u32[]{:S(2)}, u32[]{:S(2)}) %collective-permute-start.10) | collective-permute-done | bytes 184352 | tf_op jit(solution)/shard_map/ppermute | solution.py:453
  39.9 2.3 %collective-permute-done.12.refs_3_.refs_7_ = bf16[720,128]{1,0:T(8,128)(2,1)S(1)} collective-permute-done((bf16[720,128]{1,0:T(8,128)(2,1)S(1)}, bf16[720,128]{1,0:T(8,128)(2,1)S(1)}, u32[]{:S(2)}, u32[]{:S(2)}) %collective-permute-start.12) | collective-permute-done | bytes 184352 | tf_op jit(solution)/shard_map/ppermute | solution.py:453
  42.1 0.6 shard_map.49.refs_8_
  42.7 2.0 %collective-permute-start.13 = (bf16[368,128]{1,0:T(8,128)(2,1)S(1)}, bf16[368,128]{1,0:T(8,128)(2,1)S(1)}, u32[]{:S(2)}, u32[]{:S(2)}) collective-permute-start(bf16[368,128]{1,0:T(8,128)(2,1)S(1)} %get-tuple-element.44), channel_id=1, source_target_pairs={{0,8},{8,24},{16,0},{24,16},{1,9},{9,25},{17,1},{25,17},{2,10},{10... | collective-permute-start | bytes 282632 | tf_op jit(solution)/shard_map/ppermute | solution.py:453
  44.8 1.3 %collective-permute-start.14 = (bf16[368,128]{1,0:T(8,128)(2,1)S(1)}, bf16[368,128]{1,0:T(8,128)(2,1)S(1)}, u32[]{:S(2)}, u32[]{:S(2)}) collective-permute-start(bf16[368,128]{1,0:T(8,128)(2,1)S(1)} %get-tuple-element.43), channel_id=1, source_target_pairs={{8,16},{16,24},{9,17},{17,25},{10,18},{18,26},{11,19},{19,27},{12,... | collective-permute-start | bytes 282632 | tf_op jit(solution)/shard_map/ppermute | solution.py:453
  46.0 1.2 %shard_map.50 = (f32[2,352,128]{2,1,0:T(8,128)S(1)}, f32[2,352,1]{2,1,0:T(8,128)S(1)}) custom-call(s32[2]{0:T(128)S(1)} %pad_add_fusion.refs_0_.place_ref, f32[2,352,128]{2,1,0:T(8,128)S(1)} %get-tuple-element.35.refs_1_, f32[2,352,1]{2,1,0:T(8,128)S(1)} %get-tuple-element.36.refs_6_.refs_2_, ...), custom_call_target="tpu_custom_call" | custom-call | tf_op jit(solution)/shard_map/pallas_call | solution.py:499
  47.3 1.4 %collective-permute-done.13.first_ref = bf16[368,128]{1,0:T(8,128)(2,1)S(1)} collective-permute-done((bf16[368,128]{1,0:T(8,128)(2,1)S(1)}, bf16[368,128]{1,0:T(8,128)(2,1)S(1)}, u32[]{:S(2)}, u32[]{:S(2)}) %collective-permute-start.13) | collective-permute-done | bytes 94240 | tf_op jit(solution)/shard_map/ppermute | solution.py:453
  48.7 2.5 %collective-permute-done.14.below_ref = bf16[368,128]{1,0:T(8,128)(2,1)S(1)} collective-permute-done((bf16[368,128]{1,0:T(8,128)(2,1)S(1)}, bf16[368,128]{1,0:T(8,128)(2,1)S(1)}, u32[]{:S(2)}, u32[]{:S(2)}) %collective-permute-start.14) | collective-permute-done | bytes 94240 | tf_op jit(solution)/shard_map/ppermute | solution.py:453
  51.2 1.1 %shard_map.51 = (bf16[176,256]{1,0:T(8,128)(2,1)S(1)}, bf16[176,256]{1,0:T(8,128)(2,1)S(1)}) custom-call(s32[2]{0:T(128)S(1)} %pad_add_fusion.refs_0_.place_ref, f32[2,352,128]{2,1,0:T(8,128)S(1)} %get-tuple-element.37.out_ref, f32[2,352,1]{2,1,0:T(8,128)S(1)} %get-tuple-element.38.logs_ref, bf16[368,128]{1,0:T(8,128)(2,1)S(1)} %collective-permute-done.13.first_ref, ...), custom_call_target="tpu_custom_call" | custom-call | tf_op jit(solution)/shard_map/pallas_call | solution.py:503
  52.3 1.7 %collective-permute-start.15 = (bf16[176,256]{1,0:T(8,128)(2,1)S(1)}, bf16[176,256]{1,0:T(8,128)(2,1)S(1)}, u32[]{:S(2)}, u32[]{:S(2)}) collective-permute-start(bf16[176,256]{1,0:T(8,128)(2,1)S(1)} %get-tuple-element.40), channel_id=1, source_target_pairs={{0,4},{4,0},{1,5},{5,1},{2,6},{6,2},{3,7},{7,3},{8,12},{12,8},{9,1... | collective-permute-start | bytes 270344 | tf_op jit(solution)/shard_map/ppermute | solution.py:352
  54.0 2.9 %collective-permute-done.15 = bf16[176,256]{1,0:T(8,128)(2,1)S(1)} collective-permute-done((bf16[176,256]{1,0:T(8,128)(2,1)S(1)}, bf16[176,256]{1,0:T(8,128)(2,1)S(1)}, u32[]{:S(2)}, u32[]{:S(2)}) %collective-permute-start.15) | collective-permute-done | bytes 90144 | tf_op jit(solution)/shard_map/ppermute | solution.py:352
  56.9 0.7 %pad_maximum_fusion.2 = bf16[176,512]{1,0:T(8,128)(2,1)} fusion(bf16[176,256]{1,0:T(8,128)(2,1)S(1)} %get-tuple-element.46, bf16[176,256]{1,0:T(8,128)(2,1)S(1)} %get-tuple-element.45), kind=kLoop, calls=%fused_computation.7 | loop fusion | flops 360448 | bytes 360448 | tf_op jit(solution)/shard_map/concatenate | solution.py:509
  (26 shorter events, 0.5 us)
Async XLA Ops:
  0.0 13.5 %collective-permute-start = (bf16[176,1024]{1,0:T(8,128)(2,1)}, bf16[176,1024]{1,0:T(8,128)(2,1)S(1)}, u32[]{:S(2)}, u32[]{:S(2)}) collective-permute-start(bf16[176,1024]{1,0:T(8,128)(2,1)} %param.4), channel_id=1, source_target_pairs={{0,0},{1,1},{2,4},{3,5},{4,2},{5,3},{6,6},{7,7},{8,8},{9,9},{10,12... | collective-permute-start | bytes 1081352 | tf_op jit(solution)/shard_map/ppermute | solution.py:358
  1.6 11.8 %collective-permute-start.1 = (bf16[176,1024]{1,0:T(8,128)(2,1)}, bf16[176,1024]{1,0:T(8,128)(2,1)S(1)}, u32[]{:S(2)}, u32[]{:S(2)}) collective-permute-start(bf16[176,1024]{1,0:T(8,128)(2,1)} %param.4), channel_id=1, source_target_pairs={{0,2},{1,3},{2,6},{3,7},{4,0},{5,1},{6,4},{7,5},{8,10},{9,11},{10,... | collective-permute-start | bytes 1081352 | tf_op jit(solution)/shard_map/ppermute | solution.py:363
  6.9 1.2 %collective-permute-start.2 = (f32[1200]{0:T(1024)S(1)}, f32[1200]{0:T(1024)S(1)}, u32[]{:S(2)}, u32[]{:S(2)}) collective-permute-start(f32[1200]{0:T(1024)S(1)} %pad_maximum_fusion.3), channel_id=1, source_target_pairs={{0,1},{1,0},{2,3},{3,2},{4,5},{5,4},{6,7},{7,6},{8,9},{9,8},{10,11... | collective-permute-start | bytes 14408 | tf_op jit(solution)/shard_map/ppermute | solution.py:349
  8.9 4.6 %collective-permute-start.3 = (f32[2224]{0:T(1024)S(1)}, f32[2224]{0:T(1024)S(1)}, u32[]{:S(2)}, u32[]{:S(2)}) collective-permute-start(f32[2224]{0:T(1024)S(1)} %concatenate.40), channel_id=1, source_target_pairs={{0,2},{1,3},{2,0},{3,1},{4,6},{5,7},{6,4},{7,5},{8,10},{9,11},{10,... | collective-permute-start | bytes 26696 | tf_op jit(solution)/shard_map/ppermute | solution.py:349
  9.0 8.8 %copy-start = (s32[176]{0:T(256)S(1)}, s32[176]{0:T(256)}, u32[]{:S(2)}) copy-start(s32[176]{0:T(256)} %param.7) | copy-start | bytes 2116
  13.6 4.5 %collective-permute-start.4 = (bf16[176,1024]{1,0:T(8,128)(2,1)S(1)}, bf16[176,1024]{1,0:T(8,128)(2,1)S(1)}, u32[]{:S(2)}, u32[]{:S(2)}) collective-permute-start(bf16[176,1024]{1,0:T(8,128)(2,1)S(1)} %collective-permute-done.a_near), channel_id=1, source_target_pairs={{0,1},{1,0},{2,3},{3,2},{4,5},{5,4},{6,7},{7,6},{8,9},{9,8},{10,11... | collective-permute-start | bytes 1081352 | tf_op jit(solution)/shard_map/ppermute | solution.py:349
  13.6 4.4 %collective-permute-start.5 = (bf16[176,1024]{1,0:T(8,128)(2,1)S(1)}, bf16[176,1024]{1,0:T(8,128)(2,1)S(1)}, u32[]{:S(2)}, u32[]{:S(2)}) collective-permute-start(bf16[176,1024]{1,0:T(8,128)(2,1)S(1)} %collective-permute-done.1.a_far), channel_id=1, source_target_pairs={{0,1},{1,0},{2,3},{3,2},{4,5},{5,4},{6,7},{7,6},{8,9},{9,8},{10,11... | collective-permute-start | bytes 1081352 | tf_op jit(solution)/shard_map/ppermute | solution.py:349
  14.2 3.6 %collective-permute-start.6 = (f32[352]{0:T(512)S(1)}, f32[352]{0:T(512)S(1)}, u32[]{:S(2)}, u32[]{:S(2)}) collective-permute-start(f32[352]{0:T(512)S(1)} %pad_maximum_fusion.4), channel_id=1, source_target_pairs={{0,4},{4,0},{1,5},{5,1},{2,6},{6,2},{3,7},{7,3},{8,12},{12,8},{9,1... | collective-permute-start | bytes 4232 | tf_op jit(solution)/shard_map/ppermute | solution.py:352
  22.1 9.7 %collective-permute-start.7 = (f16[1088,128]{1,0:T(8,128)(2,1)S(1)}, f16[1088,128]{1,0:T(8,128)(2,1)S(1)}, u32[]{:S(2)}, u32[]{:S(2)}) collective-permute-start(f16[1088,128]{1,0:T(8,128)(2,1)S(1)} %convert_element_type.66), channel_id=1, source_target_pairs={{0,4},{4,0},{1,5},{5,1},{2,6},{6,2},{3,7},{7,3},{8,12},{12,8},{9,1... | collective-permute-start | bytes 835592 | tf_op jit(solution)/shard_map/ppermute | solution.py:352
  24.1 11.5 %collective-permute-start.8 = (f16[1088,128]{1,0:T(8,128)(2,1)S(1)}, f16[1088,128]{1,0:T(8,128)(2,1)S(1)}, u32[]{:S(2)}, u32[]{:S(2)}) collective-permute-start(f16[1088,128]{1,0:T(8,128)(2,1)S(1)} %convert_element_type.69), channel_id=1, source_target_pairs={{0,4},{4,0},{1,5},{5,1},{2,6},{6,2},{3,7},{7,3},{8,12},{12,8},{9,1... | collective-permute-start | bytes 835592 | tf_op jit(solution)/shard_map/ppermute | solution.py:352
  31.8 1.8 %collective-permute-start.9 = (bf16[16,128]{1,0:T(8,128)(2,1)S(1)}, bf16[16,128]{1,0:T(8,128)(2,1)S(1)}, u32[]{:S(2)}, u32[]{:S(2)}) collective-permute-start(bf16[16,128]{1,0:T(8,128)(2,1)S(1)} %slice.49), channel_id=1, source_target_pairs={{2,3}} | collective-permute-start | bytes 12296 | tf_op jit(solution)/shard_map/ppermute | solution.py:474
  32.6 7.3 %collective-permute-start.10 = (bf16[720,128]{1,0:T(8,128)(2,1)S(1)}, bf16[720,128]{1,0:T(8,128)(2,1)S(1)}, u32[]{:S(2)}, u32[]{:S(2)}) collective-permute-start(bf16[720,128]{1,0:T(8,128)(2,1)S(1)} %get-tuple-element.42), channel_id=1, source_target_pairs={{0,16},{24,8},{8,0},{16,24},{1,17},{25,9},{9,1},{17,25},{2,18},{26... | collective-permute-start | bytes 552968 | tf_op jit(solution)/shard_map/ppermute | solution.py:453
  33.0 6.9 %collective-permute-start.11 = (bf16[720,128]{1,0:T(8,128)(2,1)S(1)}, bf16[720,128]{1,0:T(8,128)(2,1)S(1)}, u32[]{:S(2)}, u32[]{:S(2)}) collective-permute-start(bf16[720,128]{1,0:T(8,128)(2,1)S(1)} %get-tuple-element.41), channel_id=1, source_target_pairs={{8,16},{16,8},{0,0},{24,24},{9,17},{17,9},{1,1},{25,25},{10,18},{1... | collective-permute-start | bytes 552968 | tf_op jit(solution)/shard_map/ppermute | solution.py:453
  35.8 6.3 %collective-permute-start.12 = (bf16[720,128]{1,0:T(8,128)(2,1)S(1)}, bf16[720,128]{1,0:T(8,128)(2,1)S(1)}, u32[]{:S(2)}, u32[]{:S(2)}) collective-permute-start(bf16[720,128]{1,0:T(8,128)(2,1)S(1)} %constant_dynamic-slice_fusion), channel_id=1, source_target_pairs={{0,8},{8,0},{16,24},{24,16},{1,9},{9,1},{17,25},{25,17},{2,10},{10... | collective-permute-start | bytes 552968 | tf_op jit(solution)/shard_map/ppermute | solution.py:453
  42.7 5.9 %collective-permute-start.13 = (bf16[368,128]{1,0:T(8,128)(2,1)S(1)}, bf16[368,128]{1,0:T(8,128)(2,1)S(1)}, u32[]{:S(2)}, u32[]{:S(2)}) collective-permute-start(bf16[368,128]{1,0:T(8,128)(2,1)S(1)} %get-tuple-element.44), channel_id=1, source_target_pairs={{0,8},{8,24},{16,0},{24,16},{1,9},{9,25},{17,1},{25,17},{2,10},{10... | collective-permute-start | bytes 282632 | tf_op jit(solution)/shard_map/ppermute | solution.py:453
  44.8 6.5 %collective-permute-start.14 = (bf16[368,128]{1,0:T(8,128)(2,1)S(1)}, bf16[368,128]{1,0:T(8,128)(2,1)S(1)}, u32[]{:S(2)}, u32[]{:S(2)}) collective-permute-start(bf16[368,128]{1,0:T(8,128)(2,1)S(1)} %get-tuple-element.43), channel_id=1, source_target_pairs={{8,16},{16,24},{9,17},{17,25},{10,18},{18,26},{11,19},{19,27},{12,... | collective-permute-start | bytes 282632 | tf_op jit(solution)/shard_map/ppermute | solution.py:453
  52.3 4.6 %collective-permute-start.15 = (bf16[176,256]{1,0:T(8,128)(2,1)S(1)}, bf16[176,256]{1,0:T(8,128)(2,1)S(1)}, u32[]{:S(2)}, u32[]{:S(2)}) collective-permute-start(bf16[176,256]{1,0:T(8,128)(2,1)S(1)} %get-tuple-element.40), channel_id=1, source_target_pairs={{0,4},{4,0},{1,5},{5,1},{2,6},{6,2},{3,7},{7,3},{8,12},{12,8},{9,1... | collective-permute-start | bytes 270344 | tf_op jit(solution)/shard_map/ppermute | solution.py:352

commit v16 on v14

--- a/solution.py
+++ b/solution.py
@@ -51,15 +51,11 @@
 
 def normalise_project_kernel(
     place_ref, a_near, a_far, b_near, b_far, squares_ref, gain_ref, cos_ref, sin_ref, weight_ref,
-    one_ref, two_ref, normed_ref, own_hbm, semaphore,
+    out_ref, normed_ref,
 ):
     rows, size = a_near.shape[0], cos_ref.shape[1]
     features = 2 * gain_ref.shape[0] * gain_ref.shape[2]
-    core, near_row, away, own = place_ref[0], place_ref[1], place_ref[2], place_ref[3]
-    copy = pltpu.make_async_copy(
-        weight_ref.at[:, pl.ds(pl.multiple_of(own, size), 6 * size)], own_hbm, semaphore
-    )
-    copy.start()
+    core, near_row, away = place_ref[0], place_ref[1], place_ref[2]
     for shards, half in (((a_near, a_far), core), ((b_near, b_far), 1 - core)):
         gain = gain_ref[half]
         for shard, row in zip(shards, (near_row, 1 - near_row)):
@@ -68,12 +64,27 @@
             normed_ref[half, at, :] = (shard[...].astype(jnp.float32) * factor * gain).astype(
                 jnp.bfloat16
             )
-    nothing = jnp.zeros((EXTRA, size), jnp.float32)
-    for chunk, (keys, query) in enumerate(CHUNKS):
-        project_chunk(
-            normed_ref, weight_ref, away + keys * size, away + query * size, cos_ref, sin_ref, nothing,
-            (one_ref, two_ref)[chunk],
-        )
+    keys, query = CHUNKS[0]
+    project_chunk(
+        normed_ref, weight_ref, away + keys * size, away + query * size, cos_ref, sin_ref,
+        jnp.zeros((EXTRA, size), jnp.float32), out_ref,
+    )
+
+
+def second_kernel(
+    place_ref, normed_ref, cos_ref, sin_ref, weight_ref, out_ref, own_hbm, semaphore
+):
+    size = cos_ref.shape[1]
+    away, own = place_ref[2], place_ref[3]
+    copy = pltpu.make_async_copy(
+        weight_ref.at[:, pl.ds(pl.multiple_of(own, size), 6 * size)], own_hbm, semaphore
+    )
+    copy.start()
+    keys, query = CHUNKS[1]
+    project_chunk(
+        normed_ref, weight_ref, away + keys * size, away + query * size, cos_ref, sin_ref,
+        jnp.zeros((EXTRA, size), jnp.float32), out_ref,
+    )
     copy.wait()
 
 
@@ -367,24 +378,27 @@
 
     partial_sums = jax.ShapeDtypeStruct((taller, size), jnp.float32)
     no_cost = pl.CostEstimate(flops=0, bytes_accessed=0, transcendentals=0)
-    *away, normed, own_weight = pl.pallas_call(
+    columns = jnp.stack([core, chip, (1 - row) * (pair * triple), row * (pair * triple)])
+    first, normed = pl.pallas_call(
         normalise_project_kernel,
-        out_shape=(
-            partial_sums,
-            partial_sums,
-            jax.ShapeDtypeStruct((2, block, width), jnp.bfloat16),
-            pltpu.HBM((span, pair * triple), jnp.bfloat16),
-        ),
+        out_shape=(partial_sums, jax.ShapeDtypeStruct((2, block, width), jnp.bfloat16)),
         in_specs=[pl.BlockSpec(memory_space=pltpu.SMEM)] + in_vmem(9),
-        out_specs=tuple(in_vmem(3)) + (pl.BlockSpec(memory_space=pltpu.HBM),),
+        out_specs=tuple(in_vmem(2)),
+        compiler_params=pltpu.CompilerParams(vmem_limit_bytes=12 * MIB),
+        cost_estimate=no_cost,
+    )(
+        columns, near, far, near_other, far_other, squares, gain, cosine, sine, flat_weight,
+    )
+    second, own_weight = pl.pallas_call(
+        second_kernel,
+        out_shape=(partial_sums, pltpu.HBM((span, pair * triple), jnp.bfloat16)),
+        in_specs=[pl.BlockSpec(memory_space=pltpu.SMEM)] + in_vmem(4),
+        out_specs=(in_vmem(1)[0], pl.BlockSpec(memory_space=pltpu.HBM)),
         scratch_shapes=[pltpu.SemaphoreType.DMA(())],
         compiler_params=pltpu.CompilerParams(vmem_limit_bytes=12 * MIB),
         cost_estimate=no_cost,
-    )(
-        jnp.stack([core, chip, (1 - row) * (pair * triple), row * (pair * triple)]),
-        near, far, near_other, far_other, squares, gain, cosine, sine, flat_weight,
-    )
-    arrived = [by_row(chunk.astype(jnp.float16)) for chunk in away]
+    )(columns, normed, cosine, sine, flat_weight)
+    arrived = [by_row(chunk.astype(jnp.float16)) for chunk in (first, second)]
     own = pl.pallas_call(
         project_kernel,
         out_shape=(partial_sums, partial_sums),

time: 56.6 us -> 60.5 us (1.069)
  local copies, waits for them, and re-layouts: 4.41 us -> 9.83 us
  waiting for transfers between devices: 17.9 us -> 14 us
  Pallas kernels: 11 us -> 12.5 us
  starting transfers between devices: 16.5 us -> 17.8 us
    unnamed x3 -> x7, local copies, waits for them, and re-layouts: 3.97 us -> 9.38 us
    ppermute x4, waiting for transfers between devices: 9.82 us -> 5.44 us  [by_row(): return lax.ppermute(value, 'row', [(0, 1), (1, 0)])]
    ppermute x5, starting transfers between devices: 4.68 us -> 6.33 us  [along_tok(): return lax.ppermute(value, 'tok', pairs)]
    pallas_call x1 -> x2, Pallas kernels: 2.69 us -> 4.16 us  [the longest x1 2.24 us: per_device(): pl.pallas_call(second_kernel, out_shape=(partial_sums, pltpu.HBM((span, p...]
  transfers between devices with their start and end apart: 16 -> 16, of which waited for: 9 -> 9; matrix products, arithmetic and copies ran while one was open for 17% -> 15% of each run, Pallas kernels for 12% -> 15%
where the time goes in v16:
time: 60.5 us; the launch traced here: 60 us
  starting transfers between devices  17.8 us (29%)
  waiting for transfers between devices  14 us (23%)
  Pallas kernels  12.5 us (21%)
  local copies, waits for them, and re-layouts  9.83 us (16%)
  other arithmetic  5.66 us (9%)
    unnamed x7, local copies, waits for them, and re-layouts  9.38 us
    ppermute x5, waiting for transfers between devices, along_tok(): return lax.ppermute(value, 'tok', pairs)  7.56 us
    ppermute x5, starting transfers between devices, along_tok(): return lax.ppermute(value, 'tok', pairs)  6.33 us
    ppermute x4, starting transfers between devices, by_row(): return lax.ppermute(value, 'row', [(0, 1), (1, 0)])  5.56 us
    ppermute x4, waiting for transfers between devices, by_row(): return lax.ppermute(value, 'row', [(0, 1), (1, 0)])  5.44 us
    pallas_call x1, Pallas kernels, per_device(): pl.pallas_call(project_kernel, out_shape=(partial_sums, partial_sums), in...  3.66 us
    ppermute x1, starting transfers between devices, per_device(): lax.ppermute(activations, ('row', 'col'), [(r * 4 + c, c // 2 * 4 + 2 * (...  3.31 us
    pallas_call x1, Pallas kernels, per_device(): pl.pallas_call(second_kernel, out_shape=(partial_sums, pltpu.HBM((span, p...  2.24 us
  transfers between devices with their start and end apart: 16, of which 9 were waited for; matrix products, arithmetic and copies ran while one was open for 15% of the time, Pallas kernels for 15%

profile of v16, /device:TPU:24, one launch (start us, length us, event | category | flops | bytes accessed | tf_op | source)
XLA Modules:
  0.0 60.0 jit_solution(10619702182270752320)
XLA Ops:
  0.0 1.6 %collective-permute-start = (bf16[176,1024]{1,0:T(8,128)(2,1)}, bf16[176,1024]{1,0:T(8,128)(2,1)S(1)}, u32[]{:S(2)}, u32[]{:S(2)}) collective-permute-start(bf16[176,1024]{1,0:T(8,128)(2,1)} %param.4), channel_id=1, source_target_pairs={{0,0},{1,1},{2,4},{3,5},{4,2},{5,3},{6,6},{7,7},{8,8},{9,9},{10,12... | collective-permute-start | bytes 1081352 | tf_op jit(solution)/shard_map/ppermute | solution.py:344
  1.6 3.3 %collective-permute-start.1 = (bf16[176,1024]{1,0:T(8,128)(2,1)}, bf16[176,1024]{1,0:T(8,128)(2,1)S(1)}, u32[]{:S(2)}, u32[]{:S(2)}) collective-permute-start(bf16[176,1024]{1,0:T(8,128)(2,1)} %param.4), channel_id=1, source_target_pairs={{0,2},{1,3},{2,6},{3,7},{4,0},{5,1},{6,4},{7,5},{8,10},{9,11},{10,... | collective-permute-start | bytes 1081352 | tf_op jit(solution)/shard_map/ppermute | solution.py:349
  4.9 1.2 %multiply_reduce_fusion = f32[176]{0:T(256)S(1)} fusion(bf16[176,1024]{1,0:T(8,128)(2,1)} %param.4), kind=kLoop, calls=%fused_computation | loop fusion | flops 540496 | bytes 361152 | tf_op jit(solution)/shard_map/reduce_sum | solution.py:355
  6.1 0.7 %convert_element_type.61 = f32[1024]{0:T(1024)S(1)} convert(bf16[1024]{0:T(1024)(128)(2,1)} %param.5) | non-fusion elementwise | flops 1024 | bytes 6144 | tf_op jit(solution)/shard_map/convert_element_type | solution.py:356
  6.8 0.1 pad_maximum_fusion.3
  6.9 0.7 %convert_add_fusion = f32[176]{0:T(256)S(1)} fusion(s32[176]{0:T(256)} %param.7), kind=kLoop, calls=%fused_computation.28 | loop fusion | flops 352 | bytes 1408 | tf_op jit(solution)/shard_map/add | solution.py:368
  7.6 0.5 collective-permute-done.2
  8.0 0.8 %slice_select_fusion = (f32[1024]{0:T(1024)S(1)}, f32[1024]{0:T(1024)S(1)}) fusion(f32[1200]{0:T(1024)S(1)} %collective-permute-done.2, bf16[1024]{0:T(1024)(128)(2,1)} %param.5, pred[]{:T(512)S(6)} %eq.22), kind=kLoop, calls=%fused_computation.18 | loop fusion | flops 3072 | bytes 14337 | tf_op jit(solution)/shard_map/jit(_where)/select_n | solution.py:342
  8.8 0.1 concatenate.40
  8.9 0.1 pad_add_fusion.1.place_ref
  9.0 4.0 %copy.6 = bf16[256,8,4,384]{3,1,2,0:T(8,128)(2,1)S(1)} copy(bf16[256,8,4,384]{3,2,1,0:T(4,128)(2,1)} %bitcast.26) | data formatting | bytes 12582912
  12.9 0.5 collective-permute-done.3
  13.6 0.1 pad_maximum_fusion.4
  13.7 1.8 %collective-permute-start.6 = (f32[352]{0:T(512)S(1)}, f32[352]{0:T(512)S(1)}, u32[]{:S(2)}, u32[]{:S(2)}) collective-permute-start(f32[352]{0:T(512)S(1)} %pad_maximum_fusion.4), channel_id=1, source_target_pairs={{0,4},{4,0},{1,5},{5,1},{2,6},{6,2},{3,7},{7,3},{8,12},{12,8},{9,1... | collective-permute-start | bytes 4232 | tf_op jit(solution)/shard_map/ppermute | solution.py:338
  15.5 0.2 collective-permute-start.5
  15.7 0.7 %fusion = (f32[352,64]{1,0:T(8,128)S(1)}, f32[352,64]{1,0:T(8,128)S(1)}, f32[352,64]{1,0:T(8,128)S(1)}) fusion(f32[64]{0:T(128)S(1)} %fusion.2, f32[352]{0:T(512)S(1)} %add_convert_fusion.2), kind=kLoop, calls=%fused_computation.12 | loop fusion | flops 45056 | bytes 272000 | tf_op jit(solution)/shard_map/neg | solution.py:26
  16.4 0.2 pad_maximum_fusion
  16.6 0.7 %collective-permute-done.6 = f32[352]{0:T(512)S(1)} collective-permute-done((f32[352]{0:T(512)S(1)}, f32[352]{0:T(512)S(1)}, u32[]{:S(2)}, u32[]{:S(2)}) %collective-permute-start.6) | collective-permute-done | bytes 1440 | tf_op jit(solution)/shard_map/ppermute | solution.py:338
  17.4 0.1 pad_maximum_fusion.5
  17.4 0.1 reshape.71.squares_ref
  17.6 1.9 %shard_map.46 = (f32[1088,128]{1,0:T(8,128)S(1)}, bf16[2,352,1024]{2,1,0:T(8,128)(2,1)S(1)}) custom-call(s32[4]{0:T(128)S(1)} %pad_add_fusion.1.place_ref, bf16[176,1024]{1,0:T(8,128)(2,1)S(1)} %collective-permute-done.a_near, bf16[176,1024]{1,0:T(8,128)(2,1)S(1)} %collective-permute-done.1.a_far, bf16[176,1024]{1,0:T(8,128)(2,1)S(1)} %collective-permute-done.4.b_near, ...), custom_call_target="tpu_custom_call" | custom-call | tf_op jit(solution)/shard_map/pallas_call | solution.py:382
  19.5 2.6 %copy-done = bf16[256,8,4,384]{3,1,2,0:T(8,128)(2,1)} copy-done((bf16[256,8,4,384]{3,1,2,0:T(8,128)(2,1)}, bf16[256,8,4,384]{3,1,2,0:T(8,128)(2,1)S(1)}, u32[]{:S(2)}) %copy-start) | copy-done | bytes 6291480
  22.2 1.9 %collective-permute-start.7 = (f16[1088,128]{1,0:T(8,128)(2,1)S(1)}, f16[1088,128]{1,0:T(8,128)(2,1)S(1)}, u32[]{:S(2)}, u32[]{:S(2)}) collective-permute-start(f16[1088,128]{1,0:T(8,128)(2,1)S(1)} %convert_element_type.66), channel_id=1, source_target_pairs={{0,4},{4,0},{1,5},{5,1},{2,6},{6,2},{3,7},{7,3},{8,12},{12,8},{9,1... | collective-permute-start | bytes 835592 | tf_op jit(solution)/shard_map/ppermute | solution.py:338
  24.0 0.1 fusion.1.docs_ref
  24.1 2.8 %copy-done.1 = bf16[256,8,4,384]{3,1,2,0:T(8,128)(2,1)S(1)} copy-done((bf16[256,8,4,384]{3,1,2,0:T(8,128)(2,1)S(1)}, bf16[256,8,4,384]{3,1,2,0:T(8,128)(2,1)}, u32[]{:S(2)}) %copy-start.1) | copy-done | bytes 6291480
  26.9 2.2 %shard_map.47 = (f32[1088,128]{1,0:T(8,128)S(1)}, bf16[2048,768]{1,0:T(8,128)(2,1)}) custom-call(s32[4]{0:T(128)S(1)} %pad_add_fusion.1.place_ref, bf16[2,352,1024]{2,1,0:T(8,128)(2,1)S(1)} %get-tuple-element.29.normed_ref, f32[352,128]{1,0:T(8,128)S(1)} %get-tuple-element.58.cos_ref, f32[352,128]{1,0:T(8,128)S(1)} %get-tuple-element.59.sin_ref, ...), custom_call_target="tpu_custom_call" | custom-call | tf_op jit(solution)/shard_map/pallas_call | solution.py:392
  29.2 0.3 collective-permute-start.8
  29.5 3.7 %shard_map.48 = (f32[1088,128]{1,0:T(8,128)S(1)}, f32[1088,128]{1,0:T(8,128)S(1)}) custom-call(bf16[2,352,1024]{2,1,0:T(8,128)(2,1)S(1)} %get-tuple-element.29.normed_ref, f32[16,128]{1,0:T(8,128)S(1)} %fusion.1.docs_ref, f32[352,128]{1,0:T(8,128)S(1)} %get-tuple-element.58.cos_ref, f32[352,128]{1,0:T(8,128)S(1)} %get-tuple-element.59.sin_ref, ...), custom_call_target="tpu_custom_call" | custom-call | tf_op jit(solution)/shard_map/pallas_call | solution.py:402
  33.2 0.7 %collective-permute-start.9 = (bf16[16,128]{1,0:T(8,128)(2,1)S(1)}, bf16[16,128]{1,0:T(8,128)(2,1)S(1)}, u32[]{:S(2)}, u32[]{:S(2)}) collective-permute-start(bf16[16,128]{1,0:T(8,128)(2,1)S(1)} %slice.49), channel_id=1, source_target_pairs={{2,3}} | collective-permute-start | bytes 12296 | tf_op jit(solution)/shard_map/ppermute | solution.py:460
  33.9 0.1 constant_dynamic-slice_fusion.1
  34.0 0.4 collective-permute-start.10
  34.4 0.7 %collective-permute-start.11 = (bf16[720,128]{1,0:T(8,128)(2,1)S(1)}, bf16[720,128]{1,0:T(8,128)(2,1)S(1)}, u32[]{:S(2)}, u32[]{:S(2)}) collective-permute-start(bf16[720,128]{1,0:T(8,128)(2,1)S(1)} %get-tuple-element.41), channel_id=1, source_target_pairs={{8,16},{16,8},{0,0},{24,24},{9,17},{17,9},{1,1},{25,25},{10,18},{1... | collective-permute-start | bytes 552968 | tf_op jit(solution)/shard_map/ppermute | solution.py:439
  35.1 1.8 %collective-permute-done.8 = f16[1088,128]{1,0:T(8,128)(2,1)S(1)} collective-permute-done((f16[1088,128]{1,0:T(8,128)(2,1)S(1)}, f16[1088,128]{1,0:T(8,128)(2,1)S(1)}, u32[]{:S(2)}, u32[]{:S(2)}) %collective-permute-start.8) | collective-permute-done | bytes 278560 | tf_op jit(solution)/shard_map/ppermute | solution.py:338
  36.9 0.1 add_convert_fusion.refs_2_.refs_5_.refs_4_
  37.0 1.2 %collective-permute-start.12 = (bf16[720,128]{1,0:T(8,128)(2,1)S(1)}, bf16[720,128]{1,0:T(8,128)(2,1)S(1)}, u32[]{:S(2)}, u32[]{:S(2)}) collective-permute-start(bf16[720,128]{1,0:T(8,128)(2,1)S(1)} %constant_dynamic-slice_fusion), channel_id=1, source_target_pairs={{0,8},{8,0},{16,24},{24,16},{1,9},{9,1},{17,25},{25,17},{2,10},{10... | collective-permute-start | bytes 552968 | tf_op jit(solution)/shard_map/ppermute | solution.py:439
  38.4 1.8 %shard_map.49 = (f32[2,352,128]{2,1,0:T(8,128)S(1)}, f32[2,352,1]{2,1,0:T(8,128)S(1)}) custom-call(s32[2]{0:T(128)S(1)} %pad_add_fusion.refs_0_.place_ref, bf16[1088,128]{1,0:T(8,128)(2,1)S(1)} %add_convert_fusion.1.refs_1_.refs_4_.refs_3_, bf16[1088,128]{1,0:T(8,128)(2,1)S(1)} %add_convert_fusion.refs_2_.refs_5_.refs_4_), custom_call_target="tpu_custom_call" | custom-call | tf_op jit(solution)/shard_map/pallas_call | solution.py:474
  40.2 1.4 %collective-permute-done.10.refs_1_.refs_5_ = bf16[720,128]{1,0:T(8,128)(2,1)S(1)} collective-permute-done((bf16[720,128]{1,0:T(8,128)(2,1)S(1)}, bf16[720,128]{1,0:T(8,128)(2,1)S(1)}, u32[]{:S(2)}, u32[]{:S(2)}) %collective-permute-start.10) | collective-permute-done | bytes 184352 | tf_op jit(solution)/shard_map/ppermute | solution.py:439
  41.7 2.2 %collective-permute-done.12.refs_3_.refs_7_ = bf16[720,128]{1,0:T(8,128)(2,1)S(1)} collective-permute-done((bf16[720,128]{1,0:T(8,128)(2,1)S(1)}, bf16[720,128]{1,0:T(8,128)(2,1)S(1)}, u32[]{:S(2)}, u32[]{:S(2)}) %collective-permute-start.12) | collective-permute-done | bytes 184352 | tf_op jit(solution)/shard_map/ppermute | solution.py:439
  43.8 0.6 shard_map.50.refs_8_
  44.4 2.7 %collective-permute-start.13 = (bf16[368,128]{1,0:T(8,128)(2,1)S(1)}, bf16[368,128]{1,0:T(8,128)(2,1)S(1)}, u32[]{:S(2)}, u32[]{:S(2)}) collective-permute-start(bf16[368,128]{1,0:T(8,128)(2,1)S(1)} %get-tuple-element.44), channel_id=1, source_target_pairs={{0,8},{8,24},{16,0},{24,16},{1,9},{9,25},{17,1},{25,17},{2,10},{10... | collective-permute-start | bytes 282632 | tf_op jit(solution)/shard_map/ppermute | solution.py:439
  47.2 1.3 %collective-permute-start.14 = (bf16[368,128]{1,0:T(8,128)(2,1)S(1)}, bf16[368,128]{1,0:T(8,128)(2,1)S(1)}, u32[]{:S(2)}, u32[]{:S(2)}) collective-permute-start(bf16[368,128]{1,0:T(8,128)(2,1)S(1)} %get-tuple-element.43), channel_id=1, source_target_pairs={{8,16},{16,24},{9,17},{17,25},{10,18},{18,26},{11,19},{19,27},{12,... | collective-permute-start | bytes 282632 | tf_op jit(solution)/shard_map/ppermute | solution.py:439
  48.5 1.2 %shard_map.51 = (f32[2,352,128]{2,1,0:T(8,128)S(1)}, f32[2,352,1]{2,1,0:T(8,128)S(1)}) custom-call(s32[2]{0:T(128)S(1)} %pad_add_fusion.refs_0_.place_ref, f32[2,352,128]{2,1,0:T(8,128)S(1)} %get-tuple-element.35.refs_1_, f32[2,352,1]{2,1,0:T(8,128)S(1)} %get-tuple-element.36.refs_6_.refs_2_, ...), custom_call_target="tpu_custom_call" | custom-call | tf_op jit(solution)/shard_map/pallas_call | solution.py:485
  49.7 0.4 collective-permute-done.13.first_ref
  50.1 3.5 %collective-permute-done.14.below_ref = bf16[368,128]{1,0:T(8,128)(2,1)S(1)} collective-permute-done((bf16[368,128]{1,0:T(8,128)(2,1)S(1)}, bf16[368,128]{1,0:T(8,128)(2,1)S(1)}, u32[]{:S(2)}, u32[]{:S(2)}) %collective-permute-start.14) | collective-permute-done | bytes 94240 | tf_op jit(solution)/shard_map/ppermute | solution.py:439
  53.6 1.1 %shard_map.52 = (bf16[176,256]{1,0:T(8,128)(2,1)S(1)}, bf16[176,256]{1,0:T(8,128)(2,1)S(1)}) custom-call(s32[2]{0:T(128)S(1)} %pad_add_fusion.refs_0_.place_ref, f32[2,352,128]{2,1,0:T(8,128)S(1)} %get-tuple-element.37.out_ref, f32[2,352,1]{2,1,0:T(8,128)S(1)} %get-tuple-element.38.logs_ref, bf16[368,128]{1,0:T(8,128)(2,1)S(1)} %collective-permute-done.13.first_ref, ...), custom_call_target="tpu_custom_call" | custom-call | tf_op jit(solution)/shard_map/pallas_call | solution.py:489
  54.7 1.6 %collective-permute-start.15 = (bf16[176,256]{1,0:T(8,128)(2,1)S(1)}, bf16[176,256]{1,0:T(8,128)(2,1)S(1)}, u32[]{:S(2)}, u32[]{:S(2)}) collective-permute-start(bf16[176,256]{1,0:T(8,128)(2,1)S(1)} %get-tuple-element.40), channel_id=1, source_target_pairs={{0,4},{4,0},{1,5},{5,1},{2,6},{6,2},{3,7},{7,3},{8,12},{12,8},{9,1... | collective-permute-start | bytes 270344 | tf_op jit(solution)/shard_map/ppermute | solution.py:338
  56.3 3.0 %collective-permute-done.15 = bf16[176,256]{1,0:T(8,128)(2,1)S(1)} collective-permute-done((bf16[176,256]{1,0:T(8,128)(2,1)S(1)}, bf16[176,256]{1,0:T(8,128)(2,1)S(1)}, u32[]{:S(2)}, u32[]{:S(2)}) %collective-permute-start.15) | collective-permute-done | bytes 90144 | tf_op jit(solution)/shard_map/ppermute | solution.py:338
  59.3 0.7 %pad_maximum_fusion.2 = bf16[176,512]{1,0:T(8,128)(2,1)} fusion(bf16[176,256]{1,0:T(8,128)(2,1)S(1)} %get-tuple-element.46, bf16[176,256]{1,0:T(8,128)(2,1)S(1)} %get-tuple-element.45), kind=kLoop, calls=%fused_computation.7 | loop fusion | flops 360448 | bytes 360448 | tf_op jit(solution)/shard_map/concatenate | solution.py:495
  (30 shorter events, 0.6 us)
Async XLA Ops:
  0.0 13.5 %collective-permute-start = (bf16[176,1024]{1,0:T(8,128)(2,1)}, bf16[176,1024]{1,0:T(8,128)(2,1)S(1)}, u32[]{:S(2)}, u32[]{:S(2)}) collective-permute-start(bf16[176,1024]{1,0:T(8,128)(2,1)} %param.4), channel_id=1, source_target_pairs={{0,0},{1,1},{2,4},{3,5},{4,2},{5,3},{6,6},{7,7},{8,8},{9,9},{10,12... | collective-permute-start | bytes 1081352 | tf_op jit(solution)/shard_map/ppermute | solution.py:344
  1.6 11.8 %collective-permute-start.1 = (bf16[176,1024]{1,0:T(8,128)(2,1)}, bf16[176,1024]{1,0:T(8,128)(2,1)S(1)}, u32[]{:S(2)}, u32[]{:S(2)}) collective-permute-start(bf16[176,1024]{1,0:T(8,128)(2,1)} %param.4), channel_id=1, source_target_pairs={{0,2},{1,3},{2,6},{3,7},{4,0},{5,1},{6,4},{7,5},{8,10},{9,11},{10,... | collective-permute-start | bytes 1081352 | tf_op jit(solution)/shard_map/ppermute | solution.py:349
  6.9 1.2 %collective-permute-start.2 = (f32[1200]{0:T(1024)S(1)}, f32[1200]{0:T(1024)S(1)}, u32[]{:S(2)}, u32[]{:S(2)}) collective-permute-start(f32[1200]{0:T(1024)S(1)} %pad_maximum_fusion.3), channel_id=1, source_target_pairs={{0,1},{1,0},{2,3},{3,2},{4,5},{5,4},{6,7},{7,6},{8,9},{9,8},{10,11... | collective-permute-start | bytes 14408 | tf_op jit(solution)/shard_map/ppermute | solution.py:335
  8.9 4.6 %collective-permute-start.3 = (f32[2224]{0:T(1024)S(1)}, f32[2224]{0:T(1024)S(1)}, u32[]{:S(2)}, u32[]{:S(2)}) collective-permute-start(f32[2224]{0:T(1024)S(1)} %concatenate.40), channel_id=1, source_target_pairs={{0,2},{1,3},{2,0},{3,1},{4,6},{5,7},{6,4},{7,5},{8,10},{9,11},{10,... | collective-permute-start | bytes 26696 | tf_op jit(solution)/shard_map/ppermute | solution.py:335
  9.0 8.3 %copy-start.2 = (s32[176]{0:T(256)S(1)}, s32[176]{0:T(256)}, u32[]{:S(2)}) copy-start(s32[176]{0:T(256)} %param.7) | copy-start | bytes 2116
  13.6 4.0 %collective-permute-start.4 = (bf16[176,1024]{1,0:T(8,128)(2,1)S(1)}, bf16[176,1024]{1,0:T(8,128)(2,1)S(1)}, u32[]{:S(2)}, u32[]{:S(2)}) collective-permute-start(bf16[176,1024]{1,0:T(8,128)(2,1)S(1)} %collective-permute-done.a_near), channel_id=1, source_target_pairs={{0,1},{1,0},{2,3},{3,2},{4,5},{5,4},{6,7},{7,6},{8,9},{9,8},{10,11... | collective-permute-start | bytes 1081352 | tf_op jit(solution)/shard_map/ppermute | solution.py:335
  13.7 3.6 %collective-permute-start.6 = (f32[352]{0:T(512)S(1)}, f32[352]{0:T(512)S(1)}, u32[]{:S(2)}, u32[]{:S(2)}) collective-permute-start(f32[352]{0:T(512)S(1)} %pad_maximum_fusion.4), channel_id=1, source_target_pairs={{0,4},{4,0},{1,5},{5,1},{2,6},{6,2},{3,7},{7,3},{8,12},{12,8},{9,1... | collective-permute-start | bytes 4232 | tf_op jit(solution)/shard_map/ppermute | solution.py:338
  15.5 2.1 %collective-permute-start.5 = (bf16[176,1024]{1,0:T(8,128)(2,1)S(1)}, bf16[176,1024]{1,0:T(8,128)(2,1)S(1)}, u32[]{:S(2)}, u32[]{:S(2)}) collective-permute-start(bf16[176,1024]{1,0:T(8,128)(2,1)S(1)} %collective-permute-done.1.a_far), channel_id=1, source_target_pairs={{0,1},{1,0},{2,3},{3,2},{4,5},{5,4},{6,7},{7,6},{8,9},{9,8},{10,11... | collective-permute-start | bytes 1081352 | tf_op jit(solution)/shard_map/ppermute | solution.py:335
  19.5 2.6 %copy-start = (bf16[256,8,4,384]{3,1,2,0:T(8,128)(2,1)}, bf16[256,8,4,384]{3,1,2,0:T(8,128)(2,1)S(1)}, u32[]{:S(2)}) copy-start(bf16[256,8,4,384]{3,1,2,0:T(8,128)(2,1)S(1)} %copy.6) | copy-start | bytes 18874372
  22.2 11.0 %collective-permute-start.7 = (f16[1088,128]{1,0:T(8,128)(2,1)S(1)}, f16[1088,128]{1,0:T(8,128)(2,1)S(1)}, u32[]{:S(2)}, u32[]{:S(2)}) collective-permute-start(f16[1088,128]{1,0:T(8,128)(2,1)S(1)} %convert_element_type.66), channel_id=1, source_target_pairs={{0,4},{4,0},{1,5},{5,1},{2,6},{6,2},{3,7},{7,3},{8,12},{12,8},{9,1... | collective-permute-start | bytes 835592 | tf_op jit(solution)/shard_map/ppermute | solution.py:338
  24.1 2.8 %copy-start.1 = (bf16[256,8,4,384]{3,1,2,0:T(8,128)(2,1)S(1)}, bf16[256,8,4,384]{3,1,2,0:T(8,128)(2,1)}, u32[]{:S(2)}) copy-start(bf16[256,8,4,384]{3,1,2,0:T(8,128)(2,1)} %copy-done) | copy-start | bytes 18874372
  29.2 7.7 %collective-permute-start.8 = (f16[1088,128]{1,0:T(8,128)(2,1)S(1)}, f16[1088,128]{1,0:T(8,128)(2,1)S(1)}, u32[]{:S(2)}, u32[]{:S(2)}) collective-permute-start(f16[1088,128]{1,0:T(8,128)(2,1)S(1)} %convert_element_type.69), channel_id=1, source_target_pairs={{0,4},{4,0},{1,5},{5,1},{2,6},{6,2},{3,7},{7,3},{8,12},{12,8},{9,1... | collective-permute-start | bytes 835592 | tf_op jit(solution)/shard_map/ppermute | solution.py:338
  33.2 1.8 %collective-permute-start.9 = (bf16[16,128]{1,0:T(8,128)(2,1)S(1)}, bf16[16,128]{1,0:T(8,128)(2,1)S(1)}, u32[]{:S(2)}, u32[]{:S(2)}) collective-permute-start(bf16[16,128]{1,0:T(8,128)(2,1)S(1)} %slice.49), channel_id=1, source_target_pairs={{2,3}} | collective-permute-start | bytes 12296 | tf_op jit(solution)/shard_map/ppermute | solution.py:460
  34.0 7.6 %collective-permute-start.10 = (bf16[720,128]{1,0:T(8,128)(2,1)S(1)}, bf16[720,128]{1,0:T(8,128)(2,1)S(1)}, u32[]{:S(2)}, u32[]{:S(2)}) collective-permute-start(bf16[720,128]{1,0:T(8,128)(2,1)S(1)} %get-tuple-element.42), channel_id=1, source_target_pairs={{0,16},{24,8},{8,0},{16,24},{1,17},{25,9},{9,1},{17,25},{2,18},{26... | collective-permute-start | bytes 552968 | tf_op jit(solution)/shard_map/ppermute | solution.py:439
  34.4 7.2 %collective-permute-start.11 = (bf16[720,128]{1,0:T(8,128)(2,1)S(1)}, bf16[720,128]{1,0:T(8,128)(2,1)S(1)}, u32[]{:S(2)}, u32[]{:S(2)}) collective-permute-start(bf16[720,128]{1,0:T(8,128)(2,1)S(1)} %get-tuple-element.41), channel_id=1, source_target_pairs={{8,16},{16,8},{0,0},{24,24},{9,17},{17,9},{1,1},{25,25},{10,18},{1... | collective-permute-start | bytes 552968 | tf_op jit(solution)/shard_map/ppermute | solution.py:439
  37.0 6.8 %collective-permute-start.12 = (bf16[720,128]{1,0:T(8,128)(2,1)S(1)}, bf16[720,128]{1,0:T(8,128)(2,1)S(1)}, u32[]{:S(2)}, u32[]{:S(2)}) collective-permute-start(bf16[720,128]{1,0:T(8,128)(2,1)S(1)} %constant_dynamic-slice_fusion), channel_id=1, source_target_pairs={{0,8},{8,0},{16,24},{24,16},{1,9},{9,1},{17,25},{25,17},{2,10},{10... | collective-permute-start | bytes 552968 | tf_op jit(solution)/shard_map/ppermute | solution.py:439
  44.4 5.7 %collective-permute-start.13 = (bf16[368,128]{1,0:T(8,128)(2,1)S(1)}, bf16[368,128]{1,0:T(8,128)(2,1)S(1)}, u32[]{:S(2)}, u32[]{:S(2)}) collective-permute-start(bf16[368,128]{1,0:T(8,128)(2,1)S(1)} %get-tuple-element.44), channel_id=1, source_target_pairs={{0,8},{8,24},{16,0},{24,16},{1,9},{9,25},{17,1},{25,17},{2,10},{10... | collective-permute-start | bytes 282632 | tf_op jit(solution)/shard_map/ppermute | solution.py:439
  47.2 6.5 %collective-permute-start.14 = (bf16[368,128]{1,0:T(8,128)(2,1)S(1)}, bf16[368,128]{1,0:T(8,128)(2,1)S(1)}, u32[]{:S(2)}, u32[]{:S(2)}) collective-permute-start(bf16[368,128]{1,0:T(8,128)(2,1)S(1)} %get-tuple-element.43), channel_id=1, source_target_pairs={{8,16},{16,24},{9,17},{17,25},{10,18},{18,26},{11,19},{19,27},{12,... | collective-permute-start | bytes 282632 | tf_op jit(solution)/shard_map/ppermute | solution.py:439
  54.7 4.6 %collective-permute-start.15 = (bf16[176,256]{1,0:T(8,128)(2,1)S(1)}, bf16[176,256]{1,0:T(8,128)(2,1)S(1)}, u32[]{:S(2)}, u32[]{:S(2)}) collective-permute-start(bf16[176,256]{1,0:T(8,128)(2,1)S(1)} %get-tuple-element.40), channel_id=1, source_target_pairs={{0,4},{4,0},{1,5},{5,1},{2,6},{6,2},{3,7},{7,3},{8,12},{12,8},{9,1... | collective-permute-start | bytes 270344 | tf_op jit(solution)/shard_map/ppermute | solution.py:338

commit v17 on v16

--- a/solution.py
+++ b/solution.py
@@ -51,11 +51,21 @@
 
 def normalise_project_kernel(
     place_ref, a_near, a_far, b_near, b_far, squares_ref, gain_ref, cos_ref, sin_ref, weight_ref,
-    out_ref, normed_ref,
+    out_ref, normed_ref, second_ref, own_ref, semaphores,
 ):
     rows, size = a_near.shape[0], cos_ref.shape[1]
     features = 2 * gain_ref.shape[0] * gain_ref.shape[2]
-    core, near_row, away = place_ref[0], place_ref[1], place_ref[2]
+    core, near_row, away, own = place_ref[0], place_ref[1], place_ref[2], place_ref[3]
+    copies = [
+        pltpu.make_async_copy(
+            weight_ref.at[:, pl.ds(pl.multiple_of(first, size), target.shape[1])],
+            target,
+            semaphores.at[index],
+        )
+        for index, (first, target) in enumerate(((away + size, second_ref), (own, own_ref)))
+    ]
+    for copy in copies:
+        copy.start()
     for shards, half in (((a_near, a_far), core), ((b_near, b_far), 1 - core)):
         gain = gain_ref[half]
         for shard, row in zip(shards, (near_row, 1 - near_row)):
@@ -69,35 +79,24 @@
         normed_ref, weight_ref, away + keys * size, away + query * size, cos_ref, sin_ref,
         jnp.zeros((EXTRA, size), jnp.float32), out_ref,
     )
-
-
-def second_kernel(
-    place_ref, normed_ref, cos_ref, sin_ref, weight_ref, out_ref, own_hbm, semaphore
-):
+    for copy in copies:
+        copy.wait()
+
+
+def second_kernel(normed_ref, cos_ref, sin_ref, weight_ref, out_ref):
     size = cos_ref.shape[1]
-    away, own = place_ref[2], place_ref[3]
-    copy = pltpu.make_async_copy(
-        weight_ref.at[:, pl.ds(pl.multiple_of(own, size), 6 * size)], own_hbm, semaphore
-    )
-    copy.start()
     keys, query = CHUNKS[1]
     project_chunk(
-        normed_ref, weight_ref, away + keys * size, away + query * size, cos_ref, sin_ref,
+        normed_ref, weight_ref, 0, (query - keys) * size, cos_ref, sin_ref,
         jnp.zeros((EXTRA, size), jnp.float32), out_ref,
     )
-    copy.wait()
-
-
-def project_kernel(
-    normed_ref, docs_ref, cos_ref, sin_ref, own_hbm, one_ref, two_ref, weight_buffer, semaphore
-):
-    copy = pltpu.make_async_copy(own_hbm, weight_buffer, semaphore)
-    copy.start()
-    copy.wait()
+
+
+def project_kernel(normed_ref, docs_ref, cos_ref, sin_ref, weight_ref, one_ref, two_ref):
     size = cos_ref.shape[1]
     for chunk, (keys, query) in enumerate(CHUNKS):
         project_chunk(
-            normed_ref, weight_buffer, keys * size, query * size, cos_ref, sin_ref, docs_ref[...],
+            normed_ref, weight_ref, keys * size, query * size, cos_ref, sin_ref, docs_ref[...],
             (one_ref, two_ref)[chunk],
         )
 
@@ -379,40 +378,39 @@
     partial_sums = jax.ShapeDtypeStruct((taller, size), jnp.float32)
     no_cost = pl.CostEstimate(flops=0, bytes_accessed=0, transcendentals=0)
     columns = jnp.stack([core, chip, (1 - row) * (pair * triple), row * (pair * triple)])
-    first, normed = pl.pallas_call(
+    first, normed, second_weight, own_weight = pl.pallas_call(
         normalise_project_kernel,
-        out_shape=(partial_sums, jax.ShapeDtypeStruct((2, block, width), jnp.bfloat16)),
+        out_shape=(
+            partial_sums,
+            jax.ShapeDtypeStruct((2, block, width), jnp.bfloat16),
+            jax.ShapeDtypeStruct((span, triple), jnp.bfloat16),
+            jax.ShapeDtypeStruct((span, pair * triple), jnp.bfloat16),
+        ),
         in_specs=[pl.BlockSpec(memory_space=pltpu.SMEM)] + in_vmem(9),
-        out_specs=tuple(in_vmem(2)),
-        compiler_params=pltpu.CompilerParams(vmem_limit_bytes=12 * MIB),
+        out_specs=tuple(in_vmem(4)),
+        scratch_shapes=[pltpu.SemaphoreType.DMA((2,))],
+        compiler_params=pltpu.CompilerParams(vmem_limit_bytes=16 * MIB),
         cost_estimate=no_cost,
     )(
         columns, near, far, near_other, far_other, squares, gain, cosine, sine, flat_weight,
     )
-    second, own_weight = pl.pallas_call(
+    second = pl.pallas_call(
         second_kernel,
-        out_shape=(partial_sums, pltpu.HBM((span, pair * triple), jnp.bfloat16)),
-        in_specs=[pl.BlockSpec(memory_space=pltpu.SMEM)] + in_vmem(4),
-        out_specs=(in_vmem(1)[0], pl.BlockSpec(memory_space=pltpu.HBM)),
-        scratch_shapes=[pltpu.SemaphoreType.DMA(())],
-        compiler_params=pltpu.CompilerParams(vmem_limit_bytes=12 * MIB),
+        out_shape=partial_sums,
+        in_specs=in_vmem(4),
+        out_specs=in_vmem(1)[0],
+        compiler_params=pltpu.CompilerParams(vmem_limit_bytes=8 * MIB),
         cost_estimate=no_cost,
-    )(columns, normed, cosine, sine, flat_weight)
+    )(normed, cosine, sine, second_weight)
     arrived = [by_row(chunk.astype(jnp.float16)) for chunk in (first, second)]
     own = pl.pallas_call(
         project_kernel,
         out_shape=(partial_sums, partial_sums),
-        in_specs=in_vmem(4) + [pl.BlockSpec(memory_space=pltpu.HBM)],
+        in_specs=in_vmem(5),
         out_specs=tuple(in_vmem(2)),
-        scratch_shapes=[
-            pltpu.VMEM((span, pair * triple), jnp.bfloat16),
-            pltpu.SemaphoreType.DMA(()),
-        ],
         compiler_params=pltpu.CompilerParams(vmem_limit_bytes=8 * MIB),
         cost_estimate=no_cost,
-    )(
-        normed, doc_rows, cosine, sine, pltpu.with_memory_space_constraint(own_weight, pltpu.HBM)
-    )
+    )(normed, doc_rows, cosine, sine, own_weight)
     scale = 1.0 / math.sqrt(size)
 
     def summed(chunk):

time: 60.5 us -> 61.9 us (1.023)
  waiting for transfers between devices: 14 us -> 17.6 us
  Pallas kernels: 12.5 us -> 9.76 us
  other arithmetic: 5.66 us -> 7.34 us
  local copies, waits for them, and re-layouts: 9.83 us -> 8.49 us
    ppermute x4, waiting for transfers between devices: 5.44 us -> 9.35 us  [by_row(): return lax.ppermute(value, 'row', [(0, 1), (1, 0)])]
    pallas_call x1, Pallas kernels: 3.66 us -> 1.77 us  [per_device(): pl.pallas_call(project_kernel, out_shape=(partial_sums, partial_sums), in...]
    unnamed x7 -> x15, local copies, waits for them, and re-layouts: 9.38 us -> 8.05 us
    pallas_call x1, Pallas kernels: 2.24 us -> 0.98 us  [per_device(): pl.pallas_call(second_kernel, out_shape=partial_sums, in_specs=in_vmem(4)...]
    convert_element_type x2, other arithmetic: 0.15 us -> 1.13 us  [summed(): (own[chunk] + arrived[chunk].astype(jnp.float32)).astype(jnp.bfloat16)]
    ppermute x5, starting transfers between devices: 6.33 us -> 5.43 us  [along_tok(): return lax.ppermute(value, 'tok', pairs)]
    convert_element_type x2, other arithmetic: 0.08 us -> 0.78 us  [per_device(): arrived = [by_row(chunk.astype(jnp.float16)) for chunk in (first, second)]]
  transfers between devices with their start and end apart: 16 -> 16, of which waited for: 9 -> 10; matrix products, arithmetic and copies ran while one was open for 15% -> 17% of each run, Pallas kernels for 15% -> 10%
where the time goes in v17:
time: 61.9 us; the launch traced here: 60.8 us
  waiting for transfers between devices  17.6 us (28%)
  starting transfers between devices  17.3 us (28%)
  Pallas kernels  9.76 us (16%)
  local copies, waits for them, and re-layouts  8.49 us (14%)
  other arithmetic  7.34 us (12%)
    ppermute x4, waiting for transfers between devices, by_row(): return lax.ppermute(value, 'row', [(0, 1), (1, 0)])  9.35 us
    unnamed x15, local copies, waits for them, and re-layouts  8.05 us
    ppermute x5, waiting for transfers between devices, along_tok(): return lax.ppermute(value, 'tok', pairs)  7.29 us
    ppermute x4, starting transfers between devices, by_row(): return lax.ppermute(value, 'row', [(0, 1), (1, 0)])  5.97 us
    ppermute x5, starting transfers between devices, along_tok(): return lax.ppermute(value, 'tok', pairs)  5.43 us
    ppermute x1, starting transfers between devices, per_device(): lax.ppermute(activations, ('row', 'col'), [(r * 4 + c, c // 2 * 4 + 2 * (...  3.31 us
    pallas_call x1, Pallas kernels, per_device(): pl.pallas_call(normalise_project_kernel, out_shape=(partial_sums, jax.Sha...  2.3 us
    pallas_call x1, Pallas kernels, per_device(): on_place(lambda *refs: own_block_kernel(scale, *refs), part_shapes, 2)  1.85 us
  transfers between devices with their start and end apart: 16, of which 10 were waited for; matrix products, arithmetic and copies ran while one was open for 17% of the time, Pallas kernels for 10%

profile of v17, /device:TPU:24, one launch (start us, length us, event | category | flops | bytes accessed | tf_op | source)
XLA Modules:
  0.0 60.8 jit_solution(15927529163008181099)
XLA Ops:
  0.0 1.6 %collective-permute-start = (bf16[176,1024]{1,0:T(8,128)(2,1)}, bf16[176,1024]{1,0:T(8,128)(2,1)S(1)}, u32[]{:S(2)}, u32[]{:S(2)}) collective-permute-start(bf16[176,1024]{1,0:T(8,128)(2,1)} %param.4), channel_id=1, source_target_pairs={{0,0},{1,1},{2,4},{3,5},{4,2},{5,3},{6,6},{7,7},{8,8},{9,9},{10,12... | collective-permute-start | bytes 1081352 | tf_op jit(solution)/shard_map/ppermute | solution.py:343
  1.6 3.3 %collective-permute-start.1 = (bf16[176,1024]{1,0:T(8,128)(2,1)}, bf16[176,1024]{1,0:T(8,128)(2,1)S(1)}, u32[]{:S(2)}, u32[]{:S(2)}) collective-permute-start(bf16[176,1024]{1,0:T(8,128)(2,1)} %param.4), channel_id=1, source_target_pairs={{0,2},{1,3},{2,6},{3,7},{4,0},{5,1},{6,4},{7,5},{8,10},{9,11},{10,... | collective-permute-start | bytes 1081352 | tf_op jit(solution)/shard_map/ppermute | solution.py:348
  4.9 1.2 %multiply_reduce_fusion = f32[176]{0:T(256)S(1)} fusion(bf16[176,1024]{1,0:T(8,128)(2,1)} %param.4), kind=kLoop, calls=%fused_computation | loop fusion | flops 540496 | bytes 361152 | tf_op jit(solution)/shard_map/reduce_sum | solution.py:354
  6.1 0.7 %convert_element_type.61 = f32[1024]{0:T(1024)S(1)} convert(bf16[1024]{0:T(1024)(128)(2,1)} %param.5) | non-fusion elementwise | flops 1024 | bytes 6144 | tf_op jit(solution)/shard_map/convert_element_type | solution.py:355
  6.9 0.7 %convert_add_fusion = f32[176]{0:T(256)S(1)} fusion(s32[176]{0:T(256)} %param.7), kind=kLoop, calls=%fused_computation.28 | loop fusion | flops 352 | bytes 1408 | tf_op jit(solution)/shard_map/add | solution.py:367
  7.6 0.5 collective-permute-done.2
  8.0 0.8 %slice_select_fusion = (f32[1024]{0:T(1024)S(1)}, f32[1024]{0:T(1024)S(1)}) fusion(f32[1200]{0:T(1024)S(1)} %collective-permute-done.2, bf16[1024]{0:T(1024)(128)(2,1)} %param.5, pred[]{:T(512)S(6)} %eq.22), kind=kLoop, calls=%fused_computation.18 | loop fusion | flops 3072 | bytes 14337 | tf_op jit(solution)/shard_map/jit(_where)/select_n | solution.py:341
  8.9 0.1 pad_add_fusion.1.place_ref
  9.0 4.0 %copy.6 = bf16[256,8,4,384]{3,1,2,0:T(8,128)(2,1)S(1)} copy(bf16[256,8,4,384]{3,2,1,0:T(4,128)(2,1)} %bitcast.25) | data formatting | bytes 12582912
  12.9 0.5 collective-permute-done.3
  13.7 1.8 %collective-permute-start.6 = (f32[352]{0:T(512)S(1)}, f32[352]{0:T(512)S(1)}, u32[]{:S(2)}, u32[]{:S(2)}) collective-permute-start(f32[352]{0:T(512)S(1)} %pad_maximum_fusion.4), channel_id=1, source_target_pairs={{0,4},{4,0},{1,5},{5,1},{2,6},{6,2},{3,7},{7,3},{8,12},{12,8},{9,1... | collective-permute-start | bytes 4232 | tf_op jit(solution)/shard_map/ppermute | solution.py:337
  15.5 0.2 collective-permute-start.5
  15.7 0.7 %fusion = (f32[352,64]{1,0:T(8,128)S(1)}, f32[352,64]{1,0:T(8,128)S(1)}, f32[352,64]{1,0:T(8,128)S(1)}) fusion(f32[64]{0:T(128)S(1)} %fusion.2, f32[352]{0:T(512)S(1)} %add_convert_fusion.2), kind=kLoop, calls=%fused_computation.12 | loop fusion | flops 45056 | bytes 272000 | tf_op jit(solution)/shard_map/neg | solution.py:26
  16.5 0.2 pad_maximum_fusion
  16.6 0.7 %collective-permute-done.6 = f32[352]{0:T(512)S(1)} collective-permute-done((f32[352]{0:T(512)S(1)}, f32[352]{0:T(512)S(1)}, u32[]{:S(2)}, u32[]{:S(2)}) %collective-permute-start.6) | collective-permute-done | bytes 1440 | tf_op jit(solution)/shard_map/ppermute | solution.py:337
  17.5 0.1 reshape.71.squares_ref
  17.6 1.0 %copy-done.3 = bf16[176,1024]{1,0:T(8,128)(2,1)S(1)} copy-done((bf16[176,1024]{1,0:T(8,128)(2,1)S(1)}, bf16[176,1024]{1,0:T(8,128)(2,1)}, u32[]{:S(2)}) %copy-start.3) | copy-done | bytes 360472
  18.6 1.0 %copy-done.5 = bf16[176,1024]{1,0:T(8,128)(2,1)S(1)} copy-done((bf16[176,1024]{1,0:T(8,128)(2,1)S(1)}, bf16[176,1024]{1,0:T(8,128)(2,1)}, u32[]{:S(2)}) %copy-start.5) | copy-done | bytes 360472
  19.6 2.3 %shard_map.46 = (f32[1088,128]{1,0:T(8,128)S(1)}, bf16[2,352,1024]{2,1,0:T(8,128)(2,1)S(1)}, bf16[2048,384]{1,0:T(8,128)(2,1)S(1)}, bf16[2048,768]{1,0:T(8,128)(2,1)S(1)}) custom-call(s32[4]{0:T(128)S(1)} %pad_add_fusion.1.place_ref, bf16[176,1024]{1,0:T(8,128)(2,1)S(1)} %copy-done.3, bf16[176,1024]{1,0:T(8,128)(2,1)S(1)} %copy-done.5, ...), custom_call_target="tpu_custom_call" | custom-call | tf_op jit(solution)/shard_map/pallas_call | solution.py:381
  21.9 1.6 %copy-done = bf16[2048,768]{1,0:T(8,128)(2,1)} copy-done((bf16[2048,768]{1,0:T(8,128)(2,1)}, bf16[2048,768]{1,0:T(8,128)(2,1)S(1)}, u32[]{:S(2)}) %copy-start) | copy-done | bytes 3145752
  23.5 0.7 %convert_element_type.66 = f16[1088,128]{1,0:T(8,128)(2,1)} convert(f32[1088,128]{1,0:T(8,128)S(1)} %get-tuple-element.32) | non-fusion elementwise | flops 139264 | bytes 835584 | tf_op jit(solution)/shard_map/convert_element_type | solution.py:405
  24.3 1.8 %collective-permute-start.7 = (f16[1088,128]{1,0:T(8,128)(2,1)}, f16[1088,128]{1,0:T(8,128)(2,1)}, u32[]{:S(2)}, u32[]{:S(2)}) collective-permute-start(f16[1088,128]{1,0:T(8,128)(2,1)} %convert_element_type.66), channel_id=1, source_target_pairs={{0,4},{4,0},{1,5},{5,1},{2,6},{6,2},{3,7},{7,3},{8,12},{12,8},{9,1... | collective-permute-start | bytes 835592 | tf_op jit(solution)/shard_map/ppermute | solution.py:337
  26.1 1.0 %shard_map.48 = f32[1088,128]{1,0:T(8,128)S(1)} custom-call(bf16[2,352,1024]{2,1,0:T(8,128)(2,1)S(1)} %get-tuple-element.29.normed_ref, f32[352,128]{1,0:T(8,128)S(1)} %get-tuple-element.58.cos_ref, f32[352,128]{1,0:T(8,128)S(1)} %get-tuple-element.59.sin_ref, bf16[2048,384]{1,0:T(8,128)(2,1)S(1)} %get-tuple-element.34.weight_ref), custom_call_target="tpu_custom_call" | custom-call | tf_op jit(solution)/shard_map/pallas_call | solution.py:397
  27.2 0.3 collective-permute-start.8
  27.5 0.5 copy-done.1
  27.9 1.8 %shard_map.47 = (f32[1088,128]{1,0:T(8,128)S(1)}, f32[1088,128]{1,0:T(8,128)S(1)}) custom-call(bf16[2,352,1024]{2,1,0:T(8,128)(2,1)S(1)} %get-tuple-element.29.normed_ref, f32[16,128]{1,0:T(8,128)S(1)} %fusion.1.docs_ref, f32[352,128]{1,0:T(8,128)S(1)} %get-tuple-element.58.cos_ref, f32[352,128]{1,0:T(8,128)S(1)} %get-tuple-element.59.sin_ref, ...), custom_call_target="tpu_custom_call" | custom-call | tf_op jit(solution)/shard_map/pallas_call | solution.py:406
  29.7 4.4 %collective-permute-done.7 = f16[1088,128]{1,0:T(8,128)(2,1)} collective-permute-done((f16[1088,128]{1,0:T(8,128)(2,1)}, f16[1088,128]{1,0:T(8,128)(2,1)}, u32[]{:S(2)}, u32[]{:S(2)}) %collective-permute-start.7) | collective-permute-done | bytes 278560 | tf_op jit(solution)/shard_map/ppermute | solution.py:337
  34.1 1.0 %add_convert_fusion.1.refs_1_.refs_4_.refs_3_ = bf16[1088,128]{1,0:T(8,128)(2,1)S(1)} fusion(f32[1088,128]{1,0:T(8,128)S(1)} %get-tuple-element.31, f16[1088,128]{1,0:T(8,128)(2,1)} %collective-permute-done.7), kind=kLoop, calls=%fused_computation.2 | loop fusion | flops 417792 | bytes 1114112 | tf_op jit(solution)/shard_map/convert_element_type | solution.py:417
  35.2 0.7 %collective-permute-start.9 = (bf16[16,128]{1,0:T(8,128)(2,1)S(1)}, bf16[16,128]{1,0:T(8,128)(2,1)S(1)}, u32[]{:S(2)}, u32[]{:S(2)}) collective-permute-start(bf16[16,128]{1,0:T(8,128)(2,1)S(1)} %slice.49), channel_id=1, source_target_pairs={{2,3}} | collective-permute-start | bytes 12296 | tf_op jit(solution)/shard_map/ppermute | solution.py:458
  35.9 0.1 constant_dynamic-slice_fusion.1
  36.0 0.4 collective-permute-start.10
  36.4 0.7 %collective-permute-start.11 = (bf16[720,128]{1,0:T(8,128)(2,1)S(1)}, bf16[720,128]{1,0:T(8,128)(2,1)S(1)}, u32[]{:S(2)}, u32[]{:S(2)}) collective-permute-start(bf16[720,128]{1,0:T(8,128)(2,1)S(1)} %get-tuple-element.41), channel_id=1, source_target_pairs={{8,16},{16,8},{0,0},{24,24},{9,17},{17,9},{1,1},{25,25},{10,18},{1... | collective-permute-start | bytes 552968 | tf_op jit(solution)/shard_map/ppermute | solution.py:437
  37.1 1.7 %collective-permute-done.8 = f16[1088,128]{1,0:T(8,128)(2,1)S(1)} collective-permute-done((f16[1088,128]{1,0:T(8,128)(2,1)S(1)}, f16[1088,128]{1,0:T(8,128)(2,1)S(1)}, u32[]{:S(2)}, u32[]{:S(2)}) %collective-permute-start.8) | collective-permute-done | bytes 278560 | tf_op jit(solution)/shard_map/ppermute | solution.py:337
  38.8 0.1 add_convert_fusion.refs_2_.refs_5_.refs_4_
  39.0 1.3 %collective-permute-start.12 = (bf16[720,128]{1,0:T(8,128)(2,1)S(1)}, bf16[720,128]{1,0:T(8,128)(2,1)S(1)}, u32[]{:S(2)}, u32[]{:S(2)}) collective-permute-start(bf16[720,128]{1,0:T(8,128)(2,1)S(1)} %constant_dynamic-slice_fusion), channel_id=1, source_target_pairs={{0,8},{8,0},{16,24},{24,16},{1,9},{9,1},{17,25},{25,17},{2,10},{10... | collective-permute-start | bytes 552968 | tf_op jit(solution)/shard_map/ppermute | solution.py:437
  40.3 1.8 %shard_map.49 = (f32[2,352,128]{2,1,0:T(8,128)S(1)}, f32[2,352,1]{2,1,0:T(8,128)S(1)}) custom-call(s32[2]{0:T(128)S(1)} %pad_add_fusion.refs_0_.place_ref, bf16[1088,128]{1,0:T(8,128)(2,1)S(1)} %add_convert_fusion.1.refs_1_.refs_4_.refs_3_, bf16[1088,128]{1,0:T(8,128)(2,1)S(1)} %add_convert_fusion.refs_2_.refs_5_.refs_4_), custom_call_target="tpu_custom_call" | custom-call | tf_op jit(solution)/shard_map/pallas_call | solution.py:472
  42.2 0.4 collective-permute-done.10.refs_1_.refs_5_
  42.6 2.9 %collective-permute-done.12.refs_3_.refs_7_ = bf16[720,128]{1,0:T(8,128)(2,1)S(1)} collective-permute-done((bf16[720,128]{1,0:T(8,128)(2,1)S(1)}, bf16[720,128]{1,0:T(8,128)(2,1)S(1)}, u32[]{:S(2)}, u32[]{:S(2)}) %collective-permute-start.12) | collective-permute-done | bytes 184352 | tf_op jit(solution)/shard_map/ppermute | solution.py:437
  45.5 0.6 shard_map.50.refs_8_
  46.1 1.8 %collective-permute-start.13 = (bf16[368,128]{1,0:T(8,128)(2,1)S(1)}, bf16[368,128]{1,0:T(8,128)(2,1)S(1)}, u32[]{:S(2)}, u32[]{:S(2)}) collective-permute-start(bf16[368,128]{1,0:T(8,128)(2,1)S(1)} %get-tuple-element.44), channel_id=1, source_target_pairs={{0,8},{8,24},{16,0},{24,16},{1,9},{9,25},{17,1},{25,17},{2,10},{10... | collective-permute-start | bytes 282632 | tf_op jit(solution)/shard_map/ppermute | solution.py:437
  47.9 1.3 %collective-permute-start.14 = (bf16[368,128]{1,0:T(8,128)(2,1)S(1)}, bf16[368,128]{1,0:T(8,128)(2,1)S(1)}, u32[]{:S(2)}, u32[]{:S(2)}) collective-permute-start(bf16[368,128]{1,0:T(8,128)(2,1)S(1)} %get-tuple-element.43), channel_id=1, source_target_pairs={{8,16},{16,24},{9,17},{17,25},{10,18},{18,26},{11,19},{19,27},{12,... | collective-permute-start | bytes 282632 | tf_op jit(solution)/shard_map/ppermute | solution.py:437
  49.2 1.2 %shard_map.51 = (f32[2,352,128]{2,1,0:T(8,128)S(1)}, f32[2,352,1]{2,1,0:T(8,128)S(1)}) custom-call(s32[2]{0:T(128)S(1)} %pad_add_fusion.refs_0_.place_ref, f32[2,352,128]{2,1,0:T(8,128)S(1)} %get-tuple-element.35.refs_1_, f32[2,352,1]{2,1,0:T(8,128)S(1)} %get-tuple-element.36.refs_6_.refs_2_, ...), custom_call_target="tpu_custom_call" | custom-call | tf_op jit(solution)/shard_map/pallas_call | solution.py:483
  50.5 1.6 %collective-permute-done.13.first_ref = bf16[368,128]{1,0:T(8,128)(2,1)S(1)} collective-permute-done((bf16[368,128]{1,0:T(8,128)(2,1)S(1)}, bf16[368,128]{1,0:T(8,128)(2,1)S(1)}, u32[]{:S(2)}, u32[]{:S(2)}) %collective-permute-start.13) | collective-permute-done | bytes 94240 | tf_op jit(solution)/shard_map/ppermute | solution.py:437
  52.1 2.3 %collective-permute-done.14.below_ref = bf16[368,128]{1,0:T(8,128)(2,1)S(1)} collective-permute-done((bf16[368,128]{1,0:T(8,128)(2,1)S(1)}, bf16[368,128]{1,0:T(8,128)(2,1)S(1)}, u32[]{:S(2)}, u32[]{:S(2)}) %collective-permute-start.14) | collective-permute-done | bytes 94240 | tf_op jit(solution)/shard_map/ppermute | solution.py:437
  54.4 1.1 %shard_map.52 = (bf16[176,256]{1,0:T(8,128)(2,1)S(1)}, bf16[176,256]{1,0:T(8,128)(2,1)S(1)}) custom-call(s32[2]{0:T(128)S(1)} %pad_add_fusion.refs_0_.place_ref, f32[2,352,128]{2,1,0:T(8,128)S(1)} %get-tuple-element.37.out_ref, f32[2,352,1]{2,1,0:T(8,128)S(1)} %get-tuple-element.38.logs_ref, bf16[368,128]{1,0:T(8,128)(2,1)S(1)} %collective-permute-done.13.first_ref, ...), custom_call_target="tpu_custom_call" | custom-call | tf_op jit(solution)/shard_map/pallas_call | solution.py:487
  55.5 2.1 %collective-permute-start.15 = (bf16[176,256]{1,0:T(8,128)(2,1)S(1)}, bf16[176,256]{1,0:T(8,128)(2,1)S(1)}, u32[]{:S(2)}, u32[]{:S(2)}) collective-permute-start(bf16[176,256]{1,0:T(8,128)(2,1)S(1)} %get-tuple-element.40), channel_id=1, source_target_pairs={{0,4},{4,0},{1,5},{5,1},{2,6},{6,2},{3,7},{7,3},{8,12},{12,8},{9,1... | collective-permute-start | bytes 270344 | tf_op jit(solution)/shard_map/ppermute | solution.py:337
  57.6 2.5 %collective-permute-done.15 = bf16[176,256]{1,0:T(8,128)(2,1)S(1)} collective-permute-done((bf16[176,256]{1,0:T(8,128)(2,1)S(1)}, bf16[176,256]{1,0:T(8,128)(2,1)S(1)}, u32[]{:S(2)}, u32[]{:S(2)}) %collective-permute-start.15) | collective-permute-done | bytes 90144 | tf_op jit(solution)/shard_map/ppermute | solution.py:337
  60.1 0.7 %pad_maximum_fusion.2 = bf16[176,512]{1,0:T(8,128)(2,1)} fusion(bf16[176,256]{1,0:T(8,128)(2,1)S(1)} %get-tuple-element.46, bf16[176,256]{1,0:T(8,128)(2,1)S(1)} %get-tuple-element.45), kind=kLoop, calls=%fused_computation.7 | loop fusion | flops 360448 | bytes 360448 | tf_op jit(solution)/shard_map/concatenate | solution.py:493
  (38 shorter events, 0.9 us)
Async XLA Ops:
  0.0 13.5 %collective-permute-start = (bf16[176,1024]{1,0:T(8,128)(2,1)}, bf16[176,1024]{1,0:T(8,128)(2,1)S(1)}, u32[]{:S(2)}, u32[]{:S(2)}) collective-permute-start(bf16[176,1024]{1,0:T(8,128)(2,1)} %param.4), channel_id=1, source_target_pairs={{0,0},{1,1},{2,4},{3,5},{4,2},{5,3},{6,6},{7,7},{8,8},{9,9},{10,12... | collective-permute-start | bytes 1081352 | tf_op jit(solution)/shard_map/ppermute | solution.py:343
  1.6 11.8 %collective-permute-start.1 = (bf16[176,1024]{1,0:T(8,128)(2,1)}, bf16[176,1024]{1,0:T(8,128)(2,1)S(1)}, u32[]{:S(2)}, u32[]{:S(2)}) collective-permute-start(bf16[176,1024]{1,0:T(8,128)(2,1)} %param.4), channel_id=1, source_target_pairs={{0,2},{1,3},{2,6},{3,7},{4,0},{5,1},{6,4},{7,5},{8,10},{9,11},{10,... | collective-permute-start | bytes 1081352 | tf_op jit(solution)/shard_map/ppermute | solution.py:348
  6.9 1.2 %collective-permute-start.2 = (f32[1200]{0:T(1024)S(1)}, f32[1200]{0:T(1024)S(1)}, u32[]{:S(2)}, u32[]{:S(2)}) collective-permute-start(f32[1200]{0:T(1024)S(1)} %pad_maximum_fusion.3), channel_id=1, source_target_pairs={{0,1},{1,0},{2,3},{3,2},{4,5},{5,4},{6,7},{7,6},{8,9},{9,8},{10,11... | collective-permute-start | bytes 14408 | tf_op jit(solution)/shard_map/ppermute | solution.py:334
  8.9 4.6 %collective-permute-start.3 = (f32[2224]{0:T(1024)S(1)}, f32[2224]{0:T(1024)S(1)}, u32[]{:S(2)}, u32[]{:S(2)}) collective-permute-start(f32[2224]{0:T(1024)S(1)} %concatenate.40), channel_id=1, source_target_pairs={{0,2},{1,3},{2,0},{3,1},{4,6},{5,7},{6,4},{7,5},{8,10},{9,11},{10,... | collective-permute-start | bytes 26696 | tf_op jit(solution)/shard_map/ppermute | solution.py:334
  9.0 8.3 %copy-start.6 = (s32[176]{0:T(256)S(1)}, s32[176]{0:T(256)}, u32[]{:S(2)}) copy-start(s32[176]{0:T(256)} %param.7) | copy-start | bytes 2116
  13.5 4.1 %copy-start.2 = (bf16[176,1024]{1,0:T(8,128)(2,1)}, bf16[176,1024]{1,0:T(8,128)(2,1)S(1)}, u32[]{:S(2)}) copy-start(bf16[176,1024]{1,0:T(8,128)(2,1)S(1)} %collective-permute-done.a_near) | copy-start | bytes 1081348
  13.5 4.1 %copy-start.4 = (bf16[176,1024]{1,0:T(8,128)(2,1)}, bf16[176,1024]{1,0:T(8,128)(2,1)S(1)}, u32[]{:S(2)}) copy-start(bf16[176,1024]{1,0:T(8,128)(2,1)S(1)} %collective-permute-done.1.a_far) | copy-start | bytes 1081348
  13.6 4.0 %collective-permute-start.4 = (bf16[176,1024]{1,0:T(8,128)(2,1)S(1)}, bf16[176,1024]{1,0:T(8,128)(2,1)S(1)}, u32[]{:S(2)}, u32[]{:S(2)}) collective-permute-start(bf16[176,1024]{1,0:T(8,128)(2,1)S(1)} %collective-permute-done.a_near), channel_id=1, source_target_pairs={{0,1},{1,0},{2,3},{3,2},{4,5},{5,4},{6,7},{7,6},{8,9},{9,8},{10,11... | collective-permute-start | bytes 1081352 | tf_op jit(solution)/shard_map/ppermute | solution.py:334
  13.7 3.6 %collective-permute-start.6 = (f32[352]{0:T(512)S(1)}, f32[352]{0:T(512)S(1)}, u32[]{:S(2)}, u32[]{:S(2)}) collective-permute-start(f32[352]{0:T(512)S(1)} %pad_maximum_fusion.4), channel_id=1, source_target_pairs={{0,4},{4,0},{1,5},{5,1},{2,6},{6,2},{3,7},{7,3},{8,12},{12,8},{9,1... | collective-permute-start | bytes 4232 | tf_op jit(solution)/shard_map/ppermute | solution.py:337
  15.5 2.1 %collective-permute-start.5 = (bf16[176,1024]{1,0:T(8,128)(2,1)S(1)}, bf16[176,1024]{1,0:T(8,128)(2,1)S(1)}, u32[]{:S(2)}, u32[]{:S(2)}) collective-permute-start(bf16[176,1024]{1,0:T(8,128)(2,1)S(1)} %collective-permute-done.1.a_far), channel_id=1, source_target_pairs={{0,1},{1,0},{2,3},{3,2},{4,5},{5,4},{6,7},{7,6},{8,9},{9,8},{10,11... | collective-permute-start | bytes 1081352 | tf_op jit(solution)/shard_map/ppermute | solution.py:334
  17.6 1.0 %copy-start.3 = (bf16[176,1024]{1,0:T(8,128)(2,1)S(1)}, bf16[176,1024]{1,0:T(8,128)(2,1)}, u32[]{:S(2)}) copy-start(bf16[176,1024]{1,0:T(8,128)(2,1)} %copy-done.2) | copy-start | bytes 1081348
  18.6 1.0 %copy-start.5 = (bf16[176,1024]{1,0:T(8,128)(2,1)S(1)}, bf16[176,1024]{1,0:T(8,128)(2,1)}, u32[]{:S(2)}) copy-start(bf16[176,1024]{1,0:T(8,128)(2,1)} %copy-done.4) | copy-start | bytes 1081348
  21.9 1.6 %copy-start = (bf16[2048,768]{1,0:T(8,128)(2,1)}, bf16[2048,768]{1,0:T(8,128)(2,1)S(1)}, u32[]{:S(2)}) copy-start(bf16[2048,768]{1,0:T(8,128)(2,1)S(1)} %get-tuple-element.30.weight_ref) | copy-start | bytes 9437188
  24.3 9.9 %collective-permute-start.7 = (f16[1088,128]{1,0:T(8,128)(2,1)}, f16[1088,128]{1,0:T(8,128)(2,1)}, u32[]{:S(2)}, u32[]{:S(2)}) collective-permute-start(f16[1088,128]{1,0:T(8,128)(2,1)} %convert_element_type.66), channel_id=1, source_target_pairs={{0,4},{4,0},{1,5},{5,1},{2,6},{6,2},{3,7},{7,3},{8,12},{12,8},{9,1... | collective-permute-start | bytes 835592 | tf_op jit(solution)/shard_map/ppermute | solution.py:337
  26.1 1.9 %copy-start.1 = (bf16[2048,768]{1,0:T(8,128)(2,1)S(1)}, bf16[2048,768]{1,0:T(8,128)(2,1)}, u32[]{:S(2)}) copy-start(bf16[2048,768]{1,0:T(8,128)(2,1)} %copy-done) | copy-start | bytes 9437188
  27.2 11.6 %collective-permute-start.8 = (f16[1088,128]{1,0:T(8,128)(2,1)S(1)}, f16[1088,128]{1,0:T(8,128)(2,1)S(1)}, u32[]{:S(2)}, u32[]{:S(2)}) collective-permute-start(f16[1088,128]{1,0:T(8,128)(2,1)S(1)} %convert_element_type.69), channel_id=1, source_target_pairs={{0,4},{4,0},{1,5},{5,1},{2,6},{6,2},{3,7},{7,3},{8,12},{12,8},{9,1... | collective-permute-start | bytes 835592 | tf_op jit(solution)/shard_map/ppermute | solution.py:337
  35.2 1.9 %collective-permute-start.9 = (bf16[16,128]{1,0:T(8,128)(2,1)S(1)}, bf16[16,128]{1,0:T(8,128)(2,1)S(1)}, u32[]{:S(2)}, u32[]{:S(2)}) collective-permute-start(bf16[16,128]{1,0:T(8,128)(2,1)S(1)} %slice.49), channel_id=1, source_target_pairs={{2,3}} | collective-permute-start | bytes 12296 | tf_op jit(solution)/shard_map/ppermute | solution.py:458
  36.0 6.6 %collective-permute-start.10 = (bf16[720,128]{1,0:T(8,128)(2,1)S(1)}, bf16[720,128]{1,0:T(8,128)(2,1)S(1)}, u32[]{:S(2)}, u32[]{:S(2)}) collective-permute-start(bf16[720,128]{1,0:T(8,128)(2,1)S(1)} %get-tuple-element.42), channel_id=1, source_target_pairs={{0,16},{24,8},{8,0},{16,24},{1,17},{25,9},{9,1},{17,25},{2,18},{26... | collective-permute-start | bytes 552968 | tf_op jit(solution)/shard_map/ppermute | solution.py:437
  36.4 6.2 %collective-permute-start.11 = (bf16[720,128]{1,0:T(8,128)(2,1)S(1)}, bf16[720,128]{1,0:T(8,128)(2,1)S(1)}, u32[]{:S(2)}, u32[]{:S(2)}) collective-permute-start(bf16[720,128]{1,0:T(8,128)(2,1)S(1)} %get-tuple-element.41), channel_id=1, source_target_pairs={{8,16},{16,8},{0,0},{24,24},{9,17},{17,9},{1,1},{25,25},{10,18},{1... | collective-permute-start | bytes 552968 | tf_op jit(solution)/shard_map/ppermute | solution.py:437
  39.0 6.5 %collective-permute-start.12 = (bf16[720,128]{1,0:T(8,128)(2,1)S(1)}, bf16[720,128]{1,0:T(8,128)(2,1)S(1)}, u32[]{:S(2)}, u32[]{:S(2)}) collective-permute-start(bf16[720,128]{1,0:T(8,128)(2,1)S(1)} %constant_dynamic-slice_fusion), channel_id=1, source_target_pairs={{0,8},{8,0},{16,24},{24,16},{1,9},{9,1},{17,25},{25,17},{2,10},{10... | collective-permute-start | bytes 552968 | tf_op jit(solution)/shard_map/ppermute | solution.py:437
  46.1 6.0 %collective-permute-start.13 = (bf16[368,128]{1,0:T(8,128)(2,1)S(1)}, bf16[368,128]{1,0:T(8,128)(2,1)S(1)}, u32[]{:S(2)}, u32[]{:S(2)}) collective-permute-start(bf16[368,128]{1,0:T(8,128)(2,1)S(1)} %get-tuple-element.44), channel_id=1, source_target_pairs={{0,8},{8,24},{16,0},{24,16},{1,9},{9,25},{17,1},{25,17},{2,10},{10... | collective-permute-start | bytes 282632 | tf_op jit(solution)/shard_map/ppermute | solution.py:437
  47.9 6.5 %collective-permute-start.14 = (bf16[368,128]{1,0:T(8,128)(2,1)S(1)}, bf16[368,128]{1,0:T(8,128)(2,1)S(1)}, u32[]{:S(2)}, u32[]{:S(2)}) collective-permute-start(bf16[368,128]{1,0:T(8,128)(2,1)S(1)} %get-tuple-element.43), channel_id=1, source_target_pairs={{8,16},{16,24},{9,17},{17,25},{10,18},{18,26},{11,19},{19,27},{12,... | collective-permute-start | bytes 282632 | tf_op jit(solution)/shard_map/ppermute | solution.py:437
  55.5 4.6 %collective-permute-start.15 = (bf16[176,256]{1,0:T(8,128)(2,1)S(1)}, bf16[176,256]{1,0:T(8,128)(2,1)S(1)}, u32[]{:S(2)}, u32[]{:S(2)}) collective-permute-start(bf16[176,256]{1,0:T(8,128)(2,1)S(1)} %get-tuple-element.40), channel_id=1, source_target_pairs={{0,4},{4,0},{1,5},{5,1},{2,6},{6,2},{3,7},{7,3},{8,12},{12,8},{9,1... | collective-permute-start | bytes 270344 | tf_op jit(solution)/shard_map/ppermute | solution.py:337

commit v18 on v17

--- a/solution.py
+++ b/solution.py
@@ -389,7 +389,7 @@
         in_specs=[pl.BlockSpec(memory_space=pltpu.SMEM)] + in_vmem(9),
         out_specs=tuple(in_vmem(4)),
         scratch_shapes=[pltpu.SemaphoreType.DMA((2,))],
-        compiler_params=pltpu.CompilerParams(vmem_limit_bytes=16 * MIB),
+        compiler_params=pltpu.CompilerParams(vmem_limit_bytes=5 * MIB),
         cost_estimate=no_cost,
     )(
         columns, near, far, near_other, far_other, squares, gain, cosine, sine, flat_weight,
@@ -399,7 +399,7 @@
         out_shape=partial_sums,
         in_specs=in_vmem(4),
         out_specs=in_vmem(1)[0],
-        compiler_params=pltpu.CompilerParams(vmem_limit_bytes=8 * MIB),
+        compiler_params=pltpu.CompilerParams(vmem_limit_bytes=4 * MIB),
         cost_estimate=no_cost,
     )(normed, cosine, sine, second_weight)
     arrived = [by_row(chunk.astype(jnp.float16)) for chunk in (first, second)]
@@ -408,7 +408,7 @@
         out_shape=(partial_sums, partial_sums),
         in_specs=in_vmem(5),
         out_specs=tuple(in_vmem(2)),
-        compiler_params=pltpu.CompilerParams(vmem_limit_bytes=8 * MIB),
+        compiler_params=pltpu.CompilerParams(vmem_limit_bytes=4 * MIB),
         cost_estimate=no_cost,
     )(normed, doc_rows, cosine, sine, own_weight)
     scale = 1.0 / math.sqrt(size)

time: 61.9 us -> 61.9 us (level)
  no operation moved by 1% of the time
where the time goes in v18:
time: 61.9 us; the launch traced here: 60.8 us
  waiting for transfers between devices  17.7 us (29%)
  starting transfers between devices  17.3 us (28%)
  Pallas kernels  9.75 us (16%)
  local copies, waits for them, and re-layouts  8.47 us (14%)
  other arithmetic  7.32 us (12%)
    ppermute x4, waiting for transfers between devices, by_row(): return lax.ppermute(value, 'row', [(0, 1), (1, 0)])  9.42 us
    unnamed x15, local copies, waits for them, and re-layouts  8.03 us
    ppermute x5, waiting for transfers between devices, along_tok(): return lax.ppermute(value, 'tok', pairs)  7.29 us
    ppermute x4, starting transfers between devices, by_row(): return lax.ppermute(value, 'row', [(0, 1), (1, 0)])  5.94 us
    ppermute x5, starting transfers between devices, along_tok(): return lax.ppermute(value, 'tok', pairs)  5.43 us
    ppermute x1, starting transfers between devices, per_device(): lax.ppermute(activations, ('row', 'col'), [(r * 4 + c, c // 2 * 4 + 2 * (...  3.31 us
    pallas_call x1, Pallas kernels, per_device(): pl.pallas_call(normalise_project_kernel, out_shape=(partial_sums, jax.Sha...  2.31 us
    pallas_call x1, Pallas kernels, per_device(): on_place(lambda *refs: own_block_kernel(scale, *refs), part_shapes, 2)  1.85 us
  transfers between devices with their start and end apart: 16, of which 10 were waited for; matrix products, arithmetic and copies ran while one was open for 17% of the time, Pallas kernels for 10%

profile of v18, /device:TPU:24, one launch (start us, length us, event | category | flops | bytes accessed | tf_op | source)
XLA Modules:
  0.0 60.8 jit_solution(10913436469000626527)
XLA Ops:
  0.0 1.6 %collective-permute-start = (bf16[176,1024]{1,0:T(8,128)(2,1)}, bf16[176,1024]{1,0:T(8,128)(2,1)S(1)}, u32[]{:S(2)}, u32[]{:S(2)}) collective-permute-start(bf16[176,1024]{1,0:T(8,128)(2,1)} %param.4), channel_id=1, source_target_pairs={{0,0},{1,1},{2,4},{3,5},{4,2},{5,3},{6,6},{7,7},{8,8},{9,9},{10,12... | collective-permute-start | bytes 1081352 | tf_op jit(solution)/shard_map/ppermute | solution.py:343
  1.6 3.3 %collective-permute-start.1 = (bf16[176,1024]{1,0:T(8,128)(2,1)}, bf16[176,1024]{1,0:T(8,128)(2,1)S(1)}, u32[]{:S(2)}, u32[]{:S(2)}) collective-permute-start(bf16[176,1024]{1,0:T(8,128)(2,1)} %param.4), channel_id=1, source_target_pairs={{0,2},{1,3},{2,6},{3,7},{4,0},{5,1},{6,4},{7,5},{8,10},{9,11},{10,... | collective-permute-start | bytes 1081352 | tf_op jit(solution)/shard_map/ppermute | solution.py:348
  4.9 1.2 %multiply_reduce_fusion = f32[176]{0:T(256)S(1)} fusion(bf16[176,1024]{1,0:T(8,128)(2,1)} %param.4), kind=kLoop, calls=%fused_computation | loop fusion | flops 540496 | bytes 361152 | tf_op jit(solution)/shard_map/reduce_sum | solution.py:354
  6.1 0.7 %convert_element_type.61 = f32[1024]{0:T(1024)S(1)} convert(bf16[1024]{0:T(1024)(128)(2,1)} %param.5) | non-fusion elementwise | flops 1024 | bytes 6144 | tf_op jit(solution)/shard_map/convert_element_type | solution.py:355
  6.9 0.7 %convert_add_fusion = f32[176]{0:T(256)S(1)} fusion(s32[176]{0:T(256)} %param.7), kind=kLoop, calls=%fused_computation.28 | loop fusion | flops 352 | bytes 1408 | tf_op jit(solution)/shard_map/add | solution.py:367
  7.6 0.5 collective-permute-done.2
  8.0 0.8 %slice_select_fusion = (f32[1024]{0:T(1024)S(1)}, f32[1024]{0:T(1024)S(1)}) fusion(f32[1200]{0:T(1024)S(1)} %collective-permute-done.2, bf16[1024]{0:T(1024)(128)(2,1)} %param.5, pred[]{:T(512)S(6)} %eq.22), kind=kLoop, calls=%fused_computation.18 | loop fusion | flops 3072 | bytes 14337 | tf_op jit(solution)/shard_map/jit(_where)/select_n | solution.py:341
  8.9 0.1 pad_add_fusion.1.place_ref
  9.0 4.0 %copy.6 = bf16[256,8,4,384]{3,1,2,0:T(8,128)(2,1)S(1)} copy(bf16[256,8,4,384]{3,2,1,0:T(4,128)(2,1)} %bitcast.25) | data formatting | bytes 12582912
  12.9 0.5 collective-permute-done.3
  13.7 1.8 %collective-permute-start.6 = (f32[352]{0:T(512)S(1)}, f32[352]{0:T(512)S(1)}, u32[]{:S(2)}, u32[]{:S(2)}) collective-permute-start(f32[352]{0:T(512)S(1)} %pad_maximum_fusion.4), channel_id=1, source_target_pairs={{0,4},{4,0},{1,5},{5,1},{2,6},{6,2},{3,7},{7,3},{8,12},{12,8},{9,1... | collective-permute-start | bytes 4232 | tf_op jit(solution)/shard_map/ppermute | solution.py:337
  15.5 0.2 collective-permute-start.5
  15.7 0.7 %fusion = (f32[352,64]{1,0:T(8,128)S(1)}, f32[352,64]{1,0:T(8,128)S(1)}, f32[352,64]{1,0:T(8,128)S(1)}) fusion(f32[64]{0:T(128)S(1)} %fusion.2, f32[352]{0:T(512)S(1)} %add_convert_fusion.2), kind=kLoop, calls=%fused_computation.12 | loop fusion | flops 45056 | bytes 272000 | tf_op jit(solution)/shard_map/neg | solution.py:26
  16.5 0.2 pad_maximum_fusion
  16.6 0.7 %collective-permute-done.6 = f32[352]{0:T(512)S(1)} collective-permute-done((f32[352]{0:T(512)S(1)}, f32[352]{0:T(512)S(1)}, u32[]{:S(2)}, u32[]{:S(2)}) %collective-permute-start.6) | collective-permute-done | bytes 1440 | tf_op jit(solution)/shard_map/ppermute | solution.py:337
  17.5 0.1 reshape.71.squares_ref
  17.6 1.0 %copy-done.3 = bf16[176,1024]{1,0:T(8,128)(2,1)S(1)} copy-done((bf16[176,1024]{1,0:T(8,128)(2,1)S(1)}, bf16[176,1024]{1,0:T(8,128)(2,1)}, u32[]{:S(2)}) %copy-start.3) | copy-done | bytes 360472
  18.6 1.0 %copy-done.5 = bf16[176,1024]{1,0:T(8,128)(2,1)S(1)} copy-done((bf16[176,1024]{1,0:T(8,128)(2,1)S(1)}, bf16[176,1024]{1,0:T(8,128)(2,1)}, u32[]{:S(2)}) %copy-start.5) | copy-done | bytes 360472
  19.6 2.3 %shard_map.46 = (f32[1088,128]{1,0:T(8,128)S(1)}, bf16[2,352,1024]{2,1,0:T(8,128)(2,1)S(1)}, bf16[2048,384]{1,0:T(8,128)(2,1)S(1)}, bf16[2048,768]{1,0:T(8,128)(2,1)S(1)}) custom-call(s32[4]{0:T(128)S(1)} %pad_add_fusion.1.place_ref, bf16[176,1024]{1,0:T(8,128)(2,1)S(1)} %copy-done.3, bf16[176,1024]{1,0:T(8,128)(2,1)S(1)} %copy-done.5, ...), custom_call_target="tpu_custom_call" | custom-call | tf_op jit(solution)/shard_map/pallas_call | solution.py:381
  21.9 1.6 %copy-done = bf16[2048,768]{1,0:T(8,128)(2,1)} copy-done((bf16[2048,768]{1,0:T(8,128)(2,1)}, bf16[2048,768]{1,0:T(8,128)(2,1)S(1)}, u32[]{:S(2)}) %copy-start) | copy-done | bytes 3145752
  23.5 0.7 %convert_element_type.66 = f16[1088,128]{1,0:T(8,128)(2,1)} convert(f32[1088,128]{1,0:T(8,128)S(1)} %get-tuple-element.32) | non-fusion elementwise | flops 139264 | bytes 835584 | tf_op jit(solution)/shard_map/convert_element_type | solution.py:405
  24.3 1.8 %collective-permute-start.7 = (f16[1088,128]{1,0:T(8,128)(2,1)}, f16[1088,128]{1,0:T(8,128)(2,1)}, u32[]{:S(2)}, u32[]{:S(2)}) collective-permute-start(f16[1088,128]{1,0:T(8,128)(2,1)} %convert_element_type.66), channel_id=1, source_target_pairs={{0,4},{4,0},{1,5},{5,1},{2,6},{6,2},{3,7},{7,3},{8,12},{12,8},{9,1... | collective-permute-start | bytes 835592 | tf_op jit(solution)/shard_map/ppermute | solution.py:337
  26.1 1.0 %shard_map.48 = f32[1088,128]{1,0:T(8,128)S(1)} custom-call(bf16[2,352,1024]{2,1,0:T(8,128)(2,1)S(1)} %get-tuple-element.29.normed_ref, f32[352,128]{1,0:T(8,128)S(1)} %get-tuple-element.58.cos_ref, f32[352,128]{1,0:T(8,128)S(1)} %get-tuple-element.59.sin_ref, bf16[2048,384]{1,0:T(8,128)(2,1)S(1)} %get-tuple-element.34.weight_ref), custom_call_target="tpu_custom_call" | custom-call | tf_op jit(solution)/shard_map/pallas_call | solution.py:397
  27.2 0.3 collective-permute-start.8
  27.5 0.5 copy-done.1
  27.9 1.7 %shard_map.47 = (f32[1088,128]{1,0:T(8,128)S(1)}, f32[1088,128]{1,0:T(8,128)S(1)}) custom-call(bf16[2,352,1024]{2,1,0:T(8,128)(2,1)S(1)} %get-tuple-element.29.normed_ref, f32[16,128]{1,0:T(8,128)S(1)} %fusion.1.docs_ref, f32[352,128]{1,0:T(8,128)S(1)} %get-tuple-element.58.cos_ref, f32[352,128]{1,0:T(8,128)S(1)} %get-tuple-element.59.sin_ref, ...), custom_call_target="tpu_custom_call" | custom-call | tf_op jit(solution)/shard_map/pallas_call | solution.py:406
  29.7 4.5 %collective-permute-done.7 = f16[1088,128]{1,0:T(8,128)(2,1)} collective-permute-done((f16[1088,128]{1,0:T(8,128)(2,1)}, f16[1088,128]{1,0:T(8,128)(2,1)}, u32[]{:S(2)}, u32[]{:S(2)}) %collective-permute-start.7) | collective-permute-done | bytes 278560 | tf_op jit(solution)/shard_map/ppermute | solution.py:337
  34.1 1.0 %add_convert_fusion.1.refs_1_.refs_4_.refs_3_ = bf16[1088,128]{1,0:T(8,128)(2,1)S(1)} fusion(f32[1088,128]{1,0:T(8,128)S(1)} %get-tuple-element.31, f16[1088,128]{1,0:T(8,128)(2,1)} %collective-permute-done.7), kind=kLoop, calls=%fused_computation.2 | loop fusion | flops 417792 | bytes 1114112 | tf_op jit(solution)/shard_map/convert_element_type | solution.py:417
  35.2 0.7 %collective-permute-start.9 = (bf16[16,128]{1,0:T(8,128)(2,1)S(1)}, bf16[16,128]{1,0:T(8,128)(2,1)S(1)}, u32[]{:S(2)}, u32[]{:S(2)}) collective-permute-start(bf16[16,128]{1,0:T(8,128)(2,1)S(1)} %slice.49), channel_id=1, source_target_pairs={{2,3}} | collective-permute-start | bytes 12296 | tf_op jit(solution)/shard_map/ppermute | solution.py:458
  35.9 0.1 constant_dynamic-slice_fusion.1
  36.0 0.4 collective-permute-start.10
  36.4 0.7 %collective-permute-start.11 = (bf16[720,128]{1,0:T(8,128)(2,1)S(1)}, bf16[720,128]{1,0:T(8,128)(2,1)S(1)}, u32[]{:S(2)}, u32[]{:S(2)}) collective-permute-start(bf16[720,128]{1,0:T(8,128)(2,1)S(1)} %get-tuple-element.41), channel_id=1, source_target_pairs={{8,16},{16,8},{0,0},{24,24},{9,17},{17,9},{1,1},{25,25},{10,18},{1... | collective-permute-start | bytes 552968 | tf_op jit(solution)/shard_map/ppermute | solution.py:437
  37.1 1.8 %collective-permute-done.8 = f16[1088,128]{1,0:T(8,128)(2,1)S(1)} collective-permute-done((f16[1088,128]{1,0:T(8,128)(2,1)S(1)}, f16[1088,128]{1,0:T(8,128)(2,1)S(1)}, u32[]{:S(2)}, u32[]{:S(2)}) %collective-permute-start.8) | collective-permute-done | bytes 278560 | tf_op jit(solution)/shard_map/ppermute | solution.py:337
  38.8 0.1 add_convert_fusion.refs_2_.refs_5_.refs_4_
  39.0 1.3 %collective-permute-start.12 = (bf16[720,128]{1,0:T(8,128)(2,1)S(1)}, bf16[720,128]{1,0:T(8,128)(2,1)S(1)}, u32[]{:S(2)}, u32[]{:S(2)}) collective-permute-start(bf16[720,128]{1,0:T(8,128)(2,1)S(1)} %constant_dynamic-slice_fusion), channel_id=1, source_target_pairs={{0,8},{8,0},{16,24},{24,16},{1,9},{9,1},{17,25},{25,17},{2,10},{10... | collective-permute-start | bytes 552968 | tf_op jit(solution)/shard_map/ppermute | solution.py:437
  40.3 1.8 %shard_map.49 = (f32[2,352,128]{2,1,0:T(8,128)S(1)}, f32[2,352,1]{2,1,0:T(8,128)S(1)}) custom-call(s32[2]{0:T(128)S(1)} %pad_add_fusion.refs_0_.place_ref, bf16[1088,128]{1,0:T(8,128)(2,1)S(1)} %add_convert_fusion.1.refs_1_.refs_4_.refs_3_, bf16[1088,128]{1,0:T(8,128)(2,1)S(1)} %add_convert_fusion.refs_2_.refs_5_.refs_4_), custom_call_target="tpu_custom_call" | custom-call | tf_op jit(solution)/shard_map/pallas_call | solution.py:472
  42.2 0.4 collective-permute-done.10.refs_1_.refs_5_
  42.6 2.9 %collective-permute-done.12.refs_3_.refs_7_ = bf16[720,128]{1,0:T(8,128)(2,1)S(1)} collective-permute-done((bf16[720,128]{1,0:T(8,128)(2,1)S(1)}, bf16[720,128]{1,0:T(8,128)(2,1)S(1)}, u32[]{:S(2)}, u32[]{:S(2)}) %collective-permute-start.12) | collective-permute-done | bytes 184352 | tf_op jit(solution)/shard_map/ppermute | solution.py:437
  45.5 0.6 shard_map.50.refs_8_
  46.1 1.8 %collective-permute-start.13 = (bf16[368,128]{1,0:T(8,128)(2,1)S(1)}, bf16[368,128]{1,0:T(8,128)(2,1)S(1)}, u32[]{:S(2)}, u32[]{:S(2)}) collective-permute-start(bf16[368,128]{1,0:T(8,128)(2,1)S(1)} %get-tuple-element.44), channel_id=1, source_target_pairs={{0,8},{8,24},{16,0},{24,16},{1,9},{9,25},{17,1},{25,17},{2,10},{10... | collective-permute-start | bytes 282632 | tf_op jit(solution)/shard_map/ppermute | solution.py:437
  48.0 1.3 %collective-permute-start.14 = (bf16[368,128]{1,0:T(8,128)(2,1)S(1)}, bf16[368,128]{1,0:T(8,128)(2,1)S(1)}, u32[]{:S(2)}, u32[]{:S(2)}) collective-permute-start(bf16[368,128]{1,0:T(8,128)(2,1)S(1)} %get-tuple-element.43), channel_id=1, source_target_pairs={{8,16},{16,24},{9,17},{17,25},{10,18},{18,26},{11,19},{19,27},{12,... | collective-permute-start | bytes 282632 | tf_op jit(solution)/shard_map/ppermute | solution.py:437
  49.2 1.2 %shard_map.51 = (f32[2,352,128]{2,1,0:T(8,128)S(1)}, f32[2,352,1]{2,1,0:T(8,128)S(1)}) custom-call(s32[2]{0:T(128)S(1)} %pad_add_fusion.refs_0_.place_ref, f32[2,352,128]{2,1,0:T(8,128)S(1)} %get-tuple-element.35.refs_1_, f32[2,352,1]{2,1,0:T(8,128)S(1)} %get-tuple-element.36.refs_6_.refs_2_, ...), custom_call_target="tpu_custom_call" | custom-call | tf_op jit(solution)/shard_map/pallas_call | solution.py:483
  50.5 1.6 %collective-permute-done.13.first_ref = bf16[368,128]{1,0:T(8,128)(2,1)S(1)} collective-permute-done((bf16[368,128]{1,0:T(8,128)(2,1)S(1)}, bf16[368,128]{1,0:T(8,128)(2,1)S(1)}, u32[]{:S(2)}, u32[]{:S(2)}) %collective-permute-start.13) | collective-permute-done | bytes 94240 | tf_op jit(solution)/shard_map/ppermute | solution.py:437
  52.1 2.3 %collective-permute-done.14.below_ref = bf16[368,128]{1,0:T(8,128)(2,1)S(1)} collective-permute-done((bf16[368,128]{1,0:T(8,128)(2,1)S(1)}, bf16[368,128]{1,0:T(8,128)(2,1)S(1)}, u32[]{:S(2)}, u32[]{:S(2)}) %collective-permute-start.14) | collective-permute-done | bytes 94240 | tf_op jit(solution)/shard_map/ppermute | solution.py:437
  54.4 1.1 %shard_map.52 = (bf16[176,256]{1,0:T(8,128)(2,1)S(1)}, bf16[176,256]{1,0:T(8,128)(2,1)S(1)}) custom-call(s32[2]{0:T(128)S(1)} %pad_add_fusion.refs_0_.place_ref, f32[2,352,128]{2,1,0:T(8,128)S(1)} %get-tuple-element.37.out_ref, f32[2,352,1]{2,1,0:T(8,128)S(1)} %get-tuple-element.38.logs_ref, bf16[368,128]{1,0:T(8,128)(2,1)S(1)} %collective-permute-done.13.first_ref, ...), custom_call_target="tpu_custom_call" | custom-call | tf_op jit(solution)/shard_map/pallas_call | solution.py:487
  55.5 2.1 %collective-permute-start.15 = (bf16[176,256]{1,0:T(8,128)(2,1)S(1)}, bf16[176,256]{1,0:T(8,128)(2,1)S(1)}, u32[]{:S(2)}, u32[]{:S(2)}) collective-permute-start(bf16[176,256]{1,0:T(8,128)(2,1)S(1)} %get-tuple-element.40), channel_id=1, source_target_pairs={{0,4},{4,0},{1,5},{5,1},{2,6},{6,2},{3,7},{7,3},{8,12},{12,8},{9,1... | collective-permute-start | bytes 270344 | tf_op jit(solution)/shard_map/ppermute | solution.py:337
  57.6 2.5 %collective-permute-done.15 = bf16[176,256]{1,0:T(8,128)(2,1)S(1)} collective-permute-done((bf16[176,256]{1,0:T(8,128)(2,1)S(1)}, bf16[176,256]{1,0:T(8,128)(2,1)S(1)}, u32[]{:S(2)}, u32[]{:S(2)}) %collective-permute-start.15) | collective-permute-done | bytes 90144 | tf_op jit(solution)/shard_map/ppermute | solution.py:337
  60.1 0.7 %pad_maximum_fusion.2 = bf16[176,512]{1,0:T(8,128)(2,1)} fusion(bf16[176,256]{1,0:T(8,128)(2,1)S(1)} %get-tuple-element.46, bf16[176,256]{1,0:T(8,128)(2,1)S(1)} %get-tuple-element.45), kind=kLoop, calls=%fused_computation.7 | loop fusion | flops 360448 | bytes 360448 | tf_op jit(solution)/shard_map/concatenate | solution.py:493
  (38 shorter events, 0.9 us)
Async XLA Ops:
  0.0 13.5 %collective-permute-start = (bf16[176,1024]{1,0:T(8,128)(2,1)}, bf16[176,1024]{1,0:T(8,128)(2,1)S(1)}, u32[]{:S(2)}, u32[]{:S(2)}) collective-permute-start(bf16[176,1024]{1,0:T(8,128)(2,1)} %param.4), channel_id=1, source_target_pairs={{0,0},{1,1},{2,4},{3,5},{4,2},{5,3},{6,6},{7,7},{8,8},{9,9},{10,12... | collective-permute-start | bytes 1081352 | tf_op jit(solution)/shard_map/ppermute | solution.py:343
  1.6 11.8 %collective-permute-start.1 = (bf16[176,1024]{1,0:T(8,128)(2,1)}, bf16[176,1024]{1,0:T(8,128)(2,1)S(1)}, u32[]{:S(2)}, u32[]{:S(2)}) collective-permute-start(bf16[176,1024]{1,0:T(8,128)(2,1)} %param.4), channel_id=1, source_target_pairs={{0,2},{1,3},{2,6},{3,7},{4,0},{5,1},{6,4},{7,5},{8,10},{9,11},{10,... | collective-permute-start | bytes 1081352 | tf_op jit(solution)/shard_map/ppermute | solution.py:348
  6.9 1.2 %collective-permute-start.2 = (f32[1200]{0:T(1024)S(1)}, f32[1200]{0:T(1024)S(1)}, u32[]{:S(2)}, u32[]{:S(2)}) collective-permute-start(f32[1200]{0:T(1024)S(1)} %pad_maximum_fusion.3), channel_id=1, source_target_pairs={{0,1},{1,0},{2,3},{3,2},{4,5},{5,4},{6,7},{7,6},{8,9},{9,8},{10,11... | collective-permute-start | bytes 14408 | tf_op jit(solution)/shard_map/ppermute | solution.py:334
  8.9 4.6 %collective-permute-start.3 = (f32[2224]{0:T(1024)S(1)}, f32[2224]{0:T(1024)S(1)}, u32[]{:S(2)}, u32[]{:S(2)}) collective-permute-start(f32[2224]{0:T(1024)S(1)} %concatenate.40), channel_id=1, source_target_pairs={{0,2},{1,3},{2,0},{3,1},{4,6},{5,7},{6,4},{7,5},{8,10},{9,11},{10,... | collective-permute-start | bytes 26696 | tf_op jit(solution)/shard_map/ppermute | solution.py:334
  9.0 8.3 %copy-start.6 = (s32[176]{0:T(256)S(1)}, s32[176]{0:T(256)}, u32[]{:S(2)}) copy-start(s32[176]{0:T(256)} %param.7) | copy-start | bytes 2116
  13.5 4.1 %copy-start.2 = (bf16[176,1024]{1,0:T(8,128)(2,1)}, bf16[176,1024]{1,0:T(8,128)(2,1)S(1)}, u32[]{:S(2)}) copy-start(bf16[176,1024]{1,0:T(8,128)(2,1)S(1)} %collective-permute-done.a_near) | copy-start | bytes 1081348
  13.5 4.1 %copy-start.4 = (bf16[176,1024]{1,0:T(8,128)(2,1)}, bf16[176,1024]{1,0:T(8,128)(2,1)S(1)}, u32[]{:S(2)}) copy-start(bf16[176,1024]{1,0:T(8,128)(2,1)S(1)} %collective-permute-done.1.a_far) | copy-start | bytes 1081348
  13.6 4.0 %collective-permute-start.4 = (bf16[176,1024]{1,0:T(8,128)(2,1)S(1)}, bf16[176,1024]{1,0:T(8,128)(2,1)S(1)}, u32[]{:S(2)}, u32[]{:S(2)}) collective-permute-start(bf16[176,1024]{1,0:T(8,128)(2,1)S(1)} %collective-permute-done.a_near), channel_id=1, source_target_pairs={{0,1},{1,0},{2,3},{3,2},{4,5},{5,4},{6,7},{7,6},{8,9},{9,8},{10,11... | collective-permute-start | bytes 1081352 | tf_op jit(solution)/shard_map/ppermute | solution.py:334
  13.7 3.6 %collective-permute-start.6 = (f32[352]{0:T(512)S(1)}, f32[352]{0:T(512)S(1)}, u32[]{:S(2)}, u32[]{:S(2)}) collective-permute-start(f32[352]{0:T(512)S(1)} %pad_maximum_fusion.4), channel_id=1, source_target_pairs={{0,4},{4,0},{1,5},{5,1},{2,6},{6,2},{3,7},{7,3},{8,12},{12,8},{9,1... | collective-permute-start | bytes 4232 | tf_op jit(solution)/shard_map/ppermute | solution.py:337
  15.5 2.1 %collective-permute-start.5 = (bf16[176,1024]{1,0:T(8,128)(2,1)S(1)}, bf16[176,1024]{1,0:T(8,128)(2,1)S(1)}, u32[]{:S(2)}, u32[]{:S(2)}) collective-permute-start(bf16[176,1024]{1,0:T(8,128)(2,1)S(1)} %collective-permute-done.1.a_far), channel_id=1, source_target_pairs={{0,1},{1,0},{2,3},{3,2},{4,5},{5,4},{6,7},{7,6},{8,9},{9,8},{10,11... | collective-permute-start | bytes 1081352 | tf_op jit(solution)/shard_map/ppermute | solution.py:334
  17.6 1.0 %copy-start.3 = (bf16[176,1024]{1,0:T(8,128)(2,1)S(1)}, bf16[176,1024]{1,0:T(8,128)(2,1)}, u32[]{:S(2)}) copy-start(bf16[176,1024]{1,0:T(8,128)(2,1)} %copy-done.2) | copy-start | bytes 1081348
  18.6 1.0 %copy-start.5 = (bf16[176,1024]{1,0:T(8,128)(2,1)S(1)}, bf16[176,1024]{1,0:T(8,128)(2,1)}, u32[]{:S(2)}) copy-start(bf16[176,1024]{1,0:T(8,128)(2,1)} %copy-done.4) | copy-start | bytes 1081348
  21.9 1.6 %copy-start = (bf16[2048,768]{1,0:T(8,128)(2,1)}, bf16[2048,768]{1,0:T(8,128)(2,1)S(1)}, u32[]{:S(2)}) copy-start(bf16[2048,768]{1,0:T(8,128)(2,1)S(1)} %get-tuple-element.30.weight_ref) | copy-start | bytes 9437188
  24.3 9.9 %collective-permute-start.7 = (f16[1088,128]{1,0:T(8,128)(2,1)}, f16[1088,128]{1,0:T(8,128)(2,1)}, u32[]{:S(2)}, u32[]{:S(2)}) collective-permute-start(f16[1088,128]{1,0:T(8,128)(2,1)} %convert_element_type.66), channel_id=1, source_target_pairs={{0,4},{4,0},{1,5},{5,1},{2,6},{6,2},{3,7},{7,3},{8,12},{12,8},{9,1... | collective-permute-start | bytes 835592 | tf_op jit(solution)/shard_map/ppermute | solution.py:337
  26.0 1.9 %copy-start.1 = (bf16[2048,768]{1,0:T(8,128)(2,1)S(1)}, bf16[2048,768]{1,0:T(8,128)(2,1)}, u32[]{:S(2)}) copy-start(bf16[2048,768]{1,0:T(8,128)(2,1)} %copy-done) | copy-start | bytes 9437188
  27.2 11.7 %collective-permute-start.8 = (f16[1088,128]{1,0:T(8,128)(2,1)S(1)}, f16[1088,128]{1,0:T(8,128)(2,1)S(1)}, u32[]{:S(2)}, u32[]{:S(2)}) collective-permute-start(f16[1088,128]{1,0:T(8,128)(2,1)S(1)} %convert_element_type.69), channel_id=1, source_target_pairs={{0,4},{4,0},{1,5},{5,1},{2,6},{6,2},{3,7},{7,3},{8,12},{12,8},{9,1... | collective-permute-start | bytes 835592 | tf_op jit(solution)/shard_map/ppermute | solution.py:337
  35.2 1.9 %collective-permute-start.9 = (bf16[16,128]{1,0:T(8,128)(2,1)S(1)}, bf16[16,128]{1,0:T(8,128)(2,1)S(1)}, u32[]{:S(2)}, u32[]{:S(2)}) collective-permute-start(bf16[16,128]{1,0:T(8,128)(2,1)S(1)} %slice.49), channel_id=1, source_target_pairs={{2,3}} | collective-permute-start | bytes 12296 | tf_op jit(solution)/shard_map/ppermute | solution.py:458
  36.0 6.6 %collective-permute-start.10 = (bf16[720,128]{1,0:T(8,128)(2,1)S(1)}, bf16[720,128]{1,0:T(8,128)(2,1)S(1)}, u32[]{:S(2)}, u32[]{:S(2)}) collective-permute-start(bf16[720,128]{1,0:T(8,128)(2,1)S(1)} %get-tuple-element.42), channel_id=1, source_target_pairs={{0,16},{24,8},{8,0},{16,24},{1,17},{25,9},{9,1},{17,25},{2,18},{26... | collective-permute-start | bytes 552968 | tf_op jit(solution)/shard_map/ppermute | solution.py:437
  36.4 6.2 %collective-permute-start.11 = (bf16[720,128]{1,0:T(8,128)(2,1)S(1)}, bf16[720,128]{1,0:T(8,128)(2,1)S(1)}, u32[]{:S(2)}, u32[]{:S(2)}) collective-permute-start(bf16[720,128]{1,0:T(8,128)(2,1)S(1)} %get-tuple-element.41), channel_id=1, source_target_pairs={{8,16},{16,8},{0,0},{24,24},{9,17},{17,9},{1,1},{25,25},{10,18},{1... | collective-permute-start | bytes 552968 | tf_op jit(solution)/shard_map/ppermute | solution.py:437
  39.0 6.5 %collective-permute-start.12 = (bf16[720,128]{1,0:T(8,128)(2,1)S(1)}, bf16[720,128]{1,0:T(8,128)(2,1)S(1)}, u32[]{:S(2)}, u32[]{:S(2)}) collective-permute-start(bf16[720,128]{1,0:T(8,128)(2,1)S(1)} %constant_dynamic-slice_fusion), channel_id=1, source_target_pairs={{0,8},{8,0},{16,24},{24,16},{1,9},{9,1},{17,25},{25,17},{2,10},{10... | collective-permute-start | bytes 552968 | tf_op jit(solution)/shard_map/ppermute | solution.py:437
  46.1 6.0 %collective-permute-start.13 = (bf16[368,128]{1,0:T(8,128)(2,1)S(1)}, bf16[368,128]{1,0:T(8,128)(2,1)S(1)}, u32[]{:S(2)}, u32[]{:S(2)}) collective-permute-start(bf16[368,128]{1,0:T(8,128)(2,1)S(1)} %get-tuple-element.44), channel_id=1, source_target_pairs={{0,8},{8,24},{16,0},{24,16},{1,9},{9,25},{17,1},{25,17},{2,10},{10... | collective-permute-start | bytes 282632 | tf_op jit(solution)/shard_map/ppermute | solution.py:437
  48.0 6.5 %collective-permute-start.14 = (bf16[368,128]{1,0:T(8,128)(2,1)S(1)}, bf16[368,128]{1,0:T(8,128)(2,1)S(1)}, u32[]{:S(2)}, u32[]{:S(2)}) collective-permute-start(bf16[368,128]{1,0:T(8,128)(2,1)S(1)} %get-tuple-element.43), channel_id=1, source_target_pairs={{8,16},{16,24},{9,17},{17,25},{10,18},{18,26},{11,19},{19,27},{12,... | collective-permute-start | bytes 282632 | tf_op jit(solution)/shard_map/ppermute | solution.py:437
  55.5 4.6 %collective-permute-start.15 = (bf16[176,256]{1,0:T(8,128)(2,1)S(1)}, bf16[176,256]{1,0:T(8,128)(2,1)S(1)}, u32[]{:S(2)}, u32[]{:S(2)}) collective-permute-start(bf16[176,256]{1,0:T(8,128)(2,1)S(1)} %get-tuple-element.40), channel_id=1, source_target_pairs={{0,4},{4,0},{1,5},{5,1},{2,6},{6,2},{3,7},{7,3},{8,12},{12,8},{9,1... | collective-permute-start | bytes 270344 | tf_op jit(solution)/shard_map/ppermute | solution.py:337

commit v19 on v14

--- a/solution.py
+++ b/solution.py
@@ -61,7 +61,7 @@
     )
     copy.start()
     for shards, half in (((a_near, a_far), core), ((b_near, b_far), 1 - core)):
-        gain = gain_ref[half]
+        gain = gain_ref[half].astype(jnp.float32)
         for shard, row in zip(shards, (near_row, 1 - near_row)):
             at = pl.ds(pl.multiple_of(row * rows, 16), rows)
             factor = lax.rsqrt(squares_ref[at, :] / features + EPS)
@@ -342,18 +342,17 @@
     )
     widened = activations.astype(jnp.float32)
     squares = jnp.sum(widened * widened, axis=1)
-    gain = norm_gain.astype(jnp.float32)
-    message = jnp.concatenate([squares, gain])
+    gain = ordered(core, norm_gain, by_col(norm_gain, 1))
+    gain = jnp.where(chip == row, gain, by_col(gain, 2)).reshape(2, 1, width)
+    message = squares
     message, qkv_weight = lax.optimization_barrier((message, qkv_weight))
     flat_weight = qkv_weight.reshape(span, local_heads * triple)
     got = by_col(message, 1)
-    squares = squares + got[:rows]
-    gain = ordered(core, gain, got[rows:])
-    by_chip = by_col(jnp.concatenate([squares, gain]), 2)
+    squares = squares + got
+    by_chip = by_col(squares, 2)
     near, far, by_chip, flat_weight = lax.optimization_barrier((near, far, by_chip, flat_weight))
     near_other, far_other = by_col(near, 1), by_col(far, 1)
-    squares = squares + by_chip[:rows]
-    gain = jnp.where(chip == row, gain, by_chip[rows:]).reshape(2, 1, width)
+    squares = squares + by_chip
     codes = doc_ids.astype(jnp.float32) + 1.0
     got = by_row(jnp.concatenate([squares, codes]))
     squares = ordered(row, squares, got[:rows]).reshape(block, 1)

time: 56.6 us -> 64.8 us (1.14)
  local copies, waits for them, and re-layouts: 4.41 us -> 9.69 us
  starting transfers between devices: 16.5 us -> 19.1 us
  waiting for transfers between devices: 17.9 us -> 19.1 us
  other arithmetic: 5.65 us -> 4.83 us
    unnamed x3 -> x5, local copies, waits for them, and re-layouts: 3.97 us -> 9.39 us
    ppermute x4 -> x6, starting transfers between devices: 0.27 us -> 2.86 us  [by_col(): return lax.ppermute(value, 'col', [(c, c ^ flip) for c in range(4)])]
    ppermute x4 -> x6, waiting for transfers between devices: 0.99 us -> 1.88 us  [by_col(): return lax.ppermute(value, 'col', [(c, c ^ flip) for c in range(4)])]
    select_n x2 -> x1, other arithmetic: 0.77 us -> 0.01 us  [per_device(): gain = jnp.where(chip == row, gain, by_col(gain, 2)).reshape(2, 1, width)]
    select_n x1 -> x2, other arithmetic: 0.07 us -> 0.76 us  [ordered(): jnp.where(first, own, other)]
    convert_element_type x1 -> x0, other arithmetic: 0.69 us -> none  [per_device(): gain = norm_gain.astype(jnp.float32)]
  transfers between devices with their start and end apart: 16 -> 18, of which waited for: 9 -> 9; matrix products, arithmetic and copies ran while one was open for 17% -> 17% of each run, Pallas kernels for 12% -> 11%
where the time goes in v19:
time: 64.8 us; the launch traced here: 64 us
  starting transfers between devices  19.1 us (29%)
  waiting for transfers between devices  19.1 us (29%)
  Pallas kernels  11 us (17%)
  local copies, waits for them, and re-layouts  9.69 us (15%)
  other arithmetic  4.83 us (7%)
    ppermute x4, waiting for transfers between devices, by_row(): return lax.ppermute(value, 'row', [(0, 1), (1, 0)])  9.99 us
    unnamed x5, local copies, waits for them, and re-layouts  9.39 us
    ppermute x5, waiting for transfers between devices, along_tok(): return lax.ppermute(value, 'tok', pairs)  7.23 us
    ppermute x4, starting transfers between devices, by_row(): return lax.ppermute(value, 'row', [(0, 1), (1, 0)])  5.98 us
    ppermute x5, starting transfers between devices, along_tok(): return lax.ppermute(value, 'tok', pairs)  4.68 us
    pallas_call x1, Pallas kernels, per_device(): pl.pallas_call(project_kernel, out_shape=(partial_sums, partial_sums), in...  3.65 us
    ppermute x1, starting transfers between devices, per_device(): lax.ppermute(activations, ('row', 'col'), [(r * 4 + c, c // 2 * 4 + 2 * (...  3.31 us
    ppermute x6, starting transfers between devices, by_col(): return lax.ppermute(value, 'col', [(c, c ^ flip) for c in range(4)])  2.86 us
  transfers between devices with their start and end apart: 18, of which 9 were waited for; matrix products, arithmetic and copies ran while one was open for 17% of the time, Pallas kernels for 11%

profile of v19, /device:TPU:24, one launch (start us, length us, event | category | flops | bytes accessed | tf_op | source)
XLA Modules:
  0.0 64.0 jit_solution(13453787497918865260)
XLA Ops:
  0.0 1.6 %collective-permute-start = (bf16[176,1024]{1,0:T(8,128)(2,1)}, bf16[176,1024]{1,0:T(8,128)(2,1)S(1)}, u32[]{:S(2)}, u32[]{:S(2)}) collective-permute-start(bf16[176,1024]{1,0:T(8,128)(2,1)} %param.4), channel_id=1, source_target_pairs={{0,0},{1,1},{2,4},{3,5},{4,2},{5,3},{6,6},{7,7},{8,8},{9,9},{10,12... | collective-permute-start | bytes 1081352 | tf_op jit(solution)/shard_map/ppermute | solution.py:333
  1.6 3.3 %collective-permute-start.1 = (bf16[176,1024]{1,0:T(8,128)(2,1)}, bf16[176,1024]{1,0:T(8,128)(2,1)S(1)}, u32[]{:S(2)}, u32[]{:S(2)}) collective-permute-start(bf16[176,1024]{1,0:T(8,128)(2,1)} %param.4), channel_id=1, source_target_pairs={{0,2},{1,3},{2,6},{3,7},{4,0},{5,1},{6,4},{7,5},{8,10},{9,11},{10,... | collective-permute-start | bytes 1081352 | tf_op jit(solution)/shard_map/ppermute | solution.py:338
  4.9 1.2 %multiply_reduce_fusion = f32[176]{0:T(256)S(1)} fusion(bf16[176,1024]{1,0:T(8,128)(2,1)} %param.4), kind=kLoop, calls=%fused_computation | loop fusion | flops 540496 | bytes 361152 | tf_op jit(solution)/shard_map/reduce_sum | solution.py:344
  6.2 0.5 collective-permute-start.7
  6.7 0.7 %convert_add_fusion = f32[176]{0:T(256)S(1)} fusion(s32[176]{0:T(256)} %param.7), kind=kLoop, calls=%fused_computation.27 | loop fusion | flops 352 | bytes 1408 | tf_op jit(solution)/shard_map/add | solution.py:356
  7.4 0.3 collective-permute-done.7
  7.7 0.7 %broadcast_select_fusion.4 = (bf16[1024]{0:T(1024)(128)(2,1)S(1)}, bf16[1024]{0:T(1024)(128)(2,1)S(1)}) fusion(bf16[1024]{0:T(1024)(128)(2,1)} %param.5, bf16[1024]{0:T(1024)(128)(2,1)S(1)} %collective-permute-done.7, pred[]{:T(512)S(6)} %eq.23), kind=kLoop, calls=%fused_computation.23 | loop fusion | flops 2048 | bytes 8193 | tf_op jit(solution)/shard_map/jit(_where)/select_n | solution.py:331
  8.4 0.1 pad_add_fusion.1.place_ref
  8.5 6.6 %copy.7 = bf16[256,8,4,384]{3,1,2,0:T(8,128)(2,1)} copy(bf16[256,8,4,384]{3,2,1,0:T(4,128)(2,1)} %bitcast.22) | data formatting | bytes 12582912
  15.1 2.0 %collective-permute-start.3 = (f32[176]{0:T(256)S(1)}, f32[176]{0:T(256)S(1)}, u32[]{:S(2)}, u32[]{:S(2)}) collective-permute-start(f32[176]{0:T(256)S(1)} %add.30), channel_id=1, source_target_pairs={{0,2},{1,3},{2,0},{3,1},{4,6},{5,7},{6,4},{7,5},{8,10},{9,11},{10,... | collective-permute-start | bytes 2120 | tf_op jit(solution)/shard_map/ppermute | solution.py:324
  17.1 1.5 %collective-permute-done.3 = f32[176]{0:T(256)S(1)} collective-permute-done((f32[176]{0:T(256)S(1)}, f32[176]{0:T(256)S(1)}, u32[]{:S(2)}, u32[]{:S(2)}) %collective-permute-start.3) | collective-permute-done | bytes 736 | tf_op jit(solution)/shard_map/ppermute | solution.py:324
  18.8 0.1 pad_maximum_fusion.4
  18.9 2.0 %collective-permute-start.6 = (f32[352]{0:T(512)S(1)}, f32[352]{0:T(512)S(1)}, u32[]{:S(2)}, u32[]{:S(2)}) collective-permute-start(f32[352]{0:T(512)S(1)} %pad_maximum_fusion.4), channel_id=1, source_target_pairs={{0,4},{4,0},{1,5},{5,1},{2,6},{6,2},{3,7},{7,3},{8,12},{12,8},{9,1... | collective-permute-start | bytes 4232 | tf_op jit(solution)/shard_map/ppermute | solution.py:327
  20.9 0.2 collective-permute-start.5
  21.1 0.7 %fusion = (f32[352,64]{1,0:T(8,128)S(1)}, f32[352,64]{1,0:T(8,128)S(1)}, f32[352,64]{1,0:T(8,128)S(1)}) fusion(f32[64]{0:T(128)S(1)} %fusion.2, f32[352]{0:T(512)S(1)} %add_convert_fusion.2), kind=kLoop, calls=%fused_computation.12 | loop fusion | flops 45056 | bytes 272000 | tf_op jit(solution)/shard_map/neg | solution.py:26
  21.8 0.2 pad_maximum_fusion
  21.9 0.5 collective-permute-done.6
  22.4 0.1 broadcast_select_fusion.6
  22.5 0.1 pad_maximum_fusion.5
  22.6 0.1 reshape.38.squares_ref
  22.7 2.8 %copy-done = bf16[256,8,4,384]{3,1,2,0:T(8,128)(2,1)S(1)} copy-done((bf16[256,8,4,384]{3,1,2,0:T(8,128)(2,1)S(1)}, bf16[256,8,4,384]{3,1,2,0:T(8,128)(2,1)}, u32[]{:S(2)}) %copy-start) | copy-done | bytes 6291480
  25.5 2.7 %shard_map.46 = (f32[1088,128]{1,0:T(8,128)S(1)}, f32[1088,128]{1,0:T(8,128)S(1)}, bf16[2,352,1024]{2,1,0:T(8,128)(2,1)S(1)}, bf16[2048,768]{1,0:T(8,128)(2,1)}) custom-call(s32[4]{0:T(128)S(1)} %pad_add_fusion.1.place_ref, bf16[176,1024]{1,0:T(8,128)(2,1)S(1)} %collective-permute-done.a_near, bf16[176,1024]{1,0:T(8,128)(2,1)S(1)} %collective-permute-done.1.a_far, ...), custom_call_target="tpu_custom_call" | custom-call | tf_op jit(solution)/shard_map/pallas_call | solution.py:369
  28.3 2.0 %collective-permute-start.9 = (f16[1088,128]{1,0:T(8,128)(2,1)S(1)}, f16[1088,128]{1,0:T(8,128)(2,1)S(1)}, u32[]{:S(2)}, u32[]{:S(2)}) collective-permute-start(f16[1088,128]{1,0:T(8,128)(2,1)S(1)} %convert_element_type.62), channel_id=1, source_target_pairs={{0,4},{4,0},{1,5},{5,1},{2,6},{6,2},{3,7},{7,3},{8,12},{12,8},{9,1... | collective-permute-start | bytes 835592 | tf_op jit(solution)/shard_map/ppermute | solution.py:327
  30.3 0.1 fusion.1.docs_ref
  30.4 0.1 collective-permute-start.10
  30.5 3.6 %shard_map.47 = (f32[1088,128]{1,0:T(8,128)S(1)}, f32[1088,128]{1,0:T(8,128)S(1)}) custom-call(bf16[2,352,1024]{2,1,0:T(8,128)(2,1)S(1)} %get-tuple-element.29.normed_ref, f32[16,128]{1,0:T(8,128)S(1)} %fusion.1.docs_ref, f32[352,128]{1,0:T(8,128)S(1)} %get-tuple-element.58.cos_ref, f32[352,128]{1,0:T(8,128)S(1)} %get-tuple-element.59.sin_ref, ...), custom_call_target="tpu_custom_call" | custom-call | tf_op jit(solution)/shard_map/pallas_call | solution.py:387
  34.2 3.7 %collective-permute-done.9 = f16[1088,128]{1,0:T(8,128)(2,1)S(1)} collective-permute-done((f16[1088,128]{1,0:T(8,128)(2,1)S(1)}, f16[1088,128]{1,0:T(8,128)(2,1)S(1)}, u32[]{:S(2)}, u32[]{:S(2)}) %collective-permute-start.9) | collective-permute-done | bytes 278560 | tf_op jit(solution)/shard_map/ppermute | solution.py:327
  37.8 0.1 add_convert_fusion.1.refs_1_.refs_4_.refs_3_
  37.9 0.7 %collective-permute-start.11 = (bf16[16,128]{1,0:T(8,128)(2,1)S(1)}, bf16[16,128]{1,0:T(8,128)(2,1)S(1)}, u32[]{:S(2)}, u32[]{:S(2)}) collective-permute-start(bf16[16,128]{1,0:T(8,128)(2,1)S(1)} %slice.28), channel_id=1, source_target_pairs={{2,3}} | collective-permute-start | bytes 12296 | tf_op jit(solution)/shard_map/ppermute | solution.py:445
  38.6 0.1 constant_dynamic-slice_fusion.1
  38.7 0.4 collective-permute-start.12
  39.1 0.7 %collective-permute-start.13 = (bf16[720,128]{1,0:T(8,128)(2,1)S(1)}, bf16[720,128]{1,0:T(8,128)(2,1)S(1)}, u32[]{:S(2)}, u32[]{:S(2)}) collective-permute-start(bf16[720,128]{1,0:T(8,128)(2,1)S(1)} %get-tuple-element.41), channel_id=1, source_target_pairs={{8,16},{16,8},{0,0},{24,24},{9,17},{17,9},{1,1},{25,25},{10,18},{1... | collective-permute-start | bytes 552968 | tf_op jit(solution)/shard_map/ppermute | solution.py:424
  39.8 3.0 %collective-permute-done.10 = f16[1088,128]{1,0:T(8,128)(2,1)S(1)} collective-permute-done((f16[1088,128]{1,0:T(8,128)(2,1)S(1)}, f16[1088,128]{1,0:T(8,128)(2,1)S(1)}, u32[]{:S(2)}, u32[]{:S(2)}) %collective-permute-start.10) | collective-permute-done | bytes 278560 | tf_op jit(solution)/shard_map/ppermute | solution.py:327
  42.9 0.1 add_convert_fusion.refs_2_.refs_5_.refs_4_
  43.0 0.5 collective-permute-start.14
  43.5 0.1 pad_add_fusion.refs_0_.place_ref
  43.6 1.8 %shard_map.48 = (f32[2,352,128]{2,1,0:T(8,128)S(1)}, f32[2,352,1]{2,1,0:T(8,128)S(1)}) custom-call(s32[2]{0:T(128)S(1)} %pad_add_fusion.refs_0_.place_ref, bf16[1088,128]{1,0:T(8,128)(2,1)S(1)} %add_convert_fusion.1.refs_1_.refs_4_.refs_3_, bf16[1088,128]{1,0:T(8,128)(2,1)S(1)} %add_convert_fusion.refs_2_.refs_5_.refs_4_), custom_call_target="tpu_custom_call" | custom-call | tf_op jit(solution)/shard_map/pallas_call | solution.py:459
  45.5 3.3 %collective-permute-done.14.refs_3_.refs_7_ = bf16[720,128]{1,0:T(8,128)(2,1)S(1)} collective-permute-done((bf16[720,128]{1,0:T(8,128)(2,1)S(1)}, bf16[720,128]{1,0:T(8,128)(2,1)S(1)}, u32[]{:S(2)}, u32[]{:S(2)}) %collective-permute-start.14) | collective-permute-done | bytes 184352 | tf_op jit(solution)/shard_map/ppermute | solution.py:424
  48.8 0.6 shard_map.49.refs_8_
  49.4 1.8 %collective-permute-start.15 = (bf16[368,128]{1,0:T(8,128)(2,1)S(1)}, bf16[368,128]{1,0:T(8,128)(2,1)S(1)}, u32[]{:S(2)}, u32[]{:S(2)}) collective-permute-start(bf16[368,128]{1,0:T(8,128)(2,1)S(1)} %get-tuple-element.44), channel_id=1, source_target_pairs={{0,8},{8,24},{16,0},{24,16},{1,9},{9,25},{17,1},{25,17},{2,10},{10... | collective-permute-start | bytes 282632 | tf_op jit(solution)/shard_map/ppermute | solution.py:424
  51.2 1.3 %collective-permute-start.16 = (bf16[368,128]{1,0:T(8,128)(2,1)S(1)}, bf16[368,128]{1,0:T(8,128)(2,1)S(1)}, u32[]{:S(2)}, u32[]{:S(2)}) collective-permute-start(bf16[368,128]{1,0:T(8,128)(2,1)S(1)} %get-tuple-element.43), channel_id=1, source_target_pairs={{8,16},{16,24},{9,17},{17,25},{10,18},{18,26},{11,19},{19,27},{12,... | collective-permute-start | bytes 282632 | tf_op jit(solution)/shard_map/ppermute | solution.py:424
  52.5 1.2 %shard_map.50 = (f32[2,352,128]{2,1,0:T(8,128)S(1)}, f32[2,352,1]{2,1,0:T(8,128)S(1)}) custom-call(s32[2]{0:T(128)S(1)} %pad_add_fusion.refs_0_.place_ref, f32[2,352,128]{2,1,0:T(8,128)S(1)} %get-tuple-element.35.refs_1_, f32[2,352,1]{2,1,0:T(8,128)S(1)} %get-tuple-element.36.refs_6_.refs_2_, ...), custom_call_target="tpu_custom_call" | custom-call | tf_op jit(solution)/shard_map/pallas_call | solution.py:470
  53.7 2.0 %collective-permute-done.15.first_ref = bf16[368,128]{1,0:T(8,128)(2,1)S(1)} collective-permute-done((bf16[368,128]{1,0:T(8,128)(2,1)S(1)}, bf16[368,128]{1,0:T(8,128)(2,1)S(1)}, u32[]{:S(2)}, u32[]{:S(2)}) %collective-permute-start.15) | collective-permute-done | bytes 94240 | tf_op jit(solution)/shard_map/ppermute | solution.py:424
  55.8 1.9 %collective-permute-done.16.below_ref = bf16[368,128]{1,0:T(8,128)(2,1)S(1)} collective-permute-done((bf16[368,128]{1,0:T(8,128)(2,1)S(1)}, bf16[368,128]{1,0:T(8,128)(2,1)S(1)}, u32[]{:S(2)}, u32[]{:S(2)}) %collective-permute-start.16) | collective-permute-done | bytes 94240 | tf_op jit(solution)/shard_map/ppermute | solution.py:424
  57.7 1.1 %shard_map.51 = (bf16[176,256]{1,0:T(8,128)(2,1)S(1)}, bf16[176,256]{1,0:T(8,128)(2,1)S(1)}) custom-call(s32[2]{0:T(128)S(1)} %pad_add_fusion.refs_0_.place_ref, f32[2,352,128]{2,1,0:T(8,128)S(1)} %get-tuple-element.37.out_ref, f32[2,352,1]{2,1,0:T(8,128)S(1)} %get-tuple-element.38.logs_ref, bf16[368,128]{1,0:T(8,128)(2,1)S(1)} %collective-permute-done.15.first_ref, ...), custom_call_target="tpu_custom_call" | custom-call | tf_op jit(solution)/shard_map/pallas_call | solution.py:474
  58.7 1.8 %collective-permute-start.17 = (bf16[176,256]{1,0:T(8,128)(2,1)S(1)}, bf16[176,256]{1,0:T(8,128)(2,1)S(1)}, u32[]{:S(2)}, u32[]{:S(2)}) collective-permute-start(bf16[176,256]{1,0:T(8,128)(2,1)S(1)} %get-tuple-element.40), channel_id=1, source_target_pairs={{0,4},{4,0},{1,5},{5,1},{2,6},{6,2},{3,7},{7,3},{8,12},{12,8},{9,1... | collective-permute-start | bytes 270344 | tf_op jit(solution)/shard_map/ppermute | solution.py:327
  60.6 2.8 %collective-permute-done.17 = bf16[176,256]{1,0:T(8,128)(2,1)S(1)} collective-permute-done((bf16[176,256]{1,0:T(8,128)(2,1)S(1)}, bf16[176,256]{1,0:T(8,128)(2,1)S(1)}, u32[]{:S(2)}, u32[]{:S(2)}) %collective-permute-start.17) | collective-permute-done | bytes 90144 | tf_op jit(solution)/shard_map/ppermute | solution.py:327
  63.3 0.7 %pad_maximum_fusion.2 = bf16[176,512]{1,0:T(8,128)(2,1)} fusion(bf16[176,256]{1,0:T(8,128)(2,1)S(1)} %get-tuple-element.46, bf16[176,256]{1,0:T(8,128)(2,1)S(1)} %get-tuple-element.45), kind=kLoop, calls=%fused_computation.7 | loop fusion | flops 360448 | bytes 360448 | tf_op jit(solution)/shard_map/concatenate | solution.py:480
  (29 shorter events, 0.4 us)
Async XLA Ops:
  0.0 18.7 %collective-permute-start = (bf16[176,1024]{1,0:T(8,128)(2,1)}, bf16[176,1024]{1,0:T(8,128)(2,1)S(1)}, u32[]{:S(2)}, u32[]{:S(2)}) collective-permute-start(bf16[176,1024]{1,0:T(8,128)(2,1)} %param.4), channel_id=1, source_target_pairs={{0,0},{1,1},{2,4},{3,5},{4,2},{5,3},{6,6},{7,7},{8,8},{9,9},{10,12... | collective-permute-start | bytes 1081352 | tf_op jit(solution)/shard_map/ppermute | solution.py:333
  1.6 17.0 %collective-permute-start.1 = (bf16[176,1024]{1,0:T(8,128)(2,1)}, bf16[176,1024]{1,0:T(8,128)(2,1)S(1)}, u32[]{:S(2)}, u32[]{:S(2)}) collective-permute-start(bf16[176,1024]{1,0:T(8,128)(2,1)} %param.4), channel_id=1, source_target_pairs={{0,2},{1,3},{2,6},{3,7},{4,0},{5,1},{6,4},{7,5},{8,10},{9,11},{10,... | collective-permute-start | bytes 1081352 | tf_op jit(solution)/shard_map/ppermute | solution.py:338
  6.1 9.0 %collective-permute-start.2 = (f32[176]{0:T(256)S(1)}, f32[176]{0:T(256)S(1)}, u32[]{:S(2)}, u32[]{:S(2)}) collective-permute-start(f32[176]{0:T(256)S(1)} %multiply_reduce_fusion), channel_id=1, source_target_pairs={{0,1},{1,0},{2,3},{3,2},{4,5},{5,4},{6,7},{7,6},{8,9},{9,8},{10,11... | collective-permute-start | bytes 2120 | tf_op jit(solution)/shard_map/ppermute | solution.py:324
  6.2 1.5 %collective-permute-start.7 = (bf16[1024]{0:T(1024)(128)(2,1)}, bf16[1024]{0:T(1024)(128)(2,1)S(1)}, u32[]{:S(2)}, u32[]{:S(2)}) collective-permute-start(bf16[1024]{0:T(1024)(128)(2,1)} %param.5), channel_id=1, source_target_pairs={{0,1},{1,0},{2,3},{3,2},{4,5},{5,4},{6,7},{7,6},{8,9},{9,8},{10,11... | collective-permute-start | bytes 6152 | tf_op jit(solution)/shard_map/ppermute | solution.py:324
  8.4 8.7 %collective-permute-start.8 = (bf16[2048]{0:T(1024)(128)(2,1)S(1)}, bf16[2048]{0:T(1024)(128)(2,1)S(1)}, u32[]{:S(2)}, u32[]{:S(2)}) collective-permute-start(bf16[2048]{0:T(1024)(128)(2,1)S(1)} %pad_maximum_fusion.3), channel_id=1, source_target_pairs={{0,2},{1,3},{2,0},{3,1},{4,6},{5,7},{6,4},{7,5},{8,10},{9,11},{10,... | collective-permute-start | bytes 12296 | tf_op jit(solution)/shard_map/ppermute | solution.py:324
  8.5 14.0 %copy-start.1 = (s32[176]{0:T(256)S(1)}, s32[176]{0:T(256)}, u32[]{:S(2)}) copy-start(s32[176]{0:T(256)} %param.7) | copy-start | bytes 2116
  15.1 3.6 %collective-permute-start.3 = (f32[176]{0:T(256)S(1)}, f32[176]{0:T(256)S(1)}, u32[]{:S(2)}, u32[]{:S(2)}) collective-permute-start(f32[176]{0:T(256)S(1)} %add.30), channel_id=1, source_target_pairs={{0,2},{1,3},{2,0},{3,1},{4,6},{5,7},{6,4},{7,5},{8,10},{9,11},{10,... | collective-permute-start | bytes 2120 | tf_op jit(solution)/shard_map/ppermute | solution.py:324
  18.7 4.0 %collective-permute-start.4 = (bf16[176,1024]{1,0:T(8,128)(2,1)S(1)}, bf16[176,1024]{1,0:T(8,128)(2,1)S(1)}, u32[]{:S(2)}, u32[]{:S(2)}) collective-permute-start(bf16[176,1024]{1,0:T(8,128)(2,1)S(1)} %collective-permute-done.a_near), channel_id=1, source_target_pairs={{0,1},{1,0},{2,3},{3,2},{4,5},{5,4},{6,7},{7,6},{8,9},{9,8},{10,11... | collective-permute-start | bytes 1081352 | tf_op jit(solution)/shard_map/ppermute | solution.py:324
  18.9 3.6 %collective-permute-start.6 = (f32[352]{0:T(512)S(1)}, f32[352]{0:T(512)S(1)}, u32[]{:S(2)}, u32[]{:S(2)}) collective-permute-start(f32[352]{0:T(512)S(1)} %pad_maximum_fusion.4), channel_id=1, source_target_pairs={{0,4},{4,0},{1,5},{5,1},{2,6},{6,2},{3,7},{7,3},{8,12},{12,8},{9,1... | collective-permute-start | bytes 4232 | tf_op jit(solution)/shard_map/ppermute | solution.py:327
  20.9 1.9 %collective-permute-start.5 = (bf16[176,1024]{1,0:T(8,128)(2,1)S(1)}, bf16[176,1024]{1,0:T(8,128)(2,1)S(1)}, u32[]{:S(2)}, u32[]{:S(2)}) collective-permute-start(bf16[176,1024]{1,0:T(8,128)(2,1)S(1)} %collective-permute-done.1.a_far), channel_id=1, source_target_pairs={{0,1},{1,0},{2,3},{3,2},{4,5},{5,4},{6,7},{7,6},{8,9},{9,8},{10,11... | collective-permute-start | bytes 1081352 | tf_op jit(solution)/shard_map/ppermute | solution.py:324
  22.7 2.8 %copy-start = (bf16[256,8,4,384]{3,1,2,0:T(8,128)(2,1)S(1)}, bf16[256,8,4,384]{3,1,2,0:T(8,128)(2,1)}, u32[]{:S(2)}) copy-start(bf16[256,8,4,384]{3,1,2,0:T(8,128)(2,1)} %copy.7) | copy-start | bytes 18874372
  28.3 9.6 %collective-permute-start.9 = (f16[1088,128]{1,0:T(8,128)(2,1)S(1)}, f16[1088,128]{1,0:T(8,128)(2,1)S(1)}, u32[]{:S(2)}, u32[]{:S(2)}) collective-permute-start(f16[1088,128]{1,0:T(8,128)(2,1)S(1)} %convert_element_type.62), channel_id=1, source_target_pairs={{0,4},{4,0},{1,5},{5,1},{2,6},{6,2},{3,7},{7,3},{8,12},{12,8},{9,1... | collective-permute-start | bytes 835592 | tf_op jit(solution)/shard_map/ppermute | solution.py:327
  30.4 12.4 %collective-permute-start.10 = (f16[1088,128]{1,0:T(8,128)(2,1)S(1)}, f16[1088,128]{1,0:T(8,128)(2,1)S(1)}, u32[]{:S(2)}, u32[]{:S(2)}) collective-permute-start(f16[1088,128]{1,0:T(8,128)(2,1)S(1)} %convert_element_type.65), channel_id=1, source_target_pairs={{0,4},{4,0},{1,5},{5,1},{2,6},{6,2},{3,7},{7,3},{8,12},{12,8},{9,1... | collective-permute-start | bytes 835592 | tf_op jit(solution)/shard_map/ppermute | solution.py:327
  37.9 1.8 %collective-permute-start.11 = (bf16[16,128]{1,0:T(8,128)(2,1)S(1)}, bf16[16,128]{1,0:T(8,128)(2,1)S(1)}, u32[]{:S(2)}, u32[]{:S(2)}) collective-permute-start(bf16[16,128]{1,0:T(8,128)(2,1)S(1)} %slice.28), channel_id=1, source_target_pairs={{2,3}} | collective-permute-start | bytes 12296 | tf_op jit(solution)/shard_map/ppermute | solution.py:445
  38.7 6.7 %collective-permute-start.12 = (bf16[720,128]{1,0:T(8,128)(2,1)S(1)}, bf16[720,128]{1,0:T(8,128)(2,1)S(1)}, u32[]{:S(2)}, u32[]{:S(2)}) collective-permute-start(bf16[720,128]{1,0:T(8,128)(2,1)S(1)} %get-tuple-element.42), channel_id=1, source_target_pairs={{0,16},{24,8},{8,0},{16,24},{1,17},{25,9},{9,1},{17,25},{2,18},{26... | collective-permute-start | bytes 552968 | tf_op jit(solution)/shard_map/ppermute | solution.py:424
  39.1 6.3 %collective-permute-start.13 = (bf16[720,128]{1,0:T(8,128)(2,1)S(1)}, bf16[720,128]{1,0:T(8,128)(2,1)S(1)}, u32[]{:S(2)}, u32[]{:S(2)}) collective-permute-start(bf16[720,128]{1,0:T(8,128)(2,1)S(1)} %get-tuple-element.41), channel_id=1, source_target_pairs={{8,16},{16,8},{0,0},{24,24},{9,17},{17,9},{1,1},{25,25},{10,18},{1... | collective-permute-start | bytes 552968 | tf_op jit(solution)/shard_map/ppermute | solution.py:424
  43.0 5.8 %collective-permute-start.14 = (bf16[720,128]{1,0:T(8,128)(2,1)S(1)}, bf16[720,128]{1,0:T(8,128)(2,1)S(1)}, u32[]{:S(2)}, u32[]{:S(2)}) collective-permute-start(bf16[720,128]{1,0:T(8,128)(2,1)S(1)} %constant_dynamic-slice_fusion), channel_id=1, source_target_pairs={{0,8},{8,0},{16,24},{24,16},{1,9},{9,1},{17,25},{25,17},{2,10},{10... | collective-permute-start | bytes 552968 | tf_op jit(solution)/shard_map/ppermute | solution.py:424
  49.4 6.4 %collective-permute-start.15 = (bf16[368,128]{1,0:T(8,128)(2,1)S(1)}, bf16[368,128]{1,0:T(8,128)(2,1)S(1)}, u32[]{:S(2)}, u32[]{:S(2)}) collective-permute-start(bf16[368,128]{1,0:T(8,128)(2,1)S(1)} %get-tuple-element.44), channel_id=1, source_target_pairs={{0,8},{8,24},{16,0},{24,16},{1,9},{9,25},{17,1},{25,17},{2,10},{10... | collective-permute-start | bytes 282632 | tf_op jit(solution)/shard_map/ppermute | solution.py:424
  51.2 6.5 %collective-permute-start.16 = (bf16[368,128]{1,0:T(8,128)(2,1)S(1)}, bf16[368,128]{1,0:T(8,128)(2,1)S(1)}, u32[]{:S(2)}, u32[]{:S(2)}) collective-permute-start(bf16[368,128]{1,0:T(8,128)(2,1)S(1)} %get-tuple-element.43), channel_id=1, source_target_pairs={{8,16},{16,24},{9,17},{17,25},{10,18},{18,26},{11,19},{19,27},{12,... | collective-permute-start | bytes 282632 | tf_op jit(solution)/shard_map/ppermute | solution.py:424
  58.7 4.6 %collective-permute-start.17 = (bf16[176,256]{1,0:T(8,128)(2,1)S(1)}, bf16[176,256]{1,0:T(8,128)(2,1)S(1)}, u32[]{:S(2)}, u32[]{:S(2)}) collective-permute-start(bf16[176,256]{1,0:T(8,128)(2,1)S(1)} %get-tuple-element.40), channel_id=1, source_target_pairs={{0,4},{4,0},{1,5},{5,1},{2,6},{6,2},{3,7},{7,3},{8,12},{12,8},{9,1... | collective-permute-start | bytes 270344 | tf_op jit(solution)/shard_map/ppermute | solution.py:327
